TPU v7x, 256 devices: a whole 4x4x8 slice. The times are simulated.
256 devices in a mesh: gx: 64 (over y, z, core), gy: 4 (over x).
Axes of the slice: x: 4, y: 4, z: 8, core: 2. Of those that a mesh axis runs over, the one named last changes fastest.
Arguments:
- features: bfloat16 [49152, 256], P(('gx', 'gy')), may hold values from -6 to 6
- pre_act: bfloat16 [49152, 256], P(('gx', 'gy')), may hold values from -6 to 6
- grad_out: bfloat16 [49152, 256], P(('gx', 'gy')), may hold values from -24 to 24
- weight_one: bfloat16 [256, 6912], replicated, may hold values from -0.078125 to 0.078125
- weight_two: bfloat16 [256, 6912], replicated, may hold values from -0.078125 to 0.078125
- neighbours: int32 [49152, 27], P(('gx', 'gy')), may hold values from -1 to 383, as said below
- halo_list: int32 [256, 8, 24], P(('gx', 'gy')), may hold values from -1 to 191, as said below
- send_list: int32 [256, 64, 3], P(('gx', 'gy')), may hold values from -1 to 191, as said below
Outputs:
- grad_features: bfloat16 [49152, 256], P(('gx', 'gy'))
- grad_weight_one: float32 [256, 6912], P('gx', 'gy')
- grad_weight_two: float32 [256, 6912], P('gx', 'gy')
Inputs may be any that keep to these rules, and one draw needn't show every extreme that they name: `neighbours`: A tile's live slots are its first ones: a quarter, a half, three quarters or all of its 192 slots, and tile 0 has all live. For a live slot, offset 13 names the slot itself and the others name a live slot of the same tile, a halo row (192 to 383), or -1; rows of dead slots are all -1. `halo_list`: entries are live slots of the sending tile, repeats allowed, or -1. `send_list`: every live slot of a tile appears exactly once in its list and dead slots never; -1 marks an unused place; a tile with all slots live fills all 3 places for every peer.
All inputs are finite; a program needn't handle non-finite values.
Results may differ from a plain program's by a relative error of at most 0.006.
Values may be sent and summed in bfloat16 or wider, within the bound.
No kernel may reach another device: no remote copies, remote signals or barrier semaphores. Data moves between devices by JAX's collectives and lax.ppermute only.
A program may use at most 128 MiB of HBM per device.

v0:
```python
import math

import jax
import jax.numpy as jnp
from jax import lax
from jax.sharding import PartitionSpec as P

DIRECTIONS = ((-1, -1), (-1, 0), (-1, 1), (0, -1), (0, 1), (1, -1), (1, 0), (1, 1))


def shifted(value, axis, steps):
    count = lax.axis_size(axis)
    initial, last = (max(0, -steps), min(count, count - steps))
    return lax.ppermute(value, axis, [(source, source + steps) for source in range(initial, last)])


def pick_rows(stacked, chosen_slots):
    picked_rows = jnp.take(stacked, jnp.maximum(chosen_slots, 0), axis=1)
    return jnp.where((chosen_slots >= 0)[None, :, None], picked_rows, jnp.zeros((), stacked.dtype))


def spread_direct(stacked, halo_slots):
    gy_size = lax.axis_size("gy")
    column = lax.axis_index("gy")
    blocks = []
    for heading in range(8):
        step_x, step_y = DIRECTIONS[heading]
        picked_rows = pick_rows(stacked, halo_slots[heading])
        arrived = shifted(picked_rows, ("gx", "gy"), step_x * gy_size + step_y)
        anchor = column - step_y
        inside = (anchor >= 0) & (anchor < gy_size)
        blocks.append(jnp.where(inside, arrived, jnp.zeros((), arrived.dtype)))
    return jnp.stack(blocks, 1)


def settle(blocks, halo_slots, row_count):
    target = jnp.where(halo_slots >= 0, halo_slots, row_count)
    summed = jax.ops.segment_sum(
        blocks.reshape(-1, blocks.shape[-1]), target.reshape(-1), num_segments=row_count + 1
    )
    return summed[:row_count]


def return_direct(outgoing, halo_slots, row_count):
    gy_size = lax.axis_size("gy")
    column = lax.axis_index("gy")
    blocks = []
    for heading in range(8):
        step_x, step_y = DIRECTIONS[heading]
        arrived = shifted(outgoing[heading], ("gx", "gy"), -(step_x * gy_size + step_y))
        anchor = column + step_y
        inside = (anchor >= 0) & (anchor < gy_size)
        blocks.append(jnp.where(inside, arrived, 0.0))
    return settle(jnp.stack(blocks, 0), halo_slots, row_count)


def weight_sum(columns, gradient):
    my_columns = lax.all_to_all(columns, "gy", split_axis=1, concat_axis=0, tiled=True)
    all_grads = lax.all_gather(gradient, "gy", axis=0, tiled=True)
    return lax.psum_scatter(
        lax.dot_general(
            all_grads, my_columns, (((0,), (0,)), ((), ())), preferred_element_type=jnp.float32
        ),
        "gx",
        scatter_dimension=0,
        tiled=True,
    )


def body(features, pre_act, grad_out, weight_one, weight_two, neighbours, halo_list, send_list):
    slot_count, channel_count = features.shape
    halo_slots = halo_list[0]
    halo_count = halo_slots.shape[1]
    extent = slot_count + 8 * halo_count
    norm_scale = 1.0 / math.sqrt(slot_count * lax.axis_size("gx") * lax.axis_size("gy"))
    pre_value = pre_act.astype(jnp.float32)
    hidden = jax.nn.silu(pre_value).astype(jnp.bfloat16)
    stacked = jnp.stack([features, hidden], 0)
    outside = spread_direct(stacked, halo_slots)
    where_to = jnp.where(neighbours < 0, extent, neighbours)

    def unfold(own_rows, received):
        extended = jnp.concatenate(
            [
                own_rows,
                received.reshape(8 * halo_count, channel_count),
                jnp.zeros((1, channel_count), own_rows.dtype),
            ],
            0,
        )
        return jnp.take(extended, where_to, axis=0).reshape(slot_count, -1)

    def input_grad(gradient, weight):
        spread = jnp.dot(gradient, weight, preferred_element_type=jnp.float32)
        summed = jax.ops.segment_sum(
            spread.reshape(-1, channel_count), where_to.reshape(-1), num_segments=extent + 1
        )
        outgoing = summed[slot_count:extent].reshape(8, halo_count, channel_count)
        arriving = return_direct(outgoing, halo_slots, slot_count)
        return summed[:slot_count] + arriving

    grad_two = weight_sum(unfold(hidden, outside[1]), grad_out) * norm_scale
    grad_hidden = input_grad(grad_out, weight_two)
    sigmoid_z = jax.nn.sigmoid(pre_value)
    grad_pre = (grad_hidden * sigmoid_z * (1.0 + pre_value * (1.0 - sigmoid_z))).astype(
        jnp.bfloat16
    )
    grad_one = weight_sum(unfold(features, outside[0]), grad_pre) * norm_scale
    grad_input = (grad_out.astype(jnp.float32) + input_grad(grad_pre, weight_one)).astype(
        jnp.bfloat16
    )
    send_slots = send_list[0]
    outgoing_rows = jnp.take(grad_input, jnp.maximum(send_slots, 0), axis=0)
    outgoing_rows = jnp.where(
        (send_slots >= 0)[:, :, None], outgoing_rows, jnp.zeros((), jnp.bfloat16)
    )
    balanced = lax.all_to_all(outgoing_rows, "gx", split_axis=0, concat_axis=0, tiled=True)
    return (balanced.reshape(slot_count, channel_count), grad_one, grad_two)


def solution(mesh):
    in_specs = (
        P(("gx", "gy"), None),
        P(("gx", "gy"), None),
        P(("gx", "gy"), None),
        P(),
        P(),
        P(("gx", "gy"), None),
        P(("gx", "gy"), None, None),
        P(("gx", "gy"), None, None),
    )
    out_specs = (P(("gx", "gy"), None), P("gx", "gy"), P("gx", "gy"))
    return jax.shard_map(body, mesh=mesh, in_specs=in_specs, out_specs=out_specs, check_vma=False)
```

profile of v0, /device:TPU:2, one launch (start us, length us, event | category | flops | bytes accessed | tf_op | source)
XLA Modules:
  0.0 569.7 jit_solution(2818584620847519027)
XLA Ops:
  7.2 1.5 compare_select_fusion
  8.7 1.5 copy.56
  10.2 1.7 reshape.322
  11.9 4.1 fusion.29
  16.1 6.9 %reshape.308 = f32[5184,256]{1,0:T(8,128)} reshape(f32[192,6912]{1,0:T(8,128)} %fusion.29) | data formatting | bytes 10616832 | tf_op jit(solution)/shard_map/reshape | solution.py:96
  23.0 33.6 %scatter_custom_fusion = f32[385,256]{1,0:T(8,128)S(1)} fusion(s32[5184]{0:T(1024)} %reshape.322, f32[5184,256]{1,0:T(8,128)} %reshape.308, f32[]{:T(128)} %constant.15.clone.1), kind=kCustom, calls=%fused_computation.25 | custom fusion | flops 1327104 | bytes 394752 | tf_op jit(solution)/shard_map/scatter-add | solution.py:95
  56.6 5.5 collective-permute-start
  64.7 6.8 %collective-permute-start.3 = (f32[24,256]{1,0:T(8,128)S(1)}, f32[24,256]{1,0:T(8,128)S(1)}, u32[]{:S(2)}, u32[]{:S(2)}) collective-permute-start(f32[24,256]{1,0:T(8,128)S(1)} %get-tuple-element.35), channel_id=1, source_target_pairs={{0,1},{1,2},{2,3},{3,4},{4,5},{5,6},{6,7},{7,8},{8,9},{9,10},{10,1... | collective-permute-start | bytes 73736 | tf_op jit(solution)/shard_map/ppermute | solution.py:14
  71.5 1.9 collective-permute-start.4
  74.3 1.3 collective-permute-start.5
  75.6 1.3 collective-permute-start.6
  76.9 1.3 collective-permute-start.7
  79.4 1.5 collective-permute-done.6
  80.9 3.6 collective-permute-done.7
  84.5 1.6 scatter_custom_fusion.1
  87.9 1.3 collective-permute-start.16
  89.9 1.3 collective-permute-start.17
  92.0 1.3 collective-permute-start.18
  94.0 2.7 collective-permute-start.19
  97.5 3.1 collective-permute-start.20
  102.9 5.2 collective-permute-start.21
  108.2 6.4 %collective-permute-start.22 = (bf16[2,24,256]{2,0,1:T(2,128)(2,1)S(1)}, bf16[2,24,256]{2,0,1:T(2,128)(2,1)S(1)}, u32[]{:S(2)}, u32[]{:S(2)}) collective-permute-start(bf16[2,24,256]{2,0,1:T(2,128)(2,1)S(1)} %broadcast_select_fusion.11), channel_id=1, source_target_pairs={{0,4},{1,5},{2,6},{3,7},{4,8},{5,9},{6,10},{7,11},{8,12},{9,13},{1... | collective-permute-start | bytes 73736 | tf_op jit(solution)/shard_map/ppermute | solution.py:14
  114.6 2.9 collective-permute-start.23
  119.3 15.6 %gather_fusion.9 = bf16[5184,256]{1,0:T(8,128)(2,1)S(1)} fusion(bf16[385,256]{1,0:T(8,128)(2,1)S(1)} %get-tuple-element.72, s32[6144]{0:T(1024)S(1)} %pad_clamp_fusion), kind=kCustom, calls=%fused_computation.1.clone | custom fusion | bytes 5329152 | tf_op jit(solution)/shard_map/jit(_take)/gather | solution.py:91
  135.0 2.5 reshape.371
  137.5 15.6 %gather_fusion.10 = bf16[5184,256]{1,0:T(8,128)(2,1)S(1)} fusion(bf16[385,256]{1,0:T(8,128)(2,1)S(1)} %get-tuple-element.71, s32[6144]{0:T(1024)S(1)} %pad_clamp_fusion), kind=kCustom, calls=%fused_computation.9.clone | custom fusion | bytes 5329152 | tf_op jit(solution)/shard_map/jit(_take)/gather | solution.py:91
  153.1 2.5 reshape.375
  155.6 5.6 broadcast_select_fusion
  161.2 7.6 %all_to_all.32 = bf16[192,4,1728]{2,1,0:T(4,128)(2,1)} reshape(bf16[192,27,256]{2,1,0:T(8,128)(2,1)} %get-tuple-element.46) | data formatting | bytes 5308416 | tf_op jit(solution)/shard_map/all_to_all | solution.py:58
  168.9 3.6 copy.68
  172.4 8.7 %all-to-all-start.1 = ((bf16[192,4,1728]{2,0,1:T(8,128)(2,1)}), bf16[192,4,1728]{2,0,1:T(8,128)(2,1)}, u32[]{:S(2)}, u32[]{:S(2)}) async-start(bf16[192,4,1728]{2,0,1:T(8,128)(2,1)} %copy.68), calls=%async_computation.1 | async-start | bytes 5505024 | tf_op jit(solution)/shard_map/all_to_all | solution.py:58
  182.2 4.4 all_to_all.36
  186.6 3.5 copy.71
  190.2 23.8 %all-to-all-done.1 = bf16[192,4,1728]{2,0,1:T(8,128)(2,1)} async-done(((bf16[192,4,1728]{2,0,1:T(8,128)(2,1)}), bf16[192,4,1728]{2,0,1:T(8,128)(2,1)}, u32[]{:S(2)}, u32[]{:S(2)}) %all-to-all-start.1) | async-done | bytes 2654240 | tf_op jit(solution)/shard_map/all_to_all | solution.py:58
  214.0 6.5 %all-to-all-start.2 = ((bf16[192,4,1728]{2,0,1:T(8,128)(2,1)}), bf16[192,4,1728]{2,0,1:T(8,128)(2,1)}, u32[]{:S(2)}, u32[]{:S(2)}) async-start(bf16[192,4,1728]{2,0,1:T(8,128)(2,1)} %copy.71), calls=%async_computation.2 | async-start | bytes 5505024 | tf_op jit(solution)/shard_map/all_to_all | solution.py:58
  220.5 39.8 %all_gather.7 = bf16[768,256]{1,0:T(8,128)(2,1)} all-gather(bf16[192,256]{1,0:T(8,128)(2,1)} %param.14), channel_id=1, replica_groups=mesh['gx'=64,'gy'=4] {'gy'}, dimensions={0}, use_global_device_ids=true | all-gather | bytes 491520 | tf_op jit(solution)/shard_map/all_gather | solution.py:59
  260.2 4.1 fusion.30
  264.4 6.9 %reshape.324 = f32[5184,256]{1,0:T(8,128)} reshape(f32[192,6912]{1,0:T(8,128)} %fusion.30) | data formatting | bytes 10616832 | tf_op jit(solution)/shard_map/reshape | solution.py:96
  271.3 33.7 %scatter_custom_fusion.2 = f32[385,256]{1,0:T(8,128)S(1)} fusion(s32[5184]{0:T(1024)} %reshape.322, f32[5184,256]{1,0:T(8,128)} %reshape.324, f32[]{:T(128)} %constant.15.clone.1), kind=kCustom, calls=%fused_computation.23 | custom fusion | flops 1327104 | bytes 394752 | tf_op jit(solution)/shard_map/scatter-add | solution.py:95
  305.7 2.1 collective-permute-start.8
  307.8 19.2 %all_gather.6 = bf16[768,256]{1,0:T(8,128)(2,1)S(1)} all-gather(bf16[192,256]{1,0:T(8,128)(2,1)S(1)} %copy-done.4), channel_id=1, replica_groups=mesh['gx'=64,'gy'=4] {'gy'}, dimensions={0}, use_global_device_ids=true | all-gather | bytes 491520 | tf_op jit(solution)/shard_map/all_gather | solution.py:59
  328.3 3.4 collective-permute-start.10
  331.7 2.6 collective-permute-start.11
  334.3 3.8 collective-permute-start.12
  338.2 1.3 collective-permute-start.13
  340.8 1.5 collective-permute-start.15
  342.4 4.0 fusion.31
  346.4 2.7 convolution_bitcast_fusion
  349.1 1.7 copy.72
  350.8 1.5 constant_dynamic-update-slice_fusion.12
  352.4 1.4 constant_dynamic-update-slice_fusion.11
  353.7 1.3 constant_dynamic-update-slice_fusion.10
  355.1 1.3 constant_dynamic-update-slice_fusion.9
  356.4 1.3 constant_dynamic-update-slice_fusion.8
  357.7 2.6 scatter_custom_fusion.3
  360.4 1.8 fusion.12
  362.1 2.4 gather_fusion
  364.6 1.6 reshape.297
  366.2 1.8 select_select_fusion
  368.0 23.9 %all-to-all-start = ((bf16[64,3,256]{2,1,0:T(4,128)(2,1)}), bf16[64,3,256]{2,1,0:T(4,128)(2,1)}, u32[]{:S(2)}, u32[]{:S(2)}) async-start(bf16[64,3,256]{2,1,0:T(4,128)(2,1)} %select_select_fusion), calls=%async_computation | async-start | bytes 262144 | tf_op jit(solution)/shard_map/all_to_all | solution.py:117
  393.8 8.5 %all-to-all-done = bf16[64,3,256]{2,1,0:T(4,128)(2,1)} async-done(((bf16[64,3,256]{2,1,0:T(4,128)(2,1)}), bf16[64,3,256]{2,1,0:T(4,128)(2,1)}, u32[]{:S(2)}, u32[]{:S(2)}) %all-to-all-start) | async-done | bytes 98336 | tf_op jit(solution)/shard_map/all_to_all | solution.py:117
  402.4 1.6 reshape.215
  404.0 157.4 %all-reduce.5.cloned.1.call-done = (f32[256,1728]{1,0:T(8,128)}, f32[256,1728]{1,0:T(8,128)}) async-done(((f32[256,1728]{1,0:T(8,128)}, f32[256,1728]{1,0:T(8,128)}), (f32[256,1728]{1,0:T(8,128)}, f32[256,1728]{1,0:T(8,128)})) %all-reduce.5.cloned.1.call-update) | async-done | bytes 3538960
  561.4 1.5 dynamic-slice_multiply_fusion
  (125 shorter events, 18.9 us)
Async XLA Ops:
  7.2 4.8 copy-start
  16.0 57.4 %copy-start.10 = (s32[1,8,24]{2,1,0:T(8,128)S(1)}, s32[1,8,24]{2,1,0:T(8,128)}, u32[]{:S(2)}) copy-start(s32[1,8,24]{2,1,0:T(8,128)} %param.18) | copy-start | bytes 2308
  16.0 57.6 %copy-start.7 = (s32[192,27]{0,1:T(8,128)S(1)}, s32[192,27]{0,1:T(8,128)}, u32[]{:S(2)}) copy-start(s32[192,27]{0,1:T(8,128)} %param.17) | copy-start | bytes 62212
  16.0 57.7 %copy-start.8 = (s32[192,27]{0,1:T(8,128)S(1)}, s32[192,27]{0,1:T(8,128)}, u32[]{:S(2)}) copy-start(s32[192,27]{0,1:T(8,128)} %get-tuple-element.43) | copy-start | bytes 62212
  16.0 70.1 %copy-start.9 = (bf16[192,256]{1,0:T(8,128)(2,1)S(1)}, bf16[192,256]{1,0:T(8,128)(2,1)}, u32[]{:S(2)}) copy-start(bf16[192,256]{1,0:T(8,128)(2,1)} %param.13) | copy-start | bytes 294916
  16.0 70.9 %copy-start.5 = (bf16[192,256]{1,0:T(8,128)(2,1)S(1)}, bf16[192,256]{1,0:T(8,128)(2,1)}, u32[]{:S(2)}) copy-start(bf16[192,256]{1,0:T(8,128)(2,1)} %param.12) | copy-start | bytes 294916
  56.6 17.6 %collective-permute-start = (f32[24,256]{1,0:T(8,128)S(1)}, f32[24,256]{1,0:T(8,128)S(1)}, u32[]{:S(2)}, u32[]{:S(2)}) collective-permute-start(f32[24,256]{1,0:T(8,128)S(1)} %get-tuple-element.38), channel_id=1, source_target_pairs={{0,5},{1,6},{2,7},{3,8},{4,9},{5,10},{6,11},{7,12},{8,13},{9,14},{... | collective-permute-start | bytes 73736 | tf_op jit(solution)/shard_map/ppermute | solution.py:14
  62.1 13.5 %collective-permute-start.1 = (f32[24,256]{1,0:T(8,128)S(1)}, f32[24,256]{1,0:T(8,128)S(1)}, u32[]{:S(2)}, u32[]{:S(2)}) collective-permute-start(f32[24,256]{1,0:T(8,128)S(1)} %get-tuple-element.37), channel_id=1, source_target_pairs={{0,4},{1,5},{2,6},{3,7},{4,8},{5,9},{6,10},{7,11},{8,12},{9,13},{1... | collective-permute-start | bytes 73736 | tf_op jit(solution)/shard_map/ppermute | solution.py:14
  63.4 13.5 %collective-permute-start.2 = (f32[24,256]{1,0:T(8,128)S(1)}, f32[24,256]{1,0:T(8,128)S(1)}, u32[]{:S(2)}, u32[]{:S(2)}) collective-permute-start(f32[24,256]{1,0:T(8,128)S(1)} %get-tuple-element.36), channel_id=1, source_target_pairs={{0,3},{1,4},{2,5},{3,6},{4,7},{5,8},{6,9},{7,10},{8,11},{9,12},{10... | collective-permute-start | bytes 73736 | tf_op jit(solution)/shard_map/ppermute | solution.py:14
  64.7 13.5 %collective-permute-start.3 = (f32[24,256]{1,0:T(8,128)S(1)}, f32[24,256]{1,0:T(8,128)S(1)}, u32[]{:S(2)}, u32[]{:S(2)}) collective-permute-start(f32[24,256]{1,0:T(8,128)S(1)} %get-tuple-element.35), channel_id=1, source_target_pairs={{0,1},{1,2},{2,3},{3,4},{4,5},{5,6},{6,7},{7,8},{8,9},{9,10},{10,1... | collective-permute-start | bytes 73736 | tf_op jit(solution)/shard_map/ppermute | solution.py:14
  71.5 6.7 %collective-permute-start.4 = (f32[24,256]{1,0:T(8,128)S(1)}, f32[24,256]{1,0:T(8,128)S(1)}, u32[]{:S(2)}, u32[]{:S(2)}) collective-permute-start(f32[24,256]{1,0:T(8,128)S(1)} %get-tuple-element.34), channel_id=1, source_target_pairs={{1,0},{2,1},{3,2},{4,3},{5,4},{6,5},{7,6},{8,7},{9,8},{10,9},{11,1... | collective-permute-start | bytes 73736 | tf_op jit(solution)/shard_map/ppermute | solution.py:14
  74.3 5.1 collective-permute-start.5
  75.6 5.3 collective-permute-start.6
  76.9 7.6 %collective-permute-start.7 = (f32[24,256]{1,0:T(8,128)S(1)}, f32[24,256]{1,0:T(8,128)S(1)}, u32[]{:S(2)}, u32[]{:S(2)}) collective-permute-start(f32[24,256]{1,0:T(8,128)S(1)} %get-tuple-element.31), channel_id=1, source_target_pairs={{5,0},{6,1},{7,2},{8,3},{9,4},{10,5},{11,6},{12,7},{13,8},{14,9},{... | collective-permute-start | bytes 73736 | tf_op jit(solution)/shard_map/ppermute | solution.py:14
  87.9 15.0 %collective-permute-start.16 = (bf16[2,24,256]{2,0,1:T(2,128)(2,1)S(1)}, bf16[2,24,256]{2,0,1:T(2,128)(2,1)S(1)}, u32[]{:S(2)}, u32[]{:S(2)}) collective-permute-start(bf16[2,24,256]{2,0,1:T(2,128)(2,1)S(1)} %broadcast_select_fusion.17), channel_id=1, source_target_pairs={{5,0},{6,1},{7,2},{8,3},{9,4},{10,5},{11,6},{12,7},{13,8},{14,9},{... | collective-permute-start | bytes 73736 | tf_op jit(solution)/shard_map/ppermute | solution.py:14
  89.9 18.2 %collective-permute-start.17 = (bf16[2,24,256]{2,0,1:T(2,128)(2,1)S(1)}, bf16[2,24,256]{2,0,1:T(2,128)(2,1)S(1)}, u32[]{:S(2)}, u32[]{:S(2)}) collective-permute-start(bf16[2,24,256]{2,0,1:T(2,128)(2,1)S(1)} %broadcast_select_fusion.16), channel_id=1, source_target_pairs={{4,0},{5,1},{6,2},{7,3},{8,4},{9,5},{10,6},{11,7},{12,8},{13,9},{1... | collective-permute-start | bytes 73736 | tf_op jit(solution)/shard_map/ppermute | solution.py:14
  92.0 22.6 %collective-permute-start.18 = (bf16[2,24,256]{2,0,1:T(2,128)(2,1)S(1)}, bf16[2,24,256]{2,0,1:T(2,128)(2,1)S(1)}, u32[]{:S(2)}, u32[]{:S(2)}) collective-permute-start(bf16[2,24,256]{2,0,1:T(2,128)(2,1)S(1)} %broadcast_select_fusion.15), channel_id=1, source_target_pairs={{3,0},{4,1},{5,2},{6,3},{7,4},{8,5},{9,6},{10,7},{11,8},{12,9},{13... | collective-permute-start | bytes 73736 | tf_op jit(solution)/shard_map/ppermute | solution.py:14
  94.0 23.5 %collective-permute-start.19 = (bf16[2,24,256]{2,0,1:T(2,128)(2,1)S(1)}, bf16[2,24,256]{2,0,1:T(2,128)(2,1)S(1)}, u32[]{:S(2)}, u32[]{:S(2)}) collective-permute-start(bf16[2,24,256]{2,0,1:T(2,128)(2,1)S(1)} %broadcast_select_fusion.14), channel_id=1, source_target_pairs={{1,0},{2,1},{3,2},{4,3},{5,4},{6,5},{7,6},{8,7},{9,8},{10,9},{11,1... | collective-permute-start | bytes 73736 | tf_op jit(solution)/shard_map/ppermute | solution.py:14
  97.5 20.1 %collective-permute-start.20 = (bf16[2,24,256]{2,0,1:T(2,128)(2,1)S(1)}, bf16[2,24,256]{2,0,1:T(2,128)(2,1)S(1)}, u32[]{:S(2)}, u32[]{:S(2)}) collective-permute-start(bf16[2,24,256]{2,0,1:T(2,128)(2,1)S(1)} %broadcast_select_fusion.13), channel_id=1, source_target_pairs={{0,1},{1,2},{2,3},{3,4},{4,5},{5,6},{6,7},{7,8},{8,9},{9,10},{10,1... | collective-permute-start | bytes 73736 | tf_op jit(solution)/shard_map/ppermute | solution.py:14
  102.9 14.8 %collective-permute-start.21 = (bf16[2,24,256]{2,0,1:T(2,128)(2,1)S(1)}, bf16[2,24,256]{2,0,1:T(2,128)(2,1)S(1)}, u32[]{:S(2)}, u32[]{:S(2)}) collective-permute-start(bf16[2,24,256]{2,0,1:T(2,128)(2,1)S(1)} %broadcast_select_fusion.12), channel_id=1, source_target_pairs={{0,3},{1,4},{2,5},{3,6},{4,7},{5,8},{6,9},{7,10},{8,11},{9,12},{10... | collective-permute-start | bytes 73736 | tf_op jit(solution)/shard_map/ppermute | solution.py:14
  108.2 9.5 %collective-permute-start.22 = (bf16[2,24,256]{2,0,1:T(2,128)(2,1)S(1)}, bf16[2,24,256]{2,0,1:T(2,128)(2,1)S(1)}, u32[]{:S(2)}, u32[]{:S(2)}) collective-permute-start(bf16[2,24,256]{2,0,1:T(2,128)(2,1)S(1)} %broadcast_select_fusion.11), channel_id=1, source_target_pairs={{0,4},{1,5},{2,6},{3,7},{4,8},{5,9},{6,10},{7,11},{8,12},{9,13},{1... | collective-permute-start | bytes 73736 | tf_op jit(solution)/shard_map/ppermute | solution.py:14
  114.6 4.2 collective-permute-start.23
  172.4 8.7 %copy-start.11 = (s32[1,64,3]{1,0,2:T(1,128)S(1)}, s32[1,64,3]{1,0,2:T(1,128)}, u32[]{:S(2)}) copy-start(s32[1,64,3]{1,0,2:T(1,128)} %param.19) | copy-start | bytes 2308
  172.4 41.6 %all-to-all-start.1 = ((bf16[192,4,1728]{2,0,1:T(8,128)(2,1)}), bf16[192,4,1728]{2,0,1:T(8,128)(2,1)}, u32[]{:S(2)}, u32[]{:S(2)}) async-start(bf16[192,4,1728]{2,0,1:T(8,128)(2,1)} %copy.68), calls=%async_computation.1 | async-start | bytes 5505024 | tf_op jit(solution)/shard_map/all_to_all | solution.py:58
  190.2 70.1 %copy-start.2 = (bf16[256,6912]{1,0:T(8,128)(2,1)S(1)}, bf16[256,6912]{1,0:T(8,128)(2,1)}, u32[]{:S(2)}) copy-start(bf16[256,6912]{1,0:T(8,128)(2,1)} %param.15) | copy-start | bytes 10616836
  214.0 132.4 %all-to-all-start.2 = ((bf16[192,4,1728]{2,0,1:T(8,128)(2,1)}), bf16[192,4,1728]{2,0,1:T(8,128)(2,1)}, u32[]{:S(2)}, u32[]{:S(2)}) async-start(bf16[192,4,1728]{2,0,1:T(8,128)(2,1)} %copy.71), calls=%async_computation.2 | async-start | bytes 5505024 | tf_op jit(solution)/shard_map/all_to_all | solution.py:58
  220.5 340.9 %all-reduce.5.cloned.1.call-start = ((), (), s32[]{:S(2)}) async-start(), calls=%async_computation.3 | async-start | bytes 7340032
  264.3 43.5 %copy-start.4 = (bf16[192,256]{1,0:T(8,128)(2,1)S(1)}, bf16[192,256]{1,0:T(8,128)(2,1)}, u32[]{:S(2)}) copy-start(bf16[192,256]{1,0:T(8,128)(2,1)} %get-tuple-element.42) | copy-start | bytes 294916
  271.2 75.2 %copy-start.6 = (bf16[768,256]{1,0:T(8,128)(2,1)S(1)}, bf16[768,256]{1,0:T(8,128)(2,1)}, u32[]{:S(2)}) copy-start(bf16[768,256]{1,0:T(8,128)(2,1)} %all_gather.7) | copy-start | bytes 1179652
  304.9 41.5 %copy-start.3 = (f32[385,256]{1,0:T(8,128)}, f32[385,256]{1,0:T(8,128)S(1)}, u32[]{:S(2)}) copy-start(f32[385,256]{1,0:T(8,128)S(1)} %scatter_custom_fusion.2) | copy-start | bytes 1182724
  305.7 32.5 %collective-permute-start.8 = (f32[24,256]{1,0:T(8,128)S(1)}, f32[24,256]{1,0:T(8,128)S(1)}, u32[]{:S(2)}, u32[]{:S(2)}) collective-permute-start(f32[24,256]{1,0:T(8,128)S(1)} %get-tuple-element.30), channel_id=1, source_target_pairs={{0,5},{1,6},{2,7},{3,8},{4,9},{5,10},{6,11},{7,12},{8,13},{9,14},{... | collective-permute-start | bytes 73736 | tf_op jit(solution)/shard_map/ppermute | solution.py:14
  327.0 12.5 %collective-permute-start.9 = (f32[24,256]{1,0:T(8,128)S(1)}, f32[24,256]{1,0:T(8,128)S(1)}, u32[]{:S(2)}, u32[]{:S(2)}) collective-permute-start(f32[24,256]{1,0:T(8,128)S(1)} %get-tuple-element.29), channel_id=1, source_target_pairs={{0,4},{1,5},{2,6},{3,7},{4,8},{5,9},{6,10},{7,11},{8,12},{9,13},{1... | collective-permute-start | bytes 73736 | tf_op jit(solution)/shard_map/ppermute | solution.py:14
  328.3 12.5 %collective-permute-start.10 = (f32[24,256]{1,0:T(8,128)S(1)}, f32[24,256]{1,0:T(8,128)S(1)}, u32[]{:S(2)}, u32[]{:S(2)}) collective-permute-start(f32[24,256]{1,0:T(8,128)S(1)} %get-tuple-element.28), channel_id=1, source_target_pairs={{0,3},{1,4},{2,5},{3,6},{4,7},{5,8},{6,9},{7,10},{8,11},{9,12},{10... | collective-permute-start | bytes 73736 | tf_op jit(solution)/shard_map/ppermute | solution.py:14
  331.7 19.1 %collective-permute-start.11 = (f32[24,256]{1,0:T(8,128)}, f32[24,256]{1,0:T(8,128)}, u32[]{:S(2)}, u32[]{:S(2)}) collective-permute-start(f32[24,256]{1,0:T(8,128)} %get-tuple-element.27), channel_id=1, source_target_pairs={{0,1},{1,2},{2,3},{3,4},{4,5},{5,6},{6,7},{7,8},{8,9},{9,10},{10,1... | collective-permute-start | bytes 73736 | tf_op jit(solution)/shard_map/ppermute | solution.py:14
  334.3 18.0 %collective-permute-start.12 = (f32[24,256]{1,0:T(8,128)}, f32[24,256]{1,0:T(8,128)}, u32[]{:S(2)}, u32[]{:S(2)}) collective-permute-start(f32[24,256]{1,0:T(8,128)} %get-tuple-element.26), channel_id=1, source_target_pairs={{1,0},{2,1},{3,2},{4,3},{5,4},{6,5},{7,6},{8,7},{9,8},{10,9},{11,1... | collective-permute-start | bytes 73736 | tf_op jit(solution)/shard_map/ppermute | solution.py:14
  338.2 15.5 %collective-permute-start.13 = (f32[24,256]{1,0:T(8,128)}, f32[24,256]{1,0:T(8,128)}, u32[]{:S(2)}, u32[]{:S(2)}) collective-permute-start(f32[24,256]{1,0:T(8,128)} %get-tuple-element.25), channel_id=1, source_target_pairs={{3,0},{4,1},{5,2},{6,3},{7,4},{8,5},{9,6},{10,7},{11,8},{12,9},{13... | collective-permute-start | bytes 73736 | tf_op jit(solution)/shard_map/ppermute | solution.py:14
  339.5 15.5 %collective-permute-start.14 = (f32[24,256]{1,0:T(8,128)}, f32[24,256]{1,0:T(8,128)}, u32[]{:S(2)}, u32[]{:S(2)}) collective-permute-start(f32[24,256]{1,0:T(8,128)} %get-tuple-element.24), channel_id=1, source_target_pairs={{4,0},{5,1},{6,2},{7,3},{8,4},{9,5},{10,6},{11,7},{12,8},{13,9},{1... | collective-permute-start | bytes 73736 | tf_op jit(solution)/shard_map/ppermute | solution.py:14
  340.8 15.6 %collective-permute-start.15 = (f32[24,256]{1,0:T(8,128)}, f32[24,256]{1,0:T(8,128)}, u32[]{:S(2)}, u32[]{:S(2)}) collective-permute-start(f32[24,256]{1,0:T(8,128)} %get-tuple-element.23), channel_id=1, source_target_pairs={{5,0},{6,1},{7,2},{8,3},{9,4},{10,5},{11,6},{12,7},{13,8},{14,9},{... | collective-permute-start | bytes 73736 | tf_op jit(solution)/shard_map/ppermute | solution.py:14
  342.4 4.0 copy-start.12
  350.8 212.0 %copy-start.1 = (bf16[256,6912]{1,0:T(8,128)(2,1)S(1)}, bf16[256,6912]{1,0:T(8,128)(2,1)}, u32[]{:S(2)}) copy-start(bf16[256,6912]{1,0:T(8,128)(2,1)} %param.16) | copy-start | bytes 10616836
  368.0 34.4 %all-to-all-start = ((bf16[64,3,256]{2,1,0:T(4,128)(2,1)}), bf16[64,3,256]{2,1,0:T(4,128)(2,1)}, u32[]{:S(2)}, u32[]{:S(2)}) async-start(bf16[64,3,256]{2,1,0:T(4,128)(2,1)} %select_select_fusion), calls=%async_computation | async-start | bytes 262144 | tf_op jit(solution)/shard_map/all_to_all | solution.py:117
Sparse Core Ops, SparseCore 0:
  351.0 210.3 all-reduce.4
where the time goes:
time: 572 us; the launch traced here: 570 us
  waiting for transfers between devices  197 us (34%)
  starting transfers between devices  101 us (18%)
  other arithmetic  92.9 us (16%)
  local copies, waits for them, and re-layouts  88.9 us (16%)
  blocking collectives  58.9 us (10%)
  between operations  15.5 us (3%)
  matrix products  14.9 us (3%)
    unnamed x2, waiting for transfers between devices  157 us
    scatter-add x2, other arithmetic, input_grad(): jax.ops.segment_sum(spread.reshape(-1, channel_count), where_to.reshape(-...  67.3 us
    ppermute x24, starting transfers between devices, shifted(): lax.ppermute(value, axis, [(source, source + steps) for source in range(i...  62.3 us
    all_gather x2, blocking collectives, weight_sum(): all_grads = lax.all_gather(gradient, 'gy', axis=0, tiled=True)  58.9 us
    gather x4, local copies, waits for them, and re-layouts, unfold(): return jnp.take(extended, where_to, axis=0).reshape(slot_count, -1)  36.3 us
    all_to_all x1, starting transfers between devices, body(): lax.all_to_all(outgoing_rows, 'gx', split_axis=0, concat_axis=0, tiled=True)  23.9 us
    all_to_all x2, waiting for transfers between devices, weight_sum(): lax.all_to_all(columns, 'gy', split_axis=1, concat_axis=0, tiled=True)  23.8 us
    all_to_all x4, local copies, waits for them, and re-layouts, weight_sum(): lax.all_to_all(columns, 'gy', split_axis=1, concat_axis=0, tiled=True)  19.1 us
  transfers between devices with their start and end apart: 28, of which 7 were waited for; matrix products, arithmetic and copies ran while one was open for 15% of the time, Pallas kernels for 0%

commit v1 on v0

v1 whole, which is shorter than its diff:
```python
import math

import jax
import jax.numpy as jnp
from jax import lax
from jax.experimental import pallas as pl
from jax.experimental.pallas import tpu as pltpu
from jax.sharding import PartitionSpec as P

C = 256
K = 27
S = 192
HB = 32
EXT = S + 8 * HB
QW = 1728
BF = jnp.bfloat16
F32 = jnp.float32
KSTEP = 3


def iota(shape, dim):
    return lax.broadcasted_iota(jnp.int32, shape, dim)


def onehot(mask):
    return jnp.where(mask, 1.0, 0.0).astype(BF)


def mm(a, b):
    return lax.dot_general(a, b, (((1,), (0,)), ((), ())), preferred_element_type=F32)


def mm_t(a, b):
    return lax.dot_general(a, b, (((0,), (0,)), ((), ())), preferred_element_type=F32)


def direction(a, b):
    grid = 3 * (a + 1) + (b + 1)
    return grid - jnp.where(grid > 4, 1, 0)


def channel_order():
    out = iota((C, C), 1)
    parity, rest = out // 128, out % 128
    source = 8 * (rest // 4) + 4 * parity + rest % 4
    return onehot(iota((C, C), 0) == source)


def halo_matrix(halo_row):
    return onehot(iota((S, 8 * HB), 0) == halo_row)


def pack_kernel(feat, pre, grad, nbr, halo, pay, nbt, hrow, wide):
    wide[...] = jnp.full(wide.shape, -1.0, F32)
    wide[0:S, 0:K] = nbr[...].astype(F32)
    table = jnp.transpose(wide[...])[0:32, :]
    halo_id = table - S
    heading = jnp.floor((halo_id + 0.5) * (1.0 / 24.0))
    table = jnp.where(table >= S, table + 8.0 * heading, table)
    nbt[...] = table
    shifted_up = table[:, 0:S] + 1.0
    high = jnp.floor(shifted_up * (1.0 / 16.0))
    z = pre[...].astype(F32)
    pay[0:S, 0:C] = feat[...]
    pay[0:S, C : 2 * C] = (z * (1.0 / (1.0 + jnp.exp(-z)))).astype(BF)
    pay[0:S, 2 * C : 3 * C] = mm(grad[...], channel_order()).astype(BF)
    halo_up = (halo[0] + 1).astype(F32).astype(BF)
    spread = mm(halo_up, onehot(iota((24, 8 * HB), 1) % HB == iota((24, 8 * HB), 0)))
    row = jnp.sum(
        jnp.where(iota((8, 8 * HB), 1) // HB == iota((8, 8 * HB), 0), spread, 0.0),
        axis=0,
        keepdims=True,
    )
    hrow[...] = jnp.broadcast_to(row.astype(jnp.int32) - 1, hrow.shape)
    pay[S : S + 32, :] = jnp.zeros((32, 3 * C), BF)
    pay[S : S + 32, 0:S] = high.astype(BF)
    pay[S : S + 32, C : C + S] = (shifted_up - 16.0 * high).astype(BF)
    pay[S : S + 32, 2 * C : 3 * C] = jnp.broadcast_to(row, (32, C)).astype(BF)


def spread_kernel(place, nbt, grad, weight, own, m1, m2, loc, acc):
    step = pl.program_id(0)

    @pl.when(step == 0)
    def _():
        acc[...] = jnp.zeros(acc.shape, F32)

    total = acc[...]
    terms = mm(grad[...], weight[...]).astype(BF)
    rows = iota((EXT, S), 0)
    for part in range(KSTEP):
        ids = nbt[pl.ds(step * KSTEP + part, 1), 0:S].astype(jnp.int32)
        total = total + mm(onehot(rows == ids), terms[:, part * C : (part + 1) * C])
    acc[...] = total

    @pl.when(step == K // KSTEP - 1)
    def _():
        even = place[0] % 2 == 0
        own[...] = acc[0:S, :]
        first, last = jnp.where(even, S, S + 160), jnp.where(even, S + 160, S)
        m1[...] = acc[pl.ds(pl.multiple_of(first, 32), 96), :].astype(BF)
        m2[...] = acc[pl.ds(pl.multiple_of(last, 32), 96), :].astype(BF)
        loc[...] = acc[S + 96 : S + 160, :].astype(BF)


def pass_kernel(place, loc, m1, m2, n1, n2):
    even = place[1] % 2 == 0
    first = jnp.where(even, 0, 1)
    for out, side in ((n1, first), (n2, 1 - first)):
        out[0:32, :] = loc[pl.ds(pl.multiple_of(side * 32, 32), 32), :]
        out[32:64, :] = m1[pl.ds(pl.multiple_of(side * 64, 32), 32), :]
        out[64:96, :] = m2[pl.ds(pl.multiple_of(side * 64, 32), 32), :]


def settled(place, own, m1, m2, n1, n2, hrow, back):
    da = jnp.where(place[0] % 2 == 0, 1, -1)
    db = jnp.where(place[1] % 2 == 0, 1, -1)
    back[direction(da, 0)] = m1[32:64, :]
    back[direction(-da, 0)] = m2[32:64, :]
    for ref, side in ((n1, db), (n2, -db)):
        back[direction(0, side)] = ref[0:32, :]
        back[direction(da, side)] = ref[32:64, :]
        back[direction(-da, side)] = ref[64:96, :]
    rows = back[...].reshape(8 * HB, C)
    return own[...] + mm(halo_matrix(hrow[0:1, :]), rows)


def gate_kernel(place, own, m1, m2, n1, n2, hrow, pre, out, ordered, back):
    hidden_grad = settled(place, own, m1, m2, n1, n2, hrow, back)
    z = pre[...].astype(F32)
    g = 1.0 / (1.0 + jnp.exp(-z))
    value = (hidden_grad * g * (1.0 + z * (1.0 - g))).astype(BF)
    out[...] = value
    ordered[...] = mm(value, channel_order()).astype(BF)


def rows_kernel(place, own, m1, m2, n1, n2, hrow, grad, send, out, back):
    total = settled(place, own, m1, m2, n1, n2, hrow, back)
    value = (grad[...].astype(F32) + total).astype(BF)
    chosen = onehot(iota((S, S), 0) == send[...])
    out[...] = mm_t(chosen, value).astype(BF)


def pick_kernel(place, p0, p1, p2, p3, o1, o2, loc, picked):
    column = place[1]
    for turn, pay in enumerate((p0, p1, p2, p3)):
        halo_row = pay[S : S + 16, 2 * C : 3 * C].astype(F32)[0:1, :].astype(jnp.int32) - 1
        rows = mm_t(halo_matrix(halo_row), pay[0:S, 0 : 2 * C])
        picked[column ^ turn] = rows.astype(BF)
    even = place[0] % 2 == 0
    up = pl.multiple_of(jnp.where(even, 160, 0), 32)
    down = pl.multiple_of(jnp.where(even, 0, 160), 32)
    none = jnp.zeros((HB, 2 * C), BF)
    for tile in range(4):
        for b in (-1, 0, 1):
            source = tile - b
            at = HB * (b + 1)
            inside = 0 <= source < 4
            o1[tile, at : at + HB, :] = picked[source, pl.ds(up + at, HB), :] if inside else none
            o2[tile, at : at + HB, :] = picked[source, pl.ds(down + at, HB), :] if inside else none
            if b:
                to = 0 if b < 0 else HB
                loc[tile, to : to + HB, :] = (
                    picked[source, 96 + to : 96 + to + HB, :] if inside else none
                )


def columns_kernel(
    place, p0, p1, p2, p3, r1, r2, loc, keep, send, cols_one, cols_two, ext, gt, ids, sel
):
    column = place[1]
    start = column * QW
    first_k = start // C
    offset = start % C
    even = place[0] % 2 == 0
    shift = onehot(iota((C, C), 0) == (iota((C, C), 1) + offset) % C)
    lane = iota((S, 2 * C), 1) % C
    early = lane < C - offset
    for turn, pay in enumerate((p0, p1, p2, p3)):
        tile = column ^ turn
        above, below = r1[tile], r2[tile]
        pieces = (
            (0, pay[0:S, 0 : 2 * C]),
            (S, jnp.where(even, above, below)),
            (S + 96, loc[tile]),
            (S + 160, jnp.where(even, below, above)),
        )
        for at, piece in pieces:
            size = piece.shape[0]
            ext[at : at + size, 0:C] = mm(piece[:, 0:C], shift).astype(BF)
            ext[at : at + size, C : 2 * C] = mm(piece[:, C : 2 * C], shift).astype(BF)
        gt[:, turn * S : (turn + 1) * S] = jnp.transpose(
            pay[0:S, 2 * C : 3 * C].astype(F32)
        ).astype(BF)
        high = pay[S : S + 32, 0:C].astype(F32)
        low = pay[S : S + 32, C : 2 * C].astype(F32)
        ids[0:32, :] = 16.0 * high + low - 1.0
        for part in range(8):
            sel[part : part + 1, :] = ids[pl.ds(first_k + part, 1), :]
        table = jnp.transpose(sel[...])[:, 0:8].astype(jnp.int32)
        extended = ext[...]
        previous = None
        for part in range(8):
            match = onehot(iota((S, EXT), 1) == table[0:S, part : part + 1])
            block = mm(match, extended).astype(BF)
            if part:
                merged = jnp.where(early, previous, block)
                at = (part - 1) * C
                cols_one[turn * S : (turn + 1) * S, at : at + C] = merged[:, 0:C]
                cols_two[turn * S : (turn + 1) * S, at : at + C] = merged[:, C : 2 * C]
            previous = block
    weight_blocks(place, gt, cols_two, keep, send)


def weight_blocks(place, gt, cols, keep, send):
    mine = pl.multiple_of((place[0] % 2) * 128, 128)
    other = pl.multiple_of(128 - mine, 128)
    for out, at in ((keep, mine), (send, other)):
        left = gt[pl.ds(at, 128), :]
        for part in range(7):
            out[:, part * C : (part + 1) * C] = mm(
                left, cols[:, part * C : (part + 1) * C]
            ).astype(BF)


def weight_kernel(place, g0, g1, g2, g3, cols, keep, send, gt):
    for turn, grad in enumerate((g0, g1, g2, g3)):
        gt[:, turn * S : (turn + 1) * S] = jnp.transpose(grad[...].astype(F32)).astype(BF)
    weight_blocks(place, gt, cols, keep, send)


def merge_kernel(k1, s1, k2, s2, out):
    row, col = iota((C, 128), 0), iota((C, 128), 1)
    for part in range(7):
        at = slice(part * C, (part + 1) * C)
        total = jnp.zeros((C, C), F32)
        for which, refs in enumerate(((k1, s1), (k2, s2))):
            place_of = onehot((row // 8 == col // 4) & (row % 8 == 4 * which + col % 4))
            for ref in refs:
                total = total + mm(place_of, ref[:, at])
        out[:, at] = total.astype(BF)


def final_kernel(scale, arrived, one, two):
    total = jnp.sum(arrived[...].astype(F32), axis=0) * scale
    one[...] = total[0:4, 0:QW]
    two[...] = total[4:8, 0:QW]


def sds(shape, dtype):
    return jax.ShapeDtypeStruct(shape, dtype)


SMEM = pl.BlockSpec(memory_space=pltpu.SMEM)
VM = pl.BlockSpec(memory_space=pltpu.VMEM)


def call(kernel, outs, *args, scratch=(), scalars=0, flops=10**8):
    return pl.pallas_call(
        kernel,
        out_shape=outs,
        in_specs=[SMEM] * scalars + [VM] * (len(args) - scalars),
        out_specs=jax.tree.map(lambda _: VM, outs),
        scratch_shapes=list(scratch),
        compiler_params=pltpu.CompilerParams(vmem_limit_bytes=40 * 2**20),
        cost_estimate=pl.CostEstimate(flops=flops, bytes_accessed=10**6, transcendentals=0),
    )(*args)


def spread(place, nbt, grad, weight):
    whole = lambda shape: pl.BlockSpec(shape, lambda n: (0,) * len(shape))
    return pl.pallas_call(
        spread_kernel,
        grid=(K // KSTEP,),
        out_shape=(sds((S, C), F32), sds((96, C), BF), sds((96, C), BF), sds((64, C), BF)),
        in_specs=[
            SMEM,
            whole((32, C)),
            whole((S, C)),
            pl.BlockSpec((C, KSTEP * C), lambda n: (0, n)),
        ],
        out_specs=(whole((S, C)), whole((96, C)), whole((96, C)), whole((64, C))),
        scratch_shapes=[pltpu.VMEM((EXT, C), F32)],
        compiler_params=pltpu.CompilerParams(vmem_limit_bytes=40 * 2**20),
        cost_estimate=pl.CostEstimate(
            flops=4 * 10**9, bytes_accessed=4 * 10**6, transcendentals=0
        ),
    )(place, nbt, grad, weight)


def partners(count, turn):
    if turn == 0:
        return list(range(count))
    if turn == 1:
        return [n ^ 1 for n in range(count)]
    pairs = [n - 1 if n % 2 == 0 else n + 1 for n in range(count)]
    return [n if 0 <= n < count else None for n in pairs]


def swap(value, axis, turn):
    pairs = [(n, q) for n, q in enumerate(partners(lax.axis_size(axis), turn)) if q is not None]
    return lax.ppermute(value, axis, pairs)


def cross(value, axis, mask):
    return lax.ppermute(value, axis, [(n, n ^ mask) for n in range(lax.axis_size(axis))])


def give_back(place, loc, m1, m2):
    m1, m2 = swap(m1, "gx", 1), swap(m2, "gx", 2)
    n1, n2 = call(
        pass_kernel, (sds((96, C), BF), sds((96, C), BF)), place, loc, m1, m2, scalars=1
    )
    return m1, m2, swap(n1, "gy", 1), swap(n2, "gy", 2)


def body(features, pre_act, grad_out, weight_one, weight_two, neighbours, halo_list, send_list):
    gx = lax.axis_size("gx")
    scale = 1.0 / math.sqrt(S * gx * lax.axis_size("gy"))
    place = jnp.stack([lax.axis_index("gx"), lax.axis_index("gy")]).astype(jnp.int32)
    pay, nbt, hrow = call(
        pack_kernel,
        (sds((S + 32, 3 * C), BF), sds((32, C), F32), sds((8, C), jnp.int32)),
        features,
        pre_act,
        grad_out,
        neighbours,
        halo_list,
        scratch=[pltpu.VMEM((C, 128), F32)],
    )
    pays = [pay] + [cross(pay, "gy", d) for d in (1, 2, 3)]
    own, m1, m2, loc = spread(place, nbt, grad_out, weight_two)
    m1, m2, n1, n2 = give_back(place, loc, m1, m2)
    back = pltpu.VMEM((8, HB, C), BF)
    grad_pre, ordered = call(
        gate_kernel,
        (sds((S, C), BF), sds((S, C), BF)),
        place,
        own,
        m1,
        m2,
        n1,
        n2,
        hrow,
        pre_act,
        scratch=[back],
        scalars=1,
    )
    grads = [ordered] + [cross(ordered, "gy", d) for d in (1, 2, 3)]
    own, m1, m2, loc = spread(place, nbt, grad_pre, weight_one)
    m1, m2, n1, n2 = give_back(place, loc, m1, m2)
    send = send_list.reshape(1, S)
    rows = call(
        rows_kernel,
        sds((S, C), BF),
        place,
        own,
        m1,
        m2,
        n1,
        n2,
        hrow,
        grad_out,
        send,
        scratch=[back],
        scalars=1,
    )
    balanced = lax.all_to_all(
        rows.reshape(gx, S // gx, C), "gx", split_axis=0, concat_axis=0, tiled=True
    ).reshape(S, C)

    picks = sds((4, 96, 2 * C), BF)
    o1, o2, near = call(
        pick_kernel,
        (picks, picks, sds((4, 64, 2 * C), BF)),
        place,
        *pays,
        scratch=[pltpu.VMEM((4, 8 * HB, 2 * C), BF)],
        scalars=1,
    )
    r1, r2 = swap(o1, "gx", 1), swap(o2, "gx", 2)
    wide = 7 * C
    half = sds((128, wide), BF)
    keep_two, send_two, cols_one = call(
        columns_kernel,
        (half, half, sds((4 * S, wide), BF)),
        place,
        *pays,
        r1,
        r2,
        near,
        scratch=[
            pltpu.VMEM((4 * S, wide), BF),
            pltpu.VMEM((EXT, 2 * C), BF),
            pltpu.VMEM((C, 4 * S), BF),
            pltpu.VMEM((32, C), F32),
            pltpu.VMEM((128, C), F32),
        ],
        scalars=1,
        flops=4 * 10**9,
    )
    come_two = cross(send_two, "gx", 1)
    keep_one, send_one = call(
        weight_kernel,
        (half, half),
        place,
        *grads,
        cols_one,
        scratch=[pltpu.VMEM((C, 4 * S), BF)],
        scalars=1,
        flops=10**9,
    )
    come_one = cross(send_one, "gx", 1)
    merged = call(merge_kernel, sds((C, wide), BF), keep_one, come_one, keep_two, come_two)
    groups = [[2 * c + e for c in range(gx // 2)] for e in range(2)]
    arrived = lax.all_to_all(
        merged.reshape(gx // 2, 8, wide),
        "gx",
        split_axis=0,
        concat_axis=0,
        tiled=True,
        axis_index_groups=groups,
    )
    out = sds((4, QW), F32)
    grad_one, grad_two = call(lambda *refs: final_kernel(scale, *refs), (out, out), arrived)
    return balanced, grad_one, grad_two


def solution(mesh):
    in_specs = (
        P(("gx", "gy"), None),
        P(("gx", "gy"), None),
        P(("gx", "gy"), None),
        P(),
        P(),
        P(("gx", "gy"), None),
        P(("gx", "gy"), None, None),
        P(("gx", "gy"), None, None),
    )
    out_specs = (P(("gx", "gy"), None), P("gx", "gy"), P("gx", "gy"))
    return jax.shard_map(body, mesh=mesh, in_specs=in_specs, out_specs=out_specs, check_vma=False)
```

time: 572 us -> 143 us (0.25)
  waiting for transfers between devices: 197 us -> 57 us
  other arithmetic: 92.9 us -> 0.07 us
  local copies, waits for them, and re-layouts: 88.9 us -> 8.78 us
  blocking collectives: 58.9 us -> 0 us
  starting transfers between devices: 101 us -> 48.9 us
  Pallas kernels: 0 us -> 26.7 us
  matrix products: 14.9 us -> 0 us
  between operations: 15.5 us -> 0.88 us
    unnamed x2 -> x0, waiting for transfers between devices: 157 us -> none
    scatter-add x4 -> x0, other arithmetic: 71.6 us -> none  [the longest x2 67.3 us: input_grad(): jax.ops.segment_sum(spread.reshape(-1, channel_count), where_to.reshape(-...]
    all_gather x2 -> x0, blocking collectives: 58.9 us -> none  [weight_sum(): all_grads = lax.all_gather(gradient, 'gy', axis=0, tiled=True)]
    gather x14 -> x0, local copies, waits for them, and re-layouts: 45.2 us -> none  [the longest x4 36.3 us: unfold(): return jnp.take(extended, where_to, axis=0).reshape(slot_count, -1)]
    ppermute x24 -> x18, starting transfers between devices: 62.3 us -> 24.7 us  [the longest x10 14.5 us: swap(): return lax.ppermute(value, axis, pairs)]
    pallas_call x0 -> x12, Pallas kernels: none -> 26.7 us  [the longest x10 14.6 us: call(): pl.pallas_call(kernel, out_shape=outs, in_specs=[SMEM] * scalars + [VM] *...]
    all_to_all x4 -> x0, local copies, waits for them, and re-layouts: 19.1 us -> none  [weight_sum(): lax.all_to_all(columns, 'gy', split_axis=1, concat_axis=0, tiled=True)]
    ppermute x24 -> x18, waiting for transfers between devices: 7.37 us -> 23.3 us  [the longest x8 15.7 us: cross(): lax.ppermute(value, axis, [(n, n ^ mask) for n in range(lax.axis_size(axi...]
  transfers between devices with their start and end apart: 28 -> 20, of which waited for: 7 -> 11; matrix products, arithmetic and copies ran while one was open for 15% -> 1% of each run, Pallas kernels for 0% -> 16%
where the time goes in v1:
time: 143 us; the launch traced here: 142 us
  waiting for transfers between devices  57 us (40%)
  starting transfers between devices  48.9 us (34%)
  Pallas kernels  26.7 us (19%)
  local copies, waits for them, and re-layouts  8.78 us (6%)
    all_to_all x1, waiting for transfers between devices, body(): lax.all_to_all(merged.reshape(gx // 2, 8, wide), 'gx', split_axis=0, conc...  25.4 us
    all_to_all x1, starting transfers between devices, body(): lax.all_to_all(rows.reshape(gx, S // gx, C), 'gx', split_axis=0, concat_a...  19.9 us
    ppermute x8, waiting for transfers between devices, cross(): lax.ppermute(value, axis, [(n, n ^ mask) for n in range(lax.axis_size(axi...  15.7 us
    pallas_call x10, Pallas kernels, call(): pl.pallas_call(kernel, out_shape=outs, in_specs=[SMEM] * scalars + [VM] *...  14.6 us
    ppermute x10, starting transfers between devices, swap(): return lax.ppermute(value, axis, pairs)  14.5 us
    pallas_call x2, Pallas kernels, spread(): pl.pallas_call(spread_kernel, grid=(K // KSTEP,), out_shape=(sds((S, C),...  12.1 us
    ppermute x8, starting transfers between devices, cross(): lax.ppermute(value, axis, [(n, n ^ mask) for n in range(lax.axis_size(axi...  10.3 us
    all_to_all x1, waiting for transfers between devices, body(): lax.all_to_all(rows.reshape(gx, S // gx, C), 'gx', split_axis=0, concat_a...  8.25 us
  transfers between devices with their start and end apart: 20, of which 11 were waited for; matrix products, arithmetic and copies ran while one was open for 1% of the time, Pallas kernels for 16%

profile of v1, /device:TPU:2, one launch (start us, length us, event | category | flops | bytes accessed | tf_op | source)
XLA Modules:
  0.0 142.3 jit_solution(10116776134361864501)
XLA Ops:
  0.6 0.9 copy.13.nbr
  1.5 0.9 copy-done
  2.4 0.9 copy-done.2
  3.3 0.9 copy-done.5
  4.2 0.7 copy-done.6
  4.9 0.2 shard_map.103
  5.1 2.4 %collective-permute-start.11 = (bf16[224,768]{1,0:T(8,128)(2,1)S(1)}, bf16[224,768]{1,0:T(8,128)(2,1)S(1)}, u32[]{:S(2)}, u32[]{:S(2)}) collective-permute-start(bf16[224,768]{1,0:T(8,128)(2,1)S(1)} %get-tuple-element.46.p0), channel_id=1, source_target_pairs={{0,1},{1,0},{2,3},{3,2},{4,5},{5,4},{6,7},{7,6},{8,9},{9,8},{10,11... | collective-permute-start | bytes 1032200 | tf_op jit(solution)/shard_map/ppermute | solution.py:306
  7.4 0.7 collective-permute-start.12
  8.1 0.9 collective-permute-start.13
  9.0 0.1 pad_add_fusion.place
  9.1 7.3 %collective-permute-done.11.p1 = bf16[224,768]{1,0:T(8,128)(2,1)S(1)} collective-permute-done((bf16[224,768]{1,0:T(8,128)(2,1)S(1)}, bf16[224,768]{1,0:T(8,128)(2,1)S(1)}, u32[]{:S(2)}, u32[]{:S(2)}) %collective-permute-start.11) | collective-permute-done | bytes 344096 | tf_op jit(solution)/shard_map/ppermute | solution.py:306
  16.4 7.0 %collective-permute-done.12.p2 = bf16[224,768]{1,0:T(8,128)(2,1)S(1)} collective-permute-done((bf16[224,768]{1,0:T(8,128)(2,1)S(1)}, bf16[224,768]{1,0:T(8,128)(2,1)S(1)}, u32[]{:S(2)}, u32[]{:S(2)}) %collective-permute-start.12) | collective-permute-done | bytes 344096 | tf_op jit(solution)/shard_map/ppermute | solution.py:306
  23.4 1.4 collective-permute-done.13.p3
  24.7 1.1 shard_map.110
  25.8 0.1 collective-permute-start.14
  25.9 0.7 collective-permute-start.15
  26.6 0.0 copy-start.3
  26.6 0.9 copy-done.3
  27.5 2.0 %copy-done.7 = bf16[256,6912]{1,0:T(8,128)(2,1)S(1)} copy-done((bf16[256,6912]{1,0:T(8,128)(2,1)S(1)}, bf16[256,6912]{1,0:T(8,128)(2,1)}, u32[]{:S(2)}) %copy-start.7) | copy-done | bytes 3538968
  29.5 6.0 %shard_map.104 = (f32[192,256]{1,0:T(8,128)S(1)}, bf16[96,256]{1,0:T(8,128)(2,1)S(1)}, bf16[96,256]{1,0:T(8,128)(2,1)S(1)}, bf16[64,256]{1,0:T(8,128)(2,1)S(1)}) custom-call(s32[2]{0:T(128)S(1)} %pad_add_fusion.place, f32[32,256]{1,0:T(8,128)S(1)} %get-tuple-element.30.nbt, bf16[192,256]{1,0:T(8,128)(2,1)S(1)} %copy-done.3, bf16[256,6912]{1,0:T(8,128)(2,1)S(1)} %copy-done.7), custom_call_target="tpu_custom_call" | custom-call | flops 4000000000 | bytes 4000000 | tf_op jit(solution)/shard_map/pallas_call | solution.py:272
  35.5 3.3 %collective-permute-start = (bf16[96,256]{1,0:T(8,128)(2,1)S(1)}, bf16[96,256]{1,0:T(8,128)(2,1)S(1)}, u32[]{:S(2)}, u32[]{:S(2)}) collective-permute-start(bf16[96,256]{1,0:T(8,128)(2,1)S(1)} %get-tuple-element.32), channel_id=1, source_target_pairs={{0,4},{4,0},{8,12},{12,8},{16,20},{20,16},{24,28},{28,24},{32,36},... | collective-permute-start | bytes 147464 | tf_op jit(solution)/shard_map/ppermute | solution.py:302
  38.9 0.7 collective-permute-start.1
  39.5 0.2 collective-permute-done.m1
  39.8 0.0 collective-permute-done.1.m2
  39.8 0.6 shard_map.105
  40.3 3.1 %collective-permute-start.2 = (bf16[96,256]{1,0:T(8,128)(2,1)S(1)}, bf16[96,256]{1,0:T(8,128)(2,1)S(1)}, u32[]{:S(2)}, u32[]{:S(2)}) collective-permute-start(bf16[96,256]{1,0:T(8,128)(2,1)S(1)} %get-tuple-element.35), channel_id=1, source_target_pairs={{0,1},{1,0},{2,3},{3,2},{4,5},{5,4},{6,7},{7,6},{8,9},{9,8},{10,11... | collective-permute-start | bytes 147464 | tf_op jit(solution)/shard_map/ppermute | solution.py:302
  43.4 1.9 %collective-permute-start.3 = (bf16[96,256]{1,0:T(8,128)(2,1)S(1)}, bf16[96,256]{1,0:T(8,128)(2,1)S(1)}, u32[]{:S(2)}, u32[]{:S(2)}) collective-permute-start(bf16[96,256]{1,0:T(8,128)(2,1)S(1)} %get-tuple-element.36), channel_id=1, source_target_pairs={{1,2},{2,1},{5,6},{6,5},{9,10},{10,9},{13,14},{14,13},{17,18},{18,... | collective-permute-start | bytes 147464 | tf_op jit(solution)/shard_map/ppermute | solution.py:302
  45.3 0.2 collective-permute-done.2.n1
  45.5 3.9 %collective-permute-done.3.n2 = bf16[96,256]{1,0:T(8,128)(2,1)S(1)} collective-permute-done((bf16[96,256]{1,0:T(8,128)(2,1)S(1)}, bf16[96,256]{1,0:T(8,128)(2,1)S(1)}, u32[]{:S(2)}, u32[]{:S(2)}) %collective-permute-start.3) | collective-permute-done | bytes 49184 | tf_op jit(solution)/shard_map/ppermute | solution.py:302
  49.4 0.9 shard_map.106
  50.3 0.1 collective-permute-start.10
  50.4 0.1 collective-permute-start.8
  50.5 3.4 %collective-permute-start.9 = (bf16[192,256]{1,0:T(8,128)(2,1)S(1)}, bf16[192,256]{1,0:T(8,128)(2,1)S(1)}, u32[]{:S(2)}, u32[]{:S(2)}) collective-permute-start(bf16[192,256]{1,0:T(8,128)(2,1)S(1)} %get-tuple-element.45.g0), channel_id=1, source_target_pairs={{0,2},{1,3},{2,0},{3,1},{4,6},{5,7},{6,4},{7,5},{8,10},{9,11},{10,... | collective-permute-start | bytes 294920 | tf_op jit(solution)/shard_map/ppermute | solution.py:306
  53.9 0.0 collective-permute-done.14.r1
  53.9 0.0 collective-permute-done.15.r2
  53.9 5.9 %shard_map.111 = (bf16[128,1792]{1,0:T(8,128)(2,1)S(1)}, bf16[128,1792]{1,0:T(8,128)(2,1)S(1)}, bf16[768,1792]{1,0:T(8,128)(2,1)S(1)}) custom-call(s32[2]{0:T(128)S(1)} %pad_add_fusion.place, bf16[224,768]{1,0:T(8,128)(2,1)S(1)} %get-tuple-element.46.p0, bf16[224,768]{1,0:T(8,128)(2,1)S(1)} %collective-permute-done.11.p1, ...), custom_call_target="tpu_custom_call" | custom-call | flops 4000000000 | bytes 1000000 | tf_op jit(solution)/shard_map/pallas_call | solution.py:259
  59.8 0.0 copy-start.8
  59.8 0.0 collective-permute-done.10.g3
  59.8 0.0 collective-permute-done.8.g1
  59.8 1.7 %shard_map.112 = (bf16[128,1792]{1,0:T(8,128)(2,1)S(1)}, bf16[128,1792]{1,0:T(8,128)(2,1)S(1)}) custom-call(s32[2]{0:T(128)S(1)} %pad_add_fusion.place, bf16[192,256]{1,0:T(8,128)(2,1)S(1)} %get-tuple-element.45.g0, bf16[192,256]{1,0:T(8,128)(2,1)S(1)} %collective-permute-done.8.g1, bf16[192,256]{1,0:T(8,128)(2,1)S(1)} %collective-permute-done.9.g2, ...), custom_call_target="tpu_custom_call" | custom-call | flops 1000000000 | bytes 1000000 | tf_op jit(solution)/shard_map/pallas_call | solution.py:259
  61.5 2.7 %collective-permute-start.16 = (bf16[128,1792]{1,0:T(8,128)(2,1)S(1)}, bf16[128,1792]{1,0:T(8,128)(2,1)S(1)}, u32[]{:S(2)}, u32[]{:S(2)}) collective-permute-start(bf16[128,1792]{1,0:T(8,128)(2,1)S(1)} %get-tuple-element.52), channel_id=1, source_target_pairs={{0,4},{4,0},{8,12},{12,8},{16,20},{20,16},{24,28},{28,24},{32,36},... | collective-permute-start | bytes 1376264 | tf_op jit(solution)/shard_map/ppermute | solution.py:306
  64.2 0.1 collective-permute-start.17
  64.3 6.0 %shard_map.107 = (f32[192,256]{1,0:T(8,128)S(1)}, bf16[96,256]{1,0:T(8,128)(2,1)S(1)}, bf16[96,256]{1,0:T(8,128)(2,1)S(1)}, bf16[64,256]{1,0:T(8,128)(2,1)S(1)}) custom-call(s32[2]{0:T(128)S(1)} %pad_add_fusion.place, f32[32,256]{1,0:T(8,128)S(1)} %get-tuple-element.30.nbt, bf16[192,256]{1,0:T(8,128)(2,1)S(1)} %get-tuple-element.38.grad, ...), custom_call_target="tpu_custom_call" | custom-call | flops 4000000000 | bytes 4000000 | tf_op jit(solution)/shard_map/pallas_call | solution.py:272
  70.4 0.5 collective-permute-start.4
  70.9 0.7 collective-permute-start.5
  71.5 0.2 collective-permute-done.4.m1
  71.7 0.0 collective-permute-done.5.m2
  71.7 0.6 shard_map.108
  72.3 1.0 collective-permute-start.6
  73.3 2.6 %collective-permute-start.7 = (bf16[96,256]{1,0:T(8,128)(2,1)S(1)}, bf16[96,256]{1,0:T(8,128)(2,1)S(1)}, u32[]{:S(2)}, u32[]{:S(2)}) collective-permute-start(bf16[96,256]{1,0:T(8,128)(2,1)S(1)} %get-tuple-element.44), channel_id=1, source_target_pairs={{1,2},{2,1},{5,6},{6,5},{9,10},{10,9},{13,14},{14,13},{17,18},{18,... | collective-permute-start | bytes 147464 | tf_op jit(solution)/shard_map/ppermute | solution.py:302
  75.9 0.1 copy.14
  76.0 0.1 reshape.18.send
  76.1 0.4 collective-permute-done.6.n1
  76.5 2.8 %collective-permute-done.7.n2 = bf16[96,256]{1,0:T(8,128)(2,1)S(1)} collective-permute-done((bf16[96,256]{1,0:T(8,128)(2,1)S(1)}, bf16[96,256]{1,0:T(8,128)(2,1)S(1)}, u32[]{:S(2)}, u32[]{:S(2)}) %collective-permute-start.7) | collective-permute-done | bytes 49184 | tf_op jit(solution)/shard_map/ppermute | solution.py:302
  79.3 0.9 shard_map.109
  80.2 0.7 reshape.19
  80.9 19.9 %all-to-all-start = ((bf16[64,3,256]{2,1,0:T(4,128)(2,1)}), bf16[64,3,256]{2,1,0:T(4,128)(2,1)S(1)}, u32[]{:S(2)}, u32[]{:S(2)}) async-start(bf16[64,3,256]{2,1,0:T(4,128)(2,1)} %reshape.19), calls=%async_computation | async-start | bytes 262144 | tf_op jit(solution)/shard_map/all_to_all | solution.py:368
  100.8 0.0 collective-permute-done.16.s1
  100.8 2.0 %shard_map.113 = bf16[256,1792]{1,0:T(8,128)(2,1)} custom-call(bf16[128,1792]{1,0:T(8,128)(2,1)S(1)} %get-tuple-element.51.k1, bf16[128,1792]{1,0:T(8,128)(2,1)S(1)} %collective-permute-done.16.s1, bf16[128,1792]{1,0:T(8,128)(2,1)S(1)} %get-tuple-element.53.k2, bf16[128,1792]{1,0:T(8,128)(2,1)S(1)} %collective-permute-done.17.s2), custom_call_target="tpu_custom_call" | custom-call | flops 100000000 | bytes 1000000 | tf_op jit(solution)/shard_map/pallas_call | solution.py:259
  102.9 8.2 %all-to-all-done = bf16[64,3,256]{2,1,0:T(4,128)(2,1)S(1)} async-done(((bf16[64,3,256]{2,1,0:T(4,128)(2,1)}), bf16[64,3,256]{2,1,0:T(4,128)(2,1)S(1)}, u32[]{:S(2)}, u32[]{:S(2)}) %all-to-all-start) | async-done | bytes 98336 | tf_op jit(solution)/shard_map/all_to_all | solution.py:368
  111.1 4.3 %all-to-all-start.1 = ((bf16[32,8,1792]{2,1,0:T(8,128)(2,1)}), bf16[32,8,1792]{2,1,0:T(8,128)(2,1)S(1)}, u32[]{:S(2)}, u32[]{:S(2)}) async-start(bf16[32,8,1792]{2,1,0:T(8,128)(2,1)} %bitcast.2), calls=%async_computation.1 | async-start | bytes 1835008 | tf_op jit(solution)/shard_map/all_to_all | solution.py:416
  115.4 0.7 reshape.20
  116.2 25.4 %all-to-all-done.1.refs_0_ = bf16[32,8,1792]{2,1,0:T(8,128)(2,1)S(1)} async-done(((bf16[32,8,1792]{2,1,0:T(8,128)(2,1)}), bf16[32,8,1792]{2,1,0:T(8,128)(2,1)S(1)}, u32[]{:S(2)}, u32[]{:S(2)}) %all-to-all-start.1) | async-done | bytes 917536 | tf_op jit(solution)/shard_map/all_to_all | solution.py:416
  141.5 0.8 shard_map.114
  (14 shorter events, 0.0 us)
Async XLA Ops:
  1.5 0.9 copy-start
  2.4 0.9 copy-start.2
  3.3 0.9 copy-start.5
  4.2 0.7 copy-start.6
  5.1 11.3 %collective-permute-start.11 = (bf16[224,768]{1,0:T(8,128)(2,1)S(1)}, bf16[224,768]{1,0:T(8,128)(2,1)S(1)}, u32[]{:S(2)}, u32[]{:S(2)}) collective-permute-start(bf16[224,768]{1,0:T(8,128)(2,1)S(1)} %get-tuple-element.46.p0), channel_id=1, source_target_pairs={{0,1},{1,0},{2,3},{3,2},{4,5},{5,4},{6,7},{7,6},{8,9},{9,8},{10,11... | collective-permute-start | bytes 1032200 | tf_op jit(solution)/shard_map/ppermute | solution.py:306
  7.4 15.9 %collective-permute-start.12 = (bf16[224,768]{1,0:T(8,128)(2,1)S(1)}, bf16[224,768]{1,0:T(8,128)(2,1)S(1)}, u32[]{:S(2)}, u32[]{:S(2)}) collective-permute-start(bf16[224,768]{1,0:T(8,128)(2,1)S(1)} %get-tuple-element.46.p0), channel_id=1, source_target_pairs={{0,2},{1,3},{2,0},{3,1},{4,6},{5,7},{6,4},{7,5},{8,10},{9,11},{10,... | collective-permute-start | bytes 1032200 | tf_op jit(solution)/shard_map/ppermute | solution.py:306
  8.1 16.6 %collective-permute-start.13 = (bf16[224,768]{1,0:T(8,128)(2,1)S(1)}, bf16[224,768]{1,0:T(8,128)(2,1)S(1)}, u32[]{:S(2)}, u32[]{:S(2)}) collective-permute-start(bf16[224,768]{1,0:T(8,128)(2,1)S(1)} %get-tuple-element.46.p0), channel_id=1, source_target_pairs={{0,3},{1,2},{2,1},{3,0},{4,7},{5,6},{6,5},{7,4},{8,11},{9,10},{10,... | collective-permute-start | bytes 1032200 | tf_op jit(solution)/shard_map/ppermute | solution.py:306
  25.8 28.1 %collective-permute-start.14 = (bf16[4,96,512]{2,1,0:T(8,128)(2,1)S(1)}, bf16[4,96,512]{2,1,0:T(8,128)(2,1)S(1)}, u32[]{:S(2)}, u32[]{:S(2)}) collective-permute-start(bf16[4,96,512]{2,1,0:T(8,128)(2,1)S(1)} %get-tuple-element.47), channel_id=1, source_target_pairs={{0,4},{4,0},{8,12},{12,8},{16,20},{20,16},{24,28},{28,24},{32,36},... | collective-permute-start | bytes 1179656 | tf_op jit(solution)/shard_map/ppermute | solution.py:302
  25.9 28.0 %collective-permute-start.15 = (bf16[4,96,512]{2,1,0:T(8,128)(2,1)S(1)}, bf16[4,96,512]{2,1,0:T(8,128)(2,1)S(1)}, u32[]{:S(2)}, u32[]{:S(2)}) collective-permute-start(bf16[4,96,512]{2,1,0:T(8,128)(2,1)S(1)} %get-tuple-element.48), channel_id=1, source_target_pairs={{4,8},{8,4},{12,16},{16,12},{20,24},{24,20},{28,32},{32,28},{36,40... | collective-permute-start | bytes 1179656 | tf_op jit(solution)/shard_map/ppermute | solution.py:302
  26.6 0.9 copy-start.3
  27.5 2.0 %copy-start.7 = (bf16[256,6912]{1,0:T(8,128)(2,1)S(1)}, bf16[256,6912]{1,0:T(8,128)(2,1)}, u32[]{:S(2)}) copy-start(bf16[256,6912]{1,0:T(8,128)(2,1)} %weight.2) | copy-start | bytes 10616836
  29.5 19.9 %copy-start.1 = (bf16[192,256]{1,0:T(8,128)(2,1)S(1)}, bf16[192,256]{1,0:T(8,128)(2,1)}, u32[]{:S(2)}) copy-start(bf16[192,256]{1,0:T(8,128)(2,1)} %pre.3) | copy-start | bytes 294916
  35.5 4.2 %collective-permute-start = (bf16[96,256]{1,0:T(8,128)(2,1)S(1)}, bf16[96,256]{1,0:T(8,128)(2,1)S(1)}, u32[]{:S(2)}, u32[]{:S(2)}) collective-permute-start(bf16[96,256]{1,0:T(8,128)(2,1)S(1)} %get-tuple-element.32), channel_id=1, source_target_pairs={{0,4},{4,0},{8,12},{12,8},{16,20},{20,16},{24,28},{28,24},{32,36},... | collective-permute-start | bytes 147464 | tf_op jit(solution)/shard_map/ppermute | solution.py:302
  38.9 0.9 collective-permute-start.1
  40.3 5.2 %collective-permute-start.2 = (bf16[96,256]{1,0:T(8,128)(2,1)S(1)}, bf16[96,256]{1,0:T(8,128)(2,1)S(1)}, u32[]{:S(2)}, u32[]{:S(2)}) collective-permute-start(bf16[96,256]{1,0:T(8,128)(2,1)S(1)} %get-tuple-element.35), channel_id=1, source_target_pairs={{0,1},{1,0},{2,3},{3,2},{4,5},{5,4},{6,7},{7,6},{8,9},{9,8},{10,11... | collective-permute-start | bytes 147464 | tf_op jit(solution)/shard_map/ppermute | solution.py:302
  43.4 6.0 %collective-permute-start.3 = (bf16[96,256]{1,0:T(8,128)(2,1)S(1)}, bf16[96,256]{1,0:T(8,128)(2,1)S(1)}, u32[]{:S(2)}, u32[]{:S(2)}) collective-permute-start(bf16[96,256]{1,0:T(8,128)(2,1)S(1)} %get-tuple-element.36), channel_id=1, source_target_pairs={{1,2},{2,1},{5,6},{6,5},{9,10},{10,9},{13,14},{14,13},{17,18},{18,... | collective-permute-start | bytes 147464 | tf_op jit(solution)/shard_map/ppermute | solution.py:302
  50.3 9.5 %collective-permute-start.10 = (bf16[192,256]{1,0:T(8,128)(2,1)S(1)}, bf16[192,256]{1,0:T(8,128)(2,1)S(1)}, u32[]{:S(2)}, u32[]{:S(2)}) collective-permute-start(bf16[192,256]{1,0:T(8,128)(2,1)S(1)} %get-tuple-element.45.g0), channel_id=1, source_target_pairs={{0,3},{1,2},{2,1},{3,0},{4,7},{5,6},{6,5},{7,4},{8,11},{9,10},{10,... | collective-permute-start | bytes 294920 | tf_op jit(solution)/shard_map/ppermute | solution.py:306
  50.4 9.4 %collective-permute-start.8 = (bf16[192,256]{1,0:T(8,128)(2,1)S(1)}, bf16[192,256]{1,0:T(8,128)(2,1)S(1)}, u32[]{:S(2)}, u32[]{:S(2)}) collective-permute-start(bf16[192,256]{1,0:T(8,128)(2,1)S(1)} %get-tuple-element.45.g0), channel_id=1, source_target_pairs={{0,1},{1,0},{2,3},{3,2},{4,5},{5,4},{6,7},{7,6},{8,9},{9,8},{10,11... | collective-permute-start | bytes 294920 | tf_op jit(solution)/shard_map/ppermute | solution.py:306
  50.5 9.3 %collective-permute-start.9 = (bf16[192,256]{1,0:T(8,128)(2,1)S(1)}, bf16[192,256]{1,0:T(8,128)(2,1)S(1)}, u32[]{:S(2)}, u32[]{:S(2)}) collective-permute-start(bf16[192,256]{1,0:T(8,128)(2,1)S(1)} %get-tuple-element.45.g0), channel_id=1, source_target_pairs={{0,2},{1,3},{2,0},{3,1},{4,6},{5,7},{6,4},{7,5},{8,10},{9,11},{10,... | collective-permute-start | bytes 294920 | tf_op jit(solution)/shard_map/ppermute | solution.py:306
  59.8 4.5 %copy-start.8 = (bf16[256,6912]{1,0:T(8,128)(2,1)S(1)}, bf16[256,6912]{1,0:T(8,128)(2,1)}, u32[]{:S(2)}) copy-start(bf16[256,6912]{1,0:T(8,128)(2,1)} %weight.3) | copy-start | bytes 10616836
  61.5 39.3 %collective-permute-start.16 = (bf16[128,1792]{1,0:T(8,128)(2,1)S(1)}, bf16[128,1792]{1,0:T(8,128)(2,1)S(1)}, u32[]{:S(2)}, u32[]{:S(2)}) collective-permute-start(bf16[128,1792]{1,0:T(8,128)(2,1)S(1)} %get-tuple-element.52), channel_id=1, source_target_pairs={{0,4},{4,0},{8,12},{12,8},{16,20},{20,16},{24,28},{28,24},{32,36},... | collective-permute-start | bytes 1376264 | tf_op jit(solution)/shard_map/ppermute | solution.py:306
  64.2 36.6 %collective-permute-start.17 = (bf16[128,1792]{1,0:T(8,128)(2,1)S(1)}, bf16[128,1792]{1,0:T(8,128)(2,1)S(1)}, u32[]{:S(2)}, u32[]{:S(2)}) collective-permute-start(bf16[128,1792]{1,0:T(8,128)(2,1)S(1)} %get-tuple-element.54), channel_id=1, source_target_pairs={{0,4},{4,0},{8,12},{12,8},{16,20},{20,16},{24,28},{28,24},{32,36},... | collective-permute-start | bytes 1376264 | tf_op jit(solution)/shard_map/ppermute | solution.py:306
  64.3 11.5 %copy-start.9 = (s32[1,64,3]{1,0,2:T(1,128)S(1)}, s32[1,64,3]{1,0,2:T(1,128)}, u32[]{:S(2)}) copy-start(s32[1,64,3]{1,0,2:T(1,128)} %param.15) | copy-start | bytes 2308
  64.3 15.0 %copy-start.4 = (bf16[192,256]{1,0:T(8,128)(2,1)S(1)}, bf16[192,256]{1,0:T(8,128)(2,1)}, u32[]{:S(2)}) copy-start(bf16[192,256]{1,0:T(8,128)(2,1)} %grad.5) | copy-start | bytes 294916
  70.4 1.4 collective-permute-start.4
  70.9 0.9 collective-permute-start.5
  72.3 4.2 %collective-permute-start.6 = (bf16[96,256]{1,0:T(8,128)(2,1)S(1)}, bf16[96,256]{1,0:T(8,128)(2,1)S(1)}, u32[]{:S(2)}, u32[]{:S(2)}) collective-permute-start(bf16[96,256]{1,0:T(8,128)(2,1)S(1)} %get-tuple-element.43), channel_id=1, source_target_pairs={{0,1},{1,0},{2,3},{3,2},{4,5},{5,4},{6,7},{7,6},{8,9},{9,8},{10,11... | collective-permute-start | bytes 147464 | tf_op jit(solution)/shard_map/ppermute | solution.py:302
  73.3 6.0 %collective-permute-start.7 = (bf16[96,256]{1,0:T(8,128)(2,1)S(1)}, bf16[96,256]{1,0:T(8,128)(2,1)S(1)}, u32[]{:S(2)}, u32[]{:S(2)}) collective-permute-start(bf16[96,256]{1,0:T(8,128)(2,1)S(1)} %get-tuple-element.44), channel_id=1, source_target_pairs={{1,2},{2,1},{5,6},{6,5},{9,10},{10,9},{13,14},{14,13},{17,18},{18,... | collective-permute-start | bytes 147464 | tf_op jit(solution)/shard_map/ppermute | solution.py:302
  80.9 30.2 %all-to-all-start = ((bf16[64,3,256]{2,1,0:T(4,128)(2,1)}), bf16[64,3,256]{2,1,0:T(4,128)(2,1)S(1)}, u32[]{:S(2)}, u32[]{:S(2)}) async-start(bf16[64,3,256]{2,1,0:T(4,128)(2,1)} %reshape.19), calls=%async_computation | async-start | bytes 262144 | tf_op jit(solution)/shard_map/all_to_all | solution.py:368
  111.1 30.4 %all-to-all-start.1 = ((bf16[32,8,1792]{2,1,0:T(8,128)(2,1)}), bf16[32,8,1792]{2,1,0:T(8,128)(2,1)S(1)}, u32[]{:S(2)}, u32[]{:S(2)}) async-start(bf16[32,8,1792]{2,1,0:T(8,128)(2,1)} %bitcast.2), calls=%async_computation.1 | async-start | bytes 1835008 | tf_op jit(solution)/shard_map/all_to_all | solution.py:416

commit v2 on v1

--- a/solution.py
+++ b/solution.py
@@ -15,7 +15,6 @@
 QW = 1728
 BF = jnp.bfloat16
 F32 = jnp.float32
-KSTEP = 3
 
 
 def iota(shape, dim):
@@ -50,21 +49,41 @@
     return onehot(iota((S, 8 * HB), 0) == halo_row)
 
 
-def pack_kernel(feat, pre, grad, nbr, halo, pay, nbt, hrow, wide):
-    wide[...] = jnp.full(wide.shape, -1.0, F32)
-    wide[0:S, 0:K] = nbr[...].astype(F32)
-    table = jnp.transpose(wide[...])[0:32, :]
-    halo_id = table - S
-    heading = jnp.floor((halo_id + 0.5) * (1.0 / 24.0))
+def pack_kernel(
+    place, feat, pre, grad, nbr, halo, send, pay, nbt, hrow, srow, pre_out, grad_out,
+    ids, halo_ids, send_ids, sems
+):
+    copies = [
+        pltpu.make_async_copy(source, target, sems.at[n])
+        for n, (source, target) in enumerate(
+            (
+                (nbr, ids),
+                (halo, halo_ids),
+                (send, send_ids),
+                (feat, pay.at[0:S, 0:C]),
+                (grad, grad_out),
+                (pre, pre_out),
+            )
+        )
+    ]
+    for copy in copies:
+        copy.start()
+    for copy in copies:
+        copy.wait()
+    table = ids[...].astype(F32)
+    heading = jnp.floor((table - S + 0.5) * (1.0 / 24.0))
     table = jnp.where(table >= S, table + 8.0 * heading, table)
-    nbt[...] = table
-    shifted_up = table[:, 0:S] + 1.0
+    nbt[...] = jnp.full(nbt.shape, -1.0, F32)
+    nbt[0:K, 0:S] = table
+    shifted_up = table + 1.0
     high = jnp.floor(shifted_up * (1.0 / 16.0))
-    z = pre[...].astype(F32)
-    pay[0:S, 0:C] = feat[...]
+    pay[S : S + 32, :] = jnp.zeros((32, 3 * C), BF)
+    pay[S : S + K, 0:S] = high.astype(BF)
+    pay[S : S + K, C : C + S] = (shifted_up - 16.0 * high).astype(BF)
+    z = pre_out[...].astype(F32)
     pay[0:S, C : 2 * C] = (z * (1.0 / (1.0 + jnp.exp(-z)))).astype(BF)
-    pay[0:S, 2 * C : 3 * C] = mm(grad[...], channel_order()).astype(BF)
-    halo_up = (halo[0] + 1).astype(F32).astype(BF)
+    pay[0:S, 2 * C : 3 * C] = mm(grad_out[...], channel_order()).astype(BF)
+    halo_up = (halo_ids[0] + 1).astype(F32).astype(BF)
     spread = mm(halo_up, onehot(iota((24, 8 * HB), 1) % HB == iota((24, 8 * HB), 0)))
     row = jnp.sum(
         jnp.where(iota((8, 8 * HB), 1) // HB == iota((8, 8 * HB), 0), spread, 0.0),
@@ -72,35 +91,50 @@
         keepdims=True,
     )
     hrow[...] = jnp.broadcast_to(row.astype(jnp.int32) - 1, hrow.shape)
-    pay[S : S + 32, :] = jnp.zeros((32, 3 * C), BF)
-    pay[S : S + 32, 0:S] = high.astype(BF)
-    pay[S : S + 32, C : C + S] = (shifted_up - 16.0 * high).astype(BF)
     pay[S : S + 32, 2 * C : 3 * C] = jnp.broadcast_to(row, (32, C)).astype(BF)
-
-
-def spread_kernel(place, nbt, grad, weight, own, m1, m2, loc, acc):
-    step = pl.program_id(0)
-
-    @pl.when(step == 0)
-    def _():
-        acc[...] = jnp.zeros(acc.shape, F32)
-
-    total = acc[...]
-    terms = mm(grad[...], weight[...]).astype(BF)
-    rows = iota((EXT, S), 0)
-    for part in range(KSTEP):
-        ids = nbt[pl.ds(step * KSTEP + part, 1), 0:S].astype(jnp.int32)
-        total = total + mm(onehot(rows == ids), terms[:, part * C : (part + 1) * C])
-    acc[...] = total
-
-    @pl.when(step == K // KSTEP - 1)
-    def _():
-        even = place[0] % 2 == 0
-        own[...] = acc[0:S, :]
-        first, last = jnp.where(even, S, S + 160), jnp.where(even, S + 160, S)
-        m1[...] = acc[pl.ds(pl.multiple_of(first, 32), 96), :].astype(BF)
-        m2[...] = acc[pl.ds(pl.multiple_of(last, 32), 96), :].astype(BF)
-        loc[...] = acc[S + 96 : S + 160, :].astype(BF)
+    lane, peer = iota((64, C), 1), iota((64, C), 0)
+    parity = jnp.where(lane < 128, place[0] % 2, 1 - place[0] % 2)
+    pick = onehot(peer == 2 * (lane % 32) + parity)
+    spot = (iota((1, C), 1) % 128) // 32
+    total = jnp.zeros((1, C), F32)
+    for c in range(3):
+        up = jnp.broadcast_to((send_ids[c] + 1).astype(F32), (8, 64)).astype(BF)
+        total = jnp.where(spot == c, mm(up, pick)[0:1, :], total)
+    srow[...] = jnp.broadcast_to(total.astype(jnp.int32) - 1, srow.shape)
+
+
+def spread_kernel(place, nbt, grad, weight, own, m1, m2, loc, held, acc, sems):
+    copies = [
+        pltpu.make_async_copy(
+            weight.at[:, n * 9 * C : (n + 1) * 9 * C], held.at[n], sems.at[n]
+        )
+        for n in range(3)
+    ]
+    for copy in copies:
+        copy.start()
+    rows = iota((EXT, C), 0)
+    table = nbt[...].astype(jnp.int32)
+    gradient = grad[...]
+    none = jnp.zeros((C - S, C), BF)
+    for n in range(3):
+        masks, terms = [], []
+        for part in range(9):
+            k = 9 * n + part
+            masks.append(onehot(rows == table[k : k + 1, :]))
+        copies[n].wait()
+        for part in range(9):
+            terms += [mm(gradient, held[n, :, part * C : (part + 1) * C]).astype(BF), none]
+        total = mm(jnp.concatenate(masks, axis=1), jnp.concatenate(terms, axis=0))
+        if n:
+            acc[...] += total
+        else:
+            acc[...] = total
+    even = place[0] % 2 == 0
+    own[...] = acc[0:S, :]
+    first, last = jnp.where(even, S, S + 160), jnp.where(even, S + 160, S)
+    m1[...] = acc[pl.ds(pl.multiple_of(first, 32), 96), :].astype(BF)
+    m2[...] = acc[pl.ds(pl.multiple_of(last, 32), 96), :].astype(BF)
+    loc[...] = acc[S + 96 : S + 160, :].astype(BF)
 
 
 def pass_kernel(place, loc, m1, m2, n1, n2):
@@ -134,14 +168,15 @@
     ordered[...] = mm(value, channel_order()).astype(BF)
 
 
-def rows_kernel(place, own, m1, m2, n1, n2, hrow, grad, send, out, back):
+def rows_kernel(place, own, m1, m2, n1, n2, hrow, grad, srow, keep, send, back):
     total = settled(place, own, m1, m2, n1, n2, hrow, back)
     value = (grad[...].astype(F32) + total).astype(BF)
-    chosen = onehot(iota((S, S), 0) == send[...])
-    out[...] = mm_t(chosen, value).astype(BF)
-
-
-def pick_kernel(place, p0, p1, p2, p3, o1, o2, loc, picked):
+    chosen = mm_t(onehot(iota((S, C), 0) == srow[0:1, :]), value).astype(BF)
+    keep[...] = chosen[0:128, :]
+    send[...] = chosen[128:256, :]
+
+
+def pick_kernel(place, p0, p1, p2, p3, late, o1, o2, loc, picked):
     column = place[1]
     for turn, pay in enumerate((p0, p1, p2, p3)):
         halo_row = pay[S : S + 16, 2 * C : 3 * C].astype(F32)[0:1, :].astype(jnp.int32) - 1
@@ -166,7 +201,7 @@
 
 
 def columns_kernel(
-    place, p0, p1, p2, p3, r1, r2, loc, keep, send, cols_one, cols_two, ext, gt, ids, sel
+    place, p0, p1, p2, p3, r1, r2, loc, late, keep, send, cols_one, cols_two, ext, gt, ids, sel
 ):
     column = place[1]
     start = column * QW
@@ -223,13 +258,13 @@
             ).astype(BF)
 
 
-def weight_kernel(place, g0, g1, g2, g3, cols, keep, send, gt):
+def weight_kernel(place, g0, g1, g2, g3, cols, late, keep, send, gt):
     for turn, grad in enumerate((g0, g1, g2, g3)):
         gt[:, turn * S : (turn + 1) * S] = jnp.transpose(grad[...].astype(F32)).astype(BF)
     weight_blocks(place, gt, cols, keep, send)
 
 
-def merge_kernel(k1, s1, k2, s2, out):
+def merge_kernel(place, k1, s1, k2, s2, rk, rs, out):
     row, col = iota((C, 128), 0), iota((C, 128), 1)
     for part in range(7):
         at = slice(part * C, (part + 1) * C)
@@ -239,12 +274,21 @@
             for ref in refs:
                 total = total + mm(place_of, ref[:, at])
         out[:, at] = total.astype(BF)
-
-
-def final_kernel(scale, arrived, one, two):
-    total = jnp.sum(arrived[...].astype(F32), axis=0) * scale
+    mine = place[0] % 2
+    total = jnp.zeros((C, C), F32)
+    for ref, core in ((rk, mine), (rs, 1 - mine)):
+        spot = (row // 8 == col % 32) & (row % 8 == 3 * core + col // 32) & (col < 96)
+        total = total + mm(onehot(spot), ref[...])
+    out[:, 7 * C : 8 * C] = total.astype(BF)
+
+
+def final_kernel(scale, arrived, rows, one, two):
+    total = jnp.sum(arrived[:, :, 0 : 7 * C].astype(F32), axis=0) * scale
     one[...] = total[0:4, 0:QW]
     two[...] = total[4:8, 0:QW]
+    to, at = iota((S, C), 0), iota((S, C), 1)
+    spot = (at // 8 == to // 6) & (at % 8 == to % 6)
+    rows[...] = mm(onehot(spot), arrived[:, :, 7 * C : 8 * C].reshape(C, C)).astype(BF)
 
 
 def sds(shape, dtype):
@@ -253,13 +297,17 @@
 
 SMEM = pl.BlockSpec(memory_space=pltpu.SMEM)
 VM = pl.BlockSpec(memory_space=pltpu.VMEM)
-
-
-def call(kernel, outs, *args, scratch=(), scalars=0, flops=10**8):
+HBM = pl.BlockSpec(memory_space=pltpu.HBM)
+ANY = pl.BlockSpec(memory_space=pl.ANY)
+
+
+def call(kernel, outs, *args, scratch=(), specs=None, late=0, flops=10**8):
+    if specs is None:
+        specs = [SMEM] + [VM] * (len(args) - 1 - late) + [ANY] * late
     return pl.pallas_call(
         kernel,
         out_shape=outs,
-        in_specs=[SMEM] * scalars + [VM] * (len(args) - scalars),
+        in_specs=specs,
         out_specs=jax.tree.map(lambda _: VM, outs),
         scratch_shapes=list(scratch),
         compiler_params=pltpu.CompilerParams(vmem_limit_bytes=40 * 2**20),
@@ -268,24 +316,22 @@
 
 
 def spread(place, nbt, grad, weight):
-    whole = lambda shape: pl.BlockSpec(shape, lambda n: (0,) * len(shape))
-    return pl.pallas_call(
+    edge = sds((96, C), BF)
+    return call(
         spread_kernel,
-        grid=(K // KSTEP,),
-        out_shape=(sds((S, C), F32), sds((96, C), BF), sds((96, C), BF), sds((64, C), BF)),
-        in_specs=[
-            SMEM,
-            whole((32, C)),
-            whole((S, C)),
-            pl.BlockSpec((C, KSTEP * C), lambda n: (0, n)),
+        (sds((S, C), F32), edge, edge, sds((64, C), BF)),
+        place,
+        nbt,
+        grad,
+        weight,
+        specs=[SMEM, VM, VM, HBM],
+        scratch=[
+            pltpu.VMEM((3, C, 9 * C), BF),
+            pltpu.VMEM((EXT, C), F32),
+            pltpu.SemaphoreType.DMA((3,)),
         ],
-        out_specs=(whole((S, C)), whole((96, C)), whole((96, C)), whole((64, C))),
-        scratch_shapes=[pltpu.VMEM((EXT, C), F32)],
-        compiler_params=pltpu.CompilerParams(vmem_limit_bytes=40 * 2**20),
-        cost_estimate=pl.CostEstimate(
-            flops=4 * 10**9, bytes_accessed=4 * 10**6, transcendentals=0
-        ),
-    )(place, nbt, grad, weight)
+        flops=4 * 10**9,
+    )
 
 
 def partners(count, turn):
@@ -308,77 +354,60 @@
 
 def give_back(place, loc, m1, m2):
     m1, m2 = swap(m1, "gx", 1), swap(m2, "gx", 2)
-    n1, n2 = call(
-        pass_kernel, (sds((96, C), BF), sds((96, C), BF)), place, loc, m1, m2, scalars=1
-    )
-    return m1, m2, swap(n1, "gy", 1), swap(n2, "gy", 2)
+    n1, n2 = call(pass_kernel, (sds((96, C), BF), sds((96, C), BF)), place, loc, m1, m2)
+    return (m1, m2, swap(n1, "gy", 1), swap(n2, "gy", 2)), n1
 
 
 def body(features, pre_act, grad_out, weight_one, weight_two, neighbours, halo_list, send_list):
     gx = lax.axis_size("gx")
     scale = 1.0 / math.sqrt(S * gx * lax.axis_size("gy"))
     place = jnp.stack([lax.axis_index("gx"), lax.axis_index("gy")]).astype(jnp.int32)
-    pay, nbt, hrow = call(
+    tile = sds((S, C), BF)
+    pay, nbt, hrow, srow, pre, grad = call(
         pack_kernel,
-        (sds((S + 32, 3 * C), BF), sds((32, C), F32), sds((8, C), jnp.int32)),
+        (
+            sds((S + 32, 3 * C), BF),
+            sds((32, C), F32),
+            sds((8, C), jnp.int32),
+            sds((8, C), jnp.int32),
+            tile,
+            tile,
+        ),
+        place,
         features,
         pre_act,
         grad_out,
-        neighbours,
+        neighbours.T,
         halo_list,
-        scratch=[pltpu.VMEM((C, 128), F32)],
+        jnp.transpose(send_list, (2, 0, 1)),
+        specs=[SMEM] + [HBM] * 6,
+        scratch=[
+            pltpu.VMEM((K, S), jnp.int32),
+            pltpu.VMEM((1, 8, 24), jnp.int32),
+            pltpu.VMEM((3, 1, 64), jnp.int32),
+            pltpu.SemaphoreType.DMA((6,)),
+        ],
     )
     pays = [pay] + [cross(pay, "gy", d) for d in (1, 2, 3)]
-    own, m1, m2, loc = spread(place, nbt, grad_out, weight_two)
-    m1, m2, n1, n2 = give_back(place, loc, m1, m2)
+    own, m1, m2, loc = spread(place, nbt, grad, weight_two)
     back = pltpu.VMEM((8, HB, C), BF)
-    grad_pre, ordered = call(
-        gate_kernel,
-        (sds((S, C), BF), sds((S, C), BF)),
-        place,
-        own,
-        m1,
-        m2,
-        n1,
-        n2,
-        hrow,
-        pre_act,
-        scratch=[back],
-        scalars=1,
-    )
-    grads = [ordered] + [cross(ordered, "gy", d) for d in (1, 2, 3)]
-    own, m1, m2, loc = spread(place, nbt, grad_pre, weight_one)
-    m1, m2, n1, n2 = give_back(place, loc, m1, m2)
-    send = send_list.reshape(1, S)
-    rows = call(
-        rows_kernel,
-        sds((S, C), BF),
-        place,
-        own,
-        m1,
-        m2,
-        n1,
-        n2,
-        hrow,
-        grad_out,
-        send,
-        scratch=[back],
-        scalars=1,
-    )
-    balanced = lax.all_to_all(
-        rows.reshape(gx, S // gx, C), "gx", split_axis=0, concat_axis=0, tiled=True
-    ).reshape(S, C)
-
+    arrived, passed = give_back(place, loc, m1, m2)
     picks = sds((4, 96, 2 * C), BF)
     o1, o2, near = call(
         pick_kernel,
         (picks, picks, sds((4, 64, 2 * C), BF)),
         place,
         *pays,
+        passed,
         scratch=[pltpu.VMEM((4, 8 * HB, 2 * C), BF)],
-        scalars=1,
+        late=1,
     )
     r1, r2 = swap(o1, "gx", 1), swap(o2, "gx", 2)
+    grad_pre, ordered = call(
+        gate_kernel, (tile, tile), place, own, *arrived, hrow, pre, scratch=[back]
+    )
+    grads = [ordered] + [cross(ordered, "gy", d) for d in (1, 2, 3)]
+    own, m1, m2, loc = spread(place, nbt, grad_pre, weight_one)
     wide = 7 * C
     half = sds((128, wide), BF)
     keep_two, send_two, cols_one = call(
@@ -389,6 +418,7 @@
         r1,
         r2,
         near,
+        own,
         scratch=[
             pltpu.VMEM((4 * S, wide), BF),
             pltpu.VMEM((EXT, 2 * C), BF),
@@ -396,25 +426,42 @@
             pltpu.VMEM((32, C), F32),
             pltpu.VMEM((128, C), F32),
         ],
-        scalars=1,
+        late=1,
         flops=4 * 10**9,
     )
     come_two = cross(send_two, "gx", 1)
+    arrived, passed = give_back(place, loc, m1, m2)
     keep_one, send_one = call(
         weight_kernel,
         (half, half),
         place,
         *grads,
         cols_one,
+        passed,
         scratch=[pltpu.VMEM((C, 4 * S), BF)],
-        scalars=1,
+        late=1,
         flops=10**9,
     )
     come_one = cross(send_one, "gx", 1)
-    merged = call(merge_kernel, sds((C, wide), BF), keep_one, come_one, keep_two, come_two)
+    some = sds((128, C), BF)
+    rows_keep, rows_send = call(
+        rows_kernel, (some, some), place, own, *arrived, hrow, grad, srow, scratch=[back]
+    )
+    rows_come = cross(rows_send, "gx", 1)
+    merged = call(
+        merge_kernel,
+        sds((C, 8 * C), BF),
+        place,
+        keep_one,
+        come_one,
+        keep_two,
+        come_two,
+        rows_keep,
+        rows_come,
+    )
     groups = [[2 * c + e for c in range(gx // 2)] for e in range(2)]
-    arrived = lax.all_to_all(
-        merged.reshape(gx // 2, 8, wide),
+    collected = lax.all_to_all(
+        merged.reshape(gx // 2, 8, 8 * C),
         "gx",
         split_axis=0,
         concat_axis=0,
@@ -422,8 +469,9 @@
         axis_index_groups=groups,
     )
     out = sds((4, QW), F32)
-    grad_one, grad_two = call(lambda *refs: final_kernel(scale, *refs), (out, out), arrived)
-    return balanced, grad_one, grad_two
+    return call(
+        lambda *refs: final_kernel(scale, *refs), (tile, out, out), collected, specs=[VM]
+    )
 
 
 def solution(mesh):

time: 143 us -> 116 us (0.81)
  waiting for transfers between devices: 57 us -> 7.89 us
  blocking collectives: 0 us -> 41.1 us
  starting transfers between devices: 48.9 us -> 29.5 us
  local copies, waits for them, and re-layouts: 8.78 us -> 6.8 us
  Pallas kernels: 26.7 us -> 28.4 us
    all_to_all x0 -> x1, blocking collectives: none -> 41.1 us  [body(): lax.all_to_all(merged.reshape(gx // 2, 8, 8 * C), 'gx', split_axis=0, con...]
    all_to_all x2 -> x0, waiting for transfers between devices: 33.6 us -> none  [the longest x1 25.4 us: body(): lax.all_to_all(merged.reshape(gx // 2, 8, wide), 'gx', split_axis=0, conc...]
    all_to_all x2 -> x0, starting transfers between devices: 24.2 us -> none  [the longest x1 19.9 us: body(): lax.all_to_all(rows.reshape(gx, S // gx, C), 'gx', split_axis=0, concat_a...]
    ppermute x8 -> x9, waiting for transfers between devices: 15.7 us -> 1.26 us  [cross(): lax.ppermute(value, axis, [(n, n ^ mask) for n in range(lax.axis_size(axi...]
    ppermute x10, starting transfers between devices: 14.5 us -> 18.9 us  [swap(): return lax.ppermute(value, axis, pairs)]
    pallas_call x12, Pallas kernels: 26.7 us -> 28.4 us  [call(): pl.pallas_call(kernel, out_shape=outs, in_specs=specs, out_specs=jax.tree...]
    reshape x3 -> x0, local copies, waits for them, and re-layouts: 1.56 us -> none  [the longest x1 0.72 us: body(): balanced = lax.all_to_all(rows.reshape(gx, S // gx, C), 'gx', split_axis=...]
    unnamed x22 -> x16, local copies, waits for them, and re-layouts: 7.22 us -> 6.8 us
  transfers between devices with their start and end apart: 20 -> 19, of which waited for: 11 -> 5; matrix products, arithmetic and copies ran while one was open for 1% -> 0% of each run, Pallas kernels for 16% -> 19%
where the time goes in v2:
time: 116 us; the launch traced here: 115 us
  blocking collectives  41.1 us (35%)
  starting transfers between devices  29.5 us (25%)
  Pallas kernels  28.4 us (24%)
  waiting for transfers between devices  7.89 us (7%)
  local copies, waits for them, and re-layouts  6.8 us (6%)
    all_to_all x1, blocking collectives, body(): lax.all_to_all(merged.reshape(gx // 2, 8, 8 * C), 'gx', split_axis=0, con...  41.1 us
    pallas_call x12, Pallas kernels, call(): pl.pallas_call(kernel, out_shape=outs, in_specs=specs, out_specs=jax.tree...  28.4 us
    ppermute x10, starting transfers between devices, swap(): return lax.ppermute(value, axis, pairs)  18.9 us
    ppermute x9, starting transfers between devices, cross(): lax.ppermute(value, axis, [(n, n ^ mask) for n in range(lax.axis_size(axi...  10.6 us
    unnamed x16, local copies, waits for them, and re-layouts  6.8 us
    ppermute x10, waiting for transfers between devices, swap(): return lax.ppermute(value, axis, pairs)  6.63 us
  transfers between devices with their start and end apart: 19, of which 5 were waited for; matrix products, arithmetic and copies ran while one was open for 0% of the time, Pallas kernels for 19%

profile of v2, /device:TPU:2, one launch (start us, length us, event | category | flops | bytes accessed | tf_op | source)
XLA Modules:
  0.0 114.7 jit_solution(9003535660354129886)
XLA Ops:
  0.6 0.1 pad_add_fusion.place
  0.7 0.0 copy-start.2
  0.7 0.9 copy-done.2
  1.6 0.0 copy-start.3
  1.6 0.9 copy-done.3
  2.5 0.0 copy-start.4
  2.5 0.9 copy-done.4
  3.4 0.0 copy-start.5
  3.4 0.8 copy-done.5
  4.2 0.7 copy-done.6
  4.8 0.7 copy-done.7
  5.5 1.2 %shard_map.103 = (bf16[224,768]{1,0:T(8,128)(2,1)S(1)}, f32[32,256]{1,0:T(8,128)S(1)}, s32[8,256]{1,0:T(8,128)S(1)}, s32[8,256]{1,0:T(8,128)S(1)}, bf16[192,256]...) custom-call(s32[2]{0:T(128)S(1)} %pad_add_fusion.place, bf16[192,256]{1,0:T(8,128)(2,1)S(1)} %copy-done.2, ...), custom_call_target="tpu_custom_call" | custom-call | flops 100000000 | bytes 1000000 | tf_op jit(solution)/shard_map/pallas_call | solution.py:307
  6.7 2.4 %collective-permute-start.7 = (bf16[224,768]{1,0:T(8,128)(2,1)S(1)}, bf16[224,768]{1,0:T(8,128)(2,1)S(1)}, u32[]{:S(2)}, u32[]{:S(2)}) collective-permute-start(bf16[224,768]{1,0:T(8,128)(2,1)S(1)} %get-tuple-element.44.p0), channel_id=1, source_target_pairs={{0,1},{1,0},{2,3},{3,2},{4,5},{5,4},{6,7},{7,6},{8,9},{9,8},{10,11... | collective-permute-start | bytes 1032200 | tf_op jit(solution)/shard_map/ppermute | solution.py:352
  9.1 0.7 collective-permute-start.8
  9.7 0.9 collective-permute-start.9
  10.6 2.0 %copy-done = bf16[256,6912]{1,0:T(8,128)(2,1)S(1)} copy-done((bf16[256,6912]{1,0:T(8,128)(2,1)S(1)}, bf16[256,6912]{1,0:T(8,128)(2,1)}, u32[]{:S(2)}) %copy-start) | copy-done | bytes 3538968
  12.6 6.5 %shard_map.104 = (f32[192,256]{1,0:T(8,128)S(1)}, bf16[96,256]{1,0:T(8,128)(2,1)S(1)}, bf16[96,256]{1,0:T(8,128)(2,1)S(1)}, bf16[64,256]{1,0:T(8,128)(2,1)S(1)}) custom-call(s32[2]{0:T(128)S(1)} %pad_add_fusion.place, f32[32,256]{1,0:T(8,128)S(1)} %get-tuple-element.33.nbt, bf16[192,256]{1,0:T(8,128)(2,1)S(1)} %get-tuple-element.34.grad, ...), custom_call_target="tpu_custom_call" | custom-call | flops 4000000000 | bytes 1000000 | tf_op jit(solution)/shard_map/pallas_call | solution.py:307
  19.1 0.1 collective-permute-start
  19.2 0.7 collective-permute-start.1
  19.9 0.5 collective-permute-done.m1
  20.4 0.0 collective-permute-done.1.m2
  20.4 0.6 shard_map.105
  21.0 3.2 %collective-permute-start.2 = (bf16[96,256]{1,0:T(8,128)(2,1)S(1)}, bf16[96,256]{1,0:T(8,128)(2,1)S(1)}, u32[]{:S(2)}, u32[]{:S(2)}) collective-permute-start(bf16[96,256]{1,0:T(8,128)(2,1)S(1)} %get-tuple-element.39.late), channel_id=1, source_target_pairs={{0,1},{1,0},{2,3},{3,2},{4,5},{5,4},{6,7},{7,6},{8,9},{9,8},{10,11... | collective-permute-start | bytes 147464 | tf_op jit(solution)/shard_map/ppermute | solution.py:348
  24.2 2.3 %collective-permute-start.3 = (bf16[96,256]{1,0:T(8,128)(2,1)S(1)}, bf16[96,256]{1,0:T(8,128)(2,1)S(1)}, u32[]{:S(2)}, u32[]{:S(2)}) collective-permute-start(bf16[96,256]{1,0:T(8,128)(2,1)S(1)} %get-tuple-element.40), channel_id=1, source_target_pairs={{1,2},{2,1},{5,6},{6,5},{9,10},{10,9},{13,14},{14,13},{17,18},{18,... | collective-permute-start | bytes 147464 | tf_op jit(solution)/shard_map/ppermute | solution.py:348
  26.5 0.0 collective-permute-done.2.n1
  26.6 3.6 %collective-permute-done.3.n2 = bf16[96,256]{1,0:T(8,128)(2,1)S(1)} collective-permute-done((bf16[96,256]{1,0:T(8,128)(2,1)S(1)}, bf16[96,256]{1,0:T(8,128)(2,1)S(1)}, u32[]{:S(2)}, u32[]{:S(2)}) %collective-permute-start.3) | collective-permute-done | bytes 49184 | tf_op jit(solution)/shard_map/ppermute | solution.py:348
  30.2 0.9 shard_map.106
  31.1 0.0 collective-permute-done.7.p1
  31.1 0.0 collective-permute-done.8.p2
  31.1 0.0 collective-permute-done.9.p3
  31.1 1.1 shard_map.107
  32.2 3.6 %collective-permute-start.10 = (bf16[4,96,512]{2,1,0:T(8,128)(2,1)S(1)}, bf16[4,96,512]{2,1,0:T(8,128)(2,1)S(1)}, u32[]{:S(2)}, u32[]{:S(2)}) collective-permute-start(bf16[4,96,512]{2,1,0:T(8,128)(2,1)S(1)} %get-tuple-element.45), channel_id=1, source_target_pairs={{0,4},{4,0},{8,12},{12,8},{16,20},{20,16},{24,28},{28,24},{32,36},... | collective-permute-start | bytes 1179656 | tf_op jit(solution)/shard_map/ppermute | solution.py:348
  35.8 0.9 collective-permute-start.11
  36.7 0.0 copy-done.1
  36.7 6.5 %shard_map.108 = (f32[192,256]{1,0:T(8,128)S(1)}, bf16[96,256]{1,0:T(8,128)(2,1)S(1)}, bf16[96,256]{1,0:T(8,128)(2,1)S(1)}, bf16[64,256]{1,0:T(8,128)(2,1)S(1)}) custom-call(s32[2]{0:T(128)S(1)} %pad_add_fusion.place, f32[32,256]{1,0:T(8,128)S(1)} %get-tuple-element.33.nbt, bf16[192,256]{1,0:T(8,128)(2,1)S(1)} %get-tuple-element.48.grad, ...), custom_call_target="tpu_custom_call" | custom-call | flops 4000000000 | bytes 1000000 | tf_op jit(solution)/shard_map/pallas_call | solution.py:307
  43.2 2.8 %collective-permute-start.12 = (bf16[96,256]{1,0:T(8,128)(2,1)S(1)}, bf16[96,256]{1,0:T(8,128)(2,1)S(1)}, u32[]{:S(2)}, u32[]{:S(2)}) collective-permute-start(bf16[96,256]{1,0:T(8,128)(2,1)S(1)} %get-tuple-element.52), channel_id=1, source_target_pairs={{0,4},{4,0},{8,12},{12,8},{16,20},{20,16},{24,28},{28,24},{32,36},... | collective-permute-start | bytes 147464 | tf_op jit(solution)/shard_map/ppermute | solution.py:348
  46.0 0.7 collective-permute-start.13
  46.6 0.1 collective-permute-start.4
  46.7 0.1 collective-permute-done.12.m1
  46.8 3.1 %collective-permute-start.5 = (bf16[192,256]{1,0:T(8,128)(2,1)S(1)}, bf16[192,256]{1,0:T(8,128)(2,1)S(1)}, u32[]{:S(2)}, u32[]{:S(2)}) collective-permute-start(bf16[192,256]{1,0:T(8,128)(2,1)S(1)} %get-tuple-element.43.g0), channel_id=1, source_target_pairs={{0,2},{1,3},{2,0},{3,1},{4,6},{5,7},{6,4},{7,5},{8,10},{9,11},{10,... | collective-permute-start | bytes 294920 | tf_op jit(solution)/shard_map/ppermute | solution.py:352
  49.9 0.0 collective-permute-done.13.m2
  49.9 0.3 collective-permute-start.6
  50.2 0.6 shard_map.110
  50.8 0.0 collective-permute-done.10.r1
  50.8 0.0 collective-permute-done.11.r2
  50.8 5.9 %shard_map.109 = (bf16[128,1792]{1,0:T(8,128)(2,1)S(1)}, bf16[128,1792]{1,0:T(8,128)(2,1)S(1)}, bf16[768,1792]{1,0:T(8,128)(2,1)S(1)}) custom-call(s32[2]{0:T(128)S(1)} %pad_add_fusion.place, bf16[224,768]{1,0:T(8,128)(2,1)S(1)} %get-tuple-element.44.p0, bf16[224,768]{1,0:T(8,128)(2,1)S(1)} %collective-permute-done.7.p1, ...), custom_call_target="tpu_custom_call" | custom-call | flops 4000000000 | bytes 1000000 | tf_op jit(solution)/shard_map/pallas_call | solution.py:307
  56.7 0.0 collective-permute-done.4.g1
  56.7 0.0 collective-permute-done.5.g2
  56.7 0.0 collective-permute-done.6.g3
  56.7 1.7 %shard_map.111 = (bf16[128,1792]{1,0:T(8,128)(2,1)S(1)}, bf16[128,1792]{1,0:T(8,128)(2,1)S(1)}) custom-call(s32[2]{0:T(128)S(1)} %pad_add_fusion.place, bf16[192,256]{1,0:T(8,128)(2,1)S(1)} %get-tuple-element.43.g0, bf16[192,256]{1,0:T(8,128)(2,1)S(1)} %collective-permute-done.4.g1, bf16[192,256]{1,0:T(8,128)(2,1)S(1)} %collective-permute-done.5.g2, ...), custom_call_target="tpu_custom_call" | custom-call | flops 1000000000 | bytes 1000000 | tf_op jit(solution)/shard_map/pallas_call | solution.py:307
  58.5 3.0 %collective-permute-start.14 = (bf16[128,1792]{1,0:T(8,128)(2,1)S(1)}, bf16[128,1792]{1,0:T(8,128)(2,1)S(1)}, u32[]{:S(2)}, u32[]{:S(2)}) collective-permute-start(bf16[128,1792]{1,0:T(8,128)(2,1)S(1)} %get-tuple-element.56), channel_id=1, source_target_pairs={{0,4},{4,0},{8,12},{12,8},{16,20},{20,16},{24,28},{28,24},{32,36},... | collective-permute-start | bytes 1376264 | tf_op jit(solution)/shard_map/ppermute | solution.py:352
  61.5 0.1 collective-permute-start.15
  61.6 1.1 collective-permute-start.16
  62.7 3.6 %collective-permute-start.17 = (bf16[96,256]{1,0:T(8,128)(2,1)S(1)}, bf16[96,256]{1,0:T(8,128)(2,1)S(1)}, u32[]{:S(2)}, u32[]{:S(2)}) collective-permute-start(bf16[96,256]{1,0:T(8,128)(2,1)S(1)} %get-tuple-element.59), channel_id=1, source_target_pairs={{1,2},{2,1},{5,6},{6,5},{9,10},{10,9},{13,14},{14,13},{17,18},{18,... | collective-permute-start | bytes 147464 | tf_op jit(solution)/shard_map/ppermute | solution.py:348
  66.3 0.0 collective-permute-done.16.n1
  66.3 2.3 %collective-permute-done.17.n2 = bf16[96,256]{1,0:T(8,128)(2,1)S(1)} collective-permute-done((bf16[96,256]{1,0:T(8,128)(2,1)S(1)}, bf16[96,256]{1,0:T(8,128)(2,1)S(1)}, u32[]{:S(2)}, u32[]{:S(2)}) %collective-permute-start.17) | collective-permute-done | bytes 49184 | tf_op jit(solution)/shard_map/ppermute | solution.py:348
  68.6 1.0 shard_map.112
  69.6 0.1 collective-permute-start.18
  69.7 1.2 %collective-permute-done.18.rs = bf16[128,256]{1,0:T(8,128)(2,1)S(1)} collective-permute-done((bf16[128,256]{1,0:T(8,128)(2,1)S(1)}, bf16[128,256]{1,0:T(8,128)(2,1)S(1)}, u32[]{:S(2)}, u32[]{:S(2)}) %collective-permute-start.18) | collective-permute-done | bytes 65568 | tf_op jit(solution)/shard_map/ppermute | solution.py:352
  70.9 0.0 collective-permute-done.14.s1
  70.9 0.0 collective-permute-done.15.s2
  70.9 1.7 %shard_map.113 = bf16[256,2048]{1,0:T(8,128)(2,1)S(1)} custom-call(s32[2]{0:T(128)S(1)} %pad_add_fusion.place, bf16[128,1792]{1,0:T(8,128)(2,1)S(1)} %get-tuple-element.55.k1, bf16[128,1792]{1,0:T(8,128)(2,1)S(1)} %collective-permute-done.14.s1, bf16[128,1792]{1,0:T(8,128)(2,1)S(1)} %get-tuple-element.57.k2, ...), custom_call_target="tpu_custom_call" | custom-call | flops 100000000 | bytes 1000000 | tf_op jit(solution)/shard_map/pallas_call | solution.py:307
  72.7 41.1 %all_to_all.5.refs_0_ = bf16[32,8,2048]{2,1,0:T(8,128)(2,1)S(1)} all-to-all(bf16[32,8,2048]{2,1,0:T(8,128)(2,1)S(1)} %bitcast.5), channel_id=1, replica_groups={{0,8,16,24,32,40,48,56,64,72,80,88,96,104,112,120,128,136,144,152,160,1..., dimensions={0} | all-to-all | bytes 2097152 | tf_op jit(solution)/shard_map/all_to_all | solution.py:463
  113.8 0.9 shard_map.114
  (4 shorter events, 0.0 us)
Async XLA Ops:
  0.7 0.9 copy-start.2
  1.6 0.9 copy-start.3
  2.5 0.9 copy-start.4
  3.4 0.8 copy-start.5
  4.1 0.7 copy-start.6
  4.8 0.7 copy-start.7
  6.7 24.4 %collective-permute-start.7 = (bf16[224,768]{1,0:T(8,128)(2,1)S(1)}, bf16[224,768]{1,0:T(8,128)(2,1)S(1)}, u32[]{:S(2)}, u32[]{:S(2)}) collective-permute-start(bf16[224,768]{1,0:T(8,128)(2,1)S(1)} %get-tuple-element.44.p0), channel_id=1, source_target_pairs={{0,1},{1,0},{2,3},{3,2},{4,5},{5,4},{6,7},{7,6},{8,9},{9,8},{10,11... | collective-permute-start | bytes 1032200 | tf_op jit(solution)/shard_map/ppermute | solution.py:352
  9.1 22.0 %collective-permute-start.8 = (bf16[224,768]{1,0:T(8,128)(2,1)S(1)}, bf16[224,768]{1,0:T(8,128)(2,1)S(1)}, u32[]{:S(2)}, u32[]{:S(2)}) collective-permute-start(bf16[224,768]{1,0:T(8,128)(2,1)S(1)} %get-tuple-element.44.p0), channel_id=1, source_target_pairs={{0,2},{1,3},{2,0},{3,1},{4,6},{5,7},{6,4},{7,5},{8,10},{9,11},{10,... | collective-permute-start | bytes 1032200 | tf_op jit(solution)/shard_map/ppermute | solution.py:352
  9.7 21.4 %collective-permute-start.9 = (bf16[224,768]{1,0:T(8,128)(2,1)S(1)}, bf16[224,768]{1,0:T(8,128)(2,1)S(1)}, u32[]{:S(2)}, u32[]{:S(2)}) collective-permute-start(bf16[224,768]{1,0:T(8,128)(2,1)S(1)} %get-tuple-element.44.p0), channel_id=1, source_target_pairs={{0,3},{1,2},{2,1},{3,0},{4,7},{5,6},{6,5},{7,4},{8,11},{9,10},{10,... | collective-permute-start | bytes 1032200 | tf_op jit(solution)/shard_map/ppermute | solution.py:352
  10.6 2.0 %copy-start = (bf16[256,6912]{1,0:T(8,128)(2,1)S(1)}, bf16[256,6912]{1,0:T(8,128)(2,1)}, u32[]{:S(2)}) copy-start(bf16[256,6912]{1,0:T(8,128)(2,1)} %weight.2) | copy-start | bytes 10616836
  12.6 24.1 %copy-start.1 = (bf16[256,6912]{1,0:T(8,128)(2,1)S(1)}, bf16[256,6912]{1,0:T(8,128)(2,1)}, u32[]{:S(2)}) copy-start(bf16[256,6912]{1,0:T(8,128)(2,1)} %weight.3) | copy-start | bytes 10616836
  19.1 1.3 %collective-permute-start = (bf16[96,256]{1,0:T(8,128)(2,1)S(1)}, bf16[96,256]{1,0:T(8,128)(2,1)S(1)}, u32[]{:S(2)}, u32[]{:S(2)}) collective-permute-start(bf16[96,256]{1,0:T(8,128)(2,1)S(1)} %get-tuple-element.36), channel_id=1, source_target_pairs={{0,4},{4,0},{8,12},{12,8},{16,20},{20,16},{24,28},{28,24},{32,36},... | collective-permute-start | bytes 147464 | tf_op jit(solution)/shard_map/ppermute | solution.py:348
  19.2 1.2 %collective-permute-start.1 = (bf16[96,256]{1,0:T(8,128)(2,1)S(1)}, bf16[96,256]{1,0:T(8,128)(2,1)S(1)}, u32[]{:S(2)}, u32[]{:S(2)}) collective-permute-start(bf16[96,256]{1,0:T(8,128)(2,1)S(1)} %get-tuple-element.37), channel_id=1, source_target_pairs={{4,8},{8,4},{12,16},{16,12},{20,24},{24,20},{28,32},{32,28},{36,40... | collective-permute-start | bytes 147464 | tf_op jit(solution)/shard_map/ppermute | solution.py:348
  21.0 5.6 %collective-permute-start.2 = (bf16[96,256]{1,0:T(8,128)(2,1)S(1)}, bf16[96,256]{1,0:T(8,128)(2,1)S(1)}, u32[]{:S(2)}, u32[]{:S(2)}) collective-permute-start(bf16[96,256]{1,0:T(8,128)(2,1)S(1)} %get-tuple-element.39.late), channel_id=1, source_target_pairs={{0,1},{1,0},{2,3},{3,2},{4,5},{5,4},{6,7},{7,6},{8,9},{9,8},{10,11... | collective-permute-start | bytes 147464 | tf_op jit(solution)/shard_map/ppermute | solution.py:348
  24.2 6.0 %collective-permute-start.3 = (bf16[96,256]{1,0:T(8,128)(2,1)S(1)}, bf16[96,256]{1,0:T(8,128)(2,1)S(1)}, u32[]{:S(2)}, u32[]{:S(2)}) collective-permute-start(bf16[96,256]{1,0:T(8,128)(2,1)S(1)} %get-tuple-element.40), channel_id=1, source_target_pairs={{1,2},{2,1},{5,6},{6,5},{9,10},{10,9},{13,14},{14,13},{17,18},{18,... | collective-permute-start | bytes 147464 | tf_op jit(solution)/shard_map/ppermute | solution.py:348
  32.2 18.6 %collective-permute-start.10 = (bf16[4,96,512]{2,1,0:T(8,128)(2,1)S(1)}, bf16[4,96,512]{2,1,0:T(8,128)(2,1)S(1)}, u32[]{:S(2)}, u32[]{:S(2)}) collective-permute-start(bf16[4,96,512]{2,1,0:T(8,128)(2,1)S(1)} %get-tuple-element.45), channel_id=1, source_target_pairs={{0,4},{4,0},{8,12},{12,8},{16,20},{20,16},{24,28},{28,24},{32,36},... | collective-permute-start | bytes 1179656 | tf_op jit(solution)/shard_map/ppermute | solution.py:348
  35.8 15.0 %collective-permute-start.11 = (bf16[4,96,512]{2,1,0:T(8,128)(2,1)S(1)}, bf16[4,96,512]{2,1,0:T(8,128)(2,1)S(1)}, u32[]{:S(2)}, u32[]{:S(2)}) collective-permute-start(bf16[4,96,512]{2,1,0:T(8,128)(2,1)S(1)} %get-tuple-element.46), channel_id=1, source_target_pairs={{4,8},{8,4},{12,16},{16,12},{20,24},{24,20},{28,32},{32,28},{36,40... | collective-permute-start | bytes 1179656 | tf_op jit(solution)/shard_map/ppermute | solution.py:348
  43.2 3.7 %collective-permute-start.12 = (bf16[96,256]{1,0:T(8,128)(2,1)S(1)}, bf16[96,256]{1,0:T(8,128)(2,1)S(1)}, u32[]{:S(2)}, u32[]{:S(2)}) collective-permute-start(bf16[96,256]{1,0:T(8,128)(2,1)S(1)} %get-tuple-element.52), channel_id=1, source_target_pairs={{0,4},{4,0},{8,12},{12,8},{16,20},{20,16},{24,28},{28,24},{32,36},... | collective-permute-start | bytes 147464 | tf_op jit(solution)/shard_map/ppermute | solution.py:348
  46.0 3.9 %collective-permute-start.13 = (bf16[96,256]{1,0:T(8,128)(2,1)S(1)}, bf16[96,256]{1,0:T(8,128)(2,1)S(1)}, u32[]{:S(2)}, u32[]{:S(2)}) collective-permute-start(bf16[96,256]{1,0:T(8,128)(2,1)S(1)} %get-tuple-element.53), channel_id=1, source_target_pairs={{4,8},{8,4},{12,16},{16,12},{20,24},{24,20},{28,32},{32,28},{36,40... | collective-permute-start | bytes 147464 | tf_op jit(solution)/shard_map/ppermute | solution.py:348
  46.6 10.1 %collective-permute-start.4 = (bf16[192,256]{1,0:T(8,128)(2,1)S(1)}, bf16[192,256]{1,0:T(8,128)(2,1)S(1)}, u32[]{:S(2)}, u32[]{:S(2)}) collective-permute-start(bf16[192,256]{1,0:T(8,128)(2,1)S(1)} %get-tuple-element.43.g0), channel_id=1, source_target_pairs={{0,1},{1,0},{2,3},{3,2},{4,5},{5,4},{6,7},{7,6},{8,9},{9,8},{10,11... | collective-permute-start | bytes 294920 | tf_op jit(solution)/shard_map/ppermute | solution.py:352
  46.8 9.9 %collective-permute-start.5 = (bf16[192,256]{1,0:T(8,128)(2,1)S(1)}, bf16[192,256]{1,0:T(8,128)(2,1)S(1)}, u32[]{:S(2)}, u32[]{:S(2)}) collective-permute-start(bf16[192,256]{1,0:T(8,128)(2,1)S(1)} %get-tuple-element.43.g0), channel_id=1, source_target_pairs={{0,2},{1,3},{2,0},{3,1},{4,6},{5,7},{6,4},{7,5},{8,10},{9,11},{10,... | collective-permute-start | bytes 294920 | tf_op jit(solution)/shard_map/ppermute | solution.py:352
  49.9 6.8 %collective-permute-start.6 = (bf16[192,256]{1,0:T(8,128)(2,1)S(1)}, bf16[192,256]{1,0:T(8,128)(2,1)S(1)}, u32[]{:S(2)}, u32[]{:S(2)}) collective-permute-start(bf16[192,256]{1,0:T(8,128)(2,1)S(1)} %get-tuple-element.43.g0), channel_id=1, source_target_pairs={{0,3},{1,2},{2,1},{3,0},{4,7},{5,6},{6,5},{7,4},{8,11},{9,10},{10,... | collective-permute-start | bytes 294920 | tf_op jit(solution)/shard_map/ppermute | solution.py:352
  58.5 12.5 %collective-permute-start.14 = (bf16[128,1792]{1,0:T(8,128)(2,1)S(1)}, bf16[128,1792]{1,0:T(8,128)(2,1)S(1)}, u32[]{:S(2)}, u32[]{:S(2)}) collective-permute-start(bf16[128,1792]{1,0:T(8,128)(2,1)S(1)} %get-tuple-element.56), channel_id=1, source_target_pairs={{0,4},{4,0},{8,12},{12,8},{16,20},{20,16},{24,28},{28,24},{32,36},... | collective-permute-start | bytes 1376264 | tf_op jit(solution)/shard_map/ppermute | solution.py:352
  61.5 9.5 %collective-permute-start.15 = (bf16[128,1792]{1,0:T(8,128)(2,1)S(1)}, bf16[128,1792]{1,0:T(8,128)(2,1)S(1)}, u32[]{:S(2)}, u32[]{:S(2)}) collective-permute-start(bf16[128,1792]{1,0:T(8,128)(2,1)S(1)} %get-tuple-element.58), channel_id=1, source_target_pairs={{0,4},{4,0},{8,12},{12,8},{16,20},{20,16},{24,28},{28,24},{32,36},... | collective-permute-start | bytes 1376264 | tf_op jit(solution)/shard_map/ppermute | solution.py:352
  61.6 4.8 %collective-permute-start.16 = (bf16[96,256]{1,0:T(8,128)(2,1)S(1)}, bf16[96,256]{1,0:T(8,128)(2,1)S(1)}, u32[]{:S(2)}, u32[]{:S(2)}) collective-permute-start(bf16[96,256]{1,0:T(8,128)(2,1)S(1)} %get-tuple-element.54.late), channel_id=1, source_target_pairs={{0,1},{1,0},{2,3},{3,2},{4,5},{5,4},{6,7},{7,6},{8,9},{9,8},{10,11... | collective-permute-start | bytes 147464 | tf_op jit(solution)/shard_map/ppermute | solution.py:348
  62.7 6.0 %collective-permute-start.17 = (bf16[96,256]{1,0:T(8,128)(2,1)S(1)}, bf16[96,256]{1,0:T(8,128)(2,1)S(1)}, u32[]{:S(2)}, u32[]{:S(2)}) collective-permute-start(bf16[96,256]{1,0:T(8,128)(2,1)S(1)} %get-tuple-element.59), channel_id=1, source_target_pairs={{1,2},{2,1},{5,6},{6,5},{9,10},{10,9},{13,14},{14,13},{17,18},{18,... | collective-permute-start | bytes 147464 | tf_op jit(solution)/shard_map/ppermute | solution.py:348
  69.6 1.3 %collective-permute-start.18 = (bf16[128,256]{1,0:T(8,128)(2,1)S(1)}, bf16[128,256]{1,0:T(8,128)(2,1)S(1)}, u32[]{:S(2)}, u32[]{:S(2)}) collective-permute-start(bf16[128,256]{1,0:T(8,128)(2,1)S(1)} %get-tuple-element.62), channel_id=1, source_target_pairs={{0,4},{4,0},{8,12},{12,8},{16,20},{20,16},{24,28},{28,24},{32,36},... | collective-permute-start | bytes 196616 | tf_op jit(solution)/shard_map/ppermute | solution.py:352

commit v3 on v2

--- a/solution.py
+++ b/solution.py
@@ -103,38 +103,32 @@
     srow[...] = jnp.broadcast_to(total.astype(jnp.int32) - 1, srow.shape)
 
 
-def spread_kernel(place, nbt, grad, weight, own, m1, m2, loc, held, acc, sems):
-    copies = [
-        pltpu.make_async_copy(
-            weight.at[:, n * 9 * C : (n + 1) * 9 * C], held.at[n], sems.at[n]
-        )
-        for n in range(3)
-    ]
-    for copy in copies:
-        copy.start()
+def spread_terms(place, nbt, grad, weight, own, m1, m2, loc, acc):
     rows = iota((EXT, C), 0)
     table = nbt[...].astype(jnp.int32)
     gradient = grad[...]
     none = jnp.zeros((C - S, C), BF)
-    for n in range(3):
-        masks, terms = [], []
-        for part in range(9):
-            k = 9 * n + part
-            masks.append(onehot(rows == table[k : k + 1, :]))
-        copies[n].wait()
-        for part in range(9):
-            terms += [mm(gradient, held[n, :, part * C : (part + 1) * C]).astype(BF), none]
-        total = mm(jnp.concatenate(masks, axis=1), jnp.concatenate(terms, axis=0))
-        if n:
-            acc[...] += total
-        else:
-            acc[...] = total
+    masks, terms = [], []
+    for k in range(K):
+        masks.append(onehot(rows == table[k : k + 1, :]))
+        terms += [mm(gradient, weight[:, k * C : (k + 1) * C]).astype(BF), none]
+    acc[...] = mm(jnp.concatenate(masks, axis=1), jnp.concatenate(terms, axis=0))
     even = place[0] % 2 == 0
     own[...] = acc[0:S, :]
     first, last = jnp.where(even, S, S + 160), jnp.where(even, S + 160, S)
-    m1[...] = acc[pl.ds(pl.multiple_of(first, 32), 96), :].astype(BF)
-    m2[...] = acc[pl.ds(pl.multiple_of(last, 32), 96), :].astype(BF)
+    m1[0:96, :] = acc[pl.ds(pl.multiple_of(first, 32), 96), :].astype(BF)
+    m2[0:96, :] = acc[pl.ds(pl.multiple_of(last, 32), 96), :].astype(BF)
     loc[...] = acc[S + 96 : S + 160, :].astype(BF)
+
+
+def spread_kernel(place, nbt, grad, weight, own, m1, m2, loc, acc):
+    spread_terms(place, nbt, grad, weight, own, m1, m2, loc, acc)
+
+
+def spread_with_kernel(place, nbt, grad, weight, o1, o2, own, m1, m2, loc, acc):
+    m1[96:, :] = o1[...]
+    m2[96:, :] = o2[...]
+    spread_terms(place, nbt, grad, weight, own, m1, m2, loc, acc)
 
 
 def pass_kernel(place, loc, m1, m2, n1, n2):
@@ -159,7 +153,7 @@
     return own[...] + mm(halo_matrix(hrow[0:1, :]), rows)
 
 
-def gate_kernel(place, own, m1, m2, n1, n2, hrow, pre, out, ordered, back):
+def gate_kernel(place, own, m1, m2, n1, n2, hrow, pre, late, out, ordered, back):
     hidden_grad = settled(place, own, m1, m2, n1, n2, hrow, back)
     z = pre[...].astype(F32)
     g = 1.0 / (1.0 + jnp.exp(-z))
@@ -168,7 +162,7 @@
     ordered[...] = mm(value, channel_order()).astype(BF)
 
 
-def rows_kernel(place, own, m1, m2, n1, n2, hrow, grad, srow, keep, send, back):
+def rows_kernel(place, own, m1, m2, n1, n2, hrow, grad, srow, late, keep, send, back):
     total = settled(place, own, m1, m2, n1, n2, hrow, back)
     value = (grad[...].astype(F32) + total).astype(BF)
     chosen = mm_t(onehot(iota((S, C), 0) == srow[0:1, :]), value).astype(BF)
@@ -190,18 +184,19 @@
         for b in (-1, 0, 1):
             source = tile - b
             at = HB * (b + 1)
-            inside = 0 <= source < 4
-            o1[tile, at : at + HB, :] = picked[source, pl.ds(up + at, HB), :] if inside else none
-            o2[tile, at : at + HB, :] = picked[source, pl.ds(down + at, HB), :] if inside else none
+            for out, side in ((o1, up), (o2, down)):
+                rows = picked[source, pl.ds(side + at, HB), :] if 0 <= source < 4 else none
+                to = 96 * tile + at
+                out[to : to + HB, :] = rows[:, 0:C]
+                out[to + 384 : to + 384 + HB, :] = rows[:, C : 2 * C]
             if b:
                 to = 0 if b < 0 else HB
-                loc[tile, to : to + HB, :] = (
-                    picked[source, 96 + to : 96 + to + HB, :] if inside else none
-                )
+                rows = picked[source, 96 + to : 96 + to + HB, :] if 0 <= source < 4 else none
+                loc[tile, to : to + HB, :] = rows
 
 
 def columns_kernel(
-    place, p0, p1, p2, p3, r1, r2, loc, late, keep, send, cols_one, cols_two, ext, gt, ids, sel
+    place, p0, p1, p2, p3, r1, r2, loc, late, gt, cols_one, cols_two, ext, ids, sel
 ):
     column = place[1]
     start = column * QW
@@ -213,17 +208,17 @@
     early = lane < C - offset
     for turn, pay in enumerate((p0, p1, p2, p3)):
         tile = column ^ turn
-        above, below = r1[tile], r2[tile]
-        pieces = (
-            (0, pay[0:S, 0 : 2 * C]),
-            (S, jnp.where(even, above, below)),
-            (S + 96, loc[tile]),
-            (S + 160, jnp.where(even, below, above)),
-        )
-        for at, piece in pieces:
-            size = piece.shape[0]
-            ext[at : at + size, 0:C] = mm(piece[:, 0:C], shift).astype(BF)
-            ext[at : at + size, C : 2 * C] = mm(piece[:, C : 2 * C], shift).astype(BF)
+        for half in range(2):
+            lanes = slice(half * C, (half + 1) * C)
+            at = pl.multiple_of(96 + 384 * half + 96 * tile, 32)
+            above, below = r1[pl.ds(at, 96), :], r2[pl.ds(at, 96), :]
+            for to, piece in (
+                (0, pay[0:S, lanes]),
+                (S, jnp.where(even, above, below)),
+                (S + 96, loc[tile, :, lanes]),
+                (S + 160, jnp.where(even, below, above)),
+            ):
+                ext[to : to + piece.shape[0], lanes] = mm(piece, shift).astype(BF)
         gt[:, turn * S : (turn + 1) * S] = jnp.transpose(
             pay[0:S, 2 * C : 3 * C].astype(F32)
         ).astype(BF)
@@ -244,7 +239,6 @@
                 cols_one[turn * S : (turn + 1) * S, at : at + C] = merged[:, 0:C]
                 cols_two[turn * S : (turn + 1) * S, at : at + C] = merged[:, C : 2 * C]
             previous = block
-    weight_blocks(place, gt, cols_two, keep, send)
 
 
 def weight_blocks(place, gt, cols, keep, send):
@@ -258,37 +252,56 @@
             ).astype(BF)
 
 
-def weight_kernel(place, g0, g1, g2, g3, cols, late, keep, send, gt):
+def weight_two_kernel(place, gt, cols, late, keep, send):
+    weight_blocks(place, gt, cols, keep, send)
+
+
+def weight_one_kernel(place, g0, g1, g2, g3, cols, late, keep, send, gt):
     for turn, grad in enumerate((g0, g1, g2, g3)):
         gt[:, turn * S : (turn + 1) * S] = jnp.transpose(grad[...].astype(F32)).astype(BF)
     weight_blocks(place, gt, cols, keep, send)
 
 
-def merge_kernel(place, k1, s1, k2, s2, rk, rs, out):
-    row, col = iota((C, 128), 0), iota((C, 128), 1)
-    for part in range(7):
-        at = slice(part * C, (part + 1) * C)
-        total = jnp.zeros((C, C), F32)
-        for which, refs in enumerate(((k1, s1), (k2, s2))):
-            place_of = onehot((row // 8 == col // 4) & (row % 8 == 4 * which + col % 4))
-            for ref in refs:
-                total = total + mm(place_of, ref[:, at])
-        out[:, at] = total.astype(BF)
+def merge_kernel(place, k1, s1, k2, s2, rk, rs, *outs):
+    row, col = iota((64, 128), 0), iota((64, 128), 1)
     mine = place[0] % 2
-    total = jnp.zeros((C, C), F32)
-    for ref, core in ((rk, mine), (rs, 1 - mine)):
-        spot = (row // 8 == col % 32) & (row % 8 == 3 * core + col // 32) & (col < 96)
-        total = total + mm(onehot(spot), ref[...])
-    out[:, 7 * C : 8 * C] = total.astype(BF)
+    line = place[0] // 16
+    for turn, out in enumerate(outs):
+        chip = 8 * (line ^ turn) + row // 8
+        for part in range(7):
+            at = slice(part * C, (part + 1) * C)
+            total = jnp.zeros((64, C), F32)
+            for which, refs in enumerate(((k1, s1), (k2, s2))):
+                spot = onehot((chip == col // 4) & (row % 8 == 4 * which + col % 4))
+                for ref in refs:
+                    total = total + mm(spot, ref[:, at])
+            out[:, at] = total.astype(BF)
+        total = jnp.zeros((64, C), F32)
+        for ref, core in ((rk, mine), (rs, 1 - mine)):
+            spot = (chip == col % 32) & (row % 8 == 3 * core + col // 32) & (col < 96)
+            total = total + mm(onehot(spot), ref[...])
+        out[:, 7 * C : 8 * C] = total.astype(BF)
+
+
+def line_kernel(place, a0, a1, a2, a3, out):
+    line = place[0] // 16
+    total = jnp.zeros((64, 7 * C), F32)
+    for turn, part in enumerate((a0, a1, a2, a3)):
+        total = total + part[:, 0 : 7 * C].astype(F32)
+        at = pl.multiple_of(7 * C + (line ^ turn) * C, C)
+        out[:, pl.ds(at, C)] = part[:, 7 * C : 8 * C]
+    out[:, 0 : 7 * C] = total.astype(BF)
 
 
 def final_kernel(scale, arrived, rows, one, two):
     total = jnp.sum(arrived[:, :, 0 : 7 * C].astype(F32), axis=0) * scale
     one[...] = total[0:4, 0:QW]
     two[...] = total[4:8, 0:QW]
-    to, at = iota((S, C), 0), iota((S, C), 1)
-    spot = (at // 8 == to // 6) & (at % 8 == to % 6)
-    rows[...] = mm(onehot(spot), arrived[:, :, 7 * C : 8 * C].reshape(C, C)).astype(BF)
+    to, at = iota((48, 64), 0), iota((48, 64), 1)
+    spot = onehot((at // 8 == to // 6) & (at % 8 == to % 6))
+    for line in range(4):
+        piece = arrived[:, :, (7 + line) * C : (8 + line) * C].reshape(64, C)
+        rows[48 * line : 48 * line + 48, :] = mm(spot, piece).astype(BF)
 
 
 def sds(shape, dtype):
@@ -301,7 +314,7 @@
 ANY = pl.BlockSpec(memory_space=pl.ANY)
 
 
-def call(kernel, outs, *args, scratch=(), specs=None, late=0, flops=10**8):
+def call(kernel, outs, *args, scratch=(), specs=None, late=0, flops=10**5):
     if specs is None:
         specs = [SMEM] + [VM] * (len(args) - 1 - late) + [ANY] * late
     return pl.pallas_call(
@@ -311,26 +324,21 @@
         out_specs=jax.tree.map(lambda _: VM, outs),
         scratch_shapes=list(scratch),
         compiler_params=pltpu.CompilerParams(vmem_limit_bytes=40 * 2**20),
-        cost_estimate=pl.CostEstimate(flops=flops, bytes_accessed=10**6, transcendentals=0),
+        cost_estimate=pl.CostEstimate(flops=flops, bytes_accessed=10**4, transcendentals=0),
     )(*args)
 
 
-def spread(place, nbt, grad, weight):
-    edge = sds((96, C), BF)
+def spread(place, nbt, grad, weight, *picks):
+    edge = sds((96 + (picks[0].shape[0] if picks else 0), C), BF)
     return call(
-        spread_kernel,
+        spread_with_kernel if picks else spread_kernel,
         (sds((S, C), F32), edge, edge, sds((64, C), BF)),
         place,
         nbt,
         grad,
         weight,
-        specs=[SMEM, VM, VM, HBM],
-        scratch=[
-            pltpu.VMEM((3, C, 9 * C), BF),
-            pltpu.VMEM((EXT, C), F32),
-            pltpu.SemaphoreType.DMA((3,)),
-        ],
-        flops=4 * 10**9,
+        *picks,
+        scratch=[pltpu.VMEM((EXT, C), F32)],
     )
 
 
@@ -374,13 +382,19 @@
             tile,
         ),
         place,
-        features,
-        pre_act,
-        grad_out,
-        neighbours.T,
-        halo_list,
-        jnp.transpose(send_list, (2, 0, 1)),
+        *[
+            pltpu.with_memory_space_constraint(value, pltpu.HBM)
+            for value in (
+                features,
+                pre_act,
+                grad_out,
+                neighbours.T,
+                halo_list,
+                jnp.transpose(send_list, (2, 0, 1)),
+            )
+        ],
         specs=[SMEM] + [HBM] * 6,
+        flops=4 * 10**9,
         scratch=[
             pltpu.VMEM((K, S), jnp.int32),
             pltpu.VMEM((1, 8, 24), jnp.int32),
@@ -392,7 +406,7 @@
     own, m1, m2, loc = spread(place, nbt, grad, weight_two)
     back = pltpu.VMEM((8, HB, C), BF)
     arrived, passed = give_back(place, loc, m1, m2)
-    picks = sds((4, 96, 2 * C), BF)
+    picks = sds((768, C), BF)
     o1, o2, near = call(
         pick_kernel,
         (picks, picks, sds((4, 64, 2 * C), BF)),
@@ -402,55 +416,74 @@
         scratch=[pltpu.VMEM((4, 8 * HB, 2 * C), BF)],
         late=1,
     )
-    r1, r2 = swap(o1, "gx", 1), swap(o2, "gx", 2)
     grad_pre, ordered = call(
-        gate_kernel, (tile, tile), place, own, *arrived, hrow, pre, scratch=[back]
+        gate_kernel,
+        (tile, tile),
+        place,
+        own,
+        *arrived,
+        hrow,
+        pre,
+        near,
+        scratch=[back],
+        late=1,
     )
     grads = [ordered] + [cross(ordered, "gy", d) for d in (1, 2, 3)]
-    own, m1, m2, loc = spread(place, nbt, grad_pre, weight_one)
+    own, m1, m2, loc = spread(place, nbt, grad_pre, weight_one, o1, o2)
+    arrived, passed = give_back(place, loc, m1, m2)
     wide = 7 * C
     half = sds((128, wide), BF)
-    keep_two, send_two, cols_one = call(
+    stack = sds((4 * S, wide), BF)
+    turned, cols_one, cols_two = call(
         columns_kernel,
-        (half, half, sds((4 * S, wide), BF)),
+        (sds((C, 4 * S), BF), stack, stack),
         place,
         *pays,
-        r1,
-        r2,
+        arrived[0],
+        arrived[1],
         near,
-        own,
+        passed,
         scratch=[
-            pltpu.VMEM((4 * S, wide), BF),
             pltpu.VMEM((EXT, 2 * C), BF),
-            pltpu.VMEM((C, 4 * S), BF),
             pltpu.VMEM((32, C), F32),
             pltpu.VMEM((128, C), F32),
         ],
         late=1,
-        flops=4 * 10**9,
+    )
+    some = sds((128, C), BF)
+    rows_keep, rows_send = call(
+        rows_kernel,
+        (some, some),
+        place,
+        own,
+        *arrived,
+        hrow,
+        grad,
+        srow,
+        turned,
+        scratch=[back],
+        late=1,
+    )
+    rows_come = cross(rows_send, "gx", 1)
+    keep_two, send_two = call(
+        weight_two_kernel, (half, half), place, turned, cols_two, rows_keep, late=1
     )
     come_two = cross(send_two, "gx", 1)
-    arrived, passed = give_back(place, loc, m1, m2)
     keep_one, send_one = call(
-        weight_kernel,
+        weight_one_kernel,
         (half, half),
         place,
         *grads,
         cols_one,
-        passed,
+        keep_two,
         scratch=[pltpu.VMEM((C, 4 * S), BF)],
         late=1,
-        flops=10**9,
     )
     come_one = cross(send_one, "gx", 1)
-    some = sds((128, C), BF)
-    rows_keep, rows_send = call(
-        rows_kernel, (some, some), place, own, *arrived, hrow, grad, srow, scratch=[back]
-    )
-    rows_come = cross(rows_send, "gx", 1)
-    merged = call(
+    chunk = sds((64, 8 * C), BF)
+    chunks = call(
         merge_kernel,
-        sds((C, 8 * C), BF),
+        (chunk,) * 4,
         place,
         keep_one,
         come_one,
@@ -459,9 +492,11 @@
         rows_keep,
         rows_come,
     )
-    groups = [[2 * c + e for c in range(gx // 2)] for e in range(2)]
+    chunks = [chunks[0]] + [cross(chunks[d], "gx", 16 * d) for d in (1, 2, 3)]
+    summed = call(line_kernel, sds((64, 11 * C), BF), place, *chunks)
+    groups = [[16 * y + 2 * z + e for z in range(8)] for y in range(4) for e in range(2)]
     collected = lax.all_to_all(
-        merged.reshape(gx // 2, 8, 8 * C),
+        summed.reshape(8, 8, 11 * C),
         "gx",
         split_axis=0,
         concat_axis=0,

time: 116 us -> 101 us (0.87)
  blocking collectives: 41.1 us -> 17 us
  waiting for transfers between devices: 7.89 us -> 22.1 us
  local copies, waits for them, and re-layouts: 6.8 us -> 0.01 us
  starting transfers between devices: 29.5 us -> 36 us
  Pallas kernels: 28.4 us -> 23.9 us
    all_to_all x1, blocking collectives: 41.1 us -> 17 us  [body(): lax.all_to_all(summed.reshape(8, 8, 11 * C), 'gx', split_axis=0, concat_a...]
    ppermute x9 -> x12, waiting for transfers between devices: 1.26 us -> 21.6 us  [cross(): lax.ppermute(value, axis, [(n, n ^ mask) for n in range(lax.axis_size(axi...]
    ppermute x9 -> x12, starting transfers between devices: 10.6 us -> 22.8 us  [cross(): lax.ppermute(value, axis, [(n, n ^ mask) for n in range(lax.axis_size(axi...]
    unnamed x16 -> x4, local copies, waits for them, and re-layouts: 6.8 us -> 0.01 us
    ppermute x10 -> x8, waiting for transfers between devices: 6.63 us -> 0.56 us  [swap(): return lax.ppermute(value, axis, pairs)]
    ppermute x10 -> x8, starting transfers between devices: 18.9 us -> 13.2 us  [swap(): return lax.ppermute(value, axis, pairs)]
    pallas_call x12 -> x14, Pallas kernels: 28.4 us -> 23.9 us  [call(): pl.pallas_call(kernel, out_shape=outs, in_specs=specs, out_specs=jax.tree...]
  transfers between devices with their start and end apart: 19 -> 20, of which waited for: 5 -> 7; matrix products, arithmetic and copies ran while one was open for 0% -> 0% of each run, Pallas kernels for 19% -> 13%
where the time goes in v3:
time: 101 us; the launch traced here: 100 us
  starting transfers between devices  36 us (36%)
  Pallas kernels  23.9 us (24%)
  waiting for transfers between devices  22.1 us (22%)
  blocking collectives  17 us (17%)
    pallas_call x14, Pallas kernels, call(): pl.pallas_call(kernel, out_shape=outs, in_specs=specs, out_specs=jax.tree...  23.9 us
    ppermute x12, starting transfers between devices, cross(): lax.ppermute(value, axis, [(n, n ^ mask) for n in range(lax.axis_size(axi...  22.8 us
    ppermute x12, waiting for transfers between devices, cross(): lax.ppermute(value, axis, [(n, n ^ mask) for n in range(lax.axis_size(axi...  21.6 us
    all_to_all x1, blocking collectives, body(): lax.all_to_all(summed.reshape(8, 8, 11 * C), 'gx', split_axis=0, concat_a...  17 us
    ppermute x8, starting transfers between devices, swap(): return lax.ppermute(value, axis, pairs)  13.2 us
  transfers between devices with their start and end apart: 20, of which 7 were waited for; matrix products, arithmetic and copies ran while one was open for 0% of the time, Pallas kernels for 13%

profile of v3, /device:TPU:2, one launch (start us, length us, event | category | flops | bytes accessed | tf_op | source)
XLA Modules:
  0.0 100.0 jit_solution(690217329758076104)
XLA Ops:
  0.6 0.1 pad_add_fusion.place
  0.7 0.0 copy-start.1
  0.7 2.1 %shard_map.103 = (bf16[224,768]{1,0:T(8,128)(2,1)S(1)}, f32[32,256]{1,0:T(8,128)S(1)}, s32[8,256]{1,0:T(8,128)S(1)}, s32[8,256]{1,0:T(8,128)S(1)}, bf16[192,256]...) custom-call(s32[2]{0:T(128)S(1)} %pad_add_fusion.place, bf16[192,256]{1,0:T(8,128)(2,1)} %feat.1, bf16[192,256]{1,0:T(8,128)(2,1)} %pre.1, ...), custom_call_target="tpu_custom_call" | custom-call | flops 4000000000 | bytes 10000 | tf_op jit(solution)/shard_map/pallas_call | solution.py:320
  2.9 0.0 copy-start
  2.9 2.4 %collective-permute-start.4 = (bf16[224,768]{1,0:T(8,128)(2,1)S(1)}, bf16[224,768]{1,0:T(8,128)(2,1)S(1)}, u32[]{:S(2)}, u32[]{:S(2)}) collective-permute-start(bf16[224,768]{1,0:T(8,128)(2,1)S(1)} %get-tuple-element.49.p0), channel_id=1, source_target_pairs={{0,1},{1,0},{2,3},{3,2},{4,5},{5,4},{6,7},{7,6},{8,9},{9,8},{10,11... | collective-permute-start | bytes 1032200 | tf_op jit(solution)/shard_map/ppermute | solution.py:360
  5.2 0.7 collective-permute-start.5
  5.9 0.9 collective-permute-start.6
  6.8 0.0 copy-done.1
  6.8 3.0 %shard_map.104 = (f32[192,256]{1,0:T(8,128)S(1)}, bf16[96,256]{1,0:T(8,128)(2,1)S(1)}, bf16[96,256]{1,0:T(8,128)(2,1)S(1)}, bf16[64,256]{1,0:T(8,128)(2,1)S(1)}) custom-call(s32[2]{0:T(128)S(1)} %pad_add_fusion.place, f32[32,256]{1,0:T(8,128)S(1)} %get-tuple-element.39.nbt, bf16[192,256]{1,0:T(8,128)(2,1)S(1)} %get-tuple-element.40.grad, ...), custom_call_target="tpu_custom_call" | custom-call | flops 100000 | bytes 10000 | tf_op jit(solution)/shard_map/pallas_call | solution.py:320
  9.9 0.1 collective-permute-start
  10.0 0.7 collective-permute-start.1
  10.6 0.5 collective-permute-done.m1
  11.2 0.0 collective-permute-done.1.m2
  11.2 0.6 shard_map.105
  11.7 3.2 %collective-permute-start.2 = (bf16[96,256]{1,0:T(8,128)(2,1)S(1)}, bf16[96,256]{1,0:T(8,128)(2,1)S(1)}, u32[]{:S(2)}, u32[]{:S(2)}) collective-permute-start(bf16[96,256]{1,0:T(8,128)(2,1)S(1)} %get-tuple-element.45.late), channel_id=1, source_target_pairs={{0,1},{1,0},{2,3},{3,2},{4,5},{5,4},{6,7},{7,6},{8,9},{9,8},{10,11... | collective-permute-start | bytes 147464 | tf_op jit(solution)/shard_map/ppermute | solution.py:356
  15.0 2.3 %collective-permute-start.3 = (bf16[96,256]{1,0:T(8,128)(2,1)S(1)}, bf16[96,256]{1,0:T(8,128)(2,1)S(1)}, u32[]{:S(2)}, u32[]{:S(2)}) collective-permute-start(bf16[96,256]{1,0:T(8,128)(2,1)S(1)} %get-tuple-element.46), channel_id=1, source_target_pairs={{1,2},{2,1},{5,6},{6,5},{9,10},{10,9},{13,14},{14,13},{17,18},{18,... | collective-permute-start | bytes 147464 | tf_op jit(solution)/shard_map/ppermute | solution.py:356
  17.3 0.0 collective-permute-done.4.p1
  17.3 4.2 %collective-permute-done.5.p2 = bf16[224,768]{1,0:T(8,128)(2,1)S(1)} collective-permute-done((bf16[224,768]{1,0:T(8,128)(2,1)S(1)}, bf16[224,768]{1,0:T(8,128)(2,1)S(1)}, u32[]{:S(2)}, u32[]{:S(2)}) %collective-permute-start.5) | collective-permute-done | bytes 344096 | tf_op jit(solution)/shard_map/ppermute | solution.py:360
  21.5 1.0 %collective-permute-done.6.p3 = bf16[224,768]{1,0:T(8,128)(2,1)S(1)} collective-permute-done((bf16[224,768]{1,0:T(8,128)(2,1)S(1)}, bf16[224,768]{1,0:T(8,128)(2,1)S(1)}, u32[]{:S(2)}, u32[]{:S(2)}) %collective-permute-start.6) | collective-permute-done | bytes 344096 | tf_op jit(solution)/shard_map/ppermute | solution.py:360
  22.5 1.1 %shard_map.106 = (bf16[768,256]{1,0:T(8,128)(2,1)S(1)}, bf16[768,256]{1,0:T(8,128)(2,1)S(1)}, bf16[4,64,512]{2,1,0:T(8,128)(2,1)S(1)}) custom-call(s32[2]{0:T(128)S(1)} %pad_add_fusion.place, bf16[224,768]{1,0:T(8,128)(2,1)S(1)} %get-tuple-element.49.p0, bf16[224,768]{1,0:T(8,128)(2,1)S(1)} %collective-permute-done.4.p1, ...), custom_call_target="tpu_custom_call" | custom-call | flops 100000 | bytes 10000 | tf_op jit(solution)/shard_map/pallas_call | solution.py:320
  23.6 0.0 collective-permute-done.2.n1
  23.6 0.0 collective-permute-done.3.n2
  23.6 0.9 shard_map.107
  24.5 0.0 copy-done
  24.6 3.1 %shard_map.108 = (f32[192,256]{1,0:T(8,128)S(1)}, bf16[864,256]{1,0:T(8,128)(2,1)S(1)}, bf16[864,256]{1,0:T(8,128)(2,1)S(1)}, bf16[64,256]{1,0:T(8,128)(2,1)S(1)}) custom-call(s32[2]{0:T(128)S(1)} %pad_add_fusion.place, f32[32,256]{1,0:T(8,128)S(1)} %get-tuple-element.39.nbt, bf16[192,256]{1,0:T(8,128)(2,1)S(1)} %get-tuple-element.52.grad, ...), custom_call_target="tpu_custom_call" | custom-call | flops 100000 | bytes 10000 | tf_op jit(solution)/shard_map/pallas_call | solution.py:320
  27.7 0.9 collective-permute-start.10
  28.6 0.7 collective-permute-start.11
  29.3 2.3 %collective-permute-start.7 = (bf16[192,256]{1,0:T(8,128)(2,1)S(1)}, bf16[192,256]{1,0:T(8,128)(2,1)S(1)}, u32[]{:S(2)}, u32[]{:S(2)}) collective-permute-start(bf16[192,256]{1,0:T(8,128)(2,1)S(1)} %get-tuple-element.51.g0), channel_id=1, source_target_pairs={{0,1},{1,0},{2,3},{3,2},{4,5},{5,4},{6,7},{7,6},{8,9},{9,8},{10,11... | collective-permute-start | bytes 294920 | tf_op jit(solution)/shard_map/ppermute | solution.py:360
  31.6 0.0 collective-permute-start.8
  31.6 1.6 %collective-permute-start.9 = (bf16[192,256]{1,0:T(8,128)(2,1)S(1)}, bf16[192,256]{1,0:T(8,128)(2,1)S(1)}, u32[]{:S(2)}, u32[]{:S(2)}) collective-permute-start(bf16[192,256]{1,0:T(8,128)(2,1)S(1)} %get-tuple-element.51.g0), channel_id=1, source_target_pairs={{0,3},{1,2},{2,1},{3,0},{4,7},{5,6},{6,5},{7,4},{8,11},{9,10},{10,... | collective-permute-start | bytes 294920 | tf_op jit(solution)/shard_map/ppermute | solution.py:360
  33.1 0.0 collective-permute-done.10.m1.r1
  33.1 0.0 collective-permute-done.11.m2.r2
  33.1 0.6 shard_map.109
  33.7 3.2 %collective-permute-start.12 = (bf16[96,256]{1,0:T(8,128)(2,1)S(1)}, bf16[96,256]{1,0:T(8,128)(2,1)S(1)}, u32[]{:S(2)}, u32[]{:S(2)}) collective-permute-start(bf16[96,256]{1,0:T(8,128)(2,1)S(1)} %get-tuple-element.58.late), channel_id=1, source_target_pairs={{0,1},{1,0},{2,3},{3,2},{4,5},{5,4},{6,7},{7,6},{8,9},{9,8},{10,11... | collective-permute-start | bytes 147464 | tf_op jit(solution)/shard_map/ppermute | solution.py:356
  36.9 2.1 %collective-permute-start.13 = (bf16[96,256]{1,0:T(8,128)(2,1)S(1)}, bf16[96,256]{1,0:T(8,128)(2,1)S(1)}, u32[]{:S(2)}, u32[]{:S(2)}) collective-permute-start(bf16[96,256]{1,0:T(8,128)(2,1)S(1)} %get-tuple-element.63), channel_id=1, source_target_pairs={{1,2},{2,1},{5,6},{6,5},{9,10},{10,9},{13,14},{14,13},{17,18},{18,... | collective-permute-start | bytes 147464 | tf_op jit(solution)/shard_map/ppermute | solution.py:356
  39.0 5.2 %shard_map.110 = (bf16[256,768]{1,0:T(8,128)(2,1)S(1)}, bf16[768,1792]{1,0:T(8,128)(2,1)S(1)}, bf16[768,1792]{1,0:T(8,128)(2,1)S(1)}) custom-call(s32[2]{0:T(128)S(1)} %pad_add_fusion.place, bf16[224,768]{1,0:T(8,128)(2,1)S(1)} %get-tuple-element.49.p0, bf16[224,768]{1,0:T(8,128)(2,1)S(1)} %collective-permute-done.4.p1, ...), custom_call_target="tpu_custom_call" | custom-call | flops 100000 | bytes 10000 | tf_op jit(solution)/shard_map/pallas_call | solution.py:320
  44.2 0.0 collective-permute-done.12.n1
  44.3 0.0 collective-permute-done.13.n2
  44.3 1.0 shard_map.111
  45.2 1.4 %shard_map.112 = (bf16[128,1792]{1,0:T(8,128)(2,1)S(1)}, bf16[128,1792]{1,0:T(8,128)(2,1)S(1)}) custom-call(s32[2]{0:T(128)S(1)} %pad_add_fusion.place, bf16[256,768]{1,0:T(8,128)(2,1)S(1)} %get-tuple-element.60.late.gt, bf16[768,1792]{1,0:T(8,128)(2,1)S(1)} %get-tuple-element.61.cols, bf16[128,256]{1,0:T(8,128)(2,1)S(1)} %get-tuple-element.65.late.rk), custom_call_target="tpu_custom_call" | custom-call | flops 100000 | bytes 10000 | tf_op jit(solution)/shard_map/pallas_call | solution.py:320
  46.7 0.0 collective-permute-done.7.g1
  46.7 0.0 collective-permute-done.8.g2
  46.7 0.0 collective-permute-done.9.g3
  46.7 1.7 %shard_map.113 = (bf16[128,1792]{1,0:T(8,128)(2,1)S(1)}, bf16[128,1792]{1,0:T(8,128)(2,1)S(1)}) custom-call(s32[2]{0:T(128)S(1)} %pad_add_fusion.place, bf16[192,256]{1,0:T(8,128)(2,1)S(1)} %get-tuple-element.51.g0, bf16[192,256]{1,0:T(8,128)(2,1)S(1)} %collective-permute-done.7.g1, bf16[192,256]{1,0:T(8,128)(2,1)S(1)} %collective-permute-done.8.g2, ...), custom_call_target="tpu_custom_call" | custom-call | flops 100000 | bytes 10000 | tf_op jit(solution)/shard_map/pallas_call | solution.py:320
  48.4 4.7 %collective-permute-start.14 = (bf16[128,1792]{1,0:T(8,128)(2,1)S(1)}, bf16[128,1792]{1,0:T(8,128)(2,1)S(1)}, u32[]{:S(2)}, u32[]{:S(2)}) collective-permute-start(bf16[128,1792]{1,0:T(8,128)(2,1)S(1)} %get-tuple-element.68), channel_id=1, source_target_pairs={{0,4},{4,0},{8,12},{12,8},{16,20},{20,16},{24,28},{28,24},{32,36},... | collective-permute-start | bytes 1376264 | tf_op jit(solution)/shard_map/ppermute | solution.py:360
  53.1 0.1 collective-permute-start.15
  53.2 0.4 collective-permute-start.16
  53.6 1.7 %collective-permute-done.16.rs = bf16[128,256]{1,0:T(8,128)(2,1)S(1)} collective-permute-done((bf16[128,256]{1,0:T(8,128)(2,1)S(1)}, bf16[128,256]{1,0:T(8,128)(2,1)S(1)}, u32[]{:S(2)}, u32[]{:S(2)}) %collective-permute-start.16) | collective-permute-done | bytes 65568 | tf_op jit(solution)/shard_map/ppermute | solution.py:360
  55.3 0.0 collective-permute-done.14.s1
  55.3 0.0 collective-permute-done.15.s2
  55.3 1.7 %shard_map.114 = (bf16[64,2048]{1,0:T(8,128)(2,1)S(1)}, bf16[64,2048]{1,0:T(8,128)(2,1)S(1)}, bf16[64,2048]{1,0:T(8,128)(2,1)S(1)}, bf16[64,2048]{1,0:T(8,128)(2,1)S(1)}) custom-call(s32[2]{0:T(128)S(1)} %pad_add_fusion.place, bf16[128,1792]{1,0:T(8,128)(2,1)S(1)} %get-tuple-element.67.k1, bf16[128,1792]{1,0:T(8,128)(2,1)S(1)} %collective-permute-done.14.s1, ...), custom_call_target="tpu_custom_call" | custom-call | flops 100000 | bytes 10000 | tf_op jit(solution)/shard_map/pallas_call | solution.py:320
  57.0 6.7 %collective-permute-start.17 = (bf16[64,2048]{1,0:T(8,128)(2,1)S(1)}, bf16[64,2048]{1,0:T(8,128)(2,1)S(1)}, u32[]{:S(2)}, u32[]{:S(2)}) collective-permute-start(bf16[64,2048]{1,0:T(8,128)(2,1)S(1)} %get-tuple-element.72), channel_id=1, source_target_pairs={{0,64},{4,68},{8,72},{12,76},{16,80},{20,84},{24,88},{28,92},{32,9... | collective-permute-start | bytes 786440 | tf_op jit(solution)/shard_map/ppermute | solution.py:360
  63.7 3.2 %collective-permute-start.18 = (bf16[64,2048]{1,0:T(8,128)(2,1)S(1)}, bf16[64,2048]{1,0:T(8,128)(2,1)S(1)}, u32[]{:S(2)}, u32[]{:S(2)}) collective-permute-start(bf16[64,2048]{1,0:T(8,128)(2,1)S(1)} %get-tuple-element.73), channel_id=1, source_target_pairs={{0,128},{4,132},{8,136},{12,140},{16,144},{20,148},{24,152},{28,15... | collective-permute-start | bytes 786440 | tf_op jit(solution)/shard_map/ppermute | solution.py:360
  66.9 0.0 collective-permute-start.19
  66.9 3.9 %collective-permute-done.17.a1 = bf16[64,2048]{1,0:T(8,128)(2,1)S(1)} collective-permute-done((bf16[64,2048]{1,0:T(8,128)(2,1)S(1)}, bf16[64,2048]{1,0:T(8,128)(2,1)S(1)}, u32[]{:S(2)}, u32[]{:S(2)}) %collective-permute-start.17) | collective-permute-done | bytes 262176 | tf_op jit(solution)/shard_map/ppermute | solution.py:360
  70.8 8.1 %collective-permute-done.18.a2 = bf16[64,2048]{1,0:T(8,128)(2,1)S(1)} collective-permute-done((bf16[64,2048]{1,0:T(8,128)(2,1)S(1)}, bf16[64,2048]{1,0:T(8,128)(2,1)S(1)}, u32[]{:S(2)}, u32[]{:S(2)}) %collective-permute-start.18) | collective-permute-done | bytes 262176 | tf_op jit(solution)/shard_map/ppermute | solution.py:360
  78.9 2.6 %collective-permute-done.19.a3 = bf16[64,2048]{1,0:T(8,128)(2,1)S(1)} collective-permute-done((bf16[64,2048]{1,0:T(8,128)(2,1)S(1)}, bf16[64,2048]{1,0:T(8,128)(2,1)S(1)}, u32[]{:S(2)}, u32[]{:S(2)}) %collective-permute-start.19) | collective-permute-done | bytes 262176 | tf_op jit(solution)/shard_map/ppermute | solution.py:360
  81.5 0.7 shard_map.115
  82.2 17.0 %all_to_all.5.refs_0_ = bf16[8,8,2816]{2,1,0:T(8,128)(2,1)S(1)} all-to-all(bf16[8,8,2816]{2,1,0:T(8,128)(2,1)S(1)} %bitcast.5), channel_id=1, replica_groups={{0,8,16,24,32,40,48,56},{4,12,20,28,36,44,52,60},{64,72,80,88,96,104,11..., dimensions={0} | all-to-all | bytes 720896 | tf_op jit(solution)/shard_map/all_to_all | solution.py:498
  99.2 0.8 shard_map.116
Async XLA Ops:
  0.7 6.1 %copy-start.1 = (bf16[256,6912]{1,0:T(8,128)(2,1)S(1)}, bf16[256,6912]{1,0:T(8,128)(2,1)}, u32[]{:S(2)}) copy-start(bf16[256,6912]{1,0:T(8,128)(2,1)} %weight.2) | copy-start | bytes 10616836
  2.9 21.7 %copy-start = (bf16[256,6912]{1,0:T(8,128)(2,1)S(1)}, bf16[256,6912]{1,0:T(8,128)(2,1)}, u32[]{:S(2)}) copy-start(bf16[256,6912]{1,0:T(8,128)(2,1)} %weight.3) | copy-start | bytes 10616836
  2.9 14.4 %collective-permute-start.4 = (bf16[224,768]{1,0:T(8,128)(2,1)S(1)}, bf16[224,768]{1,0:T(8,128)(2,1)S(1)}, u32[]{:S(2)}, u32[]{:S(2)}) collective-permute-start(bf16[224,768]{1,0:T(8,128)(2,1)S(1)} %get-tuple-element.49.p0), channel_id=1, source_target_pairs={{0,1},{1,0},{2,3},{3,2},{4,5},{5,4},{6,7},{7,6},{8,9},{9,8},{10,11... | collective-permute-start | bytes 1032200 | tf_op jit(solution)/shard_map/ppermute | solution.py:360
  5.2 16.3 %collective-permute-start.5 = (bf16[224,768]{1,0:T(8,128)(2,1)S(1)}, bf16[224,768]{1,0:T(8,128)(2,1)S(1)}, u32[]{:S(2)}, u32[]{:S(2)}) collective-permute-start(bf16[224,768]{1,0:T(8,128)(2,1)S(1)} %get-tuple-element.49.p0), channel_id=1, source_target_pairs={{0,2},{1,3},{2,0},{3,1},{4,6},{5,7},{6,4},{7,5},{8,10},{9,11},{10,... | collective-permute-start | bytes 1032200 | tf_op jit(solution)/shard_map/ppermute | solution.py:360
  5.9 16.6 %collective-permute-start.6 = (bf16[224,768]{1,0:T(8,128)(2,1)S(1)}, bf16[224,768]{1,0:T(8,128)(2,1)S(1)}, u32[]{:S(2)}, u32[]{:S(2)}) collective-permute-start(bf16[224,768]{1,0:T(8,128)(2,1)S(1)} %get-tuple-element.49.p0), channel_id=1, source_target_pairs={{0,3},{1,2},{2,1},{3,0},{4,7},{5,6},{6,5},{7,4},{8,11},{9,10},{10,... | collective-permute-start | bytes 1032200 | tf_op jit(solution)/shard_map/ppermute | solution.py:360
  9.9 1.3 %collective-permute-start = (bf16[96,256]{1,0:T(8,128)(2,1)S(1)}, bf16[96,256]{1,0:T(8,128)(2,1)S(1)}, u32[]{:S(2)}, u32[]{:S(2)}) collective-permute-start(bf16[96,256]{1,0:T(8,128)(2,1)S(1)} %get-tuple-element.42), channel_id=1, source_target_pairs={{0,4},{4,0},{8,12},{12,8},{16,20},{20,16},{24,28},{28,24},{32,36},... | collective-permute-start | bytes 147464 | tf_op jit(solution)/shard_map/ppermute | solution.py:356
  10.0 1.2 %collective-permute-start.1 = (bf16[96,256]{1,0:T(8,128)(2,1)S(1)}, bf16[96,256]{1,0:T(8,128)(2,1)S(1)}, u32[]{:S(2)}, u32[]{:S(2)}) collective-permute-start(bf16[96,256]{1,0:T(8,128)(2,1)S(1)} %get-tuple-element.43), channel_id=1, source_target_pairs={{4,8},{8,4},{12,16},{16,12},{20,24},{24,20},{28,32},{32,28},{36,40... | collective-permute-start | bytes 147464 | tf_op jit(solution)/shard_map/ppermute | solution.py:356
  11.7 11.9 %collective-permute-start.2 = (bf16[96,256]{1,0:T(8,128)(2,1)S(1)}, bf16[96,256]{1,0:T(8,128)(2,1)S(1)}, u32[]{:S(2)}, u32[]{:S(2)}) collective-permute-start(bf16[96,256]{1,0:T(8,128)(2,1)S(1)} %get-tuple-element.45.late), channel_id=1, source_target_pairs={{0,1},{1,0},{2,3},{3,2},{4,5},{5,4},{6,7},{7,6},{8,9},{9,8},{10,11... | collective-permute-start | bytes 147464 | tf_op jit(solution)/shard_map/ppermute | solution.py:356
  15.0 8.7 %collective-permute-start.3 = (bf16[96,256]{1,0:T(8,128)(2,1)S(1)}, bf16[96,256]{1,0:T(8,128)(2,1)S(1)}, u32[]{:S(2)}, u32[]{:S(2)}) collective-permute-start(bf16[96,256]{1,0:T(8,128)(2,1)S(1)} %get-tuple-element.46), channel_id=1, source_target_pairs={{1,2},{2,1},{5,6},{6,5},{9,10},{10,9},{13,14},{14,13},{17,18},{18,... | collective-permute-start | bytes 147464 | tf_op jit(solution)/shard_map/ppermute | solution.py:356
  27.7 5.5 %collective-permute-start.10 = (bf16[864,256]{1,0:T(8,128)(2,1)S(1)}, bf16[864,256]{1,0:T(8,128)(2,1)S(1)}, u32[]{:S(2)}, u32[]{:S(2)}) collective-permute-start(bf16[864,256]{1,0:T(8,128)(2,1)S(1)} %get-tuple-element.55), channel_id=1, source_target_pairs={{0,4},{4,0},{8,12},{12,8},{16,20},{20,16},{24,28},{28,24},{32,36},... | collective-permute-start | bytes 1327112 | tf_op jit(solution)/shard_map/ppermute | solution.py:356
  28.6 4.6 %collective-permute-start.11 = (bf16[864,256]{1,0:T(8,128)(2,1)S(1)}, bf16[864,256]{1,0:T(8,128)(2,1)S(1)}, u32[]{:S(2)}, u32[]{:S(2)}) collective-permute-start(bf16[864,256]{1,0:T(8,128)(2,1)S(1)} %get-tuple-element.56), channel_id=1, source_target_pairs={{4,8},{8,4},{12,16},{16,12},{20,24},{24,20},{28,32},{32,28},{36,40... | collective-permute-start | bytes 1327112 | tf_op jit(solution)/shard_map/ppermute | solution.py:356
  29.3 17.4 %collective-permute-start.7 = (bf16[192,256]{1,0:T(8,128)(2,1)S(1)}, bf16[192,256]{1,0:T(8,128)(2,1)S(1)}, u32[]{:S(2)}, u32[]{:S(2)}) collective-permute-start(bf16[192,256]{1,0:T(8,128)(2,1)S(1)} %get-tuple-element.51.g0), channel_id=1, source_target_pairs={{0,1},{1,0},{2,3},{3,2},{4,5},{5,4},{6,7},{7,6},{8,9},{9,8},{10,11... | collective-permute-start | bytes 294920 | tf_op jit(solution)/shard_map/ppermute | solution.py:360
  31.6 15.1 %collective-permute-start.8 = (bf16[192,256]{1,0:T(8,128)(2,1)S(1)}, bf16[192,256]{1,0:T(8,128)(2,1)S(1)}, u32[]{:S(2)}, u32[]{:S(2)}) collective-permute-start(bf16[192,256]{1,0:T(8,128)(2,1)S(1)} %get-tuple-element.51.g0), channel_id=1, source_target_pairs={{0,2},{1,3},{2,0},{3,1},{4,6},{5,7},{6,4},{7,5},{8,10},{9,11},{10,... | collective-permute-start | bytes 294920 | tf_op jit(solution)/shard_map/ppermute | solution.py:360
  31.6 15.1 %collective-permute-start.9 = (bf16[192,256]{1,0:T(8,128)(2,1)S(1)}, bf16[192,256]{1,0:T(8,128)(2,1)S(1)}, u32[]{:S(2)}, u32[]{:S(2)}) collective-permute-start(bf16[192,256]{1,0:T(8,128)(2,1)S(1)} %get-tuple-element.51.g0), channel_id=1, source_target_pairs={{0,3},{1,2},{2,1},{3,0},{4,7},{5,6},{6,5},{7,4},{8,11},{9,10},{10,... | collective-permute-start | bytes 294920 | tf_op jit(solution)/shard_map/ppermute | solution.py:360
  33.7 10.5 %collective-permute-start.12 = (bf16[96,256]{1,0:T(8,128)(2,1)S(1)}, bf16[96,256]{1,0:T(8,128)(2,1)S(1)}, u32[]{:S(2)}, u32[]{:S(2)}) collective-permute-start(bf16[96,256]{1,0:T(8,128)(2,1)S(1)} %get-tuple-element.58.late), channel_id=1, source_target_pairs={{0,1},{1,0},{2,3},{3,2},{4,5},{5,4},{6,7},{7,6},{8,9},{9,8},{10,11... | collective-permute-start | bytes 147464 | tf_op jit(solution)/shard_map/ppermute | solution.py:356
  36.9 7.3 %collective-permute-start.13 = (bf16[96,256]{1,0:T(8,128)(2,1)S(1)}, bf16[96,256]{1,0:T(8,128)(2,1)S(1)}, u32[]{:S(2)}, u32[]{:S(2)}) collective-permute-start(bf16[96,256]{1,0:T(8,128)(2,1)S(1)} %get-tuple-element.63), channel_id=1, source_target_pairs={{1,2},{2,1},{5,6},{6,5},{9,10},{10,9},{13,14},{14,13},{17,18},{18,... | collective-permute-start | bytes 147464 | tf_op jit(solution)/shard_map/ppermute | solution.py:356
  48.4 6.9 %collective-permute-start.14 = (bf16[128,1792]{1,0:T(8,128)(2,1)S(1)}, bf16[128,1792]{1,0:T(8,128)(2,1)S(1)}, u32[]{:S(2)}, u32[]{:S(2)}) collective-permute-start(bf16[128,1792]{1,0:T(8,128)(2,1)S(1)} %get-tuple-element.68), channel_id=1, source_target_pairs={{0,4},{4,0},{8,12},{12,8},{16,20},{20,16},{24,28},{28,24},{32,36},... | collective-permute-start | bytes 1376264 | tf_op jit(solution)/shard_map/ppermute | solution.py:360
  53.1 2.2 %collective-permute-start.15 = (bf16[128,1792]{1,0:T(8,128)(2,1)S(1)}, bf16[128,1792]{1,0:T(8,128)(2,1)S(1)}, u32[]{:S(2)}, u32[]{:S(2)}) collective-permute-start(bf16[128,1792]{1,0:T(8,128)(2,1)S(1)} %get-tuple-element.69), channel_id=1, source_target_pairs={{0,4},{4,0},{8,12},{12,8},{16,20},{20,16},{24,28},{28,24},{32,36},... | collective-permute-start | bytes 1376264 | tf_op jit(solution)/shard_map/ppermute | solution.py:360
  53.2 2.1 %collective-permute-start.16 = (bf16[128,256]{1,0:T(8,128)(2,1)S(1)}, bf16[128,256]{1,0:T(8,128)(2,1)S(1)}, u32[]{:S(2)}, u32[]{:S(2)}) collective-permute-start(bf16[128,256]{1,0:T(8,128)(2,1)S(1)} %get-tuple-element.70), channel_id=1, source_target_pairs={{0,4},{4,0},{8,12},{12,8},{16,20},{20,16},{24,28},{28,24},{32,36},... | collective-permute-start | bytes 196616 | tf_op jit(solution)/shard_map/ppermute | solution.py:360
  57.0 13.8 %collective-permute-start.17 = (bf16[64,2048]{1,0:T(8,128)(2,1)S(1)}, bf16[64,2048]{1,0:T(8,128)(2,1)S(1)}, u32[]{:S(2)}, u32[]{:S(2)}) collective-permute-start(bf16[64,2048]{1,0:T(8,128)(2,1)S(1)} %get-tuple-element.72), channel_id=1, source_target_pairs={{0,64},{4,68},{8,72},{12,76},{16,80},{20,84},{24,88},{28,92},{32,9... | collective-permute-start | bytes 786440 | tf_op jit(solution)/shard_map/ppermute | solution.py:360
  63.7 15.2 %collective-permute-start.18 = (bf16[64,2048]{1,0:T(8,128)(2,1)S(1)}, bf16[64,2048]{1,0:T(8,128)(2,1)S(1)}, u32[]{:S(2)}, u32[]{:S(2)}) collective-permute-start(bf16[64,2048]{1,0:T(8,128)(2,1)S(1)} %get-tuple-element.73), channel_id=1, source_target_pairs={{0,128},{4,132},{8,136},{12,140},{16,144},{20,148},{24,152},{28,15... | collective-permute-start | bytes 786440 | tf_op jit(solution)/shard_map/ppermute | solution.py:360
  66.9 14.6 %collective-permute-start.19 = (bf16[64,2048]{1,0:T(8,128)(2,1)S(1)}, bf16[64,2048]{1,0:T(8,128)(2,1)S(1)}, u32[]{:S(2)}, u32[]{:S(2)}) collective-permute-start(bf16[64,2048]{1,0:T(8,128)(2,1)S(1)} %get-tuple-element.74), channel_id=1, source_target_pairs={{0,192},{4,196},{8,200},{12,204},{16,208},{20,212},{24,216},{28,22... | collective-permute-start | bytes 786440 | tf_op jit(solution)/shard_map/ppermute | solution.py:360

commit v4 on v3

--- a/solution.py
+++ b/solution.py
@@ -94,8 +94,8 @@
     pay[S : S + 32, 2 * C : 3 * C] = jnp.broadcast_to(row, (32, C)).astype(BF)
     lane, peer = iota((64, C), 1), iota((64, C), 0)
     parity = jnp.where(lane < 128, place[0] % 2, 1 - place[0] % 2)
-    pick = onehot(peer == 2 * (lane % 32) + parity)
-    spot = (iota((1, C), 1) % 128) // 32
+    pick = onehot(peer == 2 * ((lane % 128) // 4) + parity)
+    spot = iota((1, C), 1) % 4
     total = jnp.zeros((1, C), F32)
     for c in range(3):
         up = jnp.broadcast_to((send_ids[c] + 1).astype(F32), (8, 64)).astype(BF)
@@ -131,24 +131,35 @@
     spread_terms(place, nbt, grad, weight, own, m1, m2, loc, acc)
 
 
+def inner(position, count):
+    return (position > 0) & (position < count - 1)
+
+
+def masked(keep, rows):
+    return jnp.where(keep, rows, jnp.zeros_like(rows))
+
+
 def pass_kernel(place, loc, m1, m2, n1, n2):
     even = place[1] % 2 == 0
     first = jnp.where(even, 0, 1)
+    far = inner(place[0], 64)
     for out, side in ((n1, first), (n2, 1 - first)):
         out[0:32, :] = loc[pl.ds(pl.multiple_of(side * 32, 32), 32), :]
         out[32:64, :] = m1[pl.ds(pl.multiple_of(side * 64, 32), 32), :]
-        out[64:96, :] = m2[pl.ds(pl.multiple_of(side * 64, 32), 32), :]
+        out[64:96, :] = masked(far, m2[pl.ds(pl.multiple_of(side * 64, 32), 32), :])
 
 
 def settled(place, own, m1, m2, n1, n2, hrow, back):
     da = jnp.where(place[0] % 2 == 0, 1, -1)
     db = jnp.where(place[1] % 2 == 0, 1, -1)
     back[direction(da, 0)] = m1[32:64, :]
-    back[direction(-da, 0)] = m2[32:64, :]
-    for ref, side in ((n1, db), (n2, -db)):
-        back[direction(0, side)] = ref[0:32, :]
-        back[direction(da, side)] = ref[32:64, :]
-        back[direction(-da, side)] = ref[64:96, :]
+    back[direction(-da, 0)] = masked(inner(place[0], 64), m2[32:64, :])
+    beside = inner(place[1], 4)
+    for ref, side, keep in ((n1, db, True), (n2, -db, beside)):
+        rows = ref[...] if keep is True else masked(keep, ref[...])
+        back[direction(0, side)] = rows[0:32, :]
+        back[direction(da, side)] = rows[32:64, :]
+        back[direction(-da, side)] = rows[64:96, :]
     rows = back[...].reshape(8 * HB, C)
     return own[...] + mm(halo_matrix(hrow[0:1, :]), rows)
 
@@ -162,7 +173,7 @@
     ordered[...] = mm(value, channel_order()).astype(BF)
 
 
-def rows_kernel(place, own, m1, m2, n1, n2, hrow, grad, srow, late, keep, send, back):
+def rows_kernel(place, own, m1, m2, n1, n2, hrow, grad, srow, t, g1, g2, g3, keep, send, back):
     total = settled(place, own, m1, m2, n1, n2, hrow, back)
     value = (grad[...].astype(F32) + total).astype(BF)
     chosen = mm_t(onehot(iota((S, C), 0) == srow[0:1, :]), value).astype(BF)
@@ -203,6 +214,7 @@
     first_k = start // C
     offset = start % C
     even = place[0] % 2 == 0
+    far = inner(place[0], 64)
     shift = onehot(iota((C, C), 0) == (iota((C, C), 1) + offset) % C)
     lane = iota((S, 2 * C), 1) % C
     early = lane < C - offset
@@ -211,7 +223,7 @@
         for half in range(2):
             lanes = slice(half * C, (half + 1) * C)
             at = pl.multiple_of(96 + 384 * half + 96 * tile, 32)
-            above, below = r1[pl.ds(at, 96), :], r2[pl.ds(at, 96), :]
+            above, below = r1[pl.ds(at, 96), :], masked(far, r2[pl.ds(at, 96), :])
             for to, piece in (
                 (0, pay[0:S, lanes]),
                 (S, jnp.where(even, above, below)),
@@ -249,7 +261,7 @@
         for part in range(7):
             out[:, part * C : (part + 1) * C] = mm(
                 left, cols[:, part * C : (part + 1) * C]
-            ).astype(BF)
+            ).astype(out.dtype)
 
 
 def weight_two_kernel(place, gt, cols, late, keep, send):
@@ -263,34 +275,32 @@
 
 
 def merge_kernel(place, k1, s1, k2, s2, rk, rs, *outs):
-    row, col = iota((64, 128), 0), iota((64, 128), 1)
-    mine = place[0] % 2
+    first = place[0] % 2 == 0
     line = place[0] // 16
     for turn, out in enumerate(outs):
-        chip = 8 * (line ^ turn) + row // 8
-        for part in range(7):
-            at = slice(part * C, (part + 1) * C)
-            total = jnp.zeros((64, C), F32)
-            for which, refs in enumerate(((k1, s1), (k2, s2))):
-                spot = onehot((chip == col // 4) & (row % 8 == 4 * which + col % 4))
-                for ref in refs:
-                    total = total + mm(spot, ref[:, at])
-            out[:, at] = total.astype(BF)
-        total = jnp.zeros((64, C), F32)
-        for ref, core in ((rk, mine), (rs, 1 - mine)):
-            spot = (chip == col % 32) & (row % 8 == 3 * core + col // 32) & (col < 96)
-            total = total + mm(onehot(spot), ref[...])
-        out[:, 7 * C : 8 * C] = total.astype(BF)
+        rows = pl.ds(pl.multiple_of(32 * (line ^ turn), 32), 32)
+        for at, (keep, come) in ((0, (k1, s1)), (32, (k2, s2))):
+            total = keep[rows, :].astype(F32) + come[rows, :].astype(F32)
+            out[at : at + 32, 0 : 7 * C] = total.astype(BF)
+        mine, other = rk[rows, :], rs[rows, :]
+        out[0:32, 7 * C : 8 * C] = jnp.where(first, mine, other)
+        out[32:64, 7 * C : 8 * C] = jnp.where(first, other, mine)
 
 
 def line_kernel(place, a0, a1, a2, a3, out):
     line = place[0] // 16
-    total = jnp.zeros((64, 7 * C), F32)
-    for turn, part in enumerate((a0, a1, a2, a3)):
-        total = total + part[:, 0 : 7 * C].astype(F32)
-        at = pl.multiple_of(7 * C + (line ^ turn) * C, C)
-        out[:, pl.ds(at, C)] = part[:, 7 * C : 8 * C]
-    out[:, 0 : 7 * C] = total.astype(BF)
+    to, at = iota((64, 64), 0), iota((64, 64), 1)
+    order = onehot(at == 32 * ((to % 8) // 4) + 4 * (to // 8) + to % 4)
+    parts = (a0, a1, a2, a3)
+    for n in range(7):
+        lanes = slice(n * C, (n + 1) * C)
+        total = a0[:, lanes].astype(F32)
+        for part in parts[1:]:
+            total = total + part[:, lanes].astype(F32)
+        out[:, lanes] = mm(order, total.astype(BF)).astype(BF)
+    for turn, part in enumerate(parts):
+        to = pl.multiple_of(7 * C + (line ^ turn) * C, C)
+        out[:, pl.ds(to, C)] = mm(order, part[:, 7 * C : 8 * C]).astype(BF)
 
 
 def final_kernel(scale, arrived, rows, one, two):
@@ -298,7 +308,7 @@
     one[...] = total[0:4, 0:QW]
     two[...] = total[4:8, 0:QW]
     to, at = iota((48, 64), 0), iota((48, 64), 1)
-    spot = onehot((at // 8 == to // 6) & (at % 8 == to % 6))
+    spot = onehot((at // 8 == to // 6) & (at % 8 == 4 * ((to % 6) // 3) + to % 3))
     for line in range(4):
         piece = arrived[:, :, (7 + line) * C : (8 + line) * C].reshape(64, C)
         rows[48 * line : 48 * line + 48, :] = mm(spot, piece).astype(BF)
@@ -342,17 +352,10 @@
     )
 
 
-def partners(count, turn):
-    if turn == 0:
-        return list(range(count))
-    if turn == 1:
-        return [n ^ 1 for n in range(count)]
-    pairs = [n - 1 if n % 2 == 0 else n + 1 for n in range(count)]
-    return [n if 0 <= n < count else None for n in pairs]
-
-
 def swap(value, axis, turn):
-    pairs = [(n, q) for n, q in enumerate(partners(lax.axis_size(axis), turn)) if q is not None]
+    size = lax.axis_size(axis)
+    step = 1 if turn == 1 else -1
+    pairs = [(n, (n + (step if n % 2 == 0 else -step)) % size) for n in range(size)]
     return lax.ppermute(value, axis, pairs)
 
 
@@ -461,12 +464,14 @@
         grad,
         srow,
         turned,
+        *grads[1:],
         scratch=[back],
-        late=1,
+        late=4,
     )
     rows_come = cross(rows_send, "gx", 1)
+    full = sds((128, wide), F32)
     keep_two, send_two = call(
-        weight_two_kernel, (half, half), place, turned, cols_two, rows_keep, late=1
+        weight_two_kernel, (full, full), place, turned, cols_two, rows_keep, late=1
     )
     come_two = cross(send_two, "gx", 1)
     keep_one, send_one = call(

time: 101 us -> 96.5 us (0.955)
  waiting for transfers between devices: 22.1 us -> 17.9 us
  blocking collectives: 17 us -> 18.5 us
    ppermute x12, starting transfers between devices: 22.8 us -> 14.1 us  [cross(): lax.ppermute(value, axis, [(n, n ^ mask) for n in range(lax.axis_size(axi...]
    ppermute x8, starting transfers between devices: 13.2 us -> 21.5 us  [swap(): return lax.ppermute(value, axis, pairs)]
    ppermute x12, waiting for transfers between devices: 21.6 us -> 13.8 us  [cross(): lax.ppermute(value, axis, [(n, n ^ mask) for n in range(lax.axis_size(axi...]
    ppermute x8, waiting for transfers between devices: 0.56 us -> 4.12 us  [swap(): return lax.ppermute(value, axis, pairs)]
    all_to_all x1, blocking collectives: 17 us -> 18.5 us  [body(): lax.all_to_all(summed.reshape(8, 8, 11 * C), 'gx', split_axis=0, concat_a...]
where the time goes in v4:
time: 96.5 us; the launch traced here: 96.1 us
  starting transfers between devices  35.6 us (37%)
  Pallas kernels  23.1 us (24%)
  blocking collectives  18.5 us (19%)
  waiting for transfers between devices  17.9 us (19%)
    pallas_call x14, Pallas kernels, call(): pl.pallas_call(kernel, out_shape=outs, in_specs=specs, out_specs=jax.tree...  23.1 us
    ppermute x8, starting transfers between devices, swap(): return lax.ppermute(value, axis, pairs)  21.5 us
    all_to_all x1, blocking collectives, body(): lax.all_to_all(summed.reshape(8, 8, 11 * C), 'gx', split_axis=0, concat_a...  18.5 us
    ppermute x12, starting transfers between devices, cross(): lax.ppermute(value, axis, [(n, n ^ mask) for n in range(lax.axis_size(axi...  14.1 us
    ppermute x12, waiting for transfers between devices, cross(): lax.ppermute(value, axis, [(n, n ^ mask) for n in range(lax.axis_size(axi...  13.8 us
    ppermute x8, waiting for transfers between devices, swap(): return lax.ppermute(value, axis, pairs)  4.12 us
  transfers between devices with their start and end apart: 20, of which 7 were waited for; matrix products, arithmetic and copies ran while one was open for 0% of the time, Pallas kernels for 13%

profile of v4, /device:TPU:2, one launch (start us, length us, event | category | flops | bytes accessed | tf_op | source)
XLA Modules:
  0.0 96.1 jit_solution(14467198802574524489)
XLA Ops:
  0.6 0.1 pad_add_fusion.place
  0.7 0.0 copy-start.1
  0.7 2.2 %shard_map.103 = (bf16[224,768]{1,0:T(8,128)(2,1)S(1)}, f32[32,256]{1,0:T(8,128)S(1)}, s32[8,256]{1,0:T(8,128)S(1)}, s32[8,256]{1,0:T(8,128)S(1)}, bf16[192,256]...) custom-call(s32[2]{0:T(128)S(1)} %pad_add_fusion.place, bf16[192,256]{1,0:T(8,128)(2,1)} %feat.1, bf16[192,256]{1,0:T(8,128)(2,1)} %pre.1, ...), custom_call_target="tpu_custom_call" | custom-call | flops 4000000000 | bytes 10000 | tf_op jit(solution)/shard_map/pallas_call | solution.py:330
  2.9 0.0 copy-start
  2.9 2.4 %collective-permute-start.4 = (bf16[224,768]{1,0:T(8,128)(2,1)S(1)}, bf16[224,768]{1,0:T(8,128)(2,1)S(1)}, u32[]{:S(2)}, u32[]{:S(2)}) collective-permute-start(bf16[224,768]{1,0:T(8,128)(2,1)S(1)} %get-tuple-element.49.p0), channel_id=1, source_target_pairs={{0,1},{1,0},{2,3},{3,2},{4,5},{5,4},{6,7},{7,6},{8,9},{9,8},{10,11... | collective-permute-start | bytes 1032200 | tf_op jit(solution)/shard_map/ppermute | solution.py:363
  5.2 0.7 collective-permute-start.5
  5.9 0.9 collective-permute-start.6
  6.8 0.0 copy-done.1
  6.8 3.0 %shard_map.104 = (f32[192,256]{1,0:T(8,128)S(1)}, bf16[96,256]{1,0:T(8,128)(2,1)S(1)}, bf16[96,256]{1,0:T(8,128)(2,1)S(1)}, bf16[64,256]{1,0:T(8,128)(2,1)S(1)}) custom-call(s32[2]{0:T(128)S(1)} %pad_add_fusion.place, f32[32,256]{1,0:T(8,128)S(1)} %get-tuple-element.39.nbt, bf16[192,256]{1,0:T(8,128)(2,1)S(1)} %get-tuple-element.40.grad, ...), custom_call_target="tpu_custom_call" | custom-call | flops 100000 | bytes 10000 | tf_op jit(solution)/shard_map/pallas_call | solution.py:330
  9.9 0.1 collective-permute-start
  10.0 8.1 %collective-permute-start.1 = (bf16[96,256]{1,0:T(8,128)(2,1)S(1)}, bf16[96,256]{1,0:T(8,128)(2,1)S(1)}, u32[]{:S(2)}, u32[]{:S(2)}) collective-permute-start(bf16[96,256]{1,0:T(8,128)(2,1)S(1)} %get-tuple-element.43), channel_id=1, source_target_pairs={{0,252},{4,8},{8,4},{12,16},{16,12},{20,24},{24,20},{28,32},{32,28... | collective-permute-start | bytes 147464 | tf_op jit(solution)/shard_map/ppermute | solution.py:359
  18.0 0.0 collective-permute-done.m1
  18.0 1.8 %collective-permute-done.1.m2 = bf16[96,256]{1,0:T(8,128)(2,1)S(1)} collective-permute-done((bf16[96,256]{1,0:T(8,128)(2,1)S(1)}, bf16[96,256]{1,0:T(8,128)(2,1)S(1)}, u32[]{:S(2)}, u32[]{:S(2)}) %collective-permute-start.1) | collective-permute-done | bytes 49184 | tf_op jit(solution)/shard_map/ppermute | solution.py:359
  19.8 0.6 shard_map.105
  20.4 1.8 %collective-permute-start.2 = (bf16[96,256]{1,0:T(8,128)(2,1)S(1)}, bf16[96,256]{1,0:T(8,128)(2,1)S(1)}, u32[]{:S(2)}, u32[]{:S(2)}) collective-permute-start(bf16[96,256]{1,0:T(8,128)(2,1)S(1)} %get-tuple-element.45.late), channel_id=1, source_target_pairs={{0,1},{1,0},{2,3},{3,2},{4,5},{5,4},{6,7},{7,6},{8,9},{9,8},{10,11... | collective-permute-start | bytes 147464 | tf_op jit(solution)/shard_map/ppermute | solution.py:359
  22.2 2.2 %collective-permute-start.3 = (bf16[96,256]{1,0:T(8,128)(2,1)S(1)}, bf16[96,256]{1,0:T(8,128)(2,1)S(1)}, u32[]{:S(2)}, u32[]{:S(2)}) collective-permute-start(bf16[96,256]{1,0:T(8,128)(2,1)S(1)} %get-tuple-element.46), channel_id=1, source_target_pairs={{0,3},{1,2},{2,1},{3,0},{4,7},{5,6},{6,5},{7,4},{8,11},{9,10},{10,... | collective-permute-start | bytes 147464 | tf_op jit(solution)/shard_map/ppermute | solution.py:359
  24.3 0.0 collective-permute-done.4.p1
  24.3 0.0 collective-permute-done.5.p2
  24.4 0.0 collective-permute-done.6.p3
  24.4 1.1 %shard_map.106 = (bf16[768,256]{1,0:T(8,128)(2,1)S(1)}, bf16[768,256]{1,0:T(8,128)(2,1)S(1)}, bf16[4,64,512]{2,1,0:T(8,128)(2,1)S(1)}) custom-call(s32[2]{0:T(128)S(1)} %pad_add_fusion.place, bf16[224,768]{1,0:T(8,128)(2,1)S(1)} %get-tuple-element.49.p0, bf16[224,768]{1,0:T(8,128)(2,1)S(1)} %collective-permute-done.4.p1, ...), custom_call_target="tpu_custom_call" | custom-call | flops 100000 | bytes 10000 | tf_op jit(solution)/shard_map/pallas_call | solution.py:330
  25.5 0.0 collective-permute-done.2.n1
  25.5 0.9 collective-permute-done.3.n2
  26.4 0.9 shard_map.107
  27.3 0.0 copy-done
  27.3 3.1 %shard_map.108 = (f32[192,256]{1,0:T(8,128)S(1)}, bf16[864,256]{1,0:T(8,128)(2,1)S(1)}, bf16[864,256]{1,0:T(8,128)(2,1)S(1)}, bf16[64,256]{1,0:T(8,128)(2,1)S(1)}) custom-call(s32[2]{0:T(128)S(1)} %pad_add_fusion.place, f32[32,256]{1,0:T(8,128)S(1)} %get-tuple-element.39.nbt, bf16[192,256]{1,0:T(8,128)(2,1)S(1)} %get-tuple-element.52.grad, ...), custom_call_target="tpu_custom_call" | custom-call | flops 100000 | bytes 10000 | tf_op jit(solution)/shard_map/pallas_call | solution.py:330
  30.4 0.1 collective-permute-start.10
  30.5 6.1 %collective-permute-start.11 = (bf16[864,256]{1,0:T(8,128)(2,1)S(1)}, bf16[864,256]{1,0:T(8,128)(2,1)S(1)}, u32[]{:S(2)}, u32[]{:S(2)}) collective-permute-start(bf16[864,256]{1,0:T(8,128)(2,1)S(1)} %get-tuple-element.56), channel_id=1, source_target_pairs={{0,252},{4,8},{8,4},{12,16},{16,12},{20,24},{24,20},{28,32},{32,28... | collective-permute-start | bytes 1327112 | tf_op jit(solution)/shard_map/ppermute | solution.py:359
  36.6 3.1 %collective-permute-start.7 = (bf16[192,256]{1,0:T(8,128)(2,1)S(1)}, bf16[192,256]{1,0:T(8,128)(2,1)S(1)}, u32[]{:S(2)}, u32[]{:S(2)}) collective-permute-start(bf16[192,256]{1,0:T(8,128)(2,1)S(1)} %get-tuple-element.51.g0), channel_id=1, source_target_pairs={{0,1},{1,0},{2,3},{3,2},{4,5},{5,4},{6,7},{7,6},{8,9},{9,8},{10,11... | collective-permute-start | bytes 294920 | tf_op jit(solution)/shard_map/ppermute | solution.py:363
  39.7 0.0 collective-permute-start.8
  39.7 1.5 %collective-permute-start.9 = (bf16[192,256]{1,0:T(8,128)(2,1)S(1)}, bf16[192,256]{1,0:T(8,128)(2,1)S(1)}, u32[]{:S(2)}, u32[]{:S(2)}) collective-permute-start(bf16[192,256]{1,0:T(8,128)(2,1)S(1)} %get-tuple-element.51.g0), channel_id=1, source_target_pairs={{0,3},{1,2},{2,1},{3,0},{4,7},{5,6},{6,5},{7,4},{8,11},{9,10},{10,... | collective-permute-start | bytes 294920 | tf_op jit(solution)/shard_map/ppermute | solution.py:363
  41.2 0.0 collective-permute-done.10.m1.r1
  41.2 1.4 %collective-permute-done.11.m2.r2 = bf16[864,256]{1,0:T(8,128)(2,1)S(1)} collective-permute-done((bf16[864,256]{1,0:T(8,128)(2,1)S(1)}, bf16[864,256]{1,0:T(8,128)(2,1)S(1)}, u32[]{:S(2)}, u32[]{:S(2)}) %collective-permute-start.11) | collective-permute-done | bytes 442400 | tf_op jit(solution)/shard_map/ppermute | solution.py:359
  42.6 0.6 shard_map.109
  43.1 3.2 %collective-permute-start.12 = (bf16[96,256]{1,0:T(8,128)(2,1)S(1)}, bf16[96,256]{1,0:T(8,128)(2,1)S(1)}, u32[]{:S(2)}, u32[]{:S(2)}) collective-permute-start(bf16[96,256]{1,0:T(8,128)(2,1)S(1)} %get-tuple-element.58.late), channel_id=1, source_target_pairs={{0,1},{1,0},{2,3},{3,2},{4,5},{5,4},{6,7},{7,6},{8,9},{9,8},{10,11... | collective-permute-start | bytes 147464 | tf_op jit(solution)/shard_map/ppermute | solution.py:359
  46.4 0.0 collective-permute-start.13
  46.4 5.2 %shard_map.110 = (bf16[256,768]{1,0:T(8,128)(2,1)S(1)}, bf16[768,1792]{1,0:T(8,128)(2,1)S(1)}, bf16[768,1792]{1,0:T(8,128)(2,1)S(1)}) custom-call(s32[2]{0:T(128)S(1)} %pad_add_fusion.place, bf16[224,768]{1,0:T(8,128)(2,1)S(1)} %get-tuple-element.49.p0, bf16[224,768]{1,0:T(8,128)(2,1)S(1)} %collective-permute-done.4.p1, ...), custom_call_target="tpu_custom_call" | custom-call | flops 100000 | bytes 10000 | tf_op jit(solution)/shard_map/pallas_call | solution.py:330
  51.6 0.0 collective-permute-done.7.g1
  51.6 0.0 collective-permute-done.8.g2
  51.6 0.0 collective-permute-done.9.g3
  51.6 0.0 collective-permute-done.12.n1
  51.6 0.0 collective-permute-done.13.n2
  51.6 1.0 %shard_map.111 = (bf16[128,256]{1,0:T(8,128)(2,1)S(1)}, bf16[128,256]{1,0:T(8,128)(2,1)S(1)}) custom-call(s32[2]{0:T(128)S(1)} %pad_add_fusion.place, f32[192,256]{1,0:T(8,128)S(1)} %get-tuple-element.62.own, bf16[864,256]{1,0:T(8,128)(2,1)S(1)} %collective-permute-done.10.m1.r1, bf16[864,256]{1,0:T(8,128)(2,1)S(1)} %collective-permute-done.11.m2.r2, ...), custom_call_target="tpu_custom_call" | custom-call | flops 100000 | bytes 10000 | tf_op jit(solution)/shard_map/pallas_call | solution.py:330
  52.6 1.4 %shard_map.112 = (f32[128,1792]{1,0:T(8,128)S(1)}, f32[128,1792]{1,0:T(8,128)S(1)}) custom-call(s32[2]{0:T(128)S(1)} %pad_add_fusion.place, bf16[256,768]{1,0:T(8,128)(2,1)S(1)} %get-tuple-element.60.t.gt, bf16[768,1792]{1,0:T(8,128)(2,1)S(1)} %get-tuple-element.61.cols, bf16[128,256]{1,0:T(8,128)(2,1)S(1)} %get-tuple-element.65.late.rk), custom_call_target="tpu_custom_call" | custom-call | flops 100000 | bytes 10000 | tf_op jit(solution)/shard_map/pallas_call | solution.py:330
  54.0 0.1 collective-permute-start.15
  54.1 1.7 %shard_map.113 = (bf16[128,1792]{1,0:T(8,128)(2,1)S(1)}, bf16[128,1792]{1,0:T(8,128)(2,1)S(1)}) custom-call(s32[2]{0:T(128)S(1)} %pad_add_fusion.place, bf16[192,256]{1,0:T(8,128)(2,1)S(1)} %get-tuple-element.51.g0, bf16[192,256]{1,0:T(8,128)(2,1)S(1)} %collective-permute-done.7.g1, bf16[192,256]{1,0:T(8,128)(2,1)S(1)} %collective-permute-done.8.g2, ...), custom_call_target="tpu_custom_call" | custom-call | flops 100000 | bytes 10000 | tf_op jit(solution)/shard_map/pallas_call | solution.py:330
  55.9 0.6 collective-permute-start.14
  56.4 0.1 collective-permute-start.16
  56.5 1.4 %collective-permute-done.16.rs = bf16[128,256]{1,0:T(8,128)(2,1)S(1)} collective-permute-done((bf16[128,256]{1,0:T(8,128)(2,1)S(1)}, bf16[128,256]{1,0:T(8,128)(2,1)S(1)}, u32[]{:S(2)}, u32[]{:S(2)}) %collective-permute-start.16) | collective-permute-done | bytes 65568 | tf_op jit(solution)/shard_map/ppermute | solution.py:363
  58.0 0.0 collective-permute-done.14.s1
  58.0 0.0 collective-permute-done.15.s2
  58.0 0.7 shard_map.114
  58.7 0.1 collective-permute-start.17
  58.8 2.2 %collective-permute-start.18 = (bf16[64,2048]{1,0:T(8,128)(2,1)S(1)}, bf16[64,2048]{1,0:T(8,128)(2,1)S(1)}, u32[]{:S(2)}, u32[]{:S(2)}) collective-permute-start(bf16[64,2048]{1,0:T(8,128)(2,1)S(1)} %get-tuple-element.73), channel_id=1, source_target_pairs={{0,128},{4,132},{8,136},{12,140},{16,144},{20,148},{24,152},{28,15... | collective-permute-start | bytes 786440 | tf_op jit(solution)/shard_map/ppermute | solution.py:363
  61.0 2.5 %collective-permute-start.19 = (bf16[64,2048]{1,0:T(8,128)(2,1)S(1)}, bf16[64,2048]{1,0:T(8,128)(2,1)S(1)}, u32[]{:S(2)}, u32[]{:S(2)}) collective-permute-start(bf16[64,2048]{1,0:T(8,128)(2,1)S(1)} %get-tuple-element.74), channel_id=1, source_target_pairs={{0,192},{4,196},{8,200},{12,204},{16,208},{20,212},{24,216},{28,22... | collective-permute-start | bytes 786440 | tf_op jit(solution)/shard_map/ppermute | solution.py:363
  63.5 4.4 %collective-permute-done.17.a1 = bf16[64,2048]{1,0:T(8,128)(2,1)S(1)} collective-permute-done((bf16[64,2048]{1,0:T(8,128)(2,1)S(1)}, bf16[64,2048]{1,0:T(8,128)(2,1)S(1)}, u32[]{:S(2)}, u32[]{:S(2)}) %collective-permute-start.17) | collective-permute-done | bytes 262176 | tf_op jit(solution)/shard_map/ppermute | solution.py:363
  67.9 5.4 %collective-permute-done.18.a2 = bf16[64,2048]{1,0:T(8,128)(2,1)S(1)} collective-permute-done((bf16[64,2048]{1,0:T(8,128)(2,1)S(1)}, bf16[64,2048]{1,0:T(8,128)(2,1)S(1)}, u32[]{:S(2)}, u32[]{:S(2)}) %collective-permute-start.18) | collective-permute-done | bytes 262176 | tf_op jit(solution)/shard_map/ppermute | solution.py:363
  73.3 2.6 %collective-permute-done.19.a3 = bf16[64,2048]{1,0:T(8,128)(2,1)S(1)} collective-permute-done((bf16[64,2048]{1,0:T(8,128)(2,1)S(1)}, bf16[64,2048]{1,0:T(8,128)(2,1)S(1)}, u32[]{:S(2)}, u32[]{:S(2)}) %collective-permute-start.19) | collective-permute-done | bytes 262176 | tf_op jit(solution)/shard_map/ppermute | solution.py:363
  75.9 0.9 shard_map.115
  76.7 18.5 %all_to_all.5.refs_0_ = bf16[8,8,2816]{2,1,0:T(8,128)(2,1)S(1)} all-to-all(bf16[8,8,2816]{2,1,0:T(8,128)(2,1)S(1)} %bitcast.5), channel_id=1, replica_groups={{0,8,16,24,32,40,48,56},{4,12,20,28,36,44,52,60},{64,72,80,88,96,104,11..., dimensions={0} | all-to-all | bytes 720896 | tf_op jit(solution)/shard_map/all_to_all | solution.py:503
  95.2 0.8 shard_map.116
Async XLA Ops:
  0.7 6.1 %copy-start.1 = (bf16[256,6912]{1,0:T(8,128)(2,1)S(1)}, bf16[256,6912]{1,0:T(8,128)(2,1)}, u32[]{:S(2)}) copy-start(bf16[256,6912]{1,0:T(8,128)(2,1)} %weight.2) | copy-start | bytes 10616836
  2.9 24.5 %copy-start = (bf16[256,6912]{1,0:T(8,128)(2,1)S(1)}, bf16[256,6912]{1,0:T(8,128)(2,1)}, u32[]{:S(2)}) copy-start(bf16[256,6912]{1,0:T(8,128)(2,1)} %weight.3) | copy-start | bytes 10616836
  2.9 21.5 %collective-permute-start.4 = (bf16[224,768]{1,0:T(8,128)(2,1)S(1)}, bf16[224,768]{1,0:T(8,128)(2,1)S(1)}, u32[]{:S(2)}, u32[]{:S(2)}) collective-permute-start(bf16[224,768]{1,0:T(8,128)(2,1)S(1)} %get-tuple-element.49.p0), channel_id=1, source_target_pairs={{0,1},{1,0},{2,3},{3,2},{4,5},{5,4},{6,7},{7,6},{8,9},{9,8},{10,11... | collective-permute-start | bytes 1032200 | tf_op jit(solution)/shard_map/ppermute | solution.py:363
  5.2 19.1 %collective-permute-start.5 = (bf16[224,768]{1,0:T(8,128)(2,1)S(1)}, bf16[224,768]{1,0:T(8,128)(2,1)S(1)}, u32[]{:S(2)}, u32[]{:S(2)}) collective-permute-start(bf16[224,768]{1,0:T(8,128)(2,1)S(1)} %get-tuple-element.49.p0), channel_id=1, source_target_pairs={{0,2},{1,3},{2,0},{3,1},{4,6},{5,7},{6,4},{7,5},{8,10},{9,11},{10,... | collective-permute-start | bytes 1032200 | tf_op jit(solution)/shard_map/ppermute | solution.py:363
  5.9 18.4 %collective-permute-start.6 = (bf16[224,768]{1,0:T(8,128)(2,1)S(1)}, bf16[224,768]{1,0:T(8,128)(2,1)S(1)}, u32[]{:S(2)}, u32[]{:S(2)}) collective-permute-start(bf16[224,768]{1,0:T(8,128)(2,1)S(1)} %get-tuple-element.49.p0), channel_id=1, source_target_pairs={{0,3},{1,2},{2,1},{3,0},{4,7},{5,6},{6,5},{7,4},{8,11},{9,10},{10,... | collective-permute-start | bytes 1032200 | tf_op jit(solution)/shard_map/ppermute | solution.py:363
  9.9 8.2 %collective-permute-start = (bf16[96,256]{1,0:T(8,128)(2,1)S(1)}, bf16[96,256]{1,0:T(8,128)(2,1)S(1)}, u32[]{:S(2)}, u32[]{:S(2)}) collective-permute-start(bf16[96,256]{1,0:T(8,128)(2,1)S(1)} %get-tuple-element.42), channel_id=1, source_target_pairs={{0,4},{4,0},{8,12},{12,8},{16,20},{20,16},{24,28},{28,24},{32,36},... | collective-permute-start | bytes 147464 | tf_op jit(solution)/shard_map/ppermute | solution.py:359
  10.0 9.8 %collective-permute-start.1 = (bf16[96,256]{1,0:T(8,128)(2,1)S(1)}, bf16[96,256]{1,0:T(8,128)(2,1)S(1)}, u32[]{:S(2)}, u32[]{:S(2)}) collective-permute-start(bf16[96,256]{1,0:T(8,128)(2,1)S(1)} %get-tuple-element.43), channel_id=1, source_target_pairs={{0,252},{4,8},{8,4},{12,16},{16,12},{20,24},{24,20},{28,32},{32,28... | collective-permute-start | bytes 147464 | tf_op jit(solution)/shard_map/ppermute | solution.py:359
  20.4 5.1 %collective-permute-start.2 = (bf16[96,256]{1,0:T(8,128)(2,1)S(1)}, bf16[96,256]{1,0:T(8,128)(2,1)S(1)}, u32[]{:S(2)}, u32[]{:S(2)}) collective-permute-start(bf16[96,256]{1,0:T(8,128)(2,1)S(1)} %get-tuple-element.45.late), channel_id=1, source_target_pairs={{0,1},{1,0},{2,3},{3,2},{4,5},{5,4},{6,7},{7,6},{8,9},{9,8},{10,11... | collective-permute-start | bytes 147464 | tf_op jit(solution)/shard_map/ppermute | solution.py:359
  22.2 4.2 %collective-permute-start.3 = (bf16[96,256]{1,0:T(8,128)(2,1)S(1)}, bf16[96,256]{1,0:T(8,128)(2,1)S(1)}, u32[]{:S(2)}, u32[]{:S(2)}) collective-permute-start(bf16[96,256]{1,0:T(8,128)(2,1)S(1)} %get-tuple-element.46), channel_id=1, source_target_pairs={{0,3},{1,2},{2,1},{3,0},{4,7},{5,6},{6,5},{7,4},{8,11},{9,10},{10,... | collective-permute-start | bytes 147464 | tf_op jit(solution)/shard_map/ppermute | solution.py:359
  30.4 10.8 %collective-permute-start.10 = (bf16[864,256]{1,0:T(8,128)(2,1)S(1)}, bf16[864,256]{1,0:T(8,128)(2,1)S(1)}, u32[]{:S(2)}, u32[]{:S(2)}) collective-permute-start(bf16[864,256]{1,0:T(8,128)(2,1)S(1)} %get-tuple-element.55), channel_id=1, source_target_pairs={{0,4},{4,0},{8,12},{12,8},{16,20},{20,16},{24,28},{28,24},{32,36},... | collective-permute-start | bytes 1327112 | tf_op jit(solution)/shard_map/ppermute | solution.py:359
  30.5 12.0 %collective-permute-start.11 = (bf16[864,256]{1,0:T(8,128)(2,1)S(1)}, bf16[864,256]{1,0:T(8,128)(2,1)S(1)}, u32[]{:S(2)}, u32[]{:S(2)}) collective-permute-start(bf16[864,256]{1,0:T(8,128)(2,1)S(1)} %get-tuple-element.56), channel_id=1, source_target_pairs={{0,252},{4,8},{8,4},{12,16},{16,12},{20,24},{24,20},{28,32},{32,28... | collective-permute-start | bytes 1327112 | tf_op jit(solution)/shard_map/ppermute | solution.py:359
  36.6 15.0 %collective-permute-start.7 = (bf16[192,256]{1,0:T(8,128)(2,1)S(1)}, bf16[192,256]{1,0:T(8,128)(2,1)S(1)}, u32[]{:S(2)}, u32[]{:S(2)}) collective-permute-start(bf16[192,256]{1,0:T(8,128)(2,1)S(1)} %get-tuple-element.51.g0), channel_id=1, source_target_pairs={{0,1},{1,0},{2,3},{3,2},{4,5},{5,4},{6,7},{7,6},{8,9},{9,8},{10,11... | collective-permute-start | bytes 294920 | tf_op jit(solution)/shard_map/ppermute | solution.py:363
  39.7 11.9 %collective-permute-start.8 = (bf16[192,256]{1,0:T(8,128)(2,1)S(1)}, bf16[192,256]{1,0:T(8,128)(2,1)S(1)}, u32[]{:S(2)}, u32[]{:S(2)}) collective-permute-start(bf16[192,256]{1,0:T(8,128)(2,1)S(1)} %get-tuple-element.51.g0), channel_id=1, source_target_pairs={{0,2},{1,3},{2,0},{3,1},{4,6},{5,7},{6,4},{7,5},{8,10},{9,11},{10,... | collective-permute-start | bytes 294920 | tf_op jit(solution)/shard_map/ppermute | solution.py:363
  39.7 11.9 %collective-permute-start.9 = (bf16[192,256]{1,0:T(8,128)(2,1)S(1)}, bf16[192,256]{1,0:T(8,128)(2,1)S(1)}, u32[]{:S(2)}, u32[]{:S(2)}) collective-permute-start(bf16[192,256]{1,0:T(8,128)(2,1)S(1)} %get-tuple-element.51.g0), channel_id=1, source_target_pairs={{0,3},{1,2},{2,1},{3,0},{4,7},{5,6},{6,5},{7,4},{8,11},{9,10},{10,... | collective-permute-start | bytes 294920 | tf_op jit(solution)/shard_map/ppermute | solution.py:363
  43.1 8.5 %collective-permute-start.12 = (bf16[96,256]{1,0:T(8,128)(2,1)S(1)}, bf16[96,256]{1,0:T(8,128)(2,1)S(1)}, u32[]{:S(2)}, u32[]{:S(2)}) collective-permute-start(bf16[96,256]{1,0:T(8,128)(2,1)S(1)} %get-tuple-element.58.late), channel_id=1, source_target_pairs={{0,1},{1,0},{2,3},{3,2},{4,5},{5,4},{6,7},{7,6},{8,9},{9,8},{10,11... | collective-permute-start | bytes 147464 | tf_op jit(solution)/shard_map/ppermute | solution.py:359
  46.4 5.3 %collective-permute-start.13 = (bf16[96,256]{1,0:T(8,128)(2,1)S(1)}, bf16[96,256]{1,0:T(8,128)(2,1)S(1)}, u32[]{:S(2)}, u32[]{:S(2)}) collective-permute-start(bf16[96,256]{1,0:T(8,128)(2,1)S(1)} %get-tuple-element.63), channel_id=1, source_target_pairs={{0,3},{1,2},{2,1},{3,0},{4,7},{5,6},{6,5},{7,4},{8,11},{9,10},{10,... | collective-permute-start | bytes 147464 | tf_op jit(solution)/shard_map/ppermute | solution.py:359
  54.0 3.9 %collective-permute-start.15 = (f32[128,1792]{1,0:T(8,128)S(1)}, f32[128,1792]{1,0:T(8,128)S(1)}, u32[]{:S(2)}, u32[]{:S(2)}) collective-permute-start(f32[128,1792]{1,0:T(8,128)S(1)} %get-tuple-element.69), channel_id=1, source_target_pairs={{0,4},{4,0},{8,12},{12,8},{16,20},{20,16},{24,28},{28,24},{32,36},... | collective-permute-start | bytes 2752520 | tf_op jit(solution)/shard_map/ppermute | solution.py:363
  55.9 2.1 %collective-permute-start.14 = (bf16[128,1792]{1,0:T(8,128)(2,1)S(1)}, bf16[128,1792]{1,0:T(8,128)(2,1)S(1)}, u32[]{:S(2)}, u32[]{:S(2)}) collective-permute-start(bf16[128,1792]{1,0:T(8,128)(2,1)S(1)} %get-tuple-element.68), channel_id=1, source_target_pairs={{0,4},{4,0},{8,12},{12,8},{16,20},{20,16},{24,28},{28,24},{32,36},... | collective-permute-start | bytes 1376264 | tf_op jit(solution)/shard_map/ppermute | solution.py:363
  56.4 1.5 %collective-permute-start.16 = (bf16[128,256]{1,0:T(8,128)(2,1)S(1)}, bf16[128,256]{1,0:T(8,128)(2,1)S(1)}, u32[]{:S(2)}, u32[]{:S(2)}) collective-permute-start(bf16[128,256]{1,0:T(8,128)(2,1)S(1)} %get-tuple-element.70), channel_id=1, source_target_pairs={{0,4},{4,0},{8,12},{12,8},{16,20},{20,16},{24,28},{28,24},{32,36},... | collective-permute-start | bytes 196616 | tf_op jit(solution)/shard_map/ppermute | solution.py:363
  58.7 9.2 %collective-permute-start.17 = (bf16[64,2048]{1,0:T(8,128)(2,1)S(1)}, bf16[64,2048]{1,0:T(8,128)(2,1)S(1)}, u32[]{:S(2)}, u32[]{:S(2)}) collective-permute-start(bf16[64,2048]{1,0:T(8,128)(2,1)S(1)} %get-tuple-element.72), channel_id=1, source_target_pairs={{0,64},{4,68},{8,72},{12,76},{16,80},{20,84},{24,88},{28,92},{32,9... | collective-permute-start | bytes 786440 | tf_op jit(solution)/shard_map/ppermute | solution.py:363
  58.8 14.5 %collective-permute-start.18 = (bf16[64,2048]{1,0:T(8,128)(2,1)S(1)}, bf16[64,2048]{1,0:T(8,128)(2,1)S(1)}, u32[]{:S(2)}, u32[]{:S(2)}) collective-permute-start(bf16[64,2048]{1,0:T(8,128)(2,1)S(1)} %get-tuple-element.73), channel_id=1, source_target_pairs={{0,128},{4,132},{8,136},{12,140},{16,144},{20,148},{24,152},{28,15... | collective-permute-start | bytes 786440 | tf_op jit(solution)/shard_map/ppermute | solution.py:363
  61.0 14.8 %collective-permute-start.19 = (bf16[64,2048]{1,0:T(8,128)(2,1)S(1)}, bf16[64,2048]{1,0:T(8,128)(2,1)S(1)}, u32[]{:S(2)}, u32[]{:S(2)}) collective-permute-start(bf16[64,2048]{1,0:T(8,128)(2,1)S(1)} %get-tuple-element.74), channel_id=1, source_target_pairs={{0,192},{4,196},{8,200},{12,204},{16,208},{20,212},{24,216},{28,22... | collective-permute-start | bytes 786440 | tf_op jit(solution)/shard_map/ppermute | solution.py:363

commit v5 on v4

--- a/solution.py
+++ b/solution.py
@@ -103,7 +103,7 @@
     srow[...] = jnp.broadcast_to(total.astype(jnp.int32) - 1, srow.shape)
 
 
-def spread_terms(place, nbt, grad, weight, own, m1, m2, loc, acc):
+def spread_kernel(place, nbt, grad, weight, own, m1, m2, loc, acc):
     rows = iota((EXT, C), 0)
     table = nbt[...].astype(jnp.int32)
     gradient = grad[...]
@@ -116,19 +116,9 @@
     even = place[0] % 2 == 0
     own[...] = acc[0:S, :]
     first, last = jnp.where(even, S, S + 160), jnp.where(even, S + 160, S)
-    m1[0:96, :] = acc[pl.ds(pl.multiple_of(first, 32), 96), :].astype(BF)
-    m2[0:96, :] = acc[pl.ds(pl.multiple_of(last, 32), 96), :].astype(BF)
+    m1[...] = acc[pl.ds(pl.multiple_of(first, 32), 96), :].astype(BF)
+    m2[...] = acc[pl.ds(pl.multiple_of(last, 32), 96), :].astype(BF)
     loc[...] = acc[S + 96 : S + 160, :].astype(BF)
-
-
-def spread_kernel(place, nbt, grad, weight, own, m1, m2, loc, acc):
-    spread_terms(place, nbt, grad, weight, own, m1, m2, loc, acc)
-
-
-def spread_with_kernel(place, nbt, grad, weight, o1, o2, own, m1, m2, loc, acc):
-    m1[96:, :] = o1[...]
-    m2[96:, :] = o2[...]
-    spread_terms(place, nbt, grad, weight, own, m1, m2, loc, acc)
 
 
 def inner(position, count):
@@ -139,7 +129,7 @@
     return jnp.where(keep, rows, jnp.zeros_like(rows))
 
 
-def pass_kernel(place, loc, m1, m2, n1, n2):
+def pass_kernel(place, loc, m2, m1, n2, n1):
     even = place[1] % 2 == 0
     first = jnp.where(even, 0, 1)
     far = inner(place[0], 64)
@@ -164,7 +154,7 @@
     return own[...] + mm(halo_matrix(hrow[0:1, :]), rows)
 
 
-def gate_kernel(place, own, m1, m2, n1, n2, hrow, pre, late, out, ordered, back):
+def gate_kernel(place, own, m1, m2, n1, n2, hrow, pre, out, ordered, back):
     hidden_grad = settled(place, own, m1, m2, n1, n2, hrow, back)
     z = pre[...].astype(F32)
     g = 1.0 / (1.0 + jnp.exp(-z))
@@ -173,7 +163,7 @@
     ordered[...] = mm(value, channel_order()).astype(BF)
 
 
-def rows_kernel(place, own, m1, m2, n1, n2, hrow, grad, srow, t, g1, g2, g3, keep, send, back):
+def rows_kernel(place, own, m1, m2, n1, n2, hrow, grad, srow, t, g2, g1, g3, keep, send, back):
     total = settled(place, own, m1, m2, n1, n2, hrow, back)
     value = (grad[...].astype(F32) + total).astype(BF)
     chosen = mm_t(onehot(iota((S, C), 0) == srow[0:1, :]), value).astype(BF)
@@ -181,8 +171,10 @@
     send[...] = chosen[128:256, :]
 
 
-def pick_kernel(place, p0, p1, p2, p3, late, o1, o2, loc, picked):
+def pick_kernel(place, p0, p2, p1, p3, m1, m2, o1, o2, loc, picked):
     column = place[1]
+    o1[0:96, :] = m1[...]
+    o2[0:96, :] = m2[...]
     for turn, pay in enumerate((p0, p1, p2, p3)):
         halo_row = pay[S : S + 16, 2 * C : 3 * C].astype(F32)[0:1, :].astype(jnp.int32) - 1
         rows = mm_t(halo_matrix(halo_row), pay[0:S, 0 : 2 * C])
@@ -197,7 +189,7 @@
             at = HB * (b + 1)
             for out, side in ((o1, up), (o2, down)):
                 rows = picked[source, pl.ds(side + at, HB), :] if 0 <= source < 4 else none
-                to = 96 * tile + at
+                to = 96 + 96 * tile + at
                 out[to : to + HB, :] = rows[:, 0:C]
                 out[to + 384 : to + 384 + HB, :] = rows[:, C : 2 * C]
             if b:
@@ -207,7 +199,7 @@
 
 
 def columns_kernel(
-    place, p0, p1, p2, p3, r1, r2, loc, late, gt, cols_one, cols_two, ext, ids, sel
+    place, p0, p2, p1, p3, r2, r1, loc, late, gt, cols_one, cols_two, ext, ids, sel
 ):
     column = place[1]
     start = column * QW
@@ -268,7 +260,7 @@
     weight_blocks(place, gt, cols, keep, send)
 
 
-def weight_one_kernel(place, g0, g1, g2, g3, cols, late, keep, send, gt):
+def weight_one_kernel(place, g0, g2, g1, g3, cols, late, keep, send, gt):
     for turn, grad in enumerate((g0, g1, g2, g3)):
         gt[:, turn * S : (turn + 1) * S] = jnp.transpose(grad[...].astype(F32)).astype(BF)
     weight_blocks(place, gt, cols, keep, send)
@@ -287,7 +279,7 @@
         out[32:64, 7 * C : 8 * C] = jnp.where(first, other, mine)
 
 
-def line_kernel(place, a0, a1, a2, a3, out):
+def line_kernel(place, a0, a2, a1, a3, out):
     line = place[0] // 16
     to, at = iota((64, 64), 0), iota((64, 64), 1)
     order = onehot(at == 32 * ((to % 8) // 4) + 4 * (to // 8) + to % 4)
@@ -338,34 +330,45 @@
     )(*args)
 
 
-def spread(place, nbt, grad, weight, *picks):
-    edge = sds((96 + (picks[0].shape[0] if picks else 0), C), BF)
+def spread(place, nbt, grad, weight):
+    edge = sds((96, C), BF)
     return call(
-        spread_with_kernel if picks else spread_kernel,
+        spread_kernel,
         (sds((S, C), F32), edge, edge, sds((64, C), BF)),
         place,
         nbt,
         grad,
         weight,
-        *picks,
         scratch=[pltpu.VMEM((EXT, C), F32)],
     )
 
 
 def swap(value, axis, turn):
-    size = lax.axis_size(axis)
-    step = 1 if turn == 1 else -1
-    pairs = [(n, (n + (step if n % 2 == 0 else -step)) % size) for n in range(size)]
-    return lax.ppermute(value, axis, pairs)
+    gx, gy = lax.axis_size("gx"), lax.axis_size("gy")
+    pairs = []
+    for i in range(gx):
+        for j in range(gy):
+            n, size = (i, gx) if axis == "gx" else (j, gy)
+            q = n ^ 1 if turn == 1 else ((n + 1) ^ 1) - 1
+            if axis == "gx":
+                to = (q, j) if 0 <= q < size else (i, j ^ 1)
+            else:
+                to = (i, q) if 0 <= q < size else (i ^ 1, j)
+            pairs.append((i * gy + j, to[0] * gy + to[1]))
+    return lax.ppermute(value, ("gx", "gy"), pairs)
 
 
 def cross(value, axis, mask):
     return lax.ppermute(value, axis, [(n, n ^ mask) for n in range(lax.axis_size(axis))])
 
 
+def gathered(value, axis, base=1):
+    return [value] + [cross(value, axis, base * d) for d in (2, 1, 3)]
+
+
 def give_back(place, loc, m1, m2):
-    m1, m2 = swap(m1, "gx", 1), swap(m2, "gx", 2)
-    n1, n2 = call(pass_kernel, (sds((96, C), BF), sds((96, C), BF)), place, loc, m1, m2)
+    m2, m1 = swap(m2, "gx", 2), swap(m1, "gx", 1)
+    n2, n1 = call(pass_kernel, (sds((96, C), BF), sds((96, C), BF)), place, loc, m2, m1)
     return (m1, m2, swap(n1, "gy", 1), swap(n2, "gy", 2)), n1
 
 
@@ -405,34 +408,25 @@
             pltpu.SemaphoreType.DMA((6,)),
         ],
     )
-    pays = [pay] + [cross(pay, "gy", d) for d in (1, 2, 3)]
+    pays = gathered(pay, "gy")
     own, m1, m2, loc = spread(place, nbt, grad, weight_two)
     back = pltpu.VMEM((8, HB, C), BF)
-    arrived, passed = give_back(place, loc, m1, m2)
-    picks = sds((768, C), BF)
-    o1, o2, near = call(
+    arrived, _ = give_back(place, loc, m1, m2)
+    grad_pre, ordered = call(
+        gate_kernel, (tile, tile), place, own, *arrived, hrow, pre, scratch=[back]
+    )
+    grads = gathered(ordered, "gy")
+    own, m1, m2, loc = spread(place, nbt, grad_pre, weight_one)
+    picks = sds((96 + 768, C), BF)
+    m1, m2, near = call(
         pick_kernel,
         (picks, picks, sds((4, 64, 2 * C), BF)),
         place,
         *pays,
-        passed,
+        m1,
+        m2,
         scratch=[pltpu.VMEM((4, 8 * HB, 2 * C), BF)],
-        late=1,
-    )
-    grad_pre, ordered = call(
-        gate_kernel,
-        (tile, tile),
-        place,
-        own,
-        *arrived,
-        hrow,
-        pre,
-        near,
-        scratch=[back],
-        late=1,
-    )
-    grads = [ordered] + [cross(ordered, "gy", d) for d in (1, 2, 3)]
-    own, m1, m2, loc = spread(place, nbt, grad_pre, weight_one, o1, o2)
+    )
     arrived, passed = give_back(place, loc, m1, m2)
     wide = 7 * C
     half = sds((128, wide), BF)
@@ -442,8 +436,8 @@
         (sds((C, 4 * S), BF), stack, stack),
         place,
         *pays,
+        arrived[1],
         arrived[0],
-        arrived[1],
         near,
         passed,
         scratch=[
@@ -497,7 +491,7 @@
         rows_keep,
         rows_come,
     )
-    chunks = [chunks[0]] + [cross(chunks[d], "gx", 16 * d) for d in (1, 2, 3)]
+    chunks = [chunks[0]] + [cross(chunks[d], "gx", 16 * d) for d in (2, 1, 3)]
     summed = call(line_kernel, sds((64, 11 * C), BF), place, *chunks)
     groups = [[16 * y + 2 * z + e for z in range(8)] for y in range(4) for e in range(2)]
     collected = lax.all_to_all(

time: 96.5 us -> 93.4 us (0.968); the launches traced: 96.1 us -> 91.7 us
  starting transfers between devices: 35.6 us -> 17.1 us
  waiting for transfers between devices: 17.9 us -> 33.8 us
  blocking collectives: 18.5 us -> 16.8 us
    ppermute x8, starting transfers between devices: 21.5 us -> 3.76 us  [swap(): return lax.ppermute(value, ('gx', 'gy'), pairs)]
    ppermute x8, waiting for transfers between devices: 4.12 us -> 20.7 us  [swap(): return lax.ppermute(value, ('gx', 'gy'), pairs)]
    all_to_all x1, blocking collectives: 18.5 us -> 16.8 us  [body(): lax.all_to_all(summed.reshape(8, 8, 11 * C), 'gx', split_axis=0, concat_a...]
  transfers between devices with their start and end apart: 20 -> 20, of which waited for: 7 -> 8; matrix products, arithmetic and copies ran while one was open for 0% -> 0% of each run, Pallas kernels for 13% -> 16%
where the time goes in v5:
time: 93.4 us; the launch traced here: 91.7 us
  waiting for transfers between devices  33.8 us (36%)
  Pallas kernels  23.1 us (25%)
  starting transfers between devices  17.1 us (18%)
  blocking collectives  16.8 us (18%)
    pallas_call x14, Pallas kernels, call(): pl.pallas_call(kernel, out_shape=outs, in_specs=specs, out_specs=jax.tree...  23.1 us
    ppermute x8, waiting for transfers between devices, swap(): return lax.ppermute(value, ('gx', 'gy'), pairs)  20.7 us
    all_to_all x1, blocking collectives, body(): lax.all_to_all(summed.reshape(8, 8, 11 * C), 'gx', split_axis=0, concat_a...  16.8 us
    ppermute x12, starting transfers between devices, cross(): lax.ppermute(value, axis, [(n, n ^ mask) for n in range(lax.axis_size(axi...  13.3 us
    ppermute x12, waiting for transfers between devices, cross(): lax.ppermute(value, axis, [(n, n ^ mask) for n in range(lax.axis_size(axi...  13.1 us
    ppermute x8, starting transfers between devices, swap(): return lax.ppermute(value, ('gx', 'gy'), pairs)  3.76 us
  transfers between devices with their start and end apart: 20, of which 8 were waited for; matrix products, arithmetic and copies ran while one was open for 0% of the time, Pallas kernels for 16%

profile of v5, /device:TPU:2, one launch (start us, length us, event | category | flops | bytes accessed | tf_op | source)
XLA Modules:
  0.0 91.7 jit_solution(10917968478841682927)
XLA Ops:
  0.6 0.1 pad_add_fusion.place
  0.7 0.0 copy-start
  0.7 2.2 %shard_map.103 = (bf16[224,768]{1,0:T(8,128)(2,1)S(1)}, f32[32,256]{1,0:T(8,128)S(1)}, s32[8,256]{1,0:T(8,128)S(1)}, s32[8,256]{1,0:T(8,128)S(1)}, bf16[192,256]...) custom-call(s32[2]{0:T(128)S(1)} %pad_add_fusion.place, bf16[192,256]{1,0:T(8,128)(2,1)} %feat.1, bf16[192,256]{1,0:T(8,128)(2,1)} %pre.1, ...), custom_call_target="tpu_custom_call" | custom-call | flops 4000000000 | bytes 10000 | tf_op jit(solution)/shard_map/pallas_call | solution.py:322
  2.9 0.0 copy-start.1
  2.9 2.2 %collective-permute-start.7 = (bf16[224,768]{1,0:T(8,128)(2,1)S(1)}, bf16[224,768]{1,0:T(8,128)(2,1)S(1)}, u32[]{:S(2)}, u32[]{:S(2)}) collective-permute-start(bf16[224,768]{1,0:T(8,128)(2,1)S(1)} %get-tuple-element.50.p0), channel_id=1, source_target_pairs={{0,2},{1,3},{2,0},{3,1},{4,6},{5,7},{6,4},{7,5},{8,10},{9,11},{10,... | collective-permute-start | bytes 1032200 | tf_op jit(solution)/shard_map/ppermute | solution.py:362
  5.1 1.4 %collective-permute-start.8 = (bf16[224,768]{1,0:T(8,128)(2,1)S(1)}, bf16[224,768]{1,0:T(8,128)(2,1)S(1)}, u32[]{:S(2)}, u32[]{:S(2)}) collective-permute-start(bf16[224,768]{1,0:T(8,128)(2,1)S(1)} %get-tuple-element.50.p0), channel_id=1, source_target_pairs={{0,1},{1,0},{2,3},{3,2},{4,5},{5,4},{6,7},{7,6},{8,9},{9,8},{10,11... | collective-permute-start | bytes 1032200 | tf_op jit(solution)/shard_map/ppermute | solution.py:362
  6.5 0.5 collective-permute-start.9
  7.1 0.0 copy-done
  7.1 3.0 %shard_map.104 = (f32[192,256]{1,0:T(8,128)S(1)}, bf16[96,256]{1,0:T(8,128)(2,1)S(1)}, bf16[96,256]{1,0:T(8,128)(2,1)S(1)}, bf16[64,256]{1,0:T(8,128)(2,1)S(1)}) custom-call(s32[2]{0:T(128)S(1)} %pad_add_fusion.place, f32[32,256]{1,0:T(8,128)S(1)} %get-tuple-element.39.nbt, bf16[192,256]{1,0:T(8,128)(2,1)S(1)} %get-tuple-element.40.grad, ...), custom_call_target="tpu_custom_call" | custom-call | flops 100000 | bytes 10000 | tf_op jit(solution)/shard_map/pallas_call | solution.py:322
  10.1 0.1 collective-permute-start
  10.2 2.4 %collective-permute-start.1 = (bf16[96,256]{1,0:T(8,128)(2,1)S(1)}, bf16[96,256]{1,0:T(8,128)(2,1)S(1)}, u32[]{:S(2)}, u32[]{:S(2)}) collective-permute-start(bf16[96,256]{1,0:T(8,128)(2,1)S(1)} %get-tuple-element.43), channel_id=1, source_target_pairs={{0,1},{1,0},{2,3},{3,2},{4,8},{5,9},{6,10},{7,11},{8,4},{9,5},{10,... | collective-permute-start | bytes 147464 | tf_op jit(solution)/shard_map/ppermute | solution.py:358
  12.6 0.0 collective-permute-done.m1
  12.6 10.2 %collective-permute-done.1.m2 = bf16[96,256]{1,0:T(8,128)(2,1)S(1)} collective-permute-done((bf16[96,256]{1,0:T(8,128)(2,1)S(1)}, bf16[96,256]{1,0:T(8,128)(2,1)S(1)}, u32[]{:S(2)}, u32[]{:S(2)}) %collective-permute-start.1) | collective-permute-done | bytes 49184 | tf_op jit(solution)/shard_map/ppermute | solution.py:358
  22.8 0.6 shard_map.105
  23.3 0.7 collective-permute-start.2
  24.0 0.0 collective-permute-start.3
  24.1 3.5 %collective-permute-done.2.n1 = bf16[96,256]{1,0:T(8,128)(2,1)S(1)} collective-permute-done((bf16[96,256]{1,0:T(8,128)(2,1)S(1)}, bf16[96,256]{1,0:T(8,128)(2,1)S(1)}, u32[]{:S(2)}, u32[]{:S(2)}) %collective-permute-start.2) | collective-permute-done | bytes 49184 | tf_op jit(solution)/shard_map/ppermute | solution.py:358
  27.5 0.6 collective-permute-done.3.n2
  28.1 0.9 shard_map.106
  29.0 0.0 copy-done.1
  29.0 3.0 %shard_map.107 = (f32[192,256]{1,0:T(8,128)S(1)}, bf16[96,256]{1,0:T(8,128)(2,1)S(1)}, bf16[96,256]{1,0:T(8,128)(2,1)S(1)}, bf16[64,256]{1,0:T(8,128)(2,1)S(1)}) custom-call(s32[2]{0:T(128)S(1)} %pad_add_fusion.place, f32[32,256]{1,0:T(8,128)S(1)} %get-tuple-element.39.nbt, bf16[192,256]{1,0:T(8,128)(2,1)S(1)} %get-tuple-element.51.grad, ...), custom_call_target="tpu_custom_call" | custom-call | flops 100000 | bytes 10000 | tf_op jit(solution)/shard_map/pallas_call | solution.py:322
  32.1 0.0 collective-permute-done.7.p2
  32.1 0.0 collective-permute-done.8.p1
  32.1 0.0 collective-permute-done.9.p3
  32.1 1.1 %shard_map.108 = (bf16[864,256]{1,0:T(8,128)(2,1)S(1)}, bf16[864,256]{1,0:T(8,128)(2,1)S(1)}, bf16[4,64,512]{2,1,0:T(8,128)(2,1)S(1)}) custom-call(s32[2]{0:T(128)S(1)} %pad_add_fusion.place, bf16[224,768]{1,0:T(8,128)(2,1)S(1)} %get-tuple-element.50.p0, bf16[224,768]{1,0:T(8,128)(2,1)S(1)} %collective-permute-done.7.p2, ...), custom_call_target="tpu_custom_call" | custom-call | flops 100000 | bytes 10000 | tf_op jit(solution)/shard_map/pallas_call | solution.py:322
  33.2 0.1 collective-permute-start.10
  33.3 0.1 collective-permute-start.11
  33.4 1.4 %collective-permute-start.4 = (bf16[192,256]{1,0:T(8,128)(2,1)S(1)}, bf16[192,256]{1,0:T(8,128)(2,1)S(1)}, u32[]{:S(2)}, u32[]{:S(2)}) collective-permute-start(bf16[192,256]{1,0:T(8,128)(2,1)S(1)} %get-tuple-element.49.g0), channel_id=1, source_target_pairs={{0,2},{1,3},{2,0},{3,1},{4,6},{5,7},{6,4},{7,5},{8,10},{9,11},{10,... | collective-permute-start | bytes 294920 | tf_op jit(solution)/shard_map/ppermute | solution.py:362
  34.8 0.8 collective-permute-start.5
  35.6 2.0 %collective-permute-start.6 = (bf16[192,256]{1,0:T(8,128)(2,1)S(1)}, bf16[192,256]{1,0:T(8,128)(2,1)S(1)}, u32[]{:S(2)}, u32[]{:S(2)}) collective-permute-start(bf16[192,256]{1,0:T(8,128)(2,1)S(1)} %get-tuple-element.49.g0), channel_id=1, source_target_pairs={{0,3},{1,2},{2,1},{3,0},{4,7},{5,6},{6,5},{7,4},{8,11},{9,10},{10,... | collective-permute-start | bytes 294920 | tf_op jit(solution)/shard_map/ppermute | solution.py:362
  37.6 6.5 %collective-permute-done.10.m2.r2 = bf16[864,256]{1,0:T(8,128)(2,1)S(1)} collective-permute-done((bf16[864,256]{1,0:T(8,128)(2,1)S(1)}, bf16[864,256]{1,0:T(8,128)(2,1)S(1)}, u32[]{:S(2)}, u32[]{:S(2)}) %collective-permute-start.10) | collective-permute-done | bytes 442400 | tf_op jit(solution)/shard_map/ppermute | solution.py:358
  44.1 0.0 collective-permute-done.11.m1.r1
  44.1 0.6 shard_map.109
  44.6 0.1 collective-permute-start.12
  44.7 0.3 collective-permute-start.13
  45.0 5.2 %shard_map.110 = (bf16[256,768]{1,0:T(8,128)(2,1)S(1)}, bf16[768,1792]{1,0:T(8,128)(2,1)S(1)}, bf16[768,1792]{1,0:T(8,128)(2,1)S(1)}) custom-call(s32[2]{0:T(128)S(1)} %pad_add_fusion.place, bf16[224,768]{1,0:T(8,128)(2,1)S(1)} %get-tuple-element.50.p0, bf16[224,768]{1,0:T(8,128)(2,1)S(1)} %collective-permute-done.7.p2, ...), custom_call_target="tpu_custom_call" | custom-call | flops 100000 | bytes 10000 | tf_op jit(solution)/shard_map/pallas_call | solution.py:322
  50.3 0.0 collective-permute-done.4.g2
  50.3 0.0 collective-permute-done.5.g1
  50.3 0.0 collective-permute-done.6.g3
  50.3 0.0 collective-permute-done.12.n1
  50.3 0.0 collective-permute-done.13.n2
  50.3 1.0 %shard_map.111 = (bf16[128,256]{1,0:T(8,128)(2,1)S(1)}, bf16[128,256]{1,0:T(8,128)(2,1)S(1)}) custom-call(s32[2]{0:T(128)S(1)} %pad_add_fusion.place, f32[192,256]{1,0:T(8,128)S(1)} %get-tuple-element.62.own, bf16[864,256]{1,0:T(8,128)(2,1)S(1)} %collective-permute-done.11.m1.r1, bf16[864,256]{1,0:T(8,128)(2,1)S(1)} %collective-permute-done.10.m2.r2, ...), custom_call_target="tpu_custom_call" | custom-call | flops 100000 | bytes 10000 | tf_op jit(solution)/shard_map/pallas_call | solution.py:322
  51.3 1.4 %shard_map.112 = (f32[128,1792]{1,0:T(8,128)S(1)}, f32[128,1792]{1,0:T(8,128)S(1)}) custom-call(s32[2]{0:T(128)S(1)} %pad_add_fusion.place, bf16[256,768]{1,0:T(8,128)(2,1)S(1)} %get-tuple-element.60.t.gt, bf16[768,1792]{1,0:T(8,128)(2,1)S(1)} %get-tuple-element.61.cols, bf16[128,256]{1,0:T(8,128)(2,1)S(1)} %get-tuple-element.65.late.rk), custom_call_target="tpu_custom_call" | custom-call | flops 100000 | bytes 10000 | tf_op jit(solution)/shard_map/pallas_call | solution.py:322
  52.7 0.1 collective-permute-start.15
  52.8 1.7 %shard_map.113 = (bf16[128,1792]{1,0:T(8,128)(2,1)S(1)}, bf16[128,1792]{1,0:T(8,128)(2,1)S(1)}) custom-call(s32[2]{0:T(128)S(1)} %pad_add_fusion.place, bf16[192,256]{1,0:T(8,128)(2,1)S(1)} %get-tuple-element.49.g0, bf16[192,256]{1,0:T(8,128)(2,1)S(1)} %collective-permute-done.4.g2, bf16[192,256]{1,0:T(8,128)(2,1)S(1)} %collective-permute-done.5.g1, ...), custom_call_target="tpu_custom_call" | custom-call | flops 100000 | bytes 10000 | tf_op jit(solution)/shard_map/pallas_call | solution.py:322
  54.5 0.6 collective-permute-start.14
  55.1 0.1 collective-permute-start.16
  55.2 1.4 %collective-permute-done.16.rs = bf16[128,256]{1,0:T(8,128)(2,1)S(1)} collective-permute-done((bf16[128,256]{1,0:T(8,128)(2,1)S(1)}, bf16[128,256]{1,0:T(8,128)(2,1)S(1)}, u32[]{:S(2)}, u32[]{:S(2)}) %collective-permute-start.16) | collective-permute-done | bytes 65568 | tf_op jit(solution)/shard_map/ppermute | solution.py:362
  56.6 0.0 collective-permute-done.14.s1
  56.7 0.0 collective-permute-done.15.s2
  56.7 0.7 shard_map.114
  57.4 0.1 collective-permute-start.17
  57.5 0.6 collective-permute-start.18
  58.1 3.5 %collective-permute-start.19 = (bf16[64,2048]{1,0:T(8,128)(2,1)S(1)}, bf16[64,2048]{1,0:T(8,128)(2,1)S(1)}, u32[]{:S(2)}, u32[]{:S(2)}) collective-permute-start(bf16[64,2048]{1,0:T(8,128)(2,1)S(1)} %get-tuple-element.74), channel_id=1, source_target_pairs={{0,192},{4,196},{8,200},{12,204},{16,208},{20,212},{24,216},{28,22... | collective-permute-start | bytes 786440 | tf_op jit(solution)/shard_map/ppermute | solution.py:362
  61.6 6.6 %collective-permute-done.17.a2 = bf16[64,2048]{1,0:T(8,128)(2,1)S(1)} collective-permute-done((bf16[64,2048]{1,0:T(8,128)(2,1)S(1)}, bf16[64,2048]{1,0:T(8,128)(2,1)S(1)}, u32[]{:S(2)}, u32[]{:S(2)}) %collective-permute-start.17) | collective-permute-done | bytes 262176 | tf_op jit(solution)/shard_map/ppermute | solution.py:362
  68.2 2.1 %collective-permute-done.18.a1 = bf16[64,2048]{1,0:T(8,128)(2,1)S(1)} collective-permute-done((bf16[64,2048]{1,0:T(8,128)(2,1)S(1)}, bf16[64,2048]{1,0:T(8,128)(2,1)S(1)}, u32[]{:S(2)}, u32[]{:S(2)}) %collective-permute-start.18) | collective-permute-done | bytes 262176 | tf_op jit(solution)/shard_map/ppermute | solution.py:362
  70.3 2.9 %collective-permute-done.19.a3 = bf16[64,2048]{1,0:T(8,128)(2,1)S(1)} collective-permute-done((bf16[64,2048]{1,0:T(8,128)(2,1)S(1)}, bf16[64,2048]{1,0:T(8,128)(2,1)S(1)}, u32[]{:S(2)}, u32[]{:S(2)}) %collective-permute-start.19) | collective-permute-done | bytes 262176 | tf_op jit(solution)/shard_map/ppermute | solution.py:362
  73.2 0.9 shard_map.115
  74.1 16.8 %all_to_all.5.refs_0_ = bf16[8,8,2816]{2,1,0:T(8,128)(2,1)S(1)} all-to-all(bf16[8,8,2816]{2,1,0:T(8,128)(2,1)S(1)} %bitcast.5), channel_id=1, replica_groups={{0,8,16,24,32,40,48,56},{4,12,20,28,36,44,52,60},{64,72,80,88,96,104,11..., dimensions={0} | all-to-all | bytes 720896 | tf_op jit(solution)/shard_map/all_to_all | solution.py:497
  90.9 0.8 shard_map.116
Async XLA Ops:
  0.7 6.4 %copy-start = (bf16[256,6912]{1,0:T(8,128)(2,1)S(1)}, bf16[256,6912]{1,0:T(8,128)(2,1)}, u32[]{:S(2)}) copy-start(bf16[256,6912]{1,0:T(8,128)(2,1)} %weight.2) | copy-start | bytes 10616836
  2.9 26.2 %copy-start.1 = (bf16[256,6912]{1,0:T(8,128)(2,1)S(1)}, bf16[256,6912]{1,0:T(8,128)(2,1)}, u32[]{:S(2)}) copy-start(bf16[256,6912]{1,0:T(8,128)(2,1)} %weight.3) | copy-start | bytes 10616836
  2.9 29.2 %collective-permute-start.7 = (bf16[224,768]{1,0:T(8,128)(2,1)S(1)}, bf16[224,768]{1,0:T(8,128)(2,1)S(1)}, u32[]{:S(2)}, u32[]{:S(2)}) collective-permute-start(bf16[224,768]{1,0:T(8,128)(2,1)S(1)} %get-tuple-element.50.p0), channel_id=1, source_target_pairs={{0,2},{1,3},{2,0},{3,1},{4,6},{5,7},{6,4},{7,5},{8,10},{9,11},{10,... | collective-permute-start | bytes 1032200 | tf_op jit(solution)/shard_map/ppermute | solution.py:362
  5.1 27.0 %collective-permute-start.8 = (bf16[224,768]{1,0:T(8,128)(2,1)S(1)}, bf16[224,768]{1,0:T(8,128)(2,1)S(1)}, u32[]{:S(2)}, u32[]{:S(2)}) collective-permute-start(bf16[224,768]{1,0:T(8,128)(2,1)S(1)} %get-tuple-element.50.p0), channel_id=1, source_target_pairs={{0,1},{1,0},{2,3},{3,2},{4,5},{5,4},{6,7},{7,6},{8,9},{9,8},{10,11... | collective-permute-start | bytes 1032200 | tf_op jit(solution)/shard_map/ppermute | solution.py:362
  6.5 25.6 %collective-permute-start.9 = (bf16[224,768]{1,0:T(8,128)(2,1)S(1)}, bf16[224,768]{1,0:T(8,128)(2,1)S(1)}, u32[]{:S(2)}, u32[]{:S(2)}) collective-permute-start(bf16[224,768]{1,0:T(8,128)(2,1)S(1)} %get-tuple-element.50.p0), channel_id=1, source_target_pairs={{0,3},{1,2},{2,1},{3,0},{4,7},{5,6},{6,5},{7,4},{8,11},{9,10},{10,... | collective-permute-start | bytes 1032200 | tf_op jit(solution)/shard_map/ppermute | solution.py:362
  10.1 2.5 %collective-permute-start = (bf16[96,256]{1,0:T(8,128)(2,1)S(1)}, bf16[96,256]{1,0:T(8,128)(2,1)S(1)}, u32[]{:S(2)}, u32[]{:S(2)}) collective-permute-start(bf16[96,256]{1,0:T(8,128)(2,1)S(1)} %get-tuple-element.42), channel_id=1, source_target_pairs={{0,4},{1,5},{2,6},{3,7},{4,0},{5,1},{6,2},{7,3},{8,12},{9,13},{10,... | collective-permute-start | bytes 147464 | tf_op jit(solution)/shard_map/ppermute | solution.py:358
  10.2 12.6 %collective-permute-start.1 = (bf16[96,256]{1,0:T(8,128)(2,1)S(1)}, bf16[96,256]{1,0:T(8,128)(2,1)S(1)}, u32[]{:S(2)}, u32[]{:S(2)}) collective-permute-start(bf16[96,256]{1,0:T(8,128)(2,1)S(1)} %get-tuple-element.43), channel_id=1, source_target_pairs={{0,1},{1,0},{2,3},{3,2},{4,8},{5,9},{6,10},{7,11},{8,4},{9,5},{10,... | collective-permute-start | bytes 147464 | tf_op jit(solution)/shard_map/ppermute | solution.py:358
  23.3 4.2 %collective-permute-start.2 = (bf16[96,256]{1,0:T(8,128)(2,1)S(1)}, bf16[96,256]{1,0:T(8,128)(2,1)S(1)}, u32[]{:S(2)}, u32[]{:S(2)}) collective-permute-start(bf16[96,256]{1,0:T(8,128)(2,1)S(1)} %get-tuple-element.45), channel_id=1, source_target_pairs={{0,1},{1,0},{2,3},{3,2},{4,5},{5,4},{6,7},{7,6},{8,9},{9,8},{10,11... | collective-permute-start | bytes 147464 | tf_op jit(solution)/shard_map/ppermute | solution.py:358
  24.0 4.1 %collective-permute-start.3 = (bf16[96,256]{1,0:T(8,128)(2,1)S(1)}, bf16[96,256]{1,0:T(8,128)(2,1)S(1)}, u32[]{:S(2)}, u32[]{:S(2)}) collective-permute-start(bf16[96,256]{1,0:T(8,128)(2,1)S(1)} %get-tuple-element.46), channel_id=1, source_target_pairs={{0,4},{1,2},{2,1},{3,7},{4,0},{5,6},{6,5},{7,3},{8,12},{9,10},{10,... | collective-permute-start | bytes 147464 | tf_op jit(solution)/shard_map/ppermute | solution.py:358
  33.2 10.8 %collective-permute-start.10 = (bf16[864,256]{1,0:T(8,128)(2,1)S(1)}, bf16[864,256]{1,0:T(8,128)(2,1)S(1)}, u32[]{:S(2)}, u32[]{:S(2)}) collective-permute-start(bf16[864,256]{1,0:T(8,128)(2,1)S(1)} %get-tuple-element.54), channel_id=1, source_target_pairs={{0,1},{1,0},{2,3},{3,2},{4,8},{5,9},{6,10},{7,11},{8,4},{9,5},{10,... | collective-permute-start | bytes 1327112 | tf_op jit(solution)/shard_map/ppermute | solution.py:358
  33.3 10.8 %collective-permute-start.11 = (bf16[864,256]{1,0:T(8,128)(2,1)S(1)}, bf16[864,256]{1,0:T(8,128)(2,1)S(1)}, u32[]{:S(2)}, u32[]{:S(2)}) collective-permute-start(bf16[864,256]{1,0:T(8,128)(2,1)S(1)} %get-tuple-element.55), channel_id=1, source_target_pairs={{0,4},{1,5},{2,6},{3,7},{4,0},{5,1},{6,2},{7,3},{8,12},{9,13},{10,... | collective-permute-start | bytes 1327112 | tf_op jit(solution)/shard_map/ppermute | solution.py:358
  33.4 16.8 %collective-permute-start.4 = (bf16[192,256]{1,0:T(8,128)(2,1)S(1)}, bf16[192,256]{1,0:T(8,128)(2,1)S(1)}, u32[]{:S(2)}, u32[]{:S(2)}) collective-permute-start(bf16[192,256]{1,0:T(8,128)(2,1)S(1)} %get-tuple-element.49.g0), channel_id=1, source_target_pairs={{0,2},{1,3},{2,0},{3,1},{4,6},{5,7},{6,4},{7,5},{8,10},{9,11},{10,... | collective-permute-start | bytes 294920 | tf_op jit(solution)/shard_map/ppermute | solution.py:362
  34.8 15.5 %collective-permute-start.5 = (bf16[192,256]{1,0:T(8,128)(2,1)S(1)}, bf16[192,256]{1,0:T(8,128)(2,1)S(1)}, u32[]{:S(2)}, u32[]{:S(2)}) collective-permute-start(bf16[192,256]{1,0:T(8,128)(2,1)S(1)} %get-tuple-element.49.g0), channel_id=1, source_target_pairs={{0,1},{1,0},{2,3},{3,2},{4,5},{5,4},{6,7},{7,6},{8,9},{9,8},{10,11... | collective-permute-start | bytes 294920 | tf_op jit(solution)/shard_map/ppermute | solution.py:362
  35.6 14.7 %collective-permute-start.6 = (bf16[192,256]{1,0:T(8,128)(2,1)S(1)}, bf16[192,256]{1,0:T(8,128)(2,1)S(1)}, u32[]{:S(2)}, u32[]{:S(2)}) collective-permute-start(bf16[192,256]{1,0:T(8,128)(2,1)S(1)} %get-tuple-element.49.g0), channel_id=1, source_target_pairs={{0,3},{1,2},{2,1},{3,0},{4,7},{5,6},{6,5},{7,4},{8,11},{9,10},{10,... | collective-permute-start | bytes 294920 | tf_op jit(solution)/shard_map/ppermute | solution.py:362
  44.6 5.7 %collective-permute-start.12 = (bf16[96,256]{1,0:T(8,128)(2,1)S(1)}, bf16[96,256]{1,0:T(8,128)(2,1)S(1)}, u32[]{:S(2)}, u32[]{:S(2)}) collective-permute-start(bf16[96,256]{1,0:T(8,128)(2,1)S(1)} %get-tuple-element.58.late), channel_id=1, source_target_pairs={{0,1},{1,0},{2,3},{3,2},{4,5},{5,4},{6,7},{7,6},{8,9},{9,8},{10,11... | collective-permute-start | bytes 147464 | tf_op jit(solution)/shard_map/ppermute | solution.py:358
  44.7 5.6 %collective-permute-start.13 = (bf16[96,256]{1,0:T(8,128)(2,1)S(1)}, bf16[96,256]{1,0:T(8,128)(2,1)S(1)}, u32[]{:S(2)}, u32[]{:S(2)}) collective-permute-start(bf16[96,256]{1,0:T(8,128)(2,1)S(1)} %get-tuple-element.63), channel_id=1, source_target_pairs={{0,4},{1,2},{2,1},{3,7},{4,0},{5,6},{6,5},{7,3},{8,12},{9,10},{10,... | collective-permute-start | bytes 147464 | tf_op jit(solution)/shard_map/ppermute | solution.py:358
  52.7 3.9 %collective-permute-start.15 = (f32[128,1792]{1,0:T(8,128)S(1)}, f32[128,1792]{1,0:T(8,128)S(1)}, u32[]{:S(2)}, u32[]{:S(2)}) collective-permute-start(f32[128,1792]{1,0:T(8,128)S(1)} %get-tuple-element.69), channel_id=1, source_target_pairs={{0,4},{4,0},{8,12},{12,8},{16,20},{20,16},{24,28},{28,24},{32,36},... | collective-permute-start | bytes 2752520 | tf_op jit(solution)/shard_map/ppermute | solution.py:362
  54.5 2.1 %collective-permute-start.14 = (bf16[128,1792]{1,0:T(8,128)(2,1)S(1)}, bf16[128,1792]{1,0:T(8,128)(2,1)S(1)}, u32[]{:S(2)}, u32[]{:S(2)}) collective-permute-start(bf16[128,1792]{1,0:T(8,128)(2,1)S(1)} %get-tuple-element.68), channel_id=1, source_target_pairs={{0,4},{4,0},{8,12},{12,8},{16,20},{20,16},{24,28},{28,24},{32,36},... | collective-permute-start | bytes 1376264 | tf_op jit(solution)/shard_map/ppermute | solution.py:362
  55.1 1.5 %collective-permute-start.16 = (bf16[128,256]{1,0:T(8,128)(2,1)S(1)}, bf16[128,256]{1,0:T(8,128)(2,1)S(1)}, u32[]{:S(2)}, u32[]{:S(2)}) collective-permute-start(bf16[128,256]{1,0:T(8,128)(2,1)S(1)} %get-tuple-element.70), channel_id=1, source_target_pairs={{0,4},{4,0},{8,12},{12,8},{16,20},{20,16},{24,28},{28,24},{32,36},... | collective-permute-start | bytes 196616 | tf_op jit(solution)/shard_map/ppermute | solution.py:362
  57.4 10.8 %collective-permute-start.17 = (bf16[64,2048]{1,0:T(8,128)(2,1)S(1)}, bf16[64,2048]{1,0:T(8,128)(2,1)S(1)}, u32[]{:S(2)}, u32[]{:S(2)}) collective-permute-start(bf16[64,2048]{1,0:T(8,128)(2,1)S(1)} %get-tuple-element.72), channel_id=1, source_target_pairs={{0,128},{4,132},{8,136},{12,140},{16,144},{20,148},{24,152},{28,15... | collective-permute-start | bytes 786440 | tf_op jit(solution)/shard_map/ppermute | solution.py:362
  57.5 12.8 %collective-permute-start.18 = (bf16[64,2048]{1,0:T(8,128)(2,1)S(1)}, bf16[64,2048]{1,0:T(8,128)(2,1)S(1)}, u32[]{:S(2)}, u32[]{:S(2)}) collective-permute-start(bf16[64,2048]{1,0:T(8,128)(2,1)S(1)} %get-tuple-element.73), channel_id=1, source_target_pairs={{0,64},{4,68},{8,72},{12,76},{16,80},{20,84},{24,88},{28,92},{32,9... | collective-permute-start | bytes 786440 | tf_op jit(solution)/shard_map/ppermute | solution.py:362
  58.1 15.1 %collective-permute-start.19 = (bf16[64,2048]{1,0:T(8,128)(2,1)S(1)}, bf16[64,2048]{1,0:T(8,128)(2,1)S(1)}, u32[]{:S(2)}, u32[]{:S(2)}) collective-permute-start(bf16[64,2048]{1,0:T(8,128)(2,1)S(1)} %get-tuple-element.74), channel_id=1, source_target_pairs={{0,192},{4,196},{8,200},{12,204},{16,208},{20,212},{24,216},{28,22... | collective-permute-start | bytes 786440 | tf_op jit(solution)/shard_map/ppermute | solution.py:362

commit v6 on v5

--- a/solution.py
+++ b/solution.py
@@ -1,3 +1,4 @@
+import functools
 import math
 
 import jax
@@ -77,12 +78,11 @@
     nbt[0:K, 0:S] = table
     shifted_up = table + 1.0
     high = jnp.floor(shifted_up * (1.0 / 16.0))
-    pay[S : S + 32, :] = jnp.zeros((32, 3 * C), BF)
+    pay[S : S + 32, :] = jnp.zeros((32, 2 * C), BF)
     pay[S : S + K, 0:S] = high.astype(BF)
     pay[S : S + K, C : C + S] = (shifted_up - 16.0 * high).astype(BF)
     z = pre_out[...].astype(F32)
     pay[0:S, C : 2 * C] = (z * (1.0 / (1.0 + jnp.exp(-z)))).astype(BF)
-    pay[0:S, 2 * C : 3 * C] = mm(grad_out[...], channel_order()).astype(BF)
     halo_up = (halo_ids[0] + 1).astype(F32).astype(BF)
     spread = mm(halo_up, onehot(iota((24, 8 * HB), 1) % HB == iota((24, 8 * HB), 0)))
     row = jnp.sum(
@@ -91,7 +91,8 @@
         keepdims=True,
     )
     hrow[...] = jnp.broadcast_to(row.astype(jnp.int32) - 1, hrow.shape)
-    pay[S : S + 32, 2 * C : 3 * C] = jnp.broadcast_to(row, (32, C)).astype(BF)
+    tail = pay[S + 16 : S + 32, 0:C].astype(F32)
+    pay[S + 16 : S + 32, 0:C] = jnp.where(iota((16, C), 0) == 15, row, tail).astype(BF)
     lane, peer = iota((64, C), 1), iota((64, C), 0)
     parity = jnp.where(lane < 128, place[0] % 2, 1 - place[0] % 2)
     pick = onehot(peer == 2 * ((lane % 128) // 4) + parity)
@@ -129,7 +130,7 @@
     return jnp.where(keep, rows, jnp.zeros_like(rows))
 
 
-def pass_kernel(place, loc, m2, m1, n2, n1):
+def pass_kernel(place, loc, m2, m1, late, n2, n1):
     even = place[1] % 2 == 0
     first = jnp.where(even, 0, 1)
     far = inner(place[0], 64)
@@ -154,16 +155,18 @@
     return own[...] + mm(halo_matrix(hrow[0:1, :]), rows)
 
 
-def gate_kernel(place, own, m1, m2, n1, n2, hrow, pre, out, ordered, back):
+def gate_kernel(place, own, m2, m1, n2, n1, hrow, pre, grad, late, out, ordered, back):
     hidden_grad = settled(place, own, m1, m2, n1, n2, hrow, back)
     z = pre[...].astype(F32)
     g = 1.0 / (1.0 + jnp.exp(-z))
     value = (hidden_grad * g * (1.0 + z * (1.0 - g))).astype(BF)
     out[...] = value
-    ordered[...] = mm(value, channel_order()).astype(BF)
-
-
-def rows_kernel(place, own, m1, m2, n1, n2, hrow, grad, srow, t, g2, g1, g3, keep, send, back):
+    order = channel_order()
+    ordered[:, 0:C] = mm(grad[...], order).astype(BF)
+    ordered[:, C : 2 * C] = mm(value, order).astype(BF)
+
+
+def rows_kernel(place, own, m2, m1, n2, n1, hrow, grad, srow, late, keep, send, back):
     total = settled(place, own, m1, m2, n1, n2, hrow, back)
     value = (grad[...].astype(F32) + total).astype(BF)
     chosen = mm_t(onehot(iota((S, C), 0) == srow[0:1, :]), value).astype(BF)
@@ -171,12 +174,10 @@
     send[...] = chosen[128:256, :]
 
 
-def pick_kernel(place, p0, p2, p1, p3, m1, m2, o1, o2, loc, picked):
+def pick_kernel(place, p0, p2, p1, p3, late, o2, o1, loc, picked):
     column = place[1]
-    o1[0:96, :] = m1[...]
-    o2[0:96, :] = m2[...]
     for turn, pay in enumerate((p0, p1, p2, p3)):
-        halo_row = pay[S : S + 16, 2 * C : 3 * C].astype(F32)[0:1, :].astype(jnp.int32) - 1
+        halo_row = pay[S + 16 : S + 32, 0:C].astype(F32)[15:16, :].astype(jnp.int32) - 1
         rows = mm_t(halo_matrix(halo_row), pay[0:S, 0 : 2 * C])
         picked[column ^ turn] = rows.astype(BF)
     even = place[0] % 2 == 0
@@ -189,7 +190,7 @@
             at = HB * (b + 1)
             for out, side in ((o1, up), (o2, down)):
                 rows = picked[source, pl.ds(side + at, HB), :] if 0 <= source < 4 else none
-                to = 96 + 96 * tile + at
+                to = 96 * tile + at
                 out[to : to + HB, :] = rows[:, 0:C]
                 out[to + 384 : to + 384 + HB, :] = rows[:, C : 2 * C]
             if b:
@@ -199,7 +200,7 @@
 
 
 def columns_kernel(
-    place, p0, p2, p1, p3, r2, r1, loc, late, gt, cols_one, cols_two, ext, ids, sel
+    place, p0, p2, p1, p3, r2, r1, loc, late, cols_one, cols_two, ext, ids, sel
 ):
     column = place[1]
     start = column * QW
@@ -214,7 +215,7 @@
         tile = column ^ turn
         for half in range(2):
             lanes = slice(half * C, (half + 1) * C)
-            at = pl.multiple_of(96 + 384 * half + 96 * tile, 32)
+            at = pl.multiple_of(384 * half + 96 * tile, 32)
             above, below = r1[pl.ds(at, 96), :], masked(far, r2[pl.ds(at, 96), :])
             for to, piece in (
                 (0, pay[0:S, lanes]),
@@ -223,9 +224,6 @@
                 (S + 160, jnp.where(even, below, above)),
             ):
                 ext[to : to + piece.shape[0], lanes] = mm(piece, shift).astype(BF)
-        gt[:, turn * S : (turn + 1) * S] = jnp.transpose(
-            pay[0:S, 2 * C : 3 * C].astype(F32)
-        ).astype(BF)
         high = pay[S : S + 32, 0:C].astype(F32)
         low = pay[S : S + 32, C : 2 * C].astype(F32)
         ids[0:32, :] = 16.0 * high + low - 1.0
@@ -245,25 +243,16 @@
             previous = block
 
 
-def weight_blocks(place, gt, cols, keep, send):
+def weight_kernel(lanes, place, g0, g2, g1, g3, cols, late, keep, send, gt):
+    for turn, grad in enumerate((g0, g1, g2, g3)):
+        gt[:, turn * S : (turn + 1) * S] = jnp.transpose(grad[:, lanes].astype(F32)).astype(BF)
     mine = pl.multiple_of((place[0] % 2) * 128, 128)
     other = pl.multiple_of(128 - mine, 128)
     for out, at in ((keep, mine), (send, other)):
         left = gt[pl.ds(at, 128), :]
         for part in range(7):
-            out[:, part * C : (part + 1) * C] = mm(
-                left, cols[:, part * C : (part + 1) * C]
-            ).astype(out.dtype)
-
-
-def weight_two_kernel(place, gt, cols, late, keep, send):
-    weight_blocks(place, gt, cols, keep, send)
-
-
-def weight_one_kernel(place, g0, g2, g1, g3, cols, late, keep, send, gt):
-    for turn, grad in enumerate((g0, g1, g2, g3)):
-        gt[:, turn * S : (turn + 1) * S] = jnp.transpose(grad[...].astype(F32)).astype(BF)
-    weight_blocks(place, gt, cols, keep, send)
+            lanes = slice(part * C, (part + 1) * C)
+            out[:, lanes] = mm(left, cols[:, lanes]).astype(out.dtype)
 
 
 def merge_kernel(place, k1, s1, k2, s2, rk, rs, *outs):
@@ -330,7 +319,7 @@
     )(*args)
 
 
-def spread(place, nbt, grad, weight):
+def spread(place, nbt, grad, weight, flops):
     edge = sds((96, C), BF)
     return call(
         spread_kernel,
@@ -340,6 +329,7 @@
         grad,
         weight,
         scratch=[pltpu.VMEM((EXT, C), F32)],
+        flops=flops,
     )
 
 
@@ -366,10 +356,14 @@
     return [value] + [cross(value, axis, base * d) for d in (2, 1, 3)]
 
 
-def give_back(place, loc, m1, m2):
-    m2, m1 = swap(m2, "gx", 2), swap(m1, "gx", 1)
-    n2, n1 = call(pass_kernel, (sds((96, C), BF), sds((96, C), BF)), place, loc, m2, m1)
-    return (m1, m2, swap(n1, "gy", 1), swap(n2, "gy", 2)), n1
+def halo_lines(m2, m1):
+    return swap(m2, "gx", 2), swap(m1, "gx", 1)
+
+
+def halo_columns(place, loc, m2, m1, late):
+    edge = sds((96, C), BF)
+    n2, n1 = call(pass_kernel, (edge, edge), place, loc, m2, m1, late, late=1)
+    return n1, swap(n2, "gy", 2), swap(n1, "gy", 1)
 
 
 def body(features, pre_act, grad_out, weight_one, weight_two, neighbours, halo_list, send_list):
@@ -380,7 +374,7 @@
     pay, nbt, hrow, srow, pre, grad = call(
         pack_kernel,
         (
-            sds((S + 32, 3 * C), BF),
+            sds((S + 32, 2 * C), BF),
             sds((32, C), F32),
             sds((8, C), jnp.int32),
             sds((8, C), jnp.int32),
@@ -409,75 +403,98 @@
         ],
     )
     pays = gathered(pay, "gy")
-    own, m1, m2, loc = spread(place, nbt, grad, weight_two)
     back = pltpu.VMEM((8, HB, C), BF)
-    arrived, _ = give_back(place, loc, m1, m2)
-    grad_pre, ordered = call(
-        gate_kernel, (tile, tile), place, own, *arrived, hrow, pre, scratch=[back]
-    )
-    grads = gathered(ordered, "gy")
-    own, m1, m2, loc = spread(place, nbt, grad_pre, weight_one)
-    picks = sds((96 + 768, C), BF)
-    m1, m2, near = call(
+    own, m1, m2, loc = spread(place, nbt, grad, weight_two, 10**5)
+    m2, m1 = halo_lines(m2, m1)
+    passed, n2, n1 = halo_columns(place, loc, m2, m1, own)
+    picks = sds((768, C), BF)
+    o2, o1, near = call(
         pick_kernel,
         (picks, picks, sds((4, 64, 2 * C), BF)),
         place,
         *pays,
+        passed,
+        scratch=[pltpu.VMEM((4, 8 * HB, 2 * C), BF)],
+        late=1,
+    )
+    r2, r1 = halo_lines(o2, o1)
+    grad_pre, ordered = call(
+        gate_kernel,
+        (tile, sds((S, 2 * C), BF)),
+        place,
+        own,
+        m2,
         m1,
-        m2,
-        scratch=[pltpu.VMEM((4, 8 * HB, 2 * C), BF)],
-    )
-    arrived, passed = give_back(place, loc, m1, m2)
+        n2,
+        n1,
+        hrow,
+        pre,
+        grad,
+        near,
+        scratch=[back],
+        late=1,
+    )
+    grads = gathered(ordered, "gy")
+    own, m1, m2, loc = spread(place, nbt, grad_pre, weight_one, 4 * 10**9)
+    m2, m1 = halo_lines(m2, m1)
     wide = 7 * C
-    half = sds((128, wide), BF)
     stack = sds((4 * S, wide), BF)
-    turned, cols_one, cols_two = call(
+    cols_one, cols_two = call(
         columns_kernel,
-        (sds((C, 4 * S), BF), stack, stack),
+        (stack, stack),
         place,
         *pays,
-        arrived[1],
-        arrived[0],
+        r2,
+        r1,
         near,
-        passed,
+        own,
         scratch=[
             pltpu.VMEM((EXT, 2 * C), BF),
             pltpu.VMEM((32, C), F32),
             pltpu.VMEM((128, C), F32),
         ],
         late=1,
-    )
+        flops=4 * 10**9,
+    )
+    passed, n2, n1 = halo_columns(place, loc, m2, m1, cols_two)
+
+    def halves(which, cols, kind, late, flops):
+        lanes = slice(which * C, (which + 1) * C)
+        half = sds((128, wide), kind)
+        return call(
+            functools.partial(weight_kernel, lanes),
+            (half, half),
+            place,
+            *grads,
+            cols,
+            late,
+            scratch=[pltpu.VMEM((C, 4 * S), BF)],
+            late=1,
+            flops=flops,
+        )
+
+    keep_two, send_two = halves(0, cols_two, F32, passed, 4 * 10**9)
+    come_two = cross(send_two, "gx", 1)
+    keep_one, send_one = halves(1, cols_one, BF, keep_two, 10**5)
     some = sds((128, C), BF)
     rows_keep, rows_send = call(
         rows_kernel,
         (some, some),
         place,
         own,
-        *arrived,
+        m2,
+        m1,
+        n2,
+        n1,
         hrow,
         grad,
         srow,
-        turned,
-        *grads[1:],
+        keep_one,
         scratch=[back],
-        late=4,
+        late=1,
+        flops=2 * 10**10,
     )
     rows_come = cross(rows_send, "gx", 1)
-    full = sds((128, wide), F32)
-    keep_two, send_two = call(
-        weight_two_kernel, (full, full), place, turned, cols_two, rows_keep, late=1
-    )
-    come_two = cross(send_two, "gx", 1)
-    keep_one, send_one = call(
-        weight_one_kernel,
-        (half, half),
-        place,
-        *grads,
-        cols_one,
-        keep_two,
-        scratch=[pltpu.VMEM((C, 4 * S), BF)],
-        late=1,
-    )
     come_one = cross(send_one, "gx", 1)
     chunk = sds((64, 8 * C), BF)
     chunks = call(

time: 93.4 us -> 85.2 us (0.912)
  waiting for transfers between devices: 33.8 us -> 19 us
  starting transfers between devices: 17.1 us -> 23.2 us
  blocking collectives: 16.8 us -> 17.8 us
    ppermute x8 -> x10, waiting for transfers between devices: 20.7 us -> 5.75 us  [swap(): return lax.ppermute(value, ('gx', 'gy'), pairs)]
    ppermute x8 -> x10, starting transfers between devices: 3.76 us -> 8.84 us  [swap(): return lax.ppermute(value, ('gx', 'gy'), pairs)]
    ppermute x12, starting transfers between devices: 13.3 us -> 14.3 us  [cross(): lax.ppermute(value, axis, [(n, n ^ mask) for n in range(lax.axis_size(axi...]
    all_to_all x1, blocking collectives: 16.8 us -> 17.8 us  [body(): lax.all_to_all(summed.reshape(8, 8, 11 * C), 'gx', split_axis=0, concat_a...]
  transfers between devices with their start and end apart: 20 -> 22, of which waited for: 8 -> 6; matrix products, arithmetic and copies ran while one was open for 0% -> 0% of each run, Pallas kernels for 16% -> 22%
where the time goes in v6:
time: 85.2 us; the launch traced here: 84.2 us
  Pallas kernels  23.3 us (27%)
  starting transfers between devices  23.2 us (27%)
  waiting for transfers between devices  19 us (22%)
  blocking collectives  17.8 us (21%)
    pallas_call x14, Pallas kernels, call(): pl.pallas_call(kernel, out_shape=outs, in_specs=specs, out_specs=jax.tree...  23.3 us
    all_to_all x1, blocking collectives, body(): lax.all_to_all(summed.reshape(8, 8, 11 * C), 'gx', split_axis=0, concat_a...  17.8 us
    ppermute x12, starting transfers between devices, cross(): lax.ppermute(value, axis, [(n, n ^ mask) for n in range(lax.axis_size(axi...  14.3 us
    ppermute x12, waiting for transfers between devices, cross(): lax.ppermute(value, axis, [(n, n ^ mask) for n in range(lax.axis_size(axi...  13.3 us
    ppermute x10, starting transfers between devices, swap(): return lax.ppermute(value, ('gx', 'gy'), pairs)  8.84 us
    ppermute x10, waiting for transfers between devices, swap(): return lax.ppermute(value, ('gx', 'gy'), pairs)  5.75 us
  transfers between devices with their start and end apart: 22, of which 6 were waited for; matrix products, arithmetic and copies ran while one was open for 0% of the time, Pallas kernels for 22%

profile of v6, /device:TPU:2, one launch (start us, length us, event | category | flops | bytes accessed | tf_op | source)
XLA Modules:
  0.0 84.2 jit_solution(15135797644179183985)
XLA Ops:
  0.6 0.1 pad_add_fusion.place
  0.7 0.0 copy-start
  0.7 2.1 %shard_map.103 = (bf16[224,512]{1,0:T(8,128)(2,1)S(1)}, f32[32,256]{1,0:T(8,128)S(1)}, s32[8,256]{1,0:T(8,128)S(1)}, s32[8,256]{1,0:T(8,128)S(1)}, bf16[192,256]...) custom-call(s32[2]{0:T(128)S(1)} %pad_add_fusion.place, bf16[192,256]{1,0:T(8,128)(2,1)} %feat.1, bf16[192,256]{1,0:T(8,128)(2,1)} %pre.1, ...), custom_call_target="tpu_custom_call" | custom-call | flops 4000000000 | bytes 10000 | tf_op jit(solution)/shard_map/pallas_call | solution.py:311
  2.8 0.0 copy-start.1
  2.8 2.2 %collective-permute-start.4 = (bf16[224,512]{1,0:T(8,128)(2,1)S(1)}, bf16[224,512]{1,0:T(8,128)(2,1)S(1)}, u32[]{:S(2)}, u32[]{:S(2)}) collective-permute-start(bf16[224,512]{1,0:T(8,128)(2,1)S(1)} %get-tuple-element.48.p0), channel_id=1, source_target_pairs={{0,2},{1,3},{2,0},{3,1},{4,6},{5,7},{6,4},{7,5},{8,10},{9,11},{10,... | collective-permute-start | bytes 688136 | tf_op jit(solution)/shard_map/ppermute | solution.py:352
  5.0 1.4 %collective-permute-start.5 = (bf16[224,512]{1,0:T(8,128)(2,1)S(1)}, bf16[224,512]{1,0:T(8,128)(2,1)S(1)}, u32[]{:S(2)}, u32[]{:S(2)}) collective-permute-start(bf16[224,512]{1,0:T(8,128)(2,1)S(1)} %get-tuple-element.48.p0), channel_id=1, source_target_pairs={{0,1},{1,0},{2,3},{3,2},{4,5},{5,4},{6,7},{7,6},{8,9},{9,8},{10,11... | collective-permute-start | bytes 688136 | tf_op jit(solution)/shard_map/ppermute | solution.py:352
  6.5 0.5 collective-permute-start.6
  7.0 0.0 copy-done
  7.0 3.0 %shard_map.104 = (f32[192,256]{1,0:T(8,128)S(1)}, bf16[96,256]{1,0:T(8,128)(2,1)S(1)}, bf16[96,256]{1,0:T(8,128)(2,1)S(1)}, bf16[64,256]{1,0:T(8,128)(2,1)S(1)}) custom-call(s32[2]{0:T(128)S(1)} %pad_add_fusion.place, f32[32,256]{1,0:T(8,128)S(1)} %get-tuple-element.38.nbt, bf16[192,256]{1,0:T(8,128)(2,1)S(1)} %get-tuple-element.39.grad, ...), custom_call_target="tpu_custom_call" | custom-call | flops 100000 | bytes 10000 | tf_op jit(solution)/shard_map/pallas_call | solution.py:311
  10.1 2.4 %collective-permute-start = (bf16[96,256]{1,0:T(8,128)(2,1)S(1)}, bf16[96,256]{1,0:T(8,128)(2,1)S(1)}, u32[]{:S(2)}, u32[]{:S(2)}) collective-permute-start(bf16[96,256]{1,0:T(8,128)(2,1)S(1)} %get-tuple-element.41), channel_id=1, source_target_pairs={{0,1},{1,0},{2,3},{3,2},{4,8},{5,9},{6,10},{7,11},{8,4},{9,5},{10,... | collective-permute-start | bytes 147464 | tf_op jit(solution)/shard_map/ppermute | solution.py:348
  12.4 0.0 collective-permute-start.1
  12.4 4.9 %collective-permute-done.m2 = bf16[96,256]{1,0:T(8,128)(2,1)S(1)} collective-permute-done((bf16[96,256]{1,0:T(8,128)(2,1)S(1)}, bf16[96,256]{1,0:T(8,128)(2,1)S(1)}, u32[]{:S(2)}, u32[]{:S(2)}) %collective-permute-start) | collective-permute-done | bytes 49184 | tf_op jit(solution)/shard_map/ppermute | solution.py:348
  17.3 0.0 collective-permute-done.1.m1
  17.3 0.6 shard_map.105
  17.8 0.6 collective-permute-start.2
  18.5 0.2 collective-permute-start.3
  18.6 0.0 collective-permute-done.4.p2
  18.6 0.0 collective-permute-done.5.p1
  18.6 0.0 collective-permute-done.6.p3
  18.6 1.1 %shard_map.106 = (bf16[768,256]{1,0:T(8,128)(2,1)S(1)}, bf16[768,256]{1,0:T(8,128)(2,1)S(1)}, bf16[4,64,512]{2,1,0:T(8,128)(2,1)S(1)}) custom-call(s32[2]{0:T(128)S(1)} %pad_add_fusion.place, bf16[224,512]{1,0:T(8,128)(2,1)S(1)} %get-tuple-element.48.p0, bf16[224,512]{1,0:T(8,128)(2,1)S(1)} %collective-permute-done.4.p2, ...), custom_call_target="tpu_custom_call" | custom-call | flops 100000 | bytes 10000 | tf_op jit(solution)/shard_map/pallas_call | solution.py:311
  19.7 2.0 %collective-permute-start.10 = (bf16[768,256]{1,0:T(8,128)(2,1)S(1)}, bf16[768,256]{1,0:T(8,128)(2,1)S(1)}, u32[]{:S(2)}, u32[]{:S(2)}) collective-permute-start(bf16[768,256]{1,0:T(8,128)(2,1)S(1)} %get-tuple-element.51), channel_id=1, source_target_pairs={{0,1},{1,0},{2,3},{3,2},{4,8},{5,9},{6,10},{7,11},{8,4},{9,5},{10,... | collective-permute-start | bytes 1179656 | tf_op jit(solution)/shard_map/ppermute | solution.py:348
  21.7 0.0 collective-permute-start.11
  21.7 0.3 collective-permute-done.2.n2
  22.0 0.5 collective-permute-done.3.n1
  22.6 0.9 %shard_map.107 = (bf16[192,256]{1,0:T(8,128)(2,1)S(1)}, bf16[192,512]{1,0:T(8,128)(2,1)S(1)}) custom-call(s32[2]{0:T(128)S(1)} %pad_add_fusion.place, f32[192,256]{1,0:T(8,128)S(1)} %get-tuple-element.40.late.own, bf16[96,256]{1,0:T(8,128)(2,1)S(1)} %collective-permute-done.m2, bf16[96,256]{1,0:T(8,128)(2,1)S(1)} %collective-permute-done.1.m1, ...), custom_call_target="tpu_custom_call" | custom-call | flops 100000 | bytes 10000 | tf_op jit(solution)/shard_map/pallas_call | solution.py:311
  23.5 1.0 %collective-permute-start.7 = (bf16[192,512]{1,0:T(8,128)(2,1)S(1)}, bf16[192,512]{1,0:T(8,128)(2,1)S(1)}, u32[]{:S(2)}, u32[]{:S(2)}) collective-permute-start(bf16[192,512]{1,0:T(8,128)(2,1)S(1)} %get-tuple-element.50.g0), channel_id=1, source_target_pairs={{0,2},{1,3},{2,0},{3,1},{4,6},{5,7},{6,4},{7,5},{8,10},{9,11},{10,... | collective-permute-start | bytes 589832 | tf_op jit(solution)/shard_map/ppermute | solution.py:352
  24.5 2.6 %collective-permute-start.8 = (bf16[192,512]{1,0:T(8,128)(2,1)S(1)}, bf16[192,512]{1,0:T(8,128)(2,1)S(1)}, u32[]{:S(2)}, u32[]{:S(2)}) collective-permute-start(bf16[192,512]{1,0:T(8,128)(2,1)S(1)} %get-tuple-element.50.g0), channel_id=1, source_target_pairs={{0,1},{1,0},{2,3},{3,2},{4,5},{5,4},{6,7},{7,6},{8,9},{9,8},{10,11... | collective-permute-start | bytes 589832 | tf_op jit(solution)/shard_map/ppermute | solution.py:352
  27.1 0.5 collective-permute-start.9
  27.7 0.0 copy-done.1
  27.7 3.0 %shard_map.108 = (f32[192,256]{1,0:T(8,128)S(1)}, bf16[96,256]{1,0:T(8,128)(2,1)S(1)}, bf16[96,256]{1,0:T(8,128)(2,1)S(1)}, bf16[64,256]{1,0:T(8,128)(2,1)S(1)}) custom-call(s32[2]{0:T(128)S(1)} %pad_add_fusion.place, f32[32,256]{1,0:T(8,128)S(1)} %get-tuple-element.38.nbt, bf16[192,256]{1,0:T(8,128)(2,1)S(1)} %get-tuple-element.53.grad, ...), custom_call_target="tpu_custom_call" | custom-call | flops 4000000000 | bytes 10000 | tf_op jit(solution)/shard_map/pallas_call | solution.py:311
  30.7 0.0 collective-permute-done.10.r2
  30.7 1.3 %collective-permute-start.12 = (bf16[96,256]{1,0:T(8,128)(2,1)S(1)}, bf16[96,256]{1,0:T(8,128)(2,1)S(1)}, u32[]{:S(2)}, u32[]{:S(2)}) collective-permute-start(bf16[96,256]{1,0:T(8,128)(2,1)S(1)} %get-tuple-element.58), channel_id=1, source_target_pairs={{0,1},{1,0},{2,3},{3,2},{4,8},{5,9},{6,10},{7,11},{8,4},{9,5},{10,... | collective-permute-start | bytes 147464 | tf_op jit(solution)/shard_map/ppermute | solution.py:348
  32.0 0.0 collective-permute-done.11.r1
  32.0 0.0 collective-permute-start.13
  32.0 5.2 %shard_map.109 = (bf16[768,1792]{1,0:T(8,128)(2,1)S(1)}, bf16[768,1792]{1,0:T(8,128)(2,1)S(1)}) custom-call(s32[2]{0:T(128)S(1)} %pad_add_fusion.place, bf16[224,512]{1,0:T(8,128)(2,1)S(1)} %get-tuple-element.48.p0, bf16[224,512]{1,0:T(8,128)(2,1)S(1)} %collective-permute-done.4.p2, bf16[224,512]{1,0:T(8,128)(2,1)S(1)} %collective-permute-done.5.p1, ...), custom_call_target="tpu_custom_call" | custom-call | flops 4000000000 | bytes 10000 | tf_op jit(solution)/shard_map/pallas_call | solution.py:311
  37.2 0.0 collective-permute-done.12.m2
  37.2 0.0 collective-permute-done.13.m1
  37.2 0.6 shard_map.110
  37.8 2.4 %collective-permute-start.16 = (bf16[96,256]{1,0:T(8,128)(2,1)S(1)}, bf16[96,256]{1,0:T(8,128)(2,1)S(1)}, u32[]{:S(2)}, u32[]{:S(2)}) collective-permute-start(bf16[96,256]{1,0:T(8,128)(2,1)S(1)} %get-tuple-element.65), channel_id=1, source_target_pairs={{0,4},{1,2},{2,1},{3,7},{4,0},{5,6},{6,5},{7,3},{8,12},{9,10},{10,... | collective-permute-start | bytes 147464 | tf_op jit(solution)/shard_map/ppermute | solution.py:348
  40.2 0.0 collective-permute-start.17
  40.2 0.0 collective-permute-done.7.g2
  40.2 0.0 collective-permute-done.8.g1
  40.2 0.0 collective-permute-done.9.g3
  40.2 1.7 %shard_map.111 = (f32[128,1792]{1,0:T(8,128)S(1)}, f32[128,1792]{1,0:T(8,128)S(1)}) custom-call(s32[2]{0:T(128)S(1)} %pad_add_fusion.place, bf16[192,512]{1,0:T(8,128)(2,1)S(1)} %get-tuple-element.50.g0, bf16[192,512]{1,0:T(8,128)(2,1)S(1)} %collective-permute-done.7.g2, bf16[192,512]{1,0:T(8,128)(2,1)S(1)} %collective-permute-done.8.g1, ...), custom_call_target="tpu_custom_call" | custom-call | flops 4000000000 | bytes 10000 | tf_op jit(solution)/shard_map/pallas_call | solution.py:311
  42.0 1.7 %shard_map.112 = (bf16[128,1792]{1,0:T(8,128)(2,1)S(1)}, bf16[128,1792]{1,0:T(8,128)(2,1)S(1)}) custom-call(s32[2]{0:T(128)S(1)} %pad_add_fusion.place, bf16[192,512]{1,0:T(8,128)(2,1)S(1)} %get-tuple-element.50.g0, bf16[192,512]{1,0:T(8,128)(2,1)S(1)} %collective-permute-done.7.g2, bf16[192,512]{1,0:T(8,128)(2,1)S(1)} %collective-permute-done.8.g1, ...), custom_call_target="tpu_custom_call" | custom-call | flops 100000 | bytes 10000 | tf_op jit(solution)/shard_map/pallas_call | solution.py:311
  43.7 0.3 collective-permute-start.14
  44.0 0.3 collective-permute-start.15
  44.3 0.0 collective-permute-done.16.n2
  44.3 0.0 collective-permute-done.17.n1
  44.3 1.0 %shard_map.113 = (bf16[128,256]{1,0:T(8,128)(2,1)S(1)}, bf16[128,256]{1,0:T(8,128)(2,1)S(1)}) custom-call(s32[2]{0:T(128)S(1)} %pad_add_fusion.place, f32[192,256]{1,0:T(8,128)S(1)} %get-tuple-element.54.late.own, bf16[96,256]{1,0:T(8,128)(2,1)S(1)} %collective-permute-done.12.m2, bf16[96,256]{1,0:T(8,128)(2,1)S(1)} %collective-permute-done.13.m1, ...), custom_call_target="tpu_custom_call" | custom-call | flops 20000000000 | bytes 10000 | tf_op jit(solution)/shard_map/pallas_call | solution.py:311
  45.3 0.4 collective-permute-start.18
  45.7 1.3 %collective-permute-done.18.rs = bf16[128,256]{1,0:T(8,128)(2,1)S(1)} collective-permute-done((bf16[128,256]{1,0:T(8,128)(2,1)S(1)}, bf16[128,256]{1,0:T(8,128)(2,1)S(1)}, u32[]{:S(2)}, u32[]{:S(2)}) %collective-permute-start.18) | collective-permute-done | bytes 65568 | tf_op jit(solution)/shard_map/ppermute | solution.py:352
  47.0 0.0 collective-permute-done.14.s1
  47.0 0.0 collective-permute-done.15.s2
  47.0 0.7 shard_map.114
  47.7 3.9 %collective-permute-start.19 = (bf16[64,2048]{1,0:T(8,128)(2,1)S(1)}, bf16[64,2048]{1,0:T(8,128)(2,1)S(1)}, u32[]{:S(2)}, u32[]{:S(2)}) collective-permute-start(bf16[64,2048]{1,0:T(8,128)(2,1)S(1)} %get-tuple-element.70), channel_id=1, source_target_pairs={{0,128},{4,132},{8,136},{12,140},{16,144},{20,148},{24,152},{28,15... | collective-permute-start | bytes 786440 | tf_op jit(solution)/shard_map/ppermute | solution.py:352
  51.7 1.0 %collective-permute-start.20 = (bf16[64,2048]{1,0:T(8,128)(2,1)S(1)}, bf16[64,2048]{1,0:T(8,128)(2,1)S(1)}, u32[]{:S(2)}, u32[]{:S(2)}) collective-permute-start(bf16[64,2048]{1,0:T(8,128)(2,1)S(1)} %get-tuple-element.71), channel_id=1, source_target_pairs={{0,64},{4,68},{8,72},{12,76},{16,80},{20,84},{24,88},{28,92},{32,9... | collective-permute-start | bytes 786440 | tf_op jit(solution)/shard_map/ppermute | solution.py:352
  52.6 0.1 collective-permute-start.21
  52.7 6.1 %collective-permute-done.19.a2 = bf16[64,2048]{1,0:T(8,128)(2,1)S(1)} collective-permute-done((bf16[64,2048]{1,0:T(8,128)(2,1)S(1)}, bf16[64,2048]{1,0:T(8,128)(2,1)S(1)}, u32[]{:S(2)}, u32[]{:S(2)}) %collective-permute-start.19) | collective-permute-done | bytes 262176 | tf_op jit(solution)/shard_map/ppermute | solution.py:352
  58.8 5.8 %collective-permute-done.20.a1 = bf16[64,2048]{1,0:T(8,128)(2,1)S(1)} collective-permute-done((bf16[64,2048]{1,0:T(8,128)(2,1)S(1)}, bf16[64,2048]{1,0:T(8,128)(2,1)S(1)}, u32[]{:S(2)}, u32[]{:S(2)}) %collective-permute-start.20) | collective-permute-done | bytes 262176 | tf_op jit(solution)/shard_map/ppermute | solution.py:352
  64.6 0.0 collective-permute-done.21.a3
  64.6 0.9 %shard_map.115 = bf16[64,2816]{1,0:T(8,128)(2,1)S(1)} custom-call(s32[2]{0:T(128)S(1)} %pad_add_fusion.place, bf16[64,2048]{1,0:T(8,128)(2,1)S(1)} %get-tuple-element.69.a0, bf16[64,2048]{1,0:T(8,128)(2,1)S(1)} %collective-permute-done.19.a2, bf16[64,2048]{1,0:T(8,128)(2,1)S(1)} %collective-permute-done.20.a1, bf16[64,2048]{1,0:T(8,128)(2,1)S(1)} %collective-permute-done.21.a3), custom_call_target="tpu_custom_call" | custom-call | flops 100000 | bytes 10000 | tf_op jit(solution)/shard_map/pallas_call | solution.py:311
  65.5 17.8 %all_to_all.5.refs_0_ = bf16[8,8,2816]{2,1,0:T(8,128)(2,1)S(1)} all-to-all(bf16[8,8,2816]{2,1,0:T(8,128)(2,1)S(1)} %bitcast.5), channel_id=1, replica_groups={{0,8,16,24,32,40,48,56},{4,12,20,28,36,44,52,60},{64,72,80,88,96,104,11..., dimensions={0} | all-to-all | bytes 720896 | tf_op jit(solution)/shard_map/all_to_all | solution.py:514
  83.3 0.8 shard_map.116
Async XLA Ops:
  0.7 6.3 %copy-start = (bf16[256,6912]{1,0:T(8,128)(2,1)S(1)}, bf16[256,6912]{1,0:T(8,128)(2,1)}, u32[]{:S(2)}) copy-start(bf16[256,6912]{1,0:T(8,128)(2,1)} %weight.2) | copy-start | bytes 10616836
  2.8 24.8 %copy-start.1 = (bf16[256,6912]{1,0:T(8,128)(2,1)S(1)}, bf16[256,6912]{1,0:T(8,128)(2,1)}, u32[]{:S(2)}) copy-start(bf16[256,6912]{1,0:T(8,128)(2,1)} %weight.3) | copy-start | bytes 10616836
  2.8 15.8 %collective-permute-start.4 = (bf16[224,512]{1,0:T(8,128)(2,1)S(1)}, bf16[224,512]{1,0:T(8,128)(2,1)S(1)}, u32[]{:S(2)}, u32[]{:S(2)}) collective-permute-start(bf16[224,512]{1,0:T(8,128)(2,1)S(1)} %get-tuple-element.48.p0), channel_id=1, source_target_pairs={{0,2},{1,3},{2,0},{3,1},{4,6},{5,7},{6,4},{7,5},{8,10},{9,11},{10,... | collective-permute-start | bytes 688136 | tf_op jit(solution)/shard_map/ppermute | solution.py:352
  5.0 13.6 %collective-permute-start.5 = (bf16[224,512]{1,0:T(8,128)(2,1)S(1)}, bf16[224,512]{1,0:T(8,128)(2,1)S(1)}, u32[]{:S(2)}, u32[]{:S(2)}) collective-permute-start(bf16[224,512]{1,0:T(8,128)(2,1)S(1)} %get-tuple-element.48.p0), channel_id=1, source_target_pairs={{0,1},{1,0},{2,3},{3,2},{4,5},{5,4},{6,7},{7,6},{8,9},{9,8},{10,11... | collective-permute-start | bytes 688136 | tf_op jit(solution)/shard_map/ppermute | solution.py:352
  6.5 12.2 %collective-permute-start.6 = (bf16[224,512]{1,0:T(8,128)(2,1)S(1)}, bf16[224,512]{1,0:T(8,128)(2,1)S(1)}, u32[]{:S(2)}, u32[]{:S(2)}) collective-permute-start(bf16[224,512]{1,0:T(8,128)(2,1)S(1)} %get-tuple-element.48.p0), channel_id=1, source_target_pairs={{0,3},{1,2},{2,1},{3,0},{4,7},{5,6},{6,5},{7,4},{8,11},{9,10},{10,... | collective-permute-start | bytes 688136 | tf_op jit(solution)/shard_map/ppermute | solution.py:352
  10.1 7.2 %collective-permute-start = (bf16[96,256]{1,0:T(8,128)(2,1)S(1)}, bf16[96,256]{1,0:T(8,128)(2,1)S(1)}, u32[]{:S(2)}, u32[]{:S(2)}) collective-permute-start(bf16[96,256]{1,0:T(8,128)(2,1)S(1)} %get-tuple-element.41), channel_id=1, source_target_pairs={{0,1},{1,0},{2,3},{3,2},{4,8},{5,9},{6,10},{7,11},{8,4},{9,5},{10,... | collective-permute-start | bytes 147464 | tf_op jit(solution)/shard_map/ppermute | solution.py:348
  12.4 4.9 %collective-permute-start.1 = (bf16[96,256]{1,0:T(8,128)(2,1)S(1)}, bf16[96,256]{1,0:T(8,128)(2,1)S(1)}, u32[]{:S(2)}, u32[]{:S(2)}) collective-permute-start(bf16[96,256]{1,0:T(8,128)(2,1)S(1)} %get-tuple-element.42), channel_id=1, source_target_pairs={{0,4},{1,5},{2,6},{3,7},{4,0},{5,1},{6,2},{7,3},{8,12},{9,13},{10,... | collective-permute-start | bytes 147464 | tf_op jit(solution)/shard_map/ppermute | solution.py:348
  17.8 4.2 %collective-permute-start.2 = (bf16[96,256]{1,0:T(8,128)(2,1)S(1)}, bf16[96,256]{1,0:T(8,128)(2,1)S(1)}, u32[]{:S(2)}, u32[]{:S(2)}) collective-permute-start(bf16[96,256]{1,0:T(8,128)(2,1)S(1)} %get-tuple-element.44), channel_id=1, source_target_pairs={{0,4},{1,2},{2,1},{3,7},{4,0},{5,6},{6,5},{7,3},{8,12},{9,10},{10,... | collective-permute-start | bytes 147464 | tf_op jit(solution)/shard_map/ppermute | solution.py:348
  18.5 4.1 %collective-permute-start.3 = (bf16[96,256]{1,0:T(8,128)(2,1)S(1)}, bf16[96,256]{1,0:T(8,128)(2,1)S(1)}, u32[]{:S(2)}, u32[]{:S(2)}) collective-permute-start(bf16[96,256]{1,0:T(8,128)(2,1)S(1)} %get-tuple-element.45.late), channel_id=1, source_target_pairs={{0,1},{1,0},{2,3},{3,2},{4,5},{5,4},{6,7},{7,6},{8,9},{9,8},{10,11... | collective-permute-start | bytes 147464 | tf_op jit(solution)/shard_map/ppermute | solution.py:348
  19.7 11.0 %collective-permute-start.10 = (bf16[768,256]{1,0:T(8,128)(2,1)S(1)}, bf16[768,256]{1,0:T(8,128)(2,1)S(1)}, u32[]{:S(2)}, u32[]{:S(2)}) collective-permute-start(bf16[768,256]{1,0:T(8,128)(2,1)S(1)} %get-tuple-element.51), channel_id=1, source_target_pairs={{0,1},{1,0},{2,3},{3,2},{4,8},{5,9},{6,10},{7,11},{8,4},{9,5},{10,... | collective-permute-start | bytes 1179656 | tf_op jit(solution)/shard_map/ppermute | solution.py:348
  21.7 10.3 %collective-permute-start.11 = (bf16[768,256]{1,0:T(8,128)(2,1)S(1)}, bf16[768,256]{1,0:T(8,128)(2,1)S(1)}, u32[]{:S(2)}, u32[]{:S(2)}) collective-permute-start(bf16[768,256]{1,0:T(8,128)(2,1)S(1)} %get-tuple-element.52), channel_id=1, source_target_pairs={{0,4},{1,5},{2,6},{3,7},{4,0},{5,1},{6,2},{7,3},{8,12},{9,13},{10,... | collective-permute-start | bytes 1179656 | tf_op jit(solution)/shard_map/ppermute | solution.py:348
  23.5 16.8 %collective-permute-start.7 = (bf16[192,512]{1,0:T(8,128)(2,1)S(1)}, bf16[192,512]{1,0:T(8,128)(2,1)S(1)}, u32[]{:S(2)}, u32[]{:S(2)}) collective-permute-start(bf16[192,512]{1,0:T(8,128)(2,1)S(1)} %get-tuple-element.50.g0), channel_id=1, source_target_pairs={{0,2},{1,3},{2,0},{3,1},{4,6},{5,7},{6,4},{7,5},{8,10},{9,11},{10,... | collective-permute-start | bytes 589832 | tf_op jit(solution)/shard_map/ppermute | solution.py:352
  24.5 15.7 %collective-permute-start.8 = (bf16[192,512]{1,0:T(8,128)(2,1)S(1)}, bf16[192,512]{1,0:T(8,128)(2,1)S(1)}, u32[]{:S(2)}, u32[]{:S(2)}) collective-permute-start(bf16[192,512]{1,0:T(8,128)(2,1)S(1)} %get-tuple-element.50.g0), channel_id=1, source_target_pairs={{0,1},{1,0},{2,3},{3,2},{4,5},{5,4},{6,7},{7,6},{8,9},{9,8},{10,11... | collective-permute-start | bytes 589832 | tf_op jit(solution)/shard_map/ppermute | solution.py:352
  27.1 13.1 %collective-permute-start.9 = (bf16[192,512]{1,0:T(8,128)(2,1)S(1)}, bf16[192,512]{1,0:T(8,128)(2,1)S(1)}, u32[]{:S(2)}, u32[]{:S(2)}) collective-permute-start(bf16[192,512]{1,0:T(8,128)(2,1)S(1)} %get-tuple-element.50.g0), channel_id=1, source_target_pairs={{0,3},{1,2},{2,1},{3,0},{4,7},{5,6},{6,5},{7,4},{8,11},{9,10},{10,... | collective-permute-start | bytes 589832 | tf_op jit(solution)/shard_map/ppermute | solution.py:352
  30.7 6.5 %collective-permute-start.12 = (bf16[96,256]{1,0:T(8,128)(2,1)S(1)}, bf16[96,256]{1,0:T(8,128)(2,1)S(1)}, u32[]{:S(2)}, u32[]{:S(2)}) collective-permute-start(bf16[96,256]{1,0:T(8,128)(2,1)S(1)} %get-tuple-element.58), channel_id=1, source_target_pairs={{0,1},{1,0},{2,3},{3,2},{4,8},{5,9},{6,10},{7,11},{8,4},{9,5},{10,... | collective-permute-start | bytes 147464 | tf_op jit(solution)/shard_map/ppermute | solution.py:348
  32.0 5.2 %collective-permute-start.13 = (bf16[96,256]{1,0:T(8,128)(2,1)S(1)}, bf16[96,256]{1,0:T(8,128)(2,1)S(1)}, u32[]{:S(2)}, u32[]{:S(2)}) collective-permute-start(bf16[96,256]{1,0:T(8,128)(2,1)S(1)} %get-tuple-element.59), channel_id=1, source_target_pairs={{0,4},{1,5},{2,6},{3,7},{4,0},{5,1},{6,2},{7,3},{8,12},{9,13},{10,... | collective-permute-start | bytes 147464 | tf_op jit(solution)/shard_map/ppermute | solution.py:348
  37.8 6.5 %collective-permute-start.16 = (bf16[96,256]{1,0:T(8,128)(2,1)S(1)}, bf16[96,256]{1,0:T(8,128)(2,1)S(1)}, u32[]{:S(2)}, u32[]{:S(2)}) collective-permute-start(bf16[96,256]{1,0:T(8,128)(2,1)S(1)} %get-tuple-element.65), channel_id=1, source_target_pairs={{0,4},{1,2},{2,1},{3,7},{4,0},{5,6},{6,5},{7,3},{8,12},{9,10},{10,... | collective-permute-start | bytes 147464 | tf_op jit(solution)/shard_map/ppermute | solution.py:348
  40.2 4.1 %collective-permute-start.17 = (bf16[96,256]{1,0:T(8,128)(2,1)S(1)}, bf16[96,256]{1,0:T(8,128)(2,1)S(1)}, u32[]{:S(2)}, u32[]{:S(2)}) collective-permute-start(bf16[96,256]{1,0:T(8,128)(2,1)S(1)} %get-tuple-element.60.late), channel_id=1, source_target_pairs={{0,1},{1,0},{2,3},{3,2},{4,5},{5,4},{6,7},{7,6},{8,9},{9,8},{10,11... | collective-permute-start | bytes 147464 | tf_op jit(solution)/shard_map/ppermute | solution.py:348
  43.7 3.3 %collective-permute-start.14 = (bf16[128,1792]{1,0:T(8,128)(2,1)S(1)}, bf16[128,1792]{1,0:T(8,128)(2,1)S(1)}, u32[]{:S(2)}, u32[]{:S(2)}) collective-permute-start(bf16[128,1792]{1,0:T(8,128)(2,1)S(1)} %get-tuple-element.63), channel_id=1, source_target_pairs={{0,4},{4,0},{8,12},{12,8},{16,20},{20,16},{24,28},{28,24},{32,36},... | collective-permute-start | bytes 1376264 | tf_op jit(solution)/shard_map/ppermute | solution.py:352
  44.0 3.0 %collective-permute-start.15 = (f32[128,1792]{1,0:T(8,128)S(1)}, f32[128,1792]{1,0:T(8,128)S(1)}, u32[]{:S(2)}, u32[]{:S(2)}) collective-permute-start(f32[128,1792]{1,0:T(8,128)S(1)} %get-tuple-element.64), channel_id=1, source_target_pairs={{0,4},{4,0},{8,12},{12,8},{16,20},{20,16},{24,28},{28,24},{32,36},... | collective-permute-start | bytes 2752520 | tf_op jit(solution)/shard_map/ppermute | solution.py:352
  45.3 1.7 %collective-permute-start.18 = (bf16[128,256]{1,0:T(8,128)(2,1)S(1)}, bf16[128,256]{1,0:T(8,128)(2,1)S(1)}, u32[]{:S(2)}, u32[]{:S(2)}) collective-permute-start(bf16[128,256]{1,0:T(8,128)(2,1)S(1)} %get-tuple-element.68), channel_id=1, source_target_pairs={{0,4},{4,0},{8,12},{12,8},{16,20},{20,16},{24,28},{28,24},{32,36},... | collective-permute-start | bytes 196616 | tf_op jit(solution)/shard_map/ppermute | solution.py:352
  47.7 11.1 %collective-permute-start.19 = (bf16[64,2048]{1,0:T(8,128)(2,1)S(1)}, bf16[64,2048]{1,0:T(8,128)(2,1)S(1)}, u32[]{:S(2)}, u32[]{:S(2)}) collective-permute-start(bf16[64,2048]{1,0:T(8,128)(2,1)S(1)} %get-tuple-element.70), channel_id=1, source_target_pairs={{0,128},{4,132},{8,136},{12,140},{16,144},{20,148},{24,152},{28,15... | collective-permute-start | bytes 786440 | tf_op jit(solution)/shard_map/ppermute | solution.py:352
  51.7 12.9 %collective-permute-start.20 = (bf16[64,2048]{1,0:T(8,128)(2,1)S(1)}, bf16[64,2048]{1,0:T(8,128)(2,1)S(1)}, u32[]{:S(2)}, u32[]{:S(2)}) collective-permute-start(bf16[64,2048]{1,0:T(8,128)(2,1)S(1)} %get-tuple-element.71), channel_id=1, source_target_pairs={{0,64},{4,68},{8,72},{12,76},{16,80},{20,84},{24,88},{28,92},{32,9... | collective-permute-start | bytes 786440 | tf_op jit(solution)/shard_map/ppermute | solution.py:352
  52.6 12.0 %collective-permute-start.21 = (bf16[64,2048]{1,0:T(8,128)(2,1)S(1)}, bf16[64,2048]{1,0:T(8,128)(2,1)S(1)}, u32[]{:S(2)}, u32[]{:S(2)}) collective-permute-start(bf16[64,2048]{1,0:T(8,128)(2,1)S(1)} %get-tuple-element.72), channel_id=1, source_target_pairs={{0,192},{4,196},{8,200},{12,204},{16,208},{20,212},{24,216},{28,22... | collective-permute-start | bytes 786440 | tf_op jit(solution)/shard_map/ppermute | solution.py:352

commit v7 on v6

--- a/solution.py
+++ b/solution.py
@@ -231,68 +231,81 @@
             sel[part : part + 1, :] = ids[pl.ds(first_k + part, 1), :]
         table = jnp.transpose(sel[...])[:, 0:8].astype(jnp.int32)
         extended = ext[...]
-        previous = None
-        for part in range(8):
-            match = onehot(iota((S, EXT), 1) == table[0:S, part : part + 1])
-            block = mm(match, extended).astype(BF)
-            if part:
-                merged = jnp.where(early, previous, block)
-                at = (part - 1) * C
-                cols_one[turn * S : (turn + 1) * S, at : at + C] = merged[:, 0:C]
-                cols_two[turn * S : (turn + 1) * S, at : at + C] = merged[:, C : 2 * C]
-            previous = block
-
-
-def weight_kernel(lanes, place, g0, g2, g1, g3, cols, late, keep, send, gt):
+        match = [
+            onehot(iota((S, EXT), 1) == table[0:S, part : part + 1]) for part in range(8)
+        ]
+        found = mm(jnp.concatenate(match, axis=0), extended).astype(BF)
+        for part in range(7):
+            merged = jnp.where(
+                early, found[part * S : (part + 1) * S], found[(part + 1) * S : (part + 2) * S]
+            )
+            lanes = slice(part * C, (part + 1) * C)
+            cols_one[turn * S : (turn + 1) * S, lanes] = merged[:, 0:C]
+            cols_two[turn * S : (turn + 1) * S, lanes] = merged[:, C : 2 * C]
+
+
+def weight_kernel(lanes, place, g0, g2, g1, g3, cols, t2, t1, keep, send, gt):
     for turn, grad in enumerate((g0, g1, g2, g3)):
         gt[:, turn * S : (turn + 1) * S] = jnp.transpose(grad[:, lanes].astype(F32)).astype(BF)
     mine = pl.multiple_of((place[0] % 2) * 128, 128)
     other = pl.multiple_of(128 - mine, 128)
-    for out, at in ((keep, mine), (send, other)):
-        left = gt[pl.ds(at, 128), :]
-        for part in range(7):
-            lanes = slice(part * C, (part + 1) * C)
-            out[:, lanes] = mm(left, cols[:, lanes]).astype(out.dtype)
-
-
-def merge_kernel(place, k1, s1, k2, s2, rk, rs, *outs):
-    first = place[0] % 2 == 0
+    left = jnp.concatenate([gt[pl.ds(mine, 128), :], gt[pl.ds(other, 128), :]], axis=0)
+    for part in range(7):
+        lanes = slice(part * C, (part + 1) * C)
+        block = mm(left, cols[:, lanes])
+        keep[:, lanes] = block[0:128].astype(keep.dtype)
+        send[:, lanes] = block[128:256].astype(send.dtype)
+
+
+def merge_kernel(place, k1, s1, k2, s2, *outs):
     line = place[0] // 16
     for turn, out in enumerate(outs):
         rows = pl.ds(pl.multiple_of(32 * (line ^ turn), 32), 32)
         for at, (keep, come) in ((0, (k1, s1)), (32, (k2, s2))):
             total = keep[rows, :].astype(F32) + come[rows, :].astype(F32)
-            out[at : at + 32, 0 : 7 * C] = total.astype(BF)
+            out[at : at + 32, :] = total.astype(BF)
+
+
+def sort_kernel(place, rk, rs, *outs):
+    first = place[0] % 2 == 0
+    line = place[0] // 16
+    for turn, out in enumerate(outs):
+        rows = pl.ds(pl.multiple_of(32 * (line ^ turn), 32), 32)
         mine, other = rk[rows, :], rs[rows, :]
-        out[0:32, 7 * C : 8 * C] = jnp.where(first, mine, other)
-        out[32:64, 7 * C : 8 * C] = jnp.where(first, other, mine)
-
-
-def line_kernel(place, a0, a2, a1, a3, out):
+        out[0:32, :] = jnp.where(first, mine, other)
+        out[32:64, :] = jnp.where(first, other, mine)
+
+
+def line_kernel(place, a0, a2, a1, a3, b0, b2, b1, b3, out):
     line = place[0] // 16
     to, at = iota((64, 64), 0), iota((64, 64), 1)
     order = onehot(at == 32 * ((to % 8) // 4) + 4 * (to // 8) + to % 4)
-    parts = (a0, a1, a2, a3)
     for n in range(7):
         lanes = slice(n * C, (n + 1) * C)
         total = a0[:, lanes].astype(F32)
-        for part in parts[1:]:
+        for part in (a1, a2, a3):
             total = total + part[:, lanes].astype(F32)
         out[:, lanes] = mm(order, total.astype(BF)).astype(BF)
-    for turn, part in enumerate(parts):
-        to = pl.multiple_of(7 * C + (line ^ turn) * C, C)
-        out[:, pl.ds(to, C)] = mm(order, part[:, 7 * C : 8 * C]).astype(BF)
+    for n in range(3):
+        index = 8 * n + to % 8
+        total = jnp.zeros((64, C), F32)
+        for turn, part in enumerate((b0, b1, b2, b3)):
+            row = 32 * ((index % 6) // 3) + 4 * (to // 8) + index % 3
+            total = total + mm(onehot((index // 6 == (line ^ turn)) & (at == row)), part[...])
+        out[:, (7 + n) * C : (8 + n) * C] = total.astype(BF)
 
 
 def final_kernel(scale, arrived, rows, one, two):
     total = jnp.sum(arrived[:, :, 0 : 7 * C].astype(F32), axis=0) * scale
     one[...] = total[0:4, 0:QW]
     two[...] = total[4:8, 0:QW]
-    to, at = iota((48, 64), 0), iota((48, 64), 1)
-    spot = onehot((at // 8 == to // 6) & (at % 8 == 4 * ((to % 6) // 3) + to % 3))
-    for line in range(4):
-        piece = arrived[:, :, (7 + line) * C : (8 + line) * C].reshape(64, C)
-        rows[48 * line : 48 * line + 48, :] = mm(spot, piece).astype(BF)
+    to, at = iota((S, 64), 0), iota((S, 64), 1)
+    value = jnp.zeros((S, C), F32)
+    for n in range(3):
+        spot = (at // 8 == (to // 6) % 8) & (8 * n + at % 8 == 6 * (to // 48) + to % 6)
+        piece = arrived[:, :, (7 + n) * C : (8 + n) * C].reshape(64, C)
+        value = value + mm(onehot(spot), piece)
+    rows[...] = value.astype(BF)
 
 
 def sds(shape, dtype):
@@ -360,9 +373,9 @@
     return swap(m2, "gx", 2), swap(m1, "gx", 1)
 
 
-def halo_columns(place, loc, m2, m1, late):
+def halo_columns(place, loc, m2, m1, late, flops=10**5):
     edge = sds((96, C), BF)
-    n2, n1 = call(pass_kernel, (edge, edge), place, loc, m2, m1, late, late=1)
+    n2, n1 = call(pass_kernel, (edge, edge), place, loc, m2, m1, late, late=1, flops=flops)
     return n1, swap(n2, "gy", 2), swap(n1, "gy", 1)
 
 
@@ -456,9 +469,8 @@
         late=1,
         flops=4 * 10**9,
     )
-    passed, n2, n1 = halo_columns(place, loc, m2, m1, cols_two)
-
-    def halves(which, cols, kind, late, flops):
+
+    def halves(which, cols, kind, flops, *late):
         lanes = slice(which * C, (which + 1) * C)
         half = sds((128, wide), kind)
         return call(
@@ -467,15 +479,21 @@
             place,
             *grads,
             cols,
-            late,
+            *late,
             scratch=[pltpu.VMEM((C, 4 * S), BF)],
-            late=1,
+            late=2,
             flops=flops,
         )
 
-    keep_two, send_two = halves(0, cols_two, F32, passed, 4 * 10**9)
+    keep_two, send_two = halves(0, cols_two, F32, 4 * 10**9, m2, m1)
     come_two = cross(send_two, "gx", 1)
-    keep_one, send_one = halves(1, cols_one, BF, keep_two, 10**5)
+    keep_one, send_one = halves(1, cols_one, BF, 10**5, keep_two, keep_two)
+    come_one = cross(send_one, "gx", 1)
+    chunks = call(
+        merge_kernel, (sds((64, wide), BF),) * 4, place, keep_one, come_one, keep_two, come_two
+    )
+    sums = [chunks[0]] + [cross(chunks[d], "gx", 16 * d) for d in (2, 1, 3)]
+    n2, n1 = halo_columns(place, loc, m2, m1, chunks[0], 2 * 10**10)[1:]
     some = sds((128, C), BF)
     rows_keep, rows_send = call(
         rows_kernel,
@@ -489,30 +507,17 @@
         hrow,
         grad,
         srow,
-        keep_one,
+        n1,
         scratch=[back],
         late=1,
-        flops=2 * 10**10,
     )
     rows_come = cross(rows_send, "gx", 1)
-    come_one = cross(send_one, "gx", 1)
-    chunk = sds((64, 8 * C), BF)
-    chunks = call(
-        merge_kernel,
-        (chunk,) * 4,
-        place,
-        keep_one,
-        come_one,
-        keep_two,
-        come_two,
-        rows_keep,
-        rows_come,
-    )
-    chunks = [chunks[0]] + [cross(chunks[d], "gx", 16 * d) for d in (2, 1, 3)]
-    summed = call(line_kernel, sds((64, 11 * C), BF), place, *chunks)
+    sorts = call(sort_kernel, (sds((64, C), BF),) * 4, place, rows_keep, rows_come)
+    rows = [sorts[0]] + [cross(sorts[d], "gx", 16 * d) for d in (2, 1, 3)]
+    summed = call(line_kernel, sds((64, 10 * C), BF), place, *sums, *rows)
     groups = [[16 * y + 2 * z + e for z in range(8)] for y in range(4) for e in range(2)]
     collected = lax.all_to_all(
-        summed.reshape(8, 8, 11 * C),
+        summed.reshape(8, 8, 10 * C),
         "gx",
         split_axis=0,
         concat_axis=0,

time: 85.2 us -> 86.3 us (1.013); the launches traced: 84.2 us -> 86.2 us
  starting transfers between devices: 23.2 us -> 29.8 us
  waiting for transfers between devices: 19 us -> 16 us
  blocking collectives: 17.8 us -> 15.5 us
    ppermute x12 -> x15, starting transfers between devices: 14.3 us -> 21.7 us  [cross(): lax.ppermute(value, axis, [(n, n ^ mask) for n in range(lax.axis_size(axi...]
    ppermute x12 -> x15, waiting for transfers between devices: 13.3 us -> 6.55 us  [cross(): lax.ppermute(value, axis, [(n, n ^ mask) for n in range(lax.axis_size(axi...]
    ppermute x10, waiting for transfers between devices: 5.75 us -> 9.41 us  [swap(): return lax.ppermute(value, ('gx', 'gy'), pairs)]
    all_to_all x1, blocking collectives: 17.8 us -> 15.5 us  [body(): lax.all_to_all(summed.reshape(8, 8, 10 * C), 'gx', split_axis=0, concat_a...]
    pallas_call x14 -> x15, Pallas kernels: 23.3 us -> 24 us  [call(): pl.pallas_call(kernel, out_shape=outs, in_specs=specs, out_specs=jax.tree...]
  transfers between devices with their start and end apart: 22 -> 25, of which waited for: 6 -> 9; matrix products, arithmetic and copies ran while one was open for 0% -> 0% of each run, Pallas kernels for 22% -> 20%
where the time goes in v7:
time: 86.3 us; the launch traced here: 86.2 us
  starting transfers between devices  29.8 us (35%)
  Pallas kernels  24 us (28%)
  waiting for transfers between devices  16 us (19%)
  blocking collectives  15.5 us (18%)
    pallas_call x15, Pallas kernels, call(): pl.pallas_call(kernel, out_shape=outs, in_specs=specs, out_specs=jax.tree...  24 us
    ppermute x15, starting transfers between devices, cross(): lax.ppermute(value, axis, [(n, n ^ mask) for n in range(lax.axis_size(axi...  21.7 us
    all_to_all x1, blocking collectives, body(): lax.all_to_all(summed.reshape(8, 8, 10 * C), 'gx', split_axis=0, concat_a...  15.5 us
    ppermute x10, waiting for transfers between devices, swap(): return lax.ppermute(value, ('gx', 'gy'), pairs)  9.41 us
    ppermute x10, starting transfers between devices, swap(): return lax.ppermute(value, ('gx', 'gy'), pairs)  8.1 us
    ppermute x15, waiting for transfers between devices, cross(): lax.ppermute(value, axis, [(n, n ^ mask) for n in range(lax.axis_size(axi...  6.55 us
  transfers between devices with their start and end apart: 25, of which 9 were waited for; matrix products, arithmetic and copies ran while one was open for 0% of the time, Pallas kernels for 20%

profile of v7, /device:TPU:2, one launch (start us, length us, event | category | flops | bytes accessed | tf_op | source)
XLA Modules:
  0.0 86.2 jit_solution(873080495920452172)
XLA Ops:
  0.6 0.1 pad_add_fusion.place
  0.7 2.1 %shard_map.103 = (bf16[224,512]{1,0:T(8,128)(2,1)S(1)}, f32[32,256]{1,0:T(8,128)S(1)}, s32[8,256]{1,0:T(8,128)S(1)}, s32[8,256]{1,0:T(8,128)S(1)}, bf16[192,256]...) custom-call(s32[2]{0:T(128)S(1)} %pad_add_fusion.place, bf16[192,256]{1,0:T(8,128)(2,1)} %feat.1, bf16[192,256]{1,0:T(8,128)(2,1)} %pre.1, ...), custom_call_target="tpu_custom_call" | custom-call | flops 4000000000 | bytes 10000 | tf_op jit(solution)/shard_map/pallas_call | solution.py:324
  2.8 0.0 copy-start.1
  2.8 2.2 %collective-permute-start.4 = (bf16[224,512]{1,0:T(8,128)(2,1)S(1)}, bf16[224,512]{1,0:T(8,128)(2,1)S(1)}, u32[]{:S(2)}, u32[]{:S(2)}) collective-permute-start(bf16[224,512]{1,0:T(8,128)(2,1)S(1)} %get-tuple-element.52.p0), channel_id=1, source_target_pairs={{0,2},{1,3},{2,0},{3,1},{4,6},{5,7},{6,4},{7,5},{8,10},{9,11},{10,... | collective-permute-start | bytes 688136 | tf_op jit(solution)/shard_map/ppermute | solution.py:365
  5.0 1.4 %collective-permute-start.5 = (bf16[224,512]{1,0:T(8,128)(2,1)S(1)}, bf16[224,512]{1,0:T(8,128)(2,1)S(1)}, u32[]{:S(2)}, u32[]{:S(2)}) collective-permute-start(bf16[224,512]{1,0:T(8,128)(2,1)S(1)} %get-tuple-element.52.p0), channel_id=1, source_target_pairs={{0,1},{1,0},{2,3},{3,2},{4,5},{5,4},{6,7},{7,6},{8,9},{9,8},{10,11... | collective-permute-start | bytes 688136 | tf_op jit(solution)/shard_map/ppermute | solution.py:365
  6.5 0.5 collective-permute-start.6
  7.0 3.0 %shard_map.104 = (f32[192,256]{1,0:T(8,128)S(1)}, bf16[96,256]{1,0:T(8,128)(2,1)S(1)}, bf16[96,256]{1,0:T(8,128)(2,1)S(1)}, bf16[64,256]{1,0:T(8,128)(2,1)S(1)}) custom-call(s32[2]{0:T(128)S(1)} %pad_add_fusion.place, f32[32,256]{1,0:T(8,128)S(1)} %get-tuple-element.42.nbt, bf16[192,256]{1,0:T(8,128)(2,1)S(1)} %get-tuple-element.43.grad, ...), custom_call_target="tpu_custom_call" | custom-call | flops 100000 | bytes 10000 | tf_op jit(solution)/shard_map/pallas_call | solution.py:324
  10.1 2.4 %collective-permute-start = (bf16[96,256]{1,0:T(8,128)(2,1)S(1)}, bf16[96,256]{1,0:T(8,128)(2,1)S(1)}, u32[]{:S(2)}, u32[]{:S(2)}) collective-permute-start(bf16[96,256]{1,0:T(8,128)(2,1)S(1)} %get-tuple-element.45), channel_id=1, source_target_pairs={{0,1},{1,0},{2,3},{3,2},{4,8},{5,9},{6,10},{7,11},{8,4},{9,5},{10,... | collective-permute-start | bytes 147464 | tf_op jit(solution)/shard_map/ppermute | solution.py:361
  12.4 0.0 collective-permute-start.1
  12.4 4.9 %collective-permute-done.m2 = bf16[96,256]{1,0:T(8,128)(2,1)S(1)} collective-permute-done((bf16[96,256]{1,0:T(8,128)(2,1)S(1)}, bf16[96,256]{1,0:T(8,128)(2,1)S(1)}, u32[]{:S(2)}, u32[]{:S(2)}) %collective-permute-start) | collective-permute-done | bytes 49184 | tf_op jit(solution)/shard_map/ppermute | solution.py:361
  17.3 0.0 collective-permute-done.1.m1
  17.3 0.6 shard_map.105
  17.8 0.6 collective-permute-start.2
  18.5 0.2 collective-permute-start.3
  18.6 0.0 collective-permute-done.4.p2
  18.6 0.0 collective-permute-done.5.p1
  18.6 0.0 collective-permute-done.6.p3
  18.6 1.1 %shard_map.106 = (bf16[768,256]{1,0:T(8,128)(2,1)S(1)}, bf16[768,256]{1,0:T(8,128)(2,1)S(1)}, bf16[4,64,512]{2,1,0:T(8,128)(2,1)S(1)}) custom-call(s32[2]{0:T(128)S(1)} %pad_add_fusion.place, bf16[224,512]{1,0:T(8,128)(2,1)S(1)} %get-tuple-element.52.p0, bf16[224,512]{1,0:T(8,128)(2,1)S(1)} %collective-permute-done.4.p2, ...), custom_call_target="tpu_custom_call" | custom-call | flops 100000 | bytes 10000 | tf_op jit(solution)/shard_map/pallas_call | solution.py:324
  19.7 2.0 %collective-permute-start.10 = (bf16[768,256]{1,0:T(8,128)(2,1)S(1)}, bf16[768,256]{1,0:T(8,128)(2,1)S(1)}, u32[]{:S(2)}, u32[]{:S(2)}) collective-permute-start(bf16[768,256]{1,0:T(8,128)(2,1)S(1)} %get-tuple-element.55), channel_id=1, source_target_pairs={{0,1},{1,0},{2,3},{3,2},{4,8},{5,9},{6,10},{7,11},{8,4},{9,5},{10,... | collective-permute-start | bytes 1179656 | tf_op jit(solution)/shard_map/ppermute | solution.py:361
  21.7 0.0 collective-permute-start.11
  21.7 0.3 collective-permute-done.2.n2
  22.0 0.5 collective-permute-done.3.n1
  22.6 0.9 %shard_map.107 = (bf16[192,256]{1,0:T(8,128)(2,1)S(1)}, bf16[192,512]{1,0:T(8,128)(2,1)S(1)}) custom-call(s32[2]{0:T(128)S(1)} %pad_add_fusion.place, f32[192,256]{1,0:T(8,128)S(1)} %get-tuple-element.44.late.own, bf16[96,256]{1,0:T(8,128)(2,1)S(1)} %collective-permute-done.m2, bf16[96,256]{1,0:T(8,128)(2,1)S(1)} %collective-permute-done.1.m1, ...), custom_call_target="tpu_custom_call" | custom-call | flops 100000 | bytes 10000 | tf_op jit(solution)/shard_map/pallas_call | solution.py:324
  23.5 1.0 %collective-permute-start.7 = (bf16[192,512]{1,0:T(8,128)(2,1)S(1)}, bf16[192,512]{1,0:T(8,128)(2,1)S(1)}, u32[]{:S(2)}, u32[]{:S(2)}) collective-permute-start(bf16[192,512]{1,0:T(8,128)(2,1)S(1)} %get-tuple-element.54.g0), channel_id=1, source_target_pairs={{0,2},{1,3},{2,0},{3,1},{4,6},{5,7},{6,4},{7,5},{8,10},{9,11},{10,... | collective-permute-start | bytes 589832 | tf_op jit(solution)/shard_map/ppermute | solution.py:365
  24.5 2.6 %collective-permute-start.8 = (bf16[192,512]{1,0:T(8,128)(2,1)S(1)}, bf16[192,512]{1,0:T(8,128)(2,1)S(1)}, u32[]{:S(2)}, u32[]{:S(2)}) collective-permute-start(bf16[192,512]{1,0:T(8,128)(2,1)S(1)} %get-tuple-element.54.g0), channel_id=1, source_target_pairs={{0,1},{1,0},{2,3},{3,2},{4,5},{5,4},{6,7},{7,6},{8,9},{9,8},{10,11... | collective-permute-start | bytes 589832 | tf_op jit(solution)/shard_map/ppermute | solution.py:365
  27.1 0.5 collective-permute-start.9
  27.7 3.0 %shard_map.108 = (f32[192,256]{1,0:T(8,128)S(1)}, bf16[96,256]{1,0:T(8,128)(2,1)S(1)}, bf16[96,256]{1,0:T(8,128)(2,1)S(1)}, bf16[64,256]{1,0:T(8,128)(2,1)S(1)}) custom-call(s32[2]{0:T(128)S(1)} %pad_add_fusion.place, f32[32,256]{1,0:T(8,128)S(1)} %get-tuple-element.42.nbt, bf16[192,256]{1,0:T(8,128)(2,1)S(1)} %get-tuple-element.57.grad, ...), custom_call_target="tpu_custom_call" | custom-call | flops 4000000000 | bytes 10000 | tf_op jit(solution)/shard_map/pallas_call | solution.py:324
  30.7 0.0 collective-permute-done.10.r2
  30.7 1.3 %collective-permute-start.12 = (bf16[96,256]{1,0:T(8,128)(2,1)S(1)}, bf16[96,256]{1,0:T(8,128)(2,1)S(1)}, u32[]{:S(2)}, u32[]{:S(2)}) collective-permute-start(bf16[96,256]{1,0:T(8,128)(2,1)S(1)} %get-tuple-element.61), channel_id=1, source_target_pairs={{0,1},{1,0},{2,3},{3,2},{4,8},{5,9},{6,10},{7,11},{8,4},{9,5},{10,... | collective-permute-start | bytes 147464 | tf_op jit(solution)/shard_map/ppermute | solution.py:361
  32.0 0.0 collective-permute-done.11.r1
  32.0 5.1 %shard_map.109 = (bf16[768,1792]{1,0:T(8,128)(2,1)S(1)}, bf16[768,1792]{1,0:T(8,128)(2,1)S(1)}) custom-call(s32[2]{0:T(128)S(1)} %pad_add_fusion.place, bf16[224,512]{1,0:T(8,128)(2,1)S(1)} %get-tuple-element.52.p0, bf16[224,512]{1,0:T(8,128)(2,1)S(1)} %collective-permute-done.4.p2, bf16[224,512]{1,0:T(8,128)(2,1)S(1)} %collective-permute-done.5.p1, ...), custom_call_target="tpu_custom_call" | custom-call | flops 4000000000 | bytes 10000 | tf_op jit(solution)/shard_map/pallas_call | solution.py:324
  37.2 0.0 collective-permute-done.12.t2.m2
  37.2 0.0 collective-permute-done.13.t1.m1
  37.2 0.0 collective-permute-done.9.g3
  37.2 1.7 %shard_map.110 = (f32[128,1792]{1,0:T(8,128)S(1)}, f32[128,1792]{1,0:T(8,128)S(1)}) custom-call(s32[2]{0:T(128)S(1)} %pad_add_fusion.place, bf16[192,512]{1,0:T(8,128)(2,1)S(1)} %get-tuple-element.54.g0, bf16[192,512]{1,0:T(8,128)(2,1)S(1)} %collective-permute-done.7.g2, bf16[192,512]{1,0:T(8,128)(2,1)S(1)} %collective-permute-done.8.g1, ...), custom_call_target="tpu_custom_call" | custom-call | flops 4000000000 | bytes 10000 | tf_op jit(solution)/shard_map/pallas_call | solution.py:324
  38.9 0.6 collective-permute-start.15
  39.5 1.7 %shard_map.111 = (bf16[128,1792]{1,0:T(8,128)(2,1)S(1)}, bf16[128,1792]{1,0:T(8,128)(2,1)S(1)}) custom-call(s32[2]{0:T(128)S(1)} %pad_add_fusion.place, bf16[192,512]{1,0:T(8,128)(2,1)S(1)} %get-tuple-element.54.g0, bf16[192,512]{1,0:T(8,128)(2,1)S(1)} %collective-permute-done.7.g2, bf16[192,512]{1,0:T(8,128)(2,1)S(1)} %collective-permute-done.8.g1, ...), custom_call_target="tpu_custom_call" | custom-call | flops 100000 | bytes 10000 | tf_op jit(solution)/shard_map/pallas_call | solution.py:324
  41.2 0.1 collective-permute-start.14
  41.3 1.8 %collective-permute-done.14.s1 = bf16[128,1792]{1,0:T(8,128)(2,1)S(1)} collective-permute-done((bf16[128,1792]{1,0:T(8,128)(2,1)S(1)}, bf16[128,1792]{1,0:T(8,128)(2,1)S(1)}, u32[]{:S(2)}, u32[]{:S(2)}) %collective-permute-start.14) | collective-permute-done | bytes 458784 | tf_op jit(solution)/shard_map/ppermute | solution.py:365
  43.1 0.7 shard_map.112
  43.8 4.3 %collective-permute-start.16 = (bf16[64,1792]{1,0:T(8,128)(2,1)S(1)}, bf16[64,1792]{1,0:T(8,128)(2,1)S(1)}, u32[]{:S(2)}, u32[]{:S(2)}) collective-permute-start(bf16[64,1792]{1,0:T(8,128)(2,1)S(1)} %get-tuple-element.68), channel_id=1, source_target_pairs={{0,128},{4,132},{8,136},{12,140},{16,144},{20,148},{24,152},{28,15... | collective-permute-start | bytes 688136 | tf_op jit(solution)/shard_map/ppermute | solution.py:365
  48.1 1.0 %collective-permute-start.17 = (bf16[64,1792]{1,0:T(8,128)(2,1)S(1)}, bf16[64,1792]{1,0:T(8,128)(2,1)S(1)}, u32[]{:S(2)}, u32[]{:S(2)}) collective-permute-start(bf16[64,1792]{1,0:T(8,128)(2,1)S(1)} %get-tuple-element.69), channel_id=1, source_target_pairs={{0,64},{4,68},{8,72},{12,76},{16,80},{20,84},{24,88},{28,92},{32,9... | collective-permute-start | bytes 688136 | tf_op jit(solution)/shard_map/ppermute | solution.py:365
  49.1 0.1 collective-permute-start.18
  49.2 0.6 shard_map.113
  49.7 1.3 %collective-permute-start.19 = (bf16[96,256]{1,0:T(8,128)(2,1)S(1)}, bf16[96,256]{1,0:T(8,128)(2,1)S(1)}, u32[]{:S(2)}, u32[]{:S(2)}) collective-permute-start(bf16[96,256]{1,0:T(8,128)(2,1)S(1)} %get-tuple-element.72), channel_id=1, source_target_pairs={{0,4},{1,2},{2,1},{3,7},{4,0},{5,6},{6,5},{7,3},{8,12},{9,10},{10,... | collective-permute-start | bytes 147464 | tf_op jit(solution)/shard_map/ppermute | solution.py:361
  51.0 0.4 collective-permute-start.20
  51.4 2.5 %collective-permute-done.19.n2 = bf16[96,256]{1,0:T(8,128)(2,1)S(1)} collective-permute-done((bf16[96,256]{1,0:T(8,128)(2,1)S(1)}, bf16[96,256]{1,0:T(8,128)(2,1)S(1)}, u32[]{:S(2)}, u32[]{:S(2)}) %collective-permute-start.19) | collective-permute-done | bytes 49184 | tf_op jit(solution)/shard_map/ppermute | solution.py:361
  53.9 1.2 %collective-permute-done.20.n1.late = bf16[96,256]{1,0:T(8,128)(2,1)S(1)} collective-permute-done((bf16[96,256]{1,0:T(8,128)(2,1)S(1)}, bf16[96,256]{1,0:T(8,128)(2,1)S(1)}, u32[]{:S(2)}, u32[]{:S(2)}) %collective-permute-start.20) | collective-permute-done | bytes 49184 | tf_op jit(solution)/shard_map/ppermute | solution.py:361
  55.1 1.0 %shard_map.114 = (bf16[128,256]{1,0:T(8,128)(2,1)S(1)}, bf16[128,256]{1,0:T(8,128)(2,1)S(1)}) custom-call(s32[2]{0:T(128)S(1)} %pad_add_fusion.place, f32[192,256]{1,0:T(8,128)S(1)} %get-tuple-element.58.late.own, bf16[96,256]{1,0:T(8,128)(2,1)S(1)} %collective-permute-done.12.t2.m2, bf16[96,256]{1,0:T(8,128)(2,1)S(1)} %collective-permute-done.13.t1.m1, ...), custom_call_target="tpu_custom_call" | custom-call | flops 100000 | bytes 10000 | tf_op jit(solution)/shard_map/pallas_call | solution.py:324
  56.1 0.1 collective-permute-start.21
  56.2 1.2 %collective-permute-done.21.rs = bf16[128,256]{1,0:T(8,128)(2,1)S(1)} collective-permute-done((bf16[128,256]{1,0:T(8,128)(2,1)S(1)}, bf16[128,256]{1,0:T(8,128)(2,1)S(1)}, u32[]{:S(2)}, u32[]{:S(2)}) %collective-permute-start.21) | collective-permute-done | bytes 65568 | tf_op jit(solution)/shard_map/ppermute | solution.py:365
  57.4 0.6 shard_map.115
  58.0 2.9 %collective-permute-start.22 = (bf16[64,256]{1,0:T(8,128)(2,1)S(1)}, bf16[64,256]{1,0:T(8,128)(2,1)S(1)}, u32[]{:S(2)}, u32[]{:S(2)}) collective-permute-start(bf16[64,256]{1,0:T(8,128)(2,1)S(1)} %get-tuple-element.78), channel_id=1, source_target_pairs={{0,128},{4,132},{8,136},{12,140},{16,144},{20,148},{24,152},{28,15... | collective-permute-start | bytes 98312 | tf_op jit(solution)/shard_map/ppermute | solution.py:365
  60.9 1.0 %collective-permute-start.23 = (bf16[64,256]{1,0:T(8,128)(2,1)S(1)}, bf16[64,256]{1,0:T(8,128)(2,1)S(1)}, u32[]{:S(2)}, u32[]{:S(2)}) collective-permute-start(bf16[64,256]{1,0:T(8,128)(2,1)S(1)} %get-tuple-element.79), channel_id=1, source_target_pairs={{0,64},{4,68},{8,72},{12,76},{16,80},{20,84},{24,88},{28,92},{32,9... | collective-permute-start | bytes 98312 | tf_op jit(solution)/shard_map/ppermute | solution.py:365
  61.9 1.6 %collective-permute-done.22.b2 = bf16[64,256]{1,0:T(8,128)(2,1)S(1)} collective-permute-done((bf16[64,256]{1,0:T(8,128)(2,1)S(1)}, bf16[64,256]{1,0:T(8,128)(2,1)S(1)}, u32[]{:S(2)}, u32[]{:S(2)}) %collective-permute-start.22) | collective-permute-done | bytes 32800 | tf_op jit(solution)/shard_map/ppermute | solution.py:365
  63.5 3.3 %collective-permute-start.24 = (bf16[64,256]{1,0:T(8,128)(2,1)S(1)}, bf16[64,256]{1,0:T(8,128)(2,1)S(1)}, u32[]{:S(2)}, u32[]{:S(2)}) collective-permute-start(bf16[64,256]{1,0:T(8,128)(2,1)S(1)} %get-tuple-element.80), channel_id=1, source_target_pairs={{0,192},{4,196},{8,200},{12,204},{16,208},{20,212},{24,216},{28,22... | collective-permute-start | bytes 98312 | tf_op jit(solution)/shard_map/ppermute | solution.py:365
  66.8 0.0 collective-permute-done.23.b1
  66.8 1.9 %collective-permute-done.24.b3 = bf16[64,256]{1,0:T(8,128)(2,1)S(1)} collective-permute-done((bf16[64,256]{1,0:T(8,128)(2,1)S(1)}, bf16[64,256]{1,0:T(8,128)(2,1)S(1)}, u32[]{:S(2)}, u32[]{:S(2)}) %collective-permute-start.24) | collective-permute-done | bytes 32800 | tf_op jit(solution)/shard_map/ppermute | solution.py:365
  68.7 0.0 collective-permute-done.16.a2
  68.7 0.0 collective-permute-done.17.a1
  68.7 0.0 collective-permute-done.18.a3
  68.7 1.0 %shard_map.116 = bf16[64,2560]{1,0:T(8,128)(2,1)S(1)} custom-call(s32[2]{0:T(128)S(1)} %pad_add_fusion.place, bf16[64,1792]{1,0:T(8,128)(2,1)S(1)} %get-tuple-element.67.late.a0, bf16[64,1792]{1,0:T(8,128)(2,1)S(1)} %collective-permute-done.16.a2, bf16[64,1792]{1,0:T(8,128)(2,1)S(1)} %collective-permute-done.17.a1, ...), custom_call_target="tpu_custom_call" | custom-call | flops 100000 | bytes 10000 | tf_op jit(solution)/shard_map/pallas_call | solution.py:324
  69.7 15.5 %all_to_all.5.refs_0_ = bf16[8,8,2560]{2,1,0:T(8,128)(2,1)S(1)} all-to-all(bf16[8,8,2560]{2,1,0:T(8,128)(2,1)S(1)} %bitcast.5), channel_id=1, replica_groups={{0,8,16,24,32,40,48,56},{4,12,20,28,36,44,52,60},{64,72,80,88,96,104,11..., dimensions={0} | all-to-all | bytes 655360 | tf_op jit(solution)/shard_map/all_to_all | solution.py:519
  85.3 0.9 %shard_map.117 = (bf16[192,256]{1,0:T(8,128)(2,1)}, f32[4,1728]{1,0:T(4,128)}, f32[4,1728]{1,0:T(4,128)}) custom-call(bf16[8,8,2560]{2,1,0:T(8,128)(2,1)S(1)} %all_to_all.5.refs_0_), custom_call_target="tpu_custom_call" | custom-call | flops 100000 | bytes 10000 | tf_op jit(solution)/shard_map/pallas_call | solution.py:324
  (7 shorter events, 0.0 us)
Async XLA Ops:
  0.7 6.3 %copy-start = (bf16[256,6912]{1,0:T(8,128)(2,1)S(1)}, bf16[256,6912]{1,0:T(8,128)(2,1)}, u32[]{:S(2)}) copy-start(bf16[256,6912]{1,0:T(8,128)(2,1)} %weight.2) | copy-start | bytes 10616836
  2.8 24.8 %copy-start.1 = (bf16[256,6912]{1,0:T(8,128)(2,1)S(1)}, bf16[256,6912]{1,0:T(8,128)(2,1)}, u32[]{:S(2)}) copy-start(bf16[256,6912]{1,0:T(8,128)(2,1)} %weight.3) | copy-start | bytes 10616836
  2.8 15.8 %collective-permute-start.4 = (bf16[224,512]{1,0:T(8,128)(2,1)S(1)}, bf16[224,512]{1,0:T(8,128)(2,1)S(1)}, u32[]{:S(2)}, u32[]{:S(2)}) collective-permute-start(bf16[224,512]{1,0:T(8,128)(2,1)S(1)} %get-tuple-element.52.p0), channel_id=1, source_target_pairs={{0,2},{1,3},{2,0},{3,1},{4,6},{5,7},{6,4},{7,5},{8,10},{9,11},{10,... | collective-permute-start | bytes 688136 | tf_op jit(solution)/shard_map/ppermute | solution.py:365
  5.0 13.6 %collective-permute-start.5 = (bf16[224,512]{1,0:T(8,128)(2,1)S(1)}, bf16[224,512]{1,0:T(8,128)(2,1)S(1)}, u32[]{:S(2)}, u32[]{:S(2)}) collective-permute-start(bf16[224,512]{1,0:T(8,128)(2,1)S(1)} %get-tuple-element.52.p0), channel_id=1, source_target_pairs={{0,1},{1,0},{2,3},{3,2},{4,5},{5,4},{6,7},{7,6},{8,9},{9,8},{10,11... | collective-permute-start | bytes 688136 | tf_op jit(solution)/shard_map/ppermute | solution.py:365
  6.5 12.2 %collective-permute-start.6 = (bf16[224,512]{1,0:T(8,128)(2,1)S(1)}, bf16[224,512]{1,0:T(8,128)(2,1)S(1)}, u32[]{:S(2)}, u32[]{:S(2)}) collective-permute-start(bf16[224,512]{1,0:T(8,128)(2,1)S(1)} %get-tuple-element.52.p0), channel_id=1, source_target_pairs={{0,3},{1,2},{2,1},{3,0},{4,7},{5,6},{6,5},{7,4},{8,11},{9,10},{10,... | collective-permute-start | bytes 688136 | tf_op jit(solution)/shard_map/ppermute | solution.py:365
  10.1 7.2 %collective-permute-start = (bf16[96,256]{1,0:T(8,128)(2,1)S(1)}, bf16[96,256]{1,0:T(8,128)(2,1)S(1)}, u32[]{:S(2)}, u32[]{:S(2)}) collective-permute-start(bf16[96,256]{1,0:T(8,128)(2,1)S(1)} %get-tuple-element.45), channel_id=1, source_target_pairs={{0,1},{1,0},{2,3},{3,2},{4,8},{5,9},{6,10},{7,11},{8,4},{9,5},{10,... | collective-permute-start | bytes 147464 | tf_op jit(solution)/shard_map/ppermute | solution.py:361
  12.4 4.9 %collective-permute-start.1 = (bf16[96,256]{1,0:T(8,128)(2,1)S(1)}, bf16[96,256]{1,0:T(8,128)(2,1)S(1)}, u32[]{:S(2)}, u32[]{:S(2)}) collective-permute-start(bf16[96,256]{1,0:T(8,128)(2,1)S(1)} %get-tuple-element.46), channel_id=1, source_target_pairs={{0,4},{1,5},{2,6},{3,7},{4,0},{5,1},{6,2},{7,3},{8,12},{9,13},{10,... | collective-permute-start | bytes 147464 | tf_op jit(solution)/shard_map/ppermute | solution.py:361
  17.8 4.2 %collective-permute-start.2 = (bf16[96,256]{1,0:T(8,128)(2,1)S(1)}, bf16[96,256]{1,0:T(8,128)(2,1)S(1)}, u32[]{:S(2)}, u32[]{:S(2)}) collective-permute-start(bf16[96,256]{1,0:T(8,128)(2,1)S(1)} %get-tuple-element.48), channel_id=1, source_target_pairs={{0,4},{1,2},{2,1},{3,7},{4,0},{5,6},{6,5},{7,3},{8,12},{9,10},{10,... | collective-permute-start | bytes 147464 | tf_op jit(solution)/shard_map/ppermute | solution.py:361
  18.5 4.1 %collective-permute-start.3 = (bf16[96,256]{1,0:T(8,128)(2,1)S(1)}, bf16[96,256]{1,0:T(8,128)(2,1)S(1)}, u32[]{:S(2)}, u32[]{:S(2)}) collective-permute-start(bf16[96,256]{1,0:T(8,128)(2,1)S(1)} %get-tuple-element.49.late), channel_id=1, source_target_pairs={{0,1},{1,0},{2,3},{3,2},{4,5},{5,4},{6,7},{7,6},{8,9},{9,8},{10,11... | collective-permute-start | bytes 147464 | tf_op jit(solution)/shard_map/ppermute | solution.py:361
  19.7 11.0 %collective-permute-start.10 = (bf16[768,256]{1,0:T(8,128)(2,1)S(1)}, bf16[768,256]{1,0:T(8,128)(2,1)S(1)}, u32[]{:S(2)}, u32[]{:S(2)}) collective-permute-start(bf16[768,256]{1,0:T(8,128)(2,1)S(1)} %get-tuple-element.55), channel_id=1, source_target_pairs={{0,1},{1,0},{2,3},{3,2},{4,8},{5,9},{6,10},{7,11},{8,4},{9,5},{10,... | collective-permute-start | bytes 1179656 | tf_op jit(solution)/shard_map/ppermute | solution.py:361
  21.7 10.3 %collective-permute-start.11 = (bf16[768,256]{1,0:T(8,128)(2,1)S(1)}, bf16[768,256]{1,0:T(8,128)(2,1)S(1)}, u32[]{:S(2)}, u32[]{:S(2)}) collective-permute-start(bf16[768,256]{1,0:T(8,128)(2,1)S(1)} %get-tuple-element.56), channel_id=1, source_target_pairs={{0,4},{1,5},{2,6},{3,7},{4,0},{5,1},{6,2},{7,3},{8,12},{9,13},{10,... | collective-permute-start | bytes 1179656 | tf_op jit(solution)/shard_map/ppermute | solution.py:361
  23.5 13.7 %collective-permute-start.7 = (bf16[192,512]{1,0:T(8,128)(2,1)S(1)}, bf16[192,512]{1,0:T(8,128)(2,1)S(1)}, u32[]{:S(2)}, u32[]{:S(2)}) collective-permute-start(bf16[192,512]{1,0:T(8,128)(2,1)S(1)} %get-tuple-element.54.g0), channel_id=1, source_target_pairs={{0,2},{1,3},{2,0},{3,1},{4,6},{5,7},{6,4},{7,5},{8,10},{9,11},{10,... | collective-permute-start | bytes 589832 | tf_op jit(solution)/shard_map/ppermute | solution.py:365
  24.5 12.7 %collective-permute-start.8 = (bf16[192,512]{1,0:T(8,128)(2,1)S(1)}, bf16[192,512]{1,0:T(8,128)(2,1)S(1)}, u32[]{:S(2)}, u32[]{:S(2)}) collective-permute-start(bf16[192,512]{1,0:T(8,128)(2,1)S(1)} %get-tuple-element.54.g0), channel_id=1, source_target_pairs={{0,1},{1,0},{2,3},{3,2},{4,5},{5,4},{6,7},{7,6},{8,9},{9,8},{10,11... | collective-permute-start | bytes 589832 | tf_op jit(solution)/shard_map/ppermute | solution.py:365
  27.1 10.1 %collective-permute-start.9 = (bf16[192,512]{1,0:T(8,128)(2,1)S(1)}, bf16[192,512]{1,0:T(8,128)(2,1)S(1)}, u32[]{:S(2)}, u32[]{:S(2)}) collective-permute-start(bf16[192,512]{1,0:T(8,128)(2,1)S(1)} %get-tuple-element.54.g0), channel_id=1, source_target_pairs={{0,3},{1,2},{2,1},{3,0},{4,7},{5,6},{6,5},{7,4},{8,11},{9,10},{10,... | collective-permute-start | bytes 589832 | tf_op jit(solution)/shard_map/ppermute | solution.py:365
  30.7 6.4 %collective-permute-start.12 = (bf16[96,256]{1,0:T(8,128)(2,1)S(1)}, bf16[96,256]{1,0:T(8,128)(2,1)S(1)}, u32[]{:S(2)}, u32[]{:S(2)}) collective-permute-start(bf16[96,256]{1,0:T(8,128)(2,1)S(1)} %get-tuple-element.61), channel_id=1, source_target_pairs={{0,1},{1,0},{2,3},{3,2},{4,8},{5,9},{6,10},{7,11},{8,4},{9,5},{10,... | collective-permute-start | bytes 147464 | tf_op jit(solution)/shard_map/ppermute | solution.py:361
  32.0 5.2 %collective-permute-start.13 = (bf16[96,256]{1,0:T(8,128)(2,1)S(1)}, bf16[96,256]{1,0:T(8,128)(2,1)S(1)}, u32[]{:S(2)}, u32[]{:S(2)}) collective-permute-start(bf16[96,256]{1,0:T(8,128)(2,1)S(1)} %get-tuple-element.62), channel_id=1, source_target_pairs={{0,4},{1,5},{2,6},{3,7},{4,0},{5,1},{6,2},{7,3},{8,12},{9,13},{10,... | collective-permute-start | bytes 147464 | tf_op jit(solution)/shard_map/ppermute | solution.py:361
  38.9 4.2 %collective-permute-start.15 = (f32[128,1792]{1,0:T(8,128)S(1)}, f32[128,1792]{1,0:T(8,128)S(1)}, u32[]{:S(2)}, u32[]{:S(2)}) collective-permute-start(f32[128,1792]{1,0:T(8,128)S(1)} %get-tuple-element.66), channel_id=1, source_target_pairs={{0,4},{4,0},{8,12},{12,8},{16,20},{20,16},{24,28},{28,24},{32,36},... | collective-permute-start | bytes 2752520 | tf_op jit(solution)/shard_map/ppermute | solution.py:365
  41.2 1.9 %collective-permute-start.14 = (bf16[128,1792]{1,0:T(8,128)(2,1)S(1)}, bf16[128,1792]{1,0:T(8,128)(2,1)S(1)}, u32[]{:S(2)}, u32[]{:S(2)}) collective-permute-start(bf16[128,1792]{1,0:T(8,128)(2,1)S(1)} %get-tuple-element.65), channel_id=1, source_target_pairs={{0,4},{4,0},{8,12},{12,8},{16,20},{20,16},{24,28},{28,24},{32,36},... | collective-permute-start | bytes 1376264 | tf_op jit(solution)/shard_map/ppermute | solution.py:365
  43.8 24.8 %collective-permute-start.16 = (bf16[64,1792]{1,0:T(8,128)(2,1)S(1)}, bf16[64,1792]{1,0:T(8,128)(2,1)S(1)}, u32[]{:S(2)}, u32[]{:S(2)}) collective-permute-start(bf16[64,1792]{1,0:T(8,128)(2,1)S(1)} %get-tuple-element.68), channel_id=1, source_target_pairs={{0,128},{4,132},{8,136},{12,140},{16,144},{20,148},{24,152},{28,15... | collective-permute-start | bytes 688136 | tf_op jit(solution)/shard_map/ppermute | solution.py:365
  48.1 20.6 %collective-permute-start.17 = (bf16[64,1792]{1,0:T(8,128)(2,1)S(1)}, bf16[64,1792]{1,0:T(8,128)(2,1)S(1)}, u32[]{:S(2)}, u32[]{:S(2)}) collective-permute-start(bf16[64,1792]{1,0:T(8,128)(2,1)S(1)} %get-tuple-element.69), channel_id=1, source_target_pairs={{0,64},{4,68},{8,72},{12,76},{16,80},{20,84},{24,88},{28,92},{32,9... | collective-permute-start | bytes 688136 | tf_op jit(solution)/shard_map/ppermute | solution.py:365
  49.1 19.6 %collective-permute-start.18 = (bf16[64,1792]{1,0:T(8,128)(2,1)S(1)}, bf16[64,1792]{1,0:T(8,128)(2,1)S(1)}, u32[]{:S(2)}, u32[]{:S(2)}) collective-permute-start(bf16[64,1792]{1,0:T(8,128)(2,1)S(1)} %get-tuple-element.70), channel_id=1, source_target_pairs={{0,192},{4,196},{8,200},{12,204},{16,208},{20,212},{24,216},{28,22... | collective-permute-start | bytes 688136 | tf_op jit(solution)/shard_map/ppermute | solution.py:365
  49.7 4.2 %collective-permute-start.19 = (bf16[96,256]{1,0:T(8,128)(2,1)S(1)}, bf16[96,256]{1,0:T(8,128)(2,1)S(1)}, u32[]{:S(2)}, u32[]{:S(2)}) collective-permute-start(bf16[96,256]{1,0:T(8,128)(2,1)S(1)} %get-tuple-element.72), channel_id=1, source_target_pairs={{0,4},{1,2},{2,1},{3,7},{4,0},{5,6},{6,5},{7,3},{8,12},{9,10},{10,... | collective-permute-start | bytes 147464 | tf_op jit(solution)/shard_map/ppermute | solution.py:361
  51.0 4.1 %collective-permute-start.20 = (bf16[96,256]{1,0:T(8,128)(2,1)S(1)}, bf16[96,256]{1,0:T(8,128)(2,1)S(1)}, u32[]{:S(2)}, u32[]{:S(2)}) collective-permute-start(bf16[96,256]{1,0:T(8,128)(2,1)S(1)} %get-tuple-element.73), channel_id=1, source_target_pairs={{0,1},{1,0},{2,3},{3,2},{4,5},{5,4},{6,7},{7,6},{8,9},{9,8},{10,11... | collective-permute-start | bytes 147464 | tf_op jit(solution)/shard_map/ppermute | solution.py:361
  56.1 1.3 %collective-permute-start.21 = (bf16[128,256]{1,0:T(8,128)(2,1)S(1)}, bf16[128,256]{1,0:T(8,128)(2,1)S(1)}, u32[]{:S(2)}, u32[]{:S(2)}) collective-permute-start(bf16[128,256]{1,0:T(8,128)(2,1)S(1)} %get-tuple-element.76), channel_id=1, source_target_pairs={{0,4},{4,0},{8,12},{12,8},{16,20},{20,16},{24,28},{28,24},{32,36},... | collective-permute-start | bytes 196616 | tf_op jit(solution)/shard_map/ppermute | solution.py:365
  58.0 5.5 %collective-permute-start.22 = (bf16[64,256]{1,0:T(8,128)(2,1)S(1)}, bf16[64,256]{1,0:T(8,128)(2,1)S(1)}, u32[]{:S(2)}, u32[]{:S(2)}) collective-permute-start(bf16[64,256]{1,0:T(8,128)(2,1)S(1)} %get-tuple-element.78), channel_id=1, source_target_pairs={{0,128},{4,132},{8,136},{12,140},{16,144},{20,148},{24,152},{28,15... | collective-permute-start | bytes 98312 | tf_op jit(solution)/shard_map/ppermute | solution.py:365
  60.9 5.8 %collective-permute-start.23 = (bf16[64,256]{1,0:T(8,128)(2,1)S(1)}, bf16[64,256]{1,0:T(8,128)(2,1)S(1)}, u32[]{:S(2)}, u32[]{:S(2)}) collective-permute-start(bf16[64,256]{1,0:T(8,128)(2,1)S(1)} %get-tuple-element.79), channel_id=1, source_target_pairs={{0,64},{4,68},{8,72},{12,76},{16,80},{20,84},{24,88},{28,92},{32,9... | collective-permute-start | bytes 98312 | tf_op jit(solution)/shard_map/ppermute | solution.py:365
  63.5 5.2 %collective-permute-start.24 = (bf16[64,256]{1,0:T(8,128)(2,1)S(1)}, bf16[64,256]{1,0:T(8,128)(2,1)S(1)}, u32[]{:S(2)}, u32[]{:S(2)}) collective-permute-start(bf16[64,256]{1,0:T(8,128)(2,1)S(1)} %get-tuple-element.80), channel_id=1, source_target_pairs={{0,192},{4,196},{8,200},{12,204},{16,208},{20,212},{24,216},{28,22... | collective-permute-start | bytes 98312 | tf_op jit(solution)/shard_map/ppermute | solution.py:365

commit v8 on v7

--- a/solution.py
+++ b/solution.py
@@ -244,7 +244,7 @@
             cols_two[turn * S : (turn + 1) * S, lanes] = merged[:, C : 2 * C]
 
 
-def weight_kernel(lanes, place, g0, g2, g1, g3, cols, t2, t1, keep, send, gt):
+def weight_kernel(lanes, place, g0, g2, g1, g3, cols, late, keep, send, gt):
     for turn, grad in enumerate((g0, g1, g2, g3)):
         gt[:, turn * S : (turn + 1) * S] = jnp.transpose(grad[:, lanes].astype(F32)).astype(BF)
     mine = pl.multiple_of((place[0] % 2) * 128, 128)
@@ -257,41 +257,53 @@
         send[:, lanes] = block[128:256].astype(send.dtype)
 
 
-def merge_kernel(place, k1, s1, k2, s2, *outs):
+def merge_two_kernel(place, keep, come, late, *outs):
     line = place[0] // 16
     for turn, out in enumerate(outs):
         rows = pl.ds(pl.multiple_of(32 * (line ^ turn), 32), 32)
-        for at, (keep, come) in ((0, (k1, s1)), (32, (k2, s2))):
-            total = keep[rows, :].astype(F32) + come[rows, :].astype(F32)
-            out[at : at + 32, :] = total.astype(BF)
-
-
-def sort_kernel(place, rk, rs, *outs):
+        out[...] = (keep[rows, :] + come[rows, :]).astype(BF)
+
+
+def merge_one_kernel(place, keep, come, rk, rs, late, *outs):
     first = place[0] % 2 == 0
     line = place[0] // 16
     for turn, out in enumerate(outs):
         rows = pl.ds(pl.multiple_of(32 * (line ^ turn), 32), 32)
+        total = keep[rows, :].astype(F32) + come[rows, :].astype(F32)
+        out[:, 0 : 7 * C] = total.astype(BF)
         mine, other = rk[rows, :], rs[rows, :]
-        out[0:32, :] = jnp.where(first, mine, other)
-        out[32:64, :] = jnp.where(first, other, mine)
-
-
-def line_kernel(place, a0, a2, a1, a3, b0, b2, b1, b3, out):
+        out[:, 7 * C : 8 * C] = jnp.where(first, mine, other)
+        out[:, 8 * C : 9 * C] = jnp.where(first, other, mine)
+
+
+def line_two_kernel(place, a0, a2, a1, a3, out):
+    total = a0[...].astype(F32)
+    for part in (a1, a2, a3):
+        total = total + part[...].astype(F32)
+    out[...] = total.astype(BF)
+
+
+def line_one_kernel(place, two, b0, b2, b1, b3, out):
     line = place[0] // 16
-    to, at = iota((64, 64), 0), iota((64, 64), 1)
-    order = onehot(at == 32 * ((to % 8) // 4) + 4 * (to // 8) + to % 4)
+    to, at = iota((64, 32), 0), iota((64, 32), 1)
     for n in range(7):
         lanes = slice(n * C, (n + 1) * C)
-        total = a0[:, lanes].astype(F32)
-        for part in (a1, a2, a3):
+        total = b0[:, lanes].astype(F32)
+        for part in (b1, b2, b3):
             total = total + part[:, lanes].astype(F32)
-        out[:, lanes] = mm(order, total.astype(BF)).astype(BF)
+        block = jnp.zeros((64, C), F32)
+        for which, value in ((0, total.astype(BF)), (1, two[:, lanes])):
+            spot = ((to % 8) // 4 == which) & (at == 4 * (to // 8) + to % 4)
+            block = block + mm(onehot(spot), value)
+        out[:, lanes] = block.astype(BF)
     for n in range(3):
         index = 8 * n + to % 8
         total = jnp.zeros((64, C), F32)
         for turn, part in enumerate((b0, b1, b2, b3)):
-            row = 32 * ((index % 6) // 3) + 4 * (to // 8) + index % 3
-            total = total + mm(onehot((index // 6 == (line ^ turn)) & (at == row)), part[...])
+            from_line = (index // 6 == (line ^ turn)) & (at == 4 * (to // 8) + index % 3)
+            for core in range(2):
+                spot = onehot(from_line & ((index % 6) // 3 == core))
+                total = total + mm(spot, part[:, (7 + core) * C : (8 + core) * C])
         out[:, (7 + n) * C : (8 + n) * C] = total.astype(BF)
 
 
@@ -469,8 +481,9 @@
         late=1,
         flops=4 * 10**9,
     )
-
-    def halves(which, cols, kind, flops, *late):
+    passed, n2, n1 = halo_columns(place, loc, m2, m1, cols_two)
+
+    def halves(which, cols, kind, flops, late):
         lanes = slice(which * C, (which + 1) * C)
         half = sds((128, wide), kind)
         return call(
@@ -479,21 +492,16 @@
             place,
             *grads,
             cols,
-            *late,
+            late,
             scratch=[pltpu.VMEM((C, 4 * S), BF)],
-            late=2,
+            late=1,
             flops=flops,
         )
 
-    keep_two, send_two = halves(0, cols_two, F32, 4 * 10**9, m2, m1)
+    keep_two, send_two = halves(0, cols_two, F32, 4 * 10**9, passed)
     come_two = cross(send_two, "gx", 1)
-    keep_one, send_one = halves(1, cols_one, BF, 10**5, keep_two, keep_two)
+    keep_one, send_one = halves(1, cols_one, BF, 10**5, keep_two)
     come_one = cross(send_one, "gx", 1)
-    chunks = call(
-        merge_kernel, (sds((64, wide), BF),) * 4, place, keep_one, come_one, keep_two, come_two
-    )
-    sums = [chunks[0]] + [cross(chunks[d], "gx", 16 * d) for d in (2, 1, 3)]
-    n2, n1 = halo_columns(place, loc, m2, m1, chunks[0], 2 * 10**10)[1:]
     some = sds((128, C), BF)
     rows_keep, rows_send = call(
         rows_kernel,
@@ -507,14 +515,41 @@
         hrow,
         grad,
         srow,
-        n1,
+        keep_one,
         scratch=[back],
         late=1,
+        flops=2 * 10**10,
     )
     rows_come = cross(rows_send, "gx", 1)
-    sorts = call(sort_kernel, (sds((64, C), BF),) * 4, place, rows_keep, rows_come)
-    rows = [sorts[0]] + [cross(sorts[d], "gx", 16 * d) for d in (2, 1, 3)]
-    summed = call(line_kernel, sds((64, 10 * C), BF), place, *sums, *rows)
+
+    def lines(chunks):
+        return [chunks[0]] + [cross(chunks[d], "gx", 16 * d) for d in (2, 1, 3)]
+
+    two = call(
+        merge_two_kernel,
+        (sds((32, wide), BF),) * 4,
+        place,
+        keep_two,
+        come_two,
+        rows_keep,
+        late=1,
+    )
+    one = call(
+        merge_one_kernel,
+        (sds((32, 9 * C), BF),) * 4,
+        place,
+        keep_one,
+        come_one,
+        rows_keep,
+        rows_come,
+        two[0],
+        late=1,
+        flops=2 * 10**10,
+    )
+    sum_two = call(
+        line_two_kernel, sds((32, wide), BF), place, *lines(two), flops=2 * 10**10
+    )
+    summed = call(line_one_kernel, sds((64, 10 * C), BF), place, sum_two, *lines(one))
     groups = [[16 * y + 2 * z + e for z in range(8)] for y in range(4) for e in range(2)]
     collected = lax.all_to_all(
         summed.reshape(8, 8, 10 * C),

time: 86.3 us -> 83.7 us (0.970)
  waiting for transfers between devices: 16 us -> 11 us
  blocking collectives: 15.5 us -> 17.2 us
    ppermute x10, waiting for transfers between devices: 9.41 us -> 5.74 us  [swap(): return lax.ppermute(value, ('gx', 'gy'), pairs)]
    all_to_all x1, blocking collectives: 15.5 us -> 17.2 us  [body(): lax.all_to_all(summed.reshape(8, 8, 10 * C), 'gx', split_axis=0, concat_a...]
    ppermute x15, starting transfers between devices: 21.7 us -> 20.2 us  [cross(): lax.ppermute(value, axis, [(n, n ^ mask) for n in range(lax.axis_size(axi...]
    ppermute x15, waiting for transfers between devices: 6.55 us -> 5.3 us  [cross(): lax.ppermute(value, axis, [(n, n ^ mask) for n in range(lax.axis_size(axi...]
    pallas_call x15 -> x16, Pallas kernels: 24 us -> 24.7 us  [call(): pl.pallas_call(kernel, out_shape=outs, in_specs=specs, out_specs=jax.tree...]
  transfers between devices with their start and end apart: 25 -> 25, of which waited for: 9 -> 6; matrix products, arithmetic and copies ran while one was open for 0% -> 0% of each run, Pallas kernels for 20% -> 25%
where the time goes in v8:
time: 83.7 us; the launch traced here: 82.9 us
  starting transfers between devices  29.1 us (35%)
  Pallas kernels  24.7 us (30%)
  blocking collectives  17.2 us (21%)
  waiting for transfers between devices  11 us (13%)
    pallas_call x16, Pallas kernels, call(): pl.pallas_call(kernel, out_shape=outs, in_specs=specs, out_specs=jax.tree...  24.7 us
    ppermute x15, starting transfers between devices, cross(): lax.ppermute(value, axis, [(n, n ^ mask) for n in range(lax.axis_size(axi...  20.2 us
    all_to_all x1, blocking collectives, body(): lax.all_to_all(summed.reshape(8, 8, 10 * C), 'gx', split_axis=0, concat_a...  17.2 us
    ppermute x10, starting transfers between devices, swap(): return lax.ppermute(value, ('gx', 'gy'), pairs)  8.84 us
    ppermute x10, waiting for transfers between devices, swap(): return lax.ppermute(value, ('gx', 'gy'), pairs)  5.74 us
    ppermute x15, waiting for transfers between devices, cross(): lax.ppermute(value, axis, [(n, n ^ mask) for n in range(lax.axis_size(axi...  5.3 us
  transfers between devices with their start and end apart: 25, of which 6 were waited for; matrix products, arithmetic and copies ran while one was open for 0% of the time, Pallas kernels for 25%

profile of v8, /device:TPU:2, one launch (start us, length us, event | category | flops | bytes accessed | tf_op | source)
XLA Modules:
  0.0 82.9 jit_solution(7055936005009256694)
XLA Ops:
  0.6 0.1 pad_add_fusion.place
  0.7 2.1 %shard_map.103 = (bf16[224,512]{1,0:T(8,128)(2,1)S(1)}, f32[32,256]{1,0:T(8,128)S(1)}, s32[8,256]{1,0:T(8,128)S(1)}, s32[8,256]{1,0:T(8,128)S(1)}, bf16[192,256]...) custom-call(s32[2]{0:T(128)S(1)} %pad_add_fusion.place, bf16[192,256]{1,0:T(8,128)(2,1)} %feat.1, bf16[192,256]{1,0:T(8,128)(2,1)} %pre.1, ...), custom_call_target="tpu_custom_call" | custom-call | flops 4000000000 | bytes 10000 | tf_op jit(solution)/shard_map/pallas_call | solution.py:336
  2.8 0.0 copy-start.1
  2.8 2.2 %collective-permute-start.4 = (bf16[224,512]{1,0:T(8,128)(2,1)S(1)}, bf16[224,512]{1,0:T(8,128)(2,1)S(1)}, u32[]{:S(2)}, u32[]{:S(2)}) collective-permute-start(bf16[224,512]{1,0:T(8,128)(2,1)S(1)} %get-tuple-element.52.p0), channel_id=1, source_target_pairs={{0,2},{1,3},{2,0},{3,1},{4,6},{5,7},{6,4},{7,5},{8,10},{9,11},{10,... | collective-permute-start | bytes 688136 | tf_op jit(solution)/shard_map/ppermute | solution.py:377
  5.0 1.4 %collective-permute-start.5 = (bf16[224,512]{1,0:T(8,128)(2,1)S(1)}, bf16[224,512]{1,0:T(8,128)(2,1)S(1)}, u32[]{:S(2)}, u32[]{:S(2)}) collective-permute-start(bf16[224,512]{1,0:T(8,128)(2,1)S(1)} %get-tuple-element.52.p0), channel_id=1, source_target_pairs={{0,1},{1,0},{2,3},{3,2},{4,5},{5,4},{6,7},{7,6},{8,9},{9,8},{10,11... | collective-permute-start | bytes 688136 | tf_op jit(solution)/shard_map/ppermute | solution.py:377
  6.5 0.5 collective-permute-start.6
  7.0 3.0 %shard_map.104 = (f32[192,256]{1,0:T(8,128)S(1)}, bf16[96,256]{1,0:T(8,128)(2,1)S(1)}, bf16[96,256]{1,0:T(8,128)(2,1)S(1)}, bf16[64,256]{1,0:T(8,128)(2,1)S(1)}) custom-call(s32[2]{0:T(128)S(1)} %pad_add_fusion.place, f32[32,256]{1,0:T(8,128)S(1)} %get-tuple-element.42.nbt, bf16[192,256]{1,0:T(8,128)(2,1)S(1)} %get-tuple-element.43.grad, ...), custom_call_target="tpu_custom_call" | custom-call | flops 100000 | bytes 10000 | tf_op jit(solution)/shard_map/pallas_call | solution.py:336
  10.1 2.4 %collective-permute-start = (bf16[96,256]{1,0:T(8,128)(2,1)S(1)}, bf16[96,256]{1,0:T(8,128)(2,1)S(1)}, u32[]{:S(2)}, u32[]{:S(2)}) collective-permute-start(bf16[96,256]{1,0:T(8,128)(2,1)S(1)} %get-tuple-element.45), channel_id=1, source_target_pairs={{0,1},{1,0},{2,3},{3,2},{4,8},{5,9},{6,10},{7,11},{8,4},{9,5},{10,... | collective-permute-start | bytes 147464 | tf_op jit(solution)/shard_map/ppermute | solution.py:373
  12.4 0.0 collective-permute-start.1
  12.4 4.9 %collective-permute-done.m2 = bf16[96,256]{1,0:T(8,128)(2,1)S(1)} collective-permute-done((bf16[96,256]{1,0:T(8,128)(2,1)S(1)}, bf16[96,256]{1,0:T(8,128)(2,1)S(1)}, u32[]{:S(2)}, u32[]{:S(2)}) %collective-permute-start) | collective-permute-done | bytes 49184 | tf_op jit(solution)/shard_map/ppermute | solution.py:373
  17.3 0.0 collective-permute-done.1.m1
  17.3 0.6 shard_map.105
  17.8 0.6 collective-permute-start.2
  18.5 0.2 collective-permute-start.3
  18.6 0.0 collective-permute-done.4.p2
  18.6 0.0 collective-permute-done.6.p3
  18.6 1.1 %shard_map.106 = (bf16[768,256]{1,0:T(8,128)(2,1)S(1)}, bf16[768,256]{1,0:T(8,128)(2,1)S(1)}, bf16[4,64,512]{2,1,0:T(8,128)(2,1)S(1)}) custom-call(s32[2]{0:T(128)S(1)} %pad_add_fusion.place, bf16[224,512]{1,0:T(8,128)(2,1)S(1)} %get-tuple-element.52.p0, bf16[224,512]{1,0:T(8,128)(2,1)S(1)} %collective-permute-done.4.p2, ...), custom_call_target="tpu_custom_call" | custom-call | flops 100000 | bytes 10000 | tf_op jit(solution)/shard_map/pallas_call | solution.py:336
  19.7 2.0 %collective-permute-start.10 = (bf16[768,256]{1,0:T(8,128)(2,1)S(1)}, bf16[768,256]{1,0:T(8,128)(2,1)S(1)}, u32[]{:S(2)}, u32[]{:S(2)}) collective-permute-start(bf16[768,256]{1,0:T(8,128)(2,1)S(1)} %get-tuple-element.55), channel_id=1, source_target_pairs={{0,1},{1,0},{2,3},{3,2},{4,8},{5,9},{6,10},{7,11},{8,4},{9,5},{10,... | collective-permute-start | bytes 1179656 | tf_op jit(solution)/shard_map/ppermute | solution.py:373
  21.7 0.0 collective-permute-start.11
  21.7 0.3 collective-permute-done.2.n2
  22.0 0.5 collective-permute-done.3.n1
  22.6 0.9 %shard_map.107 = (bf16[192,256]{1,0:T(8,128)(2,1)S(1)}, bf16[192,512]{1,0:T(8,128)(2,1)S(1)}) custom-call(s32[2]{0:T(128)S(1)} %pad_add_fusion.place, f32[192,256]{1,0:T(8,128)S(1)} %get-tuple-element.44.late.own, bf16[96,256]{1,0:T(8,128)(2,1)S(1)} %collective-permute-done.m2, bf16[96,256]{1,0:T(8,128)(2,1)S(1)} %collective-permute-done.1.m1, ...), custom_call_target="tpu_custom_call" | custom-call | flops 100000 | bytes 10000 | tf_op jit(solution)/shard_map/pallas_call | solution.py:336
  23.5 1.0 %collective-permute-start.7 = (bf16[192,512]{1,0:T(8,128)(2,1)S(1)}, bf16[192,512]{1,0:T(8,128)(2,1)S(1)}, u32[]{:S(2)}, u32[]{:S(2)}) collective-permute-start(bf16[192,512]{1,0:T(8,128)(2,1)S(1)} %get-tuple-element.54.g0), channel_id=1, source_target_pairs={{0,2},{1,3},{2,0},{3,1},{4,6},{5,7},{6,4},{7,5},{8,10},{9,11},{10,... | collective-permute-start | bytes 589832 | tf_op jit(solution)/shard_map/ppermute | solution.py:377
  24.5 2.6 %collective-permute-start.8 = (bf16[192,512]{1,0:T(8,128)(2,1)S(1)}, bf16[192,512]{1,0:T(8,128)(2,1)S(1)}, u32[]{:S(2)}, u32[]{:S(2)}) collective-permute-start(bf16[192,512]{1,0:T(8,128)(2,1)S(1)} %get-tuple-element.54.g0), channel_id=1, source_target_pairs={{0,1},{1,0},{2,3},{3,2},{4,5},{5,4},{6,7},{7,6},{8,9},{9,8},{10,11... | collective-permute-start | bytes 589832 | tf_op jit(solution)/shard_map/ppermute | solution.py:377
  27.1 0.5 collective-permute-start.9
  27.7 3.0 %shard_map.108 = (f32[192,256]{1,0:T(8,128)S(1)}, bf16[96,256]{1,0:T(8,128)(2,1)S(1)}, bf16[96,256]{1,0:T(8,128)(2,1)S(1)}, bf16[64,256]{1,0:T(8,128)(2,1)S(1)}) custom-call(s32[2]{0:T(128)S(1)} %pad_add_fusion.place, f32[32,256]{1,0:T(8,128)S(1)} %get-tuple-element.42.nbt, bf16[192,256]{1,0:T(8,128)(2,1)S(1)} %get-tuple-element.57.grad, ...), custom_call_target="tpu_custom_call" | custom-call | flops 4000000000 | bytes 10000 | tf_op jit(solution)/shard_map/pallas_call | solution.py:336
  30.7 0.0 collective-permute-done.10.r2
  30.7 1.3 %collective-permute-start.12 = (bf16[96,256]{1,0:T(8,128)(2,1)S(1)}, bf16[96,256]{1,0:T(8,128)(2,1)S(1)}, u32[]{:S(2)}, u32[]{:S(2)}) collective-permute-start(bf16[96,256]{1,0:T(8,128)(2,1)S(1)} %get-tuple-element.61), channel_id=1, source_target_pairs={{0,1},{1,0},{2,3},{3,2},{4,8},{5,9},{6,10},{7,11},{8,4},{9,5},{10,... | collective-permute-start | bytes 147464 | tf_op jit(solution)/shard_map/ppermute | solution.py:373
  32.0 0.0 collective-permute-done.11.r1
  32.0 0.0 collective-permute-start.13
  32.0 5.1 %shard_map.109 = (bf16[768,1792]{1,0:T(8,128)(2,1)S(1)}, bf16[768,1792]{1,0:T(8,128)(2,1)S(1)}) custom-call(s32[2]{0:T(128)S(1)} %pad_add_fusion.place, bf16[224,512]{1,0:T(8,128)(2,1)S(1)} %get-tuple-element.52.p0, bf16[224,512]{1,0:T(8,128)(2,1)S(1)} %collective-permute-done.4.p2, bf16[224,512]{1,0:T(8,128)(2,1)S(1)} %collective-permute-done.5.p1, ...), custom_call_target="tpu_custom_call" | custom-call | flops 4000000000 | bytes 10000 | tf_op jit(solution)/shard_map/pallas_call | solution.py:336
  37.2 0.0 collective-permute-done.13.m1
  37.2 0.6 shard_map.110
  37.8 2.4 %collective-permute-start.15 = (bf16[96,256]{1,0:T(8,128)(2,1)S(1)}, bf16[96,256]{1,0:T(8,128)(2,1)S(1)}, u32[]{:S(2)}, u32[]{:S(2)}) collective-permute-start(bf16[96,256]{1,0:T(8,128)(2,1)S(1)} %get-tuple-element.66), channel_id=1, source_target_pairs={{0,4},{1,2},{2,1},{3,7},{4,0},{5,6},{6,5},{7,3},{8,12},{9,10},{10,... | collective-permute-start | bytes 147464 | tf_op jit(solution)/shard_map/ppermute | solution.py:373
  40.2 0.0 collective-permute-start.16
  40.2 0.0 collective-permute-done.7.g2
  40.2 0.0 collective-permute-done.8.g1
  40.2 1.7 %shard_map.111 = (f32[128,1792]{1,0:T(8,128)S(1)}, f32[128,1792]{1,0:T(8,128)S(1)}) custom-call(s32[2]{0:T(128)S(1)} %pad_add_fusion.place, bf16[192,512]{1,0:T(8,128)(2,1)S(1)} %get-tuple-element.54.g0, bf16[192,512]{1,0:T(8,128)(2,1)S(1)} %collective-permute-done.7.g2, bf16[192,512]{1,0:T(8,128)(2,1)S(1)} %collective-permute-done.8.g1, ...), custom_call_target="tpu_custom_call" | custom-call | flops 4000000000 | bytes 10000 | tf_op jit(solution)/shard_map/pallas_call | solution.py:336
  41.9 0.3 collective-permute-start.14
  42.2 1.7 %shard_map.112 = (bf16[128,1792]{1,0:T(8,128)(2,1)S(1)}, bf16[128,1792]{1,0:T(8,128)(2,1)S(1)}) custom-call(s32[2]{0:T(128)S(1)} %pad_add_fusion.place, bf16[192,512]{1,0:T(8,128)(2,1)S(1)} %get-tuple-element.54.g0, bf16[192,512]{1,0:T(8,128)(2,1)S(1)} %collective-permute-done.7.g2, bf16[192,512]{1,0:T(8,128)(2,1)S(1)} %collective-permute-done.8.g1, ...), custom_call_target="tpu_custom_call" | custom-call | flops 100000 | bytes 10000 | tf_op jit(solution)/shard_map/pallas_call | solution.py:336
  43.9 0.6 collective-permute-start.20
  44.5 0.0 collective-permute-done.15.n2
  44.5 0.0 collective-permute-done.16.n1
  44.5 1.0 %shard_map.113 = (bf16[128,256]{1,0:T(8,128)(2,1)S(1)}, bf16[128,256]{1,0:T(8,128)(2,1)S(1)}) custom-call(s32[2]{0:T(128)S(1)} %pad_add_fusion.place, f32[192,256]{1,0:T(8,128)S(1)} %get-tuple-element.58.late.own, bf16[96,256]{1,0:T(8,128)(2,1)S(1)} %collective-permute-done.12.m2, bf16[96,256]{1,0:T(8,128)(2,1)S(1)} %collective-permute-done.13.m1, ...), custom_call_target="tpu_custom_call" | custom-call | flops 20000000000 | bytes 10000 | tf_op jit(solution)/shard_map/pallas_call | solution.py:336
  45.5 0.3 collective-permute-start.21
  45.8 0.6 shard_map.114
  46.5 3.8 %collective-permute-start.17 = (bf16[32,1792]{1,0:T(8,128)(2,1)S(1)}, bf16[32,1792]{1,0:T(8,128)(2,1)S(1)}, u32[]{:S(2)}, u32[]{:S(2)}) collective-permute-start(bf16[32,1792]{1,0:T(8,128)(2,1)S(1)} %get-tuple-element.72), channel_id=1, source_target_pairs={{0,128},{4,132},{8,136},{12,140},{16,144},{20,148},{24,152},{28,15... | collective-permute-start | bytes 344072 | tf_op jit(solution)/shard_map/ppermute | solution.py:377
  50.2 1.0 %collective-permute-start.18 = (bf16[32,1792]{1,0:T(8,128)(2,1)S(1)}, bf16[32,1792]{1,0:T(8,128)(2,1)S(1)}, u32[]{:S(2)}, u32[]{:S(2)}) collective-permute-start(bf16[32,1792]{1,0:T(8,128)(2,1)S(1)} %get-tuple-element.73), channel_id=1, source_target_pairs={{0,64},{4,68},{8,72},{12,76},{16,80},{20,84},{24,88},{28,92},{32,9... | collective-permute-start | bytes 344072 | tf_op jit(solution)/shard_map/ppermute | solution.py:377
  51.2 0.1 collective-permute-start.19
  51.3 0.0 collective-permute-done.21.rs
  51.3 0.0 collective-permute-done.20.come
  51.3 0.7 shard_map.116
  51.9 3.1 %collective-permute-start.22 = (bf16[32,2304]{1,0:T(8,128)(2,1)S(1)}, bf16[32,2304]{1,0:T(8,128)(2,1)S(1)}, u32[]{:S(2)}, u32[]{:S(2)}) collective-permute-start(bf16[32,2304]{1,0:T(8,128)(2,1)S(1)} %get-tuple-element.78), channel_id=1, source_target_pairs={{0,128},{4,132},{8,136},{12,140},{16,144},{20,148},{24,152},{28,15... | collective-permute-start | bytes 442376 | tf_op jit(solution)/shard_map/ppermute | solution.py:377
  55.1 1.0 %collective-permute-start.23 = (bf16[32,2304]{1,0:T(8,128)(2,1)S(1)}, bf16[32,2304]{1,0:T(8,128)(2,1)S(1)}, u32[]{:S(2)}, u32[]{:S(2)}) collective-permute-start(bf16[32,2304]{1,0:T(8,128)(2,1)S(1)} %get-tuple-element.79), channel_id=1, source_target_pairs={{0,64},{4,68},{8,72},{12,76},{16,80},{20,84},{24,88},{28,92},{32,9... | collective-permute-start | bytes 442376 | tf_op jit(solution)/shard_map/ppermute | solution.py:377
  56.0 0.0 collective-permute-done.17.a2
  56.0 1.7 %collective-permute-start.24 = (bf16[32,2304]{1,0:T(8,128)(2,1)S(1)}, bf16[32,2304]{1,0:T(8,128)(2,1)S(1)}, u32[]{:S(2)}, u32[]{:S(2)}) collective-permute-start(bf16[32,2304]{1,0:T(8,128)(2,1)S(1)} %get-tuple-element.80), channel_id=1, source_target_pairs={{0,192},{4,196},{8,200},{12,204},{16,208},{20,212},{24,216},{28,22... | collective-permute-start | bytes 442376 | tf_op jit(solution)/shard_map/ppermute | solution.py:377
  57.8 3.5 %collective-permute-done.19.a3 = bf16[32,1792]{1,0:T(8,128)(2,1)S(1)} collective-permute-done((bf16[32,1792]{1,0:T(8,128)(2,1)S(1)}, bf16[32,1792]{1,0:T(8,128)(2,1)S(1)}, u32[]{:S(2)}, u32[]{:S(2)}) %collective-permute-start.19) | collective-permute-done | bytes 114720 | tf_op jit(solution)/shard_map/ppermute | solution.py:377
  61.3 0.6 shard_map.115.two
  61.9 0.0 collective-permute-done.22.b2
  61.9 1.6 %collective-permute-done.23.b1 = bf16[32,2304]{1,0:T(8,128)(2,1)S(1)} collective-permute-done((bf16[32,2304]{1,0:T(8,128)(2,1)S(1)}, bf16[32,2304]{1,0:T(8,128)(2,1)S(1)}, u32[]{:S(2)}, u32[]{:S(2)}) %collective-permute-start.23) | collective-permute-done | bytes 147488 | tf_op jit(solution)/shard_map/ppermute | solution.py:377
  63.5 0.2 collective-permute-done.24.b3
  63.7 1.1 %shard_map.117 = bf16[64,2560]{1,0:T(8,128)(2,1)S(1)} custom-call(s32[2]{0:T(128)S(1)} %pad_add_fusion.place, bf16[32,1792]{1,0:T(8,128)(2,1)S(1)} %shard_map.115.two, bf16[32,2304]{1,0:T(8,128)(2,1)S(1)} %get-tuple-element.77.b0, bf16[32,2304]{1,0:T(8,128)(2,1)S(1)} %collective-permute-done.22.b2, bf16[32,2304]{1,0:T(8,128)(2,1)S(1)} %collective-permute-done.23.b1, ...), custom_call_target="tpu_custom_call" | custom-call | flops 100000 | bytes 10000 | tf_op jit(solution)/shard_map/pallas_call | solution.py:336
  64.8 17.2 %all_to_all.5.refs_0_ = bf16[8,8,2560]{2,1,0:T(8,128)(2,1)S(1)} all-to-all(bf16[8,8,2560]{2,1,0:T(8,128)(2,1)S(1)} %bitcast.5), channel_id=1, replica_groups={{0,8,16,24,32,40,48,56},{4,12,20,28,36,44,52,60},{64,72,80,88,96,104,11..., dimensions={0} | all-to-all | bytes 655360 | tf_op jit(solution)/shard_map/all_to_all | solution.py:554
  82.0 0.9 %shard_map.118 = (bf16[192,256]{1,0:T(8,128)(2,1)}, f32[4,1728]{1,0:T(4,128)}, f32[4,1728]{1,0:T(4,128)}) custom-call(bf16[8,8,2560]{2,1,0:T(8,128)(2,1)S(1)} %all_to_all.5.refs_0_), custom_call_target="tpu_custom_call" | custom-call | flops 100000 | bytes 10000 | tf_op jit(solution)/shard_map/pallas_call | solution.py:336
  (8 shorter events, 0.0 us)
Async XLA Ops:
  0.7 6.3 %copy-start = (bf16[256,6912]{1,0:T(8,128)(2,1)S(1)}, bf16[256,6912]{1,0:T(8,128)(2,1)}, u32[]{:S(2)}) copy-start(bf16[256,6912]{1,0:T(8,128)(2,1)} %weight.2) | copy-start | bytes 10616836
  2.8 24.8 %copy-start.1 = (bf16[256,6912]{1,0:T(8,128)(2,1)S(1)}, bf16[256,6912]{1,0:T(8,128)(2,1)}, u32[]{:S(2)}) copy-start(bf16[256,6912]{1,0:T(8,128)(2,1)} %weight.3) | copy-start | bytes 10616836
  2.8 15.8 %collective-permute-start.4 = (bf16[224,512]{1,0:T(8,128)(2,1)S(1)}, bf16[224,512]{1,0:T(8,128)(2,1)S(1)}, u32[]{:S(2)}, u32[]{:S(2)}) collective-permute-start(bf16[224,512]{1,0:T(8,128)(2,1)S(1)} %get-tuple-element.52.p0), channel_id=1, source_target_pairs={{0,2},{1,3},{2,0},{3,1},{4,6},{5,7},{6,4},{7,5},{8,10},{9,11},{10,... | collective-permute-start | bytes 688136 | tf_op jit(solution)/shard_map/ppermute | solution.py:377
  5.0 13.6 %collective-permute-start.5 = (bf16[224,512]{1,0:T(8,128)(2,1)S(1)}, bf16[224,512]{1,0:T(8,128)(2,1)S(1)}, u32[]{:S(2)}, u32[]{:S(2)}) collective-permute-start(bf16[224,512]{1,0:T(8,128)(2,1)S(1)} %get-tuple-element.52.p0), channel_id=1, source_target_pairs={{0,1},{1,0},{2,3},{3,2},{4,5},{5,4},{6,7},{7,6},{8,9},{9,8},{10,11... | collective-permute-start | bytes 688136 | tf_op jit(solution)/shard_map/ppermute | solution.py:377
  6.5 12.2 %collective-permute-start.6 = (bf16[224,512]{1,0:T(8,128)(2,1)S(1)}, bf16[224,512]{1,0:T(8,128)(2,1)S(1)}, u32[]{:S(2)}, u32[]{:S(2)}) collective-permute-start(bf16[224,512]{1,0:T(8,128)(2,1)S(1)} %get-tuple-element.52.p0), channel_id=1, source_target_pairs={{0,3},{1,2},{2,1},{3,0},{4,7},{5,6},{6,5},{7,4},{8,11},{9,10},{10,... | collective-permute-start | bytes 688136 | tf_op jit(solution)/shard_map/ppermute | solution.py:377
  10.1 7.2 %collective-permute-start = (bf16[96,256]{1,0:T(8,128)(2,1)S(1)}, bf16[96,256]{1,0:T(8,128)(2,1)S(1)}, u32[]{:S(2)}, u32[]{:S(2)}) collective-permute-start(bf16[96,256]{1,0:T(8,128)(2,1)S(1)} %get-tuple-element.45), channel_id=1, source_target_pairs={{0,1},{1,0},{2,3},{3,2},{4,8},{5,9},{6,10},{7,11},{8,4},{9,5},{10,... | collective-permute-start | bytes 147464 | tf_op jit(solution)/shard_map/ppermute | solution.py:373
  12.4 4.9 %collective-permute-start.1 = (bf16[96,256]{1,0:T(8,128)(2,1)S(1)}, bf16[96,256]{1,0:T(8,128)(2,1)S(1)}, u32[]{:S(2)}, u32[]{:S(2)}) collective-permute-start(bf16[96,256]{1,0:T(8,128)(2,1)S(1)} %get-tuple-element.46), channel_id=1, source_target_pairs={{0,4},{1,5},{2,6},{3,7},{4,0},{5,1},{6,2},{7,3},{8,12},{9,13},{10,... | collective-permute-start | bytes 147464 | tf_op jit(solution)/shard_map/ppermute | solution.py:373
  17.8 4.2 %collective-permute-start.2 = (bf16[96,256]{1,0:T(8,128)(2,1)S(1)}, bf16[96,256]{1,0:T(8,128)(2,1)S(1)}, u32[]{:S(2)}, u32[]{:S(2)}) collective-permute-start(bf16[96,256]{1,0:T(8,128)(2,1)S(1)} %get-tuple-element.48), channel_id=1, source_target_pairs={{0,4},{1,2},{2,1},{3,7},{4,0},{5,6},{6,5},{7,3},{8,12},{9,10},{10,... | collective-permute-start | bytes 147464 | tf_op jit(solution)/shard_map/ppermute | solution.py:373
  18.5 4.1 %collective-permute-start.3 = (bf16[96,256]{1,0:T(8,128)(2,1)S(1)}, bf16[96,256]{1,0:T(8,128)(2,1)S(1)}, u32[]{:S(2)}, u32[]{:S(2)}) collective-permute-start(bf16[96,256]{1,0:T(8,128)(2,1)S(1)} %get-tuple-element.49.late), channel_id=1, source_target_pairs={{0,1},{1,0},{2,3},{3,2},{4,5},{5,4},{6,7},{7,6},{8,9},{9,8},{10,11... | collective-permute-start | bytes 147464 | tf_op jit(solution)/shard_map/ppermute | solution.py:373
  19.7 11.0 %collective-permute-start.10 = (bf16[768,256]{1,0:T(8,128)(2,1)S(1)}, bf16[768,256]{1,0:T(8,128)(2,1)S(1)}, u32[]{:S(2)}, u32[]{:S(2)}) collective-permute-start(bf16[768,256]{1,0:T(8,128)(2,1)S(1)} %get-tuple-element.55), channel_id=1, source_target_pairs={{0,1},{1,0},{2,3},{3,2},{4,8},{5,9},{6,10},{7,11},{8,4},{9,5},{10,... | collective-permute-start | bytes 1179656 | tf_op jit(solution)/shard_map/ppermute | solution.py:373
  21.7 10.3 %collective-permute-start.11 = (bf16[768,256]{1,0:T(8,128)(2,1)S(1)}, bf16[768,256]{1,0:T(8,128)(2,1)S(1)}, u32[]{:S(2)}, u32[]{:S(2)}) collective-permute-start(bf16[768,256]{1,0:T(8,128)(2,1)S(1)} %get-tuple-element.56), channel_id=1, source_target_pairs={{0,4},{1,5},{2,6},{3,7},{4,0},{5,1},{6,2},{7,3},{8,12},{9,13},{10,... | collective-permute-start | bytes 1179656 | tf_op jit(solution)/shard_map/ppermute | solution.py:373
  23.5 16.7 %collective-permute-start.7 = (bf16[192,512]{1,0:T(8,128)(2,1)S(1)}, bf16[192,512]{1,0:T(8,128)(2,1)S(1)}, u32[]{:S(2)}, u32[]{:S(2)}) collective-permute-start(bf16[192,512]{1,0:T(8,128)(2,1)S(1)} %get-tuple-element.54.g0), channel_id=1, source_target_pairs={{0,2},{1,3},{2,0},{3,1},{4,6},{5,7},{6,4},{7,5},{8,10},{9,11},{10,... | collective-permute-start | bytes 589832 | tf_op jit(solution)/shard_map/ppermute | solution.py:377
  24.5 15.7 %collective-permute-start.8 = (bf16[192,512]{1,0:T(8,128)(2,1)S(1)}, bf16[192,512]{1,0:T(8,128)(2,1)S(1)}, u32[]{:S(2)}, u32[]{:S(2)}) collective-permute-start(bf16[192,512]{1,0:T(8,128)(2,1)S(1)} %get-tuple-element.54.g0), channel_id=1, source_target_pairs={{0,1},{1,0},{2,3},{3,2},{4,5},{5,4},{6,7},{7,6},{8,9},{9,8},{10,11... | collective-permute-start | bytes 589832 | tf_op jit(solution)/shard_map/ppermute | solution.py:377
  27.1 13.1 %collective-permute-start.9 = (bf16[192,512]{1,0:T(8,128)(2,1)S(1)}, bf16[192,512]{1,0:T(8,128)(2,1)S(1)}, u32[]{:S(2)}, u32[]{:S(2)}) collective-permute-start(bf16[192,512]{1,0:T(8,128)(2,1)S(1)} %get-tuple-element.54.g0), channel_id=1, source_target_pairs={{0,3},{1,2},{2,1},{3,0},{4,7},{5,6},{6,5},{7,4},{8,11},{9,10},{10,... | collective-permute-start | bytes 589832 | tf_op jit(solution)/shard_map/ppermute | solution.py:377
  30.7 6.5 %collective-permute-start.12 = (bf16[96,256]{1,0:T(8,128)(2,1)S(1)}, bf16[96,256]{1,0:T(8,128)(2,1)S(1)}, u32[]{:S(2)}, u32[]{:S(2)}) collective-permute-start(bf16[96,256]{1,0:T(8,128)(2,1)S(1)} %get-tuple-element.61), channel_id=1, source_target_pairs={{0,1},{1,0},{2,3},{3,2},{4,8},{5,9},{6,10},{7,11},{8,4},{9,5},{10,... | collective-permute-start | bytes 147464 | tf_op jit(solution)/shard_map/ppermute | solution.py:373
  32.0 5.2 %collective-permute-start.13 = (bf16[96,256]{1,0:T(8,128)(2,1)S(1)}, bf16[96,256]{1,0:T(8,128)(2,1)S(1)}, u32[]{:S(2)}, u32[]{:S(2)}) collective-permute-start(bf16[96,256]{1,0:T(8,128)(2,1)S(1)} %get-tuple-element.62), channel_id=1, source_target_pairs={{0,4},{1,5},{2,6},{3,7},{4,0},{5,1},{6,2},{7,3},{8,12},{9,13},{10,... | collective-permute-start | bytes 147464 | tf_op jit(solution)/shard_map/ppermute | solution.py:373
  37.8 6.8 %collective-permute-start.15 = (bf16[96,256]{1,0:T(8,128)(2,1)S(1)}, bf16[96,256]{1,0:T(8,128)(2,1)S(1)}, u32[]{:S(2)}, u32[]{:S(2)}) collective-permute-start(bf16[96,256]{1,0:T(8,128)(2,1)S(1)} %get-tuple-element.66), channel_id=1, source_target_pairs={{0,4},{1,2},{2,1},{3,7},{4,0},{5,6},{6,5},{7,3},{8,12},{9,10},{10,... | collective-permute-start | bytes 147464 | tf_op jit(solution)/shard_map/ppermute | solution.py:373
  40.2 4.3 %collective-permute-start.16 = (bf16[96,256]{1,0:T(8,128)(2,1)S(1)}, bf16[96,256]{1,0:T(8,128)(2,1)S(1)}, u32[]{:S(2)}, u32[]{:S(2)}) collective-permute-start(bf16[96,256]{1,0:T(8,128)(2,1)S(1)} %get-tuple-element.63.late), channel_id=1, source_target_pairs={{0,1},{1,0},{2,3},{3,2},{4,5},{5,4},{6,7},{7,6},{8,9},{9,8},{10,11... | collective-permute-start | bytes 147464 | tf_op jit(solution)/shard_map/ppermute | solution.py:373
  41.9 3.9 %collective-permute-start.14 = (f32[128,1792]{1,0:T(8,128)S(1)}, f32[128,1792]{1,0:T(8,128)S(1)}, u32[]{:S(2)}, u32[]{:S(2)}) collective-permute-start(f32[128,1792]{1,0:T(8,128)S(1)} %get-tuple-element.65), channel_id=1, source_target_pairs={{0,4},{4,0},{8,12},{12,8},{16,20},{20,16},{24,28},{28,24},{32,36},... | collective-permute-start | bytes 2752520 | tf_op jit(solution)/shard_map/ppermute | solution.py:377
  43.9 7.3 %collective-permute-start.20 = (bf16[128,1792]{1,0:T(8,128)(2,1)S(1)}, bf16[128,1792]{1,0:T(8,128)(2,1)S(1)}, u32[]{:S(2)}, u32[]{:S(2)}) collective-permute-start(bf16[128,1792]{1,0:T(8,128)(2,1)S(1)} %get-tuple-element.75), channel_id=1, source_target_pairs={{0,4},{4,0},{8,12},{12,8},{16,20},{20,16},{24,28},{28,24},{32,36},... | collective-permute-start | bytes 1376264 | tf_op jit(solution)/shard_map/ppermute | solution.py:377
  45.5 5.8 %collective-permute-start.21 = (bf16[128,256]{1,0:T(8,128)(2,1)S(1)}, bf16[128,256]{1,0:T(8,128)(2,1)S(1)}, u32[]{:S(2)}, u32[]{:S(2)}) collective-permute-start(bf16[128,256]{1,0:T(8,128)(2,1)S(1)} %get-tuple-element.76), channel_id=1, source_target_pairs={{0,4},{4,0},{8,12},{12,8},{16,20},{20,16},{24,28},{28,24},{32,36},... | collective-permute-start | bytes 196616 | tf_op jit(solution)/shard_map/ppermute | solution.py:377
  46.5 9.6 %collective-permute-start.17 = (bf16[32,1792]{1,0:T(8,128)(2,1)S(1)}, bf16[32,1792]{1,0:T(8,128)(2,1)S(1)}, u32[]{:S(2)}, u32[]{:S(2)}) collective-permute-start(bf16[32,1792]{1,0:T(8,128)(2,1)S(1)} %get-tuple-element.72), channel_id=1, source_target_pairs={{0,128},{4,132},{8,136},{12,140},{16,144},{20,148},{24,152},{28,15... | collective-permute-start | bytes 344072 | tf_op jit(solution)/shard_map/ppermute | solution.py:377
  50.2 7.6 %collective-permute-start.18 = (bf16[32,1792]{1,0:T(8,128)(2,1)S(1)}, bf16[32,1792]{1,0:T(8,128)(2,1)S(1)}, u32[]{:S(2)}, u32[]{:S(2)}) collective-permute-start(bf16[32,1792]{1,0:T(8,128)(2,1)S(1)} %get-tuple-element.73), channel_id=1, source_target_pairs={{0,64},{4,68},{8,72},{12,76},{16,80},{20,84},{24,88},{28,92},{32,9... | collective-permute-start | bytes 344072 | tf_op jit(solution)/shard_map/ppermute | solution.py:377
  51.2 10.1 %collective-permute-start.19 = (bf16[32,1792]{1,0:T(8,128)(2,1)S(1)}, bf16[32,1792]{1,0:T(8,128)(2,1)S(1)}, u32[]{:S(2)}, u32[]{:S(2)}) collective-permute-start(bf16[32,1792]{1,0:T(8,128)(2,1)S(1)} %get-tuple-element.74), channel_id=1, source_target_pairs={{0,192},{4,196},{8,200},{12,204},{16,208},{20,212},{24,216},{28,22... | collective-permute-start | bytes 344072 | tf_op jit(solution)/shard_map/ppermute | solution.py:377
  51.9 9.9 %collective-permute-start.22 = (bf16[32,2304]{1,0:T(8,128)(2,1)S(1)}, bf16[32,2304]{1,0:T(8,128)(2,1)S(1)}, u32[]{:S(2)}, u32[]{:S(2)}) collective-permute-start(bf16[32,2304]{1,0:T(8,128)(2,1)S(1)} %get-tuple-element.78), channel_id=1, source_target_pairs={{0,128},{4,132},{8,136},{12,140},{16,144},{20,148},{24,152},{28,15... | collective-permute-start | bytes 442376 | tf_op jit(solution)/shard_map/ppermute | solution.py:377
  55.1 8.4 %collective-permute-start.23 = (bf16[32,2304]{1,0:T(8,128)(2,1)S(1)}, bf16[32,2304]{1,0:T(8,128)(2,1)S(1)}, u32[]{:S(2)}, u32[]{:S(2)}) collective-permute-start(bf16[32,2304]{1,0:T(8,128)(2,1)S(1)} %get-tuple-element.79), channel_id=1, source_target_pairs={{0,64},{4,68},{8,72},{12,76},{16,80},{20,84},{24,88},{28,92},{32,9... | collective-permute-start | bytes 442376 | tf_op jit(solution)/shard_map/ppermute | solution.py:377
  56.0 7.6 %collective-permute-start.24 = (bf16[32,2304]{1,0:T(8,128)(2,1)S(1)}, bf16[32,2304]{1,0:T(8,128)(2,1)S(1)}, u32[]{:S(2)}, u32[]{:S(2)}) collective-permute-start(bf16[32,2304]{1,0:T(8,128)(2,1)S(1)} %get-tuple-element.80), channel_id=1, source_target_pairs={{0,192},{4,196},{8,200},{12,204},{16,208},{20,212},{24,216},{28,22... | collective-permute-start | bytes 442376 | tf_op jit(solution)/shard_map/ppermute | solution.py:377

commit v9 on v8

--- a/solution.py
+++ b/solution.py
@@ -283,7 +283,8 @@
     out[...] = total.astype(BF)
 
 
-def line_one_kernel(place, two, b0, b2, b1, b3, out):
+def line_one_kernel(place, two, b0, b2, b1, b3, *outs_and_whole):
+    outs, whole = outs_and_whole[:-1], outs_and_whole[-1]
     line = place[0] // 16
     to, at = iota((64, 32), 0), iota((64, 32), 1)
     for n in range(7):
@@ -295,7 +296,7 @@
         for which, value in ((0, total.astype(BF)), (1, two[:, lanes])):
             spot = ((to % 8) // 4 == which) & (at == 4 * (to // 8) + to % 4)
             block = block + mm(onehot(spot), value)
-        out[:, lanes] = block.astype(BF)
+        whole[:, lanes] = block
     for n in range(3):
         index = 8 * n + to % 8
         total = jnp.zeros((64, C), F32)
@@ -304,20 +305,34 @@
             for core in range(2):
                 spot = onehot(from_line & ((index % 6) // 3 == core))
                 total = total + mm(spot, part[:, (7 + core) * C : (8 + core) * C])
-        out[:, (7 + n) * C : (8 + n) * C] = total.astype(BF)
-
-
-def final_kernel(scale, arrived, rows, one, two):
-    total = jnp.sum(arrived[:, :, 0 : 7 * C].astype(F32), axis=0) * scale
-    one[...] = total[0:4, 0:QW]
-    two[...] = total[4:8, 0:QW]
+        whole[:, (7 + n) * C : (8 + n) * C] = total
+    chip = (place[0] // 2) % 8
+    for turn, out in enumerate(outs):
+        part = whole[pl.ds(pl.multiple_of(8 * (chip ^ turn), 8), 8), :]
+        out[...] = jnp.concatenate([part[:, 0 : 5 * C], part[:, 5 * C : 10 * C]], axis=0).astype(BF)
+
+
+def final_kernel(scale, place, *refs):
+    arrived, (rows, one, two, spread) = refs[:-4], refs[-4:]
+    chip = (place[0] // 2) % 8
+    total = jnp.zeros((16, 5 * C), F32)
+    for (turn, _), ref in zip(TURNS, arrived):
+        part = ref[...].astype(F32)
+        total = total + part
+        spread[pl.ds(pl.multiple_of(8 * (chip ^ turn), 8), 8), :] = part[8:16, 2 * C : 5 * C]
+    total = total * scale
+    for out, at in ((one, 0), (two, 4)):
+        out[:, 0 : 5 * C] = total[at : at + 4, :]
+        out[:, 5 * C : QW] = total[8 + at : 12 + at, 0 : QW - 5 * C]
     to, at = iota((S, 64), 0), iota((S, 64), 1)
     value = jnp.zeros((S, C), F32)
     for n in range(3):
         spot = (at // 8 == (to // 6) % 8) & (8 * n + at % 8 == 6 * (to // 48) + to % 6)
-        piece = arrived[:, :, (7 + n) * C : (8 + n) * C].reshape(64, C)
-        value = value + mm(onehot(spot), piece)
+        value = value + mm(onehot(spot), spread[:, n * C : (n + 1) * C].astype(BF))
     rows[...] = value.astype(BF)
+
+
+TURNS = ((0, 0), (4, 8), (3, 6), (5, 10), (2, 4), (6, 12), (1, 2), (7, 14))
 
 
 def sds(shape, dtype):
@@ -392,8 +407,7 @@
 
 
 def body(features, pre_act, grad_out, weight_one, weight_two, neighbours, halo_list, send_list):
-    gx = lax.axis_size("gx")
-    scale = 1.0 / math.sqrt(S * gx * lax.axis_size("gy"))
+    scale = 1.0 / math.sqrt(S * lax.axis_size("gx") * lax.axis_size("gy"))
     place = jnp.stack([lax.axis_index("gx"), lax.axis_index("gy")]).astype(jnp.int32)
     tile = sds((S, C), BF)
     pay, nbt, hrow, srow, pre, grad = call(
@@ -549,19 +563,22 @@
     sum_two = call(
         line_two_kernel, sds((32, wide), BF), place, *lines(two), flops=2 * 10**10
     )
-    summed = call(line_one_kernel, sds((64, 10 * C), BF), place, sum_two, *lines(one))
-    groups = [[16 * y + 2 * z + e for z in range(8)] for y in range(4) for e in range(2)]
-    collected = lax.all_to_all(
-        summed.reshape(8, 8, 10 * C),
-        "gx",
-        split_axis=0,
-        concat_axis=0,
-        tiled=True,
-        axis_index_groups=groups,
-    )
+    pieces = call(
+        line_one_kernel,
+        (sds((16, 5 * C), BF),) * 8,
+        place,
+        sum_two,
+        *lines(one),
+        scratch=[pltpu.VMEM((64, 10 * C), F32)],
+    )
+    collected = [cross(pieces[turn], "gx", mask) if mask else pieces[0] for turn, mask in TURNS]
     out = sds((4, QW), F32)
     return call(
-        lambda *refs: final_kernel(scale, *refs), (tile, out, out), collected, specs=[VM]
+        functools.partial(final_kernel, scale),
+        (tile, out, out),
+        place,
+        *collected,
+        scratch=[pltpu.VMEM((64, 3 * C), F32)],
     )
 
 

time: 83.7 us -> 85.2 us (1.018)
  blocking collectives: 17.2 us -> 0 us
  starting transfers between devices: 29.1 us -> 42.7 us
  waiting for transfers between devices: 11 us -> 15.1 us
    all_to_all x1 -> x0, blocking collectives: 17.2 us -> none  [body(): lax.all_to_all(summed.reshape(8, 8, 10 * C), 'gx', split_axis=0, concat_a...]
    ppermute x15 -> x22, starting transfers between devices: 20.2 us -> 33.9 us  [cross(): lax.ppermute(value, axis, [(n, n ^ mask) for n in range(lax.axis_size(axi...]
    ppermute x15 -> x22, waiting for transfers between devices: 5.3 us -> 9.38 us  [cross(): lax.ppermute(value, axis, [(n, n ^ mask) for n in range(lax.axis_size(axi...]
  transfers between devices with their start and end apart: 25 -> 32, of which waited for: 6 -> 8; matrix products, arithmetic and copies ran while one was open for 0% -> 0% of each run, Pallas kernels for 25% -> 25%
where the time goes in v9:
time: 85.2 us; the launch traced here: 84 us
  starting transfers between devices  42.7 us (50%)
  Pallas kernels  25.3 us (30%)
  waiting for transfers between devices  15.1 us (18%)
    ppermute x22, starting transfers between devices, cross(): lax.ppermute(value, axis, [(n, n ^ mask) for n in range(lax.axis_size(axi...  33.9 us
    pallas_call x16, Pallas kernels, call(): pl.pallas_call(kernel, out_shape=outs, in_specs=specs, out_specs=jax.tree...  25.3 us
    ppermute x22, waiting for transfers between devices, cross(): lax.ppermute(value, axis, [(n, n ^ mask) for n in range(lax.axis_size(axi...  9.38 us
    ppermute x10, starting transfers between devices, swap(): return lax.ppermute(value, ('gx', 'gy'), pairs)  8.83 us
    ppermute x10, waiting for transfers between devices, swap(): return lax.ppermute(value, ('gx', 'gy'), pairs)  5.74 us
  transfers between devices with their start and end apart: 32, of which 8 were waited for; matrix products, arithmetic and copies ran while one was open for 0% of the time, Pallas kernels for 25%

profile of v9, /device:TPU:2, one launch (start us, length us, event | category | flops | bytes accessed | tf_op | source)
XLA Modules:
  0.0 84.0 jit_solution(12804467005920302008)
XLA Ops:
  0.6 0.1 pad_add_fusion.place
  0.7 2.1 %shard_map.103 = (bf16[224,512]{1,0:T(8,128)(2,1)S(1)}, f32[32,256]{1,0:T(8,128)S(1)}, s32[8,256]{1,0:T(8,128)S(1)}, s32[8,256]{1,0:T(8,128)S(1)}, bf16[192,256]...) custom-call(s32[2]{0:T(128)S(1)} %pad_add_fusion.place, bf16[192,256]{1,0:T(8,128)(2,1)} %feat.1, bf16[192,256]{1,0:T(8,128)(2,1)} %pre.1, ...), custom_call_target="tpu_custom_call" | custom-call | flops 4000000000 | bytes 10000 | tf_op jit(solution)/shard_map/pallas_call | solution.py:351
  2.8 0.0 copy-start.1
  2.8 2.2 %collective-permute-start.4 = (bf16[224,512]{1,0:T(8,128)(2,1)S(1)}, bf16[224,512]{1,0:T(8,128)(2,1)S(1)}, u32[]{:S(2)}, u32[]{:S(2)}) collective-permute-start(bf16[224,512]{1,0:T(8,128)(2,1)S(1)} %get-tuple-element.60.p0), channel_id=1, source_target_pairs={{0,2},{1,3},{2,0},{3,1},{4,6},{5,7},{6,4},{7,5},{8,10},{9,11},{10,... | collective-permute-start | bytes 688136 | tf_op jit(solution)/shard_map/ppermute | solution.py:392
  5.0 1.4 %collective-permute-start.5 = (bf16[224,512]{1,0:T(8,128)(2,1)S(1)}, bf16[224,512]{1,0:T(8,128)(2,1)S(1)}, u32[]{:S(2)}, u32[]{:S(2)}) collective-permute-start(bf16[224,512]{1,0:T(8,128)(2,1)S(1)} %get-tuple-element.60.p0), channel_id=1, source_target_pairs={{0,1},{1,0},{2,3},{3,2},{4,5},{5,4},{6,7},{7,6},{8,9},{9,8},{10,11... | collective-permute-start | bytes 688136 | tf_op jit(solution)/shard_map/ppermute | solution.py:392
  6.5 0.5 collective-permute-start.6
  7.0 3.0 %shard_map.104 = (f32[192,256]{1,0:T(8,128)S(1)}, bf16[96,256]{1,0:T(8,128)(2,1)S(1)}, bf16[96,256]{1,0:T(8,128)(2,1)S(1)}, bf16[64,256]{1,0:T(8,128)(2,1)S(1)}) custom-call(s32[2]{0:T(128)S(1)} %pad_add_fusion.place, f32[32,256]{1,0:T(8,128)S(1)} %get-tuple-element.50.nbt, bf16[192,256]{1,0:T(8,128)(2,1)S(1)} %get-tuple-element.51.grad, ...), custom_call_target="tpu_custom_call" | custom-call | flops 100000 | bytes 10000 | tf_op jit(solution)/shard_map/pallas_call | solution.py:351
  10.1 2.4 %collective-permute-start = (bf16[96,256]{1,0:T(8,128)(2,1)S(1)}, bf16[96,256]{1,0:T(8,128)(2,1)S(1)}, u32[]{:S(2)}, u32[]{:S(2)}) collective-permute-start(bf16[96,256]{1,0:T(8,128)(2,1)S(1)} %get-tuple-element.53), channel_id=1, source_target_pairs={{0,1},{1,0},{2,3},{3,2},{4,8},{5,9},{6,10},{7,11},{8,4},{9,5},{10,... | collective-permute-start | bytes 147464 | tf_op jit(solution)/shard_map/ppermute | solution.py:388
  12.4 0.0 collective-permute-start.1
  12.4 4.9 %collective-permute-done.m2 = bf16[96,256]{1,0:T(8,128)(2,1)S(1)} collective-permute-done((bf16[96,256]{1,0:T(8,128)(2,1)S(1)}, bf16[96,256]{1,0:T(8,128)(2,1)S(1)}, u32[]{:S(2)}, u32[]{:S(2)}) %collective-permute-start) | collective-permute-done | bytes 49184 | tf_op jit(solution)/shard_map/ppermute | solution.py:388
  17.3 0.6 shard_map.105
  17.8 0.6 collective-permute-start.2
  18.5 0.2 collective-permute-start.3
  18.6 1.1 %shard_map.106 = (bf16[768,256]{1,0:T(8,128)(2,1)S(1)}, bf16[768,256]{1,0:T(8,128)(2,1)S(1)}, bf16[4,64,512]{2,1,0:T(8,128)(2,1)S(1)}) custom-call(s32[2]{0:T(128)S(1)} %pad_add_fusion.place, bf16[224,512]{1,0:T(8,128)(2,1)S(1)} %get-tuple-element.60.p0, bf16[224,512]{1,0:T(8,128)(2,1)S(1)} %collective-permute-done.4.p2, ...), custom_call_target="tpu_custom_call" | custom-call | flops 100000 | bytes 10000 | tf_op jit(solution)/shard_map/pallas_call | solution.py:351
  19.7 2.0 %collective-permute-start.10 = (bf16[768,256]{1,0:T(8,128)(2,1)S(1)}, bf16[768,256]{1,0:T(8,128)(2,1)S(1)}, u32[]{:S(2)}, u32[]{:S(2)}) collective-permute-start(bf16[768,256]{1,0:T(8,128)(2,1)S(1)} %get-tuple-element.63), channel_id=1, source_target_pairs={{0,1},{1,0},{2,3},{3,2},{4,8},{5,9},{6,10},{7,11},{8,4},{9,5},{10,... | collective-permute-start | bytes 1179656 | tf_op jit(solution)/shard_map/ppermute | solution.py:388
  21.7 0.0 collective-permute-start.11
  21.7 0.3 collective-permute-done.2.n2
  22.0 0.5 collective-permute-done.3.n1
  22.6 0.9 %shard_map.107 = (bf16[192,256]{1,0:T(8,128)(2,1)S(1)}, bf16[192,512]{1,0:T(8,128)(2,1)S(1)}) custom-call(s32[2]{0:T(128)S(1)} %pad_add_fusion.place, f32[192,256]{1,0:T(8,128)S(1)} %get-tuple-element.52.late.own, bf16[96,256]{1,0:T(8,128)(2,1)S(1)} %collective-permute-done.m2, bf16[96,256]{1,0:T(8,128)(2,1)S(1)} %collective-permute-done.1.m1, ...), custom_call_target="tpu_custom_call" | custom-call | flops 100000 | bytes 10000 | tf_op jit(solution)/shard_map/pallas_call | solution.py:351
  23.5 1.0 %collective-permute-start.7 = (bf16[192,512]{1,0:T(8,128)(2,1)S(1)}, bf16[192,512]{1,0:T(8,128)(2,1)S(1)}, u32[]{:S(2)}, u32[]{:S(2)}) collective-permute-start(bf16[192,512]{1,0:T(8,128)(2,1)S(1)} %get-tuple-element.62.g0), channel_id=1, source_target_pairs={{0,2},{1,3},{2,0},{3,1},{4,6},{5,7},{6,4},{7,5},{8,10},{9,11},{10,... | collective-permute-start | bytes 589832 | tf_op jit(solution)/shard_map/ppermute | solution.py:392
  24.5 2.6 %collective-permute-start.8 = (bf16[192,512]{1,0:T(8,128)(2,1)S(1)}, bf16[192,512]{1,0:T(8,128)(2,1)S(1)}, u32[]{:S(2)}, u32[]{:S(2)}) collective-permute-start(bf16[192,512]{1,0:T(8,128)(2,1)S(1)} %get-tuple-element.62.g0), channel_id=1, source_target_pairs={{0,1},{1,0},{2,3},{3,2},{4,5},{5,4},{6,7},{7,6},{8,9},{9,8},{10,11... | collective-permute-start | bytes 589832 | tf_op jit(solution)/shard_map/ppermute | solution.py:392
  27.1 0.5 collective-permute-start.9
  27.7 3.0 %shard_map.108 = (f32[192,256]{1,0:T(8,128)S(1)}, bf16[96,256]{1,0:T(8,128)(2,1)S(1)}, bf16[96,256]{1,0:T(8,128)(2,1)S(1)}, bf16[64,256]{1,0:T(8,128)(2,1)S(1)}) custom-call(s32[2]{0:T(128)S(1)} %pad_add_fusion.place, f32[32,256]{1,0:T(8,128)S(1)} %get-tuple-element.50.nbt, bf16[192,256]{1,0:T(8,128)(2,1)S(1)} %get-tuple-element.65.grad, ...), custom_call_target="tpu_custom_call" | custom-call | flops 4000000000 | bytes 10000 | tf_op jit(solution)/shard_map/pallas_call | solution.py:351
  30.7 0.0 collective-permute-done.10.r2
  30.7 1.3 %collective-permute-start.12 = (bf16[96,256]{1,0:T(8,128)(2,1)S(1)}, bf16[96,256]{1,0:T(8,128)(2,1)S(1)}, u32[]{:S(2)}, u32[]{:S(2)}) collective-permute-start(bf16[96,256]{1,0:T(8,128)(2,1)S(1)} %get-tuple-element.69), channel_id=1, source_target_pairs={{0,1},{1,0},{2,3},{3,2},{4,8},{5,9},{6,10},{7,11},{8,4},{9,5},{10,... | collective-permute-start | bytes 147464 | tf_op jit(solution)/shard_map/ppermute | solution.py:388
  32.0 0.0 collective-permute-done.11.r1
  32.0 0.0 collective-permute-start.13
  32.0 5.1 %shard_map.109 = (bf16[768,1792]{1,0:T(8,128)(2,1)S(1)}, bf16[768,1792]{1,0:T(8,128)(2,1)S(1)}) custom-call(s32[2]{0:T(128)S(1)} %pad_add_fusion.place, bf16[224,512]{1,0:T(8,128)(2,1)S(1)} %get-tuple-element.60.p0, bf16[224,512]{1,0:T(8,128)(2,1)S(1)} %collective-permute-done.4.p2, bf16[224,512]{1,0:T(8,128)(2,1)S(1)} %collective-permute-done.5.p1, ...), custom_call_target="tpu_custom_call" | custom-call | flops 4000000000 | bytes 10000 | tf_op jit(solution)/shard_map/pallas_call | solution.py:351
  37.2 0.0 collective-permute-done.13.m1
  37.2 0.6 shard_map.110
  37.8 2.4 %collective-permute-start.15 = (bf16[96,256]{1,0:T(8,128)(2,1)S(1)}, bf16[96,256]{1,0:T(8,128)(2,1)S(1)}, u32[]{:S(2)}, u32[]{:S(2)}) collective-permute-start(bf16[96,256]{1,0:T(8,128)(2,1)S(1)} %get-tuple-element.74), channel_id=1, source_target_pairs={{0,4},{1,2},{2,1},{3,7},{4,0},{5,6},{6,5},{7,3},{8,12},{9,10},{10,... | collective-permute-start | bytes 147464 | tf_op jit(solution)/shard_map/ppermute | solution.py:388
  40.2 0.0 collective-permute-done.7.g2
  40.2 0.0 collective-permute-done.8.g1
  40.2 1.7 %shard_map.111 = (f32[128,1792]{1,0:T(8,128)S(1)}, f32[128,1792]{1,0:T(8,128)S(1)}) custom-call(s32[2]{0:T(128)S(1)} %pad_add_fusion.place, bf16[192,512]{1,0:T(8,128)(2,1)S(1)} %get-tuple-element.62.g0, bf16[192,512]{1,0:T(8,128)(2,1)S(1)} %collective-permute-done.7.g2, bf16[192,512]{1,0:T(8,128)(2,1)S(1)} %collective-permute-done.8.g1, ...), custom_call_target="tpu_custom_call" | custom-call | flops 4000000000 | bytes 10000 | tf_op jit(solution)/shard_map/pallas_call | solution.py:351
  41.9 0.3 collective-permute-start.14
  42.2 1.7 %shard_map.112 = (bf16[128,1792]{1,0:T(8,128)(2,1)S(1)}, bf16[128,1792]{1,0:T(8,128)(2,1)S(1)}) custom-call(s32[2]{0:T(128)S(1)} %pad_add_fusion.place, bf16[192,512]{1,0:T(8,128)(2,1)S(1)} %get-tuple-element.62.g0, bf16[192,512]{1,0:T(8,128)(2,1)S(1)} %collective-permute-done.7.g2, bf16[192,512]{1,0:T(8,128)(2,1)S(1)} %collective-permute-done.8.g1, ...), custom_call_target="tpu_custom_call" | custom-call | flops 100000 | bytes 10000 | tf_op jit(solution)/shard_map/pallas_call | solution.py:351
  43.9 0.6 collective-permute-start.20
  44.5 0.0 collective-permute-done.15.n2
  44.5 0.0 collective-permute-done.16.n1
  44.5 1.0 %shard_map.113 = (bf16[128,256]{1,0:T(8,128)(2,1)S(1)}, bf16[128,256]{1,0:T(8,128)(2,1)S(1)}) custom-call(s32[2]{0:T(128)S(1)} %pad_add_fusion.place, f32[192,256]{1,0:T(8,128)S(1)} %get-tuple-element.66.late.own, bf16[96,256]{1,0:T(8,128)(2,1)S(1)} %collective-permute-done.12.m2, bf16[96,256]{1,0:T(8,128)(2,1)S(1)} %collective-permute-done.13.m1, ...), custom_call_target="tpu_custom_call" | custom-call | flops 20000000000 | bytes 10000 | tf_op jit(solution)/shard_map/pallas_call | solution.py:351
  45.5 0.3 collective-permute-start.21
  45.8 0.6 shard_map.114
  46.5 3.8 %collective-permute-start.17 = (bf16[32,1792]{1,0:T(8,128)(2,1)S(1)}, bf16[32,1792]{1,0:T(8,128)(2,1)S(1)}, u32[]{:S(2)}, u32[]{:S(2)}) collective-permute-start(bf16[32,1792]{1,0:T(8,128)(2,1)S(1)} %get-tuple-element.80), channel_id=1, source_target_pairs={{0,128},{4,132},{8,136},{12,140},{16,144},{20,148},{24,152},{28,15... | collective-permute-start | bytes 344072 | tf_op jit(solution)/shard_map/ppermute | solution.py:392
  50.2 1.0 %collective-permute-start.18 = (bf16[32,1792]{1,0:T(8,128)(2,1)S(1)}, bf16[32,1792]{1,0:T(8,128)(2,1)S(1)}, u32[]{:S(2)}, u32[]{:S(2)}) collective-permute-start(bf16[32,1792]{1,0:T(8,128)(2,1)S(1)} %get-tuple-element.81), channel_id=1, source_target_pairs={{0,64},{4,68},{8,72},{12,76},{16,80},{20,84},{24,88},{28,92},{32,9... | collective-permute-start | bytes 344072 | tf_op jit(solution)/shard_map/ppermute | solution.py:392
  51.2 0.1 collective-permute-start.19
  51.3 0.7 shard_map.116
  51.9 3.1 %collective-permute-start.22 = (bf16[32,2304]{1,0:T(8,128)(2,1)S(1)}, bf16[32,2304]{1,0:T(8,128)(2,1)S(1)}, u32[]{:S(2)}, u32[]{:S(2)}) collective-permute-start(bf16[32,2304]{1,0:T(8,128)(2,1)S(1)} %get-tuple-element.86), channel_id=1, source_target_pairs={{0,128},{4,132},{8,136},{12,140},{16,144},{20,148},{24,152},{28,15... | collective-permute-start | bytes 442376 | tf_op jit(solution)/shard_map/ppermute | solution.py:392
  55.1 1.0 %collective-permute-start.23 = (bf16[32,2304]{1,0:T(8,128)(2,1)S(1)}, bf16[32,2304]{1,0:T(8,128)(2,1)S(1)}, u32[]{:S(2)}, u32[]{:S(2)}) collective-permute-start(bf16[32,2304]{1,0:T(8,128)(2,1)S(1)} %get-tuple-element.87), channel_id=1, source_target_pairs={{0,64},{4,68},{8,72},{12,76},{16,80},{20,84},{24,88},{28,92},{32,9... | collective-permute-start | bytes 442376 | tf_op jit(solution)/shard_map/ppermute | solution.py:392
  56.0 1.7 %collective-permute-start.24 = (bf16[32,2304]{1,0:T(8,128)(2,1)S(1)}, bf16[32,2304]{1,0:T(8,128)(2,1)S(1)}, u32[]{:S(2)}, u32[]{:S(2)}) collective-permute-start(bf16[32,2304]{1,0:T(8,128)(2,1)S(1)} %get-tuple-element.88), channel_id=1, source_target_pairs={{0,192},{4,196},{8,200},{12,204},{16,208},{20,212},{24,216},{28,22... | collective-permute-start | bytes 442376 | tf_op jit(solution)/shard_map/ppermute | solution.py:392
  57.8 3.5 %collective-permute-done.19.a3 = bf16[32,1792]{1,0:T(8,128)(2,1)S(1)} collective-permute-done((bf16[32,1792]{1,0:T(8,128)(2,1)S(1)}, bf16[32,1792]{1,0:T(8,128)(2,1)S(1)}, u32[]{:S(2)}, u32[]{:S(2)}) %collective-permute-start.19) | collective-permute-done | bytes 114720 | tf_op jit(solution)/shard_map/ppermute | solution.py:392
  61.2 0.6 shard_map.115.two
  61.9 1.6 %collective-permute-done.23.b1 = bf16[32,2304]{1,0:T(8,128)(2,1)S(1)} collective-permute-done((bf16[32,2304]{1,0:T(8,128)(2,1)S(1)}, bf16[32,2304]{1,0:T(8,128)(2,1)S(1)}, u32[]{:S(2)}, u32[]{:S(2)}) %collective-permute-start.23) | collective-permute-done | bytes 147488 | tf_op jit(solution)/shard_map/ppermute | solution.py:392
  63.5 0.2 collective-permute-done.24.b3
  63.7 1.1 %shard_map.117 = (bf16[16,1280]{1,0:T(8,128)(2,1)S(1)}, bf16[16,1280]{1,0:T(8,128)(2,1)S(1)}, bf16[16,1280]{1,0:T(8,128)(2,1)S(1)}, bf16[16,1280]{1,0:T(8,128)(2...) custom-call(s32[2]{0:T(128)S(1)} %pad_add_fusion.place, ...), custom_call_target="tpu_custom_call" | custom-call | flops 100000 | bytes 10000 | tf_op jit(solution)/shard_map/pallas_call | solution.py:351
  64.8 3.1 %collective-permute-start.25 = (bf16[16,1280]{1,0:T(8,128)(2,1)S(1)}, bf16[16,1280]{1,0:T(8,128)(2,1)S(1)}, u32[]{:S(2)}, u32[]{:S(2)}) collective-permute-start(bf16[16,1280]{1,0:T(8,128)(2,1)S(1)} %get-tuple-element.90), channel_id=1, source_target_pairs={{0,32},{4,36},{8,40},{12,44},{16,48},{20,52},{24,56},{28,60},{32,0... | collective-permute-start | bytes 122888 | tf_op jit(solution)/shard_map/ppermute | solution.py:392
  67.9 2.4 %collective-permute-start.26 = (bf16[16,1280]{1,0:T(8,128)(2,1)S(1)}, bf16[16,1280]{1,0:T(8,128)(2,1)S(1)}, u32[]{:S(2)}, u32[]{:S(2)}) collective-permute-start(bf16[16,1280]{1,0:T(8,128)(2,1)S(1)} %get-tuple-element.91), channel_id=1, source_target_pairs={{0,24},{4,28},{8,16},{12,20},{16,8},{20,12},{24,0},{28,4},{32,56},... | collective-permute-start | bytes 122888 | tf_op jit(solution)/shard_map/ppermute | solution.py:392
  70.2 1.5 %collective-permute-start.27 = (bf16[16,1280]{1,0:T(8,128)(2,1)S(1)}, bf16[16,1280]{1,0:T(8,128)(2,1)S(1)}, u32[]{:S(2)}, u32[]{:S(2)}) collective-permute-start(bf16[16,1280]{1,0:T(8,128)(2,1)S(1)} %get-tuple-element.92), channel_id=1, source_target_pairs={{0,40},{4,44},{8,32},{12,36},{16,56},{20,60},{24,48},{28,52},{32,8... | collective-permute-start | bytes 122888 | tf_op jit(solution)/shard_map/ppermute | solution.py:392
  71.7 2.0 %collective-permute-start.28 = (bf16[16,1280]{1,0:T(8,128)(2,1)S(1)}, bf16[16,1280]{1,0:T(8,128)(2,1)S(1)}, u32[]{:S(2)}, u32[]{:S(2)}) collective-permute-start(bf16[16,1280]{1,0:T(8,128)(2,1)S(1)} %get-tuple-element.93), channel_id=1, source_target_pairs={{0,16},{4,20},{8,24},{12,28},{16,0},{20,4},{24,8},{28,12},{32,48},... | collective-permute-start | bytes 122888 | tf_op jit(solution)/shard_map/ppermute | solution.py:392
  73.7 1.7 %collective-permute-start.29 = (bf16[16,1280]{1,0:T(8,128)(2,1)S(1)}, bf16[16,1280]{1,0:T(8,128)(2,1)S(1)}, u32[]{:S(2)}, u32[]{:S(2)}) collective-permute-start(bf16[16,1280]{1,0:T(8,128)(2,1)S(1)} %get-tuple-element.94), channel_id=1, source_target_pairs={{0,48},{4,52},{8,56},{12,60},{16,32},{20,36},{24,40},{28,44},{32,1... | collective-permute-start | bytes 122888 | tf_op jit(solution)/shard_map/ppermute | solution.py:392
  75.4 1.9 %collective-permute-start.30 = (bf16[16,1280]{1,0:T(8,128)(2,1)S(1)}, bf16[16,1280]{1,0:T(8,128)(2,1)S(1)}, u32[]{:S(2)}, u32[]{:S(2)}) collective-permute-start(bf16[16,1280]{1,0:T(8,128)(2,1)S(1)} %get-tuple-element.95), channel_id=1, source_target_pairs={{0,8},{4,12},{8,0},{12,4},{16,24},{20,28},{24,16},{28,20},{32,40},... | collective-permute-start | bytes 122888 | tf_op jit(solution)/shard_map/ppermute | solution.py:392
  77.3 1.1 %collective-permute-start.31 = (bf16[16,1280]{1,0:T(8,128)(2,1)S(1)}, bf16[16,1280]{1,0:T(8,128)(2,1)S(1)}, u32[]{:S(2)}, u32[]{:S(2)}) collective-permute-start(bf16[16,1280]{1,0:T(8,128)(2,1)S(1)} %get-tuple-element.96), channel_id=1, source_target_pairs={{0,56},{4,60},{8,48},{12,52},{16,40},{20,44},{24,32},{28,36},{32,2... | collective-permute-start | bytes 122888 | tf_op jit(solution)/shard_map/ppermute | solution.py:392
  78.5 1.4 %collective-permute-done.29.refs_5_ = bf16[16,1280]{1,0:T(8,128)(2,1)S(1)} collective-permute-done((bf16[16,1280]{1,0:T(8,128)(2,1)S(1)}, bf16[16,1280]{1,0:T(8,128)(2,1)S(1)}, u32[]{:S(2)}, u32[]{:S(2)}) %collective-permute-start.29) | collective-permute-done | bytes 40992 | tf_op jit(solution)/shard_map/ppermute | solution.py:392
  79.9 2.6 %collective-permute-done.31.refs_7_ = bf16[16,1280]{1,0:T(8,128)(2,1)S(1)} collective-permute-done((bf16[16,1280]{1,0:T(8,128)(2,1)S(1)}, bf16[16,1280]{1,0:T(8,128)(2,1)S(1)}, u32[]{:S(2)}, u32[]{:S(2)}) %collective-permute-start.31) | collective-permute-done | bytes 40992 | tf_op jit(solution)/shard_map/ppermute | solution.py:392
  82.5 1.5 %shard_map.118 = (bf16[192,256]{1,0:T(8,128)(2,1)}, f32[4,1728]{1,0:T(4,128)}, f32[4,1728]{1,0:T(4,128)}) custom-call(s32[2]{0:T(128)S(1)} %pad_add_fusion.place, bf16[16,1280]{1,0:T(8,128)(2,1)S(1)} %get-tuple-element.89.refs_0_, bf16[16,1280]{1,0:T(8,128)(2,1)S(1)} %collective-permute-done.25.refs_1_, ...), custom_call_target="tpu_custom_call" | custom-call | flops 100000 | bytes 10000 | tf_op jit(solution)/shard_map/pallas_call | solution.py:351
  (21 shorter events, 0.1 us)
Async XLA Ops:
  0.7 6.3 %copy-start = (bf16[256,6912]{1,0:T(8,128)(2,1)S(1)}, bf16[256,6912]{1,0:T(8,128)(2,1)}, u32[]{:S(2)}) copy-start(bf16[256,6912]{1,0:T(8,128)(2,1)} %weight.2) | copy-start | bytes 10616836
  2.8 24.8 %copy-start.1 = (bf16[256,6912]{1,0:T(8,128)(2,1)S(1)}, bf16[256,6912]{1,0:T(8,128)(2,1)}, u32[]{:S(2)}) copy-start(bf16[256,6912]{1,0:T(8,128)(2,1)} %weight.3) | copy-start | bytes 10616836
  2.8 15.8 %collective-permute-start.4 = (bf16[224,512]{1,0:T(8,128)(2,1)S(1)}, bf16[224,512]{1,0:T(8,128)(2,1)S(1)}, u32[]{:S(2)}, u32[]{:S(2)}) collective-permute-start(bf16[224,512]{1,0:T(8,128)(2,1)S(1)} %get-tuple-element.60.p0), channel_id=1, source_target_pairs={{0,2},{1,3},{2,0},{3,1},{4,6},{5,7},{6,4},{7,5},{8,10},{9,11},{10,... | collective-permute-start | bytes 688136 | tf_op jit(solution)/shard_map/ppermute | solution.py:392
  5.0 13.6 %collective-permute-start.5 = (bf16[224,512]{1,0:T(8,128)(2,1)S(1)}, bf16[224,512]{1,0:T(8,128)(2,1)S(1)}, u32[]{:S(2)}, u32[]{:S(2)}) collective-permute-start(bf16[224,512]{1,0:T(8,128)(2,1)S(1)} %get-tuple-element.60.p0), channel_id=1, source_target_pairs={{0,1},{1,0},{2,3},{3,2},{4,5},{5,4},{6,7},{7,6},{8,9},{9,8},{10,11... | collective-permute-start | bytes 688136 | tf_op jit(solution)/shard_map/ppermute | solution.py:392
  6.5 12.2 %collective-permute-start.6 = (bf16[224,512]{1,0:T(8,128)(2,1)S(1)}, bf16[224,512]{1,0:T(8,128)(2,1)S(1)}, u32[]{:S(2)}, u32[]{:S(2)}) collective-permute-start(bf16[224,512]{1,0:T(8,128)(2,1)S(1)} %get-tuple-element.60.p0), channel_id=1, source_target_pairs={{0,3},{1,2},{2,1},{3,0},{4,7},{5,6},{6,5},{7,4},{8,11},{9,10},{10,... | collective-permute-start | bytes 688136 | tf_op jit(solution)/shard_map/ppermute | solution.py:392
  10.1 7.2 %collective-permute-start = (bf16[96,256]{1,0:T(8,128)(2,1)S(1)}, bf16[96,256]{1,0:T(8,128)(2,1)S(1)}, u32[]{:S(2)}, u32[]{:S(2)}) collective-permute-start(bf16[96,256]{1,0:T(8,128)(2,1)S(1)} %get-tuple-element.53), channel_id=1, source_target_pairs={{0,1},{1,0},{2,3},{3,2},{4,8},{5,9},{6,10},{7,11},{8,4},{9,5},{10,... | collective-permute-start | bytes 147464 | tf_op jit(solution)/shard_map/ppermute | solution.py:388
  12.4 4.9 %collective-permute-start.1 = (bf16[96,256]{1,0:T(8,128)(2,1)S(1)}, bf16[96,256]{1,0:T(8,128)(2,1)S(1)}, u32[]{:S(2)}, u32[]{:S(2)}) collective-permute-start(bf16[96,256]{1,0:T(8,128)(2,1)S(1)} %get-tuple-element.54), channel_id=1, source_target_pairs={{0,4},{1,5},{2,6},{3,7},{4,0},{5,1},{6,2},{7,3},{8,12},{9,13},{10,... | collective-permute-start | bytes 147464 | tf_op jit(solution)/shard_map/ppermute | solution.py:388
  17.8 4.2 %collective-permute-start.2 = (bf16[96,256]{1,0:T(8,128)(2,1)S(1)}, bf16[96,256]{1,0:T(8,128)(2,1)S(1)}, u32[]{:S(2)}, u32[]{:S(2)}) collective-permute-start(bf16[96,256]{1,0:T(8,128)(2,1)S(1)} %get-tuple-element.56), channel_id=1, source_target_pairs={{0,4},{1,2},{2,1},{3,7},{4,0},{5,6},{6,5},{7,3},{8,12},{9,10},{10,... | collective-permute-start | bytes 147464 | tf_op jit(solution)/shard_map/ppermute | solution.py:388
  18.5 4.1 %collective-permute-start.3 = (bf16[96,256]{1,0:T(8,128)(2,1)S(1)}, bf16[96,256]{1,0:T(8,128)(2,1)S(1)}, u32[]{:S(2)}, u32[]{:S(2)}) collective-permute-start(bf16[96,256]{1,0:T(8,128)(2,1)S(1)} %get-tuple-element.57.late), channel_id=1, source_target_pairs={{0,1},{1,0},{2,3},{3,2},{4,5},{5,4},{6,7},{7,6},{8,9},{9,8},{10,11... | collective-permute-start | bytes 147464 | tf_op jit(solution)/shard_map/ppermute | solution.py:388
  19.7 11.0 %collective-permute-start.10 = (bf16[768,256]{1,0:T(8,128)(2,1)S(1)}, bf16[768,256]{1,0:T(8,128)(2,1)S(1)}, u32[]{:S(2)}, u32[]{:S(2)}) collective-permute-start(bf16[768,256]{1,0:T(8,128)(2,1)S(1)} %get-tuple-element.63), channel_id=1, source_target_pairs={{0,1},{1,0},{2,3},{3,2},{4,8},{5,9},{6,10},{7,11},{8,4},{9,5},{10,... | collective-permute-start | bytes 1179656 | tf_op jit(solution)/shard_map/ppermute | solution.py:388
  21.7 10.3 %collective-permute-start.11 = (bf16[768,256]{1,0:T(8,128)(2,1)S(1)}, bf16[768,256]{1,0:T(8,128)(2,1)S(1)}, u32[]{:S(2)}, u32[]{:S(2)}) collective-permute-start(bf16[768,256]{1,0:T(8,128)(2,1)S(1)} %get-tuple-element.64), channel_id=1, source_target_pairs={{0,4},{1,5},{2,6},{3,7},{4,0},{5,1},{6,2},{7,3},{8,12},{9,13},{10,... | collective-permute-start | bytes 1179656 | tf_op jit(solution)/shard_map/ppermute | solution.py:388
  23.5 16.7 %collective-permute-start.7 = (bf16[192,512]{1,0:T(8,128)(2,1)S(1)}, bf16[192,512]{1,0:T(8,128)(2,1)S(1)}, u32[]{:S(2)}, u32[]{:S(2)}) collective-permute-start(bf16[192,512]{1,0:T(8,128)(2,1)S(1)} %get-tuple-element.62.g0), channel_id=1, source_target_pairs={{0,2},{1,3},{2,0},{3,1},{4,6},{5,7},{6,4},{7,5},{8,10},{9,11},{10,... | collective-permute-start | bytes 589832 | tf_op jit(solution)/shard_map/ppermute | solution.py:392
  24.5 15.7 %collective-permute-start.8 = (bf16[192,512]{1,0:T(8,128)(2,1)S(1)}, bf16[192,512]{1,0:T(8,128)(2,1)S(1)}, u32[]{:S(2)}, u32[]{:S(2)}) collective-permute-start(bf16[192,512]{1,0:T(8,128)(2,1)S(1)} %get-tuple-element.62.g0), channel_id=1, source_target_pairs={{0,1},{1,0},{2,3},{3,2},{4,5},{5,4},{6,7},{7,6},{8,9},{9,8},{10,11... | collective-permute-start | bytes 589832 | tf_op jit(solution)/shard_map/ppermute | solution.py:392
  27.1 13.1 %collective-permute-start.9 = (bf16[192,512]{1,0:T(8,128)(2,1)S(1)}, bf16[192,512]{1,0:T(8,128)(2,1)S(1)}, u32[]{:S(2)}, u32[]{:S(2)}) collective-permute-start(bf16[192,512]{1,0:T(8,128)(2,1)S(1)} %get-tuple-element.62.g0), channel_id=1, source_target_pairs={{0,3},{1,2},{2,1},{3,0},{4,7},{5,6},{6,5},{7,4},{8,11},{9,10},{10,... | collective-permute-start | bytes 589832 | tf_op jit(solution)/shard_map/ppermute | solution.py:392
  30.7 6.4 %collective-permute-start.12 = (bf16[96,256]{1,0:T(8,128)(2,1)S(1)}, bf16[96,256]{1,0:T(8,128)(2,1)S(1)}, u32[]{:S(2)}, u32[]{:S(2)}) collective-permute-start(bf16[96,256]{1,0:T(8,128)(2,1)S(1)} %get-tuple-element.69), channel_id=1, source_target_pairs={{0,1},{1,0},{2,3},{3,2},{4,8},{5,9},{6,10},{7,11},{8,4},{9,5},{10,... | collective-permute-start | bytes 147464 | tf_op jit(solution)/shard_map/ppermute | solution.py:388
  32.0 5.2 %collective-permute-start.13 = (bf16[96,256]{1,0:T(8,128)(2,1)S(1)}, bf16[96,256]{1,0:T(8,128)(2,1)S(1)}, u32[]{:S(2)}, u32[]{:S(2)}) collective-permute-start(bf16[96,256]{1,0:T(8,128)(2,1)S(1)} %get-tuple-element.70), channel_id=1, source_target_pairs={{0,4},{1,5},{2,6},{3,7},{4,0},{5,1},{6,2},{7,3},{8,12},{9,13},{10,... | collective-permute-start | bytes 147464 | tf_op jit(solution)/shard_map/ppermute | solution.py:388
  37.8 6.8 %collective-permute-start.15 = (bf16[96,256]{1,0:T(8,128)(2,1)S(1)}, bf16[96,256]{1,0:T(8,128)(2,1)S(1)}, u32[]{:S(2)}, u32[]{:S(2)}) collective-permute-start(bf16[96,256]{1,0:T(8,128)(2,1)S(1)} %get-tuple-element.74), channel_id=1, source_target_pairs={{0,4},{1,2},{2,1},{3,7},{4,0},{5,6},{6,5},{7,3},{8,12},{9,10},{10,... | collective-permute-start | bytes 147464 | tf_op jit(solution)/shard_map/ppermute | solution.py:388
  40.2 4.3 %collective-permute-start.16 = (bf16[96,256]{1,0:T(8,128)(2,1)S(1)}, bf16[96,256]{1,0:T(8,128)(2,1)S(1)}, u32[]{:S(2)}, u32[]{:S(2)}) collective-permute-start(bf16[96,256]{1,0:T(8,128)(2,1)S(1)} %get-tuple-element.71.late), channel_id=1, source_target_pairs={{0,1},{1,0},{2,3},{3,2},{4,5},{5,4},{6,7},{7,6},{8,9},{9,8},{10,11... | collective-permute-start | bytes 147464 | tf_op jit(solution)/shard_map/ppermute | solution.py:388
  41.9 3.9 %collective-permute-start.14 = (f32[128,1792]{1,0:T(8,128)S(1)}, f32[128,1792]{1,0:T(8,128)S(1)}, u32[]{:S(2)}, u32[]{:S(2)}) collective-permute-start(f32[128,1792]{1,0:T(8,128)S(1)} %get-tuple-element.73), channel_id=1, source_target_pairs={{0,4},{4,0},{8,12},{12,8},{16,20},{20,16},{24,28},{28,24},{32,36},... | collective-permute-start | bytes 2752520 | tf_op jit(solution)/shard_map/ppermute | solution.py:392
  43.9 7.3 %collective-permute-start.20 = (bf16[128,1792]{1,0:T(8,128)(2,1)S(1)}, bf16[128,1792]{1,0:T(8,128)(2,1)S(1)}, u32[]{:S(2)}, u32[]{:S(2)}) collective-permute-start(bf16[128,1792]{1,0:T(8,128)(2,1)S(1)} %get-tuple-element.83), channel_id=1, source_target_pairs={{0,4},{4,0},{8,12},{12,8},{16,20},{20,16},{24,28},{28,24},{32,36},... | collective-permute-start | bytes 1376264 | tf_op jit(solution)/shard_map/ppermute | solution.py:392
  45.5 5.8 %collective-permute-start.21 = (bf16[128,256]{1,0:T(8,128)(2,1)S(1)}, bf16[128,256]{1,0:T(8,128)(2,1)S(1)}, u32[]{:S(2)}, u32[]{:S(2)}) collective-permute-start(bf16[128,256]{1,0:T(8,128)(2,1)S(1)} %get-tuple-element.84), channel_id=1, source_target_pairs={{0,4},{4,0},{8,12},{12,8},{16,20},{20,16},{24,28},{28,24},{32,36},... | collective-permute-start | bytes 196616 | tf_op jit(solution)/shard_map/ppermute | solution.py:392
  46.5 9.6 %collective-permute-start.17 = (bf16[32,1792]{1,0:T(8,128)(2,1)S(1)}, bf16[32,1792]{1,0:T(8,128)(2,1)S(1)}, u32[]{:S(2)}, u32[]{:S(2)}) collective-permute-start(bf16[32,1792]{1,0:T(8,128)(2,1)S(1)} %get-tuple-element.80), channel_id=1, source_target_pairs={{0,128},{4,132},{8,136},{12,140},{16,144},{20,148},{24,152},{28,15... | collective-permute-start | bytes 344072 | tf_op jit(solution)/shard_map/ppermute | solution.py:392
  50.2 7.6 %collective-permute-start.18 = (bf16[32,1792]{1,0:T(8,128)(2,1)S(1)}, bf16[32,1792]{1,0:T(8,128)(2,1)S(1)}, u32[]{:S(2)}, u32[]{:S(2)}) collective-permute-start(bf16[32,1792]{1,0:T(8,128)(2,1)S(1)} %get-tuple-element.81), channel_id=1, source_target_pairs={{0,64},{4,68},{8,72},{12,76},{16,80},{20,84},{24,88},{28,92},{32,9... | collective-permute-start | bytes 344072 | tf_op jit(solution)/shard_map/ppermute | solution.py:392
  51.2 10.1 %collective-permute-start.19 = (bf16[32,1792]{1,0:T(8,128)(2,1)S(1)}, bf16[32,1792]{1,0:T(8,128)(2,1)S(1)}, u32[]{:S(2)}, u32[]{:S(2)}) collective-permute-start(bf16[32,1792]{1,0:T(8,128)(2,1)S(1)} %get-tuple-element.82), channel_id=1, source_target_pairs={{0,192},{4,196},{8,200},{12,204},{16,208},{20,212},{24,216},{28,22... | collective-permute-start | bytes 344072 | tf_op jit(solution)/shard_map/ppermute | solution.py:392
  51.9 9.9 %collective-permute-start.22 = (bf16[32,2304]{1,0:T(8,128)(2,1)S(1)}, bf16[32,2304]{1,0:T(8,128)(2,1)S(1)}, u32[]{:S(2)}, u32[]{:S(2)}) collective-permute-start(bf16[32,2304]{1,0:T(8,128)(2,1)S(1)} %get-tuple-element.86), channel_id=1, source_target_pairs={{0,128},{4,132},{8,136},{12,140},{16,144},{20,148},{24,152},{28,15... | collective-permute-start | bytes 442376 | tf_op jit(solution)/shard_map/ppermute | solution.py:392
  55.1 8.4 %collective-permute-start.23 = (bf16[32,2304]{1,0:T(8,128)(2,1)S(1)}, bf16[32,2304]{1,0:T(8,128)(2,1)S(1)}, u32[]{:S(2)}, u32[]{:S(2)}) collective-permute-start(bf16[32,2304]{1,0:T(8,128)(2,1)S(1)} %get-tuple-element.87), channel_id=1, source_target_pairs={{0,64},{4,68},{8,72},{12,76},{16,80},{20,84},{24,88},{28,92},{32,9... | collective-permute-start | bytes 442376 | tf_op jit(solution)/shard_map/ppermute | solution.py:392
  56.0 7.6 %collective-permute-start.24 = (bf16[32,2304]{1,0:T(8,128)(2,1)S(1)}, bf16[32,2304]{1,0:T(8,128)(2,1)S(1)}, u32[]{:S(2)}, u32[]{:S(2)}) collective-permute-start(bf16[32,2304]{1,0:T(8,128)(2,1)S(1)} %get-tuple-element.88), channel_id=1, source_target_pairs={{0,192},{4,196},{8,200},{12,204},{16,208},{20,212},{24,216},{28,22... | collective-permute-start | bytes 442376 | tf_op jit(solution)/shard_map/ppermute | solution.py:392
  64.8 10.6 %collective-permute-start.25 = (bf16[16,1280]{1,0:T(8,128)(2,1)S(1)}, bf16[16,1280]{1,0:T(8,128)(2,1)S(1)}, u32[]{:S(2)}, u32[]{:S(2)}) collective-permute-start(bf16[16,1280]{1,0:T(8,128)(2,1)S(1)} %get-tuple-element.90), channel_id=1, source_target_pairs={{0,32},{4,36},{8,40},{12,44},{16,48},{20,52},{24,56},{28,60},{32,0... | collective-permute-start | bytes 122888 | tf_op jit(solution)/shard_map/ppermute | solution.py:392
  67.9 9.4 %collective-permute-start.26 = (bf16[16,1280]{1,0:T(8,128)(2,1)S(1)}, bf16[16,1280]{1,0:T(8,128)(2,1)S(1)}, u32[]{:S(2)}, u32[]{:S(2)}) collective-permute-start(bf16[16,1280]{1,0:T(8,128)(2,1)S(1)} %get-tuple-element.91), channel_id=1, source_target_pairs={{0,24},{4,28},{8,16},{12,20},{16,8},{20,12},{24,0},{28,4},{32,56},... | collective-permute-start | bytes 122888 | tf_op jit(solution)/shard_map/ppermute | solution.py:392
  70.2 8.2 %collective-permute-start.27 = (bf16[16,1280]{1,0:T(8,128)(2,1)S(1)}, bf16[16,1280]{1,0:T(8,128)(2,1)S(1)}, u32[]{:S(2)}, u32[]{:S(2)}) collective-permute-start(bf16[16,1280]{1,0:T(8,128)(2,1)S(1)} %get-tuple-element.92), channel_id=1, source_target_pairs={{0,40},{4,44},{8,32},{12,36},{16,56},{20,60},{24,48},{28,52},{32,8... | collective-permute-start | bytes 122888 | tf_op jit(solution)/shard_map/ppermute | solution.py:392
  71.7 6.7 %collective-permute-start.28 = (bf16[16,1280]{1,0:T(8,128)(2,1)S(1)}, bf16[16,1280]{1,0:T(8,128)(2,1)S(1)}, u32[]{:S(2)}, u32[]{:S(2)}) collective-permute-start(bf16[16,1280]{1,0:T(8,128)(2,1)S(1)} %get-tuple-element.93), channel_id=1, source_target_pairs={{0,16},{4,20},{8,24},{12,28},{16,0},{20,4},{24,8},{28,12},{32,48},... | collective-permute-start | bytes 122888 | tf_op jit(solution)/shard_map/ppermute | solution.py:392
  73.7 6.2 %collective-permute-start.29 = (bf16[16,1280]{1,0:T(8,128)(2,1)S(1)}, bf16[16,1280]{1,0:T(8,128)(2,1)S(1)}, u32[]{:S(2)}, u32[]{:S(2)}) collective-permute-start(bf16[16,1280]{1,0:T(8,128)(2,1)S(1)} %get-tuple-element.94), channel_id=1, source_target_pairs={{0,48},{4,52},{8,56},{12,60},{16,32},{20,36},{24,40},{28,44},{32,1... | collective-permute-start | bytes 122888 | tf_op jit(solution)/shard_map/ppermute | solution.py:392
  75.4 4.5 %collective-permute-start.30 = (bf16[16,1280]{1,0:T(8,128)(2,1)S(1)}, bf16[16,1280]{1,0:T(8,128)(2,1)S(1)}, u32[]{:S(2)}, u32[]{:S(2)}) collective-permute-start(bf16[16,1280]{1,0:T(8,128)(2,1)S(1)} %get-tuple-element.95), channel_id=1, source_target_pairs={{0,8},{4,12},{8,0},{12,4},{16,24},{20,28},{24,16},{28,20},{32,40},... | collective-permute-start | bytes 122888 | tf_op jit(solution)/shard_map/ppermute | solution.py:392
  77.3 5.2 %collective-permute-start.31 = (bf16[16,1280]{1,0:T(8,128)(2,1)S(1)}, bf16[16,1280]{1,0:T(8,128)(2,1)S(1)}, u32[]{:S(2)}, u32[]{:S(2)}) collective-permute-start(bf16[16,1280]{1,0:T(8,128)(2,1)S(1)} %get-tuple-element.96), channel_id=1, source_target_pairs={{0,56},{4,60},{8,48},{12,52},{16,40},{20,44},{24,32},{28,36},{32,2... | collective-permute-start | bytes 122888 | tf_op jit(solution)/shard_map/ppermute | solution.py:392

commit v10 on v8

--- a/solution.py
+++ b/solution.py
@@ -51,8 +51,8 @@
 
 
 def pack_kernel(
-    place, feat, pre, grad, nbr, halo, send, pay, nbt, hrow, srow, pre_out, grad_out,
-    ids, halo_ids, send_ids, sems
+    place, feat, pre, grad, nbr, halo, send, pay, p2, p1, p3, nbt, hrow, srow, pre_out,
+    grad_out, ids, halo_ids, send_ids, feat_in, sems
 ):
     copies = [
         pltpu.make_async_copy(source, target, sems.at[n])
@@ -61,7 +61,7 @@
                 (nbr, ids),
                 (halo, halo_ids),
                 (send, send_ids),
-                (feat, pay.at[0:S, 0:C]),
+                (feat, feat_in),
                 (grad, grad_out),
                 (pre, pre_out),
             )
@@ -78,11 +78,9 @@
     nbt[0:K, 0:S] = table
     shifted_up = table + 1.0
     high = jnp.floor(shifted_up * (1.0 / 16.0))
-    pay[S : S + 32, :] = jnp.zeros((32, 2 * C), BF)
-    pay[S : S + K, 0:S] = high.astype(BF)
-    pay[S : S + K, C : C + S] = (shifted_up - 16.0 * high).astype(BF)
+    tail = jnp.zeros((32, 2 * C), F32)
     z = pre_out[...].astype(F32)
-    pay[0:S, C : 2 * C] = (z * (1.0 / (1.0 + jnp.exp(-z)))).astype(BF)
+    hidden = (z * (1.0 / (1.0 + jnp.exp(-z)))).astype(BF)
     halo_up = (halo_ids[0] + 1).astype(F32).astype(BF)
     spread = mm(halo_up, onehot(iota((24, 8 * HB), 1) % HB == iota((24, 8 * HB), 0)))
     row = jnp.sum(
@@ -91,8 +89,19 @@
         keepdims=True,
     )
     hrow[...] = jnp.broadcast_to(row.astype(jnp.int32) - 1, hrow.shape)
-    tail = pay[S + 16 : S + 32, 0:C].astype(F32)
-    pay[S + 16 : S + 32, 0:C] = jnp.where(iota((16, C), 0) == 15, row, tail).astype(BF)
+    pay[S : S + 32, :] = tail.astype(BF)
+    pay[S : S + K, 0:S] = high.astype(BF)
+    pay[S : S + K, C : C + S] = (shifted_up - 16.0 * high).astype(BF)
+    last = pay[S + 16 : S + 32, 0:C].astype(F32)
+    pay[S + 16 : S + 32, 0:C] = jnp.where(iota((16, C), 0) == 15, row, last).astype(BF)
+    both = jnp.concatenate([feat_in[...], hidden], axis=0)
+    for turn, out in ((0, pay), (1, p1), (2, p2), (3, p3)):
+        offset = ((place[1] ^ turn) * QW) % C
+        turned = mm(both, onehot(iota((C, C), 0) == (iota((C, C), 1) + offset) % C)).astype(BF)
+        out[0:S, 0:C] = turned[0:S]
+        out[0:S, C : 2 * C] = turned[S : 2 * S]
+        if turn:
+            out[S : S + 32, :] = pay[S : S + 32, :]
     lane, peer = iota((64, C), 1), iota((64, C), 0)
     parity = jnp.where(lane < 128, place[0] % 2, 1 - place[0] % 2)
     pick = onehot(peer == 2 * ((lane % 128) // 4) + parity)
@@ -208,7 +217,6 @@
     offset = start % C
     even = place[0] % 2 == 0
     far = inner(place[0], 64)
-    shift = onehot(iota((C, C), 0) == (iota((C, C), 1) + offset) % C)
     lane = iota((S, 2 * C), 1) % C
     early = lane < C - offset
     for turn, pay in enumerate((p0, p1, p2, p3)):
@@ -223,7 +231,7 @@
                 (S + 96, loc[tile, :, lanes]),
                 (S + 160, jnp.where(even, below, above)),
             ):
-                ext[to : to + piece.shape[0], lanes] = mm(piece, shift).astype(BF)
+                ext[to : to + piece.shape[0], lanes] = piece
         high = pay[S : S + 32, 0:C].astype(F32)
         low = pay[S : S + 32, C : 2 * C].astype(F32)
         ids[0:32, :] = 16.0 * high + low - 1.0
@@ -396,10 +404,10 @@
     scale = 1.0 / math.sqrt(S * gx * lax.axis_size("gy"))
     place = jnp.stack([lax.axis_index("gx"), lax.axis_index("gy")]).astype(jnp.int32)
     tile = sds((S, C), BF)
-    pay, nbt, hrow, srow, pre, grad = call(
+    pay, p2, p1, p3, nbt, hrow, srow, pre, grad = call(
         pack_kernel,
         (
-            sds((S + 32, 2 * C), BF),
+            *[sds((S + 32, 2 * C), BF)] * 4,
             sds((32, C), F32),
             sds((8, C), jnp.int32),
             sds((8, C), jnp.int32),
@@ -424,10 +432,11 @@
             pltpu.VMEM((K, S), jnp.int32),
             pltpu.VMEM((1, 8, 24), jnp.int32),
             pltpu.VMEM((3, 1, 64), jnp.int32),
+            pltpu.VMEM((S, C), BF),
             pltpu.SemaphoreType.DMA((6,)),
         ],
     )
-    pays = gathered(pay, "gy")
+    pays = [pay] + [cross(value, "gy", d) for d, value in ((2, p2), (1, p1), (3, p3))]
     back = pltpu.VMEM((8, HB, C), BF)
     own, m1, m2, loc = spread(place, nbt, grad, weight_two, 10**5)
     m2, m1 = halo_lines(m2, m1)

time: 83.7 us -> 83.1 us (level)
  transfers between devices with their start and end apart: 25 -> 25, of which waited for: 6 -> 7; matrix products, arithmetic and copies ran while one was open for 0% -> 0% of each run, Pallas kernels for 25% -> 24%
where the time goes in v10:
time: 83.1 us; the launch traced here: 82.3 us
  starting transfers between devices  28.8 us (35%)
  Pallas kernels  24 us (29%)
  blocking collectives  17.2 us (21%)
  waiting for transfers between devices  11.3 us (14%)
    pallas_call x16, Pallas kernels, call(): pl.pallas_call(kernel, out_shape=outs, in_specs=specs, out_specs=jax.tree...  24 us
    ppermute x15, starting transfers between devices, cross(): lax.ppermute(value, axis, [(n, n ^ mask) for n in range(lax.axis_size(axi...  20.2 us
    all_to_all x1, blocking collectives, body(): lax.all_to_all(summed.reshape(8, 8, 10 * C), 'gx', split_axis=0, concat_a...  17.2 us
    ppermute x10, starting transfers between devices, swap(): return lax.ppermute(value, ('gx', 'gy'), pairs)  8.57 us
    ppermute x10, waiting for transfers between devices, swap(): return lax.ppermute(value, ('gx', 'gy'), pairs)  6.01 us
    ppermute x15, waiting for transfers between devices, cross(): lax.ppermute(value, axis, [(n, n ^ mask) for n in range(lax.axis_size(axi...  5.31 us
  transfers between devices with their start and end apart: 25, of which 7 were waited for; matrix products, arithmetic and copies ran while one was open for 0% of the time, Pallas kernels for 24%

profile of v10, /device:TPU:2, one launch (start us, length us, event | category | flops | bytes accessed | tf_op | source)
XLA Modules:
  0.0 82.3 jit_solution(11156362255084355256)
XLA Ops:
  0.6 0.1 pad_add_fusion.place
  0.7 2.3 %shard_map.103 = (bf16[224,512]{1,0:T(8,128)(2,1)S(1)}, bf16[224,512]{1,0:T(8,128)(2,1)S(1)}, bf16[224,512]{1,0:T(8,128)(2,1)S(1)}, bf16[224,512]{1,0:T(8,128)(2...) custom-call(s32[2]{0:T(128)S(1)} %pad_add_fusion.place, ...), custom_call_target="tpu_custom_call" | custom-call | flops 4000000000 | bytes 10000 | tf_op jit(solution)/shard_map/pallas_call | solution.py:344
  3.0 0.0 copy-start.1
  3.0 2.2 %collective-permute-start.4 = (bf16[224,512]{1,0:T(8,128)(2,1)S(1)}, bf16[224,512]{1,0:T(8,128)(2,1)S(1)}, u32[]{:S(2)}, u32[]{:S(2)}) collective-permute-start(bf16[224,512]{1,0:T(8,128)(2,1)S(1)} %get-tuple-element.56), channel_id=1, source_target_pairs={{0,2},{1,3},{2,0},{3,1},{4,6},{5,7},{6,4},{7,5},{8,10},{9,11},{10,... | collective-permute-start | bytes 688136 | tf_op jit(solution)/shard_map/ppermute | solution.py:385
  5.3 1.4 %collective-permute-start.5 = (bf16[224,512]{1,0:T(8,128)(2,1)S(1)}, bf16[224,512]{1,0:T(8,128)(2,1)S(1)}, u32[]{:S(2)}, u32[]{:S(2)}) collective-permute-start(bf16[224,512]{1,0:T(8,128)(2,1)S(1)} %get-tuple-element.57), channel_id=1, source_target_pairs={{0,1},{1,0},{2,3},{3,2},{4,5},{5,4},{6,7},{7,6},{8,9},{9,8},{10,11... | collective-permute-start | bytes 688136 | tf_op jit(solution)/shard_map/ppermute | solution.py:385
  6.7 0.5 collective-permute-start.6
  7.2 3.0 %shard_map.104 = (f32[192,256]{1,0:T(8,128)S(1)}, bf16[96,256]{1,0:T(8,128)(2,1)S(1)}, bf16[96,256]{1,0:T(8,128)(2,1)S(1)}, bf16[64,256]{1,0:T(8,128)(2,1)S(1)}) custom-call(s32[2]{0:T(128)S(1)} %pad_add_fusion.place, f32[32,256]{1,0:T(8,128)S(1)} %get-tuple-element.45.nbt, bf16[192,256]{1,0:T(8,128)(2,1)S(1)} %get-tuple-element.46.grad, ...), custom_call_target="tpu_custom_call" | custom-call | flops 100000 | bytes 10000 | tf_op jit(solution)/shard_map/pallas_call | solution.py:344
  10.3 2.4 %collective-permute-start = (bf16[96,256]{1,0:T(8,128)(2,1)S(1)}, bf16[96,256]{1,0:T(8,128)(2,1)S(1)}, u32[]{:S(2)}, u32[]{:S(2)}) collective-permute-start(bf16[96,256]{1,0:T(8,128)(2,1)S(1)} %get-tuple-element.48), channel_id=1, source_target_pairs={{0,1},{1,0},{2,3},{3,2},{4,8},{5,9},{6,10},{7,11},{8,4},{9,5},{10,... | collective-permute-start | bytes 147464 | tf_op jit(solution)/shard_map/ppermute | solution.py:381
  12.6 0.0 collective-permute-start.1
  12.6 4.9 %collective-permute-done.m2 = bf16[96,256]{1,0:T(8,128)(2,1)S(1)} collective-permute-done((bf16[96,256]{1,0:T(8,128)(2,1)S(1)}, bf16[96,256]{1,0:T(8,128)(2,1)S(1)}, u32[]{:S(2)}, u32[]{:S(2)}) %collective-permute-start) | collective-permute-done | bytes 49184 | tf_op jit(solution)/shard_map/ppermute | solution.py:381
  17.5 0.0 collective-permute-done.1.m1
  17.5 0.6 shard_map.105
  18.1 0.6 collective-permute-start.2
  18.7 0.2 collective-permute-start.3
  18.8 0.0 collective-permute-done.4.p2
  18.8 0.0 collective-permute-done.5.p1
  18.8 0.0 collective-permute-done.6.p3
  18.9 1.1 %shard_map.106 = (bf16[768,256]{1,0:T(8,128)(2,1)S(1)}, bf16[768,256]{1,0:T(8,128)(2,1)S(1)}, bf16[4,64,512]{2,1,0:T(8,128)(2,1)S(1)}) custom-call(s32[2]{0:T(128)S(1)} %pad_add_fusion.place, bf16[224,512]{1,0:T(8,128)(2,1)S(1)} %get-tuple-element.55.p0, bf16[224,512]{1,0:T(8,128)(2,1)S(1)} %collective-permute-done.4.p2, ...), custom_call_target="tpu_custom_call" | custom-call | flops 100000 | bytes 10000 | tf_op jit(solution)/shard_map/pallas_call | solution.py:344
  19.9 2.0 %collective-permute-start.10 = (bf16[768,256]{1,0:T(8,128)(2,1)S(1)}, bf16[768,256]{1,0:T(8,128)(2,1)S(1)}, u32[]{:S(2)}, u32[]{:S(2)}) collective-permute-start(bf16[768,256]{1,0:T(8,128)(2,1)S(1)} %get-tuple-element.61), channel_id=1, source_target_pairs={{0,1},{1,0},{2,3},{3,2},{4,8},{5,9},{6,10},{7,11},{8,4},{9,5},{10,... | collective-permute-start | bytes 1179656 | tf_op jit(solution)/shard_map/ppermute | solution.py:381
  21.9 0.0 collective-permute-start.11
  21.9 0.3 collective-permute-done.2.n2
  22.2 0.5 collective-permute-done.3.n1
  22.8 0.9 %shard_map.107 = (bf16[192,256]{1,0:T(8,128)(2,1)S(1)}, bf16[192,512]{1,0:T(8,128)(2,1)S(1)}) custom-call(s32[2]{0:T(128)S(1)} %pad_add_fusion.place, f32[192,256]{1,0:T(8,128)S(1)} %get-tuple-element.47.late.own, bf16[96,256]{1,0:T(8,128)(2,1)S(1)} %collective-permute-done.m2, bf16[96,256]{1,0:T(8,128)(2,1)S(1)} %collective-permute-done.1.m1, ...), custom_call_target="tpu_custom_call" | custom-call | flops 100000 | bytes 10000 | tf_op jit(solution)/shard_map/pallas_call | solution.py:344
  23.7 1.0 %collective-permute-start.7 = (bf16[192,512]{1,0:T(8,128)(2,1)S(1)}, bf16[192,512]{1,0:T(8,128)(2,1)S(1)}, u32[]{:S(2)}, u32[]{:S(2)}) collective-permute-start(bf16[192,512]{1,0:T(8,128)(2,1)S(1)} %get-tuple-element.60.g0), channel_id=1, source_target_pairs={{0,2},{1,3},{2,0},{3,1},{4,6},{5,7},{6,4},{7,5},{8,10},{9,11},{10,... | collective-permute-start | bytes 589832 | tf_op jit(solution)/shard_map/ppermute | solution.py:385
  24.7 2.6 %collective-permute-start.8 = (bf16[192,512]{1,0:T(8,128)(2,1)S(1)}, bf16[192,512]{1,0:T(8,128)(2,1)S(1)}, u32[]{:S(2)}, u32[]{:S(2)}) collective-permute-start(bf16[192,512]{1,0:T(8,128)(2,1)S(1)} %get-tuple-element.60.g0), channel_id=1, source_target_pairs={{0,1},{1,0},{2,3},{3,2},{4,5},{5,4},{6,7},{7,6},{8,9},{9,8},{10,11... | collective-permute-start | bytes 589832 | tf_op jit(solution)/shard_map/ppermute | solution.py:385
  27.3 0.5 collective-permute-start.9
  27.9 3.0 %shard_map.108 = (f32[192,256]{1,0:T(8,128)S(1)}, bf16[96,256]{1,0:T(8,128)(2,1)S(1)}, bf16[96,256]{1,0:T(8,128)(2,1)S(1)}, bf16[64,256]{1,0:T(8,128)(2,1)S(1)}) custom-call(s32[2]{0:T(128)S(1)} %pad_add_fusion.place, f32[32,256]{1,0:T(8,128)S(1)} %get-tuple-element.45.nbt, bf16[192,256]{1,0:T(8,128)(2,1)S(1)} %get-tuple-element.63.grad, ...), custom_call_target="tpu_custom_call" | custom-call | flops 4000000000 | bytes 10000 | tf_op jit(solution)/shard_map/pallas_call | solution.py:344
  30.9 0.0 collective-permute-done.10.r2
  30.9 1.3 %collective-permute-start.12 = (bf16[96,256]{1,0:T(8,128)(2,1)S(1)}, bf16[96,256]{1,0:T(8,128)(2,1)S(1)}, u32[]{:S(2)}, u32[]{:S(2)}) collective-permute-start(bf16[96,256]{1,0:T(8,128)(2,1)S(1)} %get-tuple-element.67), channel_id=1, source_target_pairs={{0,1},{1,0},{2,3},{3,2},{4,8},{5,9},{6,10},{7,11},{8,4},{9,5},{10,... | collective-permute-start | bytes 147464 | tf_op jit(solution)/shard_map/ppermute | solution.py:381
  32.2 0.0 collective-permute-done.11.r1
  32.2 0.0 collective-permute-start.13
  32.2 4.3 %shard_map.109 = (bf16[768,1792]{1,0:T(8,128)(2,1)S(1)}, bf16[768,1792]{1,0:T(8,128)(2,1)S(1)}) custom-call(s32[2]{0:T(128)S(1)} %pad_add_fusion.place, bf16[224,512]{1,0:T(8,128)(2,1)S(1)} %get-tuple-element.55.p0, bf16[224,512]{1,0:T(8,128)(2,1)S(1)} %collective-permute-done.4.p2, bf16[224,512]{1,0:T(8,128)(2,1)S(1)} %collective-permute-done.5.p1, ...), custom_call_target="tpu_custom_call" | custom-call | flops 4000000000 | bytes 10000 | tf_op jit(solution)/shard_map/pallas_call | solution.py:344
  36.5 0.3 collective-permute-done.12.m2
  36.8 0.0 collective-permute-done.13.m1
  36.8 0.6 shard_map.110
  37.4 2.2 %collective-permute-start.15 = (bf16[96,256]{1,0:T(8,128)(2,1)S(1)}, bf16[96,256]{1,0:T(8,128)(2,1)S(1)}, u32[]{:S(2)}, u32[]{:S(2)}) collective-permute-start(bf16[96,256]{1,0:T(8,128)(2,1)S(1)} %get-tuple-element.72), channel_id=1, source_target_pairs={{0,4},{1,2},{2,1},{3,7},{4,0},{5,6},{6,5},{7,3},{8,12},{9,10},{10,... | collective-permute-start | bytes 147464 | tf_op jit(solution)/shard_map/ppermute | solution.py:381
  39.5 0.0 collective-permute-start.16
  39.6 0.0 collective-permute-done.9.g3
  39.6 1.7 %shard_map.111 = (f32[128,1792]{1,0:T(8,128)S(1)}, f32[128,1792]{1,0:T(8,128)S(1)}) custom-call(s32[2]{0:T(128)S(1)} %pad_add_fusion.place, bf16[192,512]{1,0:T(8,128)(2,1)S(1)} %get-tuple-element.60.g0, bf16[192,512]{1,0:T(8,128)(2,1)S(1)} %collective-permute-done.7.g2, bf16[192,512]{1,0:T(8,128)(2,1)S(1)} %collective-permute-done.8.g1, ...), custom_call_target="tpu_custom_call" | custom-call | flops 4000000000 | bytes 10000 | tf_op jit(solution)/shard_map/pallas_call | solution.py:344
  41.3 0.3 collective-permute-start.14
  41.6 1.7 %shard_map.112 = (bf16[128,1792]{1,0:T(8,128)(2,1)S(1)}, bf16[128,1792]{1,0:T(8,128)(2,1)S(1)}) custom-call(s32[2]{0:T(128)S(1)} %pad_add_fusion.place, bf16[192,512]{1,0:T(8,128)(2,1)S(1)} %get-tuple-element.60.g0, bf16[192,512]{1,0:T(8,128)(2,1)S(1)} %collective-permute-done.7.g2, bf16[192,512]{1,0:T(8,128)(2,1)S(1)} %collective-permute-done.8.g1, ...), custom_call_target="tpu_custom_call" | custom-call | flops 100000 | bytes 10000 | tf_op jit(solution)/shard_map/pallas_call | solution.py:344
  43.3 0.4 collective-permute-start.20
  43.7 0.0 collective-permute-done.15.n2
  43.7 0.0 collective-permute-done.16.n1
  43.7 1.0 %shard_map.113 = (bf16[128,256]{1,0:T(8,128)(2,1)S(1)}, bf16[128,256]{1,0:T(8,128)(2,1)S(1)}) custom-call(s32[2]{0:T(128)S(1)} %pad_add_fusion.place, f32[192,256]{1,0:T(8,128)S(1)} %get-tuple-element.64.late.own, bf16[96,256]{1,0:T(8,128)(2,1)S(1)} %collective-permute-done.12.m2, bf16[96,256]{1,0:T(8,128)(2,1)S(1)} %collective-permute-done.13.m1, ...), custom_call_target="tpu_custom_call" | custom-call | flops 20000000000 | bytes 10000 | tf_op jit(solution)/shard_map/pallas_call | solution.py:344
  44.6 0.3 collective-permute-start.21
  45.0 0.6 shard_map.114
  45.6 4.0 %collective-permute-start.17 = (bf16[32,1792]{1,0:T(8,128)(2,1)S(1)}, bf16[32,1792]{1,0:T(8,128)(2,1)S(1)}, u32[]{:S(2)}, u32[]{:S(2)}) collective-permute-start(bf16[32,1792]{1,0:T(8,128)(2,1)S(1)} %get-tuple-element.78), channel_id=1, source_target_pairs={{0,128},{4,132},{8,136},{12,140},{16,144},{20,148},{24,152},{28,15... | collective-permute-start | bytes 344072 | tf_op jit(solution)/shard_map/ppermute | solution.py:385
  49.6 1.0 %collective-permute-start.18 = (bf16[32,1792]{1,0:T(8,128)(2,1)S(1)}, bf16[32,1792]{1,0:T(8,128)(2,1)S(1)}, u32[]{:S(2)}, u32[]{:S(2)}) collective-permute-start(bf16[32,1792]{1,0:T(8,128)(2,1)S(1)} %get-tuple-element.79), channel_id=1, source_target_pairs={{0,64},{4,68},{8,72},{12,76},{16,80},{20,84},{24,88},{28,92},{32,9... | collective-permute-start | bytes 344072 | tf_op jit(solution)/shard_map/ppermute | solution.py:385
  50.5 0.1 collective-permute-start.19
  50.6 0.0 collective-permute-done.21.rs
  50.6 0.0 collective-permute-done.20.come
  50.6 0.7 shard_map.116
  51.3 3.1 %collective-permute-start.22 = (bf16[32,2304]{1,0:T(8,128)(2,1)S(1)}, bf16[32,2304]{1,0:T(8,128)(2,1)S(1)}, u32[]{:S(2)}, u32[]{:S(2)}) collective-permute-start(bf16[32,2304]{1,0:T(8,128)(2,1)S(1)} %get-tuple-element.84), channel_id=1, source_target_pairs={{0,128},{4,132},{8,136},{12,140},{16,144},{20,148},{24,152},{28,15... | collective-permute-start | bytes 442376 | tf_op jit(solution)/shard_map/ppermute | solution.py:385
  54.4 1.0 %collective-permute-start.23 = (bf16[32,2304]{1,0:T(8,128)(2,1)S(1)}, bf16[32,2304]{1,0:T(8,128)(2,1)S(1)}, u32[]{:S(2)}, u32[]{:S(2)}) collective-permute-start(bf16[32,2304]{1,0:T(8,128)(2,1)S(1)} %get-tuple-element.85), channel_id=1, source_target_pairs={{0,64},{4,68},{8,72},{12,76},{16,80},{20,84},{24,88},{28,92},{32,9... | collective-permute-start | bytes 442376 | tf_op jit(solution)/shard_map/ppermute | solution.py:385
  55.4 0.0 collective-permute-done.17.a2
  55.4 1.7 %collective-permute-start.24 = (bf16[32,2304]{1,0:T(8,128)(2,1)S(1)}, bf16[32,2304]{1,0:T(8,128)(2,1)S(1)}, u32[]{:S(2)}, u32[]{:S(2)}) collective-permute-start(bf16[32,2304]{1,0:T(8,128)(2,1)S(1)} %get-tuple-element.86), channel_id=1, source_target_pairs={{0,192},{4,196},{8,200},{12,204},{16,208},{20,212},{24,216},{28,22... | collective-permute-start | bytes 442376 | tf_op jit(solution)/shard_map/ppermute | solution.py:385
  57.2 3.5 %collective-permute-done.19.a3 = bf16[32,1792]{1,0:T(8,128)(2,1)S(1)} collective-permute-done((bf16[32,1792]{1,0:T(8,128)(2,1)S(1)}, bf16[32,1792]{1,0:T(8,128)(2,1)S(1)}, u32[]{:S(2)}, u32[]{:S(2)}) %collective-permute-start.19) | collective-permute-done | bytes 114720 | tf_op jit(solution)/shard_map/ppermute | solution.py:385
  60.6 0.6 shard_map.115.two
  61.2 1.6 %collective-permute-done.23.b1 = bf16[32,2304]{1,0:T(8,128)(2,1)S(1)} collective-permute-done((bf16[32,2304]{1,0:T(8,128)(2,1)S(1)}, bf16[32,2304]{1,0:T(8,128)(2,1)S(1)}, u32[]{:S(2)}, u32[]{:S(2)}) %collective-permute-start.23) | collective-permute-done | bytes 147488 | tf_op jit(solution)/shard_map/ppermute | solution.py:385
  62.9 0.2 collective-permute-done.24.b3
  63.0 1.1 %shard_map.117 = bf16[64,2560]{1,0:T(8,128)(2,1)S(1)} custom-call(s32[2]{0:T(128)S(1)} %pad_add_fusion.place, bf16[32,1792]{1,0:T(8,128)(2,1)S(1)} %shard_map.115.two, bf16[32,2304]{1,0:T(8,128)(2,1)S(1)} %get-tuple-element.83.b0, bf16[32,2304]{1,0:T(8,128)(2,1)S(1)} %collective-permute-done.22.b2, bf16[32,2304]{1,0:T(8,128)(2,1)S(1)} %collective-permute-done.23.b1, ...), custom_call_target="tpu_custom_call" | custom-call | flops 100000 | bytes 10000 | tf_op jit(solution)/shard_map/pallas_call | solution.py:344
  64.2 17.2 %all_to_all.5.refs_0_ = bf16[8,8,2560]{2,1,0:T(8,128)(2,1)S(1)} all-to-all(bf16[8,8,2560]{2,1,0:T(8,128)(2,1)S(1)} %bitcast.5), channel_id=1, replica_groups={{0,8,16,24,32,40,48,56},{4,12,20,28,36,44,52,60},{64,72,80,88,96,104,11..., dimensions={0} | all-to-all | bytes 655360 | tf_op jit(solution)/shard_map/all_to_all | solution.py:563
  81.4 0.9 %shard_map.118 = (bf16[192,256]{1,0:T(8,128)(2,1)}, f32[4,1728]{1,0:T(4,128)}, f32[4,1728]{1,0:T(4,128)}) custom-call(bf16[8,8,2560]{2,1,0:T(8,128)(2,1)S(1)} %all_to_all.5.refs_0_), custom_call_target="tpu_custom_call" | custom-call | flops 100000 | bytes 10000 | tf_op jit(solution)/shard_map/pallas_call | solution.py:344
  (8 shorter events, 0.0 us)
Async XLA Ops:
  0.7 6.5 %copy-start = (bf16[256,6912]{1,0:T(8,128)(2,1)S(1)}, bf16[256,6912]{1,0:T(8,128)(2,1)}, u32[]{:S(2)}) copy-start(bf16[256,6912]{1,0:T(8,128)(2,1)} %weight.2) | copy-start | bytes 10616836
  3.0 24.8 %copy-start.1 = (bf16[256,6912]{1,0:T(8,128)(2,1)S(1)}, bf16[256,6912]{1,0:T(8,128)(2,1)}, u32[]{:S(2)}) copy-start(bf16[256,6912]{1,0:T(8,128)(2,1)} %weight.3) | copy-start | bytes 10616836
  3.0 15.8 %collective-permute-start.4 = (bf16[224,512]{1,0:T(8,128)(2,1)S(1)}, bf16[224,512]{1,0:T(8,128)(2,1)S(1)}, u32[]{:S(2)}, u32[]{:S(2)}) collective-permute-start(bf16[224,512]{1,0:T(8,128)(2,1)S(1)} %get-tuple-element.56), channel_id=1, source_target_pairs={{0,2},{1,3},{2,0},{3,1},{4,6},{5,7},{6,4},{7,5},{8,10},{9,11},{10,... | collective-permute-start | bytes 688136 | tf_op jit(solution)/shard_map/ppermute | solution.py:385
  5.3 13.6 %collective-permute-start.5 = (bf16[224,512]{1,0:T(8,128)(2,1)S(1)}, bf16[224,512]{1,0:T(8,128)(2,1)S(1)}, u32[]{:S(2)}, u32[]{:S(2)}) collective-permute-start(bf16[224,512]{1,0:T(8,128)(2,1)S(1)} %get-tuple-element.57), channel_id=1, source_target_pairs={{0,1},{1,0},{2,3},{3,2},{4,5},{5,4},{6,7},{7,6},{8,9},{9,8},{10,11... | collective-permute-start | bytes 688136 | tf_op jit(solution)/shard_map/ppermute | solution.py:385
  6.7 12.2 %collective-permute-start.6 = (bf16[224,512]{1,0:T(8,128)(2,1)S(1)}, bf16[224,512]{1,0:T(8,128)(2,1)S(1)}, u32[]{:S(2)}, u32[]{:S(2)}) collective-permute-start(bf16[224,512]{1,0:T(8,128)(2,1)S(1)} %get-tuple-element.58), channel_id=1, source_target_pairs={{0,3},{1,2},{2,1},{3,0},{4,7},{5,6},{6,5},{7,4},{8,11},{9,10},{10,... | collective-permute-start | bytes 688136 | tf_op jit(solution)/shard_map/ppermute | solution.py:385
  10.3 7.2 %collective-permute-start = (bf16[96,256]{1,0:T(8,128)(2,1)S(1)}, bf16[96,256]{1,0:T(8,128)(2,1)S(1)}, u32[]{:S(2)}, u32[]{:S(2)}) collective-permute-start(bf16[96,256]{1,0:T(8,128)(2,1)S(1)} %get-tuple-element.48), channel_id=1, source_target_pairs={{0,1},{1,0},{2,3},{3,2},{4,8},{5,9},{6,10},{7,11},{8,4},{9,5},{10,... | collective-permute-start | bytes 147464 | tf_op jit(solution)/shard_map/ppermute | solution.py:381
  12.6 4.9 %collective-permute-start.1 = (bf16[96,256]{1,0:T(8,128)(2,1)S(1)}, bf16[96,256]{1,0:T(8,128)(2,1)S(1)}, u32[]{:S(2)}, u32[]{:S(2)}) collective-permute-start(bf16[96,256]{1,0:T(8,128)(2,1)S(1)} %get-tuple-element.49), channel_id=1, source_target_pairs={{0,4},{1,5},{2,6},{3,7},{4,0},{5,1},{6,2},{7,3},{8,12},{9,13},{10,... | collective-permute-start | bytes 147464 | tf_op jit(solution)/shard_map/ppermute | solution.py:381
  18.1 4.2 %collective-permute-start.2 = (bf16[96,256]{1,0:T(8,128)(2,1)S(1)}, bf16[96,256]{1,0:T(8,128)(2,1)S(1)}, u32[]{:S(2)}, u32[]{:S(2)}) collective-permute-start(bf16[96,256]{1,0:T(8,128)(2,1)S(1)} %get-tuple-element.51), channel_id=1, source_target_pairs={{0,4},{1,2},{2,1},{3,7},{4,0},{5,6},{6,5},{7,3},{8,12},{9,10},{10,... | collective-permute-start | bytes 147464 | tf_op jit(solution)/shard_map/ppermute | solution.py:381
  18.7 4.1 %collective-permute-start.3 = (bf16[96,256]{1,0:T(8,128)(2,1)S(1)}, bf16[96,256]{1,0:T(8,128)(2,1)S(1)}, u32[]{:S(2)}, u32[]{:S(2)}) collective-permute-start(bf16[96,256]{1,0:T(8,128)(2,1)S(1)} %get-tuple-element.52.late), channel_id=1, source_target_pairs={{0,1},{1,0},{2,3},{3,2},{4,5},{5,4},{6,7},{7,6},{8,9},{9,8},{10,11... | collective-permute-start | bytes 147464 | tf_op jit(solution)/shard_map/ppermute | solution.py:381
  19.9 11.0 %collective-permute-start.10 = (bf16[768,256]{1,0:T(8,128)(2,1)S(1)}, bf16[768,256]{1,0:T(8,128)(2,1)S(1)}, u32[]{:S(2)}, u32[]{:S(2)}) collective-permute-start(bf16[768,256]{1,0:T(8,128)(2,1)S(1)} %get-tuple-element.61), channel_id=1, source_target_pairs={{0,1},{1,0},{2,3},{3,2},{4,8},{5,9},{6,10},{7,11},{8,4},{9,5},{10,... | collective-permute-start | bytes 1179656 | tf_op jit(solution)/shard_map/ppermute | solution.py:381
  21.9 10.3 %collective-permute-start.11 = (bf16[768,256]{1,0:T(8,128)(2,1)S(1)}, bf16[768,256]{1,0:T(8,128)(2,1)S(1)}, u32[]{:S(2)}, u32[]{:S(2)}) collective-permute-start(bf16[768,256]{1,0:T(8,128)(2,1)S(1)} %get-tuple-element.62), channel_id=1, source_target_pairs={{0,4},{1,5},{2,6},{3,7},{4,0},{5,1},{6,2},{7,3},{8,12},{9,13},{10,... | collective-permute-start | bytes 1179656 | tf_op jit(solution)/shard_map/ppermute | solution.py:381
  23.7 15.9 %collective-permute-start.7 = (bf16[192,512]{1,0:T(8,128)(2,1)S(1)}, bf16[192,512]{1,0:T(8,128)(2,1)S(1)}, u32[]{:S(2)}, u32[]{:S(2)}) collective-permute-start(bf16[192,512]{1,0:T(8,128)(2,1)S(1)} %get-tuple-element.60.g0), channel_id=1, source_target_pairs={{0,2},{1,3},{2,0},{3,1},{4,6},{5,7},{6,4},{7,5},{8,10},{9,11},{10,... | collective-permute-start | bytes 589832 | tf_op jit(solution)/shard_map/ppermute | solution.py:385
  24.7 14.8 %collective-permute-start.8 = (bf16[192,512]{1,0:T(8,128)(2,1)S(1)}, bf16[192,512]{1,0:T(8,128)(2,1)S(1)}, u32[]{:S(2)}, u32[]{:S(2)}) collective-permute-start(bf16[192,512]{1,0:T(8,128)(2,1)S(1)} %get-tuple-element.60.g0), channel_id=1, source_target_pairs={{0,1},{1,0},{2,3},{3,2},{4,5},{5,4},{6,7},{7,6},{8,9},{9,8},{10,11... | collective-permute-start | bytes 589832 | tf_op jit(solution)/shard_map/ppermute | solution.py:385
  27.3 12.2 %collective-permute-start.9 = (bf16[192,512]{1,0:T(8,128)(2,1)S(1)}, bf16[192,512]{1,0:T(8,128)(2,1)S(1)}, u32[]{:S(2)}, u32[]{:S(2)}) collective-permute-start(bf16[192,512]{1,0:T(8,128)(2,1)S(1)} %get-tuple-element.60.g0), channel_id=1, source_target_pairs={{0,3},{1,2},{2,1},{3,0},{4,7},{5,6},{6,5},{7,4},{8,11},{9,10},{10,... | collective-permute-start | bytes 589832 | tf_op jit(solution)/shard_map/ppermute | solution.py:385
  30.9 5.9 %collective-permute-start.12 = (bf16[96,256]{1,0:T(8,128)(2,1)S(1)}, bf16[96,256]{1,0:T(8,128)(2,1)S(1)}, u32[]{:S(2)}, u32[]{:S(2)}) collective-permute-start(bf16[96,256]{1,0:T(8,128)(2,1)S(1)} %get-tuple-element.67), channel_id=1, source_target_pairs={{0,1},{1,0},{2,3},{3,2},{4,8},{5,9},{6,10},{7,11},{8,4},{9,5},{10,... | collective-permute-start | bytes 147464 | tf_op jit(solution)/shard_map/ppermute | solution.py:381
  32.2 4.6 %collective-permute-start.13 = (bf16[96,256]{1,0:T(8,128)(2,1)S(1)}, bf16[96,256]{1,0:T(8,128)(2,1)S(1)}, u32[]{:S(2)}, u32[]{:S(2)}) collective-permute-start(bf16[96,256]{1,0:T(8,128)(2,1)S(1)} %get-tuple-element.68), channel_id=1, source_target_pairs={{0,4},{1,5},{2,6},{3,7},{4,0},{5,1},{6,2},{7,3},{8,12},{9,13},{10,... | collective-permute-start | bytes 147464 | tf_op jit(solution)/shard_map/ppermute | solution.py:381
  37.4 6.3 %collective-permute-start.15 = (bf16[96,256]{1,0:T(8,128)(2,1)S(1)}, bf16[96,256]{1,0:T(8,128)(2,1)S(1)}, u32[]{:S(2)}, u32[]{:S(2)}) collective-permute-start(bf16[96,256]{1,0:T(8,128)(2,1)S(1)} %get-tuple-element.72), channel_id=1, source_target_pairs={{0,4},{1,2},{2,1},{3,7},{4,0},{5,6},{6,5},{7,3},{8,12},{9,10},{10,... | collective-permute-start | bytes 147464 | tf_op jit(solution)/shard_map/ppermute | solution.py:381
  39.5 4.1 %collective-permute-start.16 = (bf16[96,256]{1,0:T(8,128)(2,1)S(1)}, bf16[96,256]{1,0:T(8,128)(2,1)S(1)}, u32[]{:S(2)}, u32[]{:S(2)}) collective-permute-start(bf16[96,256]{1,0:T(8,128)(2,1)S(1)} %get-tuple-element.69.late), channel_id=1, source_target_pairs={{0,1},{1,0},{2,3},{3,2},{4,5},{5,4},{6,7},{7,6},{8,9},{9,8},{10,11... | collective-permute-start | bytes 147464 | tf_op jit(solution)/shard_map/ppermute | solution.py:381
  41.3 3.7 %collective-permute-start.14 = (f32[128,1792]{1,0:T(8,128)S(1)}, f32[128,1792]{1,0:T(8,128)S(1)}, u32[]{:S(2)}, u32[]{:S(2)}) collective-permute-start(f32[128,1792]{1,0:T(8,128)S(1)} %get-tuple-element.71), channel_id=1, source_target_pairs={{0,4},{4,0},{8,12},{12,8},{16,20},{20,16},{24,28},{28,24},{32,36},... | collective-permute-start | bytes 2752520 | tf_op jit(solution)/shard_map/ppermute | solution.py:385
  43.3 7.3 %collective-permute-start.20 = (bf16[128,1792]{1,0:T(8,128)(2,1)S(1)}, bf16[128,1792]{1,0:T(8,128)(2,1)S(1)}, u32[]{:S(2)}, u32[]{:S(2)}) collective-permute-start(bf16[128,1792]{1,0:T(8,128)(2,1)S(1)} %get-tuple-element.81), channel_id=1, source_target_pairs={{0,4},{4,0},{8,12},{12,8},{16,20},{20,16},{24,28},{28,24},{32,36},... | collective-permute-start | bytes 1376264 | tf_op jit(solution)/shard_map/ppermute | solution.py:385
  44.6 6.0 %collective-permute-start.21 = (bf16[128,256]{1,0:T(8,128)(2,1)S(1)}, bf16[128,256]{1,0:T(8,128)(2,1)S(1)}, u32[]{:S(2)}, u32[]{:S(2)}) collective-permute-start(bf16[128,256]{1,0:T(8,128)(2,1)S(1)} %get-tuple-element.82), channel_id=1, source_target_pairs={{0,4},{4,0},{8,12},{12,8},{16,20},{20,16},{24,28},{28,24},{32,36},... | collective-permute-start | bytes 196616 | tf_op jit(solution)/shard_map/ppermute | solution.py:385
  45.6 9.8 %collective-permute-start.17 = (bf16[32,1792]{1,0:T(8,128)(2,1)S(1)}, bf16[32,1792]{1,0:T(8,128)(2,1)S(1)}, u32[]{:S(2)}, u32[]{:S(2)}) collective-permute-start(bf16[32,1792]{1,0:T(8,128)(2,1)S(1)} %get-tuple-element.78), channel_id=1, source_target_pairs={{0,128},{4,132},{8,136},{12,140},{16,144},{20,148},{24,152},{28,15... | collective-permute-start | bytes 344072 | tf_op jit(solution)/shard_map/ppermute | solution.py:385
  49.6 7.6 %collective-permute-start.18 = (bf16[32,1792]{1,0:T(8,128)(2,1)S(1)}, bf16[32,1792]{1,0:T(8,128)(2,1)S(1)}, u32[]{:S(2)}, u32[]{:S(2)}) collective-permute-start(bf16[32,1792]{1,0:T(8,128)(2,1)S(1)} %get-tuple-element.79), channel_id=1, source_target_pairs={{0,64},{4,68},{8,72},{12,76},{16,80},{20,84},{24,88},{28,92},{32,9... | collective-permute-start | bytes 344072 | tf_op jit(solution)/shard_map/ppermute | solution.py:385
  50.5 10.1 %collective-permute-start.19 = (bf16[32,1792]{1,0:T(8,128)(2,1)S(1)}, bf16[32,1792]{1,0:T(8,128)(2,1)S(1)}, u32[]{:S(2)}, u32[]{:S(2)}) collective-permute-start(bf16[32,1792]{1,0:T(8,128)(2,1)S(1)} %get-tuple-element.80), channel_id=1, source_target_pairs={{0,192},{4,196},{8,200},{12,204},{16,208},{20,212},{24,216},{28,22... | collective-permute-start | bytes 344072 | tf_op jit(solution)/shard_map/ppermute | solution.py:385
  51.3 9.9 %collective-permute-start.22 = (bf16[32,2304]{1,0:T(8,128)(2,1)S(1)}, bf16[32,2304]{1,0:T(8,128)(2,1)S(1)}, u32[]{:S(2)}, u32[]{:S(2)}) collective-permute-start(bf16[32,2304]{1,0:T(8,128)(2,1)S(1)} %get-tuple-element.84), channel_id=1, source_target_pairs={{0,128},{4,132},{8,136},{12,140},{16,144},{20,148},{24,152},{28,15... | collective-permute-start | bytes 442376 | tf_op jit(solution)/shard_map/ppermute | solution.py:385
  54.4 8.4 %collective-permute-start.23 = (bf16[32,2304]{1,0:T(8,128)(2,1)S(1)}, bf16[32,2304]{1,0:T(8,128)(2,1)S(1)}, u32[]{:S(2)}, u32[]{:S(2)}) collective-permute-start(bf16[32,2304]{1,0:T(8,128)(2,1)S(1)} %get-tuple-element.85), channel_id=1, source_target_pairs={{0,64},{4,68},{8,72},{12,76},{16,80},{20,84},{24,88},{28,92},{32,9... | collective-permute-start | bytes 442376 | tf_op jit(solution)/shard_map/ppermute | solution.py:385
  55.4 7.6 %collective-permute-start.24 = (bf16[32,2304]{1,0:T(8,128)(2,1)S(1)}, bf16[32,2304]{1,0:T(8,128)(2,1)S(1)}, u32[]{:S(2)}, u32[]{:S(2)}) collective-permute-start(bf16[32,2304]{1,0:T(8,128)(2,1)S(1)} %get-tuple-element.86), channel_id=1, source_target_pairs={{0,192},{4,196},{8,200},{12,204},{16,208},{20,212},{24,216},{28,22... | collective-permute-start | bytes 442376 | tf_op jit(solution)/shard_map/ppermute | solution.py:385

commit v11 on v10

--- a/solution.py
+++ b/solution.py
@@ -14,6 +14,7 @@
 HB = 32
 EXT = S + 8 * HB
 QW = 1728
+HALF = 896
 BF = jnp.bfloat16
 F32 = jnp.float32
 
@@ -265,54 +266,91 @@
         send[:, lanes] = block[128:256].astype(send.dtype)
 
 
-def merge_two_kernel(place, keep, come, late, *outs):
+def chunk(place, turn):
+    return pl.ds(pl.multiple_of(32 * ((place[0] // 16) ^ turn), 32), 32)
+
+
+def merge_two_kernel(place, keep, come, late, to1, to3, own, across):
+    part = [keep[chunk(place, t), :] + come[chunk(place, t), :] for t in range(4)]
+    to1[0:32, :] = part[1][:, 0:HALF].astype(BF)
+    to1[32:64, :] = part[2][:, 0:HALF].astype(BF)
+    to3[0:32, :] = part[3][:, HALF:].astype(BF)
+    to3[32:64, :] = part[2][:, HALF:].astype(BF)
+    own[...] = part[0]
+    across[:, 0:HALF] = part[3][:, 0:HALF]
+    across[:, HALF:] = part[1][:, HALF:]
+
+
+def merge_one_kernel(place, keep, come, rk, rs, late, to1, to3, own, across, mine):
+    part = [
+        keep[chunk(place, t), :].astype(F32) + come[chunk(place, t), :].astype(F32)
+        for t in range(4)
+    ]
+    first = place[0] % 2 == 0
+    rows = []
+    for t in range(4):
+        here, other = rk[chunk(place, t), :], rs[chunk(place, t), :]
+        rows.append((jnp.where(first, here, other), jnp.where(first, other, here)))
+    for out, t, lanes, core in ((to1, 1, slice(0, HALF), 0), (to3, 3, slice(HALF, 7 * C), 1)):
+        out[0:32, 0:HALF] = part[t][:, lanes].astype(BF)
+        out[32:64, 0:HALF] = part[2][:, lanes].astype(BF)
+        out[0:32, HALF : HALF + C] = rows[t][0]
+        out[32:64, HALF : HALF + C] = rows[t][1]
+        out[0:32, HALF + C : HALF + C + 128] = rows[2][core][:, 0:128]
+        out[32:64, HALF + C : HALF + C + 128] = rows[2][core][:, 128:256]
+    own[...] = part[0]
+    across[:, 0:HALF] = part[3][:, 0:HALF]
+    across[:, HALF:] = part[1][:, HALF:]
+    mine[:, 0:C] = rows[0][0]
+    mine[:, C : 2 * C] = rows[0][1]
+
+
+def half_two_kernel(place, own, across, a1, a3, to3, to1, total):
+    to3[...] = (across[:, 0:HALF] + a1[32:64, :].astype(F32)).astype(BF)
+    to1[...] = (across[:, HALF:] + a3[32:64, :].astype(F32)).astype(BF)
+    total[:, 0:HALF] = own[:, 0:HALF] + a1[0:32, :].astype(F32)
+    total[:, HALF:] = own[:, HALF:] + a3[0:32, :].astype(F32)
+
+
+def half_one_kernel(place, own, across, a1, a3, to3, to1, total):
+    for out, ref, lanes in ((to3, a1, slice(0, HALF)), (to1, a3, slice(HALF, 7 * C))):
+        out[:, 0:HALF] = (across[:, lanes] + ref[32:64, 0:HALF].astype(F32)).astype(BF)
+        out[:, HALF : HALF + 128] = ref[0:32, HALF + C : HALF + C + 128]
+        out[:, HALF + 128 : HALF + C] = ref[32:64, HALF + C : HALF + C + 128]
+        total[:, lanes] = own[:, lanes] + ref[0:32, 0:HALF].astype(F32)
+
+
+def line_two_kernel(place, total, b3, b1, out):
+    out[:, 0:HALF] = (total[:, 0:HALF] + b3[...].astype(F32)).astype(BF)
+    out[:, HALF:] = (total[:, HALF:] + b1[...].astype(F32)).astype(BF)
+
+
+def line_one_kernel(place, two, total, mine, a1, a3, b3, b1, out, one):
     line = place[0] // 16
-    for turn, out in enumerate(outs):
-        rows = pl.ds(pl.multiple_of(32 * (line ^ turn), 32), 32)
-        out[...] = (keep[rows, :] + come[rows, :]).astype(BF)
-
-
-def merge_one_kernel(place, keep, come, rk, rs, late, *outs):
-    first = place[0] % 2 == 0
-    line = place[0] // 16
-    for turn, out in enumerate(outs):
-        rows = pl.ds(pl.multiple_of(32 * (line ^ turn), 32), 32)
-        total = keep[rows, :].astype(F32) + come[rows, :].astype(F32)
-        out[:, 0 : 7 * C] = total.astype(BF)
-        mine, other = rk[rows, :], rs[rows, :]
-        out[:, 7 * C : 8 * C] = jnp.where(first, mine, other)
-        out[:, 8 * C : 9 * C] = jnp.where(first, other, mine)
-
-
-def line_two_kernel(place, a0, a2, a1, a3, out):
-    total = a0[...].astype(F32)
-    for part in (a1, a2, a3):
-        total = total + part[...].astype(F32)
-    out[...] = total.astype(BF)
-
-
-def line_one_kernel(place, two, b0, b2, b1, b3, out):
-    line = place[0] // 16
+    one[:, 0:HALF] = (total[:, 0:HALF] + b3[:, 0:HALF].astype(F32)).astype(BF)
+    one[:, HALF:] = (total[:, HALF:] + b1[:, 0:HALF].astype(F32)).astype(BF)
     to, at = iota((64, 32), 0), iota((64, 32), 1)
+    spots = [onehot(((to % 8) // 4 == n) & (at == 4 * (to // 8) + to % 4)) for n in range(2)]
     for n in range(7):
         lanes = slice(n * C, (n + 1) * C)
-        total = b0[:, lanes].astype(F32)
-        for part in (b1, b2, b3):
-            total = total + part[:, lanes].astype(F32)
-        block = jnp.zeros((64, C), F32)
-        for which, value in ((0, total.astype(BF)), (1, two[:, lanes])):
-            spot = ((to % 8) // 4 == which) & (at == 4 * (to // 8) + to % 4)
-            block = block + mm(onehot(spot), value)
+        block = mm(spots[0], one[:, lanes]) + mm(spots[1], two[:, lanes])
         out[:, lanes] = block.astype(BF)
+    direct = slice(HALF, HALF + C)
+    sources = (
+        (0, (mine[:, 0:C], mine[:, C : 2 * C])),
+        (1, (a1[0:32, direct], a1[32:64, direct])),
+        (2, (b3[:, direct], b1[:, direct])),
+        (3, (a3[0:32, direct], a3[32:64, direct])),
+    )
     for n in range(3):
         index = 8 * n + to % 8
-        total = jnp.zeros((64, C), F32)
-        for turn, part in enumerate((b0, b1, b2, b3)):
+        found = jnp.zeros((64, C), F32)
+        for turn, cores in sources:
             from_line = (index // 6 == (line ^ turn)) & (at == 4 * (to // 8) + index % 3)
             for core in range(2):
                 spot = onehot(from_line & ((index % 6) // 3 == core))
-                total = total + mm(spot, part[:, (7 + core) * C : (8 + core) * C])
-        out[:, (7 + n) * C : (8 + n) * C] = total.astype(BF)
+                found = found + mm(spot, cores[core])
+        out[:, (7 + n) * C : (8 + n) * C] = found.astype(BF)
 
 
 def final_kernel(scale, arrived, rows, one, two):
@@ -531,34 +569,59 @@
     )
     rows_come = cross(rows_send, "gx", 1)
 
-    def lines(chunks):
-        return [chunks[0]] + [cross(chunks[d], "gx", 16 * d) for d in (2, 1, 3)]
-
-    two = call(
+    both = lambda a, b: (cross(a, "gx", 16), cross(b, "gx", 48))
+    full = sds((32, wide), F32)
+    first = sds((64, HALF), BF)
+    *sent, own_two, across = call(
         merge_two_kernel,
-        (sds((32, wide), BF),) * 4,
+        (first, first, full, full),
         place,
         keep_two,
         come_two,
         rows_keep,
         late=1,
     )
-    one = call(
+    a1, a3 = both(*sent)
+    second = sds((32, HALF), BF)
+    to3, to1, sum_two = call(
+        half_two_kernel, (second, second, full), place, own_two, across, a1, a3, flops=4 * 10**9
+    )
+    b1, b3 = both(to1, to3)
+    sum_two = call(
+        line_two_kernel, sds((32, wide), BF), place, sum_two, b3, b1, flops=2 * 10**9
+    )
+    first = sds((64, HALF + C + 128), BF)
+    *sent, own_one, across, mine = call(
         merge_one_kernel,
-        (sds((32, 9 * C), BF),) * 4,
+        (first, first, full, full, sds((32, 2 * C), BF)),
         place,
         keep_one,
         come_one,
         rows_keep,
         rows_come,
-        two[0],
+        own_two,
         late=1,
         flops=2 * 10**10,
     )
-    sum_two = call(
-        line_two_kernel, sds((32, wide), BF), place, *lines(two), flops=2 * 10**10
-    )
-    summed = call(line_one_kernel, sds((64, 10 * C), BF), place, sum_two, *lines(one))
+    a1, a3 = both(*sent)
+    second = sds((32, HALF + C), BF)
+    to3, to1, sum_one = call(
+        half_one_kernel, (second, second, full), place, own_one, across, a1, a3
+    )
+    b1, b3 = both(to1, to3)
+    summed = call(
+        line_one_kernel,
+        sds((64, 10 * C), BF),
+        place,
+        sum_two,
+        sum_one,
+        mine,
+        a1,
+        a3,
+        b3,
+        b1,
+        scratch=[pltpu.VMEM((32, wide), BF)],
+    )
     groups = [[16 * y + 2 * z + e for z in range(8)] for y in range(4) for e in range(2)]
     collected = lax.all_to_all(
         summed.reshape(8, 8, 10 * C),

time: 83.1 us -> 83.3 us (level)
  waiting for transfers between devices: 11.3 us -> 13.3 us
  blocking collectives: 17.2 us -> 15.4 us
  Pallas kernels: 24 us -> 25.1 us
    ppermute x15 -> x17, waiting for transfers between devices: 5.31 us -> 7.34 us  [cross(): lax.ppermute(value, axis, [(n, n ^ mask) for n in range(lax.axis_size(axi...]
    all_to_all x1, blocking collectives: 17.2 us -> 15.4 us  [body(): lax.all_to_all(summed.reshape(8, 8, 10 * C), 'gx', split_axis=0, concat_a...]
    pallas_call x16 -> x18, Pallas kernels: 24 us -> 25.1 us  [call(): pl.pallas_call(kernel, out_shape=outs, in_specs=specs, out_specs=jax.tree...]
    ppermute x15 -> x17, starting transfers between devices: 20.2 us -> 19.6 us  [cross(): lax.ppermute(value, axis, [(n, n ^ mask) for n in range(lax.axis_size(axi...]
  transfers between devices with their start and end apart: 25 -> 27, of which waited for: 7 -> 8; matrix products, arithmetic and copies ran while one was open for 0% -> 0% of each run, Pallas kernels for 24% -> 25%
where the time goes in v11:
time: 83.3 us; the launch traced here: 83 us
  starting transfers between devices  28.2 us (34%)
  Pallas kernels  25.1 us (30%)
  blocking collectives  15.4 us (18%)
  waiting for transfers between devices  13.3 us (16%)
    pallas_call x18, Pallas kernels, call(): pl.pallas_call(kernel, out_shape=outs, in_specs=specs, out_specs=jax.tree...  25.1 us
    ppermute x17, starting transfers between devices, cross(): lax.ppermute(value, axis, [(n, n ^ mask) for n in range(lax.axis_size(axi...  19.6 us
    all_to_all x1, blocking collectives, body(): lax.all_to_all(summed.reshape(8, 8, 10 * C), 'gx', split_axis=0, concat_a...  15.4 us
    ppermute x10, starting transfers between devices, swap(): return lax.ppermute(value, ('gx', 'gy'), pairs)  8.57 us
    ppermute x17, waiting for transfers between devices, cross(): lax.ppermute(value, axis, [(n, n ^ mask) for n in range(lax.axis_size(axi...  7.34 us
    ppermute x10, waiting for transfers between devices, swap(): return lax.ppermute(value, ('gx', 'gy'), pairs)  6.01 us
  transfers between devices with their start and end apart: 27, of which 8 were waited for; matrix products, arithmetic and copies ran while one was open for 0% of the time, Pallas kernels for 25%

profile of v11, /device:TPU:2, one launch (start us, length us, event | category | flops | bytes accessed | tf_op | source)
XLA Modules:
  0.0 83.0 jit_solution(15200193722681828044)
XLA Ops:
  0.6 0.1 pad_add_fusion.place
  0.7 2.3 %shard_map.103 = (bf16[224,512]{1,0:T(8,128)(2,1)S(1)}, bf16[224,512]{1,0:T(8,128)(2,1)S(1)}, bf16[224,512]{1,0:T(8,128)(2,1)S(1)}, bf16[224,512]{1,0:T(8,128)(2...) custom-call(s32[2]{0:T(128)S(1)} %pad_add_fusion.place, ...), custom_call_target="tpu_custom_call" | custom-call | flops 4000000000 | bytes 10000 | tf_op jit(solution)/shard_map/pallas_call | solution.py:382
  3.0 0.0 copy-start.1
  3.0 2.2 %collective-permute-start.4 = (bf16[224,512]{1,0:T(8,128)(2,1)S(1)}, bf16[224,512]{1,0:T(8,128)(2,1)S(1)}, u32[]{:S(2)}, u32[]{:S(2)}) collective-permute-start(bf16[224,512]{1,0:T(8,128)(2,1)S(1)} %get-tuple-element.63), channel_id=1, source_target_pairs={{0,2},{1,3},{2,0},{3,1},{4,6},{5,7},{6,4},{7,5},{8,10},{9,11},{10,... | collective-permute-start | bytes 688136 | tf_op jit(solution)/shard_map/ppermute | solution.py:423
  5.3 1.4 %collective-permute-start.5 = (bf16[224,512]{1,0:T(8,128)(2,1)S(1)}, bf16[224,512]{1,0:T(8,128)(2,1)S(1)}, u32[]{:S(2)}, u32[]{:S(2)}) collective-permute-start(bf16[224,512]{1,0:T(8,128)(2,1)S(1)} %get-tuple-element.64), channel_id=1, source_target_pairs={{0,1},{1,0},{2,3},{3,2},{4,5},{5,4},{6,7},{7,6},{8,9},{9,8},{10,11... | collective-permute-start | bytes 688136 | tf_op jit(solution)/shard_map/ppermute | solution.py:423
  6.7 0.5 collective-permute-start.6
  7.2 3.0 %shard_map.104 = (f32[192,256]{1,0:T(8,128)S(1)}, bf16[96,256]{1,0:T(8,128)(2,1)S(1)}, bf16[96,256]{1,0:T(8,128)(2,1)S(1)}, bf16[64,256]{1,0:T(8,128)(2,1)S(1)}) custom-call(s32[2]{0:T(128)S(1)} %pad_add_fusion.place, f32[32,256]{1,0:T(8,128)S(1)} %get-tuple-element.52.nbt, bf16[192,256]{1,0:T(8,128)(2,1)S(1)} %get-tuple-element.53.grad, ...), custom_call_target="tpu_custom_call" | custom-call | flops 100000 | bytes 10000 | tf_op jit(solution)/shard_map/pallas_call | solution.py:382
  10.3 2.4 %collective-permute-start = (bf16[96,256]{1,0:T(8,128)(2,1)S(1)}, bf16[96,256]{1,0:T(8,128)(2,1)S(1)}, u32[]{:S(2)}, u32[]{:S(2)}) collective-permute-start(bf16[96,256]{1,0:T(8,128)(2,1)S(1)} %get-tuple-element.55), channel_id=1, source_target_pairs={{0,1},{1,0},{2,3},{3,2},{4,8},{5,9},{6,10},{7,11},{8,4},{9,5},{10,... | collective-permute-start | bytes 147464 | tf_op jit(solution)/shard_map/ppermute | solution.py:419
  12.6 0.0 collective-permute-start.1
  12.6 4.9 %collective-permute-done.m2 = bf16[96,256]{1,0:T(8,128)(2,1)S(1)} collective-permute-done((bf16[96,256]{1,0:T(8,128)(2,1)S(1)}, bf16[96,256]{1,0:T(8,128)(2,1)S(1)}, u32[]{:S(2)}, u32[]{:S(2)}) %collective-permute-start) | collective-permute-done | bytes 49184 | tf_op jit(solution)/shard_map/ppermute | solution.py:419
  17.5 0.6 shard_map.105
  18.1 0.6 collective-permute-start.2
  18.7 0.2 collective-permute-start.3
  18.8 0.0 collective-permute-done.4.p2
  18.8 0.0 collective-permute-done.5.p1
  18.8 0.0 collective-permute-done.6.p3
  18.9 1.1 %shard_map.106 = (bf16[768,256]{1,0:T(8,128)(2,1)S(1)}, bf16[768,256]{1,0:T(8,128)(2,1)S(1)}, bf16[4,64,512]{2,1,0:T(8,128)(2,1)S(1)}) custom-call(s32[2]{0:T(128)S(1)} %pad_add_fusion.place, bf16[224,512]{1,0:T(8,128)(2,1)S(1)} %get-tuple-element.62.p0, bf16[224,512]{1,0:T(8,128)(2,1)S(1)} %collective-permute-done.4.p2, ...), custom_call_target="tpu_custom_call" | custom-call | flops 100000 | bytes 10000 | tf_op jit(solution)/shard_map/pallas_call | solution.py:382
  19.9 2.0 %collective-permute-start.10 = (bf16[768,256]{1,0:T(8,128)(2,1)S(1)}, bf16[768,256]{1,0:T(8,128)(2,1)S(1)}, u32[]{:S(2)}, u32[]{:S(2)}) collective-permute-start(bf16[768,256]{1,0:T(8,128)(2,1)S(1)} %get-tuple-element.68), channel_id=1, source_target_pairs={{0,1},{1,0},{2,3},{3,2},{4,8},{5,9},{6,10},{7,11},{8,4},{9,5},{10,... | collective-permute-start | bytes 1179656 | tf_op jit(solution)/shard_map/ppermute | solution.py:419
  21.9 0.3 collective-permute-done.2.n2
  22.2 0.5 collective-permute-done.3.n1
  22.8 0.9 %shard_map.107 = (bf16[192,256]{1,0:T(8,128)(2,1)S(1)}, bf16[192,512]{1,0:T(8,128)(2,1)S(1)}) custom-call(s32[2]{0:T(128)S(1)} %pad_add_fusion.place, f32[192,256]{1,0:T(8,128)S(1)} %get-tuple-element.54.late.own, bf16[96,256]{1,0:T(8,128)(2,1)S(1)} %collective-permute-done.m2, bf16[96,256]{1,0:T(8,128)(2,1)S(1)} %collective-permute-done.1.m1, ...), custom_call_target="tpu_custom_call" | custom-call | flops 100000 | bytes 10000 | tf_op jit(solution)/shard_map/pallas_call | solution.py:382
  23.7 1.0 %collective-permute-start.7 = (bf16[192,512]{1,0:T(8,128)(2,1)S(1)}, bf16[192,512]{1,0:T(8,128)(2,1)S(1)}, u32[]{:S(2)}, u32[]{:S(2)}) collective-permute-start(bf16[192,512]{1,0:T(8,128)(2,1)S(1)} %get-tuple-element.67.g0), channel_id=1, source_target_pairs={{0,2},{1,3},{2,0},{3,1},{4,6},{5,7},{6,4},{7,5},{8,10},{9,11},{10,... | collective-permute-start | bytes 589832 | tf_op jit(solution)/shard_map/ppermute | solution.py:423
  24.7 2.6 %collective-permute-start.8 = (bf16[192,512]{1,0:T(8,128)(2,1)S(1)}, bf16[192,512]{1,0:T(8,128)(2,1)S(1)}, u32[]{:S(2)}, u32[]{:S(2)}) collective-permute-start(bf16[192,512]{1,0:T(8,128)(2,1)S(1)} %get-tuple-element.67.g0), channel_id=1, source_target_pairs={{0,1},{1,0},{2,3},{3,2},{4,5},{5,4},{6,7},{7,6},{8,9},{9,8},{10,11... | collective-permute-start | bytes 589832 | tf_op jit(solution)/shard_map/ppermute | solution.py:423
  27.3 0.5 collective-permute-start.9
  27.9 3.0 %shard_map.108 = (f32[192,256]{1,0:T(8,128)S(1)}, bf16[96,256]{1,0:T(8,128)(2,1)S(1)}, bf16[96,256]{1,0:T(8,128)(2,1)S(1)}, bf16[64,256]{1,0:T(8,128)(2,1)S(1)}) custom-call(s32[2]{0:T(128)S(1)} %pad_add_fusion.place, f32[32,256]{1,0:T(8,128)S(1)} %get-tuple-element.52.nbt, bf16[192,256]{1,0:T(8,128)(2,1)S(1)} %get-tuple-element.70.grad, ...), custom_call_target="tpu_custom_call" | custom-call | flops 4000000000 | bytes 10000 | tf_op jit(solution)/shard_map/pallas_call | solution.py:382
  30.9 0.0 collective-permute-done.10.r2
  30.9 1.3 %collective-permute-start.12 = (bf16[96,256]{1,0:T(8,128)(2,1)S(1)}, bf16[96,256]{1,0:T(8,128)(2,1)S(1)}, u32[]{:S(2)}, u32[]{:S(2)}) collective-permute-start(bf16[96,256]{1,0:T(8,128)(2,1)S(1)} %get-tuple-element.74), channel_id=1, source_target_pairs={{0,1},{1,0},{2,3},{3,2},{4,8},{5,9},{6,10},{7,11},{8,4},{9,5},{10,... | collective-permute-start | bytes 147464 | tf_op jit(solution)/shard_map/ppermute | solution.py:419
  32.2 0.0 collective-permute-done.11.r1
  32.2 4.3 %shard_map.109 = (bf16[768,1792]{1,0:T(8,128)(2,1)S(1)}, bf16[768,1792]{1,0:T(8,128)(2,1)S(1)}) custom-call(s32[2]{0:T(128)S(1)} %pad_add_fusion.place, bf16[224,512]{1,0:T(8,128)(2,1)S(1)} %get-tuple-element.62.p0, bf16[224,512]{1,0:T(8,128)(2,1)S(1)} %collective-permute-done.4.p2, bf16[224,512]{1,0:T(8,128)(2,1)S(1)} %collective-permute-done.5.p1, ...), custom_call_target="tpu_custom_call" | custom-call | flops 4000000000 | bytes 10000 | tf_op jit(solution)/shard_map/pallas_call | solution.py:382
  36.5 0.3 collective-permute-done.12.m2
  36.8 0.6 shard_map.110
  37.4 2.2 %collective-permute-start.15 = (bf16[96,256]{1,0:T(8,128)(2,1)S(1)}, bf16[96,256]{1,0:T(8,128)(2,1)S(1)}, u32[]{:S(2)}, u32[]{:S(2)}) collective-permute-start(bf16[96,256]{1,0:T(8,128)(2,1)S(1)} %get-tuple-element.79), channel_id=1, source_target_pairs={{0,4},{1,2},{2,1},{3,7},{4,0},{5,6},{6,5},{7,3},{8,12},{9,10},{10,... | collective-permute-start | bytes 147464 | tf_op jit(solution)/shard_map/ppermute | solution.py:419
  39.5 0.0 collective-permute-start.16
  39.5 0.0 collective-permute-done.7.g2
  39.6 0.0 collective-permute-done.9.g3
  39.6 1.7 %shard_map.111 = (f32[128,1792]{1,0:T(8,128)S(1)}, f32[128,1792]{1,0:T(8,128)S(1)}) custom-call(s32[2]{0:T(128)S(1)} %pad_add_fusion.place, bf16[192,512]{1,0:T(8,128)(2,1)S(1)} %get-tuple-element.67.g0, bf16[192,512]{1,0:T(8,128)(2,1)S(1)} %collective-permute-done.7.g2, bf16[192,512]{1,0:T(8,128)(2,1)S(1)} %collective-permute-done.8.g1, ...), custom_call_target="tpu_custom_call" | custom-call | flops 4000000000 | bytes 10000 | tf_op jit(solution)/shard_map/pallas_call | solution.py:382
  41.3 0.3 collective-permute-start.14
  41.6 1.7 %shard_map.112 = (bf16[128,1792]{1,0:T(8,128)(2,1)S(1)}, bf16[128,1792]{1,0:T(8,128)(2,1)S(1)}) custom-call(s32[2]{0:T(128)S(1)} %pad_add_fusion.place, bf16[192,512]{1,0:T(8,128)(2,1)S(1)} %get-tuple-element.67.g0, bf16[192,512]{1,0:T(8,128)(2,1)S(1)} %collective-permute-done.7.g2, bf16[192,512]{1,0:T(8,128)(2,1)S(1)} %collective-permute-done.8.g1, ...), custom_call_target="tpu_custom_call" | custom-call | flops 100000 | bytes 10000 | tf_op jit(solution)/shard_map/pallas_call | solution.py:382
  43.3 0.4 collective-permute-start.21
  43.7 0.0 collective-permute-done.15.n2
  43.7 0.0 collective-permute-done.16.n1
  43.7 1.0 %shard_map.113 = (bf16[128,256]{1,0:T(8,128)(2,1)S(1)}, bf16[128,256]{1,0:T(8,128)(2,1)S(1)}) custom-call(s32[2]{0:T(128)S(1)} %pad_add_fusion.place, f32[192,256]{1,0:T(8,128)S(1)} %get-tuple-element.71.late.own, bf16[96,256]{1,0:T(8,128)(2,1)S(1)} %collective-permute-done.12.m2, bf16[96,256]{1,0:T(8,128)(2,1)S(1)} %collective-permute-done.13.m1, ...), custom_call_target="tpu_custom_call" | custom-call | flops 20000000000 | bytes 10000 | tf_op jit(solution)/shard_map/pallas_call | solution.py:382
  44.6 0.3 collective-permute-start.22
  45.0 0.6 shard_map.114
  45.6 2.3 %collective-permute-start.17 = (bf16[64,896]{1,0:T(8,128)(2,1)S(1)}, bf16[64,896]{1,0:T(8,128)(2,1)S(1)}, u32[]{:S(2)}, u32[]{:S(2)}) collective-permute-start(bf16[64,896]{1,0:T(8,128)(2,1)S(1)} %get-tuple-element.86), channel_id=1, source_target_pairs={{0,64},{4,68},{8,72},{12,76},{16,80},{20,84},{24,88},{28,92},{32,9... | collective-permute-start | bytes 344072 | tf_op jit(solution)/shard_map/ppermute | solution.py:423
  48.0 2.2 %collective-permute-start.18 = (bf16[64,896]{1,0:T(8,128)(2,1)S(1)}, bf16[64,896]{1,0:T(8,128)(2,1)S(1)}, u32[]{:S(2)}, u32[]{:S(2)}) collective-permute-start(bf16[64,896]{1,0:T(8,128)(2,1)S(1)} %get-tuple-element.87), channel_id=1, source_target_pairs={{0,192},{4,196},{8,200},{12,204},{16,208},{20,212},{24,216},{28,22... | collective-permute-start | bytes 344072 | tf_op jit(solution)/shard_map/ppermute | solution.py:423
  50.1 0.0 collective-permute-done.22.rs
  50.1 0.7 shard_map.117
  50.8 1.1 %collective-permute-start.23 = (bf16[64,1280]{1,0:T(8,128)(2,1)S(1)}, bf16[64,1280]{1,0:T(8,128)(2,1)S(1)}, u32[]{:S(2)}, u32[]{:S(2)}) collective-permute-start(bf16[64,1280]{1,0:T(8,128)(2,1)S(1)} %get-tuple-element.95), channel_id=1, source_target_pairs={{0,64},{4,68},{8,72},{12,76},{16,80},{20,84},{24,88},{28,92},{32,9... | collective-permute-start | bytes 491528 | tf_op jit(solution)/shard_map/ppermute | solution.py:423
  51.9 0.6 collective-permute-start.24
  52.5 1.9 %collective-permute-done.18.a3 = bf16[64,896]{1,0:T(8,128)(2,1)S(1)} collective-permute-done((bf16[64,896]{1,0:T(8,128)(2,1)S(1)}, bf16[64,896]{1,0:T(8,128)(2,1)S(1)}, u32[]{:S(2)}, u32[]{:S(2)}) %collective-permute-start.18) | collective-permute-done | bytes 114720 | tf_op jit(solution)/shard_map/ppermute | solution.py:423
  54.4 0.6 shard_map.115
  55.0 2.6 %collective-permute-start.19 = (bf16[32,896]{1,0:T(8,128)(2,1)S(1)}, bf16[32,896]{1,0:T(8,128)(2,1)S(1)}, u32[]{:S(2)}, u32[]{:S(2)}) collective-permute-start(bf16[32,896]{1,0:T(8,128)(2,1)S(1)} %get-tuple-element.89), channel_id=1, source_target_pairs={{0,192},{4,196},{8,200},{12,204},{16,208},{20,212},{24,216},{28,22... | collective-permute-start | bytes 172040 | tf_op jit(solution)/shard_map/ppermute | solution.py:423
  57.6 0.2 collective-permute-start.20
  57.8 1.6 %collective-permute-done.24.a3 = bf16[64,1280]{1,0:T(8,128)(2,1)S(1)} collective-permute-done((bf16[64,1280]{1,0:T(8,128)(2,1)S(1)}, bf16[64,1280]{1,0:T(8,128)(2,1)S(1)}, u32[]{:S(2)}, u32[]{:S(2)}) %collective-permute-start.24) | collective-permute-done | bytes 163872 | tf_op jit(solution)/shard_map/ppermute | solution.py:423
  59.3 0.6 shard_map.118
  59.9 0.9 %collective-permute-start.25 = (bf16[32,1152]{1,0:T(8,128)(2,1)S(1)}, bf16[32,1152]{1,0:T(8,128)(2,1)S(1)}, u32[]{:S(2)}, u32[]{:S(2)}) collective-permute-start(bf16[32,1152]{1,0:T(8,128)(2,1)S(1)} %get-tuple-element.99), channel_id=1, source_target_pairs={{0,192},{4,196},{8,200},{12,204},{16,208},{20,212},{24,216},{28,22... | collective-permute-start | bytes 221192 | tf_op jit(solution)/shard_map/ppermute | solution.py:423
  60.8 0.4 collective-permute-start.26
  61.2 0.6 collective-permute-done.20.b1
  61.8 0.6 shard_map.116.two
  62.4 3.2 %collective-permute-done.25.b3 = bf16[32,1152]{1,0:T(8,128)(2,1)S(1)} collective-permute-done((bf16[32,1152]{1,0:T(8,128)(2,1)S(1)}, bf16[32,1152]{1,0:T(8,128)(2,1)S(1)}, u32[]{:S(2)}, u32[]{:S(2)}) %collective-permute-start.25) | collective-permute-done | bytes 73760 | tf_op jit(solution)/shard_map/ppermute | solution.py:423
  65.6 1.1 %shard_map.119 = bf16[64,2560]{1,0:T(8,128)(2,1)S(1)} custom-call(s32[2]{0:T(128)S(1)} %pad_add_fusion.place, bf16[32,1792]{1,0:T(8,128)(2,1)S(1)} %shard_map.116.two, f32[32,1792]{1,0:T(8,128)S(1)} %get-tuple-element.97.total, bf16[32,512]{1,0:T(8,128)(2,1)S(1)} %get-tuple-element.98.mine, bf16[64,1280]{1,0:T(8,128)(2,1)S(1)} %collective-permute-done.23.a1, ...), custom_call_target="tpu_custom_call" | custom-call | flops 100000 | bytes 10000 | tf_op jit(solution)/shard_map/pallas_call | solution.py:382
  66.7 15.4 %all_to_all.5.refs_0_ = bf16[8,8,2560]{2,1,0:T(8,128)(2,1)S(1)} all-to-all(bf16[8,8,2560]{2,1,0:T(8,128)(2,1)S(1)} %bitcast.5), channel_id=1, replica_groups={{0,8,16,24,32,40,48,56},{4,12,20,28,36,44,52,60},{64,72,80,88,96,104,11..., dimensions={0} | all-to-all | bytes 655360 | tf_op jit(solution)/shard_map/all_to_all | solution.py:626
  82.0 0.9 %shard_map.120 = (bf16[192,256]{1,0:T(8,128)(2,1)}, f32[4,1728]{1,0:T(4,128)}, f32[4,1728]{1,0:T(4,128)}) custom-call(bf16[8,8,2560]{2,1,0:T(8,128)(2,1)S(1)} %all_to_all.5.refs_0_), custom_call_target="tpu_custom_call" | custom-call | flops 100000 | bytes 10000 | tf_op jit(solution)/shard_map/pallas_call | solution.py:382
  (14 shorter events, 0.0 us)
Async XLA Ops:
  0.7 6.5 %copy-start = (bf16[256,6912]{1,0:T(8,128)(2,1)S(1)}, bf16[256,6912]{1,0:T(8,128)(2,1)}, u32[]{:S(2)}) copy-start(bf16[256,6912]{1,0:T(8,128)(2,1)} %weight.2) | copy-start | bytes 10616836
  3.0 24.8 %copy-start.1 = (bf16[256,6912]{1,0:T(8,128)(2,1)S(1)}, bf16[256,6912]{1,0:T(8,128)(2,1)}, u32[]{:S(2)}) copy-start(bf16[256,6912]{1,0:T(8,128)(2,1)} %weight.3) | copy-start | bytes 10616836
  3.0 15.8 %collective-permute-start.4 = (bf16[224,512]{1,0:T(8,128)(2,1)S(1)}, bf16[224,512]{1,0:T(8,128)(2,1)S(1)}, u32[]{:S(2)}, u32[]{:S(2)}) collective-permute-start(bf16[224,512]{1,0:T(8,128)(2,1)S(1)} %get-tuple-element.63), channel_id=1, source_target_pairs={{0,2},{1,3},{2,0},{3,1},{4,6},{5,7},{6,4},{7,5},{8,10},{9,11},{10,... | collective-permute-start | bytes 688136 | tf_op jit(solution)/shard_map/ppermute | solution.py:423
  5.3 13.6 %collective-permute-start.5 = (bf16[224,512]{1,0:T(8,128)(2,1)S(1)}, bf16[224,512]{1,0:T(8,128)(2,1)S(1)}, u32[]{:S(2)}, u32[]{:S(2)}) collective-permute-start(bf16[224,512]{1,0:T(8,128)(2,1)S(1)} %get-tuple-element.64), channel_id=1, source_target_pairs={{0,1},{1,0},{2,3},{3,2},{4,5},{5,4},{6,7},{7,6},{8,9},{9,8},{10,11... | collective-permute-start | bytes 688136 | tf_op jit(solution)/shard_map/ppermute | solution.py:423
  6.7 12.2 %collective-permute-start.6 = (bf16[224,512]{1,0:T(8,128)(2,1)S(1)}, bf16[224,512]{1,0:T(8,128)(2,1)S(1)}, u32[]{:S(2)}, u32[]{:S(2)}) collective-permute-start(bf16[224,512]{1,0:T(8,128)(2,1)S(1)} %get-tuple-element.65), channel_id=1, source_target_pairs={{0,3},{1,2},{2,1},{3,0},{4,7},{5,6},{6,5},{7,4},{8,11},{9,10},{10,... | collective-permute-start | bytes 688136 | tf_op jit(solution)/shard_map/ppermute | solution.py:423
  10.3 7.2 %collective-permute-start = (bf16[96,256]{1,0:T(8,128)(2,1)S(1)}, bf16[96,256]{1,0:T(8,128)(2,1)S(1)}, u32[]{:S(2)}, u32[]{:S(2)}) collective-permute-start(bf16[96,256]{1,0:T(8,128)(2,1)S(1)} %get-tuple-element.55), channel_id=1, source_target_pairs={{0,1},{1,0},{2,3},{3,2},{4,8},{5,9},{6,10},{7,11},{8,4},{9,5},{10,... | collective-permute-start | bytes 147464 | tf_op jit(solution)/shard_map/ppermute | solution.py:419
  12.6 4.9 %collective-permute-start.1 = (bf16[96,256]{1,0:T(8,128)(2,1)S(1)}, bf16[96,256]{1,0:T(8,128)(2,1)S(1)}, u32[]{:S(2)}, u32[]{:S(2)}) collective-permute-start(bf16[96,256]{1,0:T(8,128)(2,1)S(1)} %get-tuple-element.56), channel_id=1, source_target_pairs={{0,4},{1,5},{2,6},{3,7},{4,0},{5,1},{6,2},{7,3},{8,12},{9,13},{10,... | collective-permute-start | bytes 147464 | tf_op jit(solution)/shard_map/ppermute | solution.py:419
  18.1 4.2 %collective-permute-start.2 = (bf16[96,256]{1,0:T(8,128)(2,1)S(1)}, bf16[96,256]{1,0:T(8,128)(2,1)S(1)}, u32[]{:S(2)}, u32[]{:S(2)}) collective-permute-start(bf16[96,256]{1,0:T(8,128)(2,1)S(1)} %get-tuple-element.58), channel_id=1, source_target_pairs={{0,4},{1,2},{2,1},{3,7},{4,0},{5,6},{6,5},{7,3},{8,12},{9,10},{10,... | collective-permute-start | bytes 147464 | tf_op jit(solution)/shard_map/ppermute | solution.py:419
  18.7 4.1 %collective-permute-start.3 = (bf16[96,256]{1,0:T(8,128)(2,1)S(1)}, bf16[96,256]{1,0:T(8,128)(2,1)S(1)}, u32[]{:S(2)}, u32[]{:S(2)}) collective-permute-start(bf16[96,256]{1,0:T(8,128)(2,1)S(1)} %get-tuple-element.59.late), channel_id=1, source_target_pairs={{0,1},{1,0},{2,3},{3,2},{4,5},{5,4},{6,7},{7,6},{8,9},{9,8},{10,11... | collective-permute-start | bytes 147464 | tf_op jit(solution)/shard_map/ppermute | solution.py:419
  19.9 11.0 %collective-permute-start.10 = (bf16[768,256]{1,0:T(8,128)(2,1)S(1)}, bf16[768,256]{1,0:T(8,128)(2,1)S(1)}, u32[]{:S(2)}, u32[]{:S(2)}) collective-permute-start(bf16[768,256]{1,0:T(8,128)(2,1)S(1)} %get-tuple-element.68), channel_id=1, source_target_pairs={{0,1},{1,0},{2,3},{3,2},{4,8},{5,9},{6,10},{7,11},{8,4},{9,5},{10,... | collective-permute-start | bytes 1179656 | tf_op jit(solution)/shard_map/ppermute | solution.py:419
  21.9 10.3 %collective-permute-start.11 = (bf16[768,256]{1,0:T(8,128)(2,1)S(1)}, bf16[768,256]{1,0:T(8,128)(2,1)S(1)}, u32[]{:S(2)}, u32[]{:S(2)}) collective-permute-start(bf16[768,256]{1,0:T(8,128)(2,1)S(1)} %get-tuple-element.69), channel_id=1, source_target_pairs={{0,4},{1,5},{2,6},{3,7},{4,0},{5,1},{6,2},{7,3},{8,12},{9,13},{10,... | collective-permute-start | bytes 1179656 | tf_op jit(solution)/shard_map/ppermute | solution.py:419
  23.7 15.9 %collective-permute-start.7 = (bf16[192,512]{1,0:T(8,128)(2,1)S(1)}, bf16[192,512]{1,0:T(8,128)(2,1)S(1)}, u32[]{:S(2)}, u32[]{:S(2)}) collective-permute-start(bf16[192,512]{1,0:T(8,128)(2,1)S(1)} %get-tuple-element.67.g0), channel_id=1, source_target_pairs={{0,2},{1,3},{2,0},{3,1},{4,6},{5,7},{6,4},{7,5},{8,10},{9,11},{10,... | collective-permute-start | bytes 589832 | tf_op jit(solution)/shard_map/ppermute | solution.py:423
  24.7 14.8 %collective-permute-start.8 = (bf16[192,512]{1,0:T(8,128)(2,1)S(1)}, bf16[192,512]{1,0:T(8,128)(2,1)S(1)}, u32[]{:S(2)}, u32[]{:S(2)}) collective-permute-start(bf16[192,512]{1,0:T(8,128)(2,1)S(1)} %get-tuple-element.67.g0), channel_id=1, source_target_pairs={{0,1},{1,0},{2,3},{3,2},{4,5},{5,4},{6,7},{7,6},{8,9},{9,8},{10,11... | collective-permute-start | bytes 589832 | tf_op jit(solution)/shard_map/ppermute | solution.py:423
  27.3 12.2 %collective-permute-start.9 = (bf16[192,512]{1,0:T(8,128)(2,1)S(1)}, bf16[192,512]{1,0:T(8,128)(2,1)S(1)}, u32[]{:S(2)}, u32[]{:S(2)}) collective-permute-start(bf16[192,512]{1,0:T(8,128)(2,1)S(1)} %get-tuple-element.67.g0), channel_id=1, source_target_pairs={{0,3},{1,2},{2,1},{3,0},{4,7},{5,6},{6,5},{7,4},{8,11},{9,10},{10,... | collective-permute-start | bytes 589832 | tf_op jit(solution)/shard_map/ppermute | solution.py:423
  30.9 5.9 %collective-permute-start.12 = (bf16[96,256]{1,0:T(8,128)(2,1)S(1)}, bf16[96,256]{1,0:T(8,128)(2,1)S(1)}, u32[]{:S(2)}, u32[]{:S(2)}) collective-permute-start(bf16[96,256]{1,0:T(8,128)(2,1)S(1)} %get-tuple-element.74), channel_id=1, source_target_pairs={{0,1},{1,0},{2,3},{3,2},{4,8},{5,9},{6,10},{7,11},{8,4},{9,5},{10,... | collective-permute-start | bytes 147464 | tf_op jit(solution)/shard_map/ppermute | solution.py:419
  32.2 4.6 %collective-permute-start.13 = (bf16[96,256]{1,0:T(8,128)(2,1)S(1)}, bf16[96,256]{1,0:T(8,128)(2,1)S(1)}, u32[]{:S(2)}, u32[]{:S(2)}) collective-permute-start(bf16[96,256]{1,0:T(8,128)(2,1)S(1)} %get-tuple-element.75), channel_id=1, source_target_pairs={{0,4},{1,5},{2,6},{3,7},{4,0},{5,1},{6,2},{7,3},{8,12},{9,13},{10,... | collective-permute-start | bytes 147464 | tf_op jit(solution)/shard_map/ppermute | solution.py:419
  37.4 6.3 %collective-permute-start.15 = (bf16[96,256]{1,0:T(8,128)(2,1)S(1)}, bf16[96,256]{1,0:T(8,128)(2,1)S(1)}, u32[]{:S(2)}, u32[]{:S(2)}) collective-permute-start(bf16[96,256]{1,0:T(8,128)(2,1)S(1)} %get-tuple-element.79), channel_id=1, source_target_pairs={{0,4},{1,2},{2,1},{3,7},{4,0},{5,6},{6,5},{7,3},{8,12},{9,10},{10,... | collective-permute-start | bytes 147464 | tf_op jit(solution)/shard_map/ppermute | solution.py:419
  39.5 4.1 %collective-permute-start.16 = (bf16[96,256]{1,0:T(8,128)(2,1)S(1)}, bf16[96,256]{1,0:T(8,128)(2,1)S(1)}, u32[]{:S(2)}, u32[]{:S(2)}) collective-permute-start(bf16[96,256]{1,0:T(8,128)(2,1)S(1)} %get-tuple-element.76.late), channel_id=1, source_target_pairs={{0,1},{1,0},{2,3},{3,2},{4,5},{5,4},{6,7},{7,6},{8,9},{9,8},{10,11... | collective-permute-start | bytes 147464 | tf_op jit(solution)/shard_map/ppermute | solution.py:419
  41.3 3.7 %collective-permute-start.14 = (f32[128,1792]{1,0:T(8,128)S(1)}, f32[128,1792]{1,0:T(8,128)S(1)}, u32[]{:S(2)}, u32[]{:S(2)}) collective-permute-start(f32[128,1792]{1,0:T(8,128)S(1)} %get-tuple-element.78), channel_id=1, source_target_pairs={{0,4},{4,0},{8,12},{12,8},{16,20},{20,16},{24,28},{28,24},{32,36},... | collective-permute-start | bytes 2752520 | tf_op jit(solution)/shard_map/ppermute | solution.py:423
  43.3 6.8 %collective-permute-start.21 = (bf16[128,1792]{1,0:T(8,128)(2,1)S(1)}, bf16[128,1792]{1,0:T(8,128)(2,1)S(1)}, u32[]{:S(2)}, u32[]{:S(2)}) collective-permute-start(bf16[128,1792]{1,0:T(8,128)(2,1)S(1)} %get-tuple-element.91), channel_id=1, source_target_pairs={{0,4},{4,0},{8,12},{12,8},{16,20},{20,16},{24,28},{28,24},{32,36},... | collective-permute-start | bytes 1376264 | tf_op jit(solution)/shard_map/ppermute | solution.py:423
  44.6 5.5 %collective-permute-start.22 = (bf16[128,256]{1,0:T(8,128)(2,1)S(1)}, bf16[128,256]{1,0:T(8,128)(2,1)S(1)}, u32[]{:S(2)}, u32[]{:S(2)}) collective-permute-start(bf16[128,256]{1,0:T(8,128)(2,1)S(1)} %get-tuple-element.92), channel_id=1, source_target_pairs={{0,4},{4,0},{8,12},{12,8},{16,20},{20,16},{24,28},{28,24},{32,36},... | collective-permute-start | bytes 196616 | tf_op jit(solution)/shard_map/ppermute | solution.py:423
  45.6 6.9 %collective-permute-start.17 = (bf16[64,896]{1,0:T(8,128)(2,1)S(1)}, bf16[64,896]{1,0:T(8,128)(2,1)S(1)}, u32[]{:S(2)}, u32[]{:S(2)}) collective-permute-start(bf16[64,896]{1,0:T(8,128)(2,1)S(1)} %get-tuple-element.86), channel_id=1, source_target_pairs={{0,64},{4,68},{8,72},{12,76},{16,80},{20,84},{24,88},{28,92},{32,9... | collective-permute-start | bytes 344072 | tf_op jit(solution)/shard_map/ppermute | solution.py:423
  48.0 6.5 %collective-permute-start.18 = (bf16[64,896]{1,0:T(8,128)(2,1)S(1)}, bf16[64,896]{1,0:T(8,128)(2,1)S(1)}, u32[]{:S(2)}, u32[]{:S(2)}) collective-permute-start(bf16[64,896]{1,0:T(8,128)(2,1)S(1)} %get-tuple-element.87), channel_id=1, source_target_pairs={{0,192},{4,196},{8,200},{12,204},{16,208},{20,212},{24,216},{28,22... | collective-permute-start | bytes 344072 | tf_op jit(solution)/shard_map/ppermute | solution.py:423
  50.8 7.0 %collective-permute-start.23 = (bf16[64,1280]{1,0:T(8,128)(2,1)S(1)}, bf16[64,1280]{1,0:T(8,128)(2,1)S(1)}, u32[]{:S(2)}, u32[]{:S(2)}) collective-permute-start(bf16[64,1280]{1,0:T(8,128)(2,1)S(1)} %get-tuple-element.95), channel_id=1, source_target_pairs={{0,64},{4,68},{8,72},{12,76},{16,80},{20,84},{24,88},{28,92},{32,9... | collective-permute-start | bytes 491528 | tf_op jit(solution)/shard_map/ppermute | solution.py:423
  51.9 7.5 %collective-permute-start.24 = (bf16[64,1280]{1,0:T(8,128)(2,1)S(1)}, bf16[64,1280]{1,0:T(8,128)(2,1)S(1)}, u32[]{:S(2)}, u32[]{:S(2)}) collective-permute-start(bf16[64,1280]{1,0:T(8,128)(2,1)S(1)} %get-tuple-element.96), channel_id=1, source_target_pairs={{0,192},{4,196},{8,200},{12,204},{16,208},{20,212},{24,216},{28,22... | collective-permute-start | bytes 491528 | tf_op jit(solution)/shard_map/ppermute | solution.py:423
  55.0 6.2 %collective-permute-start.19 = (bf16[32,896]{1,0:T(8,128)(2,1)S(1)}, bf16[32,896]{1,0:T(8,128)(2,1)S(1)}, u32[]{:S(2)}, u32[]{:S(2)}) collective-permute-start(bf16[32,896]{1,0:T(8,128)(2,1)S(1)} %get-tuple-element.89), channel_id=1, source_target_pairs={{0,192},{4,196},{8,200},{12,204},{16,208},{20,212},{24,216},{28,22... | collective-permute-start | bytes 172040 | tf_op jit(solution)/shard_map/ppermute | solution.py:423
  57.6 4.2 %collective-permute-start.20 = (bf16[32,896]{1,0:T(8,128)(2,1)S(1)}, bf16[32,896]{1,0:T(8,128)(2,1)S(1)}, u32[]{:S(2)}, u32[]{:S(2)}) collective-permute-start(bf16[32,896]{1,0:T(8,128)(2,1)S(1)} %get-tuple-element.90), channel_id=1, source_target_pairs={{0,64},{4,68},{8,72},{12,76},{16,80},{20,84},{24,88},{28,92},{32,9... | collective-permute-start | bytes 172040 | tf_op jit(solution)/shard_map/ppermute | solution.py:423
  59.9 5.7 %collective-permute-start.25 = (bf16[32,1152]{1,0:T(8,128)(2,1)S(1)}, bf16[32,1152]{1,0:T(8,128)(2,1)S(1)}, u32[]{:S(2)}, u32[]{:S(2)}) collective-permute-start(bf16[32,1152]{1,0:T(8,128)(2,1)S(1)} %get-tuple-element.99), channel_id=1, source_target_pairs={{0,192},{4,196},{8,200},{12,204},{16,208},{20,212},{24,216},{28,22... | collective-permute-start | bytes 221192 | tf_op jit(solution)/shard_map/ppermute | solution.py:423
  60.8 4.8 %collective-permute-start.26 = (bf16[32,1152]{1,0:T(8,128)(2,1)S(1)}, bf16[32,1152]{1,0:T(8,128)(2,1)S(1)}, u32[]{:S(2)}, u32[]{:S(2)}) collective-permute-start(bf16[32,1152]{1,0:T(8,128)(2,1)S(1)} %get-tuple-element.100), channel_id=1, source_target_pairs={{0,64},{4,68},{8,72},{12,76},{16,80},{20,84},{24,88},{28,92},{32,9... | collective-permute-start | bytes 221192 | tf_op jit(solution)/shard_map/ppermute | solution.py:423

commit v12 on v11

--- a/solution.py
+++ b/solution.py
@@ -270,78 +270,64 @@
     return pl.ds(pl.multiple_of(32 * ((place[0] // 16) ^ turn), 32), 32)
 
 
-def merge_two_kernel(place, keep, come, late, to1, to3, own, across):
-    part = [keep[chunk(place, t), :] + come[chunk(place, t), :] for t in range(4)]
-    to1[0:32, :] = part[1][:, 0:HALF].astype(BF)
-    to1[32:64, :] = part[2][:, 0:HALF].astype(BF)
-    to3[0:32, :] = part[3][:, HALF:].astype(BF)
-    to3[32:64, :] = part[2][:, HALF:].astype(BF)
-    own[...] = part[0]
-    across[:, 0:HALF] = part[3][:, 0:HALF]
-    across[:, HALF:] = part[1][:, HALF:]
-
-
-def merge_one_kernel(place, keep, come, rk, rs, late, to1, to3, own, across, mine):
-    part = [
-        keep[chunk(place, t), :].astype(F32) + come[chunk(place, t), :].astype(F32)
-        for t in range(4)
-    ]
+def merge_kernel(place, k2, s2, k1, s1, rk, rs, to1, to3, own, across, mine):
     first = place[0] % 2 == 0
     rows = []
     for t in range(4):
         here, other = rk[chunk(place, t), :], rs[chunk(place, t), :]
         rows.append((jnp.where(first, here, other), jnp.where(first, other, here)))
-    for out, t, lanes, core in ((to1, 1, slice(0, HALF), 0), (to3, 3, slice(HALF, 7 * C), 1)):
-        out[0:32, 0:HALF] = part[t][:, lanes].astype(BF)
-        out[32:64, 0:HALF] = part[2][:, lanes].astype(BF)
-        out[0:32, HALF : HALF + C] = rows[t][0]
-        out[32:64, HALF : HALF + C] = rows[t][1]
-        out[0:32, HALF + C : HALF + C + 128] = rows[2][core][:, 0:128]
-        out[32:64, HALF + C : HALF + C + 128] = rows[2][core][:, 128:256]
-    own[...] = part[0]
-    across[:, 0:HALF] = part[3][:, 0:HALF]
-    across[:, HALF:] = part[1][:, HALF:]
+    for at, keep, come in ((0, k2, s2), (1, k1, s1)):
+        part = [
+            keep[chunk(place, t), :].astype(F32) + come[chunk(place, t), :].astype(F32)
+            for t in range(4)
+        ]
+        lanes = slice(at * HALF, (at + 1) * HALF)
+        low, high = slice(0, HALF), slice(HALF, 2 * HALF)
+        for out, t, side in ((to1, 1, low), (to3, 3, high)):
+            out[0:32, lanes] = part[t][:, side].astype(BF)
+            out[32:64, lanes] = part[2][:, side].astype(BF)
+        own[at] = part[0]
+        across[at, :, low] = part[3][:, low]
+        across[at, :, high] = part[1][:, high]
+    for out, t, core in ((to1, 1, 0), (to3, 3, 1)):
+        out[0:32, 7 * C : 8 * C] = rows[t][0]
+        out[32:64, 7 * C : 8 * C] = rows[t][1]
+        out[0:32, 8 * C : 8 * C + 128] = rows[2][core][:, 0:128]
+        out[32:64, 8 * C : 8 * C + 128] = rows[2][core][:, 128:256]
     mine[:, 0:C] = rows[0][0]
     mine[:, C : 2 * C] = rows[0][1]
 
 
-def half_two_kernel(place, own, across, a1, a3, to3, to1, total):
-    to3[...] = (across[:, 0:HALF] + a1[32:64, :].astype(F32)).astype(BF)
-    to1[...] = (across[:, HALF:] + a3[32:64, :].astype(F32)).astype(BF)
-    total[:, 0:HALF] = own[:, 0:HALF] + a1[0:32, :].astype(F32)
-    total[:, HALF:] = own[:, HALF:] + a3[0:32, :].astype(F32)
-
-
-def half_one_kernel(place, own, across, a1, a3, to3, to1, total):
-    for out, ref, lanes in ((to3, a1, slice(0, HALF)), (to1, a3, slice(HALF, 7 * C))):
-        out[:, 0:HALF] = (across[:, lanes] + ref[32:64, 0:HALF].astype(F32)).astype(BF)
-        out[:, HALF : HALF + 128] = ref[0:32, HALF + C : HALF + C + 128]
-        out[:, HALF + 128 : HALF + C] = ref[32:64, HALF + C : HALF + C + 128]
-        total[:, lanes] = own[:, lanes] + ref[0:32, 0:HALF].astype(F32)
-
-
-def line_two_kernel(place, total, b3, b1, out):
-    out[:, 0:HALF] = (total[:, 0:HALF] + b3[...].astype(F32)).astype(BF)
-    out[:, HALF:] = (total[:, HALF:] + b1[...].astype(F32)).astype(BF)
-
-
-def line_one_kernel(place, two, total, mine, a1, a3, b3, b1, out, one):
+def half_kernel(place, own, across, a1, a3, to3, to1, total):
+    for out, ref, side in ((to3, a1, slice(0, HALF)), (to1, a3, slice(HALF, 2 * HALF))):
+        for at in range(2):
+            lanes = slice(at * HALF, (at + 1) * HALF)
+            out[:, lanes] = (across[at, :, side] + ref[32:64, lanes].astype(F32)).astype(BF)
+            total[at, :, side] = own[at, :, side] + ref[0:32, lanes].astype(F32)
+        out[:, 7 * C : 7 * C + 128] = ref[0:32, 8 * C : 8 * C + 128]
+        out[:, 7 * C + 128 : 8 * C] = ref[32:64, 8 * C : 8 * C + 128]
+
+
+def line_kernel(place, total, mine, a1, a3, b3, b1, out, both):
     line = place[0] // 16
-    one[:, 0:HALF] = (total[:, 0:HALF] + b3[:, 0:HALF].astype(F32)).astype(BF)
-    one[:, HALF:] = (total[:, HALF:] + b1[:, 0:HALF].astype(F32)).astype(BF)
-    to, at = iota((64, 32), 0), iota((64, 32), 1)
-    spots = [onehot(((to % 8) // 4 == n) & (at == 4 * (to // 8) + to % 4)) for n in range(2)]
+    for ref, side in ((b3, slice(0, HALF)), (b1, slice(HALF, 2 * HALF))):
+        for at in range(2):
+            lanes = slice(at * HALF, (at + 1) * HALF)
+            value = total[at, :, side] + ref[:, lanes].astype(F32)
+            both[32 * (1 - at) : 32 * (2 - at), side] = value.astype(BF)
+    to, at = iota((64, 64), 0), iota((64, 64), 1)
+    order = onehot(at == 32 * ((to % 8) // 4) + 4 * (to // 8) + to % 4)
     for n in range(7):
         lanes = slice(n * C, (n + 1) * C)
-        block = mm(spots[0], one[:, lanes]) + mm(spots[1], two[:, lanes])
-        out[:, lanes] = block.astype(BF)
-    direct = slice(HALF, HALF + C)
+        out[:, lanes] = mm(order, both[:, lanes]).astype(BF)
+    direct = slice(7 * C, 8 * C)
     sources = (
         (0, (mine[:, 0:C], mine[:, C : 2 * C])),
         (1, (a1[0:32, direct], a1[32:64, direct])),
         (2, (b3[:, direct], b1[:, direct])),
         (3, (a3[0:32, direct], a3[32:64, direct])),
     )
+    to, at = iota((64, 32), 0), iota((64, 32), 1)
     for n in range(3):
         index = 8 * n + to % 8
         found = jnp.zeros((64, C), F32)
@@ -570,57 +556,36 @@
     rows_come = cross(rows_send, "gx", 1)
 
     both = lambda a, b: (cross(a, "gx", 16), cross(b, "gx", 48))
-    full = sds((32, wide), F32)
-    first = sds((64, HALF), BF)
-    *sent, own_two, across = call(
-        merge_two_kernel,
-        (first, first, full, full),
+    step = sds((64, 8 * C + 128), BF)
+    full = sds((2, 32, wide), F32)
+    to1, to3, own_sum, across, mine = call(
+        merge_kernel,
+        (step, step, full, full, sds((32, 2 * C), BF)),
         place,
         keep_two,
         come_two,
-        rows_keep,
-        late=1,
-    )
-    a1, a3 = both(*sent)
-    second = sds((32, HALF), BF)
-    to3, to1, sum_two = call(
-        half_two_kernel, (second, second, full), place, own_two, across, a1, a3, flops=4 * 10**9
-    )
-    b1, b3 = both(to1, to3)
-    sum_two = call(
-        line_two_kernel, sds((32, wide), BF), place, sum_two, b3, b1, flops=2 * 10**9
-    )
-    first = sds((64, HALF + C + 128), BF)
-    *sent, own_one, across, mine = call(
-        merge_one_kernel,
-        (first, first, full, full, sds((32, 2 * C), BF)),
-        place,
         keep_one,
         come_one,
         rows_keep,
         rows_come,
-        own_two,
-        late=1,
-        flops=2 * 10**10,
-    )
-    a1, a3 = both(*sent)
-    second = sds((32, HALF + C), BF)
-    to3, to1, sum_one = call(
-        half_one_kernel, (second, second, full), place, own_one, across, a1, a3
+    )
+    a1, a3 = both(to1, to3)
+    step = sds((32, 8 * C), BF)
+    to3, to1, total = call(
+        half_kernel, (step, step, full), place, own_sum, across, a1, a3
     )
     b1, b3 = both(to1, to3)
     summed = call(
-        line_one_kernel,
+        line_kernel,
         sds((64, 10 * C), BF),
         place,
-        sum_two,
-        sum_one,
+        total,
         mine,
         a1,
         a3,
         b3,
         b1,
-        scratch=[pltpu.VMEM((32, wide), BF)],
+        scratch=[pltpu.VMEM((64, wide), BF)],
     )
     groups = [[16 * y + 2 * z + e for z in range(8)] for y in range(4) for e in range(2)]
     collected = lax.all_to_all(

time: 83.3 us -> 85.1 us (1.022)
  waiting for transfers between devices: 13.3 us -> 19.9 us
  starting transfers between devices: 28.2 us -> 24.8 us
  Pallas kernels: 25.1 us -> 23.5 us
    ppermute x17 -> x13, waiting for transfers between devices: 7.34 us -> 13.8 us  [cross(): lax.ppermute(value, axis, [(n, n ^ mask) for n in range(lax.axis_size(axi...]
    ppermute x17 -> x13, starting transfers between devices: 19.6 us -> 16.2 us  [cross(): lax.ppermute(value, axis, [(n, n ^ mask) for n in range(lax.axis_size(axi...]
    pallas_call x18 -> x15, Pallas kernels: 25.1 us -> 23.5 us  [call(): pl.pallas_call(kernel, out_shape=outs, in_specs=specs, out_specs=jax.tree...]
  transfers between devices with their start and end apart: 27 -> 23, of which waited for: 8 -> 10; matrix products, arithmetic and copies ran while one was open for 0% -> 0% of each run, Pallas kernels for 25% -> 21%
where the time goes in v12:
time: 85.1 us; the launch traced here: 84.7 us
  starting transfers between devices  24.8 us (29%)
  Pallas kernels  23.5 us (28%)
  waiting for transfers between devices  19.9 us (23%)
  blocking collectives  15.7 us (18%)
    pallas_call x15, Pallas kernels, call(): pl.pallas_call(kernel, out_shape=outs, in_specs=specs, out_specs=jax.tree...  23.5 us
    ppermute x13, starting transfers between devices, cross(): lax.ppermute(value, axis, [(n, n ^ mask) for n in range(lax.axis_size(axi...  16.2 us
    all_to_all x1, blocking collectives, body(): lax.all_to_all(summed.reshape(8, 8, 10 * C), 'gx', split_axis=0, concat_a...  15.7 us
    ppermute x13, waiting for transfers between devices, cross(): lax.ppermute(value, axis, [(n, n ^ mask) for n in range(lax.axis_size(axi...  13.8 us
    ppermute x10, starting transfers between devices, swap(): return lax.ppermute(value, ('gx', 'gy'), pairs)  8.57 us
    ppermute x10, waiting for transfers between devices, swap(): return lax.ppermute(value, ('gx', 'gy'), pairs)  6.07 us
  transfers between devices with their start and end apart: 23, of which 10 were waited for; matrix products, arithmetic and copies ran while one was open for 0% of the time, Pallas kernels for 21%

profile of v12, /device:TPU:2, one launch (start us, length us, event | category | flops | bytes accessed | tf_op | source)
XLA Modules:
  0.0 84.7 jit_solution(8307502883961842080)
XLA Ops:
  0.6 0.1 pad_add_fusion.place
  0.7 2.3 %shard_map.103 = (bf16[224,512]{1,0:T(8,128)(2,1)S(1)}, bf16[224,512]{1,0:T(8,128)(2,1)S(1)}, bf16[224,512]{1,0:T(8,128)(2,1)S(1)}, bf16[224,512]{1,0:T(8,128)(2...) custom-call(s32[2]{0:T(128)S(1)} %pad_add_fusion.place, ...), custom_call_target="tpu_custom_call" | custom-call | flops 4000000000 | bytes 10000 | tf_op jit(solution)/shard_map/pallas_call | solution.py:368
  3.0 0.0 copy-start.1
  3.0 2.2 %collective-permute-start.4 = (bf16[224,512]{1,0:T(8,128)(2,1)S(1)}, bf16[224,512]{1,0:T(8,128)(2,1)S(1)}, u32[]{:S(2)}, u32[]{:S(2)}) collective-permute-start(bf16[224,512]{1,0:T(8,128)(2,1)S(1)} %get-tuple-element.56), channel_id=1, source_target_pairs={{0,2},{1,3},{2,0},{3,1},{4,6},{5,7},{6,4},{7,5},{8,10},{9,11},{10,... | collective-permute-start | bytes 688136 | tf_op jit(solution)/shard_map/ppermute | solution.py:409
  5.3 1.4 %collective-permute-start.5 = (bf16[224,512]{1,0:T(8,128)(2,1)S(1)}, bf16[224,512]{1,0:T(8,128)(2,1)S(1)}, u32[]{:S(2)}, u32[]{:S(2)}) collective-permute-start(bf16[224,512]{1,0:T(8,128)(2,1)S(1)} %get-tuple-element.57), channel_id=1, source_target_pairs={{0,1},{1,0},{2,3},{3,2},{4,5},{5,4},{6,7},{7,6},{8,9},{9,8},{10,11... | collective-permute-start | bytes 688136 | tf_op jit(solution)/shard_map/ppermute | solution.py:409
  6.7 0.5 collective-permute-start.6
  7.2 3.0 %shard_map.104 = (f32[192,256]{1,0:T(8,128)S(1)}, bf16[96,256]{1,0:T(8,128)(2,1)S(1)}, bf16[96,256]{1,0:T(8,128)(2,1)S(1)}, bf16[64,256]{1,0:T(8,128)(2,1)S(1)}) custom-call(s32[2]{0:T(128)S(1)} %pad_add_fusion.place, f32[32,256]{1,0:T(8,128)S(1)} %get-tuple-element.45.nbt, bf16[192,256]{1,0:T(8,128)(2,1)S(1)} %get-tuple-element.46.grad, ...), custom_call_target="tpu_custom_call" | custom-call | flops 100000 | bytes 10000 | tf_op jit(solution)/shard_map/pallas_call | solution.py:368
  10.3 2.4 %collective-permute-start = (bf16[96,256]{1,0:T(8,128)(2,1)S(1)}, bf16[96,256]{1,0:T(8,128)(2,1)S(1)}, u32[]{:S(2)}, u32[]{:S(2)}) collective-permute-start(bf16[96,256]{1,0:T(8,128)(2,1)S(1)} %get-tuple-element.48), channel_id=1, source_target_pairs={{0,1},{1,0},{2,3},{3,2},{4,8},{5,9},{6,10},{7,11},{8,4},{9,5},{10,... | collective-permute-start | bytes 147464 | tf_op jit(solution)/shard_map/ppermute | solution.py:405
  12.6 0.0 collective-permute-start.1
  12.6 4.9 %collective-permute-done.m2 = bf16[96,256]{1,0:T(8,128)(2,1)S(1)} collective-permute-done((bf16[96,256]{1,0:T(8,128)(2,1)S(1)}, bf16[96,256]{1,0:T(8,128)(2,1)S(1)}, u32[]{:S(2)}, u32[]{:S(2)}) %collective-permute-start) | collective-permute-done | bytes 49184 | tf_op jit(solution)/shard_map/ppermute | solution.py:405
  17.5 0.0 collective-permute-done.1.m1
  17.5 0.6 shard_map.105
  18.1 0.6 collective-permute-start.2
  18.7 0.2 collective-permute-start.3
  18.8 0.0 collective-permute-done.4.p2
  18.8 0.0 collective-permute-done.5.p1
  18.8 0.0 collective-permute-done.6.p3
  18.9 1.1 %shard_map.106 = (bf16[768,256]{1,0:T(8,128)(2,1)S(1)}, bf16[768,256]{1,0:T(8,128)(2,1)S(1)}, bf16[4,64,512]{2,1,0:T(8,128)(2,1)S(1)}) custom-call(s32[2]{0:T(128)S(1)} %pad_add_fusion.place, bf16[224,512]{1,0:T(8,128)(2,1)S(1)} %get-tuple-element.55.p0, bf16[224,512]{1,0:T(8,128)(2,1)S(1)} %collective-permute-done.4.p2, ...), custom_call_target="tpu_custom_call" | custom-call | flops 100000 | bytes 10000 | tf_op jit(solution)/shard_map/pallas_call | solution.py:368
  19.9 2.0 %collective-permute-start.10 = (bf16[768,256]{1,0:T(8,128)(2,1)S(1)}, bf16[768,256]{1,0:T(8,128)(2,1)S(1)}, u32[]{:S(2)}, u32[]{:S(2)}) collective-permute-start(bf16[768,256]{1,0:T(8,128)(2,1)S(1)} %get-tuple-element.61), channel_id=1, source_target_pairs={{0,1},{1,0},{2,3},{3,2},{4,8},{5,9},{6,10},{7,11},{8,4},{9,5},{10,... | collective-permute-start | bytes 1179656 | tf_op jit(solution)/shard_map/ppermute | solution.py:405
  21.9 0.0 collective-permute-start.11
  21.9 0.3 collective-permute-done.2.n2
  22.2 0.5 collective-permute-done.3.n1
  22.8 0.9 %shard_map.107 = (bf16[192,256]{1,0:T(8,128)(2,1)S(1)}, bf16[192,512]{1,0:T(8,128)(2,1)S(1)}) custom-call(s32[2]{0:T(128)S(1)} %pad_add_fusion.place, f32[192,256]{1,0:T(8,128)S(1)} %get-tuple-element.47.late.own, bf16[96,256]{1,0:T(8,128)(2,1)S(1)} %collective-permute-done.m2, bf16[96,256]{1,0:T(8,128)(2,1)S(1)} %collective-permute-done.1.m1, ...), custom_call_target="tpu_custom_call" | custom-call | flops 100000 | bytes 10000 | tf_op jit(solution)/shard_map/pallas_call | solution.py:368
  23.7 1.0 %collective-permute-start.7 = (bf16[192,512]{1,0:T(8,128)(2,1)S(1)}, bf16[192,512]{1,0:T(8,128)(2,1)S(1)}, u32[]{:S(2)}, u32[]{:S(2)}) collective-permute-start(bf16[192,512]{1,0:T(8,128)(2,1)S(1)} %get-tuple-element.60.g0), channel_id=1, source_target_pairs={{0,2},{1,3},{2,0},{3,1},{4,6},{5,7},{6,4},{7,5},{8,10},{9,11},{10,... | collective-permute-start | bytes 589832 | tf_op jit(solution)/shard_map/ppermute | solution.py:409
  24.7 2.6 %collective-permute-start.8 = (bf16[192,512]{1,0:T(8,128)(2,1)S(1)}, bf16[192,512]{1,0:T(8,128)(2,1)S(1)}, u32[]{:S(2)}, u32[]{:S(2)}) collective-permute-start(bf16[192,512]{1,0:T(8,128)(2,1)S(1)} %get-tuple-element.60.g0), channel_id=1, source_target_pairs={{0,1},{1,0},{2,3},{3,2},{4,5},{5,4},{6,7},{7,6},{8,9},{9,8},{10,11... | collective-permute-start | bytes 589832 | tf_op jit(solution)/shard_map/ppermute | solution.py:409
  27.3 0.5 collective-permute-start.9
  27.9 3.0 %shard_map.108 = (f32[192,256]{1,0:T(8,128)S(1)}, bf16[96,256]{1,0:T(8,128)(2,1)S(1)}, bf16[96,256]{1,0:T(8,128)(2,1)S(1)}, bf16[64,256]{1,0:T(8,128)(2,1)S(1)}) custom-call(s32[2]{0:T(128)S(1)} %pad_add_fusion.place, f32[32,256]{1,0:T(8,128)S(1)} %get-tuple-element.45.nbt, bf16[192,256]{1,0:T(8,128)(2,1)S(1)} %get-tuple-element.63.grad, ...), custom_call_target="tpu_custom_call" | custom-call | flops 4000000000 | bytes 10000 | tf_op jit(solution)/shard_map/pallas_call | solution.py:368
  30.9 0.0 collective-permute-done.10.r2
  30.9 1.3 %collective-permute-start.12 = (bf16[96,256]{1,0:T(8,128)(2,1)S(1)}, bf16[96,256]{1,0:T(8,128)(2,1)S(1)}, u32[]{:S(2)}, u32[]{:S(2)}) collective-permute-start(bf16[96,256]{1,0:T(8,128)(2,1)S(1)} %get-tuple-element.67), channel_id=1, source_target_pairs={{0,1},{1,0},{2,3},{3,2},{4,8},{5,9},{6,10},{7,11},{8,4},{9,5},{10,... | collective-permute-start | bytes 147464 | tf_op jit(solution)/shard_map/ppermute | solution.py:405
  32.2 0.0 collective-permute-done.11.r1
  32.2 0.0 collective-permute-start.13
  32.2 4.3 %shard_map.109 = (bf16[768,1792]{1,0:T(8,128)(2,1)S(1)}, bf16[768,1792]{1,0:T(8,128)(2,1)S(1)}) custom-call(s32[2]{0:T(128)S(1)} %pad_add_fusion.place, bf16[224,512]{1,0:T(8,128)(2,1)S(1)} %get-tuple-element.55.p0, bf16[224,512]{1,0:T(8,128)(2,1)S(1)} %collective-permute-done.4.p2, bf16[224,512]{1,0:T(8,128)(2,1)S(1)} %collective-permute-done.5.p1, ...), custom_call_target="tpu_custom_call" | custom-call | flops 4000000000 | bytes 10000 | tf_op jit(solution)/shard_map/pallas_call | solution.py:368
  36.5 0.3 collective-permute-done.12.m2
  36.8 0.0 collective-permute-done.13.m1
  36.8 0.6 shard_map.110
  37.4 2.2 %collective-permute-start.16 = (bf16[96,256]{1,0:T(8,128)(2,1)S(1)}, bf16[96,256]{1,0:T(8,128)(2,1)S(1)}, u32[]{:S(2)}, u32[]{:S(2)}) collective-permute-start(bf16[96,256]{1,0:T(8,128)(2,1)S(1)} %get-tuple-element.75), channel_id=1, source_target_pairs={{0,4},{1,2},{2,1},{3,7},{4,0},{5,6},{6,5},{7,3},{8,12},{9,10},{10,... | collective-permute-start | bytes 147464 | tf_op jit(solution)/shard_map/ppermute | solution.py:405
  39.5 0.0 collective-permute-start.17
  39.5 0.0 collective-permute-done.7.g2
  39.6 0.0 collective-permute-done.8.g1
  39.6 0.0 collective-permute-done.9.g3
  39.6 1.7 %shard_map.111 = (f32[128,1792]{1,0:T(8,128)S(1)}, f32[128,1792]{1,0:T(8,128)S(1)}) custom-call(s32[2]{0:T(128)S(1)} %pad_add_fusion.place, bf16[192,512]{1,0:T(8,128)(2,1)S(1)} %get-tuple-element.60.g0, bf16[192,512]{1,0:T(8,128)(2,1)S(1)} %collective-permute-done.7.g2, bf16[192,512]{1,0:T(8,128)(2,1)S(1)} %collective-permute-done.8.g1, ...), custom_call_target="tpu_custom_call" | custom-call | flops 4000000000 | bytes 10000 | tf_op jit(solution)/shard_map/pallas_call | solution.py:368
  41.3 1.7 %shard_map.112 = (bf16[128,1792]{1,0:T(8,128)(2,1)S(1)}, bf16[128,1792]{1,0:T(8,128)(2,1)S(1)}) custom-call(s32[2]{0:T(128)S(1)} %pad_add_fusion.place, bf16[192,512]{1,0:T(8,128)(2,1)S(1)} %get-tuple-element.60.g0, bf16[192,512]{1,0:T(8,128)(2,1)S(1)} %collective-permute-done.7.g2, bf16[192,512]{1,0:T(8,128)(2,1)S(1)} %collective-permute-done.8.g1, ...), custom_call_target="tpu_custom_call" | custom-call | flops 100000 | bytes 10000 | tf_op jit(solution)/shard_map/pallas_call | solution.py:368
  43.0 0.3 collective-permute-start.15
  43.3 0.3 collective-permute-start.14
  43.6 0.0 collective-permute-done.16.n2
  43.6 0.1 collective-permute-done.17.n1
  43.6 1.0 %shard_map.113 = (bf16[128,256]{1,0:T(8,128)(2,1)S(1)}, bf16[128,256]{1,0:T(8,128)(2,1)S(1)}) custom-call(s32[2]{0:T(128)S(1)} %pad_add_fusion.place, f32[192,256]{1,0:T(8,128)S(1)} %get-tuple-element.64.late.own, bf16[96,256]{1,0:T(8,128)(2,1)S(1)} %collective-permute-done.12.m2, bf16[96,256]{1,0:T(8,128)(2,1)S(1)} %collective-permute-done.13.m1, ...), custom_call_target="tpu_custom_call" | custom-call | flops 20000000000 | bytes 10000 | tf_op jit(solution)/shard_map/pallas_call | solution.py:368
  44.6 0.3 collective-permute-start.18
  44.9 1.4 %collective-permute-done.18.rs = bf16[128,256]{1,0:T(8,128)(2,1)S(1)} collective-permute-done((bf16[128,256]{1,0:T(8,128)(2,1)S(1)}, bf16[128,256]{1,0:T(8,128)(2,1)S(1)}, u32[]{:S(2)}, u32[]{:S(2)}) %collective-permute-start.18) | collective-permute-done | bytes 65568 | tf_op jit(solution)/shard_map/ppermute | solution.py:409
  46.3 0.0 collective-permute-done.15.s1
  46.3 0.0 collective-permute-done.14.s2
  46.3 0.8 shard_map.114
  47.0 2.6 %collective-permute-start.19 = (bf16[64,2176]{1,0:T(8,128)(2,1)S(1)}, bf16[64,2176]{1,0:T(8,128)(2,1)S(1)}, u32[]{:S(2)}, u32[]{:S(2)}) collective-permute-start(bf16[64,2176]{1,0:T(8,128)(2,1)S(1)} %get-tuple-element.81), channel_id=1, source_target_pairs={{0,64},{4,68},{8,72},{12,76},{16,80},{20,84},{24,88},{28,92},{32,9... | collective-permute-start | bytes 835592 | tf_op jit(solution)/shard_map/ppermute | solution.py:409
  49.6 2.2 %collective-permute-start.20 = (bf16[64,2176]{1,0:T(8,128)(2,1)S(1)}, bf16[64,2176]{1,0:T(8,128)(2,1)S(1)}, u32[]{:S(2)}, u32[]{:S(2)}) collective-permute-start(bf16[64,2176]{1,0:T(8,128)(2,1)S(1)} %get-tuple-element.82), channel_id=1, source_target_pairs={{0,192},{4,196},{8,200},{12,204},{16,208},{20,212},{24,216},{28,22... | collective-permute-start | bytes 835592 | tf_op jit(solution)/shard_map/ppermute | solution.py:409
  51.8 4.8 %collective-permute-done.19.a1 = bf16[64,2176]{1,0:T(8,128)(2,1)S(1)} collective-permute-done((bf16[64,2176]{1,0:T(8,128)(2,1)S(1)}, bf16[64,2176]{1,0:T(8,128)(2,1)S(1)}, u32[]{:S(2)}, u32[]{:S(2)}) %collective-permute-start.19) | collective-permute-done | bytes 278560 | tf_op jit(solution)/shard_map/ppermute | solution.py:409
  56.6 2.7 %collective-permute-done.20.a3 = bf16[64,2176]{1,0:T(8,128)(2,1)S(1)} collective-permute-done((bf16[64,2176]{1,0:T(8,128)(2,1)S(1)}, bf16[64,2176]{1,0:T(8,128)(2,1)S(1)}, u32[]{:S(2)}, u32[]{:S(2)}) %collective-permute-start.20) | collective-permute-done | bytes 278560 | tf_op jit(solution)/shard_map/ppermute | solution.py:409
  59.2 0.6 shard_map.115
  59.9 2.3 %collective-permute-start.21 = (bf16[32,2048]{1,0:T(8,128)(2,1)S(1)}, bf16[32,2048]{1,0:T(8,128)(2,1)S(1)}, u32[]{:S(2)}, u32[]{:S(2)}) collective-permute-start(bf16[32,2048]{1,0:T(8,128)(2,1)S(1)} %get-tuple-element.85), channel_id=1, source_target_pairs={{0,192},{4,196},{8,200},{12,204},{16,208},{20,212},{24,216},{28,22... | collective-permute-start | bytes 393224 | tf_op jit(solution)/shard_map/ppermute | solution.py:409
  62.1 0.0 collective-permute-start.22
  62.1 4.0 %collective-permute-done.21.b3 = bf16[32,2048]{1,0:T(8,128)(2,1)S(1)} collective-permute-done((bf16[32,2048]{1,0:T(8,128)(2,1)S(1)}, bf16[32,2048]{1,0:T(8,128)(2,1)S(1)}, u32[]{:S(2)}, u32[]{:S(2)}) %collective-permute-start.21) | collective-permute-done | bytes 131104 | tf_op jit(solution)/shard_map/ppermute | solution.py:409
  66.1 1.0 %collective-permute-done.22.b1 = bf16[32,2048]{1,0:T(8,128)(2,1)S(1)} collective-permute-done((bf16[32,2048]{1,0:T(8,128)(2,1)S(1)}, bf16[32,2048]{1,0:T(8,128)(2,1)S(1)}, u32[]{:S(2)}, u32[]{:S(2)}) %collective-permute-start.22) | collective-permute-done | bytes 131104 | tf_op jit(solution)/shard_map/ppermute | solution.py:409
  67.1 1.1 %shard_map.116 = bf16[64,2560]{1,0:T(8,128)(2,1)S(1)} custom-call(s32[2]{0:T(128)S(1)} %pad_add_fusion.place, f32[2,32,1792]{2,1,0:T(8,128)S(1)} %get-tuple-element.83.total, bf16[32,512]{1,0:T(8,128)(2,1)S(1)} %get-tuple-element.84.mine, bf16[64,2176]{1,0:T(8,128)(2,1)S(1)} %collective-permute-done.19.a1, bf16[64,2176]{1,0:T(8,128)(2,1)S(1)} %collective-permute-done.20.a3, ...), custom_call_target="tpu_custom_call" | custom-call | flops 100000 | bytes 10000 | tf_op jit(solution)/shard_map/pallas_call | solution.py:368
  68.2 15.7 %all_to_all.5.refs_0_ = bf16[8,8,2560]{2,1,0:T(8,128)(2,1)S(1)} all-to-all(bf16[8,8,2560]{2,1,0:T(8,128)(2,1)S(1)} %bitcast.5), channel_id=1, replica_groups={{0,8,16,24,32,40,48,56},{4,12,20,28,36,44,52,60},{64,72,80,88,96,104,11..., dimensions={0} | all-to-all | bytes 655360 | tf_op jit(solution)/shard_map/all_to_all | solution.py:591
  83.8 0.9 %shard_map.117 = (bf16[192,256]{1,0:T(8,128)(2,1)}, f32[4,1728]{1,0:T(4,128)}, f32[4,1728]{1,0:T(4,128)}) custom-call(bf16[8,8,2560]{2,1,0:T(8,128)(2,1)S(1)} %all_to_all.5.refs_0_), custom_call_target="tpu_custom_call" | custom-call | flops 100000 | bytes 10000 | tf_op jit(solution)/shard_map/pallas_call | solution.py:368
  (3 shorter events, 0.0 us)
Async XLA Ops:
  0.7 6.5 %copy-start = (bf16[256,6912]{1,0:T(8,128)(2,1)S(1)}, bf16[256,6912]{1,0:T(8,128)(2,1)}, u32[]{:S(2)}) copy-start(bf16[256,6912]{1,0:T(8,128)(2,1)} %weight.2) | copy-start | bytes 10616836
  3.0 24.8 %copy-start.1 = (bf16[256,6912]{1,0:T(8,128)(2,1)S(1)}, bf16[256,6912]{1,0:T(8,128)(2,1)}, u32[]{:S(2)}) copy-start(bf16[256,6912]{1,0:T(8,128)(2,1)} %weight.3) | copy-start | bytes 10616836
  3.0 15.8 %collective-permute-start.4 = (bf16[224,512]{1,0:T(8,128)(2,1)S(1)}, bf16[224,512]{1,0:T(8,128)(2,1)S(1)}, u32[]{:S(2)}, u32[]{:S(2)}) collective-permute-start(bf16[224,512]{1,0:T(8,128)(2,1)S(1)} %get-tuple-element.56), channel_id=1, source_target_pairs={{0,2},{1,3},{2,0},{3,1},{4,6},{5,7},{6,4},{7,5},{8,10},{9,11},{10,... | collective-permute-start | bytes 688136 | tf_op jit(solution)/shard_map/ppermute | solution.py:409
  5.3 13.6 %collective-permute-start.5 = (bf16[224,512]{1,0:T(8,128)(2,1)S(1)}, bf16[224,512]{1,0:T(8,128)(2,1)S(1)}, u32[]{:S(2)}, u32[]{:S(2)}) collective-permute-start(bf16[224,512]{1,0:T(8,128)(2,1)S(1)} %get-tuple-element.57), channel_id=1, source_target_pairs={{0,1},{1,0},{2,3},{3,2},{4,5},{5,4},{6,7},{7,6},{8,9},{9,8},{10,11... | collective-permute-start | bytes 688136 | tf_op jit(solution)/shard_map/ppermute | solution.py:409
  6.7 12.2 %collective-permute-start.6 = (bf16[224,512]{1,0:T(8,128)(2,1)S(1)}, bf16[224,512]{1,0:T(8,128)(2,1)S(1)}, u32[]{:S(2)}, u32[]{:S(2)}) collective-permute-start(bf16[224,512]{1,0:T(8,128)(2,1)S(1)} %get-tuple-element.58), channel_id=1, source_target_pairs={{0,3},{1,2},{2,1},{3,0},{4,7},{5,6},{6,5},{7,4},{8,11},{9,10},{10,... | collective-permute-start | bytes 688136 | tf_op jit(solution)/shard_map/ppermute | solution.py:409
  10.3 7.2 %collective-permute-start = (bf16[96,256]{1,0:T(8,128)(2,1)S(1)}, bf16[96,256]{1,0:T(8,128)(2,1)S(1)}, u32[]{:S(2)}, u32[]{:S(2)}) collective-permute-start(bf16[96,256]{1,0:T(8,128)(2,1)S(1)} %get-tuple-element.48), channel_id=1, source_target_pairs={{0,1},{1,0},{2,3},{3,2},{4,8},{5,9},{6,10},{7,11},{8,4},{9,5},{10,... | collective-permute-start | bytes 147464 | tf_op jit(solution)/shard_map/ppermute | solution.py:405
  12.6 4.9 %collective-permute-start.1 = (bf16[96,256]{1,0:T(8,128)(2,1)S(1)}, bf16[96,256]{1,0:T(8,128)(2,1)S(1)}, u32[]{:S(2)}, u32[]{:S(2)}) collective-permute-start(bf16[96,256]{1,0:T(8,128)(2,1)S(1)} %get-tuple-element.49), channel_id=1, source_target_pairs={{0,4},{1,5},{2,6},{3,7},{4,0},{5,1},{6,2},{7,3},{8,12},{9,13},{10,... | collective-permute-start | bytes 147464 | tf_op jit(solution)/shard_map/ppermute | solution.py:405
  18.1 4.2 %collective-permute-start.2 = (bf16[96,256]{1,0:T(8,128)(2,1)S(1)}, bf16[96,256]{1,0:T(8,128)(2,1)S(1)}, u32[]{:S(2)}, u32[]{:S(2)}) collective-permute-start(bf16[96,256]{1,0:T(8,128)(2,1)S(1)} %get-tuple-element.51), channel_id=1, source_target_pairs={{0,4},{1,2},{2,1},{3,7},{4,0},{5,6},{6,5},{7,3},{8,12},{9,10},{10,... | collective-permute-start | bytes 147464 | tf_op jit(solution)/shard_map/ppermute | solution.py:405
  18.7 4.1 %collective-permute-start.3 = (bf16[96,256]{1,0:T(8,128)(2,1)S(1)}, bf16[96,256]{1,0:T(8,128)(2,1)S(1)}, u32[]{:S(2)}, u32[]{:S(2)}) collective-permute-start(bf16[96,256]{1,0:T(8,128)(2,1)S(1)} %get-tuple-element.52.late), channel_id=1, source_target_pairs={{0,1},{1,0},{2,3},{3,2},{4,5},{5,4},{6,7},{7,6},{8,9},{9,8},{10,11... | collective-permute-start | bytes 147464 | tf_op jit(solution)/shard_map/ppermute | solution.py:405
  19.9 11.0 %collective-permute-start.10 = (bf16[768,256]{1,0:T(8,128)(2,1)S(1)}, bf16[768,256]{1,0:T(8,128)(2,1)S(1)}, u32[]{:S(2)}, u32[]{:S(2)}) collective-permute-start(bf16[768,256]{1,0:T(8,128)(2,1)S(1)} %get-tuple-element.61), channel_id=1, source_target_pairs={{0,1},{1,0},{2,3},{3,2},{4,8},{5,9},{6,10},{7,11},{8,4},{9,5},{10,... | collective-permute-start | bytes 1179656 | tf_op jit(solution)/shard_map/ppermute | solution.py:405
  21.9 10.3 %collective-permute-start.11 = (bf16[768,256]{1,0:T(8,128)(2,1)S(1)}, bf16[768,256]{1,0:T(8,128)(2,1)S(1)}, u32[]{:S(2)}, u32[]{:S(2)}) collective-permute-start(bf16[768,256]{1,0:T(8,128)(2,1)S(1)} %get-tuple-element.62), channel_id=1, source_target_pairs={{0,4},{1,5},{2,6},{3,7},{4,0},{5,1},{6,2},{7,3},{8,12},{9,13},{10,... | collective-permute-start | bytes 1179656 | tf_op jit(solution)/shard_map/ppermute | solution.py:405
  23.7 15.9 %collective-permute-start.7 = (bf16[192,512]{1,0:T(8,128)(2,1)S(1)}, bf16[192,512]{1,0:T(8,128)(2,1)S(1)}, u32[]{:S(2)}, u32[]{:S(2)}) collective-permute-start(bf16[192,512]{1,0:T(8,128)(2,1)S(1)} %get-tuple-element.60.g0), channel_id=1, source_target_pairs={{0,2},{1,3},{2,0},{3,1},{4,6},{5,7},{6,4},{7,5},{8,10},{9,11},{10,... | collective-permute-start | bytes 589832 | tf_op jit(solution)/shard_map/ppermute | solution.py:409
  24.7 14.8 %collective-permute-start.8 = (bf16[192,512]{1,0:T(8,128)(2,1)S(1)}, bf16[192,512]{1,0:T(8,128)(2,1)S(1)}, u32[]{:S(2)}, u32[]{:S(2)}) collective-permute-start(bf16[192,512]{1,0:T(8,128)(2,1)S(1)} %get-tuple-element.60.g0), channel_id=1, source_target_pairs={{0,1},{1,0},{2,3},{3,2},{4,5},{5,4},{6,7},{7,6},{8,9},{9,8},{10,11... | collective-permute-start | bytes 589832 | tf_op jit(solution)/shard_map/ppermute | solution.py:409
  27.3 12.2 %collective-permute-start.9 = (bf16[192,512]{1,0:T(8,128)(2,1)S(1)}, bf16[192,512]{1,0:T(8,128)(2,1)S(1)}, u32[]{:S(2)}, u32[]{:S(2)}) collective-permute-start(bf16[192,512]{1,0:T(8,128)(2,1)S(1)} %get-tuple-element.60.g0), channel_id=1, source_target_pairs={{0,3},{1,2},{2,1},{3,0},{4,7},{5,6},{6,5},{7,4},{8,11},{9,10},{10,... | collective-permute-start | bytes 589832 | tf_op jit(solution)/shard_map/ppermute | solution.py:409
  30.9 5.9 %collective-permute-start.12 = (bf16[96,256]{1,0:T(8,128)(2,1)S(1)}, bf16[96,256]{1,0:T(8,128)(2,1)S(1)}, u32[]{:S(2)}, u32[]{:S(2)}) collective-permute-start(bf16[96,256]{1,0:T(8,128)(2,1)S(1)} %get-tuple-element.67), channel_id=1, source_target_pairs={{0,1},{1,0},{2,3},{3,2},{4,8},{5,9},{6,10},{7,11},{8,4},{9,5},{10,... | collective-permute-start | bytes 147464 | tf_op jit(solution)/shard_map/ppermute | solution.py:405
  32.2 4.6 %collective-permute-start.13 = (bf16[96,256]{1,0:T(8,128)(2,1)S(1)}, bf16[96,256]{1,0:T(8,128)(2,1)S(1)}, u32[]{:S(2)}, u32[]{:S(2)}) collective-permute-start(bf16[96,256]{1,0:T(8,128)(2,1)S(1)} %get-tuple-element.68), channel_id=1, source_target_pairs={{0,4},{1,5},{2,6},{3,7},{4,0},{5,1},{6,2},{7,3},{8,12},{9,13},{10,... | collective-permute-start | bytes 147464 | tf_op jit(solution)/shard_map/ppermute | solution.py:405
  37.4 6.2 %collective-permute-start.16 = (bf16[96,256]{1,0:T(8,128)(2,1)S(1)}, bf16[96,256]{1,0:T(8,128)(2,1)S(1)}, u32[]{:S(2)}, u32[]{:S(2)}) collective-permute-start(bf16[96,256]{1,0:T(8,128)(2,1)S(1)} %get-tuple-element.75), channel_id=1, source_target_pairs={{0,4},{1,2},{2,1},{3,7},{4,0},{5,6},{6,5},{7,3},{8,12},{9,10},{10,... | collective-permute-start | bytes 147464 | tf_op jit(solution)/shard_map/ppermute | solution.py:405
  39.5 4.1 %collective-permute-start.17 = (bf16[96,256]{1,0:T(8,128)(2,1)S(1)}, bf16[96,256]{1,0:T(8,128)(2,1)S(1)}, u32[]{:S(2)}, u32[]{:S(2)}) collective-permute-start(bf16[96,256]{1,0:T(8,128)(2,1)S(1)} %get-tuple-element.69.late), channel_id=1, source_target_pairs={{0,1},{1,0},{2,3},{3,2},{4,5},{5,4},{6,7},{7,6},{8,9},{9,8},{10,11... | collective-permute-start | bytes 147464 | tf_op jit(solution)/shard_map/ppermute | solution.py:405
  43.0 3.3 %collective-permute-start.15 = (bf16[128,1792]{1,0:T(8,128)(2,1)S(1)}, bf16[128,1792]{1,0:T(8,128)(2,1)S(1)}, u32[]{:S(2)}, u32[]{:S(2)}) collective-permute-start(bf16[128,1792]{1,0:T(8,128)(2,1)S(1)} %get-tuple-element.74), channel_id=1, source_target_pairs={{0,4},{4,0},{8,12},{12,8},{16,20},{20,16},{24,28},{28,24},{32,36},... | collective-permute-start | bytes 1376264 | tf_op jit(solution)/shard_map/ppermute | solution.py:409
  43.3 3.0 %collective-permute-start.14 = (f32[128,1792]{1,0:T(8,128)S(1)}, f32[128,1792]{1,0:T(8,128)S(1)}, u32[]{:S(2)}, u32[]{:S(2)}) collective-permute-start(f32[128,1792]{1,0:T(8,128)S(1)} %get-tuple-element.71), channel_id=1, source_target_pairs={{0,4},{4,0},{8,12},{12,8},{16,20},{20,16},{24,28},{28,24},{32,36},... | collective-permute-start | bytes 2752520 | tf_op jit(solution)/shard_map/ppermute | solution.py:409
  44.6 1.7 %collective-permute-start.18 = (bf16[128,256]{1,0:T(8,128)(2,1)S(1)}, bf16[128,256]{1,0:T(8,128)(2,1)S(1)}, u32[]{:S(2)}, u32[]{:S(2)}) collective-permute-start(bf16[128,256]{1,0:T(8,128)(2,1)S(1)} %get-tuple-element.78), channel_id=1, source_target_pairs={{0,4},{4,0},{8,12},{12,8},{16,20},{20,16},{24,28},{28,24},{32,36},... | collective-permute-start | bytes 196616 | tf_op jit(solution)/shard_map/ppermute | solution.py:409
  47.0 9.5 %collective-permute-start.19 = (bf16[64,2176]{1,0:T(8,128)(2,1)S(1)}, bf16[64,2176]{1,0:T(8,128)(2,1)S(1)}, u32[]{:S(2)}, u32[]{:S(2)}) collective-permute-start(bf16[64,2176]{1,0:T(8,128)(2,1)S(1)} %get-tuple-element.81), channel_id=1, source_target_pairs={{0,64},{4,68},{8,72},{12,76},{16,80},{20,84},{24,88},{28,92},{32,9... | collective-permute-start | bytes 835592 | tf_op jit(solution)/shard_map/ppermute | solution.py:409
  49.6 9.6 %collective-permute-start.20 = (bf16[64,2176]{1,0:T(8,128)(2,1)S(1)}, bf16[64,2176]{1,0:T(8,128)(2,1)S(1)}, u32[]{:S(2)}, u32[]{:S(2)}) collective-permute-start(bf16[64,2176]{1,0:T(8,128)(2,1)S(1)} %get-tuple-element.82), channel_id=1, source_target_pairs={{0,192},{4,196},{8,200},{12,204},{16,208},{20,212},{24,216},{28,22... | collective-permute-start | bytes 835592 | tf_op jit(solution)/shard_map/ppermute | solution.py:409
  59.9 6.3 %collective-permute-start.21 = (bf16[32,2048]{1,0:T(8,128)(2,1)S(1)}, bf16[32,2048]{1,0:T(8,128)(2,1)S(1)}, u32[]{:S(2)}, u32[]{:S(2)}) collective-permute-start(bf16[32,2048]{1,0:T(8,128)(2,1)S(1)} %get-tuple-element.85), channel_id=1, source_target_pairs={{0,192},{4,196},{8,200},{12,204},{16,208},{20,212},{24,216},{28,22... | collective-permute-start | bytes 393224 | tf_op jit(solution)/shard_map/ppermute | solution.py:409
  62.1 5.0 %collective-permute-start.22 = (bf16[32,2048]{1,0:T(8,128)(2,1)S(1)}, bf16[32,2048]{1,0:T(8,128)(2,1)S(1)}, u32[]{:S(2)}, u32[]{:S(2)}) collective-permute-start(bf16[32,2048]{1,0:T(8,128)(2,1)S(1)} %get-tuple-element.86), channel_id=1, source_target_pairs={{0,64},{4,68},{8,72},{12,76},{16,80},{20,84},{24,88},{28,92},{32,9... | collective-permute-start | bytes 393224 | tf_op jit(solution)/shard_map/ppermute | solution.py:409

commit v13 on v11

--- a/solution.py
+++ b/solution.py
@@ -312,23 +312,24 @@
     total[:, HALF:] = own[:, HALF:] + a3[0:32, :].astype(F32)
 
 
-def half_one_kernel(place, own, across, a1, a3, to3, to1, total):
-    for out, ref, lanes in ((to3, a1, slice(0, HALF)), (to1, a3, slice(HALF, 7 * C))):
-        out[:, 0:HALF] = (across[:, lanes] + ref[32:64, 0:HALF].astype(F32)).astype(BF)
-        out[:, HALF : HALF + 128] = ref[0:32, HALF + C : HALF + C + 128]
-        out[:, HALF + 128 : HALF + C] = ref[32:64, HALF + C : HALF + C + 128]
+def half_one_kernel(place, own, across, a1, a3, two3, two1, to3, to1, total):
+    for out, ref, two, lanes in (
+        (to3, a1, two3, slice(0, HALF)),
+        (to1, a3, two1, slice(HALF, 7 * C)),
+    ):
+        out[:, 0:HALF] = two[...]
+        out[:, HALF : 7 * C] = (across[:, lanes] + ref[32:64, 0:HALF].astype(F32)).astype(BF)
+        out[:, 7 * C : 7 * C + 128] = ref[0:32, HALF + C : HALF + C + 128]
+        out[:, 7 * C + 128 : 8 * C] = ref[32:64, HALF + C : HALF + C + 128]
         total[:, lanes] = own[:, lanes] + ref[0:32, 0:HALF].astype(F32)
 
 
-def line_two_kernel(place, total, b3, b1, out):
-    out[:, 0:HALF] = (total[:, 0:HALF] + b3[...].astype(F32)).astype(BF)
-    out[:, HALF:] = (total[:, HALF:] + b1[...].astype(F32)).astype(BF)
-
-
-def line_one_kernel(place, two, total, mine, a1, a3, b3, b1, out, one):
+def line_kernel(place, sum_two, sum_one, mine, a1, a3, b3, b1, out, two, one):
     line = place[0] // 16
-    one[:, 0:HALF] = (total[:, 0:HALF] + b3[:, 0:HALF].astype(F32)).astype(BF)
-    one[:, HALF:] = (total[:, HALF:] + b1[:, 0:HALF].astype(F32)).astype(BF)
+    for at, (total, into) in enumerate(((sum_two, two), (sum_one, one))):
+        lanes = slice(at * HALF, (at + 1) * HALF)
+        into[:, 0:HALF] = (total[:, 0:HALF] + b3[:, lanes].astype(F32)).astype(BF)
+        into[:, HALF:] = (total[:, HALF:] + b1[:, lanes].astype(F32)).astype(BF)
     to, at = iota((64, 32), 0), iota((64, 32), 1)
     spots = [onehot(((to % 8) // 4 == n) & (at == 4 * (to // 8) + to % 4)) for n in range(2)]
     for n in range(7):
@@ -339,7 +340,7 @@
     sources = (
         (0, (mine[:, 0:C], mine[:, C : 2 * C])),
         (1, (a1[0:32, direct], a1[32:64, direct])),
-        (2, (b3[:, direct], b1[:, direct])),
+        (2, (b3[:, 7 * C : 8 * C], b1[:, 7 * C : 8 * C])),
         (3, (a3[0:32, direct], a3[32:64, direct])),
     )
     for n in range(3):
@@ -583,12 +584,8 @@
     )
     a1, a3 = both(*sent)
     second = sds((32, HALF), BF)
-    to3, to1, sum_two = call(
-        half_two_kernel, (second, second, full), place, own_two, across, a1, a3, flops=4 * 10**9
-    )
-    b1, b3 = both(to1, to3)
-    sum_two = call(
-        line_two_kernel, sds((32, wide), BF), place, sum_two, b3, b1, flops=2 * 10**9
+    two3, two1, sum_two = call(
+        half_two_kernel, (second, second, full), place, own_two, across, a1, a3, flops=2 * 10**9
     )
     first = sds((64, HALF + C + 128), BF)
     *sent, own_one, across, mine = call(
@@ -604,13 +601,13 @@
         flops=2 * 10**10,
     )
     a1, a3 = both(*sent)
-    second = sds((32, HALF + C), BF)
+    second = sds((32, 8 * C), BF)
     to3, to1, sum_one = call(
-        half_one_kernel, (second, second, full), place, own_one, across, a1, a3
+        half_one_kernel, (second, second, full), place, own_one, across, a1, a3, two3, two1
     )
     b1, b3 = both(to1, to3)
     summed = call(
-        line_one_kernel,
+        line_kernel,
         sds((64, 10 * C), BF),
         place,
         sum_two,
@@ -620,7 +617,7 @@
         a3,
         b3,
         b1,
-        scratch=[pltpu.VMEM((32, wide), BF)],
+        scratch=[pltpu.VMEM((32, wide), BF)] * 2,
     )
     groups = [[16 * y + 2 * z + e for z in range(8)] for y in range(4) for e in range(2)]
     collected = lax.all_to_all(

time: 83.3 us -> 84 us (level)
  waiting for transfers between devices: 13.3 us -> 16.8 us
  starting transfers between devices: 28.2 us -> 25.5 us
    ppermute x17 -> x15, waiting for transfers between devices: 7.34 us -> 10.7 us  [cross(): lax.ppermute(value, axis, [(n, n ^ mask) for n in range(lax.axis_size(axi...]
    ppermute x17 -> x15, starting transfers between devices: 19.6 us -> 16.9 us  [cross(): lax.ppermute(value, axis, [(n, n ^ mask) for n in range(lax.axis_size(axi...]
    pallas_call x18 -> x17, Pallas kernels: 25.1 us -> 24.6 us  [call(): pl.pallas_call(kernel, out_shape=outs, in_specs=specs, out_specs=jax.tree...]
  transfers between devices with their start and end apart: 27 -> 25, of which waited for: 8 -> 9; matrix products, arithmetic and copies ran while one was open for 0% -> 0% of each run, Pallas kernels for 25% -> 24%
where the time goes in v13:
time: 84 us; the launch traced here: 83.6 us
  starting transfers between devices  25.5 us (30%)
  Pallas kernels  24.6 us (29%)
  waiting for transfers between devices  16.8 us (20%)
  blocking collectives  15.8 us (19%)
    pallas_call x17, Pallas kernels, call(): pl.pallas_call(kernel, out_shape=outs, in_specs=specs, out_specs=jax.tree...  24.6 us
    ppermute x15, starting transfers between devices, cross(): lax.ppermute(value, axis, [(n, n ^ mask) for n in range(lax.axis_size(axi...  16.9 us
    all_to_all x1, blocking collectives, body(): lax.all_to_all(summed.reshape(8, 8, 10 * C), 'gx', split_axis=0, concat_a...  15.8 us
    ppermute x15, waiting for transfers between devices, cross(): lax.ppermute(value, axis, [(n, n ^ mask) for n in range(lax.axis_size(axi...  10.7 us
    ppermute x10, starting transfers between devices, swap(): return lax.ppermute(value, ('gx', 'gy'), pairs)  8.57 us
    ppermute x10, waiting for transfers between devices, swap(): return lax.ppermute(value, ('gx', 'gy'), pairs)  6.01 us
  transfers between devices with their start and end apart: 25, of which 9 were waited for; matrix products, arithmetic and copies ran while one was open for 0% of the time, Pallas kernels for 24%

profile of v13, /device:TPU:2, one launch (start us, length us, event | category | flops | bytes accessed | tf_op | source)
XLA Modules:
  0.0 83.6 jit_solution(18193454855213937452)
XLA Ops:
  0.6 0.1 pad_add_fusion.place
  0.7 2.3 %shard_map.103 = (bf16[224,512]{1,0:T(8,128)(2,1)S(1)}, bf16[224,512]{1,0:T(8,128)(2,1)S(1)}, bf16[224,512]{1,0:T(8,128)(2,1)S(1)}, bf16[224,512]{1,0:T(8,128)(2...) custom-call(s32[2]{0:T(128)S(1)} %pad_add_fusion.place, ...), custom_call_target="tpu_custom_call" | custom-call | flops 4000000000 | bytes 10000 | tf_op jit(solution)/shard_map/pallas_call | solution.py:383
  3.0 0.0 copy-start.1
  3.0 2.2 %collective-permute-start.4 = (bf16[224,512]{1,0:T(8,128)(2,1)S(1)}, bf16[224,512]{1,0:T(8,128)(2,1)S(1)}, u32[]{:S(2)}, u32[]{:S(2)}) collective-permute-start(bf16[224,512]{1,0:T(8,128)(2,1)S(1)} %get-tuple-element.63), channel_id=1, source_target_pairs={{0,2},{1,3},{2,0},{3,1},{4,6},{5,7},{6,4},{7,5},{8,10},{9,11},{10,... | collective-permute-start | bytes 688136 | tf_op jit(solution)/shard_map/ppermute | solution.py:424
  5.3 1.4 %collective-permute-start.5 = (bf16[224,512]{1,0:T(8,128)(2,1)S(1)}, bf16[224,512]{1,0:T(8,128)(2,1)S(1)}, u32[]{:S(2)}, u32[]{:S(2)}) collective-permute-start(bf16[224,512]{1,0:T(8,128)(2,1)S(1)} %get-tuple-element.64), channel_id=1, source_target_pairs={{0,1},{1,0},{2,3},{3,2},{4,5},{5,4},{6,7},{7,6},{8,9},{9,8},{10,11... | collective-permute-start | bytes 688136 | tf_op jit(solution)/shard_map/ppermute | solution.py:424
  6.7 0.5 collective-permute-start.6
  7.2 3.0 %shard_map.104 = (f32[192,256]{1,0:T(8,128)S(1)}, bf16[96,256]{1,0:T(8,128)(2,1)S(1)}, bf16[96,256]{1,0:T(8,128)(2,1)S(1)}, bf16[64,256]{1,0:T(8,128)(2,1)S(1)}) custom-call(s32[2]{0:T(128)S(1)} %pad_add_fusion.place, f32[32,256]{1,0:T(8,128)S(1)} %get-tuple-element.52.nbt, bf16[192,256]{1,0:T(8,128)(2,1)S(1)} %get-tuple-element.53.grad, ...), custom_call_target="tpu_custom_call" | custom-call | flops 100000 | bytes 10000 | tf_op jit(solution)/shard_map/pallas_call | solution.py:383
  10.3 2.4 %collective-permute-start = (bf16[96,256]{1,0:T(8,128)(2,1)S(1)}, bf16[96,256]{1,0:T(8,128)(2,1)S(1)}, u32[]{:S(2)}, u32[]{:S(2)}) collective-permute-start(bf16[96,256]{1,0:T(8,128)(2,1)S(1)} %get-tuple-element.55), channel_id=1, source_target_pairs={{0,1},{1,0},{2,3},{3,2},{4,8},{5,9},{6,10},{7,11},{8,4},{9,5},{10,... | collective-permute-start | bytes 147464 | tf_op jit(solution)/shard_map/ppermute | solution.py:420
  12.6 0.0 collective-permute-start.1
  12.6 4.9 %collective-permute-done.m2 = bf16[96,256]{1,0:T(8,128)(2,1)S(1)} collective-permute-done((bf16[96,256]{1,0:T(8,128)(2,1)S(1)}, bf16[96,256]{1,0:T(8,128)(2,1)S(1)}, u32[]{:S(2)}, u32[]{:S(2)}) %collective-permute-start) | collective-permute-done | bytes 49184 | tf_op jit(solution)/shard_map/ppermute | solution.py:420
  17.5 0.0 collective-permute-done.1.m1
  17.5 0.6 shard_map.105
  18.1 0.6 collective-permute-start.2
  18.7 0.2 collective-permute-start.3
  18.8 0.0 collective-permute-done.4.p2
  18.8 0.0 collective-permute-done.5.p1
  18.8 0.0 collective-permute-done.6.p3
  18.9 1.1 %shard_map.106 = (bf16[768,256]{1,0:T(8,128)(2,1)S(1)}, bf16[768,256]{1,0:T(8,128)(2,1)S(1)}, bf16[4,64,512]{2,1,0:T(8,128)(2,1)S(1)}) custom-call(s32[2]{0:T(128)S(1)} %pad_add_fusion.place, bf16[224,512]{1,0:T(8,128)(2,1)S(1)} %get-tuple-element.62.p0, bf16[224,512]{1,0:T(8,128)(2,1)S(1)} %collective-permute-done.4.p2, ...), custom_call_target="tpu_custom_call" | custom-call | flops 100000 | bytes 10000 | tf_op jit(solution)/shard_map/pallas_call | solution.py:383
  19.9 2.0 %collective-permute-start.10 = (bf16[768,256]{1,0:T(8,128)(2,1)S(1)}, bf16[768,256]{1,0:T(8,128)(2,1)S(1)}, u32[]{:S(2)}, u32[]{:S(2)}) collective-permute-start(bf16[768,256]{1,0:T(8,128)(2,1)S(1)} %get-tuple-element.68), channel_id=1, source_target_pairs={{0,1},{1,0},{2,3},{3,2},{4,8},{5,9},{6,10},{7,11},{8,4},{9,5},{10,... | collective-permute-start | bytes 1179656 | tf_op jit(solution)/shard_map/ppermute | solution.py:420
  21.9 0.0 collective-permute-start.11
  21.9 0.3 collective-permute-done.2.n2
  22.2 0.5 collective-permute-done.3.n1
  22.8 0.9 %shard_map.107 = (bf16[192,256]{1,0:T(8,128)(2,1)S(1)}, bf16[192,512]{1,0:T(8,128)(2,1)S(1)}) custom-call(s32[2]{0:T(128)S(1)} %pad_add_fusion.place, f32[192,256]{1,0:T(8,128)S(1)} %get-tuple-element.54.late.own, bf16[96,256]{1,0:T(8,128)(2,1)S(1)} %collective-permute-done.m2, bf16[96,256]{1,0:T(8,128)(2,1)S(1)} %collective-permute-done.1.m1, ...), custom_call_target="tpu_custom_call" | custom-call | flops 100000 | bytes 10000 | tf_op jit(solution)/shard_map/pallas_call | solution.py:383
  23.7 1.0 %collective-permute-start.7 = (bf16[192,512]{1,0:T(8,128)(2,1)S(1)}, bf16[192,512]{1,0:T(8,128)(2,1)S(1)}, u32[]{:S(2)}, u32[]{:S(2)}) collective-permute-start(bf16[192,512]{1,0:T(8,128)(2,1)S(1)} %get-tuple-element.67.g0), channel_id=1, source_target_pairs={{0,2},{1,3},{2,0},{3,1},{4,6},{5,7},{6,4},{7,5},{8,10},{9,11},{10,... | collective-permute-start | bytes 589832 | tf_op jit(solution)/shard_map/ppermute | solution.py:424
  24.7 2.6 %collective-permute-start.8 = (bf16[192,512]{1,0:T(8,128)(2,1)S(1)}, bf16[192,512]{1,0:T(8,128)(2,1)S(1)}, u32[]{:S(2)}, u32[]{:S(2)}) collective-permute-start(bf16[192,512]{1,0:T(8,128)(2,1)S(1)} %get-tuple-element.67.g0), channel_id=1, source_target_pairs={{0,1},{1,0},{2,3},{3,2},{4,5},{5,4},{6,7},{7,6},{8,9},{9,8},{10,11... | collective-permute-start | bytes 589832 | tf_op jit(solution)/shard_map/ppermute | solution.py:424
  27.3 0.5 collective-permute-start.9
  27.9 3.0 %shard_map.108 = (f32[192,256]{1,0:T(8,128)S(1)}, bf16[96,256]{1,0:T(8,128)(2,1)S(1)}, bf16[96,256]{1,0:T(8,128)(2,1)S(1)}, bf16[64,256]{1,0:T(8,128)(2,1)S(1)}) custom-call(s32[2]{0:T(128)S(1)} %pad_add_fusion.place, f32[32,256]{1,0:T(8,128)S(1)} %get-tuple-element.52.nbt, bf16[192,256]{1,0:T(8,128)(2,1)S(1)} %get-tuple-element.70.grad, ...), custom_call_target="tpu_custom_call" | custom-call | flops 4000000000 | bytes 10000 | tf_op jit(solution)/shard_map/pallas_call | solution.py:383
  30.9 0.0 collective-permute-done.10.r2
  30.9 1.3 %collective-permute-start.12 = (bf16[96,256]{1,0:T(8,128)(2,1)S(1)}, bf16[96,256]{1,0:T(8,128)(2,1)S(1)}, u32[]{:S(2)}, u32[]{:S(2)}) collective-permute-start(bf16[96,256]{1,0:T(8,128)(2,1)S(1)} %get-tuple-element.74), channel_id=1, source_target_pairs={{0,1},{1,0},{2,3},{3,2},{4,8},{5,9},{6,10},{7,11},{8,4},{9,5},{10,... | collective-permute-start | bytes 147464 | tf_op jit(solution)/shard_map/ppermute | solution.py:420
  32.2 0.0 collective-permute-done.11.r1
  32.2 0.0 collective-permute-start.13
  32.2 4.3 %shard_map.109 = (bf16[768,1792]{1,0:T(8,128)(2,1)S(1)}, bf16[768,1792]{1,0:T(8,128)(2,1)S(1)}) custom-call(s32[2]{0:T(128)S(1)} %pad_add_fusion.place, bf16[224,512]{1,0:T(8,128)(2,1)S(1)} %get-tuple-element.62.p0, bf16[224,512]{1,0:T(8,128)(2,1)S(1)} %collective-permute-done.4.p2, bf16[224,512]{1,0:T(8,128)(2,1)S(1)} %collective-permute-done.5.p1, ...), custom_call_target="tpu_custom_call" | custom-call | flops 4000000000 | bytes 10000 | tf_op jit(solution)/shard_map/pallas_call | solution.py:383
  36.5 0.3 collective-permute-done.12.m2
  36.8 0.0 collective-permute-done.13.m1
  36.8 0.6 shard_map.110
  37.4 2.2 %collective-permute-start.15 = (bf16[96,256]{1,0:T(8,128)(2,1)S(1)}, bf16[96,256]{1,0:T(8,128)(2,1)S(1)}, u32[]{:S(2)}, u32[]{:S(2)}) collective-permute-start(bf16[96,256]{1,0:T(8,128)(2,1)S(1)} %get-tuple-element.79), channel_id=1, source_target_pairs={{0,4},{1,2},{2,1},{3,7},{4,0},{5,6},{6,5},{7,3},{8,12},{9,10},{10,... | collective-permute-start | bytes 147464 | tf_op jit(solution)/shard_map/ppermute | solution.py:420
  39.5 0.0 collective-permute-start.16
  39.5 0.0 collective-permute-done.7.g2
  39.6 0.0 collective-permute-done.9.g3
  39.6 1.7 %shard_map.111 = (f32[128,1792]{1,0:T(8,128)S(1)}, f32[128,1792]{1,0:T(8,128)S(1)}) custom-call(s32[2]{0:T(128)S(1)} %pad_add_fusion.place, bf16[192,512]{1,0:T(8,128)(2,1)S(1)} %get-tuple-element.67.g0, bf16[192,512]{1,0:T(8,128)(2,1)S(1)} %collective-permute-done.7.g2, bf16[192,512]{1,0:T(8,128)(2,1)S(1)} %collective-permute-done.8.g1, ...), custom_call_target="tpu_custom_call" | custom-call | flops 4000000000 | bytes 10000 | tf_op jit(solution)/shard_map/pallas_call | solution.py:383
  41.3 0.3 collective-permute-start.14
  41.6 1.7 %shard_map.112 = (bf16[128,1792]{1,0:T(8,128)(2,1)S(1)}, bf16[128,1792]{1,0:T(8,128)(2,1)S(1)}) custom-call(s32[2]{0:T(128)S(1)} %pad_add_fusion.place, bf16[192,512]{1,0:T(8,128)(2,1)S(1)} %get-tuple-element.67.g0, bf16[192,512]{1,0:T(8,128)(2,1)S(1)} %collective-permute-done.7.g2, bf16[192,512]{1,0:T(8,128)(2,1)S(1)} %collective-permute-done.8.g1, ...), custom_call_target="tpu_custom_call" | custom-call | flops 100000 | bytes 10000 | tf_op jit(solution)/shard_map/pallas_call | solution.py:383
  43.3 0.4 collective-permute-start.19
  43.7 1.0 %shard_map.113 = (bf16[128,256]{1,0:T(8,128)(2,1)S(1)}, bf16[128,256]{1,0:T(8,128)(2,1)S(1)}) custom-call(s32[2]{0:T(128)S(1)} %pad_add_fusion.place, f32[192,256]{1,0:T(8,128)S(1)} %get-tuple-element.71.late.own, bf16[96,256]{1,0:T(8,128)(2,1)S(1)} %collective-permute-done.12.m2, bf16[96,256]{1,0:T(8,128)(2,1)S(1)} %collective-permute-done.13.m1, ...), custom_call_target="tpu_custom_call" | custom-call | flops 20000000000 | bytes 10000 | tf_op jit(solution)/shard_map/pallas_call | solution.py:383
  44.6 0.3 collective-permute-start.20
  45.0 0.0 collective-permute-done.14.come
  45.0 0.6 shard_map.114
  45.6 2.3 %collective-permute-start.17 = (bf16[64,896]{1,0:T(8,128)(2,1)S(1)}, bf16[64,896]{1,0:T(8,128)(2,1)S(1)}, u32[]{:S(2)}, u32[]{:S(2)}) collective-permute-start(bf16[64,896]{1,0:T(8,128)(2,1)S(1)} %get-tuple-element.86), channel_id=1, source_target_pairs={{0,64},{4,68},{8,72},{12,76},{16,80},{20,84},{24,88},{28,92},{32,9... | collective-permute-start | bytes 344072 | tf_op jit(solution)/shard_map/ppermute | solution.py:424
  48.0 2.2 %collective-permute-start.18 = (bf16[64,896]{1,0:T(8,128)(2,1)S(1)}, bf16[64,896]{1,0:T(8,128)(2,1)S(1)}, u32[]{:S(2)}, u32[]{:S(2)}) collective-permute-start(bf16[64,896]{1,0:T(8,128)(2,1)S(1)} %get-tuple-element.87), channel_id=1, source_target_pairs={{0,192},{4,196},{8,200},{12,204},{16,208},{20,212},{24,216},{28,22... | collective-permute-start | bytes 344072 | tf_op jit(solution)/shard_map/ppermute | solution.py:424
  50.1 0.7 shard_map.116
  50.8 1.1 %collective-permute-start.21 = (bf16[64,1280]{1,0:T(8,128)(2,1)S(1)}, bf16[64,1280]{1,0:T(8,128)(2,1)S(1)}, u32[]{:S(2)}, u32[]{:S(2)}) collective-permute-start(bf16[64,1280]{1,0:T(8,128)(2,1)S(1)} %get-tuple-element.93), channel_id=1, source_target_pairs={{0,64},{4,68},{8,72},{12,76},{16,80},{20,84},{24,88},{28,92},{32,9... | collective-permute-start | bytes 491528 | tf_op jit(solution)/shard_map/ppermute | solution.py:424
  51.9 0.6 collective-permute-start.22
  52.5 0.0 collective-permute-done.17.a1
  52.5 1.9 %collective-permute-done.18.a3 = bf16[64,896]{1,0:T(8,128)(2,1)S(1)} collective-permute-done((bf16[64,896]{1,0:T(8,128)(2,1)S(1)}, bf16[64,896]{1,0:T(8,128)(2,1)S(1)}, u32[]{:S(2)}, u32[]{:S(2)}) %collective-permute-start.18) | collective-permute-done | bytes 114720 | tf_op jit(solution)/shard_map/ppermute | solution.py:424
  54.4 0.6 shard_map.115
  55.0 1.9 %collective-permute-done.21.a1 = bf16[64,1280]{1,0:T(8,128)(2,1)S(1)} collective-permute-done((bf16[64,1280]{1,0:T(8,128)(2,1)S(1)}, bf16[64,1280]{1,0:T(8,128)(2,1)S(1)}, u32[]{:S(2)}, u32[]{:S(2)}) %collective-permute-start.21) | collective-permute-done | bytes 163872 | tf_op jit(solution)/shard_map/ppermute | solution.py:424
  56.9 1.9 %collective-permute-done.22.a3 = bf16[64,1280]{1,0:T(8,128)(2,1)S(1)} collective-permute-done((bf16[64,1280]{1,0:T(8,128)(2,1)S(1)}, bf16[64,1280]{1,0:T(8,128)(2,1)S(1)}, u32[]{:S(2)}, u32[]{:S(2)}) %collective-permute-start.22) | collective-permute-done | bytes 163872 | tf_op jit(solution)/shard_map/ppermute | solution.py:424
  58.8 0.6 shard_map.117
  59.4 1.4 %collective-permute-start.23 = (bf16[32,2048]{1,0:T(8,128)(2,1)S(1)}, bf16[32,2048]{1,0:T(8,128)(2,1)S(1)}, u32[]{:S(2)}, u32[]{:S(2)}) collective-permute-start(bf16[32,2048]{1,0:T(8,128)(2,1)S(1)} %get-tuple-element.99), channel_id=1, source_target_pairs={{0,192},{4,196},{8,200},{12,204},{16,208},{20,212},{24,216},{28,22... | collective-permute-start | bytes 393224 | tf_op jit(solution)/shard_map/ppermute | solution.py:424
  60.8 4.9 %collective-permute-done.23.b3 = bf16[32,2048]{1,0:T(8,128)(2,1)S(1)} collective-permute-done((bf16[32,2048]{1,0:T(8,128)(2,1)S(1)}, bf16[32,2048]{1,0:T(8,128)(2,1)S(1)}, u32[]{:S(2)}, u32[]{:S(2)}) %collective-permute-start.23) | collective-permute-done | bytes 131104 | tf_op jit(solution)/shard_map/ppermute | solution.py:424
  65.7 0.1 collective-permute-done.24.b1
  65.8 1.1 %shard_map.118 = bf16[64,2560]{1,0:T(8,128)(2,1)S(1)} custom-call(s32[2]{0:T(128)S(1)} %pad_add_fusion.place, f32[32,1792]{1,0:T(8,128)S(1)} %get-tuple-element.88.sum_two, f32[32,1792]{1,0:T(8,128)S(1)} %get-tuple-element.97.sum_one, bf16[32,512]{1,0:T(8,128)(2,1)S(1)} %get-tuple-element.98.mine, bf16[64,1280]{1,0:T(8,128)(2,1)S(1)} %collective-permute-done.21.a1, ...), custom_call_target="tpu_custom_call" | custom-call | flops 100000 | bytes 10000 | tf_op jit(solution)/shard_map/pallas_call | solution.py:383
  66.9 15.8 %all_to_all.5.refs_0_ = bf16[8,8,2560]{2,1,0:T(8,128)(2,1)S(1)} all-to-all(bf16[8,8,2560]{2,1,0:T(8,128)(2,1)S(1)} %bitcast.5), channel_id=1, replica_groups={{0,8,16,24,32,40,48,56},{4,12,20,28,36,44,52,60},{64,72,80,88,96,104,11..., dimensions={0} | all-to-all | bytes 655360 | tf_op jit(solution)/shard_map/all_to_all | solution.py:623
  82.7 0.9 %shard_map.119 = (bf16[192,256]{1,0:T(8,128)(2,1)}, f32[4,1728]{1,0:T(4,128)}, f32[4,1728]{1,0:T(4,128)}) custom-call(bf16[8,8,2560]{2,1,0:T(8,128)(2,1)S(1)} %all_to_all.5.refs_0_), custom_call_target="tpu_custom_call" | custom-call | flops 100000 | bytes 10000 | tf_op jit(solution)/shard_map/pallas_call | solution.py:383
  (9 shorter events, 0.0 us)
Async XLA Ops:
  0.7 6.5 %copy-start = (bf16[256,6912]{1,0:T(8,128)(2,1)S(1)}, bf16[256,6912]{1,0:T(8,128)(2,1)}, u32[]{:S(2)}) copy-start(bf16[256,6912]{1,0:T(8,128)(2,1)} %weight.2) | copy-start | bytes 10616836
  3.0 24.8 %copy-start.1 = (bf16[256,6912]{1,0:T(8,128)(2,1)S(1)}, bf16[256,6912]{1,0:T(8,128)(2,1)}, u32[]{:S(2)}) copy-start(bf16[256,6912]{1,0:T(8,128)(2,1)} %weight.3) | copy-start | bytes 10616836
  3.0 15.8 %collective-permute-start.4 = (bf16[224,512]{1,0:T(8,128)(2,1)S(1)}, bf16[224,512]{1,0:T(8,128)(2,1)S(1)}, u32[]{:S(2)}, u32[]{:S(2)}) collective-permute-start(bf16[224,512]{1,0:T(8,128)(2,1)S(1)} %get-tuple-element.63), channel_id=1, source_target_pairs={{0,2},{1,3},{2,0},{3,1},{4,6},{5,7},{6,4},{7,5},{8,10},{9,11},{10,... | collective-permute-start | bytes 688136 | tf_op jit(solution)/shard_map/ppermute | solution.py:424
  5.3 13.6 %collective-permute-start.5 = (bf16[224,512]{1,0:T(8,128)(2,1)S(1)}, bf16[224,512]{1,0:T(8,128)(2,1)S(1)}, u32[]{:S(2)}, u32[]{:S(2)}) collective-permute-start(bf16[224,512]{1,0:T(8,128)(2,1)S(1)} %get-tuple-element.64), channel_id=1, source_target_pairs={{0,1},{1,0},{2,3},{3,2},{4,5},{5,4},{6,7},{7,6},{8,9},{9,8},{10,11... | collective-permute-start | bytes 688136 | tf_op jit(solution)/shard_map/ppermute | solution.py:424
  6.7 12.2 %collective-permute-start.6 = (bf16[224,512]{1,0:T(8,128)(2,1)S(1)}, bf16[224,512]{1,0:T(8,128)(2,1)S(1)}, u32[]{:S(2)}, u32[]{:S(2)}) collective-permute-start(bf16[224,512]{1,0:T(8,128)(2,1)S(1)} %get-tuple-element.65), channel_id=1, source_target_pairs={{0,3},{1,2},{2,1},{3,0},{4,7},{5,6},{6,5},{7,4},{8,11},{9,10},{10,... | collective-permute-start | bytes 688136 | tf_op jit(solution)/shard_map/ppermute | solution.py:424
  10.3 7.2 %collective-permute-start = (bf16[96,256]{1,0:T(8,128)(2,1)S(1)}, bf16[96,256]{1,0:T(8,128)(2,1)S(1)}, u32[]{:S(2)}, u32[]{:S(2)}) collective-permute-start(bf16[96,256]{1,0:T(8,128)(2,1)S(1)} %get-tuple-element.55), channel_id=1, source_target_pairs={{0,1},{1,0},{2,3},{3,2},{4,8},{5,9},{6,10},{7,11},{8,4},{9,5},{10,... | collective-permute-start | bytes 147464 | tf_op jit(solution)/shard_map/ppermute | solution.py:420
  12.6 4.9 %collective-permute-start.1 = (bf16[96,256]{1,0:T(8,128)(2,1)S(1)}, bf16[96,256]{1,0:T(8,128)(2,1)S(1)}, u32[]{:S(2)}, u32[]{:S(2)}) collective-permute-start(bf16[96,256]{1,0:T(8,128)(2,1)S(1)} %get-tuple-element.56), channel_id=1, source_target_pairs={{0,4},{1,5},{2,6},{3,7},{4,0},{5,1},{6,2},{7,3},{8,12},{9,13},{10,... | collective-permute-start | bytes 147464 | tf_op jit(solution)/shard_map/ppermute | solution.py:420
  18.1 4.2 %collective-permute-start.2 = (bf16[96,256]{1,0:T(8,128)(2,1)S(1)}, bf16[96,256]{1,0:T(8,128)(2,1)S(1)}, u32[]{:S(2)}, u32[]{:S(2)}) collective-permute-start(bf16[96,256]{1,0:T(8,128)(2,1)S(1)} %get-tuple-element.58), channel_id=1, source_target_pairs={{0,4},{1,2},{2,1},{3,7},{4,0},{5,6},{6,5},{7,3},{8,12},{9,10},{10,... | collective-permute-start | bytes 147464 | tf_op jit(solution)/shard_map/ppermute | solution.py:420
  18.7 4.1 %collective-permute-start.3 = (bf16[96,256]{1,0:T(8,128)(2,1)S(1)}, bf16[96,256]{1,0:T(8,128)(2,1)S(1)}, u32[]{:S(2)}, u32[]{:S(2)}) collective-permute-start(bf16[96,256]{1,0:T(8,128)(2,1)S(1)} %get-tuple-element.59.late), channel_id=1, source_target_pairs={{0,1},{1,0},{2,3},{3,2},{4,5},{5,4},{6,7},{7,6},{8,9},{9,8},{10,11... | collective-permute-start | bytes 147464 | tf_op jit(solution)/shard_map/ppermute | solution.py:420
  19.9 11.0 %collective-permute-start.10 = (bf16[768,256]{1,0:T(8,128)(2,1)S(1)}, bf16[768,256]{1,0:T(8,128)(2,1)S(1)}, u32[]{:S(2)}, u32[]{:S(2)}) collective-permute-start(bf16[768,256]{1,0:T(8,128)(2,1)S(1)} %get-tuple-element.68), channel_id=1, source_target_pairs={{0,1},{1,0},{2,3},{3,2},{4,8},{5,9},{6,10},{7,11},{8,4},{9,5},{10,... | collective-permute-start | bytes 1179656 | tf_op jit(solution)/shard_map/ppermute | solution.py:420
  21.9 10.3 %collective-permute-start.11 = (bf16[768,256]{1,0:T(8,128)(2,1)S(1)}, bf16[768,256]{1,0:T(8,128)(2,1)S(1)}, u32[]{:S(2)}, u32[]{:S(2)}) collective-permute-start(bf16[768,256]{1,0:T(8,128)(2,1)S(1)} %get-tuple-element.69), channel_id=1, source_target_pairs={{0,4},{1,5},{2,6},{3,7},{4,0},{5,1},{6,2},{7,3},{8,12},{9,13},{10,... | collective-permute-start | bytes 1179656 | tf_op jit(solution)/shard_map/ppermute | solution.py:420
  23.7 15.9 %collective-permute-start.7 = (bf16[192,512]{1,0:T(8,128)(2,1)S(1)}, bf16[192,512]{1,0:T(8,128)(2,1)S(1)}, u32[]{:S(2)}, u32[]{:S(2)}) collective-permute-start(bf16[192,512]{1,0:T(8,128)(2,1)S(1)} %get-tuple-element.67.g0), channel_id=1, source_target_pairs={{0,2},{1,3},{2,0},{3,1},{4,6},{5,7},{6,4},{7,5},{8,10},{9,11},{10,... | collective-permute-start | bytes 589832 | tf_op jit(solution)/shard_map/ppermute | solution.py:424
  24.7 14.8 %collective-permute-start.8 = (bf16[192,512]{1,0:T(8,128)(2,1)S(1)}, bf16[192,512]{1,0:T(8,128)(2,1)S(1)}, u32[]{:S(2)}, u32[]{:S(2)}) collective-permute-start(bf16[192,512]{1,0:T(8,128)(2,1)S(1)} %get-tuple-element.67.g0), channel_id=1, source_target_pairs={{0,1},{1,0},{2,3},{3,2},{4,5},{5,4},{6,7},{7,6},{8,9},{9,8},{10,11... | collective-permute-start | bytes 589832 | tf_op jit(solution)/shard_map/ppermute | solution.py:424
  27.3 12.2 %collective-permute-start.9 = (bf16[192,512]{1,0:T(8,128)(2,1)S(1)}, bf16[192,512]{1,0:T(8,128)(2,1)S(1)}, u32[]{:S(2)}, u32[]{:S(2)}) collective-permute-start(bf16[192,512]{1,0:T(8,128)(2,1)S(1)} %get-tuple-element.67.g0), channel_id=1, source_target_pairs={{0,3},{1,2},{2,1},{3,0},{4,7},{5,6},{6,5},{7,4},{8,11},{9,10},{10,... | collective-permute-start | bytes 589832 | tf_op jit(solution)/shard_map/ppermute | solution.py:424
  30.9 5.9 %collective-permute-start.12 = (bf16[96,256]{1,0:T(8,128)(2,1)S(1)}, bf16[96,256]{1,0:T(8,128)(2,1)S(1)}, u32[]{:S(2)}, u32[]{:S(2)}) collective-permute-start(bf16[96,256]{1,0:T(8,128)(2,1)S(1)} %get-tuple-element.74), channel_id=1, source_target_pairs={{0,1},{1,0},{2,3},{3,2},{4,8},{5,9},{6,10},{7,11},{8,4},{9,5},{10,... | collective-permute-start | bytes 147464 | tf_op jit(solution)/shard_map/ppermute | solution.py:420
  32.2 4.6 %collective-permute-start.13 = (bf16[96,256]{1,0:T(8,128)(2,1)S(1)}, bf16[96,256]{1,0:T(8,128)(2,1)S(1)}, u32[]{:S(2)}, u32[]{:S(2)}) collective-permute-start(bf16[96,256]{1,0:T(8,128)(2,1)S(1)} %get-tuple-element.75), channel_id=1, source_target_pairs={{0,4},{1,5},{2,6},{3,7},{4,0},{5,1},{6,2},{7,3},{8,12},{9,13},{10,... | collective-permute-start | bytes 147464 | tf_op jit(solution)/shard_map/ppermute | solution.py:420
  37.4 6.3 %collective-permute-start.15 = (bf16[96,256]{1,0:T(8,128)(2,1)S(1)}, bf16[96,256]{1,0:T(8,128)(2,1)S(1)}, u32[]{:S(2)}, u32[]{:S(2)}) collective-permute-start(bf16[96,256]{1,0:T(8,128)(2,1)S(1)} %get-tuple-element.79), channel_id=1, source_target_pairs={{0,4},{1,2},{2,1},{3,7},{4,0},{5,6},{6,5},{7,3},{8,12},{9,10},{10,... | collective-permute-start | bytes 147464 | tf_op jit(solution)/shard_map/ppermute | solution.py:420
  39.5 4.1 %collective-permute-start.16 = (bf16[96,256]{1,0:T(8,128)(2,1)S(1)}, bf16[96,256]{1,0:T(8,128)(2,1)S(1)}, u32[]{:S(2)}, u32[]{:S(2)}) collective-permute-start(bf16[96,256]{1,0:T(8,128)(2,1)S(1)} %get-tuple-element.76.late), channel_id=1, source_target_pairs={{0,1},{1,0},{2,3},{3,2},{4,5},{5,4},{6,7},{7,6},{8,9},{9,8},{10,11... | collective-permute-start | bytes 147464 | tf_op jit(solution)/shard_map/ppermute | solution.py:420
  41.3 3.7 %collective-permute-start.14 = (f32[128,1792]{1,0:T(8,128)S(1)}, f32[128,1792]{1,0:T(8,128)S(1)}, u32[]{:S(2)}, u32[]{:S(2)}) collective-permute-start(f32[128,1792]{1,0:T(8,128)S(1)} %get-tuple-element.78), channel_id=1, source_target_pairs={{0,4},{4,0},{8,12},{12,8},{16,20},{20,16},{24,28},{28,24},{32,36},... | collective-permute-start | bytes 2752520 | tf_op jit(solution)/shard_map/ppermute | solution.py:424
  43.3 6.8 %collective-permute-start.19 = (bf16[128,1792]{1,0:T(8,128)(2,1)S(1)}, bf16[128,1792]{1,0:T(8,128)(2,1)S(1)}, u32[]{:S(2)}, u32[]{:S(2)}) collective-permute-start(bf16[128,1792]{1,0:T(8,128)(2,1)S(1)} %get-tuple-element.89), channel_id=1, source_target_pairs={{0,4},{4,0},{8,12},{12,8},{16,20},{20,16},{24,28},{28,24},{32,36},... | collective-permute-start | bytes 1376264 | tf_op jit(solution)/shard_map/ppermute | solution.py:424
  44.6 5.5 %collective-permute-start.20 = (bf16[128,256]{1,0:T(8,128)(2,1)S(1)}, bf16[128,256]{1,0:T(8,128)(2,1)S(1)}, u32[]{:S(2)}, u32[]{:S(2)}) collective-permute-start(bf16[128,256]{1,0:T(8,128)(2,1)S(1)} %get-tuple-element.90), channel_id=1, source_target_pairs={{0,4},{4,0},{8,12},{12,8},{16,20},{20,16},{24,28},{28,24},{32,36},... | collective-permute-start | bytes 196616 | tf_op jit(solution)/shard_map/ppermute | solution.py:424
  45.6 6.9 %collective-permute-start.17 = (bf16[64,896]{1,0:T(8,128)(2,1)S(1)}, bf16[64,896]{1,0:T(8,128)(2,1)S(1)}, u32[]{:S(2)}, u32[]{:S(2)}) collective-permute-start(bf16[64,896]{1,0:T(8,128)(2,1)S(1)} %get-tuple-element.86), channel_id=1, source_target_pairs={{0,64},{4,68},{8,72},{12,76},{16,80},{20,84},{24,88},{28,92},{32,9... | collective-permute-start | bytes 344072 | tf_op jit(solution)/shard_map/ppermute | solution.py:424
  48.0 6.5 %collective-permute-start.18 = (bf16[64,896]{1,0:T(8,128)(2,1)S(1)}, bf16[64,896]{1,0:T(8,128)(2,1)S(1)}, u32[]{:S(2)}, u32[]{:S(2)}) collective-permute-start(bf16[64,896]{1,0:T(8,128)(2,1)S(1)} %get-tuple-element.87), channel_id=1, source_target_pairs={{0,192},{4,196},{8,200},{12,204},{16,208},{20,212},{24,216},{28,22... | collective-permute-start | bytes 344072 | tf_op jit(solution)/shard_map/ppermute | solution.py:424
  50.8 6.1 %collective-permute-start.21 = (bf16[64,1280]{1,0:T(8,128)(2,1)S(1)}, bf16[64,1280]{1,0:T(8,128)(2,1)S(1)}, u32[]{:S(2)}, u32[]{:S(2)}) collective-permute-start(bf16[64,1280]{1,0:T(8,128)(2,1)S(1)} %get-tuple-element.93), channel_id=1, source_target_pairs={{0,64},{4,68},{8,72},{12,76},{16,80},{20,84},{24,88},{28,92},{32,9... | collective-permute-start | bytes 491528 | tf_op jit(solution)/shard_map/ppermute | solution.py:424
  51.9 7.0 %collective-permute-start.22 = (bf16[64,1280]{1,0:T(8,128)(2,1)S(1)}, bf16[64,1280]{1,0:T(8,128)(2,1)S(1)}, u32[]{:S(2)}, u32[]{:S(2)}) collective-permute-start(bf16[64,1280]{1,0:T(8,128)(2,1)S(1)} %get-tuple-element.94), channel_id=1, source_target_pairs={{0,192},{4,196},{8,200},{12,204},{16,208},{20,212},{24,216},{28,22... | collective-permute-start | bytes 491528 | tf_op jit(solution)/shard_map/ppermute | solution.py:424
  59.4 6.3 %collective-permute-start.23 = (bf16[32,2048]{1,0:T(8,128)(2,1)S(1)}, bf16[32,2048]{1,0:T(8,128)(2,1)S(1)}, u32[]{:S(2)}, u32[]{:S(2)}) collective-permute-start(bf16[32,2048]{1,0:T(8,128)(2,1)S(1)} %get-tuple-element.99), channel_id=1, source_target_pairs={{0,192},{4,196},{8,200},{12,204},{16,208},{20,212},{24,216},{28,22... | collective-permute-start | bytes 393224 | tf_op jit(solution)/shard_map/ppermute | solution.py:424
  60.8 5.0 %collective-permute-start.24 = (bf16[32,2048]{1,0:T(8,128)(2,1)S(1)}, bf16[32,2048]{1,0:T(8,128)(2,1)S(1)}, u32[]{:S(2)}, u32[]{:S(2)}) collective-permute-start(bf16[32,2048]{1,0:T(8,128)(2,1)S(1)} %get-tuple-element.100), channel_id=1, source_target_pairs={{0,64},{4,68},{8,72},{12,76},{16,80},{20,84},{24,88},{28,92},{32,9... | collective-permute-start | bytes 393224 | tf_op jit(solution)/shard_map/ppermute | solution.py:424

commit v14 on v10

--- a/solution.py
+++ b/solution.py
@@ -183,12 +183,15 @@
     send[...] = chosen[128:256, :]
 
 
-def pick_kernel(place, p0, p2, p1, p3, late, o2, o1, loc, picked):
+def pick_kernel(place, p0, p2, p1, p3, late, o2, o1, loc, picked, ids):
     column = place[1]
-    for turn, pay in enumerate((p0, p1, p2, p3)):
-        halo_row = pay[S + 16 : S + 32, 0:C].astype(F32)[15:16, :].astype(jnp.int32) - 1
-        rows = mm_t(halo_matrix(halo_row), pay[0:S, 0 : 2 * C])
-        picked[column ^ turn] = rows.astype(BF)
+    pays = (p0, p1, p2, p3)
+    for turn, pay in enumerate(pays):
+        ids[turn : turn + 1, :] = pay[S + 16 : S + 32, 0:C].astype(F32)[15:16, :] - 1.0
+    slots = jnp.transpose(ids[...])[:, 0:8].astype(jnp.int32)
+    for turn, pay in enumerate(pays):
+        chosen = onehot(iota((8 * HB, S), 1) == slots[:, turn : turn + 1])
+        picked[column ^ turn] = mm(chosen, pay[0:S, 0 : 2 * C]).astype(BF)
     even = place[0] % 2 == 0
     up = pl.multiple_of(jnp.where(even, 160, 0), 32)
     down = pl.multiple_of(jnp.where(even, 0, 160), 32)
@@ -293,39 +296,40 @@
 
 def line_one_kernel(place, two, b0, b2, b1, b3, out):
     line = place[0] // 16
-    to, at = iota((64, 32), 0), iota((64, 32), 1)
+    to, at = iota((64, 64), 0), iota((64, 64), 1)
+    order = onehot(at == 32 * ((to % 8) // 4) + 4 * (to // 8) + to % 4)
     for n in range(7):
         lanes = slice(n * C, (n + 1) * C)
         total = b0[:, lanes].astype(F32)
         for part in (b1, b2, b3):
             total = total + part[:, lanes].astype(F32)
-        block = jnp.zeros((64, C), F32)
-        for which, value in ((0, total.astype(BF)), (1, two[:, lanes])):
-            spot = ((to % 8) // 4 == which) & (at == 4 * (to // 8) + to % 4)
-            block = block + mm(onehot(spot), value)
-        out[:, lanes] = block.astype(BF)
+        value = jnp.concatenate([total.astype(BF), two[:, lanes]], axis=0)
+        out[:, lanes] = mm(order, value).astype(BF)
+    sources = [
+        part[:, (7 + core) * C : (8 + core) * C] for part in (b0, b1, b2, b3) for core in range(2)
+    ]
+    stacked = jnp.concatenate(sources, axis=0)
+    to, at = iota((64, C), 0), iota((64, C), 1)
     for n in range(3):
         index = 8 * n + to % 8
-        total = jnp.zeros((64, C), F32)
-        for turn, part in enumerate((b0, b1, b2, b3)):
-            from_line = (index // 6 == (line ^ turn)) & (at == 4 * (to // 8) + index % 3)
-            for core in range(2):
-                spot = onehot(from_line & ((index % 6) // 3 == core))
-                total = total + mm(spot, part[:, (7 + core) * C : (8 + core) * C])
-        out[:, (7 + n) * C : (8 + n) * C] = total.astype(BF)
+        spot = (
+            (index // 6 == (line ^ (at // 64)))
+            & ((index % 6) // 3 == (at // 32) % 2)
+            & (at % 32 == 4 * (to // 8) + index % 3)
+        )
+        out[:, (7 + n) * C : (8 + n) * C] = mm(onehot(spot), stacked).astype(BF)
 
 
 def final_kernel(scale, arrived, rows, one, two):
     total = jnp.sum(arrived[:, :, 0 : 7 * C].astype(F32), axis=0) * scale
     one[...] = total[0:4, 0:QW]
     two[...] = total[4:8, 0:QW]
-    to, at = iota((S, 64), 0), iota((S, 64), 1)
-    value = jnp.zeros((S, C), F32)
-    for n in range(3):
-        spot = (at // 8 == (to // 6) % 8) & (8 * n + at % 8 == 6 * (to // 48) + to % 6)
-        piece = arrived[:, :, (7 + n) * C : (8 + n) * C].reshape(64, C)
-        value = value + mm(onehot(spot), piece)
-    rows[...] = value.astype(BF)
+    to, at = iota((S, S), 0), iota((S, S), 1)
+    spot = ((at % 64) // 8 == (to // 6) % 8) & (
+        8 * (at // 64) + at % 8 == 6 * (to // 48) + to % 6
+    )
+    pieces = [arrived[:, :, (7 + n) * C : (8 + n) * C].reshape(64, C) for n in range(3)]
+    rows[...] = mm(onehot(spot), jnp.concatenate(pieces, axis=0)).astype(BF)
 
 
 def sds(shape, dtype):
@@ -448,7 +452,7 @@
         place,
         *pays,
         passed,
-        scratch=[pltpu.VMEM((4, 8 * HB, 2 * C), BF)],
+        scratch=[pltpu.VMEM((4, 8 * HB, 2 * C), BF), pltpu.VMEM((128, C), F32)],
         late=1,
     )
     r2, r1 = halo_lines(o2, o1)

time: 83.1 us -> 82.9 us (level)
  no operation moved by 1% of the time
where the time goes in v14:
time: 82.9 us; the launch traced here: 82.2 us
  starting transfers between devices  29 us (35%)
  Pallas kernels  24 us (29%)
  blocking collectives  17.2 us (21%)
  waiting for transfers between devices  11.1 us (13%)
    pallas_call x16, Pallas kernels, call(): pl.pallas_call(kernel, out_shape=outs, in_specs=specs, out_specs=jax.tree...  24 us
    ppermute x15, starting transfers between devices, cross(): lax.ppermute(value, axis, [(n, n ^ mask) for n in range(lax.axis_size(axi...  20.2 us
    all_to_all x1, blocking collectives, body(): lax.all_to_all(summed.reshape(8, 8, 10 * C), 'gx', split_axis=0, concat_a...  17.2 us
    ppermute x10, starting transfers between devices, swap(): return lax.ppermute(value, ('gx', 'gy'), pairs)  8.75 us
    ppermute x10, waiting for transfers between devices, swap(): return lax.ppermute(value, ('gx', 'gy'), pairs)  5.84 us
    ppermute x15, waiting for transfers between devices, cross(): lax.ppermute(value, axis, [(n, n ^ mask) for n in range(lax.axis_size(axi...  5.31 us
  transfers between devices with their start and end apart: 25, of which 7 were waited for; matrix products, arithmetic and copies ran while one was open for 0% of the time, Pallas kernels for 24%

profile of v14, /device:TPU:2, one launch (start us, length us, event | category | flops | bytes accessed | tf_op | source)
XLA Modules:
  0.0 82.2 jit_solution(13188496526118287320)
XLA Ops:
  0.6 0.1 pad_add_fusion.place
  0.7 2.3 %shard_map.103 = (bf16[224,512]{1,0:T(8,128)(2,1)S(1)}, bf16[224,512]{1,0:T(8,128)(2,1)S(1)}, bf16[224,512]{1,0:T(8,128)(2,1)S(1)}, bf16[224,512]{1,0:T(8,128)(2...) custom-call(s32[2]{0:T(128)S(1)} %pad_add_fusion.place, ...), custom_call_target="tpu_custom_call" | custom-call | flops 4000000000 | bytes 10000 | tf_op jit(solution)/shard_map/pallas_call | solution.py:348
  3.0 0.0 copy-start.1
  3.0 2.2 %collective-permute-start.4 = (bf16[224,512]{1,0:T(8,128)(2,1)S(1)}, bf16[224,512]{1,0:T(8,128)(2,1)S(1)}, u32[]{:S(2)}, u32[]{:S(2)}) collective-permute-start(bf16[224,512]{1,0:T(8,128)(2,1)S(1)} %get-tuple-element.56), channel_id=1, source_target_pairs={{0,2},{1,3},{2,0},{3,1},{4,6},{5,7},{6,4},{7,5},{8,10},{9,11},{10,... | collective-permute-start | bytes 688136 | tf_op jit(solution)/shard_map/ppermute | solution.py:389
  5.3 1.4 %collective-permute-start.5 = (bf16[224,512]{1,0:T(8,128)(2,1)S(1)}, bf16[224,512]{1,0:T(8,128)(2,1)S(1)}, u32[]{:S(2)}, u32[]{:S(2)}) collective-permute-start(bf16[224,512]{1,0:T(8,128)(2,1)S(1)} %get-tuple-element.57), channel_id=1, source_target_pairs={{0,1},{1,0},{2,3},{3,2},{4,5},{5,4},{6,7},{7,6},{8,9},{9,8},{10,11... | collective-permute-start | bytes 688136 | tf_op jit(solution)/shard_map/ppermute | solution.py:389
  6.7 0.5 collective-permute-start.6
  7.2 3.0 %shard_map.104 = (f32[192,256]{1,0:T(8,128)S(1)}, bf16[96,256]{1,0:T(8,128)(2,1)S(1)}, bf16[96,256]{1,0:T(8,128)(2,1)S(1)}, bf16[64,256]{1,0:T(8,128)(2,1)S(1)}) custom-call(s32[2]{0:T(128)S(1)} %pad_add_fusion.place, f32[32,256]{1,0:T(8,128)S(1)} %get-tuple-element.45.nbt, bf16[192,256]{1,0:T(8,128)(2,1)S(1)} %get-tuple-element.46.grad, ...), custom_call_target="tpu_custom_call" | custom-call | flops 100000 | bytes 10000 | tf_op jit(solution)/shard_map/pallas_call | solution.py:348
  10.3 2.4 %collective-permute-start = (bf16[96,256]{1,0:T(8,128)(2,1)S(1)}, bf16[96,256]{1,0:T(8,128)(2,1)S(1)}, u32[]{:S(2)}, u32[]{:S(2)}) collective-permute-start(bf16[96,256]{1,0:T(8,128)(2,1)S(1)} %get-tuple-element.48), channel_id=1, source_target_pairs={{0,1},{1,0},{2,3},{3,2},{4,8},{5,9},{6,10},{7,11},{8,4},{9,5},{10,... | collective-permute-start | bytes 147464 | tf_op jit(solution)/shard_map/ppermute | solution.py:385
  12.6 0.0 collective-permute-start.1
  12.6 4.9 %collective-permute-done.m2 = bf16[96,256]{1,0:T(8,128)(2,1)S(1)} collective-permute-done((bf16[96,256]{1,0:T(8,128)(2,1)S(1)}, bf16[96,256]{1,0:T(8,128)(2,1)S(1)}, u32[]{:S(2)}, u32[]{:S(2)}) %collective-permute-start) | collective-permute-done | bytes 49184 | tf_op jit(solution)/shard_map/ppermute | solution.py:385
  17.5 0.0 collective-permute-done.1.m1
  17.5 0.6 shard_map.105
  18.1 0.6 collective-permute-start.2
  18.7 0.2 collective-permute-start.3
  18.8 0.0 collective-permute-done.4.p2
  18.8 0.0 collective-permute-done.5.p1
  18.8 0.0 collective-permute-done.6.p3
  18.9 1.3 %shard_map.106 = (bf16[768,256]{1,0:T(8,128)(2,1)S(1)}, bf16[768,256]{1,0:T(8,128)(2,1)S(1)}, bf16[4,64,512]{2,1,0:T(8,128)(2,1)S(1)}) custom-call(s32[2]{0:T(128)S(1)} %pad_add_fusion.place, bf16[224,512]{1,0:T(8,128)(2,1)S(1)} %get-tuple-element.55.p0, bf16[224,512]{1,0:T(8,128)(2,1)S(1)} %collective-permute-done.4.p2, ...), custom_call_target="tpu_custom_call" | custom-call | flops 100000 | bytes 10000 | tf_op jit(solution)/shard_map/pallas_call | solution.py:348
  20.1 2.0 %collective-permute-start.10 = (bf16[768,256]{1,0:T(8,128)(2,1)S(1)}, bf16[768,256]{1,0:T(8,128)(2,1)S(1)}, u32[]{:S(2)}, u32[]{:S(2)}) collective-permute-start(bf16[768,256]{1,0:T(8,128)(2,1)S(1)} %get-tuple-element.61), channel_id=1, source_target_pairs={{0,1},{1,0},{2,3},{3,2},{4,8},{5,9},{6,10},{7,11},{8,4},{9,5},{10,... | collective-permute-start | bytes 1179656 | tf_op jit(solution)/shard_map/ppermute | solution.py:385
  22.1 0.2 collective-permute-done.2.n2
  22.2 0.5 collective-permute-done.3.n1
  22.8 0.9 %shard_map.107 = (bf16[192,256]{1,0:T(8,128)(2,1)S(1)}, bf16[192,512]{1,0:T(8,128)(2,1)S(1)}) custom-call(s32[2]{0:T(128)S(1)} %pad_add_fusion.place, f32[192,256]{1,0:T(8,128)S(1)} %get-tuple-element.47.late.own, bf16[96,256]{1,0:T(8,128)(2,1)S(1)} %collective-permute-done.m2, bf16[96,256]{1,0:T(8,128)(2,1)S(1)} %collective-permute-done.1.m1, ...), custom_call_target="tpu_custom_call" | custom-call | flops 100000 | bytes 10000 | tf_op jit(solution)/shard_map/pallas_call | solution.py:348
  23.7 1.0 %collective-permute-start.7 = (bf16[192,512]{1,0:T(8,128)(2,1)S(1)}, bf16[192,512]{1,0:T(8,128)(2,1)S(1)}, u32[]{:S(2)}, u32[]{:S(2)}) collective-permute-start(bf16[192,512]{1,0:T(8,128)(2,1)S(1)} %get-tuple-element.60.g0), channel_id=1, source_target_pairs={{0,2},{1,3},{2,0},{3,1},{4,6},{5,7},{6,4},{7,5},{8,10},{9,11},{10,... | collective-permute-start | bytes 589832 | tf_op jit(solution)/shard_map/ppermute | solution.py:389
  24.7 2.6 %collective-permute-start.8 = (bf16[192,512]{1,0:T(8,128)(2,1)S(1)}, bf16[192,512]{1,0:T(8,128)(2,1)S(1)}, u32[]{:S(2)}, u32[]{:S(2)}) collective-permute-start(bf16[192,512]{1,0:T(8,128)(2,1)S(1)} %get-tuple-element.60.g0), channel_id=1, source_target_pairs={{0,1},{1,0},{2,3},{3,2},{4,5},{5,4},{6,7},{7,6},{8,9},{9,8},{10,11... | collective-permute-start | bytes 589832 | tf_op jit(solution)/shard_map/ppermute | solution.py:389
  27.3 0.5 collective-permute-start.9
  27.9 3.0 %shard_map.108 = (f32[192,256]{1,0:T(8,128)S(1)}, bf16[96,256]{1,0:T(8,128)(2,1)S(1)}, bf16[96,256]{1,0:T(8,128)(2,1)S(1)}, bf16[64,256]{1,0:T(8,128)(2,1)S(1)}) custom-call(s32[2]{0:T(128)S(1)} %pad_add_fusion.place, f32[32,256]{1,0:T(8,128)S(1)} %get-tuple-element.45.nbt, bf16[192,256]{1,0:T(8,128)(2,1)S(1)} %get-tuple-element.63.grad, ...), custom_call_target="tpu_custom_call" | custom-call | flops 4000000000 | bytes 10000 | tf_op jit(solution)/shard_map/pallas_call | solution.py:348
  30.9 1.5 %collective-permute-start.12 = (bf16[96,256]{1,0:T(8,128)(2,1)S(1)}, bf16[96,256]{1,0:T(8,128)(2,1)S(1)}, u32[]{:S(2)}, u32[]{:S(2)}) collective-permute-start(bf16[96,256]{1,0:T(8,128)(2,1)S(1)} %get-tuple-element.67), channel_id=1, source_target_pairs={{0,1},{1,0},{2,3},{3,2},{4,8},{5,9},{6,10},{7,11},{8,4},{9,5},{10,... | collective-permute-start | bytes 147464 | tf_op jit(solution)/shard_map/ppermute | solution.py:385
  32.4 0.0 collective-permute-done.11.r1
  32.4 4.3 %shard_map.109 = (bf16[768,1792]{1,0:T(8,128)(2,1)S(1)}, bf16[768,1792]{1,0:T(8,128)(2,1)S(1)}) custom-call(s32[2]{0:T(128)S(1)} %pad_add_fusion.place, bf16[224,512]{1,0:T(8,128)(2,1)S(1)} %get-tuple-element.55.p0, bf16[224,512]{1,0:T(8,128)(2,1)S(1)} %collective-permute-done.4.p2, bf16[224,512]{1,0:T(8,128)(2,1)S(1)} %collective-permute-done.5.p1, ...), custom_call_target="tpu_custom_call" | custom-call | flops 4000000000 | bytes 10000 | tf_op jit(solution)/shard_map/pallas_call | solution.py:348
  36.7 0.3 collective-permute-done.12.m2
  37.0 0.0 collective-permute-done.13.m1
  37.0 0.6 shard_map.110
  37.6 2.2 %collective-permute-start.15 = (bf16[96,256]{1,0:T(8,128)(2,1)S(1)}, bf16[96,256]{1,0:T(8,128)(2,1)S(1)}, u32[]{:S(2)}, u32[]{:S(2)}) collective-permute-start(bf16[96,256]{1,0:T(8,128)(2,1)S(1)} %get-tuple-element.72), channel_id=1, source_target_pairs={{0,4},{1,2},{2,1},{3,7},{4,0},{5,6},{6,5},{7,3},{8,12},{9,10},{10,... | collective-permute-start | bytes 147464 | tf_op jit(solution)/shard_map/ppermute | solution.py:385
  39.7 0.0 collective-permute-start.16
  39.7 0.0 collective-permute-done.7.g2
  39.7 0.0 collective-permute-done.9.g3
  39.7 1.7 %shard_map.111 = (f32[128,1792]{1,0:T(8,128)S(1)}, f32[128,1792]{1,0:T(8,128)S(1)}) custom-call(s32[2]{0:T(128)S(1)} %pad_add_fusion.place, bf16[192,512]{1,0:T(8,128)(2,1)S(1)} %get-tuple-element.60.g0, bf16[192,512]{1,0:T(8,128)(2,1)S(1)} %collective-permute-done.7.g2, bf16[192,512]{1,0:T(8,128)(2,1)S(1)} %collective-permute-done.8.g1, ...), custom_call_target="tpu_custom_call" | custom-call | flops 4000000000 | bytes 10000 | tf_op jit(solution)/shard_map/pallas_call | solution.py:348
  41.4 0.3 collective-permute-start.14
  41.8 1.7 %shard_map.112 = (bf16[128,1792]{1,0:T(8,128)(2,1)S(1)}, bf16[128,1792]{1,0:T(8,128)(2,1)S(1)}) custom-call(s32[2]{0:T(128)S(1)} %pad_add_fusion.place, bf16[192,512]{1,0:T(8,128)(2,1)S(1)} %get-tuple-element.60.g0, bf16[192,512]{1,0:T(8,128)(2,1)S(1)} %collective-permute-done.7.g2, bf16[192,512]{1,0:T(8,128)(2,1)S(1)} %collective-permute-done.8.g1, ...), custom_call_target="tpu_custom_call" | custom-call | flops 100000 | bytes 10000 | tf_op jit(solution)/shard_map/pallas_call | solution.py:348
  43.5 0.4 collective-permute-start.20
  43.8 0.0 collective-permute-done.15.n2
  43.8 0.0 collective-permute-done.16.n1
  43.8 1.0 %shard_map.113 = (bf16[128,256]{1,0:T(8,128)(2,1)S(1)}, bf16[128,256]{1,0:T(8,128)(2,1)S(1)}) custom-call(s32[2]{0:T(128)S(1)} %pad_add_fusion.place, f32[192,256]{1,0:T(8,128)S(1)} %get-tuple-element.64.late.own, bf16[96,256]{1,0:T(8,128)(2,1)S(1)} %collective-permute-done.12.m2, bf16[96,256]{1,0:T(8,128)(2,1)S(1)} %collective-permute-done.13.m1, ...), custom_call_target="tpu_custom_call" | custom-call | flops 20000000000 | bytes 10000 | tf_op jit(solution)/shard_map/pallas_call | solution.py:348
  44.8 0.3 collective-permute-start.21
  45.1 0.0 collective-permute-done.14.come
  45.1 0.6 shard_map.114
  45.8 4.0 %collective-permute-start.17 = (bf16[32,1792]{1,0:T(8,128)(2,1)S(1)}, bf16[32,1792]{1,0:T(8,128)(2,1)S(1)}, u32[]{:S(2)}, u32[]{:S(2)}) collective-permute-start(bf16[32,1792]{1,0:T(8,128)(2,1)S(1)} %get-tuple-element.78), channel_id=1, source_target_pairs={{0,128},{4,132},{8,136},{12,140},{16,144},{20,148},{24,152},{28,15... | collective-permute-start | bytes 344072 | tf_op jit(solution)/shard_map/ppermute | solution.py:389
  49.7 1.0 %collective-permute-start.18 = (bf16[32,1792]{1,0:T(8,128)(2,1)S(1)}, bf16[32,1792]{1,0:T(8,128)(2,1)S(1)}, u32[]{:S(2)}, u32[]{:S(2)}) collective-permute-start(bf16[32,1792]{1,0:T(8,128)(2,1)S(1)} %get-tuple-element.79), channel_id=1, source_target_pairs={{0,64},{4,68},{8,72},{12,76},{16,80},{20,84},{24,88},{28,92},{32,9... | collective-permute-start | bytes 344072 | tf_op jit(solution)/shard_map/ppermute | solution.py:389
  50.7 0.1 collective-permute-start.19
  50.8 0.0 collective-permute-done.21.rs
  50.8 0.0 collective-permute-done.20.come
  50.8 0.7 shard_map.116
  51.5 3.1 %collective-permute-start.22 = (bf16[32,2304]{1,0:T(8,128)(2,1)S(1)}, bf16[32,2304]{1,0:T(8,128)(2,1)S(1)}, u32[]{:S(2)}, u32[]{:S(2)}) collective-permute-start(bf16[32,2304]{1,0:T(8,128)(2,1)S(1)} %get-tuple-element.84), channel_id=1, source_target_pairs={{0,128},{4,132},{8,136},{12,140},{16,144},{20,148},{24,152},{28,15... | collective-permute-start | bytes 442376 | tf_op jit(solution)/shard_map/ppermute | solution.py:389
  54.6 1.0 %collective-permute-start.23 = (bf16[32,2304]{1,0:T(8,128)(2,1)S(1)}, bf16[32,2304]{1,0:T(8,128)(2,1)S(1)}, u32[]{:S(2)}, u32[]{:S(2)}) collective-permute-start(bf16[32,2304]{1,0:T(8,128)(2,1)S(1)} %get-tuple-element.85), channel_id=1, source_target_pairs={{0,64},{4,68},{8,72},{12,76},{16,80},{20,84},{24,88},{28,92},{32,9... | collective-permute-start | bytes 442376 | tf_op jit(solution)/shard_map/ppermute | solution.py:389
  55.6 0.0 collective-permute-done.17.a2
  55.6 1.7 %collective-permute-start.24 = (bf16[32,2304]{1,0:T(8,128)(2,1)S(1)}, bf16[32,2304]{1,0:T(8,128)(2,1)S(1)}, u32[]{:S(2)}, u32[]{:S(2)}) collective-permute-start(bf16[32,2304]{1,0:T(8,128)(2,1)S(1)} %get-tuple-element.86), channel_id=1, source_target_pairs={{0,192},{4,196},{8,200},{12,204},{16,208},{20,212},{24,216},{28,22... | collective-permute-start | bytes 442376 | tf_op jit(solution)/shard_map/ppermute | solution.py:389
  57.3 0.0 collective-permute-done.18.a1
  57.3 3.5 %collective-permute-done.19.a3 = bf16[32,1792]{1,0:T(8,128)(2,1)S(1)} collective-permute-done((bf16[32,1792]{1,0:T(8,128)(2,1)S(1)}, bf16[32,1792]{1,0:T(8,128)(2,1)S(1)}, u32[]{:S(2)}, u32[]{:S(2)}) %collective-permute-start.19) | collective-permute-done | bytes 114720 | tf_op jit(solution)/shard_map/ppermute | solution.py:389
  60.8 0.6 shard_map.115.two
  61.4 1.6 %collective-permute-done.23.b1 = bf16[32,2304]{1,0:T(8,128)(2,1)S(1)} collective-permute-done((bf16[32,2304]{1,0:T(8,128)(2,1)S(1)}, bf16[32,2304]{1,0:T(8,128)(2,1)S(1)}, u32[]{:S(2)}, u32[]{:S(2)}) %collective-permute-start.23) | collective-permute-done | bytes 147488 | tf_op jit(solution)/shard_map/ppermute | solution.py:389
  63.0 0.2 collective-permute-done.24.b3
  63.2 0.9 %shard_map.117 = bf16[64,2560]{1,0:T(8,128)(2,1)S(1)} custom-call(s32[2]{0:T(128)S(1)} %pad_add_fusion.place, bf16[32,1792]{1,0:T(8,128)(2,1)S(1)} %shard_map.115.two, bf16[32,2304]{1,0:T(8,128)(2,1)S(1)} %get-tuple-element.83.b0, bf16[32,2304]{1,0:T(8,128)(2,1)S(1)} %collective-permute-done.22.b2, bf16[32,2304]{1,0:T(8,128)(2,1)S(1)} %collective-permute-done.23.b1, ...), custom_call_target="tpu_custom_call" | custom-call | flops 100000 | bytes 10000 | tf_op jit(solution)/shard_map/pallas_call | solution.py:348
  64.1 17.2 %all_to_all.5.refs_0_ = bf16[8,8,2560]{2,1,0:T(8,128)(2,1)S(1)} all-to-all(bf16[8,8,2560]{2,1,0:T(8,128)(2,1)S(1)} %bitcast.5), channel_id=1, replica_groups={{0,8,16,24,32,40,48,56},{4,12,20,28,36,44,52,60},{64,72,80,88,96,104,11..., dimensions={0} | all-to-all | bytes 655360 | tf_op jit(solution)/shard_map/all_to_all | solution.py:567
  81.4 0.9 %shard_map.118 = (bf16[192,256]{1,0:T(8,128)(2,1)}, f32[4,1728]{1,0:T(4,128)}, f32[4,1728]{1,0:T(4,128)}) custom-call(bf16[8,8,2560]{2,1,0:T(8,128)(2,1)S(1)} %all_to_all.5.refs_0_), custom_call_target="tpu_custom_call" | custom-call | flops 100000 | bytes 10000 | tf_op jit(solution)/shard_map/pallas_call | solution.py:348
  (8 shorter events, 0.0 us)
Async XLA Ops:
  0.7 6.5 %copy-start = (bf16[256,6912]{1,0:T(8,128)(2,1)S(1)}, bf16[256,6912]{1,0:T(8,128)(2,1)}, u32[]{:S(2)}) copy-start(bf16[256,6912]{1,0:T(8,128)(2,1)} %weight.2) | copy-start | bytes 10616836
  3.0 24.8 %copy-start.1 = (bf16[256,6912]{1,0:T(8,128)(2,1)S(1)}, bf16[256,6912]{1,0:T(8,128)(2,1)}, u32[]{:S(2)}) copy-start(bf16[256,6912]{1,0:T(8,128)(2,1)} %weight.3) | copy-start | bytes 10616836
  3.0 15.8 %collective-permute-start.4 = (bf16[224,512]{1,0:T(8,128)(2,1)S(1)}, bf16[224,512]{1,0:T(8,128)(2,1)S(1)}, u32[]{:S(2)}, u32[]{:S(2)}) collective-permute-start(bf16[224,512]{1,0:T(8,128)(2,1)S(1)} %get-tuple-element.56), channel_id=1, source_target_pairs={{0,2},{1,3},{2,0},{3,1},{4,6},{5,7},{6,4},{7,5},{8,10},{9,11},{10,... | collective-permute-start | bytes 688136 | tf_op jit(solution)/shard_map/ppermute | solution.py:389
  5.3 13.6 %collective-permute-start.5 = (bf16[224,512]{1,0:T(8,128)(2,1)S(1)}, bf16[224,512]{1,0:T(8,128)(2,1)S(1)}, u32[]{:S(2)}, u32[]{:S(2)}) collective-permute-start(bf16[224,512]{1,0:T(8,128)(2,1)S(1)} %get-tuple-element.57), channel_id=1, source_target_pairs={{0,1},{1,0},{2,3},{3,2},{4,5},{5,4},{6,7},{7,6},{8,9},{9,8},{10,11... | collective-permute-start | bytes 688136 | tf_op jit(solution)/shard_map/ppermute | solution.py:389
  6.7 12.2 %collective-permute-start.6 = (bf16[224,512]{1,0:T(8,128)(2,1)S(1)}, bf16[224,512]{1,0:T(8,128)(2,1)S(1)}, u32[]{:S(2)}, u32[]{:S(2)}) collective-permute-start(bf16[224,512]{1,0:T(8,128)(2,1)S(1)} %get-tuple-element.58), channel_id=1, source_target_pairs={{0,3},{1,2},{2,1},{3,0},{4,7},{5,6},{6,5},{7,4},{8,11},{9,10},{10,... | collective-permute-start | bytes 688136 | tf_op jit(solution)/shard_map/ppermute | solution.py:389
  10.3 7.2 %collective-permute-start = (bf16[96,256]{1,0:T(8,128)(2,1)S(1)}, bf16[96,256]{1,0:T(8,128)(2,1)S(1)}, u32[]{:S(2)}, u32[]{:S(2)}) collective-permute-start(bf16[96,256]{1,0:T(8,128)(2,1)S(1)} %get-tuple-element.48), channel_id=1, source_target_pairs={{0,1},{1,0},{2,3},{3,2},{4,8},{5,9},{6,10},{7,11},{8,4},{9,5},{10,... | collective-permute-start | bytes 147464 | tf_op jit(solution)/shard_map/ppermute | solution.py:385
  12.6 4.9 %collective-permute-start.1 = (bf16[96,256]{1,0:T(8,128)(2,1)S(1)}, bf16[96,256]{1,0:T(8,128)(2,1)S(1)}, u32[]{:S(2)}, u32[]{:S(2)}) collective-permute-start(bf16[96,256]{1,0:T(8,128)(2,1)S(1)} %get-tuple-element.49), channel_id=1, source_target_pairs={{0,4},{1,5},{2,6},{3,7},{4,0},{5,1},{6,2},{7,3},{8,12},{9,13},{10,... | collective-permute-start | bytes 147464 | tf_op jit(solution)/shard_map/ppermute | solution.py:385
  18.1 4.2 %collective-permute-start.2 = (bf16[96,256]{1,0:T(8,128)(2,1)S(1)}, bf16[96,256]{1,0:T(8,128)(2,1)S(1)}, u32[]{:S(2)}, u32[]{:S(2)}) collective-permute-start(bf16[96,256]{1,0:T(8,128)(2,1)S(1)} %get-tuple-element.51), channel_id=1, source_target_pairs={{0,4},{1,2},{2,1},{3,7},{4,0},{5,6},{6,5},{7,3},{8,12},{9,10},{10,... | collective-permute-start | bytes 147464 | tf_op jit(solution)/shard_map/ppermute | solution.py:385
  18.7 4.1 %collective-permute-start.3 = (bf16[96,256]{1,0:T(8,128)(2,1)S(1)}, bf16[96,256]{1,0:T(8,128)(2,1)S(1)}, u32[]{:S(2)}, u32[]{:S(2)}) collective-permute-start(bf16[96,256]{1,0:T(8,128)(2,1)S(1)} %get-tuple-element.52.late), channel_id=1, source_target_pairs={{0,1},{1,0},{2,3},{3,2},{4,5},{5,4},{6,7},{7,6},{8,9},{9,8},{10,11... | collective-permute-start | bytes 147464 | tf_op jit(solution)/shard_map/ppermute | solution.py:385
  20.1 10.8 %collective-permute-start.10 = (bf16[768,256]{1,0:T(8,128)(2,1)S(1)}, bf16[768,256]{1,0:T(8,128)(2,1)S(1)}, u32[]{:S(2)}, u32[]{:S(2)}) collective-permute-start(bf16[768,256]{1,0:T(8,128)(2,1)S(1)} %get-tuple-element.61), channel_id=1, source_target_pairs={{0,1},{1,0},{2,3},{3,2},{4,8},{5,9},{6,10},{7,11},{8,4},{9,5},{10,... | collective-permute-start | bytes 1179656 | tf_op jit(solution)/shard_map/ppermute | solution.py:385
  22.1 10.3 %collective-permute-start.11 = (bf16[768,256]{1,0:T(8,128)(2,1)S(1)}, bf16[768,256]{1,0:T(8,128)(2,1)S(1)}, u32[]{:S(2)}, u32[]{:S(2)}) collective-permute-start(bf16[768,256]{1,0:T(8,128)(2,1)S(1)} %get-tuple-element.62), channel_id=1, source_target_pairs={{0,4},{1,5},{2,6},{3,7},{4,0},{5,1},{6,2},{7,3},{8,12},{9,13},{10,... | collective-permute-start | bytes 1179656 | tf_op jit(solution)/shard_map/ppermute | solution.py:385
  23.7 16.0 %collective-permute-start.7 = (bf16[192,512]{1,0:T(8,128)(2,1)S(1)}, bf16[192,512]{1,0:T(8,128)(2,1)S(1)}, u32[]{:S(2)}, u32[]{:S(2)}) collective-permute-start(bf16[192,512]{1,0:T(8,128)(2,1)S(1)} %get-tuple-element.60.g0), channel_id=1, source_target_pairs={{0,2},{1,3},{2,0},{3,1},{4,6},{5,7},{6,4},{7,5},{8,10},{9,11},{10,... | collective-permute-start | bytes 589832 | tf_op jit(solution)/shard_map/ppermute | solution.py:389
  24.7 15.0 %collective-permute-start.8 = (bf16[192,512]{1,0:T(8,128)(2,1)S(1)}, bf16[192,512]{1,0:T(8,128)(2,1)S(1)}, u32[]{:S(2)}, u32[]{:S(2)}) collective-permute-start(bf16[192,512]{1,0:T(8,128)(2,1)S(1)} %get-tuple-element.60.g0), channel_id=1, source_target_pairs={{0,1},{1,0},{2,3},{3,2},{4,5},{5,4},{6,7},{7,6},{8,9},{9,8},{10,11... | collective-permute-start | bytes 589832 | tf_op jit(solution)/shard_map/ppermute | solution.py:389
  27.3 12.4 %collective-permute-start.9 = (bf16[192,512]{1,0:T(8,128)(2,1)S(1)}, bf16[192,512]{1,0:T(8,128)(2,1)S(1)}, u32[]{:S(2)}, u32[]{:S(2)}) collective-permute-start(bf16[192,512]{1,0:T(8,128)(2,1)S(1)} %get-tuple-element.60.g0), channel_id=1, source_target_pairs={{0,3},{1,2},{2,1},{3,0},{4,7},{5,6},{6,5},{7,4},{8,11},{9,10},{10,... | collective-permute-start | bytes 589832 | tf_op jit(solution)/shard_map/ppermute | solution.py:389
  30.9 6.0 %collective-permute-start.12 = (bf16[96,256]{1,0:T(8,128)(2,1)S(1)}, bf16[96,256]{1,0:T(8,128)(2,1)S(1)}, u32[]{:S(2)}, u32[]{:S(2)}) collective-permute-start(bf16[96,256]{1,0:T(8,128)(2,1)S(1)} %get-tuple-element.67), channel_id=1, source_target_pairs={{0,1},{1,0},{2,3},{3,2},{4,8},{5,9},{6,10},{7,11},{8,4},{9,5},{10,... | collective-permute-start | bytes 147464 | tf_op jit(solution)/shard_map/ppermute | solution.py:385
  32.4 4.6 %collective-permute-start.13 = (bf16[96,256]{1,0:T(8,128)(2,1)S(1)}, bf16[96,256]{1,0:T(8,128)(2,1)S(1)}, u32[]{:S(2)}, u32[]{:S(2)}) collective-permute-start(bf16[96,256]{1,0:T(8,128)(2,1)S(1)} %get-tuple-element.68), channel_id=1, source_target_pairs={{0,4},{1,5},{2,6},{3,7},{4,0},{5,1},{6,2},{7,3},{8,12},{9,13},{10,... | collective-permute-start | bytes 147464 | tf_op jit(solution)/shard_map/ppermute | solution.py:385
  37.6 6.3 %collective-permute-start.15 = (bf16[96,256]{1,0:T(8,128)(2,1)S(1)}, bf16[96,256]{1,0:T(8,128)(2,1)S(1)}, u32[]{:S(2)}, u32[]{:S(2)}) collective-permute-start(bf16[96,256]{1,0:T(8,128)(2,1)S(1)} %get-tuple-element.72), channel_id=1, source_target_pairs={{0,4},{1,2},{2,1},{3,7},{4,0},{5,6},{6,5},{7,3},{8,12},{9,10},{10,... | collective-permute-start | bytes 147464 | tf_op jit(solution)/shard_map/ppermute | solution.py:385
  39.7 4.1 %collective-permute-start.16 = (bf16[96,256]{1,0:T(8,128)(2,1)S(1)}, bf16[96,256]{1,0:T(8,128)(2,1)S(1)}, u32[]{:S(2)}, u32[]{:S(2)}) collective-permute-start(bf16[96,256]{1,0:T(8,128)(2,1)S(1)} %get-tuple-element.69.late), channel_id=1, source_target_pairs={{0,1},{1,0},{2,3},{3,2},{4,5},{5,4},{6,7},{7,6},{8,9},{9,8},{10,11... | collective-permute-start | bytes 147464 | tf_op jit(solution)/shard_map/ppermute | solution.py:385
  41.4 3.7 %collective-permute-start.14 = (f32[128,1792]{1,0:T(8,128)S(1)}, f32[128,1792]{1,0:T(8,128)S(1)}, u32[]{:S(2)}, u32[]{:S(2)}) collective-permute-start(f32[128,1792]{1,0:T(8,128)S(1)} %get-tuple-element.71), channel_id=1, source_target_pairs={{0,4},{4,0},{8,12},{12,8},{16,20},{20,16},{24,28},{28,24},{32,36},... | collective-permute-start | bytes 2752520 | tf_op jit(solution)/shard_map/ppermute | solution.py:389
  43.5 7.3 %collective-permute-start.20 = (bf16[128,1792]{1,0:T(8,128)(2,1)S(1)}, bf16[128,1792]{1,0:T(8,128)(2,1)S(1)}, u32[]{:S(2)}, u32[]{:S(2)}) collective-permute-start(bf16[128,1792]{1,0:T(8,128)(2,1)S(1)} %get-tuple-element.81), channel_id=1, source_target_pairs={{0,4},{4,0},{8,12},{12,8},{16,20},{20,16},{24,28},{28,24},{32,36},... | collective-permute-start | bytes 1376264 | tf_op jit(solution)/shard_map/ppermute | solution.py:389
  44.8 6.0 %collective-permute-start.21 = (bf16[128,256]{1,0:T(8,128)(2,1)S(1)}, bf16[128,256]{1,0:T(8,128)(2,1)S(1)}, u32[]{:S(2)}, u32[]{:S(2)}) collective-permute-start(bf16[128,256]{1,0:T(8,128)(2,1)S(1)} %get-tuple-element.82), channel_id=1, source_target_pairs={{0,4},{4,0},{8,12},{12,8},{16,20},{20,16},{24,28},{28,24},{32,36},... | collective-permute-start | bytes 196616 | tf_op jit(solution)/shard_map/ppermute | solution.py:389
  45.8 9.8 %collective-permute-start.17 = (bf16[32,1792]{1,0:T(8,128)(2,1)S(1)}, bf16[32,1792]{1,0:T(8,128)(2,1)S(1)}, u32[]{:S(2)}, u32[]{:S(2)}) collective-permute-start(bf16[32,1792]{1,0:T(8,128)(2,1)S(1)} %get-tuple-element.78), channel_id=1, source_target_pairs={{0,128},{4,132},{8,136},{12,140},{16,144},{20,148},{24,152},{28,15... | collective-permute-start | bytes 344072 | tf_op jit(solution)/shard_map/ppermute | solution.py:389
  49.7 7.6 %collective-permute-start.18 = (bf16[32,1792]{1,0:T(8,128)(2,1)S(1)}, bf16[32,1792]{1,0:T(8,128)(2,1)S(1)}, u32[]{:S(2)}, u32[]{:S(2)}) collective-permute-start(bf16[32,1792]{1,0:T(8,128)(2,1)S(1)} %get-tuple-element.79), channel_id=1, source_target_pairs={{0,64},{4,68},{8,72},{12,76},{16,80},{20,84},{24,88},{28,92},{32,9... | collective-permute-start | bytes 344072 | tf_op jit(solution)/shard_map/ppermute | solution.py:389
  50.7 10.1 %collective-permute-start.19 = (bf16[32,1792]{1,0:T(8,128)(2,1)S(1)}, bf16[32,1792]{1,0:T(8,128)(2,1)S(1)}, u32[]{:S(2)}, u32[]{:S(2)}) collective-permute-start(bf16[32,1792]{1,0:T(8,128)(2,1)S(1)} %get-tuple-element.80), channel_id=1, source_target_pairs={{0,192},{4,196},{8,200},{12,204},{16,208},{20,212},{24,216},{28,22... | collective-permute-start | bytes 344072 | tf_op jit(solution)/shard_map/ppermute | solution.py:389
  51.5 9.9 %collective-permute-start.22 = (bf16[32,2304]{1,0:T(8,128)(2,1)S(1)}, bf16[32,2304]{1,0:T(8,128)(2,1)S(1)}, u32[]{:S(2)}, u32[]{:S(2)}) collective-permute-start(bf16[32,2304]{1,0:T(8,128)(2,1)S(1)} %get-tuple-element.84), channel_id=1, source_target_pairs={{0,128},{4,132},{8,136},{12,140},{16,144},{20,148},{24,152},{28,15... | collective-permute-start | bytes 442376 | tf_op jit(solution)/shard_map/ppermute | solution.py:389
  54.6 8.4 %collective-permute-start.23 = (bf16[32,2304]{1,0:T(8,128)(2,1)S(1)}, bf16[32,2304]{1,0:T(8,128)(2,1)S(1)}, u32[]{:S(2)}, u32[]{:S(2)}) collective-permute-start(bf16[32,2304]{1,0:T(8,128)(2,1)S(1)} %get-tuple-element.85), channel_id=1, source_target_pairs={{0,64},{4,68},{8,72},{12,76},{16,80},{20,84},{24,88},{28,92},{32,9... | collective-permute-start | bytes 442376 | tf_op jit(solution)/shard_map/ppermute | solution.py:389
  55.6 7.6 %collective-permute-start.24 = (bf16[32,2304]{1,0:T(8,128)(2,1)S(1)}, bf16[32,2304]{1,0:T(8,128)(2,1)S(1)}, u32[]{:S(2)}, u32[]{:S(2)}) collective-permute-start(bf16[32,2304]{1,0:T(8,128)(2,1)S(1)} %get-tuple-element.86), channel_id=1, source_target_pairs={{0,192},{4,196},{8,200},{12,204},{16,208},{20,212},{24,216},{28,22... | collective-permute-start | bytes 442376 | tf_op jit(solution)/shard_map/ppermute | solution.py:389

commit v15 on v14

--- a/solution.py
+++ b/solution.py
@@ -50,9 +50,22 @@
     return onehot(iota((S, 8 * HB), 0) == halo_row)
 
 
+def turn_channels(column, both):
+    offset = (column * QW) % C
+    return mm(both[...], onehot(iota((C, C), 0) == (iota((C, C), 1) + offset) % C)).astype(BF)
+
+
+def peers_kernel(place, pay, both, p2, p1, p3):
+    for turn, out in ((2, p2), (1, p1), (3, p3)):
+        turned = turn_channels(place[1] ^ turn, both)
+        out[0:S, 0:C] = turned[0:S]
+        out[0:S, C : 2 * C] = turned[S : 2 * S]
+        out[S : S + 32, :] = pay[S : S + 32, :]
+
+
 def pack_kernel(
-    place, feat, pre, grad, nbr, halo, send, pay, p2, p1, p3, nbt, hrow, srow, pre_out,
-    grad_out, ids, halo_ids, send_ids, feat_in, sems
+    place, feat, pre, grad, nbr, halo, send, pay, both, nbt, hrow, srow, pre_out, grad_out,
+    ids, halo_ids, send_ids, feat_in, sems
 ):
     copies = [
         pltpu.make_async_copy(source, target, sems.at[n])
@@ -94,14 +107,11 @@
     pay[S : S + K, C : C + S] = (shifted_up - 16.0 * high).astype(BF)
     last = pay[S + 16 : S + 32, 0:C].astype(F32)
     pay[S + 16 : S + 32, 0:C] = jnp.where(iota((16, C), 0) == 15, row, last).astype(BF)
-    both = jnp.concatenate([feat_in[...], hidden], axis=0)
-    for turn, out in ((0, pay), (1, p1), (2, p2), (3, p3)):
-        offset = ((place[1] ^ turn) * QW) % C
-        turned = mm(both, onehot(iota((C, C), 0) == (iota((C, C), 1) + offset) % C)).astype(BF)
-        out[0:S, 0:C] = turned[0:S]
-        out[0:S, C : 2 * C] = turned[S : 2 * S]
-        if turn:
-            out[S : S + 32, :] = pay[S : S + 32, :]
+    both[0:S, :] = feat_in[...]
+    both[S : 2 * S, :] = hidden
+    turned = turn_channels(place[1], both)
+    pay[0:S, 0:C] = turned[0:S]
+    pay[0:S, C : 2 * C] = turned[S : 2 * S]
     lane, peer = iota((64, C), 1), iota((64, C), 0)
     parity = jnp.where(lane < 128, place[0] % 2, 1 - place[0] % 2)
     pick = onehot(peer == 2 * ((lane % 128) // 4) + parity)
@@ -183,15 +193,12 @@
     send[...] = chosen[128:256, :]
 
 
-def pick_kernel(place, p0, p2, p1, p3, late, o2, o1, loc, picked, ids):
+def pick_kernel(place, p0, p2, p1, p3, late, o2, o1, loc, picked):
     column = place[1]
-    pays = (p0, p1, p2, p3)
-    for turn, pay in enumerate(pays):
-        ids[turn : turn + 1, :] = pay[S + 16 : S + 32, 0:C].astype(F32)[15:16, :] - 1.0
-    slots = jnp.transpose(ids[...])[:, 0:8].astype(jnp.int32)
-    for turn, pay in enumerate(pays):
-        chosen = onehot(iota((8 * HB, S), 1) == slots[:, turn : turn + 1])
-        picked[column ^ turn] = mm(chosen, pay[0:S, 0 : 2 * C]).astype(BF)
+    for turn, pay in enumerate((p0, p1, p2, p3)):
+        halo_row = pay[S + 16 : S + 32, 0:C].astype(F32)[15:16, :].astype(jnp.int32) - 1
+        rows = mm_t(halo_matrix(halo_row), pay[0:S, 0 : 2 * C])
+        picked[column ^ turn] = rows.astype(BF)
     even = place[0] % 2 == 0
     up = pl.multiple_of(jnp.where(even, 160, 0), 32)
     down = pl.multiple_of(jnp.where(even, 0, 160), 32)
@@ -408,10 +415,11 @@
     scale = 1.0 / math.sqrt(S * gx * lax.axis_size("gy"))
     place = jnp.stack([lax.axis_index("gx"), lax.axis_index("gy")]).astype(jnp.int32)
     tile = sds((S, C), BF)
-    pay, p2, p1, p3, nbt, hrow, srow, pre, grad = call(
+    pay, both, nbt, hrow, srow, pre, grad = call(
         pack_kernel,
         (
-            *[sds((S + 32, 2 * C), BF)] * 4,
+            sds((S + 32, 2 * C), BF),
+            sds((2 * S, C), BF),
             sds((32, C), F32),
             sds((8, C), jnp.int32),
             sds((8, C), jnp.int32),
@@ -431,7 +439,6 @@
             )
         ],
         specs=[SMEM] + [HBM] * 6,
-        flops=4 * 10**9,
         scratch=[
             pltpu.VMEM((K, S), jnp.int32),
             pltpu.VMEM((1, 8, 24), jnp.int32),
@@ -440,6 +447,8 @@
             pltpu.SemaphoreType.DMA((6,)),
         ],
     )
+    peer = sds((S + 32, 2 * C), BF)
+    p2, p1, p3 = call(peers_kernel, (peer,) * 3, place, pay, both, flops=4 * 10**9)
     pays = [pay] + [cross(value, "gy", d) for d, value in ((2, p2), (1, p1), (3, p3))]
     back = pltpu.VMEM((8, HB, C), BF)
     own, m1, m2, loc = spread(place, nbt, grad, weight_two, 10**5)
@@ -452,7 +461,7 @@
         place,
         *pays,
         passed,
-        scratch=[pltpu.VMEM((4, 8 * HB, 2 * C), BF), pltpu.VMEM((128, C), F32)],
+        scratch=[pltpu.VMEM((4, 8 * HB, 2 * C), BF)],
         late=1,
     )
     r2, r1 = halo_lines(o2, o1)

time: 82.9 us -> 83.4 us (level)
    pallas_call x16 -> x17, Pallas kernels: 24 us -> 24.4 us  [call(): pl.pallas_call(kernel, out_shape=outs, in_specs=specs, out_specs=jax.tree...]
where the time goes in v15:
time: 83.4 us; the launch traced here: 82.6 us
  starting transfers between devices  28.8 us (35%)
  Pallas kernels  24.4 us (29%)
  blocking collectives  17.2 us (21%)
  waiting for transfers between devices  11.3 us (14%)
    pallas_call x17, Pallas kernels, call(): pl.pallas_call(kernel, out_shape=outs, in_specs=specs, out_specs=jax.tree...  24.4 us
    ppermute x15, starting transfers between devices, cross(): lax.ppermute(value, axis, [(n, n ^ mask) for n in range(lax.axis_size(axi...  20.2 us
    all_to_all x1, blocking collectives, body(): lax.all_to_all(summed.reshape(8, 8, 10 * C), 'gx', split_axis=0, concat_a...  17.2 us
    ppermute x10, starting transfers between devices, swap(): return lax.ppermute(value, ('gx', 'gy'), pairs)  8.57 us
    ppermute x10, waiting for transfers between devices, swap(): return lax.ppermute(value, ('gx', 'gy'), pairs)  6.01 us
    ppermute x15, waiting for transfers between devices, cross(): lax.ppermute(value, axis, [(n, n ^ mask) for n in range(lax.axis_size(axi...  5.3 us
  transfers between devices with their start and end apart: 25, of which 7 were waited for; matrix products, arithmetic and copies ran while one was open for 0% of the time, Pallas kernels for 24%

profile of v15, /device:TPU:2, one launch (start us, length us, event | category | flops | bytes accessed | tf_op | source)
XLA Modules:
  0.0 82.6 jit_solution(4171255330339078314)
XLA Ops:
  0.6 0.1 pad_add_fusion.place
  0.7 1.9 %shard_map.103 = (bf16[224,512]{1,0:T(8,128)(2,1)S(1)}, bf16[384,256]{1,0:T(8,128)(2,1)S(1)}, f32[32,256]{1,0:T(8,128)S(1)}, s32[8,256]{1,0:T(8,128)S(1)}, s32[8...) custom-call(s32[2]{0:T(128)S(1)} %pad_add_fusion.place, bf16[192,256]{1,0:T(8,128)(2,1)} %feat.1, ...), custom_call_target="tpu_custom_call" | custom-call | flops 100000 | bytes 10000 | tf_op jit(solution)/shard_map/pallas_call | solution.py:355
  2.6 0.0 copy-start
  2.6 0.9 %shard_map.106 = (bf16[224,512]{1,0:T(8,128)(2,1)S(1)}, bf16[224,512]{1,0:T(8,128)(2,1)S(1)}, bf16[224,512]{1,0:T(8,128)(2,1)S(1)}) custom-call(s32[2]{0:T(128)S(1)} %pad_add_fusion.place, bf16[224,512]{1,0:T(8,128)(2,1)S(1)} %get-tuple-element.56.pay.p0, bf16[384,256]{1,0:T(8,128)(2,1)S(1)} %get-tuple-element.57.both), custom_call_target="tpu_custom_call" | custom-call | flops 4000000000 | bytes 10000 | tf_op jit(solution)/shard_map/pallas_call | solution.py:355
  3.6 0.0 copy-start.1
  3.6 2.2 %collective-permute-start.4 = (bf16[224,512]{1,0:T(8,128)(2,1)S(1)}, bf16[224,512]{1,0:T(8,128)(2,1)S(1)}, u32[]{:S(2)}, u32[]{:S(2)}) collective-permute-start(bf16[224,512]{1,0:T(8,128)(2,1)S(1)} %get-tuple-element.58), channel_id=1, source_target_pairs={{0,2},{1,3},{2,0},{3,1},{4,6},{5,7},{6,4},{7,5},{8,10},{9,11},{10,... | collective-permute-start | bytes 688136 | tf_op jit(solution)/shard_map/ppermute | solution.py:396
  5.8 1.4 %collective-permute-start.5 = (bf16[224,512]{1,0:T(8,128)(2,1)S(1)}, bf16[224,512]{1,0:T(8,128)(2,1)S(1)}, u32[]{:S(2)}, u32[]{:S(2)}) collective-permute-start(bf16[224,512]{1,0:T(8,128)(2,1)S(1)} %get-tuple-element.59), channel_id=1, source_target_pairs={{0,1},{1,0},{2,3},{3,2},{4,5},{5,4},{6,7},{7,6},{8,9},{9,8},{10,11... | collective-permute-start | bytes 688136 | tf_op jit(solution)/shard_map/ppermute | solution.py:396
  7.2 0.5 collective-permute-start.6
  7.8 3.0 %shard_map.104 = (f32[192,256]{1,0:T(8,128)S(1)}, bf16[96,256]{1,0:T(8,128)(2,1)S(1)}, bf16[96,256]{1,0:T(8,128)(2,1)S(1)}, bf16[64,256]{1,0:T(8,128)(2,1)S(1)}) custom-call(s32[2]{0:T(128)S(1)} %pad_add_fusion.place, f32[32,256]{1,0:T(8,128)S(1)} %get-tuple-element.46.nbt, bf16[192,256]{1,0:T(8,128)(2,1)S(1)} %get-tuple-element.47.grad, ...), custom_call_target="tpu_custom_call" | custom-call | flops 100000 | bytes 10000 | tf_op jit(solution)/shard_map/pallas_call | solution.py:355
  10.8 2.4 %collective-permute-start = (bf16[96,256]{1,0:T(8,128)(2,1)S(1)}, bf16[96,256]{1,0:T(8,128)(2,1)S(1)}, u32[]{:S(2)}, u32[]{:S(2)}) collective-permute-start(bf16[96,256]{1,0:T(8,128)(2,1)S(1)} %get-tuple-element.49), channel_id=1, source_target_pairs={{0,1},{1,0},{2,3},{3,2},{4,8},{5,9},{6,10},{7,11},{8,4},{9,5},{10,... | collective-permute-start | bytes 147464 | tf_op jit(solution)/shard_map/ppermute | solution.py:392
  13.2 0.0 collective-permute-start.1
  13.2 4.9 %collective-permute-done.m2 = bf16[96,256]{1,0:T(8,128)(2,1)S(1)} collective-permute-done((bf16[96,256]{1,0:T(8,128)(2,1)S(1)}, bf16[96,256]{1,0:T(8,128)(2,1)S(1)}, u32[]{:S(2)}, u32[]{:S(2)}) %collective-permute-start) | collective-permute-done | bytes 49184 | tf_op jit(solution)/shard_map/ppermute | solution.py:392
  18.0 0.0 collective-permute-done.1.m1
  18.0 0.6 shard_map.105
  18.6 0.6 collective-permute-start.2
  19.2 0.2 collective-permute-start.3
  19.4 0.0 collective-permute-done.4.p2
  19.4 0.0 collective-permute-done.5.p1
  19.4 0.0 collective-permute-done.6.p3
  19.4 1.1 %shard_map.107 = (bf16[768,256]{1,0:T(8,128)(2,1)S(1)}, bf16[768,256]{1,0:T(8,128)(2,1)S(1)}, bf16[4,64,512]{2,1,0:T(8,128)(2,1)S(1)}) custom-call(s32[2]{0:T(128)S(1)} %pad_add_fusion.place, bf16[224,512]{1,0:T(8,128)(2,1)S(1)} %get-tuple-element.56.pay.p0, bf16[224,512]{1,0:T(8,128)(2,1)S(1)} %collective-permute-done.4.p2, ...), custom_call_target="tpu_custom_call" | custom-call | flops 100000 | bytes 10000 | tf_op jit(solution)/shard_map/pallas_call | solution.py:355
  20.5 2.0 %collective-permute-start.10 = (bf16[768,256]{1,0:T(8,128)(2,1)S(1)}, bf16[768,256]{1,0:T(8,128)(2,1)S(1)}, u32[]{:S(2)}, u32[]{:S(2)}) collective-permute-start(bf16[768,256]{1,0:T(8,128)(2,1)S(1)} %get-tuple-element.63), channel_id=1, source_target_pairs={{0,1},{1,0},{2,3},{3,2},{4,8},{5,9},{6,10},{7,11},{8,4},{9,5},{10,... | collective-permute-start | bytes 1179656 | tf_op jit(solution)/shard_map/ppermute | solution.py:392
  22.4 0.0 collective-permute-start.11
  22.4 0.3 collective-permute-done.2.n2
  22.8 0.5 collective-permute-done.3.n1
  23.3 0.9 %shard_map.108 = (bf16[192,256]{1,0:T(8,128)(2,1)S(1)}, bf16[192,512]{1,0:T(8,128)(2,1)S(1)}) custom-call(s32[2]{0:T(128)S(1)} %pad_add_fusion.place, f32[192,256]{1,0:T(8,128)S(1)} %get-tuple-element.48.late.own, bf16[96,256]{1,0:T(8,128)(2,1)S(1)} %collective-permute-done.m2, bf16[96,256]{1,0:T(8,128)(2,1)S(1)} %collective-permute-done.1.m1, ...), custom_call_target="tpu_custom_call" | custom-call | flops 100000 | bytes 10000 | tf_op jit(solution)/shard_map/pallas_call | solution.py:355
  24.2 1.0 %collective-permute-start.7 = (bf16[192,512]{1,0:T(8,128)(2,1)S(1)}, bf16[192,512]{1,0:T(8,128)(2,1)S(1)}, u32[]{:S(2)}, u32[]{:S(2)}) collective-permute-start(bf16[192,512]{1,0:T(8,128)(2,1)S(1)} %get-tuple-element.62.g0), channel_id=1, source_target_pairs={{0,2},{1,3},{2,0},{3,1},{4,6},{5,7},{6,4},{7,5},{8,10},{9,11},{10,... | collective-permute-start | bytes 589832 | tf_op jit(solution)/shard_map/ppermute | solution.py:396
  25.3 2.6 %collective-permute-start.8 = (bf16[192,512]{1,0:T(8,128)(2,1)S(1)}, bf16[192,512]{1,0:T(8,128)(2,1)S(1)}, u32[]{:S(2)}, u32[]{:S(2)}) collective-permute-start(bf16[192,512]{1,0:T(8,128)(2,1)S(1)} %get-tuple-element.62.g0), channel_id=1, source_target_pairs={{0,1},{1,0},{2,3},{3,2},{4,5},{5,4},{6,7},{7,6},{8,9},{9,8},{10,11... | collective-permute-start | bytes 589832 | tf_op jit(solution)/shard_map/ppermute | solution.py:396
  27.9 0.5 collective-permute-start.9
  28.4 3.0 %shard_map.109 = (f32[192,256]{1,0:T(8,128)S(1)}, bf16[96,256]{1,0:T(8,128)(2,1)S(1)}, bf16[96,256]{1,0:T(8,128)(2,1)S(1)}, bf16[64,256]{1,0:T(8,128)(2,1)S(1)}) custom-call(s32[2]{0:T(128)S(1)} %pad_add_fusion.place, f32[32,256]{1,0:T(8,128)S(1)} %get-tuple-element.46.nbt, bf16[192,256]{1,0:T(8,128)(2,1)S(1)} %get-tuple-element.65.grad, ...), custom_call_target="tpu_custom_call" | custom-call | flops 4000000000 | bytes 10000 | tf_op jit(solution)/shard_map/pallas_call | solution.py:355
  31.5 0.0 collective-permute-done.10.r2
  31.5 1.3 %collective-permute-start.12 = (bf16[96,256]{1,0:T(8,128)(2,1)S(1)}, bf16[96,256]{1,0:T(8,128)(2,1)S(1)}, u32[]{:S(2)}, u32[]{:S(2)}) collective-permute-start(bf16[96,256]{1,0:T(8,128)(2,1)S(1)} %get-tuple-element.69), channel_id=1, source_target_pairs={{0,1},{1,0},{2,3},{3,2},{4,8},{5,9},{6,10},{7,11},{8,4},{9,5},{10,... | collective-permute-start | bytes 147464 | tf_op jit(solution)/shard_map/ppermute | solution.py:392
  32.8 0.0 collective-permute-done.11.r1
  32.8 0.0 collective-permute-start.13
  32.8 4.3 %shard_map.110 = (bf16[768,1792]{1,0:T(8,128)(2,1)S(1)}, bf16[768,1792]{1,0:T(8,128)(2,1)S(1)}) custom-call(s32[2]{0:T(128)S(1)} %pad_add_fusion.place, bf16[224,512]{1,0:T(8,128)(2,1)S(1)} %get-tuple-element.56.pay.p0, bf16[224,512]{1,0:T(8,128)(2,1)S(1)} %collective-permute-done.4.p2, bf16[224,512]{1,0:T(8,128)(2,1)S(1)} %collective-permute-done.5.p1, ...), custom_call_target="tpu_custom_call" | custom-call | flops 4000000000 | bytes 10000 | tf_op jit(solution)/shard_map/pallas_call | solution.py:355
  37.1 0.3 collective-permute-done.12.m2
  37.4 0.0 collective-permute-done.13.m1
  37.4 0.6 shard_map.111
  37.9 2.2 %collective-permute-start.15 = (bf16[96,256]{1,0:T(8,128)(2,1)S(1)}, bf16[96,256]{1,0:T(8,128)(2,1)S(1)}, u32[]{:S(2)}, u32[]{:S(2)}) collective-permute-start(bf16[96,256]{1,0:T(8,128)(2,1)S(1)} %get-tuple-element.74), channel_id=1, source_target_pairs={{0,4},{1,2},{2,1},{3,7},{4,0},{5,6},{6,5},{7,3},{8,12},{9,10},{10,... | collective-permute-start | bytes 147464 | tf_op jit(solution)/shard_map/ppermute | solution.py:392
  40.1 0.0 collective-permute-start.16
  40.1 0.0 collective-permute-done.7.g2
  40.1 0.0 collective-permute-done.8.g1
  40.1 1.7 %shard_map.112 = (f32[128,1792]{1,0:T(8,128)S(1)}, f32[128,1792]{1,0:T(8,128)S(1)}) custom-call(s32[2]{0:T(128)S(1)} %pad_add_fusion.place, bf16[192,512]{1,0:T(8,128)(2,1)S(1)} %get-tuple-element.62.g0, bf16[192,512]{1,0:T(8,128)(2,1)S(1)} %collective-permute-done.7.g2, bf16[192,512]{1,0:T(8,128)(2,1)S(1)} %collective-permute-done.8.g1, ...), custom_call_target="tpu_custom_call" | custom-call | flops 4000000000 | bytes 10000 | tf_op jit(solution)/shard_map/pallas_call | solution.py:355
  41.8 0.3 collective-permute-start.14
  42.1 1.7 %shard_map.113 = (bf16[128,1792]{1,0:T(8,128)(2,1)S(1)}, bf16[128,1792]{1,0:T(8,128)(2,1)S(1)}) custom-call(s32[2]{0:T(128)S(1)} %pad_add_fusion.place, bf16[192,512]{1,0:T(8,128)(2,1)S(1)} %get-tuple-element.62.g0, bf16[192,512]{1,0:T(8,128)(2,1)S(1)} %collective-permute-done.7.g2, bf16[192,512]{1,0:T(8,128)(2,1)S(1)} %collective-permute-done.8.g1, ...), custom_call_target="tpu_custom_call" | custom-call | flops 100000 | bytes 10000 | tf_op jit(solution)/shard_map/pallas_call | solution.py:355
  43.8 0.4 collective-permute-start.20
  44.2 1.0 %shard_map.114 = (bf16[128,256]{1,0:T(8,128)(2,1)S(1)}, bf16[128,256]{1,0:T(8,128)(2,1)S(1)}) custom-call(s32[2]{0:T(128)S(1)} %pad_add_fusion.place, f32[192,256]{1,0:T(8,128)S(1)} %get-tuple-element.66.late.own, bf16[96,256]{1,0:T(8,128)(2,1)S(1)} %collective-permute-done.12.m2, bf16[96,256]{1,0:T(8,128)(2,1)S(1)} %collective-permute-done.13.m1, ...), custom_call_target="tpu_custom_call" | custom-call | flops 20000000000 | bytes 10000 | tf_op jit(solution)/shard_map/pallas_call | solution.py:355
  45.2 0.3 collective-permute-start.21
  45.5 0.0 collective-permute-done.14.come
  45.5 0.6 shard_map.115
  46.1 4.0 %collective-permute-start.17 = (bf16[32,1792]{1,0:T(8,128)(2,1)S(1)}, bf16[32,1792]{1,0:T(8,128)(2,1)S(1)}, u32[]{:S(2)}, u32[]{:S(2)}) collective-permute-start(bf16[32,1792]{1,0:T(8,128)(2,1)S(1)} %get-tuple-element.80), channel_id=1, source_target_pairs={{0,128},{4,132},{8,136},{12,140},{16,144},{20,148},{24,152},{28,15... | collective-permute-start | bytes 344072 | tf_op jit(solution)/shard_map/ppermute | solution.py:396
  50.1 1.0 %collective-permute-start.18 = (bf16[32,1792]{1,0:T(8,128)(2,1)S(1)}, bf16[32,1792]{1,0:T(8,128)(2,1)S(1)}, u32[]{:S(2)}, u32[]{:S(2)}) collective-permute-start(bf16[32,1792]{1,0:T(8,128)(2,1)S(1)} %get-tuple-element.81), channel_id=1, source_target_pairs={{0,64},{4,68},{8,72},{12,76},{16,80},{20,84},{24,88},{28,92},{32,9... | collective-permute-start | bytes 344072 | tf_op jit(solution)/shard_map/ppermute | solution.py:396
  51.1 0.1 collective-permute-start.19
  51.2 0.7 shard_map.117
  51.9 3.1 %collective-permute-start.22 = (bf16[32,2304]{1,0:T(8,128)(2,1)S(1)}, bf16[32,2304]{1,0:T(8,128)(2,1)S(1)}, u32[]{:S(2)}, u32[]{:S(2)}) collective-permute-start(bf16[32,2304]{1,0:T(8,128)(2,1)S(1)} %get-tuple-element.86), channel_id=1, source_target_pairs={{0,128},{4,132},{8,136},{12,140},{16,144},{20,148},{24,152},{28,15... | collective-permute-start | bytes 442376 | tf_op jit(solution)/shard_map/ppermute | solution.py:396
  55.0 1.0 %collective-permute-start.23 = (bf16[32,2304]{1,0:T(8,128)(2,1)S(1)}, bf16[32,2304]{1,0:T(8,128)(2,1)S(1)}, u32[]{:S(2)}, u32[]{:S(2)}) collective-permute-start(bf16[32,2304]{1,0:T(8,128)(2,1)S(1)} %get-tuple-element.87), channel_id=1, source_target_pairs={{0,64},{4,68},{8,72},{12,76},{16,80},{20,84},{24,88},{28,92},{32,9... | collective-permute-start | bytes 442376 | tf_op jit(solution)/shard_map/ppermute | solution.py:396
  56.0 1.7 %collective-permute-start.24 = (bf16[32,2304]{1,0:T(8,128)(2,1)S(1)}, bf16[32,2304]{1,0:T(8,128)(2,1)S(1)}, u32[]{:S(2)}, u32[]{:S(2)}) collective-permute-start(bf16[32,2304]{1,0:T(8,128)(2,1)S(1)} %get-tuple-element.88), channel_id=1, source_target_pairs={{0,192},{4,196},{8,200},{12,204},{16,208},{20,212},{24,216},{28,22... | collective-permute-start | bytes 442376 | tf_op jit(solution)/shard_map/ppermute | solution.py:396
  57.7 0.0 collective-permute-done.18.a1
  57.7 3.5 %collective-permute-done.19.a3 = bf16[32,1792]{1,0:T(8,128)(2,1)S(1)} collective-permute-done((bf16[32,1792]{1,0:T(8,128)(2,1)S(1)}, bf16[32,1792]{1,0:T(8,128)(2,1)S(1)}, u32[]{:S(2)}, u32[]{:S(2)}) %collective-permute-start.19) | collective-permute-done | bytes 114720 | tf_op jit(solution)/shard_map/ppermute | solution.py:396
  61.2 0.6 shard_map.116.two
  61.8 1.6 %collective-permute-done.23.b1 = bf16[32,2304]{1,0:T(8,128)(2,1)S(1)} collective-permute-done((bf16[32,2304]{1,0:T(8,128)(2,1)S(1)}, bf16[32,2304]{1,0:T(8,128)(2,1)S(1)}, u32[]{:S(2)}, u32[]{:S(2)}) %collective-permute-start.23) | collective-permute-done | bytes 147488 | tf_op jit(solution)/shard_map/ppermute | solution.py:396
  63.4 0.2 collective-permute-done.24.b3
  63.6 0.9 %shard_map.118 = bf16[64,2560]{1,0:T(8,128)(2,1)S(1)} custom-call(s32[2]{0:T(128)S(1)} %pad_add_fusion.place, bf16[32,1792]{1,0:T(8,128)(2,1)S(1)} %shard_map.116.two, bf16[32,2304]{1,0:T(8,128)(2,1)S(1)} %get-tuple-element.85.b0, bf16[32,2304]{1,0:T(8,128)(2,1)S(1)} %collective-permute-done.22.b2, bf16[32,2304]{1,0:T(8,128)(2,1)S(1)} %collective-permute-done.23.b1, ...), custom_call_target="tpu_custom_call" | custom-call | flops 100000 | bytes 10000 | tf_op jit(solution)/shard_map/pallas_call | solution.py:355
  64.5 17.2 %all_to_all.5.refs_0_ = bf16[8,8,2560]{2,1,0:T(8,128)(2,1)S(1)} all-to-all(bf16[8,8,2560]{2,1,0:T(8,128)(2,1)S(1)} %bitcast.5), channel_id=1, replica_groups={{0,8,16,24,32,40,48,56},{4,12,20,28,36,44,52,60},{64,72,80,88,96,104,11..., dimensions={0} | all-to-all | bytes 655360 | tf_op jit(solution)/shard_map/all_to_all | solution.py:576
  81.7 0.9 %shard_map.119 = (bf16[192,256]{1,0:T(8,128)(2,1)}, f32[4,1728]{1,0:T(4,128)}, f32[4,1728]{1,0:T(4,128)}) custom-call(bf16[8,8,2560]{2,1,0:T(8,128)(2,1)S(1)} %all_to_all.5.refs_0_), custom_call_target="tpu_custom_call" | custom-call | flops 100000 | bytes 10000 | tf_op jit(solution)/shard_map/pallas_call | solution.py:355
  (9 shorter events, 0.0 us)
Async XLA Ops:
  2.6 5.2 %copy-start = (bf16[256,6912]{1,0:T(8,128)(2,1)S(1)}, bf16[256,6912]{1,0:T(8,128)(2,1)}, u32[]{:S(2)}) copy-start(bf16[256,6912]{1,0:T(8,128)(2,1)} %weight.2) | copy-start | bytes 10616836
  3.6 24.8 %copy-start.1 = (bf16[256,6912]{1,0:T(8,128)(2,1)S(1)}, bf16[256,6912]{1,0:T(8,128)(2,1)}, u32[]{:S(2)}) copy-start(bf16[256,6912]{1,0:T(8,128)(2,1)} %weight.3) | copy-start | bytes 10616836
  3.6 15.8 %collective-permute-start.4 = (bf16[224,512]{1,0:T(8,128)(2,1)S(1)}, bf16[224,512]{1,0:T(8,128)(2,1)S(1)}, u32[]{:S(2)}, u32[]{:S(2)}) collective-permute-start(bf16[224,512]{1,0:T(8,128)(2,1)S(1)} %get-tuple-element.58), channel_id=1, source_target_pairs={{0,2},{1,3},{2,0},{3,1},{4,6},{5,7},{6,4},{7,5},{8,10},{9,11},{10,... | collective-permute-start | bytes 688136 | tf_op jit(solution)/shard_map/ppermute | solution.py:396
  5.8 13.6 %collective-permute-start.5 = (bf16[224,512]{1,0:T(8,128)(2,1)S(1)}, bf16[224,512]{1,0:T(8,128)(2,1)S(1)}, u32[]{:S(2)}, u32[]{:S(2)}) collective-permute-start(bf16[224,512]{1,0:T(8,128)(2,1)S(1)} %get-tuple-element.59), channel_id=1, source_target_pairs={{0,1},{1,0},{2,3},{3,2},{4,5},{5,4},{6,7},{7,6},{8,9},{9,8},{10,11... | collective-permute-start | bytes 688136 | tf_op jit(solution)/shard_map/ppermute | solution.py:396
  7.2 12.2 %collective-permute-start.6 = (bf16[224,512]{1,0:T(8,128)(2,1)S(1)}, bf16[224,512]{1,0:T(8,128)(2,1)S(1)}, u32[]{:S(2)}, u32[]{:S(2)}) collective-permute-start(bf16[224,512]{1,0:T(8,128)(2,1)S(1)} %get-tuple-element.60), channel_id=1, source_target_pairs={{0,3},{1,2},{2,1},{3,0},{4,7},{5,6},{6,5},{7,4},{8,11},{9,10},{10,... | collective-permute-start | bytes 688136 | tf_op jit(solution)/shard_map/ppermute | solution.py:396
  10.8 7.2 %collective-permute-start = (bf16[96,256]{1,0:T(8,128)(2,1)S(1)}, bf16[96,256]{1,0:T(8,128)(2,1)S(1)}, u32[]{:S(2)}, u32[]{:S(2)}) collective-permute-start(bf16[96,256]{1,0:T(8,128)(2,1)S(1)} %get-tuple-element.49), channel_id=1, source_target_pairs={{0,1},{1,0},{2,3},{3,2},{4,8},{5,9},{6,10},{7,11},{8,4},{9,5},{10,... | collective-permute-start | bytes 147464 | tf_op jit(solution)/shard_map/ppermute | solution.py:392
  13.2 4.9 %collective-permute-start.1 = (bf16[96,256]{1,0:T(8,128)(2,1)S(1)}, bf16[96,256]{1,0:T(8,128)(2,1)S(1)}, u32[]{:S(2)}, u32[]{:S(2)}) collective-permute-start(bf16[96,256]{1,0:T(8,128)(2,1)S(1)} %get-tuple-element.50), channel_id=1, source_target_pairs={{0,4},{1,5},{2,6},{3,7},{4,0},{5,1},{6,2},{7,3},{8,12},{9,13},{10,... | collective-permute-start | bytes 147464 | tf_op jit(solution)/shard_map/ppermute | solution.py:392
  18.6 4.2 %collective-permute-start.2 = (bf16[96,256]{1,0:T(8,128)(2,1)S(1)}, bf16[96,256]{1,0:T(8,128)(2,1)S(1)}, u32[]{:S(2)}, u32[]{:S(2)}) collective-permute-start(bf16[96,256]{1,0:T(8,128)(2,1)S(1)} %get-tuple-element.52), channel_id=1, source_target_pairs={{0,4},{1,2},{2,1},{3,7},{4,0},{5,6},{6,5},{7,3},{8,12},{9,10},{10,... | collective-permute-start | bytes 147464 | tf_op jit(solution)/shard_map/ppermute | solution.py:392
  19.2 4.1 %collective-permute-start.3 = (bf16[96,256]{1,0:T(8,128)(2,1)S(1)}, bf16[96,256]{1,0:T(8,128)(2,1)S(1)}, u32[]{:S(2)}, u32[]{:S(2)}) collective-permute-start(bf16[96,256]{1,0:T(8,128)(2,1)S(1)} %get-tuple-element.53.late), channel_id=1, source_target_pairs={{0,1},{1,0},{2,3},{3,2},{4,5},{5,4},{6,7},{7,6},{8,9},{9,8},{10,11... | collective-permute-start | bytes 147464 | tf_op jit(solution)/shard_map/ppermute | solution.py:392
  20.5 11.0 %collective-permute-start.10 = (bf16[768,256]{1,0:T(8,128)(2,1)S(1)}, bf16[768,256]{1,0:T(8,128)(2,1)S(1)}, u32[]{:S(2)}, u32[]{:S(2)}) collective-permute-start(bf16[768,256]{1,0:T(8,128)(2,1)S(1)} %get-tuple-element.63), channel_id=1, source_target_pairs={{0,1},{1,0},{2,3},{3,2},{4,8},{5,9},{6,10},{7,11},{8,4},{9,5},{10,... | collective-permute-start | bytes 1179656 | tf_op jit(solution)/shard_map/ppermute | solution.py:392
  22.4 10.3 %collective-permute-start.11 = (bf16[768,256]{1,0:T(8,128)(2,1)S(1)}, bf16[768,256]{1,0:T(8,128)(2,1)S(1)}, u32[]{:S(2)}, u32[]{:S(2)}) collective-permute-start(bf16[768,256]{1,0:T(8,128)(2,1)S(1)} %get-tuple-element.64), channel_id=1, source_target_pairs={{0,4},{1,5},{2,6},{3,7},{4,0},{5,1},{6,2},{7,3},{8,12},{9,13},{10,... | collective-permute-start | bytes 1179656 | tf_op jit(solution)/shard_map/ppermute | solution.py:392
  24.2 15.9 %collective-permute-start.7 = (bf16[192,512]{1,0:T(8,128)(2,1)S(1)}, bf16[192,512]{1,0:T(8,128)(2,1)S(1)}, u32[]{:S(2)}, u32[]{:S(2)}) collective-permute-start(bf16[192,512]{1,0:T(8,128)(2,1)S(1)} %get-tuple-element.62.g0), channel_id=1, source_target_pairs={{0,2},{1,3},{2,0},{3,1},{4,6},{5,7},{6,4},{7,5},{8,10},{9,11},{10,... | collective-permute-start | bytes 589832 | tf_op jit(solution)/shard_map/ppermute | solution.py:396
  25.3 14.8 %collective-permute-start.8 = (bf16[192,512]{1,0:T(8,128)(2,1)S(1)}, bf16[192,512]{1,0:T(8,128)(2,1)S(1)}, u32[]{:S(2)}, u32[]{:S(2)}) collective-permute-start(bf16[192,512]{1,0:T(8,128)(2,1)S(1)} %get-tuple-element.62.g0), channel_id=1, source_target_pairs={{0,1},{1,0},{2,3},{3,2},{4,5},{5,4},{6,7},{7,6},{8,9},{9,8},{10,11... | collective-permute-start | bytes 589832 | tf_op jit(solution)/shard_map/ppermute | solution.py:396
  27.9 12.2 %collective-permute-start.9 = (bf16[192,512]{1,0:T(8,128)(2,1)S(1)}, bf16[192,512]{1,0:T(8,128)(2,1)S(1)}, u32[]{:S(2)}, u32[]{:S(2)}) collective-permute-start(bf16[192,512]{1,0:T(8,128)(2,1)S(1)} %get-tuple-element.62.g0), channel_id=1, source_target_pairs={{0,3},{1,2},{2,1},{3,0},{4,7},{5,6},{6,5},{7,4},{8,11},{9,10},{10,... | collective-permute-start | bytes 589832 | tf_op jit(solution)/shard_map/ppermute | solution.py:396
  31.5 5.9 %collective-permute-start.12 = (bf16[96,256]{1,0:T(8,128)(2,1)S(1)}, bf16[96,256]{1,0:T(8,128)(2,1)S(1)}, u32[]{:S(2)}, u32[]{:S(2)}) collective-permute-start(bf16[96,256]{1,0:T(8,128)(2,1)S(1)} %get-tuple-element.69), channel_id=1, source_target_pairs={{0,1},{1,0},{2,3},{3,2},{4,8},{5,9},{6,10},{7,11},{8,4},{9,5},{10,... | collective-permute-start | bytes 147464 | tf_op jit(solution)/shard_map/ppermute | solution.py:392
  32.8 4.6 %collective-permute-start.13 = (bf16[96,256]{1,0:T(8,128)(2,1)S(1)}, bf16[96,256]{1,0:T(8,128)(2,1)S(1)}, u32[]{:S(2)}, u32[]{:S(2)}) collective-permute-start(bf16[96,256]{1,0:T(8,128)(2,1)S(1)} %get-tuple-element.70), channel_id=1, source_target_pairs={{0,4},{1,5},{2,6},{3,7},{4,0},{5,1},{6,2},{7,3},{8,12},{9,13},{10,... | collective-permute-start | bytes 147464 | tf_op jit(solution)/shard_map/ppermute | solution.py:392
  37.9 6.3 %collective-permute-start.15 = (bf16[96,256]{1,0:T(8,128)(2,1)S(1)}, bf16[96,256]{1,0:T(8,128)(2,1)S(1)}, u32[]{:S(2)}, u32[]{:S(2)}) collective-permute-start(bf16[96,256]{1,0:T(8,128)(2,1)S(1)} %get-tuple-element.74), channel_id=1, source_target_pairs={{0,4},{1,2},{2,1},{3,7},{4,0},{5,6},{6,5},{7,3},{8,12},{9,10},{10,... | collective-permute-start | bytes 147464 | tf_op jit(solution)/shard_map/ppermute | solution.py:392
  40.1 4.1 %collective-permute-start.16 = (bf16[96,256]{1,0:T(8,128)(2,1)S(1)}, bf16[96,256]{1,0:T(8,128)(2,1)S(1)}, u32[]{:S(2)}, u32[]{:S(2)}) collective-permute-start(bf16[96,256]{1,0:T(8,128)(2,1)S(1)} %get-tuple-element.71.late), channel_id=1, source_target_pairs={{0,1},{1,0},{2,3},{3,2},{4,5},{5,4},{6,7},{7,6},{8,9},{9,8},{10,11... | collective-permute-start | bytes 147464 | tf_op jit(solution)/shard_map/ppermute | solution.py:392
  41.8 3.7 %collective-permute-start.14 = (f32[128,1792]{1,0:T(8,128)S(1)}, f32[128,1792]{1,0:T(8,128)S(1)}, u32[]{:S(2)}, u32[]{:S(2)}) collective-permute-start(f32[128,1792]{1,0:T(8,128)S(1)} %get-tuple-element.73), channel_id=1, source_target_pairs={{0,4},{4,0},{8,12},{12,8},{16,20},{20,16},{24,28},{28,24},{32,36},... | collective-permute-start | bytes 2752520 | tf_op jit(solution)/shard_map/ppermute | solution.py:396
  43.8 7.3 %collective-permute-start.20 = (bf16[128,1792]{1,0:T(8,128)(2,1)S(1)}, bf16[128,1792]{1,0:T(8,128)(2,1)S(1)}, u32[]{:S(2)}, u32[]{:S(2)}) collective-permute-start(bf16[128,1792]{1,0:T(8,128)(2,1)S(1)} %get-tuple-element.83), channel_id=1, source_target_pairs={{0,4},{4,0},{8,12},{12,8},{16,20},{20,16},{24,28},{28,24},{32,36},... | collective-permute-start | bytes 1376264 | tf_op jit(solution)/shard_map/ppermute | solution.py:396
  45.2 6.0 %collective-permute-start.21 = (bf16[128,256]{1,0:T(8,128)(2,1)S(1)}, bf16[128,256]{1,0:T(8,128)(2,1)S(1)}, u32[]{:S(2)}, u32[]{:S(2)}) collective-permute-start(bf16[128,256]{1,0:T(8,128)(2,1)S(1)} %get-tuple-element.84), channel_id=1, source_target_pairs={{0,4},{4,0},{8,12},{12,8},{16,20},{20,16},{24,28},{28,24},{32,36},... | collective-permute-start | bytes 196616 | tf_op jit(solution)/shard_map/ppermute | solution.py:396
  46.1 9.8 %collective-permute-start.17 = (bf16[32,1792]{1,0:T(8,128)(2,1)S(1)}, bf16[32,1792]{1,0:T(8,128)(2,1)S(1)}, u32[]{:S(2)}, u32[]{:S(2)}) collective-permute-start(bf16[32,1792]{1,0:T(8,128)(2,1)S(1)} %get-tuple-element.80), channel_id=1, source_target_pairs={{0,128},{4,132},{8,136},{12,140},{16,144},{20,148},{24,152},{28,15... | collective-permute-start | bytes 344072 | tf_op jit(solution)/shard_map/ppermute | solution.py:396
  50.1 7.6 %collective-permute-start.18 = (bf16[32,1792]{1,0:T(8,128)(2,1)S(1)}, bf16[32,1792]{1,0:T(8,128)(2,1)S(1)}, u32[]{:S(2)}, u32[]{:S(2)}) collective-permute-start(bf16[32,1792]{1,0:T(8,128)(2,1)S(1)} %get-tuple-element.81), channel_id=1, source_target_pairs={{0,64},{4,68},{8,72},{12,76},{16,80},{20,84},{24,88},{28,92},{32,9... | collective-permute-start | bytes 344072 | tf_op jit(solution)/shard_map/ppermute | solution.py:396
  51.1 10.1 %collective-permute-start.19 = (bf16[32,1792]{1,0:T(8,128)(2,1)S(1)}, bf16[32,1792]{1,0:T(8,128)(2,1)S(1)}, u32[]{:S(2)}, u32[]{:S(2)}) collective-permute-start(bf16[32,1792]{1,0:T(8,128)(2,1)S(1)} %get-tuple-element.82), channel_id=1, source_target_pairs={{0,192},{4,196},{8,200},{12,204},{16,208},{20,212},{24,216},{28,22... | collective-permute-start | bytes 344072 | tf_op jit(solution)/shard_map/ppermute | solution.py:396
  51.9 9.9 %collective-permute-start.22 = (bf16[32,2304]{1,0:T(8,128)(2,1)S(1)}, bf16[32,2304]{1,0:T(8,128)(2,1)S(1)}, u32[]{:S(2)}, u32[]{:S(2)}) collective-permute-start(bf16[32,2304]{1,0:T(8,128)(2,1)S(1)} %get-tuple-element.86), channel_id=1, source_target_pairs={{0,128},{4,132},{8,136},{12,140},{16,144},{20,148},{24,152},{28,15... | collective-permute-start | bytes 442376 | tf_op jit(solution)/shard_map/ppermute | solution.py:396
  55.0 8.4 %collective-permute-start.23 = (bf16[32,2304]{1,0:T(8,128)(2,1)S(1)}, bf16[32,2304]{1,0:T(8,128)(2,1)S(1)}, u32[]{:S(2)}, u32[]{:S(2)}) collective-permute-start(bf16[32,2304]{1,0:T(8,128)(2,1)S(1)} %get-tuple-element.87), channel_id=1, source_target_pairs={{0,64},{4,68},{8,72},{12,76},{16,80},{20,84},{24,88},{28,92},{32,9... | collective-permute-start | bytes 442376 | tf_op jit(solution)/shard_map/ppermute | solution.py:396
  56.0 7.6 %collective-permute-start.24 = (bf16[32,2304]{1,0:T(8,128)(2,1)S(1)}, bf16[32,2304]{1,0:T(8,128)(2,1)S(1)}, u32[]{:S(2)}, u32[]{:S(2)}) collective-permute-start(bf16[32,2304]{1,0:T(8,128)(2,1)S(1)} %get-tuple-element.88), channel_id=1, source_target_pairs={{0,192},{4,196},{8,200},{12,204},{16,208},{20,212},{24,216},{28,22... | collective-permute-start | bytes 442376 | tf_op jit(solution)/shard_map/ppermute | solution.py:396

commit v16 on v14

--- a/solution.py
+++ b/solution.py
@@ -183,15 +183,12 @@
     send[...] = chosen[128:256, :]
 
 
-def pick_kernel(place, p0, p2, p1, p3, late, o2, o1, loc, picked, ids):
+def pick_kernel(place, p0, p2, p1, p3, late, o2, o1, loc, picked):
     column = place[1]
-    pays = (p0, p1, p2, p3)
-    for turn, pay in enumerate(pays):
-        ids[turn : turn + 1, :] = pay[S + 16 : S + 32, 0:C].astype(F32)[15:16, :] - 1.0
-    slots = jnp.transpose(ids[...])[:, 0:8].astype(jnp.int32)
-    for turn, pay in enumerate(pays):
-        chosen = onehot(iota((8 * HB, S), 1) == slots[:, turn : turn + 1])
-        picked[column ^ turn] = mm(chosen, pay[0:S, 0 : 2 * C]).astype(BF)
+    for turn, pay in enumerate((p0, p1, p2, p3)):
+        halo_row = pay[S + 16 : S + 32, 0:C].astype(F32)[15:16, :].astype(jnp.int32) - 1
+        rows = mm_t(halo_matrix(halo_row), pay[0:S, 0 : 2 * C])
+        picked[column ^ turn] = rows.astype(BF)
     even = place[0] % 2 == 0
     up = pl.multiple_of(jnp.where(even, 160, 0), 32)
     down = pl.multiple_of(jnp.where(even, 0, 160), 32)
@@ -287,14 +284,14 @@
         out[:, 8 * C : 9 * C] = jnp.where(first, other, mine)
 
 
-def line_two_kernel(place, a0, a2, a1, a3, out):
+def line_two_kernel(place, a0, a1, a3, a2, out):
     total = a0[...].astype(F32)
     for part in (a1, a2, a3):
         total = total + part[...].astype(F32)
     out[...] = total.astype(BF)
 
 
-def line_one_kernel(place, two, b0, b2, b1, b3, out):
+def line_one_kernel(place, two, b0, b1, b3, b2, out):
     line = place[0] // 16
     to, at = iota((64, 64), 0), iota((64, 64), 1)
     order = onehot(at == 32 * ((to % 8) // 4) + 4 * (to // 8) + to % 4)
@@ -452,7 +449,7 @@
         place,
         *pays,
         passed,
-        scratch=[pltpu.VMEM((4, 8 * HB, 2 * C), BF), pltpu.VMEM((128, C), F32)],
+        scratch=[pltpu.VMEM((4, 8 * HB, 2 * C), BF)],
         late=1,
     )
     r2, r1 = halo_lines(o2, o1)
@@ -536,7 +533,7 @@
     rows_come = cross(rows_send, "gx", 1)
 
     def lines(chunks):
-        return [chunks[0]] + [cross(chunks[d], "gx", 16 * d) for d in (2, 1, 3)]
+        return [chunks[0]] + [cross(chunks[d], "gx", 16 * d) for d in (1, 3, 2)]
 
     two = call(
         merge_two_kernel,

time: 82.9 us -> 82.4 us (level)
  waiting for transfers between devices: 11.1 us -> 12.8 us
  starting transfers between devices: 29 us -> 27.7 us
    ppermute x15, waiting for transfers between devices: 5.31 us -> 6.83 us  [cross(): lax.ppermute(value, axis, [(n, n ^ mask) for n in range(lax.axis_size(axi...]
    ppermute x15, starting transfers between devices: 20.2 us -> 19.1 us  [cross(): lax.ppermute(value, axis, [(n, n ^ mask) for n in range(lax.axis_size(axi...]
  transfers between devices with their start and end apart: 25 -> 25, of which waited for: 7 -> 9; matrix products, arithmetic and copies ran while one was open for 0% -> 0% of each run, Pallas kernels for 24% -> 24%
where the time goes in v16:
time: 82.4 us; the launch traced here: 82 us
  starting transfers between devices  27.7 us (34%)
  Pallas kernels  23.8 us (29%)
  blocking collectives  16.8 us (20%)
  waiting for transfers between devices  12.8 us (16%)
    pallas_call x16, Pallas kernels, call(): pl.pallas_call(kernel, out_shape=outs, in_specs=specs, out_specs=jax.tree...  23.8 us
    ppermute x15, starting transfers between devices, cross(): lax.ppermute(value, axis, [(n, n ^ mask) for n in range(lax.axis_size(axi...  19.1 us
    all_to_all x1, blocking collectives, body(): lax.all_to_all(summed.reshape(8, 8, 10 * C), 'gx', split_axis=0, concat_a...  16.8 us
    ppermute x10, starting transfers between devices, swap(): return lax.ppermute(value, ('gx', 'gy'), pairs)  8.57 us
    ppermute x15, waiting for transfers between devices, cross(): lax.ppermute(value, axis, [(n, n ^ mask) for n in range(lax.axis_size(axi...  6.83 us
    ppermute x10, waiting for transfers between devices, swap(): return lax.ppermute(value, ('gx', 'gy'), pairs)  6.01 us
  transfers between devices with their start and end apart: 25, of which 9 were waited for; matrix products, arithmetic and copies ran while one was open for 0% of the time, Pallas kernels for 24%

profile of v16, /device:TPU:2, one launch (start us, length us, event | category | flops | bytes accessed | tf_op | source)
XLA Modules:
  0.0 82.0 jit_solution(17411802408453655702)
XLA Ops:
  0.6 0.1 pad_add_fusion.place
  0.7 2.3 %shard_map.103 = (bf16[224,512]{1,0:T(8,128)(2,1)S(1)}, bf16[224,512]{1,0:T(8,128)(2,1)S(1)}, bf16[224,512]{1,0:T(8,128)(2,1)S(1)}, bf16[224,512]{1,0:T(8,128)(2...) custom-call(s32[2]{0:T(128)S(1)} %pad_add_fusion.place, ...), custom_call_target="tpu_custom_call" | custom-call | flops 4000000000 | bytes 10000 | tf_op jit(solution)/shard_map/pallas_call | solution.py:345
  3.0 0.0 copy-start.1
  3.0 2.2 %collective-permute-start.4 = (bf16[224,512]{1,0:T(8,128)(2,1)S(1)}, bf16[224,512]{1,0:T(8,128)(2,1)S(1)}, u32[]{:S(2)}, u32[]{:S(2)}) collective-permute-start(bf16[224,512]{1,0:T(8,128)(2,1)S(1)} %get-tuple-element.56), channel_id=1, source_target_pairs={{0,2},{1,3},{2,0},{3,1},{4,6},{5,7},{6,4},{7,5},{8,10},{9,11},{10,... | collective-permute-start | bytes 688136 | tf_op jit(solution)/shard_map/ppermute | solution.py:386
  5.3 1.4 %collective-permute-start.5 = (bf16[224,512]{1,0:T(8,128)(2,1)S(1)}, bf16[224,512]{1,0:T(8,128)(2,1)S(1)}, u32[]{:S(2)}, u32[]{:S(2)}) collective-permute-start(bf16[224,512]{1,0:T(8,128)(2,1)S(1)} %get-tuple-element.57), channel_id=1, source_target_pairs={{0,1},{1,0},{2,3},{3,2},{4,5},{5,4},{6,7},{7,6},{8,9},{9,8},{10,11... | collective-permute-start | bytes 688136 | tf_op jit(solution)/shard_map/ppermute | solution.py:386
  6.7 0.5 collective-permute-start.6
  7.2 3.0 %shard_map.104 = (f32[192,256]{1,0:T(8,128)S(1)}, bf16[96,256]{1,0:T(8,128)(2,1)S(1)}, bf16[96,256]{1,0:T(8,128)(2,1)S(1)}, bf16[64,256]{1,0:T(8,128)(2,1)S(1)}) custom-call(s32[2]{0:T(128)S(1)} %pad_add_fusion.place, f32[32,256]{1,0:T(8,128)S(1)} %get-tuple-element.45.nbt, bf16[192,256]{1,0:T(8,128)(2,1)S(1)} %get-tuple-element.46.grad, ...), custom_call_target="tpu_custom_call" | custom-call | flops 100000 | bytes 10000 | tf_op jit(solution)/shard_map/pallas_call | solution.py:345
  10.3 2.4 %collective-permute-start = (bf16[96,256]{1,0:T(8,128)(2,1)S(1)}, bf16[96,256]{1,0:T(8,128)(2,1)S(1)}, u32[]{:S(2)}, u32[]{:S(2)}) collective-permute-start(bf16[96,256]{1,0:T(8,128)(2,1)S(1)} %get-tuple-element.48), channel_id=1, source_target_pairs={{0,1},{1,0},{2,3},{3,2},{4,8},{5,9},{6,10},{7,11},{8,4},{9,5},{10,... | collective-permute-start | bytes 147464 | tf_op jit(solution)/shard_map/ppermute | solution.py:382
  12.6 4.9 %collective-permute-done.m2 = bf16[96,256]{1,0:T(8,128)(2,1)S(1)} collective-permute-done((bf16[96,256]{1,0:T(8,128)(2,1)S(1)}, bf16[96,256]{1,0:T(8,128)(2,1)S(1)}, u32[]{:S(2)}, u32[]{:S(2)}) %collective-permute-start) | collective-permute-done | bytes 49184 | tf_op jit(solution)/shard_map/ppermute | solution.py:382
  17.5 0.0 collective-permute-done.1.m1
  17.5 0.6 shard_map.105
  18.1 0.6 collective-permute-start.2
  18.7 0.2 collective-permute-start.3
  18.8 0.0 collective-permute-done.4.p2
  18.8 0.0 collective-permute-done.5.p1
  18.8 0.0 collective-permute-done.6.p3
  18.9 1.1 %shard_map.106 = (bf16[768,256]{1,0:T(8,128)(2,1)S(1)}, bf16[768,256]{1,0:T(8,128)(2,1)S(1)}, bf16[4,64,512]{2,1,0:T(8,128)(2,1)S(1)}) custom-call(s32[2]{0:T(128)S(1)} %pad_add_fusion.place, bf16[224,512]{1,0:T(8,128)(2,1)S(1)} %get-tuple-element.55.p0, bf16[224,512]{1,0:T(8,128)(2,1)S(1)} %collective-permute-done.4.p2, ...), custom_call_target="tpu_custom_call" | custom-call | flops 100000 | bytes 10000 | tf_op jit(solution)/shard_map/pallas_call | solution.py:345
  19.9 2.0 %collective-permute-start.10 = (bf16[768,256]{1,0:T(8,128)(2,1)S(1)}, bf16[768,256]{1,0:T(8,128)(2,1)S(1)}, u32[]{:S(2)}, u32[]{:S(2)}) collective-permute-start(bf16[768,256]{1,0:T(8,128)(2,1)S(1)} %get-tuple-element.61), channel_id=1, source_target_pairs={{0,1},{1,0},{2,3},{3,2},{4,8},{5,9},{6,10},{7,11},{8,4},{9,5},{10,... | collective-permute-start | bytes 1179656 | tf_op jit(solution)/shard_map/ppermute | solution.py:382
  21.9 0.3 collective-permute-done.2.n2
  22.2 0.5 collective-permute-done.3.n1
  22.8 0.9 %shard_map.107 = (bf16[192,256]{1,0:T(8,128)(2,1)S(1)}, bf16[192,512]{1,0:T(8,128)(2,1)S(1)}) custom-call(s32[2]{0:T(128)S(1)} %pad_add_fusion.place, f32[192,256]{1,0:T(8,128)S(1)} %get-tuple-element.47.late.own, bf16[96,256]{1,0:T(8,128)(2,1)S(1)} %collective-permute-done.m2, bf16[96,256]{1,0:T(8,128)(2,1)S(1)} %collective-permute-done.1.m1, ...), custom_call_target="tpu_custom_call" | custom-call | flops 100000 | bytes 10000 | tf_op jit(solution)/shard_map/pallas_call | solution.py:345
  23.7 1.0 %collective-permute-start.7 = (bf16[192,512]{1,0:T(8,128)(2,1)S(1)}, bf16[192,512]{1,0:T(8,128)(2,1)S(1)}, u32[]{:S(2)}, u32[]{:S(2)}) collective-permute-start(bf16[192,512]{1,0:T(8,128)(2,1)S(1)} %get-tuple-element.60.g0), channel_id=1, source_target_pairs={{0,2},{1,3},{2,0},{3,1},{4,6},{5,7},{6,4},{7,5},{8,10},{9,11},{10,... | collective-permute-start | bytes 589832 | tf_op jit(solution)/shard_map/ppermute | solution.py:386
  24.7 2.6 %collective-permute-start.8 = (bf16[192,512]{1,0:T(8,128)(2,1)S(1)}, bf16[192,512]{1,0:T(8,128)(2,1)S(1)}, u32[]{:S(2)}, u32[]{:S(2)}) collective-permute-start(bf16[192,512]{1,0:T(8,128)(2,1)S(1)} %get-tuple-element.60.g0), channel_id=1, source_target_pairs={{0,1},{1,0},{2,3},{3,2},{4,5},{5,4},{6,7},{7,6},{8,9},{9,8},{10,11... | collective-permute-start | bytes 589832 | tf_op jit(solution)/shard_map/ppermute | solution.py:386
  27.3 0.5 collective-permute-start.9
  27.9 3.0 %shard_map.108 = (f32[192,256]{1,0:T(8,128)S(1)}, bf16[96,256]{1,0:T(8,128)(2,1)S(1)}, bf16[96,256]{1,0:T(8,128)(2,1)S(1)}, bf16[64,256]{1,0:T(8,128)(2,1)S(1)}) custom-call(s32[2]{0:T(128)S(1)} %pad_add_fusion.place, f32[32,256]{1,0:T(8,128)S(1)} %get-tuple-element.45.nbt, bf16[192,256]{1,0:T(8,128)(2,1)S(1)} %get-tuple-element.63.grad, ...), custom_call_target="tpu_custom_call" | custom-call | flops 4000000000 | bytes 10000 | tf_op jit(solution)/shard_map/pallas_call | solution.py:345
  30.9 0.0 collective-permute-done.10.r2
  30.9 1.3 %collective-permute-start.12 = (bf16[96,256]{1,0:T(8,128)(2,1)S(1)}, bf16[96,256]{1,0:T(8,128)(2,1)S(1)}, u32[]{:S(2)}, u32[]{:S(2)}) collective-permute-start(bf16[96,256]{1,0:T(8,128)(2,1)S(1)} %get-tuple-element.67), channel_id=1, source_target_pairs={{0,1},{1,0},{2,3},{3,2},{4,8},{5,9},{6,10},{7,11},{8,4},{9,5},{10,... | collective-permute-start | bytes 147464 | tf_op jit(solution)/shard_map/ppermute | solution.py:382
  32.2 0.0 collective-permute-done.11.r1
  32.2 0.0 collective-permute-start.13
  32.2 4.3 %shard_map.109 = (bf16[768,1792]{1,0:T(8,128)(2,1)S(1)}, bf16[768,1792]{1,0:T(8,128)(2,1)S(1)}) custom-call(s32[2]{0:T(128)S(1)} %pad_add_fusion.place, bf16[224,512]{1,0:T(8,128)(2,1)S(1)} %get-tuple-element.55.p0, bf16[224,512]{1,0:T(8,128)(2,1)S(1)} %collective-permute-done.4.p2, bf16[224,512]{1,0:T(8,128)(2,1)S(1)} %collective-permute-done.5.p1, ...), custom_call_target="tpu_custom_call" | custom-call | flops 4000000000 | bytes 10000 | tf_op jit(solution)/shard_map/pallas_call | solution.py:345
  36.5 0.3 collective-permute-done.12.m2
  36.8 0.0 collective-permute-done.13.m1
  36.8 0.6 shard_map.110
  37.4 2.2 %collective-permute-start.15 = (bf16[96,256]{1,0:T(8,128)(2,1)S(1)}, bf16[96,256]{1,0:T(8,128)(2,1)S(1)}, u32[]{:S(2)}, u32[]{:S(2)}) collective-permute-start(bf16[96,256]{1,0:T(8,128)(2,1)S(1)} %get-tuple-element.72), channel_id=1, source_target_pairs={{0,4},{1,2},{2,1},{3,7},{4,0},{5,6},{6,5},{7,3},{8,12},{9,10},{10,... | collective-permute-start | bytes 147464 | tf_op jit(solution)/shard_map/ppermute | solution.py:382
  39.5 0.0 collective-permute-start.16
  39.5 0.0 collective-permute-done.7.g2
  39.6 0.0 collective-permute-done.8.g1
  39.6 1.7 %shard_map.111 = (f32[128,1792]{1,0:T(8,128)S(1)}, f32[128,1792]{1,0:T(8,128)S(1)}) custom-call(s32[2]{0:T(128)S(1)} %pad_add_fusion.place, bf16[192,512]{1,0:T(8,128)(2,1)S(1)} %get-tuple-element.60.g0, bf16[192,512]{1,0:T(8,128)(2,1)S(1)} %collective-permute-done.7.g2, bf16[192,512]{1,0:T(8,128)(2,1)S(1)} %collective-permute-done.8.g1, ...), custom_call_target="tpu_custom_call" | custom-call | flops 4000000000 | bytes 10000 | tf_op jit(solution)/shard_map/pallas_call | solution.py:345
  41.3 0.3 collective-permute-start.14
  41.6 1.7 %shard_map.112 = (bf16[128,1792]{1,0:T(8,128)(2,1)S(1)}, bf16[128,1792]{1,0:T(8,128)(2,1)S(1)}) custom-call(s32[2]{0:T(128)S(1)} %pad_add_fusion.place, bf16[192,512]{1,0:T(8,128)(2,1)S(1)} %get-tuple-element.60.g0, bf16[192,512]{1,0:T(8,128)(2,1)S(1)} %collective-permute-done.7.g2, bf16[192,512]{1,0:T(8,128)(2,1)S(1)} %collective-permute-done.8.g1, ...), custom_call_target="tpu_custom_call" | custom-call | flops 100000 | bytes 10000 | tf_op jit(solution)/shard_map/pallas_call | solution.py:345
  43.3 0.4 collective-permute-start.20
  43.7 0.0 collective-permute-done.15.n2
  43.7 0.0 collective-permute-done.16.n1
  43.7 1.0 %shard_map.113 = (bf16[128,256]{1,0:T(8,128)(2,1)S(1)}, bf16[128,256]{1,0:T(8,128)(2,1)S(1)}) custom-call(s32[2]{0:T(128)S(1)} %pad_add_fusion.place, f32[192,256]{1,0:T(8,128)S(1)} %get-tuple-element.64.late.own, bf16[96,256]{1,0:T(8,128)(2,1)S(1)} %collective-permute-done.12.m2, bf16[96,256]{1,0:T(8,128)(2,1)S(1)} %collective-permute-done.13.m1, ...), custom_call_target="tpu_custom_call" | custom-call | flops 20000000000 | bytes 10000 | tf_op jit(solution)/shard_map/pallas_call | solution.py:345
  44.6 0.3 collective-permute-start.21
  45.0 0.0 collective-permute-done.14.come
  45.0 0.6 shard_map.114
  45.6 2.3 %collective-permute-start.17 = (bf16[32,1792]{1,0:T(8,128)(2,1)S(1)}, bf16[32,1792]{1,0:T(8,128)(2,1)S(1)}, u32[]{:S(2)}, u32[]{:S(2)}) collective-permute-start(bf16[32,1792]{1,0:T(8,128)(2,1)S(1)} %get-tuple-element.78), channel_id=1, source_target_pairs={{0,64},{4,68},{8,72},{12,76},{16,80},{20,84},{24,88},{28,92},{32,9... | collective-permute-start | bytes 344072 | tf_op jit(solution)/shard_map/ppermute | solution.py:386
  47.9 2.2 %collective-permute-start.18 = (bf16[32,1792]{1,0:T(8,128)(2,1)S(1)}, bf16[32,1792]{1,0:T(8,128)(2,1)S(1)}, u32[]{:S(2)}, u32[]{:S(2)}) collective-permute-start(bf16[32,1792]{1,0:T(8,128)(2,1)S(1)} %get-tuple-element.79), channel_id=1, source_target_pairs={{0,192},{4,196},{8,200},{12,204},{16,208},{20,212},{24,216},{28,22... | collective-permute-start | bytes 344072 | tf_op jit(solution)/shard_map/ppermute | solution.py:386
  50.1 1.0 %collective-permute-start.19 = (bf16[32,1792]{1,0:T(8,128)(2,1)S(1)}, bf16[32,1792]{1,0:T(8,128)(2,1)S(1)}, u32[]{:S(2)}, u32[]{:S(2)}) collective-permute-start(bf16[32,1792]{1,0:T(8,128)(2,1)S(1)} %get-tuple-element.80), channel_id=1, source_target_pairs={{0,128},{4,132},{8,136},{12,140},{16,144},{20,148},{24,152},{28,15... | collective-permute-start | bytes 344072 | tf_op jit(solution)/shard_map/ppermute | solution.py:386
  51.2 0.0 collective-permute-done.21.rs
  51.2 0.7 shard_map.116
  51.8 1.0 %collective-permute-start.22 = (bf16[32,2304]{1,0:T(8,128)(2,1)S(1)}, bf16[32,2304]{1,0:T(8,128)(2,1)S(1)}, u32[]{:S(2)}, u32[]{:S(2)}) collective-permute-start(bf16[32,2304]{1,0:T(8,128)(2,1)S(1)} %get-tuple-element.84), channel_id=1, source_target_pairs={{0,64},{4,68},{8,72},{12,76},{16,80},{20,84},{24,88},{28,92},{32,9... | collective-permute-start | bytes 442376 | tf_op jit(solution)/shard_map/ppermute | solution.py:386
  52.8 2.2 %collective-permute-start.23 = (bf16[32,2304]{1,0:T(8,128)(2,1)S(1)}, bf16[32,2304]{1,0:T(8,128)(2,1)S(1)}, u32[]{:S(2)}, u32[]{:S(2)}) collective-permute-start(bf16[32,2304]{1,0:T(8,128)(2,1)S(1)} %get-tuple-element.85), channel_id=1, source_target_pairs={{0,192},{4,196},{8,200},{12,204},{16,208},{20,212},{24,216},{28,22... | collective-permute-start | bytes 442376 | tf_op jit(solution)/shard_map/ppermute | solution.py:386
  55.0 1.0 %collective-permute-start.24 = (bf16[32,2304]{1,0:T(8,128)(2,1)S(1)}, bf16[32,2304]{1,0:T(8,128)(2,1)S(1)}, u32[]{:S(2)}, u32[]{:S(2)}) collective-permute-start(bf16[32,2304]{1,0:T(8,128)(2,1)S(1)} %get-tuple-element.86), channel_id=1, source_target_pairs={{0,128},{4,132},{8,136},{12,140},{16,144},{20,148},{24,152},{28,15... | collective-permute-start | bytes 442376 | tf_op jit(solution)/shard_map/ppermute | solution.py:386
  56.0 0.1 collective-permute-done.18.a3
  56.1 1.6 %collective-permute-done.19.a2 = bf16[32,1792]{1,0:T(8,128)(2,1)S(1)} collective-permute-done((bf16[32,1792]{1,0:T(8,128)(2,1)S(1)}, bf16[32,1792]{1,0:T(8,128)(2,1)S(1)}, u32[]{:S(2)}, u32[]{:S(2)}) %collective-permute-start.19) | collective-permute-done | bytes 114720 | tf_op jit(solution)/shard_map/ppermute | solution.py:386
  57.7 0.6 shard_map.115.two
  58.3 0.5 collective-permute-done.22.b1
  58.8 2.9 %collective-permute-done.23.b3 = bf16[32,2304]{1,0:T(8,128)(2,1)S(1)} collective-permute-done((bf16[32,2304]{1,0:T(8,128)(2,1)S(1)}, bf16[32,2304]{1,0:T(8,128)(2,1)S(1)}, u32[]{:S(2)}, u32[]{:S(2)}) %collective-permute-start.23) | collective-permute-done | bytes 147488 | tf_op jit(solution)/shard_map/ppermute | solution.py:386
  61.7 1.7 %collective-permute-done.24.b2 = bf16[32,2304]{1,0:T(8,128)(2,1)S(1)} collective-permute-done((bf16[32,2304]{1,0:T(8,128)(2,1)S(1)}, bf16[32,2304]{1,0:T(8,128)(2,1)S(1)}, u32[]{:S(2)}, u32[]{:S(2)}) %collective-permute-start.24) | collective-permute-done | bytes 147488 | tf_op jit(solution)/shard_map/ppermute | solution.py:386
  63.4 0.9 %shard_map.117 = bf16[64,2560]{1,0:T(8,128)(2,1)S(1)} custom-call(s32[2]{0:T(128)S(1)} %pad_add_fusion.place, bf16[32,1792]{1,0:T(8,128)(2,1)S(1)} %shard_map.115.two, bf16[32,2304]{1,0:T(8,128)(2,1)S(1)} %get-tuple-element.83.b0, bf16[32,2304]{1,0:T(8,128)(2,1)S(1)} %collective-permute-done.22.b1, bf16[32,2304]{1,0:T(8,128)(2,1)S(1)} %collective-permute-done.23.b3, ...), custom_call_target="tpu_custom_call" | custom-call | flops 100000 | bytes 10000 | tf_op jit(solution)/shard_map/pallas_call | solution.py:345
  64.4 16.8 %all_to_all.5.refs_0_ = bf16[8,8,2560]{2,1,0:T(8,128)(2,1)S(1)} all-to-all(bf16[8,8,2560]{2,1,0:T(8,128)(2,1)S(1)} %bitcast.5), channel_id=1, replica_groups={{0,8,16,24,32,40,48,56},{4,12,20,28,36,44,52,60},{64,72,80,88,96,104,11..., dimensions={0} | all-to-all | bytes 655360 | tf_op jit(solution)/shard_map/all_to_all | solution.py:564
  81.1 0.9 %shard_map.118 = (bf16[192,256]{1,0:T(8,128)(2,1)}, f32[4,1728]{1,0:T(4,128)}, f32[4,1728]{1,0:T(4,128)}) custom-call(bf16[8,8,2560]{2,1,0:T(8,128)(2,1)S(1)} %all_to_all.5.refs_0_), custom_call_target="tpu_custom_call" | custom-call | flops 100000 | bytes 10000 | tf_op jit(solution)/shard_map/pallas_call | solution.py:345
  (8 shorter events, 0.0 us)
Async XLA Ops:
  0.7 6.5 %copy-start = (bf16[256,6912]{1,0:T(8,128)(2,1)S(1)}, bf16[256,6912]{1,0:T(8,128)(2,1)}, u32[]{:S(2)}) copy-start(bf16[256,6912]{1,0:T(8,128)(2,1)} %weight.2) | copy-start | bytes 10616836
  3.0 24.8 %copy-start.1 = (bf16[256,6912]{1,0:T(8,128)(2,1)S(1)}, bf16[256,6912]{1,0:T(8,128)(2,1)}, u32[]{:S(2)}) copy-start(bf16[256,6912]{1,0:T(8,128)(2,1)} %weight.3) | copy-start | bytes 10616836
  3.0 15.8 %collective-permute-start.4 = (bf16[224,512]{1,0:T(8,128)(2,1)S(1)}, bf16[224,512]{1,0:T(8,128)(2,1)S(1)}, u32[]{:S(2)}, u32[]{:S(2)}) collective-permute-start(bf16[224,512]{1,0:T(8,128)(2,1)S(1)} %get-tuple-element.56), channel_id=1, source_target_pairs={{0,2},{1,3},{2,0},{3,1},{4,6},{5,7},{6,4},{7,5},{8,10},{9,11},{10,... | collective-permute-start | bytes 688136 | tf_op jit(solution)/shard_map/ppermute | solution.py:386
  5.3 13.6 %collective-permute-start.5 = (bf16[224,512]{1,0:T(8,128)(2,1)S(1)}, bf16[224,512]{1,0:T(8,128)(2,1)S(1)}, u32[]{:S(2)}, u32[]{:S(2)}) collective-permute-start(bf16[224,512]{1,0:T(8,128)(2,1)S(1)} %get-tuple-element.57), channel_id=1, source_target_pairs={{0,1},{1,0},{2,3},{3,2},{4,5},{5,4},{6,7},{7,6},{8,9},{9,8},{10,11... | collective-permute-start | bytes 688136 | tf_op jit(solution)/shard_map/ppermute | solution.py:386
  6.7 12.2 %collective-permute-start.6 = (bf16[224,512]{1,0:T(8,128)(2,1)S(1)}, bf16[224,512]{1,0:T(8,128)(2,1)S(1)}, u32[]{:S(2)}, u32[]{:S(2)}) collective-permute-start(bf16[224,512]{1,0:T(8,128)(2,1)S(1)} %get-tuple-element.58), channel_id=1, source_target_pairs={{0,3},{1,2},{2,1},{3,0},{4,7},{5,6},{6,5},{7,4},{8,11},{9,10},{10,... | collective-permute-start | bytes 688136 | tf_op jit(solution)/shard_map/ppermute | solution.py:386
  10.3 7.2 %collective-permute-start = (bf16[96,256]{1,0:T(8,128)(2,1)S(1)}, bf16[96,256]{1,0:T(8,128)(2,1)S(1)}, u32[]{:S(2)}, u32[]{:S(2)}) collective-permute-start(bf16[96,256]{1,0:T(8,128)(2,1)S(1)} %get-tuple-element.48), channel_id=1, source_target_pairs={{0,1},{1,0},{2,3},{3,2},{4,8},{5,9},{6,10},{7,11},{8,4},{9,5},{10,... | collective-permute-start | bytes 147464 | tf_op jit(solution)/shard_map/ppermute | solution.py:382
  12.6 4.9 %collective-permute-start.1 = (bf16[96,256]{1,0:T(8,128)(2,1)S(1)}, bf16[96,256]{1,0:T(8,128)(2,1)S(1)}, u32[]{:S(2)}, u32[]{:S(2)}) collective-permute-start(bf16[96,256]{1,0:T(8,128)(2,1)S(1)} %get-tuple-element.49), channel_id=1, source_target_pairs={{0,4},{1,5},{2,6},{3,7},{4,0},{5,1},{6,2},{7,3},{8,12},{9,13},{10,... | collective-permute-start | bytes 147464 | tf_op jit(solution)/shard_map/ppermute | solution.py:382
  18.1 4.2 %collective-permute-start.2 = (bf16[96,256]{1,0:T(8,128)(2,1)S(1)}, bf16[96,256]{1,0:T(8,128)(2,1)S(1)}, u32[]{:S(2)}, u32[]{:S(2)}) collective-permute-start(bf16[96,256]{1,0:T(8,128)(2,1)S(1)} %get-tuple-element.51), channel_id=1, source_target_pairs={{0,4},{1,2},{2,1},{3,7},{4,0},{5,6},{6,5},{7,3},{8,12},{9,10},{10,... | collective-permute-start | bytes 147464 | tf_op jit(solution)/shard_map/ppermute | solution.py:382
  18.7 4.1 %collective-permute-start.3 = (bf16[96,256]{1,0:T(8,128)(2,1)S(1)}, bf16[96,256]{1,0:T(8,128)(2,1)S(1)}, u32[]{:S(2)}, u32[]{:S(2)}) collective-permute-start(bf16[96,256]{1,0:T(8,128)(2,1)S(1)} %get-tuple-element.52.late), channel_id=1, source_target_pairs={{0,1},{1,0},{2,3},{3,2},{4,5},{5,4},{6,7},{7,6},{8,9},{9,8},{10,11... | collective-permute-start | bytes 147464 | tf_op jit(solution)/shard_map/ppermute | solution.py:382
  19.9 11.0 %collective-permute-start.10 = (bf16[768,256]{1,0:T(8,128)(2,1)S(1)}, bf16[768,256]{1,0:T(8,128)(2,1)S(1)}, u32[]{:S(2)}, u32[]{:S(2)}) collective-permute-start(bf16[768,256]{1,0:T(8,128)(2,1)S(1)} %get-tuple-element.61), channel_id=1, source_target_pairs={{0,1},{1,0},{2,3},{3,2},{4,8},{5,9},{6,10},{7,11},{8,4},{9,5},{10,... | collective-permute-start | bytes 1179656 | tf_op jit(solution)/shard_map/ppermute | solution.py:382
  21.9 10.3 %collective-permute-start.11 = (bf16[768,256]{1,0:T(8,128)(2,1)S(1)}, bf16[768,256]{1,0:T(8,128)(2,1)S(1)}, u32[]{:S(2)}, u32[]{:S(2)}) collective-permute-start(bf16[768,256]{1,0:T(8,128)(2,1)S(1)} %get-tuple-element.62), channel_id=1, source_target_pairs={{0,4},{1,5},{2,6},{3,7},{4,0},{5,1},{6,2},{7,3},{8,12},{9,13},{10,... | collective-permute-start | bytes 1179656 | tf_op jit(solution)/shard_map/ppermute | solution.py:382
  23.7 15.9 %collective-permute-start.7 = (bf16[192,512]{1,0:T(8,128)(2,1)S(1)}, bf16[192,512]{1,0:T(8,128)(2,1)S(1)}, u32[]{:S(2)}, u32[]{:S(2)}) collective-permute-start(bf16[192,512]{1,0:T(8,128)(2,1)S(1)} %get-tuple-element.60.g0), channel_id=1, source_target_pairs={{0,2},{1,3},{2,0},{3,1},{4,6},{5,7},{6,4},{7,5},{8,10},{9,11},{10,... | collective-permute-start | bytes 589832 | tf_op jit(solution)/shard_map/ppermute | solution.py:386
  24.7 14.8 %collective-permute-start.8 = (bf16[192,512]{1,0:T(8,128)(2,1)S(1)}, bf16[192,512]{1,0:T(8,128)(2,1)S(1)}, u32[]{:S(2)}, u32[]{:S(2)}) collective-permute-start(bf16[192,512]{1,0:T(8,128)(2,1)S(1)} %get-tuple-element.60.g0), channel_id=1, source_target_pairs={{0,1},{1,0},{2,3},{3,2},{4,5},{5,4},{6,7},{7,6},{8,9},{9,8},{10,11... | collective-permute-start | bytes 589832 | tf_op jit(solution)/shard_map/ppermute | solution.py:386
  27.3 12.2 %collective-permute-start.9 = (bf16[192,512]{1,0:T(8,128)(2,1)S(1)}, bf16[192,512]{1,0:T(8,128)(2,1)S(1)}, u32[]{:S(2)}, u32[]{:S(2)}) collective-permute-start(bf16[192,512]{1,0:T(8,128)(2,1)S(1)} %get-tuple-element.60.g0), channel_id=1, source_target_pairs={{0,3},{1,2},{2,1},{3,0},{4,7},{5,6},{6,5},{7,4},{8,11},{9,10},{10,... | collective-permute-start | bytes 589832 | tf_op jit(solution)/shard_map/ppermute | solution.py:386
  30.9 5.9 %collective-permute-start.12 = (bf16[96,256]{1,0:T(8,128)(2,1)S(1)}, bf16[96,256]{1,0:T(8,128)(2,1)S(1)}, u32[]{:S(2)}, u32[]{:S(2)}) collective-permute-start(bf16[96,256]{1,0:T(8,128)(2,1)S(1)} %get-tuple-element.67), channel_id=1, source_target_pairs={{0,1},{1,0},{2,3},{3,2},{4,8},{5,9},{6,10},{7,11},{8,4},{9,5},{10,... | collective-permute-start | bytes 147464 | tf_op jit(solution)/shard_map/ppermute | solution.py:382
  32.2 4.6 %collective-permute-start.13 = (bf16[96,256]{1,0:T(8,128)(2,1)S(1)}, bf16[96,256]{1,0:T(8,128)(2,1)S(1)}, u32[]{:S(2)}, u32[]{:S(2)}) collective-permute-start(bf16[96,256]{1,0:T(8,128)(2,1)S(1)} %get-tuple-element.68), channel_id=1, source_target_pairs={{0,4},{1,5},{2,6},{3,7},{4,0},{5,1},{6,2},{7,3},{8,12},{9,13},{10,... | collective-permute-start | bytes 147464 | tf_op jit(solution)/shard_map/ppermute | solution.py:382
  37.4 6.3 %collective-permute-start.15 = (bf16[96,256]{1,0:T(8,128)(2,1)S(1)}, bf16[96,256]{1,0:T(8,128)(2,1)S(1)}, u32[]{:S(2)}, u32[]{:S(2)}) collective-permute-start(bf16[96,256]{1,0:T(8,128)(2,1)S(1)} %get-tuple-element.72), channel_id=1, source_target_pairs={{0,4},{1,2},{2,1},{3,7},{4,0},{5,6},{6,5},{7,3},{8,12},{9,10},{10,... | collective-permute-start | bytes 147464 | tf_op jit(solution)/shard_map/ppermute | solution.py:382
  39.5 4.1 %collective-permute-start.16 = (bf16[96,256]{1,0:T(8,128)(2,1)S(1)}, bf16[96,256]{1,0:T(8,128)(2,1)S(1)}, u32[]{:S(2)}, u32[]{:S(2)}) collective-permute-start(bf16[96,256]{1,0:T(8,128)(2,1)S(1)} %get-tuple-element.69.late), channel_id=1, source_target_pairs={{0,1},{1,0},{2,3},{3,2},{4,5},{5,4},{6,7},{7,6},{8,9},{9,8},{10,11... | collective-permute-start | bytes 147464 | tf_op jit(solution)/shard_map/ppermute | solution.py:382
  41.3 3.7 %collective-permute-start.14 = (f32[128,1792]{1,0:T(8,128)S(1)}, f32[128,1792]{1,0:T(8,128)S(1)}, u32[]{:S(2)}, u32[]{:S(2)}) collective-permute-start(f32[128,1792]{1,0:T(8,128)S(1)} %get-tuple-element.71), channel_id=1, source_target_pairs={{0,4},{4,0},{8,12},{12,8},{16,20},{20,16},{24,28},{28,24},{32,36},... | collective-permute-start | bytes 2752520 | tf_op jit(solution)/shard_map/ppermute | solution.py:386
  43.3 7.9 %collective-permute-start.20 = (bf16[128,1792]{1,0:T(8,128)(2,1)S(1)}, bf16[128,1792]{1,0:T(8,128)(2,1)S(1)}, u32[]{:S(2)}, u32[]{:S(2)}) collective-permute-start(bf16[128,1792]{1,0:T(8,128)(2,1)S(1)} %get-tuple-element.81), channel_id=1, source_target_pairs={{0,4},{4,0},{8,12},{12,8},{16,20},{20,16},{24,28},{28,24},{32,36},... | collective-permute-start | bytes 1376264 | tf_op jit(solution)/shard_map/ppermute | solution.py:386
  44.6 6.5 %collective-permute-start.21 = (bf16[128,256]{1,0:T(8,128)(2,1)S(1)}, bf16[128,256]{1,0:T(8,128)(2,1)S(1)}, u32[]{:S(2)}, u32[]{:S(2)}) collective-permute-start(bf16[128,256]{1,0:T(8,128)(2,1)S(1)} %get-tuple-element.82), channel_id=1, source_target_pairs={{0,4},{4,0},{8,12},{12,8},{16,20},{20,16},{24,28},{28,24},{32,36},... | collective-permute-start | bytes 196616 | tf_op jit(solution)/shard_map/ppermute | solution.py:386
  45.6 9.4 %collective-permute-start.17 = (bf16[32,1792]{1,0:T(8,128)(2,1)S(1)}, bf16[32,1792]{1,0:T(8,128)(2,1)S(1)}, u32[]{:S(2)}, u32[]{:S(2)}) collective-permute-start(bf16[32,1792]{1,0:T(8,128)(2,1)S(1)} %get-tuple-element.78), channel_id=1, source_target_pairs={{0,64},{4,68},{8,72},{12,76},{16,80},{20,84},{24,88},{28,92},{32,9... | collective-permute-start | bytes 344072 | tf_op jit(solution)/shard_map/ppermute | solution.py:386
  47.9 8.1 %collective-permute-start.18 = (bf16[32,1792]{1,0:T(8,128)(2,1)S(1)}, bf16[32,1792]{1,0:T(8,128)(2,1)S(1)}, u32[]{:S(2)}, u32[]{:S(2)}) collective-permute-start(bf16[32,1792]{1,0:T(8,128)(2,1)S(1)} %get-tuple-element.79), channel_id=1, source_target_pairs={{0,192},{4,196},{8,200},{12,204},{16,208},{20,212},{24,216},{28,22... | collective-permute-start | bytes 344072 | tf_op jit(solution)/shard_map/ppermute | solution.py:386
  50.1 7.6 %collective-permute-start.19 = (bf16[32,1792]{1,0:T(8,128)(2,1)S(1)}, bf16[32,1792]{1,0:T(8,128)(2,1)S(1)}, u32[]{:S(2)}, u32[]{:S(2)}) collective-permute-start(bf16[32,1792]{1,0:T(8,128)(2,1)S(1)} %get-tuple-element.80), channel_id=1, source_target_pairs={{0,128},{4,132},{8,136},{12,140},{16,144},{20,148},{24,152},{28,15... | collective-permute-start | bytes 344072 | tf_op jit(solution)/shard_map/ppermute | solution.py:386
  51.8 7.0 %collective-permute-start.22 = (bf16[32,2304]{1,0:T(8,128)(2,1)S(1)}, bf16[32,2304]{1,0:T(8,128)(2,1)S(1)}, u32[]{:S(2)}, u32[]{:S(2)}) collective-permute-start(bf16[32,2304]{1,0:T(8,128)(2,1)S(1)} %get-tuple-element.84), channel_id=1, source_target_pairs={{0,64},{4,68},{8,72},{12,76},{16,80},{20,84},{24,88},{28,92},{32,9... | collective-permute-start | bytes 442376 | tf_op jit(solution)/shard_map/ppermute | solution.py:386
  52.8 8.9 %collective-permute-start.23 = (bf16[32,2304]{1,0:T(8,128)(2,1)S(1)}, bf16[32,2304]{1,0:T(8,128)(2,1)S(1)}, u32[]{:S(2)}, u32[]{:S(2)}) collective-permute-start(bf16[32,2304]{1,0:T(8,128)(2,1)S(1)} %get-tuple-element.85), channel_id=1, source_target_pairs={{0,192},{4,196},{8,200},{12,204},{16,208},{20,212},{24,216},{28,22... | collective-permute-start | bytes 442376 | tf_op jit(solution)/shard_map/ppermute | solution.py:386
  55.0 8.4 %collective-permute-start.24 = (bf16[32,2304]{1,0:T(8,128)(2,1)S(1)}, bf16[32,2304]{1,0:T(8,128)(2,1)S(1)}, u32[]{:S(2)}, u32[]{:S(2)}) collective-permute-start(bf16[32,2304]{1,0:T(8,128)(2,1)S(1)} %get-tuple-element.86), channel_id=1, source_target_pairs={{0,128},{4,132},{8,136},{12,140},{16,144},{20,148},{24,152},{28,15... | collective-permute-start | bytes 442376 | tf_op jit(solution)/shard_map/ppermute | solution.py:386

commit v17 on v16

--- a/solution.py
+++ b/solution.py
@@ -76,9 +76,6 @@
     table = jnp.where(table >= S, table + 8.0 * heading, table)
     nbt[...] = jnp.full(nbt.shape, -1.0, F32)
     nbt[0:K, 0:S] = table
-    shifted_up = table + 1.0
-    high = jnp.floor(shifted_up * (1.0 / 16.0))
-    tail = jnp.zeros((32, 2 * C), F32)
     z = pre_out[...].astype(F32)
     hidden = (z * (1.0 / (1.0 + jnp.exp(-z)))).astype(BF)
     halo_up = (halo_ids[0] + 1).astype(F32).astype(BF)
@@ -89,11 +86,11 @@
         keepdims=True,
     )
     hrow[...] = jnp.broadcast_to(row.astype(jnp.int32) - 1, hrow.shape)
-    pay[S : S + 32, :] = tail.astype(BF)
-    pay[S : S + K, 0:S] = high.astype(BF)
-    pay[S : S + K, C : C + S] = (shifted_up - 16.0 * high).astype(BF)
-    last = pay[S + 16 : S + 32, 0:C].astype(F32)
-    pay[S + 16 : S + 32, 0:C] = jnp.where(iota((16, C), 0) == 15, row, last).astype(BF)
+    shifted_up = nbt[...] + 1.0
+    high = jnp.floor(shifted_up * (1.0 / 16.0))
+    low = shifted_up - 16.0 * high
+    pay[S : S + 32, 0:C] = jnp.where(iota((32, C), 0) == 31, row, high).astype(BF)
+    pay[S : S + 32, C : 2 * C] = low.astype(BF)
     both = jnp.concatenate([feat_in[...], hidden], axis=0)
     for turn, out in ((0, pay), (1, p1), (2, p2), (3, p3)):
         offset = ((place[1] ^ turn) * QW) % C
@@ -325,7 +322,8 @@
     spot = ((at % 64) // 8 == (to // 6) % 8) & (
         8 * (at // 64) + at % 8 == 6 * (to // 48) + to % 6
     )
-    pieces = [arrived[:, :, (7 + n) * C : (8 + n) * C].reshape(64, C) for n in range(3)]
+    found = arrived[:, :, 7 * C : 10 * C].astype(F32)
+    pieces = [found[:, :, n * C : (n + 1) * C].reshape(64, C).astype(BF) for n in range(3)]
     rows[...] = mm(onehot(spot), jnp.concatenate(pieces, axis=0)).astype(BF)
 
 

time: 82.4 us -> 82.4 us (level)
  no operation moved by 1% of the time
where the time goes in v17:
time: 82.4 us; the launch traced here: 82 us
  starting transfers between devices  27.7 us (34%)
  Pallas kernels  23.8 us (29%)
  blocking collectives  16.8 us (20%)
  waiting for transfers between devices  12.8 us (16%)
    pallas_call x16, Pallas kernels, call(): pl.pallas_call(kernel, out_shape=outs, in_specs=specs, out_specs=jax.tree...  23.8 us
    ppermute x15, starting transfers between devices, cross(): lax.ppermute(value, axis, [(n, n ^ mask) for n in range(lax.axis_size(axi...  19.1 us
    all_to_all x1, blocking collectives, body(): lax.all_to_all(summed.reshape(8, 8, 10 * C), 'gx', split_axis=0, concat_a...  16.8 us
    ppermute x10, starting transfers between devices, swap(): return lax.ppermute(value, ('gx', 'gy'), pairs)  8.58 us
    ppermute x15, waiting for transfers between devices, cross(): lax.ppermute(value, axis, [(n, n ^ mask) for n in range(lax.axis_size(axi...  6.83 us
    ppermute x10, waiting for transfers between devices, swap(): return lax.ppermute(value, ('gx', 'gy'), pairs)  6.01 us
  transfers between devices with their start and end apart: 25, of which 9 were waited for; matrix products, arithmetic and copies ran while one was open for 0% of the time, Pallas kernels for 24%

profile of v17, /device:TPU:2, one launch (start us, length us, event | category | flops | bytes accessed | tf_op | source)
XLA Modules:
  0.0 82.0 jit_solution(8882043532313019753)
XLA Ops:
  0.6 0.1 pad_add_fusion.place
  0.7 2.3 %shard_map.103 = (bf16[224,512]{1,0:T(8,128)(2,1)S(1)}, bf16[224,512]{1,0:T(8,128)(2,1)S(1)}, bf16[224,512]{1,0:T(8,128)(2,1)S(1)}, bf16[224,512]{1,0:T(8,128)(2...) custom-call(s32[2]{0:T(128)S(1)} %pad_add_fusion.place, ...), custom_call_target="tpu_custom_call" | custom-call | flops 4000000000 | bytes 10000 | tf_op jit(solution)/shard_map/pallas_call | solution.py:343
  3.0 0.0 copy-start.1
  3.0 2.2 %collective-permute-start.4 = (bf16[224,512]{1,0:T(8,128)(2,1)S(1)}, bf16[224,512]{1,0:T(8,128)(2,1)S(1)}, u32[]{:S(2)}, u32[]{:S(2)}) collective-permute-start(bf16[224,512]{1,0:T(8,128)(2,1)S(1)} %get-tuple-element.56), channel_id=1, source_target_pairs={{0,2},{1,3},{2,0},{3,1},{4,6},{5,7},{6,4},{7,5},{8,10},{9,11},{10,... | collective-permute-start | bytes 688136 | tf_op jit(solution)/shard_map/ppermute | solution.py:384
  5.3 1.4 %collective-permute-start.5 = (bf16[224,512]{1,0:T(8,128)(2,1)S(1)}, bf16[224,512]{1,0:T(8,128)(2,1)S(1)}, u32[]{:S(2)}, u32[]{:S(2)}) collective-permute-start(bf16[224,512]{1,0:T(8,128)(2,1)S(1)} %get-tuple-element.57), channel_id=1, source_target_pairs={{0,1},{1,0},{2,3},{3,2},{4,5},{5,4},{6,7},{7,6},{8,9},{9,8},{10,11... | collective-permute-start | bytes 688136 | tf_op jit(solution)/shard_map/ppermute | solution.py:384
  6.7 0.5 collective-permute-start.6
  7.2 3.0 %shard_map.104 = (f32[192,256]{1,0:T(8,128)S(1)}, bf16[96,256]{1,0:T(8,128)(2,1)S(1)}, bf16[96,256]{1,0:T(8,128)(2,1)S(1)}, bf16[64,256]{1,0:T(8,128)(2,1)S(1)}) custom-call(s32[2]{0:T(128)S(1)} %pad_add_fusion.place, f32[32,256]{1,0:T(8,128)S(1)} %get-tuple-element.45.nbt, bf16[192,256]{1,0:T(8,128)(2,1)S(1)} %get-tuple-element.46.grad, ...), custom_call_target="tpu_custom_call" | custom-call | flops 100000 | bytes 10000 | tf_op jit(solution)/shard_map/pallas_call | solution.py:343
  10.3 2.4 %collective-permute-start = (bf16[96,256]{1,0:T(8,128)(2,1)S(1)}, bf16[96,256]{1,0:T(8,128)(2,1)S(1)}, u32[]{:S(2)}, u32[]{:S(2)}) collective-permute-start(bf16[96,256]{1,0:T(8,128)(2,1)S(1)} %get-tuple-element.48), channel_id=1, source_target_pairs={{0,1},{1,0},{2,3},{3,2},{4,8},{5,9},{6,10},{7,11},{8,4},{9,5},{10,... | collective-permute-start | bytes 147464 | tf_op jit(solution)/shard_map/ppermute | solution.py:380
  12.6 0.0 collective-permute-start.1
  12.6 4.9 %collective-permute-done.m2 = bf16[96,256]{1,0:T(8,128)(2,1)S(1)} collective-permute-done((bf16[96,256]{1,0:T(8,128)(2,1)S(1)}, bf16[96,256]{1,0:T(8,128)(2,1)S(1)}, u32[]{:S(2)}, u32[]{:S(2)}) %collective-permute-start) | collective-permute-done | bytes 49184 | tf_op jit(solution)/shard_map/ppermute | solution.py:380
  17.5 0.0 collective-permute-done.1.m1
  17.5 0.6 shard_map.105
  18.1 0.6 collective-permute-start.2
  18.7 0.2 collective-permute-start.3
  18.8 0.0 collective-permute-done.4.p2
  18.8 0.0 collective-permute-done.5.p1
  18.8 0.0 collective-permute-done.6.p3
  18.9 1.1 %shard_map.106 = (bf16[768,256]{1,0:T(8,128)(2,1)S(1)}, bf16[768,256]{1,0:T(8,128)(2,1)S(1)}, bf16[4,64,512]{2,1,0:T(8,128)(2,1)S(1)}) custom-call(s32[2]{0:T(128)S(1)} %pad_add_fusion.place, bf16[224,512]{1,0:T(8,128)(2,1)S(1)} %get-tuple-element.55.p0, bf16[224,512]{1,0:T(8,128)(2,1)S(1)} %collective-permute-done.4.p2, ...), custom_call_target="tpu_custom_call" | custom-call | flops 100000 | bytes 10000 | tf_op jit(solution)/shard_map/pallas_call | solution.py:343
  19.9 2.0 %collective-permute-start.10 = (bf16[768,256]{1,0:T(8,128)(2,1)S(1)}, bf16[768,256]{1,0:T(8,128)(2,1)S(1)}, u32[]{:S(2)}, u32[]{:S(2)}) collective-permute-start(bf16[768,256]{1,0:T(8,128)(2,1)S(1)} %get-tuple-element.61), channel_id=1, source_target_pairs={{0,1},{1,0},{2,3},{3,2},{4,8},{5,9},{6,10},{7,11},{8,4},{9,5},{10,... | collective-permute-start | bytes 1179656 | tf_op jit(solution)/shard_map/ppermute | solution.py:380
  21.9 0.3 collective-permute-done.2.n2
  22.2 0.5 collective-permute-done.3.n1
  22.8 0.9 %shard_map.107 = (bf16[192,256]{1,0:T(8,128)(2,1)S(1)}, bf16[192,512]{1,0:T(8,128)(2,1)S(1)}) custom-call(s32[2]{0:T(128)S(1)} %pad_add_fusion.place, f32[192,256]{1,0:T(8,128)S(1)} %get-tuple-element.47.late.own, bf16[96,256]{1,0:T(8,128)(2,1)S(1)} %collective-permute-done.m2, bf16[96,256]{1,0:T(8,128)(2,1)S(1)} %collective-permute-done.1.m1, ...), custom_call_target="tpu_custom_call" | custom-call | flops 100000 | bytes 10000 | tf_op jit(solution)/shard_map/pallas_call | solution.py:343
  23.7 1.0 %collective-permute-start.7 = (bf16[192,512]{1,0:T(8,128)(2,1)S(1)}, bf16[192,512]{1,0:T(8,128)(2,1)S(1)}, u32[]{:S(2)}, u32[]{:S(2)}) collective-permute-start(bf16[192,512]{1,0:T(8,128)(2,1)S(1)} %get-tuple-element.60.g0), channel_id=1, source_target_pairs={{0,2},{1,3},{2,0},{3,1},{4,6},{5,7},{6,4},{7,5},{8,10},{9,11},{10,... | collective-permute-start | bytes 589832 | tf_op jit(solution)/shard_map/ppermute | solution.py:384
  24.7 2.6 %collective-permute-start.8 = (bf16[192,512]{1,0:T(8,128)(2,1)S(1)}, bf16[192,512]{1,0:T(8,128)(2,1)S(1)}, u32[]{:S(2)}, u32[]{:S(2)}) collective-permute-start(bf16[192,512]{1,0:T(8,128)(2,1)S(1)} %get-tuple-element.60.g0), channel_id=1, source_target_pairs={{0,1},{1,0},{2,3},{3,2},{4,5},{5,4},{6,7},{7,6},{8,9},{9,8},{10,11... | collective-permute-start | bytes 589832 | tf_op jit(solution)/shard_map/ppermute | solution.py:384
  27.3 0.5 collective-permute-start.9
  27.9 3.0 %shard_map.108 = (f32[192,256]{1,0:T(8,128)S(1)}, bf16[96,256]{1,0:T(8,128)(2,1)S(1)}, bf16[96,256]{1,0:T(8,128)(2,1)S(1)}, bf16[64,256]{1,0:T(8,128)(2,1)S(1)}) custom-call(s32[2]{0:T(128)S(1)} %pad_add_fusion.place, f32[32,256]{1,0:T(8,128)S(1)} %get-tuple-element.45.nbt, bf16[192,256]{1,0:T(8,128)(2,1)S(1)} %get-tuple-element.63.grad, ...), custom_call_target="tpu_custom_call" | custom-call | flops 4000000000 | bytes 10000 | tf_op jit(solution)/shard_map/pallas_call | solution.py:343
  30.9 0.0 collective-permute-done.10.r2
  30.9 1.3 %collective-permute-start.12 = (bf16[96,256]{1,0:T(8,128)(2,1)S(1)}, bf16[96,256]{1,0:T(8,128)(2,1)S(1)}, u32[]{:S(2)}, u32[]{:S(2)}) collective-permute-start(bf16[96,256]{1,0:T(8,128)(2,1)S(1)} %get-tuple-element.67), channel_id=1, source_target_pairs={{0,1},{1,0},{2,3},{3,2},{4,8},{5,9},{6,10},{7,11},{8,4},{9,5},{10,... | collective-permute-start | bytes 147464 | tf_op jit(solution)/shard_map/ppermute | solution.py:380
  32.2 0.0 collective-permute-start.13
  32.2 4.3 %shard_map.109 = (bf16[768,1792]{1,0:T(8,128)(2,1)S(1)}, bf16[768,1792]{1,0:T(8,128)(2,1)S(1)}) custom-call(s32[2]{0:T(128)S(1)} %pad_add_fusion.place, bf16[224,512]{1,0:T(8,128)(2,1)S(1)} %get-tuple-element.55.p0, bf16[224,512]{1,0:T(8,128)(2,1)S(1)} %collective-permute-done.4.p2, bf16[224,512]{1,0:T(8,128)(2,1)S(1)} %collective-permute-done.5.p1, ...), custom_call_target="tpu_custom_call" | custom-call | flops 4000000000 | bytes 10000 | tf_op jit(solution)/shard_map/pallas_call | solution.py:343
  36.5 0.3 collective-permute-done.12.m2
  36.8 0.6 shard_map.110
  37.4 2.2 %collective-permute-start.15 = (bf16[96,256]{1,0:T(8,128)(2,1)S(1)}, bf16[96,256]{1,0:T(8,128)(2,1)S(1)}, u32[]{:S(2)}, u32[]{:S(2)}) collective-permute-start(bf16[96,256]{1,0:T(8,128)(2,1)S(1)} %get-tuple-element.72), channel_id=1, source_target_pairs={{0,4},{1,2},{2,1},{3,7},{4,0},{5,6},{6,5},{7,3},{8,12},{9,10},{10,... | collective-permute-start | bytes 147464 | tf_op jit(solution)/shard_map/ppermute | solution.py:380
  39.5 0.0 collective-permute-start.16
  39.5 0.0 collective-permute-done.7.g2
  39.5 0.0 collective-permute-done.8.g1
  39.6 1.7 %shard_map.111 = (f32[128,1792]{1,0:T(8,128)S(1)}, f32[128,1792]{1,0:T(8,128)S(1)}) custom-call(s32[2]{0:T(128)S(1)} %pad_add_fusion.place, bf16[192,512]{1,0:T(8,128)(2,1)S(1)} %get-tuple-element.60.g0, bf16[192,512]{1,0:T(8,128)(2,1)S(1)} %collective-permute-done.7.g2, bf16[192,512]{1,0:T(8,128)(2,1)S(1)} %collective-permute-done.8.g1, ...), custom_call_target="tpu_custom_call" | custom-call | flops 4000000000 | bytes 10000 | tf_op jit(solution)/shard_map/pallas_call | solution.py:343
  41.3 0.3 collective-permute-start.14
  41.6 1.7 %shard_map.112 = (bf16[128,1792]{1,0:T(8,128)(2,1)S(1)}, bf16[128,1792]{1,0:T(8,128)(2,1)S(1)}) custom-call(s32[2]{0:T(128)S(1)} %pad_add_fusion.place, bf16[192,512]{1,0:T(8,128)(2,1)S(1)} %get-tuple-element.60.g0, bf16[192,512]{1,0:T(8,128)(2,1)S(1)} %collective-permute-done.7.g2, bf16[192,512]{1,0:T(8,128)(2,1)S(1)} %collective-permute-done.8.g1, ...), custom_call_target="tpu_custom_call" | custom-call | flops 100000 | bytes 10000 | tf_op jit(solution)/shard_map/pallas_call | solution.py:343
  43.3 0.4 collective-permute-start.20
  43.6 0.0 collective-permute-done.16.n1
  43.6 1.0 %shard_map.113 = (bf16[128,256]{1,0:T(8,128)(2,1)S(1)}, bf16[128,256]{1,0:T(8,128)(2,1)S(1)}) custom-call(s32[2]{0:T(128)S(1)} %pad_add_fusion.place, f32[192,256]{1,0:T(8,128)S(1)} %get-tuple-element.64.late.own, bf16[96,256]{1,0:T(8,128)(2,1)S(1)} %collective-permute-done.12.m2, bf16[96,256]{1,0:T(8,128)(2,1)S(1)} %collective-permute-done.13.m1, ...), custom_call_target="tpu_custom_call" | custom-call | flops 20000000000 | bytes 10000 | tf_op jit(solution)/shard_map/pallas_call | solution.py:343
  44.6 0.3 collective-permute-start.21
  44.9 0.0 collective-permute-done.14.come
  44.9 0.6 shard_map.114
  45.6 2.4 %collective-permute-start.17 = (bf16[32,1792]{1,0:T(8,128)(2,1)S(1)}, bf16[32,1792]{1,0:T(8,128)(2,1)S(1)}, u32[]{:S(2)}, u32[]{:S(2)}) collective-permute-start(bf16[32,1792]{1,0:T(8,128)(2,1)S(1)} %get-tuple-element.78), channel_id=1, source_target_pairs={{0,64},{4,68},{8,72},{12,76},{16,80},{20,84},{24,88},{28,92},{32,9... | collective-permute-start | bytes 344072 | tf_op jit(solution)/shard_map/ppermute | solution.py:384
  47.9 2.2 %collective-permute-start.18 = (bf16[32,1792]{1,0:T(8,128)(2,1)S(1)}, bf16[32,1792]{1,0:T(8,128)(2,1)S(1)}, u32[]{:S(2)}, u32[]{:S(2)}) collective-permute-start(bf16[32,1792]{1,0:T(8,128)(2,1)S(1)} %get-tuple-element.79), channel_id=1, source_target_pairs={{0,192},{4,196},{8,200},{12,204},{16,208},{20,212},{24,216},{28,22... | collective-permute-start | bytes 344072 | tf_op jit(solution)/shard_map/ppermute | solution.py:384
  50.1 1.0 %collective-permute-start.19 = (bf16[32,1792]{1,0:T(8,128)(2,1)S(1)}, bf16[32,1792]{1,0:T(8,128)(2,1)S(1)}, u32[]{:S(2)}, u32[]{:S(2)}) collective-permute-start(bf16[32,1792]{1,0:T(8,128)(2,1)S(1)} %get-tuple-element.80), channel_id=1, source_target_pairs={{0,128},{4,132},{8,136},{12,140},{16,144},{20,148},{24,152},{28,15... | collective-permute-start | bytes 344072 | tf_op jit(solution)/shard_map/ppermute | solution.py:384
  51.1 0.0 collective-permute-done.21.rs
  51.1 0.0 collective-permute-done.20.come
  51.2 0.7 shard_map.116
  51.8 1.0 %collective-permute-start.22 = (bf16[32,2304]{1,0:T(8,128)(2,1)S(1)}, bf16[32,2304]{1,0:T(8,128)(2,1)S(1)}, u32[]{:S(2)}, u32[]{:S(2)}) collective-permute-start(bf16[32,2304]{1,0:T(8,128)(2,1)S(1)} %get-tuple-element.84), channel_id=1, source_target_pairs={{0,64},{4,68},{8,72},{12,76},{16,80},{20,84},{24,88},{28,92},{32,9... | collective-permute-start | bytes 442376 | tf_op jit(solution)/shard_map/ppermute | solution.py:384
  52.8 2.2 %collective-permute-start.23 = (bf16[32,2304]{1,0:T(8,128)(2,1)S(1)}, bf16[32,2304]{1,0:T(8,128)(2,1)S(1)}, u32[]{:S(2)}, u32[]{:S(2)}) collective-permute-start(bf16[32,2304]{1,0:T(8,128)(2,1)S(1)} %get-tuple-element.85), channel_id=1, source_target_pairs={{0,192},{4,196},{8,200},{12,204},{16,208},{20,212},{24,216},{28,22... | collective-permute-start | bytes 442376 | tf_op jit(solution)/shard_map/ppermute | solution.py:384
  55.0 0.0 collective-permute-done.17.a1
  55.0 1.0 %collective-permute-start.24 = (bf16[32,2304]{1,0:T(8,128)(2,1)S(1)}, bf16[32,2304]{1,0:T(8,128)(2,1)S(1)}, u32[]{:S(2)}, u32[]{:S(2)}) collective-permute-start(bf16[32,2304]{1,0:T(8,128)(2,1)S(1)} %get-tuple-element.86), channel_id=1, source_target_pairs={{0,128},{4,132},{8,136},{12,140},{16,144},{20,148},{24,152},{28,15... | collective-permute-start | bytes 442376 | tf_op jit(solution)/shard_map/ppermute | solution.py:384
  56.0 0.1 collective-permute-done.18.a3
  56.1 1.6 %collective-permute-done.19.a2 = bf16[32,1792]{1,0:T(8,128)(2,1)S(1)} collective-permute-done((bf16[32,1792]{1,0:T(8,128)(2,1)S(1)}, bf16[32,1792]{1,0:T(8,128)(2,1)S(1)}, u32[]{:S(2)}, u32[]{:S(2)}) %collective-permute-start.19) | collective-permute-done | bytes 114720 | tf_op jit(solution)/shard_map/ppermute | solution.py:384
  57.7 0.6 shard_map.115.two
  58.3 0.5 collective-permute-done.22.b1
  58.8 2.9 %collective-permute-done.23.b3 = bf16[32,2304]{1,0:T(8,128)(2,1)S(1)} collective-permute-done((bf16[32,2304]{1,0:T(8,128)(2,1)S(1)}, bf16[32,2304]{1,0:T(8,128)(2,1)S(1)}, u32[]{:S(2)}, u32[]{:S(2)}) %collective-permute-start.23) | collective-permute-done | bytes 147488 | tf_op jit(solution)/shard_map/ppermute | solution.py:384
  61.7 1.7 %collective-permute-done.24.b2 = bf16[32,2304]{1,0:T(8,128)(2,1)S(1)} collective-permute-done((bf16[32,2304]{1,0:T(8,128)(2,1)S(1)}, bf16[32,2304]{1,0:T(8,128)(2,1)S(1)}, u32[]{:S(2)}, u32[]{:S(2)}) %collective-permute-start.24) | collective-permute-done | bytes 147488 | tf_op jit(solution)/shard_map/ppermute | solution.py:384
  63.4 0.9 %shard_map.117 = bf16[64,2560]{1,0:T(8,128)(2,1)S(1)} custom-call(s32[2]{0:T(128)S(1)} %pad_add_fusion.place, bf16[32,1792]{1,0:T(8,128)(2,1)S(1)} %shard_map.115.two, bf16[32,2304]{1,0:T(8,128)(2,1)S(1)} %get-tuple-element.83.b0, bf16[32,2304]{1,0:T(8,128)(2,1)S(1)} %collective-permute-done.22.b1, bf16[32,2304]{1,0:T(8,128)(2,1)S(1)} %collective-permute-done.23.b3, ...), custom_call_target="tpu_custom_call" | custom-call | flops 100000 | bytes 10000 | tf_op jit(solution)/shard_map/pallas_call | solution.py:343
  64.3 16.8 %all_to_all.5.refs_0_ = bf16[8,8,2560]{2,1,0:T(8,128)(2,1)S(1)} all-to-all(bf16[8,8,2560]{2,1,0:T(8,128)(2,1)S(1)} %bitcast.5), channel_id=1, replica_groups={{0,8,16,24,32,40,48,56},{4,12,20,28,36,44,52,60},{64,72,80,88,96,104,11..., dimensions={0} | all-to-all | bytes 655360 | tf_op jit(solution)/shard_map/all_to_all | solution.py:562
  81.1 0.9 %shard_map.118 = (bf16[192,256]{1,0:T(8,128)(2,1)}, f32[4,1728]{1,0:T(4,128)}, f32[4,1728]{1,0:T(4,128)}) custom-call(bf16[8,8,2560]{2,1,0:T(8,128)(2,1)S(1)} %all_to_all.5.refs_0_), custom_call_target="tpu_custom_call" | custom-call | flops 100000 | bytes 10000 | tf_op jit(solution)/shard_map/pallas_call | solution.py:343
  (8 shorter events, 0.0 us)
Async XLA Ops:
  0.7 6.5 %copy-start = (bf16[256,6912]{1,0:T(8,128)(2,1)S(1)}, bf16[256,6912]{1,0:T(8,128)(2,1)}, u32[]{:S(2)}) copy-start(bf16[256,6912]{1,0:T(8,128)(2,1)} %weight.2) | copy-start | bytes 10616836
  3.0 24.8 %copy-start.1 = (bf16[256,6912]{1,0:T(8,128)(2,1)S(1)}, bf16[256,6912]{1,0:T(8,128)(2,1)}, u32[]{:S(2)}) copy-start(bf16[256,6912]{1,0:T(8,128)(2,1)} %weight.3) | copy-start | bytes 10616836
  3.0 15.8 %collective-permute-start.4 = (bf16[224,512]{1,0:T(8,128)(2,1)S(1)}, bf16[224,512]{1,0:T(8,128)(2,1)S(1)}, u32[]{:S(2)}, u32[]{:S(2)}) collective-permute-start(bf16[224,512]{1,0:T(8,128)(2,1)S(1)} %get-tuple-element.56), channel_id=1, source_target_pairs={{0,2},{1,3},{2,0},{3,1},{4,6},{5,7},{6,4},{7,5},{8,10},{9,11},{10,... | collective-permute-start | bytes 688136 | tf_op jit(solution)/shard_map/ppermute | solution.py:384
  5.3 13.6 %collective-permute-start.5 = (bf16[224,512]{1,0:T(8,128)(2,1)S(1)}, bf16[224,512]{1,0:T(8,128)(2,1)S(1)}, u32[]{:S(2)}, u32[]{:S(2)}) collective-permute-start(bf16[224,512]{1,0:T(8,128)(2,1)S(1)} %get-tuple-element.57), channel_id=1, source_target_pairs={{0,1},{1,0},{2,3},{3,2},{4,5},{5,4},{6,7},{7,6},{8,9},{9,8},{10,11... | collective-permute-start | bytes 688136 | tf_op jit(solution)/shard_map/ppermute | solution.py:384
  6.7 12.2 %collective-permute-start.6 = (bf16[224,512]{1,0:T(8,128)(2,1)S(1)}, bf16[224,512]{1,0:T(8,128)(2,1)S(1)}, u32[]{:S(2)}, u32[]{:S(2)}) collective-permute-start(bf16[224,512]{1,0:T(8,128)(2,1)S(1)} %get-tuple-element.58), channel_id=1, source_target_pairs={{0,3},{1,2},{2,1},{3,0},{4,7},{5,6},{6,5},{7,4},{8,11},{9,10},{10,... | collective-permute-start | bytes 688136 | tf_op jit(solution)/shard_map/ppermute | solution.py:384
  10.3 7.2 %collective-permute-start = (bf16[96,256]{1,0:T(8,128)(2,1)S(1)}, bf16[96,256]{1,0:T(8,128)(2,1)S(1)}, u32[]{:S(2)}, u32[]{:S(2)}) collective-permute-start(bf16[96,256]{1,0:T(8,128)(2,1)S(1)} %get-tuple-element.48), channel_id=1, source_target_pairs={{0,1},{1,0},{2,3},{3,2},{4,8},{5,9},{6,10},{7,11},{8,4},{9,5},{10,... | collective-permute-start | bytes 147464 | tf_op jit(solution)/shard_map/ppermute | solution.py:380
  12.6 4.9 %collective-permute-start.1 = (bf16[96,256]{1,0:T(8,128)(2,1)S(1)}, bf16[96,256]{1,0:T(8,128)(2,1)S(1)}, u32[]{:S(2)}, u32[]{:S(2)}) collective-permute-start(bf16[96,256]{1,0:T(8,128)(2,1)S(1)} %get-tuple-element.49), channel_id=1, source_target_pairs={{0,4},{1,5},{2,6},{3,7},{4,0},{5,1},{6,2},{7,3},{8,12},{9,13},{10,... | collective-permute-start | bytes 147464 | tf_op jit(solution)/shard_map/ppermute | solution.py:380
  18.1 4.2 %collective-permute-start.2 = (bf16[96,256]{1,0:T(8,128)(2,1)S(1)}, bf16[96,256]{1,0:T(8,128)(2,1)S(1)}, u32[]{:S(2)}, u32[]{:S(2)}) collective-permute-start(bf16[96,256]{1,0:T(8,128)(2,1)S(1)} %get-tuple-element.51), channel_id=1, source_target_pairs={{0,4},{1,2},{2,1},{3,7},{4,0},{5,6},{6,5},{7,3},{8,12},{9,10},{10,... | collective-permute-start | bytes 147464 | tf_op jit(solution)/shard_map/ppermute | solution.py:380
  18.7 4.1 %collective-permute-start.3 = (bf16[96,256]{1,0:T(8,128)(2,1)S(1)}, bf16[96,256]{1,0:T(8,128)(2,1)S(1)}, u32[]{:S(2)}, u32[]{:S(2)}) collective-permute-start(bf16[96,256]{1,0:T(8,128)(2,1)S(1)} %get-tuple-element.52.late), channel_id=1, source_target_pairs={{0,1},{1,0},{2,3},{3,2},{4,5},{5,4},{6,7},{7,6},{8,9},{9,8},{10,11... | collective-permute-start | bytes 147464 | tf_op jit(solution)/shard_map/ppermute | solution.py:380
  19.9 11.0 %collective-permute-start.10 = (bf16[768,256]{1,0:T(8,128)(2,1)S(1)}, bf16[768,256]{1,0:T(8,128)(2,1)S(1)}, u32[]{:S(2)}, u32[]{:S(2)}) collective-permute-start(bf16[768,256]{1,0:T(8,128)(2,1)S(1)} %get-tuple-element.61), channel_id=1, source_target_pairs={{0,1},{1,0},{2,3},{3,2},{4,8},{5,9},{6,10},{7,11},{8,4},{9,5},{10,... | collective-permute-start | bytes 1179656 | tf_op jit(solution)/shard_map/ppermute | solution.py:380
  21.9 10.3 %collective-permute-start.11 = (bf16[768,256]{1,0:T(8,128)(2,1)S(1)}, bf16[768,256]{1,0:T(8,128)(2,1)S(1)}, u32[]{:S(2)}, u32[]{:S(2)}) collective-permute-start(bf16[768,256]{1,0:T(8,128)(2,1)S(1)} %get-tuple-element.62), channel_id=1, source_target_pairs={{0,4},{1,5},{2,6},{3,7},{4,0},{5,1},{6,2},{7,3},{8,12},{9,13},{10,... | collective-permute-start | bytes 1179656 | tf_op jit(solution)/shard_map/ppermute | solution.py:380
  23.7 15.9 %collective-permute-start.7 = (bf16[192,512]{1,0:T(8,128)(2,1)S(1)}, bf16[192,512]{1,0:T(8,128)(2,1)S(1)}, u32[]{:S(2)}, u32[]{:S(2)}) collective-permute-start(bf16[192,512]{1,0:T(8,128)(2,1)S(1)} %get-tuple-element.60.g0), channel_id=1, source_target_pairs={{0,2},{1,3},{2,0},{3,1},{4,6},{5,7},{6,4},{7,5},{8,10},{9,11},{10,... | collective-permute-start | bytes 589832 | tf_op jit(solution)/shard_map/ppermute | solution.py:384
  24.7 14.8 %collective-permute-start.8 = (bf16[192,512]{1,0:T(8,128)(2,1)S(1)}, bf16[192,512]{1,0:T(8,128)(2,1)S(1)}, u32[]{:S(2)}, u32[]{:S(2)}) collective-permute-start(bf16[192,512]{1,0:T(8,128)(2,1)S(1)} %get-tuple-element.60.g0), channel_id=1, source_target_pairs={{0,1},{1,0},{2,3},{3,2},{4,5},{5,4},{6,7},{7,6},{8,9},{9,8},{10,11... | collective-permute-start | bytes 589832 | tf_op jit(solution)/shard_map/ppermute | solution.py:384
  27.3 12.2 %collective-permute-start.9 = (bf16[192,512]{1,0:T(8,128)(2,1)S(1)}, bf16[192,512]{1,0:T(8,128)(2,1)S(1)}, u32[]{:S(2)}, u32[]{:S(2)}) collective-permute-start(bf16[192,512]{1,0:T(8,128)(2,1)S(1)} %get-tuple-element.60.g0), channel_id=1, source_target_pairs={{0,3},{1,2},{2,1},{3,0},{4,7},{5,6},{6,5},{7,4},{8,11},{9,10},{10,... | collective-permute-start | bytes 589832 | tf_op jit(solution)/shard_map/ppermute | solution.py:384
  30.9 5.9 %collective-permute-start.12 = (bf16[96,256]{1,0:T(8,128)(2,1)S(1)}, bf16[96,256]{1,0:T(8,128)(2,1)S(1)}, u32[]{:S(2)}, u32[]{:S(2)}) collective-permute-start(bf16[96,256]{1,0:T(8,128)(2,1)S(1)} %get-tuple-element.67), channel_id=1, source_target_pairs={{0,1},{1,0},{2,3},{3,2},{4,8},{5,9},{6,10},{7,11},{8,4},{9,5},{10,... | collective-permute-start | bytes 147464 | tf_op jit(solution)/shard_map/ppermute | solution.py:380
  32.2 4.6 %collective-permute-start.13 = (bf16[96,256]{1,0:T(8,128)(2,1)S(1)}, bf16[96,256]{1,0:T(8,128)(2,1)S(1)}, u32[]{:S(2)}, u32[]{:S(2)}) collective-permute-start(bf16[96,256]{1,0:T(8,128)(2,1)S(1)} %get-tuple-element.68), channel_id=1, source_target_pairs={{0,4},{1,5},{2,6},{3,7},{4,0},{5,1},{6,2},{7,3},{8,12},{9,13},{10,... | collective-permute-start | bytes 147464 | tf_op jit(solution)/shard_map/ppermute | solution.py:380
  37.4 6.3 %collective-permute-start.15 = (bf16[96,256]{1,0:T(8,128)(2,1)S(1)}, bf16[96,256]{1,0:T(8,128)(2,1)S(1)}, u32[]{:S(2)}, u32[]{:S(2)}) collective-permute-start(bf16[96,256]{1,0:T(8,128)(2,1)S(1)} %get-tuple-element.72), channel_id=1, source_target_pairs={{0,4},{1,2},{2,1},{3,7},{4,0},{5,6},{6,5},{7,3},{8,12},{9,10},{10,... | collective-permute-start | bytes 147464 | tf_op jit(solution)/shard_map/ppermute | solution.py:380
  39.5 4.1 %collective-permute-start.16 = (bf16[96,256]{1,0:T(8,128)(2,1)S(1)}, bf16[96,256]{1,0:T(8,128)(2,1)S(1)}, u32[]{:S(2)}, u32[]{:S(2)}) collective-permute-start(bf16[96,256]{1,0:T(8,128)(2,1)S(1)} %get-tuple-element.69.late), channel_id=1, source_target_pairs={{0,1},{1,0},{2,3},{3,2},{4,5},{5,4},{6,7},{7,6},{8,9},{9,8},{10,11... | collective-permute-start | bytes 147464 | tf_op jit(solution)/shard_map/ppermute | solution.py:380
  41.3 3.7 %collective-permute-start.14 = (f32[128,1792]{1,0:T(8,128)S(1)}, f32[128,1792]{1,0:T(8,128)S(1)}, u32[]{:S(2)}, u32[]{:S(2)}) collective-permute-start(f32[128,1792]{1,0:T(8,128)S(1)} %get-tuple-element.71), channel_id=1, source_target_pairs={{0,4},{4,0},{8,12},{12,8},{16,20},{20,16},{24,28},{28,24},{32,36},... | collective-permute-start | bytes 2752520 | tf_op jit(solution)/shard_map/ppermute | solution.py:384
  43.3 7.9 %collective-permute-start.20 = (bf16[128,1792]{1,0:T(8,128)(2,1)S(1)}, bf16[128,1792]{1,0:T(8,128)(2,1)S(1)}, u32[]{:S(2)}, u32[]{:S(2)}) collective-permute-start(bf16[128,1792]{1,0:T(8,128)(2,1)S(1)} %get-tuple-element.81), channel_id=1, source_target_pairs={{0,4},{4,0},{8,12},{12,8},{16,20},{20,16},{24,28},{28,24},{32,36},... | collective-permute-start | bytes 1376264 | tf_op jit(solution)/shard_map/ppermute | solution.py:384
  44.6 6.5 %collective-permute-start.21 = (bf16[128,256]{1,0:T(8,128)(2,1)S(1)}, bf16[128,256]{1,0:T(8,128)(2,1)S(1)}, u32[]{:S(2)}, u32[]{:S(2)}) collective-permute-start(bf16[128,256]{1,0:T(8,128)(2,1)S(1)} %get-tuple-element.82), channel_id=1, source_target_pairs={{0,4},{4,0},{8,12},{12,8},{16,20},{20,16},{24,28},{28,24},{32,36},... | collective-permute-start | bytes 196616 | tf_op jit(solution)/shard_map/ppermute | solution.py:384
  45.6 9.4 %collective-permute-start.17 = (bf16[32,1792]{1,0:T(8,128)(2,1)S(1)}, bf16[32,1792]{1,0:T(8,128)(2,1)S(1)}, u32[]{:S(2)}, u32[]{:S(2)}) collective-permute-start(bf16[32,1792]{1,0:T(8,128)(2,1)S(1)} %get-tuple-element.78), channel_id=1, source_target_pairs={{0,64},{4,68},{8,72},{12,76},{16,80},{20,84},{24,88},{28,92},{32,9... | collective-permute-start | bytes 344072 | tf_op jit(solution)/shard_map/ppermute | solution.py:384
  47.9 8.1 %collective-permute-start.18 = (bf16[32,1792]{1,0:T(8,128)(2,1)S(1)}, bf16[32,1792]{1,0:T(8,128)(2,1)S(1)}, u32[]{:S(2)}, u32[]{:S(2)}) collective-permute-start(bf16[32,1792]{1,0:T(8,128)(2,1)S(1)} %get-tuple-element.79), channel_id=1, source_target_pairs={{0,192},{4,196},{8,200},{12,204},{16,208},{20,212},{24,216},{28,22... | collective-permute-start | bytes 344072 | tf_op jit(solution)/shard_map/ppermute | solution.py:384
  50.1 7.6 %collective-permute-start.19 = (bf16[32,1792]{1,0:T(8,128)(2,1)S(1)}, bf16[32,1792]{1,0:T(8,128)(2,1)S(1)}, u32[]{:S(2)}, u32[]{:S(2)}) collective-permute-start(bf16[32,1792]{1,0:T(8,128)(2,1)S(1)} %get-tuple-element.80), channel_id=1, source_target_pairs={{0,128},{4,132},{8,136},{12,140},{16,144},{20,148},{24,152},{28,15... | collective-permute-start | bytes 344072 | tf_op jit(solution)/shard_map/ppermute | solution.py:384
  51.8 7.0 %collective-permute-start.22 = (bf16[32,2304]{1,0:T(8,128)(2,1)S(1)}, bf16[32,2304]{1,0:T(8,128)(2,1)S(1)}, u32[]{:S(2)}, u32[]{:S(2)}) collective-permute-start(bf16[32,2304]{1,0:T(8,128)(2,1)S(1)} %get-tuple-element.84), channel_id=1, source_target_pairs={{0,64},{4,68},{8,72},{12,76},{16,80},{20,84},{24,88},{28,92},{32,9... | collective-permute-start | bytes 442376 | tf_op jit(solution)/shard_map/ppermute | solution.py:384
  52.8 8.9 %collective-permute-start.23 = (bf16[32,2304]{1,0:T(8,128)(2,1)S(1)}, bf16[32,2304]{1,0:T(8,128)(2,1)S(1)}, u32[]{:S(2)}, u32[]{:S(2)}) collective-permute-start(bf16[32,2304]{1,0:T(8,128)(2,1)S(1)} %get-tuple-element.85), channel_id=1, source_target_pairs={{0,192},{4,196},{8,200},{12,204},{16,208},{20,212},{24,216},{28,22... | collective-permute-start | bytes 442376 | tf_op jit(solution)/shard_map/ppermute | solution.py:384
  55.0 8.4 %collective-permute-start.24 = (bf16[32,2304]{1,0:T(8,128)(2,1)S(1)}, bf16[32,2304]{1,0:T(8,128)(2,1)S(1)}, u32[]{:S(2)}, u32[]{:S(2)}) collective-permute-start(bf16[32,2304]{1,0:T(8,128)(2,1)S(1)} %get-tuple-element.86), channel_id=1, source_target_pairs={{0,128},{4,132},{8,136},{12,140},{16,144},{20,148},{24,152},{28,15... | collective-permute-start | bytes 442376 | tf_op jit(solution)/shard_map/ppermute | solution.py:384

commit v18 on v17

--- a/solution.py
+++ b/solution.py
@@ -266,7 +266,7 @@
     line = place[0] // 16
     for turn, out in enumerate(outs):
         rows = pl.ds(pl.multiple_of(32 * (line ^ turn), 32), 32)
-        out[...] = (keep[rows, :] + come[rows, :]).astype(BF)
+        out[...] = (keep[rows, :] + come[rows, :].astype(F32)).astype(BF)
 
 
 def merge_one_kernel(place, keep, come, rk, rs, late, *outs):
@@ -496,7 +496,7 @@
         half = sds((128, wide), kind)
         return call(
             functools.partial(weight_kernel, lanes),
-            (half, half),
+            (half, sds((128, wide), BF)),
             place,
             *grads,
             cols,

time: 82.4 us -> 82.4 us (level)
  no operation moved by 1% of the time
where the time goes in v18:
time: 82.4 us; the launch traced here: 82 us
  starting transfers between devices  27.7 us (34%)
  Pallas kernels  23.8 us (29%)
  blocking collectives  16.8 us (20%)
  waiting for transfers between devices  12.8 us (16%)
    pallas_call x16, Pallas kernels, call(): pl.pallas_call(kernel, out_shape=outs, in_specs=specs, out_specs=jax.tree...  23.8 us
    ppermute x15, starting transfers between devices, cross(): lax.ppermute(value, axis, [(n, n ^ mask) for n in range(lax.axis_size(axi...  19.1 us
    all_to_all x1, blocking collectives, body(): lax.all_to_all(summed.reshape(8, 8, 10 * C), 'gx', split_axis=0, concat_a...  16.8 us
    ppermute x10, starting transfers between devices, swap(): return lax.ppermute(value, ('gx', 'gy'), pairs)  8.58 us
    ppermute x15, waiting for transfers between devices, cross(): lax.ppermute(value, axis, [(n, n ^ mask) for n in range(lax.axis_size(axi...  6.83 us
    ppermute x10, waiting for transfers between devices, swap(): return lax.ppermute(value, ('gx', 'gy'), pairs)  6.01 us
  transfers between devices with their start and end apart: 25, of which 9 were waited for; matrix products, arithmetic and copies ran while one was open for 0% of the time, Pallas kernels for 24%

profile of v18, /device:TPU:2, one launch (start us, length us, event | category | flops | bytes accessed | tf_op | source)
XLA Modules:
  0.0 82.0 jit_solution(8067539246678434537)
XLA Ops:
  0.6 0.1 pad_add_fusion.place
  0.7 2.3 %shard_map.103 = (bf16[224,512]{1,0:T(8,128)(2,1)S(1)}, bf16[224,512]{1,0:T(8,128)(2,1)S(1)}, bf16[224,512]{1,0:T(8,128)(2,1)S(1)}, bf16[224,512]{1,0:T(8,128)(2...) custom-call(s32[2]{0:T(128)S(1)} %pad_add_fusion.place, ...), custom_call_target="tpu_custom_call" | custom-call | flops 4000000000 | bytes 10000 | tf_op jit(solution)/shard_map/pallas_call | solution.py:343
  3.0 0.0 copy-start.1
  3.0 2.2 %collective-permute-start.4 = (bf16[224,512]{1,0:T(8,128)(2,1)S(1)}, bf16[224,512]{1,0:T(8,128)(2,1)S(1)}, u32[]{:S(2)}, u32[]{:S(2)}) collective-permute-start(bf16[224,512]{1,0:T(8,128)(2,1)S(1)} %get-tuple-element.56), channel_id=1, source_target_pairs={{0,2},{1,3},{2,0},{3,1},{4,6},{5,7},{6,4},{7,5},{8,10},{9,11},{10,... | collective-permute-start | bytes 688136 | tf_op jit(solution)/shard_map/ppermute | solution.py:384
  5.3 1.4 %collective-permute-start.5 = (bf16[224,512]{1,0:T(8,128)(2,1)S(1)}, bf16[224,512]{1,0:T(8,128)(2,1)S(1)}, u32[]{:S(2)}, u32[]{:S(2)}) collective-permute-start(bf16[224,512]{1,0:T(8,128)(2,1)S(1)} %get-tuple-element.57), channel_id=1, source_target_pairs={{0,1},{1,0},{2,3},{3,2},{4,5},{5,4},{6,7},{7,6},{8,9},{9,8},{10,11... | collective-permute-start | bytes 688136 | tf_op jit(solution)/shard_map/ppermute | solution.py:384
  6.7 0.5 collective-permute-start.6
  7.2 3.0 %shard_map.104 = (f32[192,256]{1,0:T(8,128)S(1)}, bf16[96,256]{1,0:T(8,128)(2,1)S(1)}, bf16[96,256]{1,0:T(8,128)(2,1)S(1)}, bf16[64,256]{1,0:T(8,128)(2,1)S(1)}) custom-call(s32[2]{0:T(128)S(1)} %pad_add_fusion.place, f32[32,256]{1,0:T(8,128)S(1)} %get-tuple-element.45.nbt, bf16[192,256]{1,0:T(8,128)(2,1)S(1)} %get-tuple-element.46.grad, ...), custom_call_target="tpu_custom_call" | custom-call | flops 100000 | bytes 10000 | tf_op jit(solution)/shard_map/pallas_call | solution.py:343
  10.3 2.4 %collective-permute-start = (bf16[96,256]{1,0:T(8,128)(2,1)S(1)}, bf16[96,256]{1,0:T(8,128)(2,1)S(1)}, u32[]{:S(2)}, u32[]{:S(2)}) collective-permute-start(bf16[96,256]{1,0:T(8,128)(2,1)S(1)} %get-tuple-element.48), channel_id=1, source_target_pairs={{0,1},{1,0},{2,3},{3,2},{4,8},{5,9},{6,10},{7,11},{8,4},{9,5},{10,... | collective-permute-start | bytes 147464 | tf_op jit(solution)/shard_map/ppermute | solution.py:380
  12.6 0.0 collective-permute-start.1
  12.6 4.9 %collective-permute-done.m2 = bf16[96,256]{1,0:T(8,128)(2,1)S(1)} collective-permute-done((bf16[96,256]{1,0:T(8,128)(2,1)S(1)}, bf16[96,256]{1,0:T(8,128)(2,1)S(1)}, u32[]{:S(2)}, u32[]{:S(2)}) %collective-permute-start) | collective-permute-done | bytes 49184 | tf_op jit(solution)/shard_map/ppermute | solution.py:380
  17.5 0.6 shard_map.105
  18.1 0.6 collective-permute-start.2
  18.7 0.2 collective-permute-start.3
  18.9 1.1 %shard_map.106 = (bf16[768,256]{1,0:T(8,128)(2,1)S(1)}, bf16[768,256]{1,0:T(8,128)(2,1)S(1)}, bf16[4,64,512]{2,1,0:T(8,128)(2,1)S(1)}) custom-call(s32[2]{0:T(128)S(1)} %pad_add_fusion.place, bf16[224,512]{1,0:T(8,128)(2,1)S(1)} %get-tuple-element.55.p0, bf16[224,512]{1,0:T(8,128)(2,1)S(1)} %collective-permute-done.4.p2, ...), custom_call_target="tpu_custom_call" | custom-call | flops 100000 | bytes 10000 | tf_op jit(solution)/shard_map/pallas_call | solution.py:343
  19.9 2.0 %collective-permute-start.10 = (bf16[768,256]{1,0:T(8,128)(2,1)S(1)}, bf16[768,256]{1,0:T(8,128)(2,1)S(1)}, u32[]{:S(2)}, u32[]{:S(2)}) collective-permute-start(bf16[768,256]{1,0:T(8,128)(2,1)S(1)} %get-tuple-element.61), channel_id=1, source_target_pairs={{0,1},{1,0},{2,3},{3,2},{4,8},{5,9},{6,10},{7,11},{8,4},{9,5},{10,... | collective-permute-start | bytes 1179656 | tf_op jit(solution)/shard_map/ppermute | solution.py:380
  21.9 0.0 collective-permute-start.11
  21.9 0.3 collective-permute-done.2.n2
  22.2 0.5 collective-permute-done.3.n1
  22.8 0.9 %shard_map.107 = (bf16[192,256]{1,0:T(8,128)(2,1)S(1)}, bf16[192,512]{1,0:T(8,128)(2,1)S(1)}) custom-call(s32[2]{0:T(128)S(1)} %pad_add_fusion.place, f32[192,256]{1,0:T(8,128)S(1)} %get-tuple-element.47.late.own, bf16[96,256]{1,0:T(8,128)(2,1)S(1)} %collective-permute-done.m2, bf16[96,256]{1,0:T(8,128)(2,1)S(1)} %collective-permute-done.1.m1, ...), custom_call_target="tpu_custom_call" | custom-call | flops 100000 | bytes 10000 | tf_op jit(solution)/shard_map/pallas_call | solution.py:343
  23.7 1.0 %collective-permute-start.7 = (bf16[192,512]{1,0:T(8,128)(2,1)S(1)}, bf16[192,512]{1,0:T(8,128)(2,1)S(1)}, u32[]{:S(2)}, u32[]{:S(2)}) collective-permute-start(bf16[192,512]{1,0:T(8,128)(2,1)S(1)} %get-tuple-element.60.g0), channel_id=1, source_target_pairs={{0,2},{1,3},{2,0},{3,1},{4,6},{5,7},{6,4},{7,5},{8,10},{9,11},{10,... | collective-permute-start | bytes 589832 | tf_op jit(solution)/shard_map/ppermute | solution.py:384
  24.7 2.6 %collective-permute-start.8 = (bf16[192,512]{1,0:T(8,128)(2,1)S(1)}, bf16[192,512]{1,0:T(8,128)(2,1)S(1)}, u32[]{:S(2)}, u32[]{:S(2)}) collective-permute-start(bf16[192,512]{1,0:T(8,128)(2,1)S(1)} %get-tuple-element.60.g0), channel_id=1, source_target_pairs={{0,1},{1,0},{2,3},{3,2},{4,5},{5,4},{6,7},{7,6},{8,9},{9,8},{10,11... | collective-permute-start | bytes 589832 | tf_op jit(solution)/shard_map/ppermute | solution.py:384
  27.3 0.5 collective-permute-start.9
  27.9 3.0 %shard_map.108 = (f32[192,256]{1,0:T(8,128)S(1)}, bf16[96,256]{1,0:T(8,128)(2,1)S(1)}, bf16[96,256]{1,0:T(8,128)(2,1)S(1)}, bf16[64,256]{1,0:T(8,128)(2,1)S(1)}) custom-call(s32[2]{0:T(128)S(1)} %pad_add_fusion.place, f32[32,256]{1,0:T(8,128)S(1)} %get-tuple-element.45.nbt, bf16[192,256]{1,0:T(8,128)(2,1)S(1)} %get-tuple-element.63.grad, ...), custom_call_target="tpu_custom_call" | custom-call | flops 4000000000 | bytes 10000 | tf_op jit(solution)/shard_map/pallas_call | solution.py:343
  30.9 0.0 collective-permute-done.10.r2
  30.9 1.3 %collective-permute-start.12 = (bf16[96,256]{1,0:T(8,128)(2,1)S(1)}, bf16[96,256]{1,0:T(8,128)(2,1)S(1)}, u32[]{:S(2)}, u32[]{:S(2)}) collective-permute-start(bf16[96,256]{1,0:T(8,128)(2,1)S(1)} %get-tuple-element.67), channel_id=1, source_target_pairs={{0,1},{1,0},{2,3},{3,2},{4,8},{5,9},{6,10},{7,11},{8,4},{9,5},{10,... | collective-permute-start | bytes 147464 | tf_op jit(solution)/shard_map/ppermute | solution.py:380
  32.2 0.0 collective-permute-done.11.r1
  32.2 0.0 collective-permute-start.13
  32.2 4.3 %shard_map.109 = (bf16[768,1792]{1,0:T(8,128)(2,1)S(1)}, bf16[768,1792]{1,0:T(8,128)(2,1)S(1)}) custom-call(s32[2]{0:T(128)S(1)} %pad_add_fusion.place, bf16[224,512]{1,0:T(8,128)(2,1)S(1)} %get-tuple-element.55.p0, bf16[224,512]{1,0:T(8,128)(2,1)S(1)} %collective-permute-done.4.p2, bf16[224,512]{1,0:T(8,128)(2,1)S(1)} %collective-permute-done.5.p1, ...), custom_call_target="tpu_custom_call" | custom-call | flops 4000000000 | bytes 10000 | tf_op jit(solution)/shard_map/pallas_call | solution.py:343
  36.5 0.3 collective-permute-done.12.m2
  36.8 0.0 collective-permute-done.13.m1
  36.8 0.6 shard_map.110
  37.4 2.2 %collective-permute-start.15 = (bf16[96,256]{1,0:T(8,128)(2,1)S(1)}, bf16[96,256]{1,0:T(8,128)(2,1)S(1)}, u32[]{:S(2)}, u32[]{:S(2)}) collective-permute-start(bf16[96,256]{1,0:T(8,128)(2,1)S(1)} %get-tuple-element.72), channel_id=1, source_target_pairs={{0,4},{1,2},{2,1},{3,7},{4,0},{5,6},{6,5},{7,3},{8,12},{9,10},{10,... | collective-permute-start | bytes 147464 | tf_op jit(solution)/shard_map/ppermute | solution.py:380
  39.5 0.0 collective-permute-start.16
  39.5 0.0 collective-permute-done.7.g2
  39.5 0.0 collective-permute-done.8.g1
  39.5 0.0 collective-permute-done.9.g3
  39.6 1.7 %shard_map.111 = (f32[128,1792]{1,0:T(8,128)S(1)}, bf16[128,1792]{1,0:T(8,128)(2,1)S(1)}) custom-call(s32[2]{0:T(128)S(1)} %pad_add_fusion.place, bf16[192,512]{1,0:T(8,128)(2,1)S(1)} %get-tuple-element.60.g0, bf16[192,512]{1,0:T(8,128)(2,1)S(1)} %collective-permute-done.7.g2, bf16[192,512]{1,0:T(8,128)(2,1)S(1)} %collective-permute-done.8.g1, ...), custom_call_target="tpu_custom_call" | custom-call | flops 4000000000 | bytes 10000 | tf_op jit(solution)/shard_map/pallas_call | solution.py:343
  41.3 0.3 collective-permute-start.14
  41.6 1.7 %shard_map.112 = (bf16[128,1792]{1,0:T(8,128)(2,1)S(1)}, bf16[128,1792]{1,0:T(8,128)(2,1)S(1)}) custom-call(s32[2]{0:T(128)S(1)} %pad_add_fusion.place, bf16[192,512]{1,0:T(8,128)(2,1)S(1)} %get-tuple-element.60.g0, bf16[192,512]{1,0:T(8,128)(2,1)S(1)} %collective-permute-done.7.g2, bf16[192,512]{1,0:T(8,128)(2,1)S(1)} %collective-permute-done.8.g1, ...), custom_call_target="tpu_custom_call" | custom-call | flops 100000 | bytes 10000 | tf_op jit(solution)/shard_map/pallas_call | solution.py:343
  43.3 0.4 collective-permute-start.20
  43.6 0.0 collective-permute-done.15.n2
  43.6 0.0 collective-permute-done.16.n1
  43.6 1.0 %shard_map.113 = (bf16[128,256]{1,0:T(8,128)(2,1)S(1)}, bf16[128,256]{1,0:T(8,128)(2,1)S(1)}) custom-call(s32[2]{0:T(128)S(1)} %pad_add_fusion.place, f32[192,256]{1,0:T(8,128)S(1)} %get-tuple-element.64.late.own, bf16[96,256]{1,0:T(8,128)(2,1)S(1)} %collective-permute-done.12.m2, bf16[96,256]{1,0:T(8,128)(2,1)S(1)} %collective-permute-done.13.m1, ...), custom_call_target="tpu_custom_call" | custom-call | flops 20000000000 | bytes 10000 | tf_op jit(solution)/shard_map/pallas_call | solution.py:343
  44.6 0.3 collective-permute-start.21
  44.9 0.6 shard_map.114
  45.6 2.4 %collective-permute-start.17 = (bf16[32,1792]{1,0:T(8,128)(2,1)S(1)}, bf16[32,1792]{1,0:T(8,128)(2,1)S(1)}, u32[]{:S(2)}, u32[]{:S(2)}) collective-permute-start(bf16[32,1792]{1,0:T(8,128)(2,1)S(1)} %get-tuple-element.78), channel_id=1, source_target_pairs={{0,64},{4,68},{8,72},{12,76},{16,80},{20,84},{24,88},{28,92},{32,9... | collective-permute-start | bytes 344072 | tf_op jit(solution)/shard_map/ppermute | solution.py:384
  47.9 2.2 %collective-permute-start.18 = (bf16[32,1792]{1,0:T(8,128)(2,1)S(1)}, bf16[32,1792]{1,0:T(8,128)(2,1)S(1)}, u32[]{:S(2)}, u32[]{:S(2)}) collective-permute-start(bf16[32,1792]{1,0:T(8,128)(2,1)S(1)} %get-tuple-element.79), channel_id=1, source_target_pairs={{0,192},{4,196},{8,200},{12,204},{16,208},{20,212},{24,216},{28,22... | collective-permute-start | bytes 344072 | tf_op jit(solution)/shard_map/ppermute | solution.py:384
  50.1 1.0 %collective-permute-start.19 = (bf16[32,1792]{1,0:T(8,128)(2,1)S(1)}, bf16[32,1792]{1,0:T(8,128)(2,1)S(1)}, u32[]{:S(2)}, u32[]{:S(2)}) collective-permute-start(bf16[32,1792]{1,0:T(8,128)(2,1)S(1)} %get-tuple-element.80), channel_id=1, source_target_pairs={{0,128},{4,132},{8,136},{12,140},{16,144},{20,148},{24,152},{28,15... | collective-permute-start | bytes 344072 | tf_op jit(solution)/shard_map/ppermute | solution.py:384
  51.1 0.0 collective-permute-done.21.rs
  51.1 0.0 collective-permute-done.20.come
  51.1 0.7 shard_map.116
  51.8 1.0 %collective-permute-start.22 = (bf16[32,2304]{1,0:T(8,128)(2,1)S(1)}, bf16[32,2304]{1,0:T(8,128)(2,1)S(1)}, u32[]{:S(2)}, u32[]{:S(2)}) collective-permute-start(bf16[32,2304]{1,0:T(8,128)(2,1)S(1)} %get-tuple-element.84), channel_id=1, source_target_pairs={{0,64},{4,68},{8,72},{12,76},{16,80},{20,84},{24,88},{28,92},{32,9... | collective-permute-start | bytes 442376 | tf_op jit(solution)/shard_map/ppermute | solution.py:384
  52.8 2.2 %collective-permute-start.23 = (bf16[32,2304]{1,0:T(8,128)(2,1)S(1)}, bf16[32,2304]{1,0:T(8,128)(2,1)S(1)}, u32[]{:S(2)}, u32[]{:S(2)}) collective-permute-start(bf16[32,2304]{1,0:T(8,128)(2,1)S(1)} %get-tuple-element.85), channel_id=1, source_target_pairs={{0,192},{4,196},{8,200},{12,204},{16,208},{20,212},{24,216},{28,22... | collective-permute-start | bytes 442376 | tf_op jit(solution)/shard_map/ppermute | solution.py:384
  55.0 0.0 collective-permute-done.17.a1
  55.0 1.0 %collective-permute-start.24 = (bf16[32,2304]{1,0:T(8,128)(2,1)S(1)}, bf16[32,2304]{1,0:T(8,128)(2,1)S(1)}, u32[]{:S(2)}, u32[]{:S(2)}) collective-permute-start(bf16[32,2304]{1,0:T(8,128)(2,1)S(1)} %get-tuple-element.86), channel_id=1, source_target_pairs={{0,128},{4,132},{8,136},{12,140},{16,144},{20,148},{24,152},{28,15... | collective-permute-start | bytes 442376 | tf_op jit(solution)/shard_map/ppermute | solution.py:384
  56.0 0.1 collective-permute-done.18.a3
  56.1 1.6 %collective-permute-done.19.a2 = bf16[32,1792]{1,0:T(8,128)(2,1)S(1)} collective-permute-done((bf16[32,1792]{1,0:T(8,128)(2,1)S(1)}, bf16[32,1792]{1,0:T(8,128)(2,1)S(1)}, u32[]{:S(2)}, u32[]{:S(2)}) %collective-permute-start.19) | collective-permute-done | bytes 114720 | tf_op jit(solution)/shard_map/ppermute | solution.py:384
  57.7 0.6 shard_map.115.two
  58.3 0.5 collective-permute-done.22.b1
  58.8 2.9 %collective-permute-done.23.b3 = bf16[32,2304]{1,0:T(8,128)(2,1)S(1)} collective-permute-done((bf16[32,2304]{1,0:T(8,128)(2,1)S(1)}, bf16[32,2304]{1,0:T(8,128)(2,1)S(1)}, u32[]{:S(2)}, u32[]{:S(2)}) %collective-permute-start.23) | collective-permute-done | bytes 147488 | tf_op jit(solution)/shard_map/ppermute | solution.py:384
  61.7 1.7 %collective-permute-done.24.b2 = bf16[32,2304]{1,0:T(8,128)(2,1)S(1)} collective-permute-done((bf16[32,2304]{1,0:T(8,128)(2,1)S(1)}, bf16[32,2304]{1,0:T(8,128)(2,1)S(1)}, u32[]{:S(2)}, u32[]{:S(2)}) %collective-permute-start.24) | collective-permute-done | bytes 147488 | tf_op jit(solution)/shard_map/ppermute | solution.py:384
  63.4 0.9 %shard_map.117 = bf16[64,2560]{1,0:T(8,128)(2,1)S(1)} custom-call(s32[2]{0:T(128)S(1)} %pad_add_fusion.place, bf16[32,1792]{1,0:T(8,128)(2,1)S(1)} %shard_map.115.two, bf16[32,2304]{1,0:T(8,128)(2,1)S(1)} %get-tuple-element.83.b0, bf16[32,2304]{1,0:T(8,128)(2,1)S(1)} %collective-permute-done.22.b1, bf16[32,2304]{1,0:T(8,128)(2,1)S(1)} %collective-permute-done.23.b3, ...), custom_call_target="tpu_custom_call" | custom-call | flops 100000 | bytes 10000 | tf_op jit(solution)/shard_map/pallas_call | solution.py:343
  64.3 16.8 %all_to_all.5.refs_0_ = bf16[8,8,2560]{2,1,0:T(8,128)(2,1)S(1)} all-to-all(bf16[8,8,2560]{2,1,0:T(8,128)(2,1)S(1)} %bitcast.5), channel_id=1, replica_groups={{0,8,16,24,32,40,48,56},{4,12,20,28,36,44,52,60},{64,72,80,88,96,104,11..., dimensions={0} | all-to-all | bytes 655360 | tf_op jit(solution)/shard_map/all_to_all | solution.py:562
  81.1 0.9 %shard_map.118 = (bf16[192,256]{1,0:T(8,128)(2,1)}, f32[4,1728]{1,0:T(4,128)}, f32[4,1728]{1,0:T(4,128)}) custom-call(bf16[8,8,2560]{2,1,0:T(8,128)(2,1)S(1)} %all_to_all.5.refs_0_), custom_call_target="tpu_custom_call" | custom-call | flops 100000 | bytes 10000 | tf_op jit(solution)/shard_map/pallas_call | solution.py:343
  (8 shorter events, 0.0 us)
Async XLA Ops:
  0.7 6.5 %copy-start = (bf16[256,6912]{1,0:T(8,128)(2,1)S(1)}, bf16[256,6912]{1,0:T(8,128)(2,1)}, u32[]{:S(2)}) copy-start(bf16[256,6912]{1,0:T(8,128)(2,1)} %weight.2) | copy-start | bytes 10616836
  3.0 24.8 %copy-start.1 = (bf16[256,6912]{1,0:T(8,128)(2,1)S(1)}, bf16[256,6912]{1,0:T(8,128)(2,1)}, u32[]{:S(2)}) copy-start(bf16[256,6912]{1,0:T(8,128)(2,1)} %weight.3) | copy-start | bytes 10616836
  3.0 15.8 %collective-permute-start.4 = (bf16[224,512]{1,0:T(8,128)(2,1)S(1)}, bf16[224,512]{1,0:T(8,128)(2,1)S(1)}, u32[]{:S(2)}, u32[]{:S(2)}) collective-permute-start(bf16[224,512]{1,0:T(8,128)(2,1)S(1)} %get-tuple-element.56), channel_id=1, source_target_pairs={{0,2},{1,3},{2,0},{3,1},{4,6},{5,7},{6,4},{7,5},{8,10},{9,11},{10,... | collective-permute-start | bytes 688136 | tf_op jit(solution)/shard_map/ppermute | solution.py:384
  5.3 13.6 %collective-permute-start.5 = (bf16[224,512]{1,0:T(8,128)(2,1)S(1)}, bf16[224,512]{1,0:T(8,128)(2,1)S(1)}, u32[]{:S(2)}, u32[]{:S(2)}) collective-permute-start(bf16[224,512]{1,0:T(8,128)(2,1)S(1)} %get-tuple-element.57), channel_id=1, source_target_pairs={{0,1},{1,0},{2,3},{3,2},{4,5},{5,4},{6,7},{7,6},{8,9},{9,8},{10,11... | collective-permute-start | bytes 688136 | tf_op jit(solution)/shard_map/ppermute | solution.py:384
  6.7 12.2 %collective-permute-start.6 = (bf16[224,512]{1,0:T(8,128)(2,1)S(1)}, bf16[224,512]{1,0:T(8,128)(2,1)S(1)}, u32[]{:S(2)}, u32[]{:S(2)}) collective-permute-start(bf16[224,512]{1,0:T(8,128)(2,1)S(1)} %get-tuple-element.58), channel_id=1, source_target_pairs={{0,3},{1,2},{2,1},{3,0},{4,7},{5,6},{6,5},{7,4},{8,11},{9,10},{10,... | collective-permute-start | bytes 688136 | tf_op jit(solution)/shard_map/ppermute | solution.py:384
  10.3 7.2 %collective-permute-start = (bf16[96,256]{1,0:T(8,128)(2,1)S(1)}, bf16[96,256]{1,0:T(8,128)(2,1)S(1)}, u32[]{:S(2)}, u32[]{:S(2)}) collective-permute-start(bf16[96,256]{1,0:T(8,128)(2,1)S(1)} %get-tuple-element.48), channel_id=1, source_target_pairs={{0,1},{1,0},{2,3},{3,2},{4,8},{5,9},{6,10},{7,11},{8,4},{9,5},{10,... | collective-permute-start | bytes 147464 | tf_op jit(solution)/shard_map/ppermute | solution.py:380
  12.6 4.9 %collective-permute-start.1 = (bf16[96,256]{1,0:T(8,128)(2,1)S(1)}, bf16[96,256]{1,0:T(8,128)(2,1)S(1)}, u32[]{:S(2)}, u32[]{:S(2)}) collective-permute-start(bf16[96,256]{1,0:T(8,128)(2,1)S(1)} %get-tuple-element.49), channel_id=1, source_target_pairs={{0,4},{1,5},{2,6},{3,7},{4,0},{5,1},{6,2},{7,3},{8,12},{9,13},{10,... | collective-permute-start | bytes 147464 | tf_op jit(solution)/shard_map/ppermute | solution.py:380
  18.1 4.2 %collective-permute-start.2 = (bf16[96,256]{1,0:T(8,128)(2,1)S(1)}, bf16[96,256]{1,0:T(8,128)(2,1)S(1)}, u32[]{:S(2)}, u32[]{:S(2)}) collective-permute-start(bf16[96,256]{1,0:T(8,128)(2,1)S(1)} %get-tuple-element.51), channel_id=1, source_target_pairs={{0,4},{1,2},{2,1},{3,7},{4,0},{5,6},{6,5},{7,3},{8,12},{9,10},{10,... | collective-permute-start | bytes 147464 | tf_op jit(solution)/shard_map/ppermute | solution.py:380
  18.7 4.1 %collective-permute-start.3 = (bf16[96,256]{1,0:T(8,128)(2,1)S(1)}, bf16[96,256]{1,0:T(8,128)(2,1)S(1)}, u32[]{:S(2)}, u32[]{:S(2)}) collective-permute-start(bf16[96,256]{1,0:T(8,128)(2,1)S(1)} %get-tuple-element.52.late), channel_id=1, source_target_pairs={{0,1},{1,0},{2,3},{3,2},{4,5},{5,4},{6,7},{7,6},{8,9},{9,8},{10,11... | collective-permute-start | bytes 147464 | tf_op jit(solution)/shard_map/ppermute | solution.py:380
  19.9 11.0 %collective-permute-start.10 = (bf16[768,256]{1,0:T(8,128)(2,1)S(1)}, bf16[768,256]{1,0:T(8,128)(2,1)S(1)}, u32[]{:S(2)}, u32[]{:S(2)}) collective-permute-start(bf16[768,256]{1,0:T(8,128)(2,1)S(1)} %get-tuple-element.61), channel_id=1, source_target_pairs={{0,1},{1,0},{2,3},{3,2},{4,8},{5,9},{6,10},{7,11},{8,4},{9,5},{10,... | collective-permute-start | bytes 1179656 | tf_op jit(solution)/shard_map/ppermute | solution.py:380
  21.9 10.3 %collective-permute-start.11 = (bf16[768,256]{1,0:T(8,128)(2,1)S(1)}, bf16[768,256]{1,0:T(8,128)(2,1)S(1)}, u32[]{:S(2)}, u32[]{:S(2)}) collective-permute-start(bf16[768,256]{1,0:T(8,128)(2,1)S(1)} %get-tuple-element.62), channel_id=1, source_target_pairs={{0,4},{1,5},{2,6},{3,7},{4,0},{5,1},{6,2},{7,3},{8,12},{9,13},{10,... | collective-permute-start | bytes 1179656 | tf_op jit(solution)/shard_map/ppermute | solution.py:380
  23.7 15.9 %collective-permute-start.7 = (bf16[192,512]{1,0:T(8,128)(2,1)S(1)}, bf16[192,512]{1,0:T(8,128)(2,1)S(1)}, u32[]{:S(2)}, u32[]{:S(2)}) collective-permute-start(bf16[192,512]{1,0:T(8,128)(2,1)S(1)} %get-tuple-element.60.g0), channel_id=1, source_target_pairs={{0,2},{1,3},{2,0},{3,1},{4,6},{5,7},{6,4},{7,5},{8,10},{9,11},{10,... | collective-permute-start | bytes 589832 | tf_op jit(solution)/shard_map/ppermute | solution.py:384
  24.7 14.8 %collective-permute-start.8 = (bf16[192,512]{1,0:T(8,128)(2,1)S(1)}, bf16[192,512]{1,0:T(8,128)(2,1)S(1)}, u32[]{:S(2)}, u32[]{:S(2)}) collective-permute-start(bf16[192,512]{1,0:T(8,128)(2,1)S(1)} %get-tuple-element.60.g0), channel_id=1, source_target_pairs={{0,1},{1,0},{2,3},{3,2},{4,5},{5,4},{6,7},{7,6},{8,9},{9,8},{10,11... | collective-permute-start | bytes 589832 | tf_op jit(solution)/shard_map/ppermute | solution.py:384
  27.3 12.2 %collective-permute-start.9 = (bf16[192,512]{1,0:T(8,128)(2,1)S(1)}, bf16[192,512]{1,0:T(8,128)(2,1)S(1)}, u32[]{:S(2)}, u32[]{:S(2)}) collective-permute-start(bf16[192,512]{1,0:T(8,128)(2,1)S(1)} %get-tuple-element.60.g0), channel_id=1, source_target_pairs={{0,3},{1,2},{2,1},{3,0},{4,7},{5,6},{6,5},{7,4},{8,11},{9,10},{10,... | collective-permute-start | bytes 589832 | tf_op jit(solution)/shard_map/ppermute | solution.py:384
  30.9 5.9 %collective-permute-start.12 = (bf16[96,256]{1,0:T(8,128)(2,1)S(1)}, bf16[96,256]{1,0:T(8,128)(2,1)S(1)}, u32[]{:S(2)}, u32[]{:S(2)}) collective-permute-start(bf16[96,256]{1,0:T(8,128)(2,1)S(1)} %get-tuple-element.67), channel_id=1, source_target_pairs={{0,1},{1,0},{2,3},{3,2},{4,8},{5,9},{6,10},{7,11},{8,4},{9,5},{10,... | collective-permute-start | bytes 147464 | tf_op jit(solution)/shard_map/ppermute | solution.py:380
  32.2 4.6 %collective-permute-start.13 = (bf16[96,256]{1,0:T(8,128)(2,1)S(1)}, bf16[96,256]{1,0:T(8,128)(2,1)S(1)}, u32[]{:S(2)}, u32[]{:S(2)}) collective-permute-start(bf16[96,256]{1,0:T(8,128)(2,1)S(1)} %get-tuple-element.68), channel_id=1, source_target_pairs={{0,4},{1,5},{2,6},{3,7},{4,0},{5,1},{6,2},{7,3},{8,12},{9,13},{10,... | collective-permute-start | bytes 147464 | tf_op jit(solution)/shard_map/ppermute | solution.py:380
  37.4 6.3 %collective-permute-start.15 = (bf16[96,256]{1,0:T(8,128)(2,1)S(1)}, bf16[96,256]{1,0:T(8,128)(2,1)S(1)}, u32[]{:S(2)}, u32[]{:S(2)}) collective-permute-start(bf16[96,256]{1,0:T(8,128)(2,1)S(1)} %get-tuple-element.72), channel_id=1, source_target_pairs={{0,4},{1,2},{2,1},{3,7},{4,0},{5,6},{6,5},{7,3},{8,12},{9,10},{10,... | collective-permute-start | bytes 147464 | tf_op jit(solution)/shard_map/ppermute | solution.py:380
  39.5 4.1 %collective-permute-start.16 = (bf16[96,256]{1,0:T(8,128)(2,1)S(1)}, bf16[96,256]{1,0:T(8,128)(2,1)S(1)}, u32[]{:S(2)}, u32[]{:S(2)}) collective-permute-start(bf16[96,256]{1,0:T(8,128)(2,1)S(1)} %get-tuple-element.69.late), channel_id=1, source_target_pairs={{0,1},{1,0},{2,3},{3,2},{4,5},{5,4},{6,7},{7,6},{8,9},{9,8},{10,11... | collective-permute-start | bytes 147464 | tf_op jit(solution)/shard_map/ppermute | solution.py:380
  41.3 3.7 %collective-permute-start.14 = (bf16[128,1792]{1,0:T(8,128)(2,1)S(1)}, bf16[128,1792]{1,0:T(8,128)(2,1)S(1)}, u32[]{:S(2)}, u32[]{:S(2)}) collective-permute-start(bf16[128,1792]{1,0:T(8,128)(2,1)S(1)} %get-tuple-element.71), channel_id=1, source_target_pairs={{0,4},{4,0},{8,12},{12,8},{16,20},{20,16},{24,28},{28,24},{32,36},... | collective-permute-start | bytes 1376264 | tf_op jit(solution)/shard_map/ppermute | solution.py:384
  43.3 7.9 %collective-permute-start.20 = (bf16[128,1792]{1,0:T(8,128)(2,1)S(1)}, bf16[128,1792]{1,0:T(8,128)(2,1)S(1)}, u32[]{:S(2)}, u32[]{:S(2)}) collective-permute-start(bf16[128,1792]{1,0:T(8,128)(2,1)S(1)} %get-tuple-element.81), channel_id=1, source_target_pairs={{0,4},{4,0},{8,12},{12,8},{16,20},{20,16},{24,28},{28,24},{32,36},... | collective-permute-start | bytes 1376264 | tf_op jit(solution)/shard_map/ppermute | solution.py:384
  44.6 6.5 %collective-permute-start.21 = (bf16[128,256]{1,0:T(8,128)(2,1)S(1)}, bf16[128,256]{1,0:T(8,128)(2,1)S(1)}, u32[]{:S(2)}, u32[]{:S(2)}) collective-permute-start(bf16[128,256]{1,0:T(8,128)(2,1)S(1)} %get-tuple-element.82), channel_id=1, source_target_pairs={{0,4},{4,0},{8,12},{12,8},{16,20},{20,16},{24,28},{28,24},{32,36},... | collective-permute-start | bytes 196616 | tf_op jit(solution)/shard_map/ppermute | solution.py:384
  45.6 9.4 %collective-permute-start.17 = (bf16[32,1792]{1,0:T(8,128)(2,1)S(1)}, bf16[32,1792]{1,0:T(8,128)(2,1)S(1)}, u32[]{:S(2)}, u32[]{:S(2)}) collective-permute-start(bf16[32,1792]{1,0:T(8,128)(2,1)S(1)} %get-tuple-element.78), channel_id=1, source_target_pairs={{0,64},{4,68},{8,72},{12,76},{16,80},{20,84},{24,88},{28,92},{32,9... | collective-permute-start | bytes 344072 | tf_op jit(solution)/shard_map/ppermute | solution.py:384
  47.9 8.1 %collective-permute-start.18 = (bf16[32,1792]{1,0:T(8,128)(2,1)S(1)}, bf16[32,1792]{1,0:T(8,128)(2,1)S(1)}, u32[]{:S(2)}, u32[]{:S(2)}) collective-permute-start(bf16[32,1792]{1,0:T(8,128)(2,1)S(1)} %get-tuple-element.79), channel_id=1, source_target_pairs={{0,192},{4,196},{8,200},{12,204},{16,208},{20,212},{24,216},{28,22... | collective-permute-start | bytes 344072 | tf_op jit(solution)/shard_map/ppermute | solution.py:384
  50.1 7.6 %collective-permute-start.19 = (bf16[32,1792]{1,0:T(8,128)(2,1)S(1)}, bf16[32,1792]{1,0:T(8,128)(2,1)S(1)}, u32[]{:S(2)}, u32[]{:S(2)}) collective-permute-start(bf16[32,1792]{1,0:T(8,128)(2,1)S(1)} %get-tuple-element.80), channel_id=1, source_target_pairs={{0,128},{4,132},{8,136},{12,140},{16,144},{20,148},{24,152},{28,15... | collective-permute-start | bytes 344072 | tf_op jit(solution)/shard_map/ppermute | solution.py:384
  51.8 7.0 %collective-permute-start.22 = (bf16[32,2304]{1,0:T(8,128)(2,1)S(1)}, bf16[32,2304]{1,0:T(8,128)(2,1)S(1)}, u32[]{:S(2)}, u32[]{:S(2)}) collective-permute-start(bf16[32,2304]{1,0:T(8,128)(2,1)S(1)} %get-tuple-element.84), channel_id=1, source_target_pairs={{0,64},{4,68},{8,72},{12,76},{16,80},{20,84},{24,88},{28,92},{32,9... | collective-permute-start | bytes 442376 | tf_op jit(solution)/shard_map/ppermute | solution.py:384
  52.8 8.9 %collective-permute-start.23 = (bf16[32,2304]{1,0:T(8,128)(2,1)S(1)}, bf16[32,2304]{1,0:T(8,128)(2,1)S(1)}, u32[]{:S(2)}, u32[]{:S(2)}) collective-permute-start(bf16[32,2304]{1,0:T(8,128)(2,1)S(1)} %get-tuple-element.85), channel_id=1, source_target_pairs={{0,192},{4,196},{8,200},{12,204},{16,208},{20,212},{24,216},{28,22... | collective-permute-start | bytes 442376 | tf_op jit(solution)/shard_map/ppermute | solution.py:384
  55.0 8.4 %collective-permute-start.24 = (bf16[32,2304]{1,0:T(8,128)(2,1)S(1)}, bf16[32,2304]{1,0:T(8,128)(2,1)S(1)}, u32[]{:S(2)}, u32[]{:S(2)}) collective-permute-start(bf16[32,2304]{1,0:T(8,128)(2,1)S(1)} %get-tuple-element.86), channel_id=1, source_target_pairs={{0,128},{4,132},{8,136},{12,140},{16,144},{20,148},{24,152},{28,15... | collective-permute-start | bytes 442376 | tf_op jit(solution)/shard_map/ppermute | solution.py:384
